TPU v7x, 32 devices: a whole 2x2x4 slice. The times are simulated.
32 devices in a mesh: context: 16 (over z, y, core), heads: 2 (over x).
Axes of the slice: x: 2, y: 2, z: 4, core: 2. Of those that a mesh axis runs over, the one named last changes fastest.
Arguments:
- upstream: bfloat16 [4096, 1024], P(('context', 'heads')), may hold values from -48 to 48
- out_weight: bfloat16 [1024, 1024], P('heads'), may hold values from -0.1875 to 0.1875
- query_rows: bfloat16 [4096, 1024], P('context', 'heads'), may hold values from -6 to 6
- key_rows: bfloat16 [4096, 1024], P('context', 'heads'), may hold values from -6 to 6
- value_rows: bfloat16 [4096, 1024], P('context', 'heads'), may hold values from -6 to 6
- head_offsets: int32 [16], replicated, may hold values from 0 to 15, each once
Outputs:
- query_grad: bfloat16 [4096, 1024], P('context', 'heads')
- key_grad: bfloat16 [4096, 1024], P('context', 'heads')
- value_grad: bfloat16 [4096, 1024], P('context', 'heads')
Inputs may be any that keep to these rules, and one draw needn't show every extreme that they name: `head_offsets`: every value of 0 to 15 occurs once.
All inputs are finite; a program needn't handle non-finite values.
Results may differ from a plain program's by a relative error of at most 0.008.
Values may be sent and summed in bfloat16 or wider, within the bound.
No kernel may reach another device: no remote copies, remote signals or barrier semaphores. Data moves between devices by JAX's collectives and lax.ppermute only.
A program may use at most 128 MiB of HBM per device.

v0:
```python
import math

import jax
import jax.numpy as jnp
from jax import lax
from jax.sharding import PartitionSpec as P

HEAD_SIZE = 64
DILATION_RATE = 16
FIRST_SEGMENT = 2048


def partner_2(value, axis, apart):
    mask = 2**apart
    pairs = [(source, source ^ mask) for source in range(lax.axis_size(axis))]
    return lax.ppermute(value, axis, pairs)


def dot_rows(left, right):
    return lax.dot_general(
        left, right, (((1,), (1,)), ((), ())), preferred_element_type=jnp.float32
    )


def dot_cols(left, right):
    return lax.dot_general(
        left, right, (((0,), (0,)), ((), ())), preferred_element_type=jnp.float32
    )


def pick_rows(payload_arrays, mask_stack):
    span_length, block_width = payload_arrays.shape
    head_count = mask_stack.shape[1]
    launch_layout = payload_arrays.reshape(
        span_length // DILATION_RATE, DILATION_RATE, head_count, block_width // head_count
    )
    selected_rows = jnp.where(
        mask_stack[None, :, :, None], launch_layout, jnp.zeros((), payload_arrays.dtype)
    )
    return jnp.sum(selected_rows, axis=1).reshape(span_length // DILATION_RATE, block_width)


def place_rows(picked, mask_stack):
    total_count, block_width = picked.shape
    head_count = mask_stack.shape[1]
    launch_layout = picked.reshape(total_count, 1, head_count, block_width // head_count)
    dispersal_rows = jnp.where(
        mask_stack[None, :, :, None], launch_layout, jnp.zeros((), picked.dtype)
    )
    return dispersal_rows.reshape(total_count * DILATION_RATE, block_width)


def spread_rows(value_tensor, head_shift):
    total_count = value_tensor.shape[0]
    matched_flag = jnp.arange(DILATION_RATE, dtype=jnp.int32)[None, :] == head_shift
    return jnp.where(
        matched_flag, value_tensor[:, None], jnp.zeros((), value_tensor.dtype)
    ).reshape(total_count * DILATION_RATE)


def double_up(buffer, levels, position):
    for level in range(levels):
        partner = partner_2(buffer, "context", level)
        lower = position >> level & 1 == 0
        buffer = jnp.where(
            lower, jnp.concatenate([buffer, partner], 1), jnp.concatenate([partner, buffer], 1)
        )
    return buffer


def halve_down(buffer, levels, position):
    for level in range(levels - 1, -1, -1):
        middle = buffer.shape[1] // 2
        lower_half = buffer[:, :middle]
        upper_half = buffer[:, middle:]
        lower = position >> level & 1 == 0
        kept = jnp.where(lower, lower_half, upper_half)
        outgoing = jnp.where(lower, upper_half, lower_half)
        incoming = partner_2(outgoing, "context", level)
        buffer = kept + incoming
    return buffer


def body(upstream, out_weight, query_rows, key_rows, value_rows, head_offsets):
    position = lax.axis_index("context")
    span_length, block_width = query_rows.shape
    head_count = block_width // HEAD_SIZE
    scale = 1.0 / math.sqrt(HEAD_SIZE)
    partial_rows = dot_rows(upstream, lax.all_gather(out_weight, "heads", axis=0, tiled=True))
    attn_grad = lax.all_to_all(
        partial_rows.astype(jnp.bfloat16), "heads", split_axis=1, concat_axis=0, tiled=True
    )
    local_shifts = lax.dynamic_slice_in_dim(
        head_offsets, lax.axis_index("heads") * head_count, head_count
    )
    mask_stack = jnp.arange(DILATION_RATE, dtype=jnp.int32)[:, None] == local_shifts[None, :]
    query_pick = pick_rows(query_rows, mask_stack)
    grad_pick = pick_rows(attn_grad, mask_stack)
    key_pick = pick_rows(key_rows, mask_stack)
    value_pick = pick_rows(value_rows, mask_stack)
    picked_pair = jnp.stack([key_pick, value_pick])
    dense_span = FIRST_SEGMENT // span_length
    dense_levels = dense_span.bit_length() - 1
    near_pair = double_up(jnp.stack([key_rows, value_rows]), dense_levels, position)
    far_pair = lax.all_gather(picked_pair, "context", axis=1, tiled=True)
    block_rows = min(512, span_length)
    num_blocks = span_length // block_rows
    current_row_index = jnp.arange(span_length, dtype=jnp.int32)
    dq_near_list, dk_near_list, dv_near_list = ([], [], [])
    dq_far_list, dk_far_list, dv_far_list = ([], [], [])
    lse_list, delta_list = ([], [])
    for head in range(head_count):
        columns = slice(head * HEAD_SIZE, (head + 1) * HEAD_SIZE)
        head_shift = local_shifts[head]
        query_head = query_rows[:, columns]
        grad_head = attn_grad[:, columns]
        near_keys = near_pair[0][:, columns]
        near_values = near_pair[1][:, columns]
        query_sel = query_pick[:, columns]
        grad_sel = grad_pick[:, columns]
        far_keys = far_pair[0][:, columns]
        far_values = far_pair[1][:, columns]
        score_near = dot_rows(query_sel, near_keys) * scale
        score_far = dot_rows(query_sel, far_keys) * scale
        row_max = jnp.maximum(jnp.max(score_near, 1), jnp.max(score_far, 1))
        row_sum = jnp.sum(jnp.exp(score_near - row_max[:, None]), 1) + jnp.sum(
            jnp.exp(score_far - row_max[:, None]), 1
        )
        lse_sel = row_max + jnp.log(row_sum)
        prob_near = jnp.exp(score_near - lse_sel[:, None])
        prob_far = jnp.exp(score_far - lse_sel[:, None])
        dprob_near = dot_rows(grad_sel, near_values)
        dprob_far = dot_rows(grad_sel, far_values)
        delta_sel = jnp.sum(prob_near * dprob_near, 1) + jnp.sum(prob_far * dprob_far, 1)
        dscore_far = (prob_far * (dprob_far - delta_sel[:, None])).astype(jnp.bfloat16)
        dq_far_list.append(
            jnp.dot(dscore_far, far_keys, preferred_element_type=jnp.float32) * scale
        )
        lse_list.append(lse_sel)
        delta_list.append(delta_sel)
        prob_far16 = prob_far.astype(jnp.bfloat16)
        dk_far_list.append(dot_cols(dscore_far, query_sel) * scale)
        dv_far_list.append(dot_cols(prob_far16, grad_sel))
        lse_rows = spread_rows(lse_sel, head_shift)
        delta_rows = spread_rows(delta_sel, head_shift)
        selected_rows = current_row_index % DILATION_RATE == head_shift

        def step(carry, inputs):
            key_acc, value_acc = carry
            query_blk, grad_blk, lse_blk, delta_blk, mask_blk = inputs
            scores = dot_rows(query_blk, near_keys) * scale
            blk_max = jnp.max(scores, 1)
            blk_sum = jnp.sum(jnp.exp(scores - blk_max[:, None]), 1)
            lse_all = jnp.where(mask_blk, lse_blk, blk_max + jnp.log(blk_sum))
            probs = jnp.exp(scores - lse_all[:, None])
            dprobs = dot_rows(grad_blk, near_values)
            delta_all = jnp.where(mask_blk, delta_blk, jnp.sum(probs * dprobs, 1))
            dscores = (probs * (dprobs - delta_all[:, None])).astype(jnp.bfloat16)
            probs16 = probs.astype(jnp.bfloat16)
            dq_blk = jnp.dot(dscores, near_keys, preferred_element_type=jnp.float32) * scale
            key_acc = key_acc + dot_cols(dscores, query_blk) * scale
            value_acc = value_acc + dot_cols(probs16, grad_blk)
            return ((key_acc, value_acc), dq_blk)

        zeros_acc = jnp.zeros((near_keys.shape[0], HEAD_SIZE), jnp.float32)
        (key_acc, value_acc), dq_blocks = lax.scan(
            step,
            (zeros_acc, zeros_acc),
            (
                query_head.reshape(num_blocks, block_rows, HEAD_SIZE),
                grad_head.reshape(num_blocks, block_rows, HEAD_SIZE),
                lse_rows.reshape(num_blocks, block_rows),
                delta_rows.reshape(num_blocks, block_rows),
                selected_rows.reshape(num_blocks, block_rows),
            ),
        )
        dq_near_list.append(dq_blocks.reshape(span_length, HEAD_SIZE))
        dk_near_list.append(key_acc)
        dv_near_list.append(value_acc)
    near_terms = jnp.stack([jnp.concatenate(dk_near_list, 1), jnp.concatenate(dv_near_list, 1)])
    near_back = halve_down(near_terms, dense_levels, position)
    far_terms = jnp.stack([jnp.concatenate(dk_far_list, 1), jnp.concatenate(dv_far_list, 1)])
    far_back = lax.psum_scatter(far_terms, "context", scatter_dimension=1, tiled=True)
    far_key_grad = far_back[0]
    far_value_grad = far_back[1]
    query_grad = (
        jnp.concatenate(dq_near_list, 1) + place_rows(jnp.concatenate(dq_far_list, 1), mask_stack)
    ).astype(jnp.bfloat16)
    key_grad = (near_back[0] + place_rows(far_key_grad, mask_stack)).astype(jnp.bfloat16)
    value_grad = (near_back[1] + place_rows(far_value_grad, mask_stack)).astype(jnp.bfloat16)
    return (query_grad, key_grad, value_grad)


def solution(mesh):
    return jax.shard_map(
        body,
        mesh=mesh,
        in_specs=(
            P(("context", "heads"), None),
            P("heads", None),
            P("context", "heads"),
            P("context", "heads"),
            P("context", "heads"),
            P(),
        ),
        out_specs=(P("context", "heads"), P("context", "heads"), P("context", "heads")),
        check_vma=False,
    )
```

profile of v0, /device:TPU:0, one launch (start us, length us, event | category | flops | bytes accessed | tf_op | source)
XLA Modules:
  0.0 430.0 jit_solution(16658555262435492845)
XLA Ops:
  8.0 1.1 pad_maximum_fusion.2
  9.9 1.1 reshape.726
  10.9 1.1 reshape.723
  14.0 1.2 iota_compare_fusion.1
  15.2 1.1 iota_compare_fusion.2
  16.3 1.2 iota_compare_fusion.3
  17.5 1.7 maximum_select_fusion.2
  19.2 2.6 collective-permute-start.1
  21.8 1.2 iota_compare_fusion.4
  23.0 1.2 iota_compare_fusion.5
  24.2 1.1 iota_compare_fusion.6
  25.3 1.1 iota_compare_fusion.7
  26.4 1.2 iota_compare_fusion.8
  27.5 17.9 %all-gather.2.cloned.1.call-done = bf16[1024,1024]{1,0:T(8,128)(2,1)} async-done(((bf16[512,1024]{1,0:T(8,128)(2,1)}), bf16[1024,1024]{1,0:T(8,128)(2,1)}) %all-gather.2.cloned.1.call-update) | async-done | bytes 2097168 | tf_op jit(solution)/shard_map/all_gather | solution.py:89
  45.5 2.4 convolution_convert_fusion
  48.6 3.4 all-to-all-start
  52.1 2.8 maximum_select_fusion.1
  54.9 1.6 collective-permute-start.2
  56.5 1.0 all-to-all-done
  57.5 1.1 reshape.727
  58.6 2.0 select_reduce_fusion
  60.8 57.7 %all_gather.6 = bf16[2,256,512]{2,1,0:T(8,128)(2,1)S(1)} all-gather(bf16[2,16,512]{2,1,0:T(8,128)(2,1)S(1)} %pad_maximum_fusion.3), channel_id=1, replica_groups=mesh['context'=16,'heads'=2] {'context'}, dimensions={1}, use_global_device_ids=true | all-gather | bytes 557056 | tf_op jit(solution)/shard_map/all_gather | solution.py:105
  121.2 3.6 maximum_select_fusion
  136.6 0.9 multiply_reduce_fusion
  138.0 1.9 fusion.277
  139.9 1.8 fusion.274
  141.7 1.9 fusion.271
  143.5 1.7 fusion.268
  145.3 1.9 fusion.265
  147.2 1.8 fusion.262
  149.0 1.9 fusion.259
  150.9 1.8 fusion.256
  152.9 2.1 exponential_reduce_fusion.7
  155.6 2.9 fusion.23
  158.5 1.2 convolution_dynamic-update-slice_fusion.7
  170.9 2.3 exponential_reduce_fusion
  173.9 2.4 fusion.9
  177.9 1.0 copy-done.8
  183.0 1.0 copy-done.6
  188.2 1.0 copy-done.4
  190.8 1.5 copy-done.15
  211.0 2.4 broadcast_select_fusion
  218.3 88.8 %collective-permute-done.3 = f32[2,1024,512]{1,2,0:T(8,128)} collective-permute-done((f32[2,1024,512]{1,2,0:T(8,128)}, f32[2,1024,512]{1,2,0:T(8,128)}, u32[]{:S(2)}, u32[]{:S(2)}) %collective-permute-start.3) | collective-permute-done | bytes 4194336 | tf_op jit(solution)/shard_map/ppermute | solution.py:16
  307.1 5.3 %select_add_fusion = f32[2,1024,512]{1,2,0:T(8,128)S(1)} fusion(f32[2,1024,512]{1,2,0:T(8,128)} %collective-permute-done.3, pred[]{:T(512)S(6)} %eq.246, f32[1,2048,512]{1,2,0:T(8,128)} %bitcast.155, f32[1,2048,512]{1,2,0:T(8,128)} %bitcast.157), kind=kLoop, calls=%fused_computation.5 | loop fusion | flops 4194304 | bytes 16777216 | tf_op jit(solution)/shard_map/add | solution.py:80
  312.4 2.1 slice_select_fusion
  316.1 1.0 pad_maximum_fusion.1
  317.1 2.3 copy.75
  319.5 2.3 fusion.48
  321.8 2.5 fusion.47
  324.3 1.0 fusion.46
  325.3 1.2 fusion.45
  326.5 0.9 fusion.44
  327.5 1.2 fusion.43
  328.7 37.6 %collective-permute-done.4 = f32[2,512,512]{1,2,0:T(8,128)} collective-permute-done((f32[2,512,512]{1,2,0:T(8,128)}, f32[2,512,512]{1,2,0:T(8,128)}, u32[]{:S(2)}, u32[]{:S(2)}) %collective-permute-start.4) | collective-permute-done | bytes 2097184 | tf_op jit(solution)/shard_map/ppermute | solution.py:16
  366.3 2.3 select_add_fusion.1
  368.7 1.1 slice_select_fusion.1
  370.7 0.9 fusion.42
  371.7 1.2 fusion.41
  372.9 39.2 %all-reduce.3.cloned.1.call-done = f32[2,256,512]{2,0,1:T(2,128)} async-done(((f32[2,256,512]{2,0,1:T(2,128)}), f32[2,256,512]{2,0,1:T(2,128)}) %all-reduce.3.cloned.1.call-update) | async-done | bytes 1048592
  412.1 1.1 dynamic-slice_reduce_fusion
  413.8 1.1 select_n.562
  414.8 1.2 copy.77
  416.6 1.1 add_convert_fusion
  419.0 2.1 select_add_fusion.2
  (396 shorter events, 72.1 us)
Async XLA Ops:
  7.2 38.3 %copy-start = (bf16[128,1024]{1,0:T(8,128)(2,1)S(1)}, bf16[128,1024]{1,0:T(8,128)(2,1)}, u32[]{:S(2)}) copy-start(bf16[128,1024]{1,0:T(8,128)(2,1)} %param.6) | copy-start | bytes 786436
  7.2 4.8 %copy-start.91 = (u32[32]{0:T(128)S(1)}, u32[32]{0:T(128)}, u32[]{:S(2)}) copy-start(u32[32]{0:T(128)} %constant.219) | copy-start | bytes 388
  7.2 3.7 copy-start.31
  7.2 6.0 %copy-start.90 = (s32[16]{0:T(128)S(1)}, s32[16]{0:T(128)}, u32[]{:S(2)}) copy-start(s32[16]{0:T(128)} %param.11) | copy-start | bytes 196
  7.2 38.2 %all-gather.2.cloned.1.call-start = ((), (), s32[]{:S(2)}) async-start(), calls=%async_computation.1 | async-start | bytes 3145728 | tf_op jit(solution)/shard_map/all_gather | solution.py:89
  9.1 8.4 %collective-permute-start = (bf16[2,256,512]{2,1,0:T(8,128)(2,1)S(1)}, bf16[2,256,512]{2,1,0:T(8,128)(2,1)}, u32[]{:S(2)}, u32[]{:S(2)}) collective-permute-start(bf16[2,256,512]{2,1,0:T(8,128)(2,1)S(1)} %pad_maximum_fusion.2), channel_id=1, source_target_pairs={{0,2},{2,0},{4,6},{6,4},{8,10},{10,8},{12,14},{14,12},{16,18},{18,... | collective-permute-start | bytes 1572872 | tf_op jit(solution)/shard_map/ppermute | solution.py:16
  19.1 33.0 %copy-start.34 = (bf16[2,512,512]{2,1,0:T(8,128)(2,1)}, bf16[2,512,512]{2,1,0:T(8,128)(2,1)S(1)}, u32[]{:S(2)}) copy-start(bf16[2,512,512]{2,1,0:T(8,128)(2,1)S(1)} %maximum_select_fusion.2) | copy-start | bytes 3145732
  19.2 33.0 %collective-permute-start.1 = (bf16[2,512,512]{2,1,0:T(8,128)(2,1)S(1)}, bf16[2,512,512]{2,1,0:T(8,128)(2,1)}, u32[]{:S(2)}, u32[]{:S(2)}) collective-permute-start(bf16[2,512,512]{2,1,0:T(8,128)(2,1)S(1)} %maximum_select_fusion.2), channel_id=1, source_target_pairs={{0,4},{2,6},{4,0},{6,2},{8,12},{10,14},{12,8},{14,10},{16,20},{18,... | collective-permute-start | bytes 3145736 | tf_op jit(solution)/shard_map/ppermute | solution.py:16
  27.5 31.0 %copy-start.55 = (pred[16,8]{1,0:T(8,128)(4,1)}, pred[16,8]{1,0:T(8,128)(4,1)S(1)}, u32[]{:S(2)}) copy-start(pred[16,8]{1,0:T(8,128)(4,1)S(1)} %iota_compare_fusion) | copy-start | bytes 388
  48.6 8.9 %all-to-all-start = ((bf16[128,2,512]{2,0,1:T(8,128)(2,1)}), bf16[128,2,512]{2,0,1:T(8,128)(2,1)S(1)}, u32[]{:S(2)}, u32[]{:S(2)}) async-start(bf16[128,2,512]{2,0,1:T(8,128)(2,1)} %bitcast.153), calls=%async_computation | async-start | bytes 524288 | tf_op jit(solution)/shard_map/all_to_all | solution.py:90
  52.1 360.0 %all-reduce.3.cloned.1.call-start = ((), (), s32[]{:S(2)}) async-start(), calls=%async_computation.2 | async-start | bytes 2097152
  54.9 66.3 %collective-permute-start.2 = (bf16[2,1024,512]{2,1,0:T(8,128)(2,1)S(1)}, bf16[2,1024,512]{2,1,0:T(8,128)(2,1)}, u32[]{:S(2)}, u32[]{:S(2)}) collective-permute-start(bf16[2,1024,512]{2,1,0:T(8,128)(2,1)S(1)} %maximum_select_fusion.1), channel_id=1, source_target_pairs={{0,8},{2,10},{4,12},{6,14},{8,0},{10,2},{12,4},{14,6},{16,24},{18,... | collective-permute-start | bytes 6291464 | tf_op jit(solution)/shard_map/ppermute | solution.py:16
  118.8 45.4 %copy-start.32 = (bf16[256,512]{1,0:T(8,128)(2,1)}, bf16[256,512]{1,0:T(8,128)(2,1)S(1)}, u32[]{:S(2)}) copy-start(bf16[256,512]{1,0:T(8,128)(2,1)S(1)} %get-tuple-element.221) | copy-start | bytes 786436
  121.2 38.6 %copy-start.38 = (f32[16,256]{1,0:T(8,128)}, f32[16,256]{1,0:T(8,128)S(1)}, u32[]{:S(2)}) copy-start(f32[16,256]{1,0:T(8,128)S(1)} %get-tuple-element.274) | copy-start | bytes 49156
  125.0 12.5 %copy-start.2 = (bf16[2048,512]{1,0:T(8,128)(2,1)}, bf16[2048,512]{1,0:T(8,128)(2,1)S(1)}, u32[]{:S(2)}) copy-start(bf16[2048,512]{1,0:T(8,128)(2,1)S(1)} %get-tuple-element.206) | copy-start | bytes 6291460
  126.3 33.5 %copy-start.58 = (f32[16]{0:T(128)}, f32[16]{0:T(128)S(1)}, u32[]{:S(2)}) copy-start(f32[16]{0:T(128)S(1)} %log_add_fusion.7) | copy-start | bytes 196
  127.3 34.2 %copy-start.60 = (f32[16]{0:T(128)}, f32[16]{0:T(128)S(1)}, u32[]{:S(2)}) copy-start(f32[16]{0:T(128)S(1)} %log_add_fusion.6) | copy-start | bytes 196
  128.9 34.3 %copy-start.62 = (f32[16]{0:T(128)}, f32[16]{0:T(128)S(1)}, u32[]{:S(2)}) copy-start(f32[16]{0:T(128)S(1)} %log_add_fusion.5) | copy-start | bytes 196
  130.4 34.5 %copy-start.64 = (f32[16]{0:T(128)}, f32[16]{0:T(128)S(1)}, u32[]{:S(2)}) copy-start(f32[16]{0:T(128)S(1)} %log_add_fusion.4) | copy-start | bytes 196
  132.0 34.4 %copy-start.66 = (f32[16]{0:T(128)}, f32[16]{0:T(128)S(1)}, u32[]{:S(2)}) copy-start(f32[16]{0:T(128)S(1)} %log_add_fusion.3) | copy-start | bytes 196
  133.5 34.4 %copy-start.68 = (f32[16]{0:T(128)}, f32[16]{0:T(128)S(1)}, u32[]{:S(2)}) copy-start(f32[16]{0:T(128)S(1)} %log_add_fusion.2) | copy-start | bytes 196
  135.1 34.3 %copy-start.72 = (f32[16]{0:T(128)}, f32[16]{0:T(128)S(1)}, u32[]{:S(2)}) copy-start(f32[16]{0:T(128)S(1)} %log_add_fusion.1) | copy-start | bytes 196
  136.6 33.6 %copy-start.70 = (f32[16]{0:T(128)}, f32[16]{0:T(128)S(1)}, u32[]{:S(2)}) copy-start(f32[16]{0:T(128)S(1)} %log_add_fusion) | copy-start | bytes 196
  148.9 3.7 copy-start.89
  158.5 4.7 %copy-start.87 = (pred[16]{0:T(512)(128)(4,1)S(1)}, pred[16]{0:T(512)(128)(4,1)}, u32[]{:S(2)}) copy-start(pred[16]{0:T(512)(128)(4,1)} %iota_compare_fusion.6) | copy-start | bytes 52
  158.5 6.5 %copy-start.86 = (pred[16]{0:T(512)(128)(4,1)S(1)}, pred[16]{0:T(512)(128)(4,1)}, u32[]{:S(2)}) copy-start(pred[16]{0:T(512)(128)(4,1)} %iota_compare_fusion.5) | copy-start | bytes 52
  158.5 8.0 %copy-start.85 = (pred[16]{0:T(512)(128)(4,1)S(1)}, pred[16]{0:T(512)(128)(4,1)}, u32[]{:S(2)}) copy-start(pred[16]{0:T(512)(128)(4,1)} %iota_compare_fusion.4) | copy-start | bytes 52
  158.5 9.5 %copy-start.84 = (pred[16]{0:T(512)(128)(4,1)S(1)}, pred[16]{0:T(512)(128)(4,1)}, u32[]{:S(2)}) copy-start(pred[16]{0:T(512)(128)(4,1)} %iota_compare_fusion.3) | copy-start | bytes 52
  158.5 11.0 %copy-start.83 = (pred[16]{0:T(512)(128)(4,1)S(1)}, pred[16]{0:T(512)(128)(4,1)}, u32[]{:S(2)}) copy-start(pred[16]{0:T(512)(128)(4,1)} %iota_compare_fusion.2) | copy-start | bytes 52
  158.5 11.7 %copy-start.82 = (pred[16]{0:T(512)(128)(4,1)S(1)}, pred[16]{0:T(512)(128)(4,1)}, u32[]{:S(2)}) copy-start(pred[16]{0:T(512)(128)(4,1)} %iota_compare_fusion.1) | copy-start | bytes 52
  159.8 16.5 %copy-start.40 = (bf16[16,256]{1,0:T(8,128)(2,1)}, bf16[16,256]{1,0:T(8,128)(2,1)S(1)}, u32[]{:S(2)}) copy-start(bf16[16,256]{1,0:T(8,128)(2,1)S(1)} %multiply_convert_fusion.7) | copy-start | bytes 24580
  160.7 15.6 %copy-start.42 = (bf16[16,256]{1,0:T(8,128)(2,1)}, bf16[16,256]{1,0:T(8,128)(2,1)S(1)}, u32[]{:S(2)}) copy-start(bf16[16,256]{1,0:T(8,128)(2,1)S(1)} %multiply_convert_fusion.6) | copy-start | bytes 24580
  162.5 13.9 %copy-start.44 = (bf16[16,256]{1,0:T(8,128)(2,1)}, bf16[16,256]{1,0:T(8,128)(2,1)S(1)}, u32[]{:S(2)}) copy-start(bf16[16,256]{1,0:T(8,128)(2,1)S(1)} %multiply_convert_fusion.5) | copy-start | bytes 24580
  164.1 12.2 %copy-start.46 = (bf16[16,256]{1,0:T(8,128)(2,1)}, bf16[16,256]{1,0:T(8,128)(2,1)S(1)}, u32[]{:S(2)}) copy-start(bf16[16,256]{1,0:T(8,128)(2,1)S(1)} %multiply_convert_fusion.4) | copy-start | bytes 24580
  196.4 14.3 %copy-start.16 = (f32[2048,512]{0,1:T(8,128)}, f32[2048,512]{0,1:T(8,128)S(1)}, u32[]{:S(2)}) copy-start(f32[2048,512]{0,1:T(8,128)S(1)} %convolution_dynamic-update-slice_fusion) | copy-start | bytes 12582916
  200.5 9.2 %copy-start.19 = (bf16[256,2048]{0,1:T(8,128)(2,1)}, bf16[256,2048]{0,1:T(8,128)(2,1)S(1)}, u32[]{:S(2)}) copy-start(bf16[256,2048]{0,1:T(8,128)(2,1)S(1)} %fusion.12) | copy-start | bytes 3145732
  201.8 7.4 %copy-start.21 = (bf16[256,2048]{0,1:T(8,128)(2,1)}, bf16[256,2048]{0,1:T(8,128)(2,1)S(1)}, u32[]{:S(2)}) copy-start(bf16[256,2048]{0,1:T(8,128)(2,1)S(1)} %fusion.14) | copy-start | bytes 3145732
  203.2 5.6 %copy-start.23 = (bf16[256,2048]{0,1:T(8,128)(2,1)}, bf16[256,2048]{0,1:T(8,128)(2,1)S(1)}, u32[]{:S(2)}) copy-start(bf16[256,2048]{0,1:T(8,128)(2,1)S(1)} %fusion.16) | copy-start | bytes 3145732
  204.5 3.8 copy-start.25
  210.8 4.0 copy-start.51
  210.8 3.9 copy-start.52
  210.8 3.9 copy-start.53
  210.8 3.9 copy-start.54
  210.9 4.1 copy-start.41
  210.9 4.3 %copy-start.43 = (bf16[16,256]{1,0:T(8,128)(2,1)S(1)}, bf16[16,256]{1,0:T(8,128)(2,1)}, u32[]{:S(2)}) copy-start(bf16[16,256]{1,0:T(8,128)(2,1)} %copy-done.42) | copy-start | bytes 24580
  210.9 4.6 %copy-start.45 = (bf16[16,256]{1,0:T(8,128)(2,1)S(1)}, bf16[16,256]{1,0:T(8,128)(2,1)}, u32[]{:S(2)}) copy-start(bf16[16,256]{1,0:T(8,128)(2,1)} %copy-done.44) | copy-start | bytes 24580
  210.9 4.8 %copy-start.47 = (bf16[16,256]{1,0:T(8,128)(2,1)S(1)}, bf16[16,256]{1,0:T(8,128)(2,1)}, u32[]{:S(2)}) copy-start(bf16[16,256]{1,0:T(8,128)(2,1)} %copy-done.46) | copy-start | bytes 24580
  210.9 5.7 %copy-start.39 = (f32[16,256]{1,0:T(8,128)S(1)}, f32[16,256]{1,0:T(8,128)}, u32[]{:S(2)}) copy-start(f32[16,256]{1,0:T(8,128)} %copy-done.38) | copy-start | bytes 49156
  210.9 5.7 %copy-start.59 = (f32[16]{0:T(128)S(1)}, f32[16]{0:T(128)}, u32[]{:S(2)}) copy-start(f32[16]{0:T(128)} %copy-done.58) | copy-start | bytes 196
  210.9 5.9 %copy-start.61 = (f32[16]{0:T(128)S(1)}, f32[16]{0:T(128)}, u32[]{:S(2)}) copy-start(f32[16]{0:T(128)} %copy-done.60) | copy-start | bytes 196
  210.9 6.2 %copy-start.63 = (f32[16]{0:T(128)S(1)}, f32[16]{0:T(128)}, u32[]{:S(2)}) copy-start(f32[16]{0:T(128)} %copy-done.62) | copy-start | bytes 196
  210.9 6.4 %copy-start.65 = (f32[16]{0:T(128)S(1)}, f32[16]{0:T(128)}, u32[]{:S(2)}) copy-start(f32[16]{0:T(128)} %copy-done.64) | copy-start | bytes 196
  210.9 6.7 %copy-start.67 = (f32[16]{0:T(128)S(1)}, f32[16]{0:T(128)}, u32[]{:S(2)}) copy-start(f32[16]{0:T(128)} %copy-done.66) | copy-start | bytes 196
  211.0 6.9 %copy-start.69 = (f32[16]{0:T(128)S(1)}, f32[16]{0:T(128)}, u32[]{:S(2)}) copy-start(f32[16]{0:T(128)} %copy-done.68) | copy-start | bytes 196
  211.0 7.1 %copy-start.73 = (f32[16]{0:T(128)S(1)}, f32[16]{0:T(128)}, u32[]{:S(2)}) copy-start(f32[16]{0:T(128)} %copy-done.72) | copy-start | bytes 196
  214.0 93.1 %collective-permute-start.3 = (f32[2,1024,512]{1,2,0:T(8,128)}, f32[2,1024,512]{1,2,0:T(8,128)}, u32[]{:S(2)}, u32[]{:S(2)}) collective-permute-start(f32[2,1024,512]{1,2,0:T(8,128)} %broadcast_select_fusion), channel_id=1, source_target_pairs={{0,8},{2,10},{4,12},{6,14},{8,0},{10,2},{12,4},{14,6},{16,24},{18,... | collective-permute-start | bytes 12582920 | tf_op jit(solution)/shard_map/ppermute | solution.py:16
  315.0 51.3 %collective-permute-start.4 = (f32[2,512,512]{1,2,0:T(8,128)}, f32[2,512,512]{1,2,0:T(8,128)}, u32[]{:S(2)}, u32[]{:S(2)}) collective-permute-start(f32[2,512,512]{1,2,0:T(8,128)} %slice_select_fusion), channel_id=1, source_target_pairs={{0,4},{2,6},{4,0},{6,2},{8,12},{10,14},{12,8},{14,10},{16,20},{18,... | collective-permute-start | bytes 6291464 | tf_op jit(solution)/shard_map/ppermute | solution.py:16
  319.5 4.9 %copy-start.28 = (bf16[256,2048]{0,1:T(8,128)(2,1)S(1)}, bf16[256,2048]{0,1:T(8,128)(2,1)}, u32[]{:S(2)}) copy-start(bf16[256,2048]{0,1:T(8,128)(2,1)} %copy-done.27) | copy-start | bytes 3145732
  319.5 5.8 %copy-start.26 = (bf16[256,2048]{0,1:T(8,128)(2,1)S(1)}, bf16[256,2048]{0,1:T(8,128)(2,1)}, u32[]{:S(2)}) copy-start(bf16[256,2048]{0,1:T(8,128)(2,1)} %copy-done.25) | copy-start | bytes 3145732
  321.8 4.7 %copy-start.24 = (bf16[256,2048]{0,1:T(8,128)(2,1)S(1)}, bf16[256,2048]{0,1:T(8,128)(2,1)}, u32[]{:S(2)}) copy-start(bf16[256,2048]{0,1:T(8,128)(2,1)} %copy-done.23) | copy-start | bytes 3145732
  325.3 41.0 %copy-start.14 = (f32[2,1024,512]{1,2,0:T(8,128)S(1)}, f32[2,1024,512]{1,2,0:T(8,128)}, u32[]{:S(2)}) copy-start(f32[2,1024,512]{1,2,0:T(8,128)} %copy-done.13) | copy-start | bytes 12582916
  369.8 43.5 %copy-start.56 = (pred[16,8]{1,0:T(8,128)(4,1)S(1)}, pred[16,8]{1,0:T(8,128)(4,1)}, u32[]{:S(2)}) copy-start(pred[16,8]{1,0:T(8,128)(4,1)} %copy-done.55) | copy-start | bytes 388
  369.8 49.2 %collective-permute-start.5 = (f32[2,256,512]{1,2,0:T(8,128)}, f32[2,256,512]{1,2,0:T(8,128)}, u32[]{:S(2)}, u32[]{:S(2)}) collective-permute-start(f32[2,256,512]{1,2,0:T(8,128)} %slice_select_fusion.1), channel_id=1, source_target_pairs={{0,2},{2,0},{4,6},{6,4},{8,10},{10,8},{12,14},{14,12},{16,18},{18,... | collective-permute-start | bytes 3145736 | tf_op jit(solution)/shard_map/ppermute | solution.py:16
  419.0 4.0 copy-start.1
  (37 other events, 79.4 us)
Sparse Core Ops, SparseCore 0:
  9.6 35.8 all-gather.1
  319.6 92.4 all-reduce.2
where the time goes:
time: 436 us; the launch traced here: 430 us
  waiting for transfers between devices  185 us (42%)
  other arithmetic  65.3 us (15%)
  matrix products  65.2 us (15%)
  blocking collectives  57.7 us (13%)
  local copies, waits for them, and re-layouts  31.3 us (7%)
  between operations  16.4 us (4%)
  starting transfers between devices  8.76 us (2%)
    ppermute x6, waiting for transfers between devices, partner_2(): return lax.ppermute(value, axis, pairs)  126 us
    all_gather x1, blocking collectives, body(): far_pair = lax.all_gather(picked_pair, 'context', axis=1, tiled=True)  57.7 us
    unnamed x3, waiting for transfers between devices  39.9 us
    dot_general x49, matrix products, dot_rows(): lax.dot_general(left, right, (((1,), (1,)), ((), ())), preferred_element_...  37.9 us
    all_gather x1, waiting for transfers between devices, body(): lax.all_gather(out_weight, 'heads', axis=0, tiled=True)  17.9 us
    unnamed x188, local copies, waits for them, and re-layouts  13.9 us
    dot_general x32, matrix products, dot_cols(): lax.dot_general(left, right, (((0,), (0,)), ((), ())), preferred_element_...  12.2 us
    dot_general x8, matrix products, step(): jnp.dot(dscores, near_keys, preferred_element_type=jnp.float32) * scale  11.4 us
  transfers between devices with their start and end apart: 9, of which 5 were waited for; matrix products, arithmetic and copies ran while one was open for 13% of the time, Pallas kernels for 0%

commit v1 on v0

v1 whole, which is shorter than its diff:
```python
import functools
import math

import jax
import jax.numpy as jnp
from jax import lax
from jax.experimental import pallas as pl
from jax.experimental.pallas import tpu as pltpu
from jax.sharding import PartitionSpec as P

HEAD_SIZE = 64
PAIR = 2 * HEAD_SIZE
DILATION_RATE = 16
FIRST_SEGMENT = 2048
SCALE = 1.0 / math.sqrt(HEAD_SIZE)
LOG2E = math.log2(math.e)
NEG = -1e30

SMEM = pl.BlockSpec(memory_space=pltpu.SMEM)
VMEM = pl.BlockSpec(memory_space=pltpu.VMEM)


def dot_nt(left, right):
    return lax.dot_general(
        left, right, (((1,), (1,)), ((), ())), preferred_element_type=jnp.float32
    )


def dot_nn(left, right):
    return jnp.dot(left, right, preferred_element_type=jnp.float32)


def head_columns(ref, head):
    return ref[:, head * HEAD_SIZE : (head + 1) * HEAD_SIZE]


def pick_matrix(offset, picked, rows):
    source = lax.broadcasted_iota(jnp.int32, (picked, rows), 1)
    index = lax.broadcasted_iota(jnp.int32, (picked, rows), 0)
    return (source == index * DILATION_RATE + offset).astype(jnp.bfloat16)


def pack_kernel(head_count, place_ref, offset_ref, key_ref, value_ref, near_ref, far_ref):
    group = near_ref.shape[0]
    rows = near_ref.shape[1]
    picked = far_ref.shape[1]
    for head in range(head_count):
        pair = jnp.concatenate([head_columns(key_ref, head), head_columns(value_ref, head)], 1)
        offset = offset_ref[place_ref[1] * head_count + head]
        picks = dot_nn(pick_matrix(offset, picked, rows), pair).astype(jnp.bfloat16)
        for place in range(head, group, head_count):
            near_ref[place] = pair
        for place in range(head, far_ref.shape[0], head_count):
            far_ref[place] = picks


def project_kernel(head_count, place_ref, weight_ref, query_ref, *refs):
    upstream_refs, pair_ref, grad_ref = refs[:-2], refs[-2], refs[-1]
    shards = len(upstream_refs)
    rows = upstream_refs[0].shape[0]
    for step, upstream_ref in enumerate(upstream_refs):
        owner = lax.rem(place_ref[1] + (shards - step), shards)
        start = pl.multiple_of(owner * rows, rows)
        grad_ref[pl.ds(start, rows), :] = dot_nt(upstream_ref[...], weight_ref[...]).astype(
            jnp.bfloat16
        )
    for head in range(head_count):
        pair = jnp.concatenate([head_columns(query_ref, head), head_columns(grad_ref, head)], 1)
        for place in range(head, pair_ref.shape[0], head_count):
            pair_ref[place] = pair


def attend_kernel(
    head_count, place_ref, offset_ref, kv_ref, qg_ref, far_ref, near_out, far_out,
    score_ref, dprob_ref, key_t_ref, acc_ref,
):
    group, rows, _ = kv_ref.shape
    far_rows = far_ref.shape[0]
    far_chunks = far_rows // rows
    chunks = group + far_chunks
    half = rows // 2
    offset = offset_ref[place_ref[1] * head_count + lax.rem(place_ref[0], head_count)]
    lane = lax.broadcasted_iota(jnp.int32, (rows, PAIR), 1)
    left = lane < HEAD_SIZE
    row_lane = lax.broadcasted_iota(jnp.int32, (1, rows), 1)
    picked = lax.rem(row_lane, DILATION_RATE) == offset

    def pair_chunk(chunk):
        if chunk < group:
            return kv_ref[chunk]
        return far_ref[(chunk - group) * rows : (chunk - group + 1) * rows, :]

    for chunk in range(chunks):
        key_t_ref[chunk] = pair_chunk(chunk).astype(jnp.float32).T[:HEAD_SIZE].astype(jnp.bfloat16)
    acc_ref[...] = jnp.zeros_like(acc_ref)

    def block(index, carry):
        both = qg_ref[index]
        query = jnp.where(left, both, jnp.zeros((), both.dtype))
        grad = jnp.where(left, jnp.zeros((), both.dtype), both)
        weights = jnp.concatenate([query, grad], 0)
        top = jnp.full((1, rows), NEG, jnp.float32)
        for chunk in range(chunks):
            score = dot_nt(pair_chunk(chunk), query)
            if chunk >= group:
                score = jnp.where(picked, score, NEG)
            score_ref[chunk] = score
            top = jnp.maximum(top, jnp.max(score, 0, keepdims=True))
        total = jnp.zeros((1, rows), jnp.float32)
        delta = jnp.zeros((1, rows), jnp.float32)
        for chunk in range(chunks):
            prob = jnp.exp2((score_ref[chunk] - top) * (SCALE * LOG2E))
            dprob = dot_nt(pair_chunk(chunk), grad)
            total = total + jnp.sum(prob, 0, keepdims=True)
            delta = delta + jnp.sum(prob * dprob, 0, keepdims=True)
            score_ref[chunk] = prob
            dprob_ref[chunk] = dprob
        inverse = 1.0 / total
        delta = delta * inverse
        query_grad = jnp.zeros((HEAD_SIZE, rows), jnp.float32)
        for chunk in range(chunks):
            prob = score_ref[chunk] * inverse
            dscore = (prob * (dprob_ref[chunk] - delta)).astype(jnp.bfloat16)
            prob16 = prob.astype(jnp.bfloat16)
            acc_ref[chunk] += dot_nn(jnp.concatenate([dscore, prob16], 1), weights)
            query_grad = query_grad + dot_nn(key_t_ref[chunk], dscore)
        query_grad = (query_grad * SCALE).T.astype(jnp.bfloat16)
        near_out[index, rows : rows + half, :] = jnp.concatenate(
            [query_grad[:half], query_grad[half:]], 1
        )
        return carry

    lax.fori_loop(0, group, block, 0)
    factor = jnp.where(left, SCALE, 1.0)
    for chunk in range(chunks):
        terms = acc_ref[chunk] * factor
        if chunk < group:
            near_out[chunk, :rows, :] = terms.astype(jnp.bfloat16)
        else:
            far_out[(chunk - group) * rows : (chunk - group + 1) * rows, :] = terms


def unpack_kernel(
    head_count, place_ref, offset_ref, near_ref, far_ref, query_out, key_out, value_out
):
    rows = query_out.shape[0]
    half = rows // 2
    group = near_ref.shape[0]
    picked = far_ref.shape[1]
    for head in range(head_count):
        offset = offset_ref[place_ref[1] * head_count + head]
        spread = pick_matrix(offset, picked, rows)
        far = far_ref[head]
        for other in range(head + group, far_ref.shape[0], group):
            far = far + far_ref[other]
        high = far.astype(jnp.bfloat16)
        low = (far - high.astype(jnp.float32)).astype(jnp.bfloat16)
        placed = lax.dot_general(
            jnp.concatenate([spread, spread], 0),
            jnp.concatenate([high, low], 0),
            (((0,), (0,)), ((), ())),
            preferred_element_type=jnp.float32,
        )
        pair = (near_ref[head, :rows, :].astype(jnp.float32) + placed).astype(jnp.bfloat16)
        columns = slice(head * HEAD_SIZE, (head + 1) * HEAD_SIZE)
        key_out[:, columns] = pair[:, :HEAD_SIZE]
        value_out[:, columns] = pair[:, HEAD_SIZE:]
        packed = near_ref[head, rows : rows + half, :]
        query_out[:half, columns] = packed[:, :HEAD_SIZE]
        query_out[half:, columns] = packed[:, HEAD_SIZE:]


def params():
    return pltpu.CompilerParams(vmem_limit_bytes=40 * 1024 * 1024)


def body(upstream, out_weight, query_rows, key_rows, value_rows, head_offsets):
    rows, width = query_rows.shape
    head_count = width // HEAD_SIZE
    devices = lax.axis_size("context")
    shards = lax.axis_size("heads")
    group = FIRST_SEGMENT // rows
    picked = rows // DILATION_RATE
    place = jnp.stack(
        [lax.rem(lax.axis_index("context"), group), lax.axis_index("heads")]
    ).astype(jnp.int32)
    groups = [list(range(first, first + group)) for first in range(0, devices, group)]

    def swap(value):
        return lax.all_to_all(value, "context", 0, 0, axis_index_groups=groups)

    upstreams = [upstream]
    for step in range(1, shards):
        pairs = [(source, (source + step) % shards) for source in range(shards)]
        upstreams.append(lax.ppermute(upstream, "heads", pairs))

    kv_send, far_send = pl.pallas_call(
        functools.partial(pack_kernel, head_count),
        out_shape=(
            jax.ShapeDtypeStruct((group, rows, PAIR), jnp.bfloat16),
            jax.ShapeDtypeStruct((devices, picked, PAIR), jnp.bfloat16),
        ),
        in_specs=[SMEM, SMEM, VMEM, VMEM],
        out_specs=(VMEM, VMEM),
        compiler_params=params(),
        name="pack_keys_values",
    )(place, head_offsets, key_rows, value_rows)
    kv = swap(kv_send)
    far = lax.all_to_all(far_send, "context", 0, 0)

    qg_send = pl.pallas_call(
        functools.partial(project_kernel, head_count),
        out_shape=jax.ShapeDtypeStruct((group, rows, PAIR), jnp.bfloat16),
        in_specs=[SMEM] + [VMEM] * (2 + shards),
        out_specs=VMEM,
        scratch_shapes=[pltpu.VMEM((rows, width), jnp.bfloat16)],
        compiler_params=params(),
        name="project_pack",
    )(place, out_weight, query_rows, *upstreams)
    qg = swap(qg_send)

    far_rows = devices * picked
    chunks = group + far_rows // rows
    near_send, far_back = pl.pallas_call(
        functools.partial(attend_kernel, head_count),
        out_shape=(
            jax.ShapeDtypeStruct((group, rows + rows // 2, PAIR), jnp.bfloat16),
            jax.ShapeDtypeStruct((far_rows, PAIR), jnp.float32),
        ),
        in_specs=[SMEM, SMEM, VMEM, VMEM, VMEM],
        out_specs=(VMEM, VMEM),
        scratch_shapes=[
            pltpu.VMEM((chunks, rows, rows), jnp.float32),
            pltpu.VMEM((chunks, rows, rows), jnp.float32),
            pltpu.VMEM((chunks, HEAD_SIZE, rows), jnp.bfloat16),
            pltpu.VMEM((chunks, rows, PAIR), jnp.float32),
        ],
        compiler_params=params(),
        name="attend",
    )(place, head_offsets, kv, qg, far.reshape(far_rows, PAIR))
    near = swap(near_send)
    far_terms = lax.all_to_all(far_back.reshape(devices, picked, PAIR), "context", 0, 0)

    shape = jax.ShapeDtypeStruct((rows, width), jnp.bfloat16)
    return pl.pallas_call(
        functools.partial(unpack_kernel, head_count),
        out_shape=(shape, shape, shape),
        in_specs=[SMEM, SMEM, VMEM, VMEM],
        out_specs=(VMEM, VMEM, VMEM),
        compiler_params=params(),
        name="unpack",
    )(place, head_offsets, near, far_terms)


def solution(mesh):
    return jax.shard_map(
        body,
        mesh=mesh,
        in_specs=(
            P(("context", "heads"), None),
            P("heads", None),
            P("context", "heads"),
            P("context", "heads"),
            P("context", "heads"),
            P(),
        ),
        out_specs=(P("context", "heads"), P("context", "heads"), P("context", "heads")),
        check_vma=False,
    )
```

time: 436 us -> 94.1 us (0.22); the launches traced: 430 us -> 93.7 us
  waiting for transfers between devices: 185 us -> 7.05 us
  other arithmetic: 65.3 us -> 0.08 us
  matrix products: 65.2 us -> 0 us
  local copies, waits for them, and re-layouts: 31.3 us -> 3.29 us
  Pallas kernels: 0 us -> 26 us
  between operations: 16.4 us -> 0.69 us
  blocking collectives: 57.7 us -> 51.4 us
    ppermute x6 -> x1, waiting for transfers between devices: 126 us -> 7.05 us  [body(): upstreams.append(lax.ppermute(upstream, 'heads', pairs))]
    dot_general x97 -> x0, matrix products: 65.2 us -> none  [the longest x49 37.9 us: dot_rows(): lax.dot_general(left, right, (((1,), (1,)), ((), ())), preferred_element_...]
    all_gather x1 -> x0, blocking collectives: 57.7 us -> none  [body(): far_pair = lax.all_gather(picked_pair, 'context', axis=1, tiled=True)]
    all_to_all x0 -> x4, blocking collectives: none -> 51.4 us  [the longest x2 26.7 us: swap(): return lax.all_to_all(value, 'context', 0, 0, axis_index_groups=groups)]
    unnamed x3 -> x0, waiting for transfers between devices: 39.9 us -> none
    pallas_call x0 -> x4, Pallas kernels: none -> 26 us  [the longest x1 20.9 us: body(): pl.pallas_call(functools.partial(attend_kernel, head_count), out_shape=(j...]
    select_n x31 -> x0, other arithmetic: 24.6 us -> none  [the longest x3 7.98 us: double_up(): jnp.where(lower, jnp.concatenate([buffer, partner], 1), jnp.concatenate([...]
    all_gather x1 -> x0, waiting for transfers between devices: 17.9 us -> none  [body(): lax.all_gather(out_weight, 'heads', axis=0, tiled=True)]
  transfers between devices with their start and end apart: 9 -> 2, of which waited for: 5 -> 1; matrix products, arithmetic and copies ran while one was open for 13% -> 0% of each run, Pallas kernels for 0% -> 2%
where the time goes in v1:
time: 94.1 us; the launch traced here: 93.7 us
  blocking collectives  51.4 us (55%)
  Pallas kernels  26 us (28%)
  waiting for transfers between devices  7.05 us (7%)
  starting transfers between devices  5.18 us (6%)
  local copies, waits for them, and re-layouts  3.29 us (3%)
    all_to_all x2, blocking collectives, swap(): return lax.all_to_all(value, 'context', 0, 0, axis_index_groups=groups)  26.7 us
    pallas_call x1, Pallas kernels, body(): pl.pallas_call(functools.partial(attend_kernel, head_count), out_shape=(j...  20.9 us
    all_to_all x1, blocking collectives, body(): far = lax.all_to_all(far_send, 'context', 0, 0)  14.1 us
    all_to_all x1, blocking collectives, body(): lax.all_to_all(far_back.reshape(devices, picked, PAIR), 'context', 0, 0)  10.6 us
    ppermute x1, waiting for transfers between devices, body(): upstreams.append(lax.ppermute(upstream, 'heads', pairs))  7.05 us
    all_to_all x1, starting transfers between devices, swap(): return lax.all_to_all(value, 'context', 0, 0, axis_index_groups=groups)  3.62 us
    unnamed x14, local copies, waits for them, and re-layouts  3.29 us
    pallas_call x1, Pallas kernels, body(): pl.pallas_call(functools.partial(unpack_kernel, head_count), out_shape=(s...  2.08 us
  transfers between devices with their start and end apart: 2, of which 1 were waited for; matrix products, arithmetic and copies ran while one was open for 0% of the time, Pallas kernels for 2%

profile of v1, /device:TPU:0, one launch (start us, length us, event | category | flops | bytes accessed | tf_op | source)
XLA Modules:
  0.0 93.7 jit_solution(16611814382904694145)
XLA Ops:
  0.6 0.0 copy-start
  0.6 0.1 pad_add_fusion.place_ref
  0.7 0.0 copy-start.3
  0.7 1.0 %copy-done.3 = bf16[256,512]{1,0:T(8,128)(2,1)S(1)} copy-done((bf16[256,512]{1,0:T(8,128)(2,1)S(1)}, bf16[256,512]{1,0:T(8,128)(2,1)}, u32[]{:S(2)}) %copy-start.3) | copy-done | bytes 262168
  1.7 0.0 copy-start.4
  1.7 0.9 %copy-done.4 = bf16[256,512]{1,0:T(8,128)(2,1)S(1)} copy-done((bf16[256,512]{1,0:T(8,128)(2,1)S(1)}, bf16[256,512]{1,0:T(8,128)(2,1)}, u32[]{:S(2)}) %copy-start.4) | copy-done | bytes 262168
  2.7 0.0 copy-start.5
  2.7 0.7 copy-done.5
  3.4 1.5 %pack_keys_values.1 = (bf16[8,256,128]{2,1,0:T(8,128)(2,1)}, bf16[16,16,128]{2,1,0:T(8,128)(2,1)S(1)}) custom-call(s32[2]{0:T(128)S(1)} %pad_add_fusion.place_ref, s32[16]{0:T(128)S(1)} %copy-done.5, bf16[256,512]{1,0:T(8,128)(2,1)S(1)} %copy-done.3, bf16[256,512]{1,0:T(8,128)(2,1)S(1)} %copy-done.4), custom_call_target="tpu_custom_call" | custom-call | tf_op jit(solution)/shard_map/pack_keys_values/pallas_call | solution.py:197
  4.9 14.1 %all_to_all.25 = bf16[16,16,128]{2,1,0:T(8,128)(2,1)S(1)} all-to-all(bf16[16,16,128]{2,1,0:T(8,128)(2,1)S(1)} %get-tuple-element.8), channel_id=1, replica_groups=mesh['context'=16,'heads'=2] {'context'}, dimensions={0} | all-to-all | bytes 131072 | tf_op jit(solution)/shard_map/all_to_all | solution.py:209
  19.0 0.0 copy-start.2
  19.0 0.0 copy-start.1
  19.0 3.6 %all-to-all-start = ((bf16[8,256,128]{2,1,0:T(8,128)(2,1)}), bf16[8,256,128]{2,1,0:T(8,128)(2,1)S(1)}, u32[]{:S(2)}, u32[]{:S(2)}) async-start(bf16[8,256,128]{2,1,0:T(8,128)(2,1)} %get-tuple-element.7), calls=%async_computation | async-start | bytes 1048576 | tf_op jit(solution)/shard_map/all_to_all | solution.py:190
  22.6 0.0 copy-done.2
  22.6 1.6 %collective-permute-start = (bf16[128,1024]{1,0:T(8,128)(2,1)S(1)}, bf16[128,1024]{1,0:T(8,128)(2,1)S(1)}, u32[]{:S(2)}, u32[]{:S(2)}) collective-permute-start(bf16[128,1024]{1,0:T(8,128)(2,1)S(1)} %copy-done.2), channel_id=1, source_target_pairs={{0,1},{1,0},{2,3},{3,2},{4,5},{5,4},{6,7},{7,6},{8,9},{9,8},{10,11... | collective-permute-start | bytes 786440 | tf_op jit(solution)/shard_map/ppermute | solution.py:195
  24.2 7.1 %collective-permute-done.refs_1_ = bf16[128,1024]{1,0:T(8,128)(2,1)S(1)} collective-permute-done((bf16[128,1024]{1,0:T(8,128)(2,1)S(1)}, bf16[128,1024]{1,0:T(8,128)(2,1)S(1)}, u32[]{:S(2)}, u32[]{:S(2)}) %collective-permute-start) | collective-permute-done | bytes 262176 | tf_op jit(solution)/shard_map/ppermute | solution.py:195
  31.2 0.0 copy-done
  31.2 0.0 copy-done.1
  31.2 1.5 %project_pack.1 = bf16[8,256,128]{2,1,0:T(8,128)(2,1)S(1)} custom-call(s32[2]{0:T(128)S(1)} %pad_add_fusion.place_ref, bf16[512,1024]{1,0:T(8,128)(2,1)S(1)} %copy-done, bf16[256,512]{1,0:T(8,128)(2,1)S(1)} %copy-done.1, bf16[128,1024]{1,0:T(8,128)(2,1)S(1)} %copy-done.2, bf16[128,1024]{1,0:T(8,128)(2,1)S(1)} %collective-permute-done.refs_1_), custom_call_target="tpu_custom_call" | custom-call | tf_op jit(solution)/shard_map/project_pack/pallas_call | solution.py:211
  32.7 0.0 all-to-all-done.kv_ref
  32.7 12.6 %all_to_all.26.qg_ref = bf16[8,256,128]{2,1,0:T(8,128)(2,1)S(1)} all-to-all(bf16[8,256,128]{2,1,0:T(8,128)(2,1)S(1)} %project_pack.1), channel_id=1, replica_groups={{0,2,4,6,8,10,12,14},{16,18,20,22,24,26,28,30},{1,3,5,7,9,11,13,15},{17..., dimensions={0} | all-to-all | bytes 1048576 | tf_op jit(solution)/shard_map/all_to_all | solution.py:190
  45.3 0.0 copy-start.6
  45.3 0.7 copy-done.6
  46.0 20.9 %attend.1 = (bf16[8,384,128]{2,1,0:T(8,128)(2,1)S(1)}, f32[256,128]{1,0:T(8,128)S(1)}) custom-call(s32[2]{0:T(128)S(1)} %pad_add_fusion.place_ref, s32[16]{0:T(128)S(1)} %copy-done.6, bf16[8,256,128]{2,1,0:T(8,128)(2,1)S(1)} %all-to-all-done.kv_ref, bf16[8,256,128]{2,1,0:T(8,128)(2,1)S(1)} %all_to_all.26.qg_ref, bf16[256,128]{1,0:T(8,128)(2,1)S(1)} %bitcast.4), custom_call_target="tpu_custom_call" | custom-call | tf_op jit(solution)/shard_map/attend/pallas_call | solution.py:224
  66.9 10.6 %all_to_all.27.far_ref = f32[16,16,128]{2,1,0:T(8,128)S(1)} all-to-all(f32[16,16,128]{2,1,0:T(8,128)S(1)} %bitcast.5), channel_id=1, replica_groups=mesh['context'=16,'heads'=2] {'context'}, dimensions={0} | all-to-all | bytes 262144 | tf_op jit(solution)/shard_map/all_to_all | solution.py:242
  77.5 14.1 %all_to_all.28.near_ref = bf16[8,384,128]{2,1,0:T(8,128)(2,1)S(1)} all-to-all(bf16[8,384,128]{2,1,0:T(8,128)(2,1)S(1)} %get-tuple-element.9), channel_id=1, replica_groups={{0,2,4,6,8,10,12,14},{16,18,20,22,24,26,28,30},{1,3,5,7,9,11,13,15},{17..., dimensions={0} | all-to-all | bytes 1572864 | tf_op jit(solution)/shard_map/all_to_all | solution.py:190
  91.6 2.1 %unpack.1 = (bf16[256,512]{1,0:T(8,128)(2,1)}, bf16[256,512]{1,0:T(8,128)(2,1)}, bf16[256,512]{1,0:T(8,128)(2,1)}) custom-call(s32[2]{0:T(128)S(1)} %pad_add_fusion.place_ref, s32[16]{0:T(128)S(1)} %copy-done.6, bf16[8,384,128]{2,1,0:T(8,128)(2,1)S(1)} %all_to_all.28.near_ref, f32[16,16,128]{2,1,0:T(8,128)S(1)} %all_to_all.27.far_ref), custom_call_target="tpu_custom_call" | custom-call | tf_op jit(solution)/shard_map/unpack/pallas_call | solution.py:245
Async XLA Ops:
  0.6 30.6 %copy-start = (bf16[512,1024]{1,0:T(8,128)(2,1)S(1)}, bf16[512,1024]{1,0:T(8,128)(2,1)}, u32[]{:S(2)}) copy-start(bf16[512,1024]{1,0:T(8,128)(2,1)} %weight_ref.1) | copy-start | bytes 3145732
  0.7 1.0 %copy-start.3 = (bf16[256,512]{1,0:T(8,128)(2,1)S(1)}, bf16[256,512]{1,0:T(8,128)(2,1)}, u32[]{:S(2)}) copy-start(bf16[256,512]{1,0:T(8,128)(2,1)} %key_ref.1) | copy-start | bytes 786436
  1.7 0.9 %copy-start.4 = (bf16[256,512]{1,0:T(8,128)(2,1)S(1)}, bf16[256,512]{1,0:T(8,128)(2,1)}, u32[]{:S(2)}) copy-start(bf16[256,512]{1,0:T(8,128)(2,1)} %value_ref.1) | copy-start | bytes 786436
  2.7 0.7 copy-start.5
  19.0 3.6 %copy-start.2 = (bf16[128,1024]{1,0:T(8,128)(2,1)S(1)}, bf16[128,1024]{1,0:T(8,128)(2,1)}, u32[]{:S(2)}) copy-start(bf16[128,1024]{1,0:T(8,128)(2,1)} %refs_0_.1) | copy-start | bytes 786436
  19.0 12.3 %copy-start.1 = (bf16[256,512]{1,0:T(8,128)(2,1)S(1)}, bf16[256,512]{1,0:T(8,128)(2,1)}, u32[]{:S(2)}) copy-start(bf16[256,512]{1,0:T(8,128)(2,1)} %query_ref.1) | copy-start | bytes 786436
  19.0 13.8 %all-to-all-start = ((bf16[8,256,128]{2,1,0:T(8,128)(2,1)}), bf16[8,256,128]{2,1,0:T(8,128)(2,1)S(1)}, u32[]{:S(2)}, u32[]{:S(2)}) async-start(bf16[8,256,128]{2,1,0:T(8,128)(2,1)} %get-tuple-element.7), calls=%async_computation | async-start | bytes 1048576 | tf_op jit(solution)/shard_map/all_to_all | solution.py:190
  22.6 8.6 %collective-permute-start = (bf16[128,1024]{1,0:T(8,128)(2,1)S(1)}, bf16[128,1024]{1,0:T(8,128)(2,1)S(1)}, u32[]{:S(2)}, u32[]{:S(2)}) collective-permute-start(bf16[128,1024]{1,0:T(8,128)(2,1)S(1)} %copy-done.2), channel_id=1, source_target_pairs={{0,1},{1,0},{2,3},{3,2},{4,5},{5,4},{6,7},{7,6},{8,9},{9,8},{10,11... | collective-permute-start | bytes 786440 | tf_op jit(solution)/shard_map/ppermute | solution.py:195
  45.3 0.7 copy-start.6

commit v2 on v1

v2 whole, which is shorter than its diff:
```python
import functools
import math

import jax
import jax.numpy as jnp
from jax import lax
from jax.experimental import pallas as pl
from jax.experimental.pallas import tpu as pltpu
from jax.sharding import PartitionSpec as P

HEAD_SIZE = 64
PAIR = 2 * HEAD_SIZE
DILATION_RATE = 16
FIRST_SEGMENT = 2048
SCALE = 1.0 / math.sqrt(HEAD_SIZE)
LOG2E = math.log2(math.e)
SCORE_FACTOR = SCALE * LOG2E
STRIP = 64
STAT_ROWS = 16

SMEM = pl.BlockSpec(memory_space=pltpu.SMEM)
VMEM = pl.BlockSpec(memory_space=pltpu.VMEM)


def dot_nt(left, right):
    return lax.dot_general(
        left, right, (((1,), (1,)), ((), ())), preferred_element_type=jnp.float32
    )


def dot_nn(left, right):
    return jnp.dot(left, right, preferred_element_type=jnp.float32)


def head_columns(ref, head):
    return ref[:, head * HEAD_SIZE : (head + 1) * HEAD_SIZE]


def pick_matrix(offset, picked, rows):
    source = lax.broadcasted_iota(jnp.int32, (picked, rows), 1)
    index = lax.broadcasted_iota(jnp.int32, (picked, rows), 0)
    return (source == index * DILATION_RATE + offset).astype(jnp.bfloat16)


def spread_matrix(offset, first, picked, rows, axis):
    shape = (picked, rows) if axis == 0 else (rows, picked)
    index = lax.broadcasted_iota(jnp.int32, shape, axis)
    source = lax.broadcasted_iota(jnp.int32, shape, 1 - axis)
    return (source == (index - first) * DILATION_RATE + offset).astype(jnp.bfloat16)


def split_two(value):
    high = value.astype(jnp.bfloat16)
    low = (value - high.astype(jnp.float32)).astype(jnp.bfloat16)
    return high, low


def split_three(value):
    high = value.astype(jnp.bfloat16)
    rest = value - high.astype(jnp.float32)
    middle = rest.astype(jnp.bfloat16)
    low = (rest - middle.astype(jnp.float32)).astype(jnp.bfloat16)
    return high, middle, low


def fold(value, combine):
    parts = [value[start : start + 8] for start in range(0, value.shape[0], 8)]
    while len(parts) > 1:
        merged = [combine(parts[i], parts[i + 1]) for i in range(0, len(parts) - 1, 2)]
        parts = merged + parts[len(merged) * 2 :]
    return parts[0]


def left_half(shape):
    return lax.broadcasted_iota(jnp.int32, shape, 1) < HEAD_SIZE


def halves(both):
    left = left_half(both.shape)
    zero = jnp.zeros((), both.dtype)
    return jnp.where(left, both, zero), jnp.where(left, zero, both)


def send_pairs(head_count, place, stage_ref, out_refs):
    for step, out_ref in enumerate(out_refs):
        target = lax.rem(lax.bitwise_xor(place, step), head_count)
        out_ref[: stage_ref.shape[1], :] = stage_ref[target]


def pack_kernel(head_count, group, place_ref, offset_ref, key_ref, value_ref, *refs):
    pair_refs, far_ref, stage_ref = refs[:group], refs[group], refs[group + 1]
    rows = key_ref.shape[0]
    picked = far_ref.shape[1]
    for head in range(head_count):
        pair = jnp.concatenate([head_columns(key_ref, head), head_columns(value_ref, head)], 1)
        offset = offset_ref[place_ref[1] * head_count + head]
        picks = dot_nn(pick_matrix(offset, picked, rows), pair).astype(jnp.bfloat16)
        stage_ref[head] = pair
        far_ref[head] = picks
    send_pairs(head_count, place_ref[0], stage_ref, pair_refs)


def project_kernel(head_count, group, shards, others, place_ref, weight_ref, query_ref, *refs):
    upstream_refs, refs = refs[:shards], refs[shards:]
    far_refs, refs = refs[:others], refs[others:]
    pair_refs, grad_ref, stage_ref = refs[:group], refs[group], refs[group + 1]
    shard_rows = upstream_refs[0].shape[0]
    rows = query_ref.shape[0]
    for step, upstream_ref in enumerate(upstream_refs):
        owner = lax.rem(place_ref[1] + (shards - step), shards)
        start = pl.multiple_of(owner * shard_rows, shard_rows)
        grad_ref[pl.ds(start, shard_rows), :] = dot_nt(
            upstream_ref[...], weight_ref[...]
        ).astype(jnp.bfloat16)
    for head in range(head_count):
        stage_ref[head, :rows, :] = jnp.concatenate(
            [head_columns(query_ref, head), head_columns(grad_ref, head)], 1
        )
        for other, far_ref in enumerate(far_refs):
            picked = far_ref.shape[1]
            first = rows + other * picked
            stage_ref[head, first : first + picked, :] = far_ref[head]
    send_pairs(head_count, place_ref[0], stage_ref, pair_refs)


def own_offset(head_count, place_ref, offset_ref):
    return offset_ref[place_ref[1] * head_count + lax.rem(place_ref[0], head_count)]


def far_kernel(head_count, group, others, place_ref, offset_ref, *refs):
    kv_refs, refs = refs[:group], refs[group:]
    qg_refs, refs = refs[:group], refs[group:]
    keys_out, key_t_out, extra_out, own_out, other_out, keys_ref, picked_ref = refs
    rows = kv_refs[0].shape[0]
    near = group * rows
    picked = rows // DILATION_RATE
    count = group * picked
    far = count * (1 + others)
    offset = own_offset(head_count, place_ref, offset_ref)
    pick = pick_matrix(offset, picked, rows)
    for step in range(group):
        pair = kv_refs[step][...]
        keys_ref[step * rows : (step + 1) * rows, :] = pair
        keys_out[step * rows : (step + 1) * rows, :] = pair
        first = near + step * picked
        keys_ref[first : first + picked, :] = dot_nn(pick, pair).astype(jnp.bfloat16)
        for other in range(others):
            first = near + (1 + other) * count + step * picked
            source = rows + other * picked
            keys_ref[first : first + picked, :] = qg_refs[step][source : source + picked, :]
        picked_ref[step * picked : (step + 1) * picked, :] = dot_nn(
            pick, qg_refs[step][:rows, :]
        ).astype(jnp.bfloat16)
    key_t = keys_ref[...].astype(jnp.float32).T[:HEAD_SIZE].astype(jnp.bfloat16)
    key_t_out[...] = key_t[:, :near]
    query, grad = halves(picked_ref[...])
    score = dot_nt(keys_ref[...], query)
    dprob = dot_nt(keys_ref[...], grad)
    top = jnp.max(score, 0, keepdims=True)
    prob = jnp.exp2((score - top) * SCORE_FACTOR)
    total = jnp.sum(prob, 0, keepdims=True)
    inverse = 1.0 / total
    delta = jnp.sum(prob * dprob, 0, keepdims=True) * inverse
    prob_far = prob[near:] * inverse
    dscore = (prob_far * (dprob[near:] - delta)).astype(jnp.bfloat16)
    terms = dot_nn(
        jnp.concatenate([dscore, prob_far.astype(jnp.bfloat16)], 1),
        jnp.concatenate([query, grad], 0),
    ) * jnp.where(left_half((far, PAIR)), SCALE, 1.0)
    own_out[...] = terms[:count]
    other_out[...] = terms[count:]
    query_grad = dot_nn(key_t[:, near:], dscore)
    lse = top * SCORE_FACTOR + jnp.log2(total)
    extra_out[:PAIR, :] = jnp.concatenate(split_two(query_grad), 0)
    blank = jnp.zeros((STAT_ROWS - 6, count), jnp.bfloat16)
    extra_out[PAIR:, :] = jnp.concatenate([*split_three(lse), *split_three(delta), blank], 0)


def near_block(
    first, offset, keys_ref, key_t_ref, qg_ref, extra_ref, score_ref, dprob_ref, work_ref, acc_ref
):
    near = keys_ref.shape[0]
    rows = score_ref.shape[1]
    count = extra_ref.shape[1]
    query, grad = halves(qg_ref[:rows, :])
    score_ref[...] = dot_nt(keys_ref[...], query)
    dprob_ref[...] = dot_nt(keys_ref[...], grad)
    extra = dot_nn(extra_ref[...], spread_matrix(offset, first, count, rows, 0))
    row_lane = lax.broadcasted_iota(jnp.int32, (1, rows), 1)
    picked = lax.rem(row_lane, DILATION_RATE) == offset
    lse_picked = extra[PAIR : PAIR + 1] + extra[PAIR + 1 : PAIR + 2] + extra[PAIR + 2 : PAIR + 3]
    delta_picked = (
        extra[PAIR + 3 : PAIR + 4] + extra[PAIR + 4 : PAIR + 5] + extra[PAIR + 5 : PAIR + 6]
    )
    strips = [slice(start, start + STRIP) for start in range(0, near, STRIP)]
    top = None
    for strip in strips:
        part = fold(score_ref[strip, :], jnp.maximum)
        top = part if top is None else jnp.maximum(top, part)
    top = jnp.max(top, 0, keepdims=True) * SCORE_FACTOR
    top = jnp.where(picked, lse_picked, top)
    total = jnp.zeros((8, rows), jnp.float32)
    delta = jnp.zeros((8, rows), jnp.float32)
    for strip in strips:
        prob = jnp.exp2(score_ref[strip, :] * SCORE_FACTOR - top)
        total = total + fold(prob, jnp.add)
        delta = delta + fold(prob * dprob_ref[strip, :], jnp.add)
        score_ref[strip, :] = prob
    inverse = jnp.where(picked, 1.0, 1.0 / jnp.sum(total, 0, keepdims=True))
    delta = jnp.where(picked, delta_picked, jnp.sum(delta, 0, keepdims=True) * inverse)
    for strip in strips:
        prob = score_ref[strip, :] * inverse
        work_ref[strip, :rows] = (prob * (dprob_ref[strip, :] - delta)).astype(jnp.bfloat16)
        work_ref[strip, rows:] = prob.astype(jnp.bfloat16)
    acc_ref[...] += dot_nn(work_ref[...], jnp.concatenate([query, grad], 0))
    query_grad = dot_nn(key_t_ref[...], work_ref[:, :rows])
    query_grad = query_grad + extra[:HEAD_SIZE] + extra[HEAD_SIZE:PAIR]
    query_grad = (query_grad * SCALE).T.astype(jnp.bfloat16)
    half = rows // 2
    return jnp.concatenate([query_grad[:half], query_grad[half:]], 1)


def first_kernel(head_count, steps, place_ref, offset_ref, keys_ref, key_t_ref, extra_ref, *refs):
    qg_refs, refs = refs[:steps], refs[steps:]
    acc_ref, query_out, *scratch = refs
    offset = own_offset(head_count, place_ref, offset_ref)
    picked = extra_ref.shape[1] // (keys_ref.shape[0] // scratch[0].shape[2])
    acc_ref[...] = jnp.zeros_like(acc_ref)
    for step, qg_ref in enumerate(qg_refs):
        query_out[step] = near_block(
            step * picked, offset, keys_ref, key_t_ref, qg_ref, extra_ref,
            *[ref.at[step % 2] for ref in scratch], acc_ref,
        )


def second_kernel(
    head_count, steps, others, place_ref, offset_ref, keys_ref, key_t_ref, extra_ref, start_ref,
    query_ref, own_ref, *refs,
):
    back_refs, refs = refs[:others], refs[others:]
    qg_refs, refs = refs[:steps], refs[steps:]
    rows = query_ref.shape[1] * 2
    group = keys_ref.shape[0] // rows
    out_refs, refs = refs[:group], refs[group:]
    acc_ref, *scratch = refs
    count = extra_ref.shape[1]
    picked = count // group
    offset = own_offset(head_count, place_ref, offset_ref)
    acc_ref[...] = start_ref[...]
    for step, qg_ref in enumerate(qg_refs):
        place = group - steps + step
        out_refs[place][rows:, :] = near_block(
            place * picked, offset, keys_ref, key_t_ref, qg_ref, extra_ref,
            *[ref.at[step % 2] for ref in scratch], acc_ref,
        )
    terms = own_ref[...]
    for back_ref in back_refs:
        terms = terms + back_ref[...]
    terms = jnp.concatenate(split_two(terms), 0)
    factor = jnp.where(left_half((rows, PAIR)), SCALE, 1.0)
    for place in range(group):
        spread = spread_matrix(offset, place * picked, count, rows, 1)
        placed = dot_nn(jnp.concatenate([spread, spread], 1), terms)
        summed = acc_ref[place * rows : (place + 1) * rows, :] * factor + placed
        out_refs[place][:rows, :] = summed.astype(jnp.bfloat16)
        if place < group - steps:
            out_refs[place][rows:, :] = query_ref[place]


def unpack_kernel(head_count, group, place_ref, *refs):
    near_refs, refs = refs[:group], refs[group:]
    query_out, key_out, value_out, stage_ref = refs
    rows = query_out.shape[0]
    half = rows // 2
    for step, near_ref in enumerate(near_refs):
        stage_ref[lax.bitwise_xor(place_ref[0], step)] = near_ref[...]
    for head in range(head_count):
        columns = slice(head * HEAD_SIZE, (head + 1) * HEAD_SIZE)
        key_out[:, columns] = stage_ref[head, :rows, :HEAD_SIZE]
        value_out[:, columns] = stage_ref[head, :rows, HEAD_SIZE:]
        query_out[:half, columns] = stage_ref[head, rows:, :HEAD_SIZE]
        query_out[half:, columns] = stage_ref[head, rows:, HEAD_SIZE:]


def call(kernel, name, out_shape, operands, scalars, scratch=(), flops=0):
    return pl.pallas_call(
        kernel,
        out_shape=tuple(jax.ShapeDtypeStruct(*shape) for shape in out_shape),
        in_specs=[SMEM] * scalars + [VMEM] * (len(operands) - scalars),
        out_specs=tuple(VMEM for _ in out_shape),
        scratch_shapes=[pltpu.VMEM(*shape) for shape in scratch],
        compiler_params=pltpu.CompilerParams(vmem_limit_bytes=40 * 1024 * 1024),
        cost_estimate=pl.CostEstimate(flops=flops, bytes_accessed=2**21, transcendentals=0),
        name=name,
    )(*operands)


def body(upstream, out_weight, query_rows, key_rows, value_rows, head_offsets):
    rows, width = query_rows.shape
    head_count = width // HEAD_SIZE
    devices = lax.axis_size("context")
    shards = lax.axis_size("heads")
    group = FIRST_SEGMENT // rows
    others = devices // group - 1
    picked = rows // DILATION_RATE
    count = group * picked
    near = group * rows
    place = jnp.stack(
        [lax.rem(lax.axis_index("context"), group), lax.axis_index("heads")]
    ).astype(jnp.int32)

    def swap(values):
        pairs = [[(source, source ^ step) for source in range(devices)] for step in range(group)]
        return [values[0]] + [
            lax.ppermute(values[step], "context", pairs[step]) for step in range(1, group)
        ]

    def segment_shift(value, shift):
        pairs = [(source, (source + shift * group) % devices) for source in range(devices)]
        return lax.ppermute(value, "context", pairs)

    upstreams = [upstream]
    for step in range(1, shards):
        pairs = [(source, (source + step) % shards) for source in range(shards)]
        upstreams.append(lax.ppermute(upstream, "heads", pairs))

    bf16, f32 = jnp.bfloat16, jnp.float32
    *kv_send, far_send = call(
        functools.partial(pack_kernel, head_count, group), "pack_keys_values",
        [((rows, PAIR), bf16)] * group + [((head_count, picked, PAIR), bf16)],
        [place, head_offsets, key_rows, value_rows], 2,
        [((head_count, rows, PAIR), bf16)],
    )
    far_in = [segment_shift(far_send, shift) for shift in range(1, others + 1)]
    kv = swap(kv_send)

    sent_rows = rows + others * picked
    qg_send = call(
        functools.partial(project_kernel, head_count, group, shards, others), "project_pack",
        [((sent_rows, PAIR), bf16)] * group,
        [place, out_weight, query_rows, *upstreams, *far_in], 1,
        [((rows, width), bf16), ((head_count, sent_rows, PAIR), bf16)],
        flops=2 * rows * width * upstream.shape[1],
    )
    qg = swap(qg_send)

    keys, key_t, extra, own_terms, other_terms = call(
        functools.partial(far_kernel, head_count, group, others), "picked_rows",
        [
            ((near, PAIR), bf16), ((HEAD_SIZE, near), bf16), ((PAIR + STAT_ROWS, count), bf16),
            ((count, PAIR), f32), ((others * count, PAIR), f32),
        ],
        [place, head_offsets, *kv, *qg], 2,
        [((near + count * (1 + others), PAIR), bf16), ((count, PAIR), bf16)],
        flops=8 * near * count * PAIR,
    )
    back = [
        segment_shift(other_terms[(shift - 1) * count : shift * count], -shift)
        for shift in range(1, others + 1)
    ]
    steps = group // 2
    scratch = [
        ((2, near, rows), f32), ((2, near, rows), f32), ((2, near, 2 * rows), bf16),
    ]
    half_flops = 10 * near * near // 2 * PAIR
    acc, query_half = call(
        functools.partial(first_kernel, head_count, steps), "first_rows",
        [((near, PAIR), f32), ((steps, rows // 2, PAIR), bf16)],
        [place, head_offsets, keys, key_t, extra, *qg[:steps]], 2, scratch, half_flops,
    )
    near_send = call(
        functools.partial(second_kernel, head_count, group - steps, others), "second_rows",
        [((rows + rows // 2, PAIR), bf16)] * group,
        [place, head_offsets, keys, key_t, extra, acc, query_half, own_terms, *back, *qg[steps:]],
        2, [((near, PAIR), f32)] + scratch, half_flops,
    )
    return tuple(
        call(
            functools.partial(unpack_kernel, head_count, group), "unpack",
            [((rows, width), bf16)] * 3,
            [place, *swap(near_send)], 1,
            [((group, rows + rows // 2, PAIR), bf16)],
        )
    )


def solution(mesh):
    return jax.shard_map(
        body,
        mesh=mesh,
        in_specs=(
            P(("context", "heads"), None),
            P("heads", None),
            P("context", "heads"),
            P("context", "heads"),
            P("context", "heads"),
            P(),
        ),
        out_specs=(P("context", "heads"), P("context", "heads"), P("context", "heads")),
        check_vma=False,
    )
```

time: 94.1 us -> 74.1 us (0.79)
  blocking collectives: 51.4 us -> 0 us
  starting transfers between devices: 5.18 us -> 27.1 us
  waiting for transfers between devices: 7.05 us -> 14.9 us
  Pallas kernels: 26 us -> 27.4 us
    all_to_all x4 -> x0, blocking collectives: 51.4 us -> none  [the longest x2 26.7 us: swap(): return lax.all_to_all(value, 'context', 0, 0, axis_index_groups=groups)]
    ppermute x0 -> x23, starting transfers between devices: none -> 24.1 us  [the longest x21 18.5 us: swap(): lax.ppermute(values[step], 'context', pairs[step])]
    ppermute x0 -> x23, waiting for transfers between devices: none -> 14.9 us  [the longest x21 14.6 us: swap(): lax.ppermute(values[step], 'context', pairs[step])]
    ppermute x1, waiting for transfers between devices: 7.05 us -> 0.01 us  [body(): upstreams.append(lax.ppermute(upstream, 'heads', pairs))]
    all_to_all x1 -> x0, starting transfers between devices: 3.62 us -> none  [swap(): return lax.all_to_all(value, 'context', 0, 0, axis_index_groups=groups)]
    ppermute x1, starting transfers between devices: 1.56 us -> 3 us  [body(): upstreams.append(lax.ppermute(upstream, 'heads', pairs))]
    pallas_call x4 -> x6, Pallas kernels: 26 us -> 27.4 us  [call(): pl.pallas_call(kernel, out_shape=tuple((jax.ShapeDtypeStruct(*shape) for...]
    unnamed x14 -> x12, local copies, waits for them, and re-layouts: 3.29 us -> 3.71 us
  transfers between devices with their start and end apart: 2 -> 24, of which waited for: 1 -> 12; matrix products, arithmetic and copies ran while one was open for 0% -> 0% of each run, Pallas kernels for 2% -> 18%
where the time goes in v2:
time: 74.1 us; the launch traced here: 73.9 us
  Pallas kernels  27.4 us (37%)
  starting transfers between devices  27.1 us (37%)
  waiting for transfers between devices  14.9 us (20%)
  local copies, waits for them, and re-layouts  3.71 us (5%)
    pallas_call x6, Pallas kernels, call(): pl.pallas_call(kernel, out_shape=tuple((jax.ShapeDtypeStruct(*shape) for...  27.4 us
    ppermute x21, starting transfers between devices, swap(): lax.ppermute(values[step], 'context', pairs[step])  18.5 us
    ppermute x21, waiting for transfers between devices, swap(): lax.ppermute(values[step], 'context', pairs[step])  14.6 us
    ppermute x2, starting transfers between devices, segment_shift(): return lax.ppermute(value, 'context', pairs)  5.53 us
    unnamed x12, local copies, waits for them, and re-layouts  3.71 us
    ppermute x1, starting transfers between devices, body(): upstreams.append(lax.ppermute(upstream, 'heads', pairs))  3 us
  transfers between devices with their start and end apart: 24, of which 12 were waited for; matrix products, arithmetic and copies ran while one was open for 0% of the time, Pallas kernels for 18%

profile of v2, /device:TPU:0, one launch (start us, length us, event | category | flops | bytes accessed | tf_op | source)
XLA Modules:
  0.0 73.9 jit_solution(8139323778633112654)
XLA Ops:
  0.6 3.0 %collective-permute-start.7 = (bf16[128,1024]{1,0:T(8,128)(2,1)}, bf16[128,1024]{1,0:T(8,128)(2,1)S(1)}, u32[]{:S(2)}, u32[]{:S(2)}) collective-permute-start(bf16[128,1024]{1,0:T(8,128)(2,1)} %refs_0_.1), channel_id=1, source_target_pairs={{0,1},{1,0},{2,3},{3,2},{4,5},{5,4},{6,7},{7,6},{8,9},{9,8},{10,11... | collective-permute-start | bytes 786440 | tf_op jit(solution)/shard_map/ppermute | solution.py:325
  3.6 0.0 copy-start.5
  3.6 0.1 pad_add_fusion.place_ref
  3.7 0.6 copy-done.5
  4.3 0.0 copy-start.1
  4.3 0.9 %copy-done.1 = bf16[256,512]{1,0:T(8,128)(2,1)S(1)} copy-done((bf16[256,512]{1,0:T(8,128)(2,1)S(1)}, bf16[256,512]{1,0:T(8,128)(2,1)}, u32[]{:S(2)}) %copy-start.1) | copy-done | bytes 262168
  5.2 0.9 %copy-done.2 = bf16[256,512]{1,0:T(8,128)(2,1)S(1)} copy-done((bf16[256,512]{1,0:T(8,128)(2,1)S(1)}, bf16[256,512]{1,0:T(8,128)(2,1)}, u32[]{:S(2)}) %copy-start.2) | copy-done | bytes 262168
  6.2 0.9 %pack_keys_values.1 = (bf16[256,128]{1,0:T(8,128)(2,1)S(1)}, bf16[256,128]{1,0:T(8,128)(2,1)S(1)}, bf16[256,128]{1,0:T(8,128)(2,1)S(1)}, bf16[256,128]{1,0:T(8,1...) custom-call(s32[2]{0:T(128)S(1)} %pad_add_fusion.place_ref, ...), custom_call_target="tpu_custom_call" | custom-call | bytes 2097152 | tf_op jit(solution)/shard_map/pack_keys_values/pallas_call | solution.py:286
  7.1 2.6 %collective-permute-start.8 = (bf16[8,16,128]{2,1,0:T(8,128)(2,1)S(1)}, bf16[8,16,128]{2,1,0:T(8,128)(2,1)S(1)}, u32[]{:S(2)}, u32[]{:S(2)}) collective-permute-start(bf16[8,16,128]{2,1,0:T(8,128)(2,1)S(1)} %get-tuple-element.43), channel_id=1, source_target_pairs={{0,16},{2,18},{4,20},{6,22},{8,24},{10,26},{12,28},{14,30},{16,0},... | collective-permute-start | bytes 98312 | tf_op jit(solution)/shard_map/ppermute | solution.py:320
  9.7 0.0 collective-permute-start
  9.7 1.5 %collective-permute-start.1 = (bf16[256,128]{1,0:T(8,128)(2,1)S(1)}, bf16[256,128]{1,0:T(8,128)(2,1)S(1)}, u32[]{:S(2)}, u32[]{:S(2)}) collective-permute-start(bf16[256,128]{1,0:T(8,128)(2,1)S(1)} %get-tuple-element.37), channel_id=1, source_target_pairs={{0,4},{2,6},{4,0},{6,2},{8,12},{10,14},{12,8},{14,10},{16,20},{18,... | collective-permute-start | bytes 196616 | tf_op jit(solution)/shard_map/ppermute | solution.py:315
  11.2 0.3 collective-permute-start.2
  11.5 0.4 collective-permute-done.8.refs_2_
  11.9 1.6 %collective-permute-start.3 = (bf16[256,128]{1,0:T(8,128)(2,1)S(1)}, bf16[256,128]{1,0:T(8,128)(2,1)S(1)}, u32[]{:S(2)}, u32[]{:S(2)}) collective-permute-start(bf16[256,128]{1,0:T(8,128)(2,1)S(1)} %get-tuple-element.39), channel_id=1, source_target_pairs={{0,8},{2,10},{4,12},{6,14},{8,0},{10,2},{12,4},{14,6},{16,24},{18,... | collective-permute-start | bytes 196616 | tf_op jit(solution)/shard_map/ppermute | solution.py:315
  13.5 0.0 collective-permute-done.7.refs_1_
  13.5 0.0 copy-done.3
  13.5 0.0 copy-done.4
  13.5 0.0 copy-start
  13.5 1.2 %copy-done = bf16[512,1024]{1,0:T(8,128)(2,1)S(1)} copy-done((bf16[512,1024]{1,0:T(8,128)(2,1)S(1)}, bf16[512,1024]{1,0:T(8,128)(2,1)}, u32[]{:S(2)}) %copy-start) | copy-done | bytes 1048600
  14.7 1.5 %project_pack.1 = (bf16[272,128]{1,0:T(8,128)(2,1)S(1)}, bf16[272,128]{1,0:T(8,128)(2,1)S(1)}, bf16[272,128]{1,0:T(8,128)(2,1)S(1)}, bf16[272,128]{1,0:T(8,128)(...) custom-call(s32[2]{0:T(128)S(1)} %pad_add_fusion.place_ref, ...), custom_call_target="tpu_custom_call" | custom-call | flops 268435456 | bytes 2097152 | tf_op jit(solution)/shard_map/project_pack/pallas_call | solution.py:286
  16.3 0.1 collective-permute-start.9
  16.4 0.0 collective-permute-done.refs_1_
  16.4 1.6 %collective-permute-start.10 = (bf16[272,128]{1,0:T(8,128)(2,1)S(1)}, bf16[272,128]{1,0:T(8,128)(2,1)S(1)}, u32[]{:S(2)}, u32[]{:S(2)}) collective-permute-start(bf16[272,128]{1,0:T(8,128)(2,1)S(1)} %get-tuple-element.46), channel_id=1, source_target_pairs={{0,4},{2,6},{4,0},{6,2},{8,12},{10,14},{12,8},{14,10},{16,20},{18,... | collective-permute-start | bytes 208904 | tf_op jit(solution)/shard_map/ppermute | solution.py:315
  18.0 0.0 collective-permute-done.1.refs_2_
  18.0 0.2 collective-permute-start.4
  18.2 0.0 collective-permute-done.2.refs_3_
  18.2 1.5 %collective-permute-start.5 = (bf16[256,128]{1,0:T(8,128)(2,1)S(1)}, bf16[256,128]{1,0:T(8,128)(2,1)S(1)}, u32[]{:S(2)}, u32[]{:S(2)}) collective-permute-start(bf16[256,128]{1,0:T(8,128)(2,1)S(1)} %get-tuple-element.41), channel_id=1, source_target_pairs={{0,12},{2,14},{4,8},{6,10},{8,4},{10,6},{12,0},{14,2},{16,28},{18,... | collective-permute-start | bytes 196616 | tf_op jit(solution)/shard_map/ppermute | solution.py:315
  19.7 0.0 collective-permute-done.3.refs_4_
  19.7 1.1 %collective-permute-start.6 = (bf16[256,128]{1,0:T(8,128)(2,1)S(1)}, bf16[256,128]{1,0:T(8,128)(2,1)S(1)}, u32[]{:S(2)}, u32[]{:S(2)}) collective-permute-start(bf16[256,128]{1,0:T(8,128)(2,1)S(1)} %get-tuple-element.42), channel_id=1, source_target_pairs={{0,14},{2,12},{4,10},{6,8},{8,6},{10,4},{12,2},{14,0},{16,30},{18,... | collective-permute-start | bytes 196616 | tf_op jit(solution)/shard_map/ppermute | solution.py:315
  20.8 1.2 %collective-permute-done.4.refs_5_ = bf16[256,128]{1,0:T(8,128)(2,1)S(1)} collective-permute-done((bf16[256,128]{1,0:T(8,128)(2,1)S(1)}, bf16[256,128]{1,0:T(8,128)(2,1)S(1)}, u32[]{:S(2)}, u32[]{:S(2)}) %collective-permute-start.4) | collective-permute-done | bytes 65568 | tf_op jit(solution)/shard_map/ppermute | solution.py:315
  22.0 0.6 collective-permute-start.11
  22.6 1.2 %collective-permute-done.5.refs_6_ = bf16[256,128]{1,0:T(8,128)(2,1)S(1)} collective-permute-done((bf16[256,128]{1,0:T(8,128)(2,1)S(1)}, bf16[256,128]{1,0:T(8,128)(2,1)S(1)}, u32[]{:S(2)}, u32[]{:S(2)}) %collective-permute-start.5) | collective-permute-done | bytes 65568 | tf_op jit(solution)/shard_map/ppermute | solution.py:315
  23.8 1.8 %collective-permute-start.12 = (bf16[272,128]{1,0:T(8,128)(2,1)S(1)}, bf16[272,128]{1,0:T(8,128)(2,1)S(1)}, u32[]{:S(2)}, u32[]{:S(2)}) collective-permute-start(bf16[272,128]{1,0:T(8,128)(2,1)S(1)} %get-tuple-element.48), channel_id=1, source_target_pairs={{0,8},{2,10},{4,12},{6,14},{8,0},{10,2},{12,4},{14,6},{16,24},{18,... | collective-permute-start | bytes 208904 | tf_op jit(solution)/shard_map/ppermute | solution.py:315
  25.6 0.0 collective-permute-done.6.refs_7_
  25.6 0.4 collective-permute-start.13
  25.9 0.0 collective-permute-done.9.refs_9_.refs_1_
  25.9 1.7 %collective-permute-start.14 = (bf16[272,128]{1,0:T(8,128)(2,1)S(1)}, bf16[272,128]{1,0:T(8,128)(2,1)S(1)}, u32[]{:S(2)}, u32[]{:S(2)}) collective-permute-start(bf16[272,128]{1,0:T(8,128)(2,1)S(1)} %get-tuple-element.50), channel_id=1, source_target_pairs={{0,12},{2,14},{4,8},{6,10},{8,4},{10,6},{12,0},{14,2},{16,28},{18,... | collective-permute-start | bytes 208904 | tf_op jit(solution)/shard_map/ppermute | solution.py:315
  27.7 0.0 collective-permute-done.10.refs_10_.refs_2_
  27.7 0.6 collective-permute-start.15
  28.2 0.0 collective-permute-done.11.refs_11_.refs_3_
  28.3 0.0 collective-permute-done.12.refs_12_.refs_1_
  28.3 1.6 %collective-permute-done.13.refs_13_.refs_2_ = bf16[272,128]{1,0:T(8,128)(2,1)S(1)} collective-permute-done((bf16[272,128]{1,0:T(8,128)(2,1)S(1)}, bf16[272,128]{1,0:T(8,128)(2,1)S(1)}, u32[]{:S(2)}, u32[]{:S(2)}) %collective-permute-start.13) | collective-permute-done | bytes 69664 | tf_op jit(solution)/shard_map/ppermute | solution.py:315
  29.8 2.4 %collective-permute-done.14.refs_14_.refs_3_ = bf16[272,128]{1,0:T(8,128)(2,1)S(1)} collective-permute-done((bf16[272,128]{1,0:T(8,128)(2,1)S(1)}, bf16[272,128]{1,0:T(8,128)(2,1)S(1)}, u32[]{:S(2)}, u32[]{:S(2)}) %collective-permute-start.14) | collective-permute-done | bytes 69664 | tf_op jit(solution)/shard_map/ppermute | solution.py:315
  32.2 1.1 %collective-permute-done.15.refs_15_.refs_4_ = bf16[272,128]{1,0:T(8,128)(2,1)S(1)} collective-permute-done((bf16[272,128]{1,0:T(8,128)(2,1)S(1)}, bf16[272,128]{1,0:T(8,128)(2,1)S(1)}, u32[]{:S(2)}, u32[]{:S(2)}) %collective-permute-start.15) | collective-permute-done | bytes 69664 | tf_op jit(solution)/shard_map/ppermute | solution.py:315
  33.3 1.9 %picked_rows.1 = (bf16[2048,128]{1,0:T(8,128)(2,1)S(1)}, bf16[64,2048]{1,0:T(8,128)(2,1)S(1)}, bf16[144,128]{1,0:T(8,128)(2,1)S(1)}, f32[128,128]{1,0:T(8,128)S(1)}, f32[128,128]{1,0:T(8,128)S(1)}) custom-call(s32[2]{0:T(128)S(1)} %pad_add_fusion.place_ref, s32[16]{0:T(128)S(1)} %copy-done.5, bf16[256,128]{1,0:T(8,128)(2,1)S(1)} %get-tuple-element.35.refs_0_, ...), custom_call_target="tpu_custom_call" | custom-call | flops 268435456 | bytes 2097152 | tf_op jit(solution)/shard_map/picked_rows/pallas_call | solution.py:286
  35.2 2.9 %collective-permute-start.16 = (f32[128,128]{1,0:T(8,128)S(1)}, f32[128,128]{1,0:T(8,128)S(1)}, u32[]{:S(2)}, u32[]{:S(2)}) collective-permute-start(f32[128,128]{1,0:T(8,128)S(1)} %get-tuple-element.58), channel_id=1, source_target_pairs={{0,16},{2,18},{4,20},{6,22},{8,24},{10,26},{12,28},{14,30},{16,0},... | collective-permute-start | bytes 196616 | tf_op jit(solution)/shard_map/ppermute | solution.py:320
  38.1 10.6 %first_rows.1 = (f32[2048,128]{1,0:T(8,128)S(1)}, bf16[4,128,128]{2,1,0:T(8,128)(2,1)S(1)}) custom-call(s32[2]{0:T(128)S(1)} %pad_add_fusion.place_ref, s32[16]{0:T(128)S(1)} %copy-done.5, bf16[2048,128]{1,0:T(8,128)(2,1)S(1)} %get-tuple-element.52.keys_ref, bf16[64,2048]{1,0:T(8,128)(2,1)S(1)} %get-tuple-element.53.key_t_ref, ...), custom_call_target="tpu_custom_call" | custom-call | flops 2684354560 | bytes 2097152 | tf_op jit(solution)/shard_map/first_rows/pallas_call | solution.py:286
  48.7 0.0 collective-permute-done.16.refs_0_
  48.7 10.6 %second_rows.1 = (bf16[384,128]{1,0:T(8,128)(2,1)S(1)}, bf16[384,128]{1,0:T(8,128)(2,1)S(1)}, bf16[384,128]{1,0:T(8,128)(2,1)S(1)}, bf16[384,128]{1,0:T(8,128)(2...) custom-call(s32[2]{0:T(128)S(1)} %pad_add_fusion.place_ref, ...), custom_call_target="tpu_custom_call" | custom-call | flops 2684354560 | bytes 2097152 | tf_op jit(solution)/shard_map/second_rows/pallas_call | solution.py:286
  59.3 0.1 collective-permute-start.17
  59.4 0.6 collective-permute-start.18
  59.9 1.3 %collective-permute-start.19 = (bf16[384,128]{1,0:T(8,128)(2,1)S(1)}, bf16[384,128]{1,0:T(8,128)(2,1)S(1)}, u32[]{:S(2)}, u32[]{:S(2)}) collective-permute-start(bf16[384,128]{1,0:T(8,128)(2,1)S(1)} %get-tuple-element.62), channel_id=1, source_target_pairs={{0,6},{2,4},{4,2},{6,0},{8,14},{10,12},{12,10},{14,8},{16,22},{18,... | collective-permute-start | bytes 294920 | tf_op jit(solution)/shard_map/ppermute | solution.py:315
  61.2 0.8 %collective-permute-start.20 = (bf16[384,128]{1,0:T(8,128)(2,1)S(1)}, bf16[384,128]{1,0:T(8,128)(2,1)S(1)}, u32[]{:S(2)}, u32[]{:S(2)}) collective-permute-start(bf16[384,128]{1,0:T(8,128)(2,1)S(1)} %get-tuple-element.63), channel_id=1, source_target_pairs={{0,8},{2,10},{4,12},{6,14},{8,0},{10,2},{12,4},{14,6},{16,24},{18,... | collective-permute-start | bytes 294920 | tf_op jit(solution)/shard_map/ppermute | solution.py:315
  62.0 0.9 %collective-permute-start.21 = (bf16[384,128]{1,0:T(8,128)(2,1)S(1)}, bf16[384,128]{1,0:T(8,128)(2,1)S(1)}, u32[]{:S(2)}, u32[]{:S(2)}) collective-permute-start(bf16[384,128]{1,0:T(8,128)(2,1)S(1)} %get-tuple-element.64), channel_id=1, source_target_pairs={{0,10},{2,8},{4,14},{6,12},{8,2},{10,0},{12,6},{14,4},{16,26},{18,... | collective-permute-start | bytes 294920 | tf_op jit(solution)/shard_map/ppermute | solution.py:315
  62.9 0.0 collective-permute-done.17.refs_1_
  62.9 1.4 %collective-permute-start.22 = (bf16[384,128]{1,0:T(8,128)(2,1)S(1)}, bf16[384,128]{1,0:T(8,128)(2,1)S(1)}, u32[]{:S(2)}, u32[]{:S(2)}) collective-permute-start(bf16[384,128]{1,0:T(8,128)(2,1)S(1)} %get-tuple-element.65), channel_id=1, source_target_pairs={{0,12},{2,14},{4,8},{6,10},{8,4},{10,6},{12,0},{14,2},{16,28},{18,... | collective-permute-start | bytes 294920 | tf_op jit(solution)/shard_map/ppermute | solution.py:315
  64.3 0.7 collective-permute-done.18.refs_2_
  65.0 0.6 collective-permute-start.23
  65.6 0.6 collective-permute-done.19.refs_3_
  66.2 0.6 collective-permute-done.20.refs_4_
  66.8 1.0 %collective-permute-done.21.refs_5_ = bf16[384,128]{1,0:T(8,128)(2,1)S(1)} collective-permute-done((bf16[384,128]{1,0:T(8,128)(2,1)S(1)}, bf16[384,128]{1,0:T(8,128)(2,1)S(1)}, u32[]{:S(2)}, u32[]{:S(2)}) %collective-permute-start.21) | collective-permute-done | bytes 98336 | tf_op jit(solution)/shard_map/ppermute | solution.py:315
  67.8 3.2 %collective-permute-done.22.refs_6_ = bf16[384,128]{1,0:T(8,128)(2,1)S(1)} collective-permute-done((bf16[384,128]{1,0:T(8,128)(2,1)S(1)}, bf16[384,128]{1,0:T(8,128)(2,1)S(1)}, u32[]{:S(2)}, u32[]{:S(2)}) %collective-permute-start.22) | collective-permute-done | bytes 98336 | tf_op jit(solution)/shard_map/ppermute | solution.py:315
  71.0 1.0 %collective-permute-done.23.refs_7_ = bf16[384,128]{1,0:T(8,128)(2,1)S(1)} collective-permute-done((bf16[384,128]{1,0:T(8,128)(2,1)S(1)}, bf16[384,128]{1,0:T(8,128)(2,1)S(1)}, u32[]{:S(2)}, u32[]{:S(2)}) %collective-permute-start.23) | collective-permute-done | bytes 98336 | tf_op jit(solution)/shard_map/ppermute | solution.py:315
  72.0 1.9 %unpack.1 = (bf16[256,512]{1,0:T(8,128)(2,1)}, bf16[256,512]{1,0:T(8,128)(2,1)}, bf16[256,512]{1,0:T(8,128)(2,1)}) custom-call(s32[2]{0:T(128)S(1)} %pad_add_fusion.place_ref, bf16[384,128]{1,0:T(8,128)(2,1)S(1)} %get-tuple-element.59.refs_0_, bf16[384,128]{1,0:T(8,128)(2,1)S(1)} %collective-permute-done.17.refs_1_, ...), custom_call_target="tpu_custom_call" | custom-call | bytes 2097152 | tf_op jit(solution)/shard_map/unpack/pallas_call | solution.py:286
  (3 shorter events, 0.0 us)
Async XLA Ops:
  0.6 12.9 %collective-permute-start.7 = (bf16[128,1024]{1,0:T(8,128)(2,1)}, bf16[128,1024]{1,0:T(8,128)(2,1)S(1)}, u32[]{:S(2)}, u32[]{:S(2)}) collective-permute-start(bf16[128,1024]{1,0:T(8,128)(2,1)} %refs_0_.1), channel_id=1, source_target_pairs={{0,1},{1,0},{2,3},{3,2},{4,5},{5,4},{6,7},{7,6},{8,9},{9,8},{10,11... | collective-permute-start | bytes 786440 | tf_op jit(solution)/shard_map/ppermute | solution.py:325
  3.6 0.7 copy-start.5
  4.3 0.9 %copy-start.1 = (bf16[256,512]{1,0:T(8,128)(2,1)S(1)}, bf16[256,512]{1,0:T(8,128)(2,1)}, u32[]{:S(2)}) copy-start(bf16[256,512]{1,0:T(8,128)(2,1)} %key_ref.1) | copy-start | bytes 786436
  5.2 0.9 %copy-start.2 = (bf16[256,512]{1,0:T(8,128)(2,1)S(1)}, bf16[256,512]{1,0:T(8,128)(2,1)}, u32[]{:S(2)}) copy-start(bf16[256,512]{1,0:T(8,128)(2,1)} %value_ref.1) | copy-start | bytes 786436
  6.2 7.3 %copy-start.3 = (bf16[256,512]{1,0:T(8,128)(2,1)S(1)}, bf16[256,512]{1,0:T(8,128)(2,1)}, u32[]{:S(2)}) copy-start(bf16[256,512]{1,0:T(8,128)(2,1)} %query_ref.1) | copy-start | bytes 786436
  6.2 7.3 %copy-start.4 = (bf16[128,1024]{1,0:T(8,128)(2,1)S(1)}, bf16[128,1024]{1,0:T(8,128)(2,1)}, u32[]{:S(2)}) copy-start(bf16[128,1024]{1,0:T(8,128)(2,1)} %refs_0_.1) | copy-start | bytes 786436
  7.1 4.9 %collective-permute-start.8 = (bf16[8,16,128]{2,1,0:T(8,128)(2,1)S(1)}, bf16[8,16,128]{2,1,0:T(8,128)(2,1)S(1)}, u32[]{:S(2)}, u32[]{:S(2)}) collective-permute-start(bf16[8,16,128]{2,1,0:T(8,128)(2,1)S(1)} %get-tuple-element.43), channel_id=1, source_target_pairs={{0,16},{2,18},{4,20},{6,22},{8,24},{10,26},{12,28},{14,30},{16,0},... | collective-permute-start | bytes 98312 | tf_op jit(solution)/shard_map/ppermute | solution.py:320
  9.7 6.7 %collective-permute-start = (bf16[256,128]{1,0:T(8,128)(2,1)S(1)}, bf16[256,128]{1,0:T(8,128)(2,1)S(1)}, u32[]{:S(2)}, u32[]{:S(2)}) collective-permute-start(bf16[256,128]{1,0:T(8,128)(2,1)S(1)} %get-tuple-element.36), channel_id=1, source_target_pairs={{0,2},{2,0},{4,6},{6,4},{8,10},{10,8},{12,14},{14,12},{16,18},{18,... | collective-permute-start | bytes 196616 | tf_op jit(solution)/shard_map/ppermute | solution.py:315
  9.7 8.3 %collective-permute-start.1 = (bf16[256,128]{1,0:T(8,128)(2,1)S(1)}, bf16[256,128]{1,0:T(8,128)(2,1)S(1)}, u32[]{:S(2)}, u32[]{:S(2)}) collective-permute-start(bf16[256,128]{1,0:T(8,128)(2,1)S(1)} %get-tuple-element.37), channel_id=1, source_target_pairs={{0,4},{2,6},{4,0},{6,2},{8,12},{10,14},{12,8},{14,10},{16,20},{18,... | collective-permute-start | bytes 196616 | tf_op jit(solution)/shard_map/ppermute | solution.py:315
  11.2 7.0 %collective-permute-start.2 = (bf16[256,128]{1,0:T(8,128)(2,1)S(1)}, bf16[256,128]{1,0:T(8,128)(2,1)S(1)}, u32[]{:S(2)}, u32[]{:S(2)}) collective-permute-start(bf16[256,128]{1,0:T(8,128)(2,1)S(1)} %get-tuple-element.38), channel_id=1, source_target_pairs={{0,6},{2,4},{4,2},{6,0},{8,14},{10,12},{12,10},{14,8},{16,22},{18,... | collective-permute-start | bytes 196616 | tf_op jit(solution)/shard_map/ppermute | solution.py:315
  11.9 7.8 %collective-permute-start.3 = (bf16[256,128]{1,0:T(8,128)(2,1)S(1)}, bf16[256,128]{1,0:T(8,128)(2,1)S(1)}, u32[]{:S(2)}, u32[]{:S(2)}) collective-permute-start(bf16[256,128]{1,0:T(8,128)(2,1)S(1)} %get-tuple-element.39), channel_id=1, source_target_pairs={{0,8},{2,10},{4,12},{6,14},{8,0},{10,2},{12,4},{14,6},{16,24},{18,... | collective-permute-start | bytes 196616 | tf_op jit(solution)/shard_map/ppermute | solution.py:315
  13.5 1.2 %copy-start = (bf16[512,1024]{1,0:T(8,128)(2,1)S(1)}, bf16[512,1024]{1,0:T(8,128)(2,1)}, u32[]{:S(2)}) copy-start(bf16[512,1024]{1,0:T(8,128)(2,1)} %weight_ref.1) | copy-start | bytes 3145732
  16.3 9.7 %collective-permute-start.9 = (bf16[272,128]{1,0:T(8,128)(2,1)S(1)}, bf16[272,128]{1,0:T(8,128)(2,1)S(1)}, u32[]{:S(2)}, u32[]{:S(2)}) collective-permute-start(bf16[272,128]{1,0:T(8,128)(2,1)S(1)} %get-tuple-element.45), channel_id=1, source_target_pairs={{0,2},{2,0},{4,6},{6,4},{8,10},{10,8},{12,14},{14,12},{16,18},{18,... | collective-permute-start | bytes 208904 | tf_op jit(solution)/shard_map/ppermute | solution.py:315
  16.4 11.3 %collective-permute-start.10 = (bf16[272,128]{1,0:T(8,128)(2,1)S(1)}, bf16[272,128]{1,0:T(8,128)(2,1)S(1)}, u32[]{:S(2)}, u32[]{:S(2)}) collective-permute-start(bf16[272,128]{1,0:T(8,128)(2,1)S(1)} %get-tuple-element.46), channel_id=1, source_target_pairs={{0,4},{2,6},{4,0},{6,2},{8,12},{10,14},{12,8},{14,10},{16,20},{18,... | collective-permute-start | bytes 208904 | tf_op jit(solution)/shard_map/ppermute | solution.py:315
  18.0 4.1 %collective-permute-start.4 = (bf16[256,128]{1,0:T(8,128)(2,1)S(1)}, bf16[256,128]{1,0:T(8,128)(2,1)S(1)}, u32[]{:S(2)}, u32[]{:S(2)}) collective-permute-start(bf16[256,128]{1,0:T(8,128)(2,1)S(1)} %get-tuple-element.40), channel_id=1, source_target_pairs={{0,10},{2,8},{4,14},{6,12},{8,2},{10,0},{12,6},{14,4},{16,26},{18,... | collective-permute-start | bytes 196616 | tf_op jit(solution)/shard_map/ppermute | solution.py:315
  18.2 5.6 %collective-permute-start.5 = (bf16[256,128]{1,0:T(8,128)(2,1)S(1)}, bf16[256,128]{1,0:T(8,128)(2,1)S(1)}, u32[]{:S(2)}, u32[]{:S(2)}) collective-permute-start(bf16[256,128]{1,0:T(8,128)(2,1)S(1)} %get-tuple-element.41), channel_id=1, source_target_pairs={{0,12},{2,14},{4,8},{6,10},{8,4},{10,6},{12,0},{14,2},{16,28},{18,... | collective-permute-start | bytes 196616 | tf_op jit(solution)/shard_map/ppermute | solution.py:315
  19.7 5.9 %collective-permute-start.6 = (bf16[256,128]{1,0:T(8,128)(2,1)S(1)}, bf16[256,128]{1,0:T(8,128)(2,1)S(1)}, u32[]{:S(2)}, u32[]{:S(2)}) collective-permute-start(bf16[256,128]{1,0:T(8,128)(2,1)S(1)} %get-tuple-element.42), channel_id=1, source_target_pairs={{0,14},{2,12},{4,10},{6,8},{8,6},{10,4},{12,2},{14,0},{16,30},{18,... | collective-permute-start | bytes 196616 | tf_op jit(solution)/shard_map/ppermute | solution.py:315
  22.0 6.2 %collective-permute-start.11 = (bf16[272,128]{1,0:T(8,128)(2,1)S(1)}, bf16[272,128]{1,0:T(8,128)(2,1)S(1)}, u32[]{:S(2)}, u32[]{:S(2)}) collective-permute-start(bf16[272,128]{1,0:T(8,128)(2,1)S(1)} %get-tuple-element.47), channel_id=1, source_target_pairs={{0,6},{2,4},{4,2},{6,0},{8,14},{10,12},{12,10},{14,8},{16,22},{18,... | collective-permute-start | bytes 208904 | tf_op jit(solution)/shard_map/ppermute | solution.py:315
  23.8 4.4 %collective-permute-start.12 = (bf16[272,128]{1,0:T(8,128)(2,1)S(1)}, bf16[272,128]{1,0:T(8,128)(2,1)S(1)}, u32[]{:S(2)}, u32[]{:S(2)}) collective-permute-start(bf16[272,128]{1,0:T(8,128)(2,1)S(1)} %get-tuple-element.48), channel_id=1, source_target_pairs={{0,8},{2,10},{4,12},{6,14},{8,0},{10,2},{12,4},{14,6},{16,24},{18,... | collective-permute-start | bytes 208904 | tf_op jit(solution)/shard_map/ppermute | solution.py:315
  25.6 4.2 %collective-permute-start.13 = (bf16[272,128]{1,0:T(8,128)(2,1)S(1)}, bf16[272,128]{1,0:T(8,128)(2,1)S(1)}, u32[]{:S(2)}, u32[]{:S(2)}) collective-permute-start(bf16[272,128]{1,0:T(8,128)(2,1)S(1)} %get-tuple-element.49), channel_id=1, source_target_pairs={{0,10},{2,8},{4,14},{6,12},{8,2},{10,0},{12,6},{14,4},{16,26},{18,... | collective-permute-start | bytes 208904 | tf_op jit(solution)/shard_map/ppermute | solution.py:315
  25.9 6.2 %collective-permute-start.14 = (bf16[272,128]{1,0:T(8,128)(2,1)S(1)}, bf16[272,128]{1,0:T(8,128)(2,1)S(1)}, u32[]{:S(2)}, u32[]{:S(2)}) collective-permute-start(bf16[272,128]{1,0:T(8,128)(2,1)S(1)} %get-tuple-element.50), channel_id=1, source_target_pairs={{0,12},{2,14},{4,8},{6,10},{8,4},{10,6},{12,0},{14,2},{16,28},{18,... | collective-permute-start | bytes 208904 | tf_op jit(solution)/shard_map/ppermute | solution.py:315
  27.7 5.6 %collective-permute-start.15 = (bf16[272,128]{1,0:T(8,128)(2,1)S(1)}, bf16[272,128]{1,0:T(8,128)(2,1)S(1)}, u32[]{:S(2)}, u32[]{:S(2)}) collective-permute-start(bf16[272,128]{1,0:T(8,128)(2,1)S(1)} %get-tuple-element.51), channel_id=1, source_target_pairs={{0,14},{2,12},{4,10},{6,8},{8,6},{10,4},{12,2},{14,0},{16,30},{18,... | collective-permute-start | bytes 208904 | tf_op jit(solution)/shard_map/ppermute | solution.py:315
  35.2 13.5 %collective-permute-start.16 = (f32[128,128]{1,0:T(8,128)S(1)}, f32[128,128]{1,0:T(8,128)S(1)}, u32[]{:S(2)}, u32[]{:S(2)}) collective-permute-start(f32[128,128]{1,0:T(8,128)S(1)} %get-tuple-element.58), channel_id=1, source_target_pairs={{0,16},{2,18},{4,20},{6,22},{8,24},{10,26},{12,28},{14,30},{16,0},... | collective-permute-start | bytes 196616 | tf_op jit(solution)/shard_map/ppermute | solution.py:320
  59.3 3.6 %collective-permute-start.17 = (bf16[384,128]{1,0:T(8,128)(2,1)S(1)}, bf16[384,128]{1,0:T(8,128)(2,1)S(1)}, u32[]{:S(2)}, u32[]{:S(2)}) collective-permute-start(bf16[384,128]{1,0:T(8,128)(2,1)S(1)} %get-tuple-element.60), channel_id=1, source_target_pairs={{0,2},{2,0},{4,6},{6,4},{8,10},{10,8},{12,14},{14,12},{16,18},{18,... | collective-permute-start | bytes 294920 | tf_op jit(solution)/shard_map/ppermute | solution.py:315
  59.4 5.7 %collective-permute-start.18 = (bf16[384,128]{1,0:T(8,128)(2,1)S(1)}, bf16[384,128]{1,0:T(8,128)(2,1)S(1)}, u32[]{:S(2)}, u32[]{:S(2)}) collective-permute-start(bf16[384,128]{1,0:T(8,128)(2,1)S(1)} %get-tuple-element.61), channel_id=1, source_target_pairs={{0,4},{2,6},{4,0},{6,2},{8,12},{10,14},{12,8},{14,10},{16,20},{18,... | collective-permute-start | bytes 294920 | tf_op jit(solution)/shard_map/ppermute | solution.py:315
  59.9 6.3 %collective-permute-start.19 = (bf16[384,128]{1,0:T(8,128)(2,1)S(1)}, bf16[384,128]{1,0:T(8,128)(2,1)S(1)}, u32[]{:S(2)}, u32[]{:S(2)}) collective-permute-start(bf16[384,128]{1,0:T(8,128)(2,1)S(1)} %get-tuple-element.62), channel_id=1, source_target_pairs={{0,6},{2,4},{4,2},{6,0},{8,14},{10,12},{12,10},{14,8},{16,22},{18,... | collective-permute-start | bytes 294920 | tf_op jit(solution)/shard_map/ppermute | solution.py:315
  61.2 5.6 %collective-permute-start.20 = (bf16[384,128]{1,0:T(8,128)(2,1)S(1)}, bf16[384,128]{1,0:T(8,128)(2,1)S(1)}, u32[]{:S(2)}, u32[]{:S(2)}) collective-permute-start(bf16[384,128]{1,0:T(8,128)(2,1)S(1)} %get-tuple-element.63), channel_id=1, source_target_pairs={{0,8},{2,10},{4,12},{6,14},{8,0},{10,2},{12,4},{14,6},{16,24},{18,... | collective-permute-start | bytes 294920 | tf_op jit(solution)/shard_map/ppermute | solution.py:315
  62.0 5.8 %collective-permute-start.21 = (bf16[384,128]{1,0:T(8,128)(2,1)S(1)}, bf16[384,128]{1,0:T(8,128)(2,1)S(1)}, u32[]{:S(2)}, u32[]{:S(2)}) collective-permute-start(bf16[384,128]{1,0:T(8,128)(2,1)S(1)} %get-tuple-element.64), channel_id=1, source_target_pairs={{0,10},{2,8},{4,14},{6,12},{8,2},{10,0},{12,6},{14,4},{16,26},{18,... | collective-permute-start | bytes 294920 | tf_op jit(solution)/shard_map/ppermute | solution.py:315
  62.9 8.1 %collective-permute-start.22 = (bf16[384,128]{1,0:T(8,128)(2,1)S(1)}, bf16[384,128]{1,0:T(8,128)(2,1)S(1)}, u32[]{:S(2)}, u32[]{:S(2)}) collective-permute-start(bf16[384,128]{1,0:T(8,128)(2,1)S(1)} %get-tuple-element.65), channel_id=1, source_target_pairs={{0,12},{2,14},{4,8},{6,10},{8,4},{10,6},{12,0},{14,2},{16,28},{18,... | collective-permute-start | bytes 294920 | tf_op jit(solution)/shard_map/ppermute | solution.py:315
  65.0 7.0 %collective-permute-start.23 = (bf16[384,128]{1,0:T(8,128)(2,1)S(1)}, bf16[384,128]{1,0:T(8,128)(2,1)S(1)}, u32[]{:S(2)}, u32[]{:S(2)}) collective-permute-start(bf16[384,128]{1,0:T(8,128)(2,1)S(1)} %get-tuple-element.66), channel_id=1, source_target_pairs={{0,14},{2,12},{4,10},{6,8},{8,6},{10,4},{12,2},{14,0},{16,30},{18,... | collective-permute-start | bytes 294920 | tf_op jit(solution)/shard_map/ppermute | solution.py:315

commit v3 on v2

v3 whole, which is shorter than its diff:
```python
import functools
import math

import jax
import jax.numpy as jnp
from jax import lax
from jax.experimental import pallas as pl
from jax.experimental.pallas import tpu as pltpu
from jax.sharding import PartitionSpec as P

HEAD_SIZE = 64
PAIR = 2 * HEAD_SIZE
DILATION_RATE = 16
FIRST_SEGMENT = 2048
SCALE = 1.0 / math.sqrt(HEAD_SIZE)
LOG2E = math.log2(math.e)
SCORE_FACTOR = SCALE * LOG2E
STRIP = 64
STAT_ROWS = 16

SMEM = pl.BlockSpec(memory_space=pltpu.SMEM)
VMEM = pl.BlockSpec(memory_space=pltpu.VMEM)
ANY = pl.BlockSpec(memory_space=pl.ANY)


def dot_nt(left, right):
    return lax.dot_general(
        left, right, (((1,), (1,)), ((), ())), preferred_element_type=jnp.float32
    )


def dot_nn(left, right):
    return jnp.dot(left, right, preferred_element_type=jnp.float32)


def head_columns(ref, head):
    return ref[:, head * HEAD_SIZE : (head + 1) * HEAD_SIZE]


def pick_matrix(offset, picked, rows):
    source = lax.broadcasted_iota(jnp.int32, (picked, rows), 1)
    index = lax.broadcasted_iota(jnp.int32, (picked, rows), 0)
    return (source == index * DILATION_RATE + offset).astype(jnp.bfloat16)


def spread_matrix(offset, first, picked, rows, axis):
    shape = (picked, rows) if axis == 0 else (rows, picked)
    index = lax.broadcasted_iota(jnp.int32, shape, axis)
    source = lax.broadcasted_iota(jnp.int32, shape, 1 - axis)
    return (source == (index - first) * DILATION_RATE + offset).astype(jnp.bfloat16)


def split_two(value):
    high = value.astype(jnp.bfloat16)
    low = (value - high.astype(jnp.float32)).astype(jnp.bfloat16)
    return high, low


def split_three(value):
    high = value.astype(jnp.bfloat16)
    rest = value - high.astype(jnp.float32)
    middle = rest.astype(jnp.bfloat16)
    low = (rest - middle.astype(jnp.float32)).astype(jnp.bfloat16)
    return high, middle, low


def fold(value, combine):
    parts = [value[start : start + 8] for start in range(0, value.shape[0], 8)]
    while len(parts) > 1:
        merged = [combine(parts[i], parts[i + 1]) for i in range(0, len(parts) - 1, 2)]
        parts = merged + parts[len(merged) * 2 :]
    return parts[0]


def left_half(shape):
    return lax.broadcasted_iota(jnp.int32, shape, 1) < HEAD_SIZE


def side_by_side(block):
    half = block.shape[0] // 2
    return jnp.concatenate([block[:half], block[half:]], 1)


def pack_kernel(head_count, query_hbm, key_hbm, value_hbm, *refs):
    out_ref, query_ref, key_ref, value_ref, sems = refs
    rows = query_ref.shape[0]
    copies = [
        pltpu.make_async_copy(source, target, sems.at[index])
        for index, (source, target) in enumerate(
            [(key_hbm, key_ref), (value_hbm, value_ref), (query_hbm, query_ref)]
        )
    ]
    for copy in copies:
        copy.start()
    for copy in copies:
        copy.wait()
    for head in range(head_count):
        pair = jnp.concatenate([head_columns(key_ref, head), head_columns(value_ref, head)], 1)
        query = side_by_side(head_columns(query_ref, head))
        for place in range(head, out_ref.shape[0], head_count):
            out_ref[place, :rows, :] = pair
            out_ref[place, rows:, :] = query


def project_kernel(head_count, group, shards, place_ref, weight_ref, *refs):
    upstream_refs, refs = refs[:shards], refs[shards:]
    out_refs, grad_ref, stage_ref = refs[:group], refs[group], refs[group + 1]
    shard_rows = upstream_refs[0].shape[0]
    for step, upstream_ref in enumerate(upstream_refs):
        owner = lax.rem(place_ref[1] + (shards - step), shards)
        start = pl.multiple_of(owner * shard_rows, shard_rows)
        grad_ref[pl.ds(start, shard_rows), :] = dot_nt(
            upstream_ref[...], weight_ref[...]
        ).astype(jnp.bfloat16)
    for head in range(head_count):
        stage_ref[head] = side_by_side(head_columns(grad_ref, head))
    for step, out_ref in enumerate(out_refs):
        out_ref[...] = stage_ref[lax.rem(lax.bitwise_xor(place_ref[0], step), head_count)]


def own_offset(head_count, place_ref):
    return place_ref[2 + place_ref[1] * head_count + lax.rem(place_ref[0], head_count)]


def gather_kernel(head_count, place_ref, sent_ref, after_ref, keys_out, key_t_out, picks_out):
    group, sent_rows, _ = sent_ref.shape
    rows = keys_out.shape[0] // group
    picked = rows // DILATION_RATE
    pick = pick_matrix(own_offset(head_count, place_ref), picked, rows)
    for step in range(group):
        pair = sent_ref[lax.bitwise_xor(place_ref[0], step), :rows, :]
        keys_out[step * rows : (step + 1) * rows, :] = pair
        picks_out[step * picked : (step + 1) * picked, :] = dot_nn(pick, pair).astype(jnp.bfloat16)
        key_t_out[:, step * rows : (step + 1) * rows] = (
            pair.astype(jnp.float32).T[:HEAD_SIZE].astype(jnp.bfloat16)
        )


def queries_from(sent_ref, place_ref, step, rows):
    return sent_ref.at[lax.bitwise_xor(place_ref[0], step), rows:]


def query_and_grad(query_ref, grad_ref):
    query, grad = query_ref[...], grad_ref[...]
    zero = jnp.zeros((query.shape[0], HEAD_SIZE), query.dtype)
    return (
        jnp.concatenate(
            [
                jnp.concatenate([query[:, :HEAD_SIZE], zero], 1),
                jnp.concatenate([query[:, HEAD_SIZE:], zero], 1),
            ], 0,
        ),
        jnp.concatenate(
            [
                jnp.concatenate([zero, grad[:, :HEAD_SIZE]], 1),
                jnp.concatenate([zero, grad[:, HEAD_SIZE:]], 1),
            ], 0,
        ),
    )


def far_kernel(head_count, group, others, place_ref, near_ref, sent_ref, picks_ref, *refs):
    other_refs, refs = refs[:others], refs[others:]
    grad_refs, refs = refs[:group], refs[group:]
    extra_out, own_out, other_out, keys_ref, query_ref, grad_ref = refs
    near = near_ref.shape[0]
    rows = near // group
    picked = rows // DILATION_RATE
    count = group * picked
    far = count * (1 + others)
    pick = pick_matrix(own_offset(head_count, place_ref), picked, rows)
    keys_ref[:near, :] = near_ref[...]
    for index, ref in enumerate([picks_ref, *other_refs]):
        keys_ref[near + index * count : near + (index + 1) * count, :] = ref[...]
    for step in range(group):
        query, grad = query_and_grad(queries_from(sent_ref, place_ref, step, rows), grad_refs[step])
        span = slice(step * picked, (step + 1) * picked)
        query_ref[span, :] = dot_nn(pick, query).astype(jnp.bfloat16)
        grad_ref[span, :] = dot_nn(pick, grad).astype(jnp.bfloat16)
    far_t = keys_ref[near:, :].astype(jnp.float32).T[:HEAD_SIZE].astype(jnp.bfloat16)
    query, grad = query_ref[...], grad_ref[...]
    score = dot_nt(keys_ref[...], query)
    dprob = dot_nt(keys_ref[...], grad)
    top = jnp.max(score, 0, keepdims=True)
    prob = jnp.exp2((score - top) * SCORE_FACTOR)
    total = jnp.sum(prob, 0, keepdims=True)
    inverse = 1.0 / total
    delta = jnp.sum(prob * dprob, 0, keepdims=True) * inverse
    prob_far = prob[near:] * inverse
    dscore = (prob_far * (dprob[near:] - delta)).astype(jnp.bfloat16)
    terms = dot_nn(
        jnp.concatenate([dscore, prob_far.astype(jnp.bfloat16)], 1),
        jnp.concatenate([query, grad], 0),
    ) * jnp.where(left_half((far, PAIR)), SCALE, 1.0)
    own_out[...] = terms[:count]
    other_out[...] = terms[count:]
    query_grad = dot_nn(far_t, dscore)
    lse = top * SCORE_FACTOR + jnp.log2(total)
    extra_out[:PAIR, :] = jnp.concatenate(split_two(query_grad), 0)
    blank = jnp.zeros((STAT_ROWS - 6, count), jnp.bfloat16)
    extra_out[PAIR:, :] = jnp.concatenate([*split_three(lse), *split_three(delta), blank], 0)


def near_block(
    first, offset, keys_ref, key_t_ref, query_ref, grad_ref, extra_ref, score_ref, dprob_ref,
    work_ref, acc_ref,
):
    near = keys_ref.shape[0]
    rows = score_ref.shape[1]
    count = extra_ref.shape[1]
    query, grad = query_and_grad(query_ref, grad_ref)
    score_ref[...] = dot_nt(keys_ref[...], query)
    dprob_ref[...] = dot_nt(keys_ref[...], grad)
    extra = dot_nn(extra_ref[...], spread_matrix(offset, first, count, rows, 0))
    row_lane = lax.broadcasted_iota(jnp.int32, (1, rows), 1)
    picked = lax.rem(row_lane, DILATION_RATE) == offset
    lse_picked = extra[PAIR : PAIR + 1] + extra[PAIR + 1 : PAIR + 2] + extra[PAIR + 2 : PAIR + 3]
    delta_picked = (
        extra[PAIR + 3 : PAIR + 4] + extra[PAIR + 4 : PAIR + 5] + extra[PAIR + 5 : PAIR + 6]
    )
    strips = [slice(start, start + STRIP) for start in range(0, near, STRIP)]
    top = None
    for strip in strips:
        part = fold(score_ref[strip, :], jnp.maximum)
        top = part if top is None else jnp.maximum(top, part)
    top = jnp.max(top, 0, keepdims=True) * SCORE_FACTOR
    top = jnp.where(picked, lse_picked, top)
    total = jnp.zeros((8, rows), jnp.float32)
    delta = jnp.zeros((8, rows), jnp.float32)
    for strip in strips:
        prob = jnp.exp2(score_ref[strip, :] * SCORE_FACTOR - top)
        total = total + fold(prob, jnp.add)
        delta = delta + fold(prob * dprob_ref[strip, :], jnp.add)
        score_ref[strip, :] = prob
    inverse = jnp.where(picked, 1.0, 1.0 / jnp.sum(total, 0, keepdims=True))
    delta = jnp.where(picked, delta_picked, jnp.sum(delta, 0, keepdims=True) * inverse)
    for strip in strips:
        prob = score_ref[strip, :] * inverse
        work_ref[strip, :rows] = (prob * (dprob_ref[strip, :] - delta)).astype(jnp.bfloat16)
        work_ref[strip, rows:] = prob.astype(jnp.bfloat16)
    acc_ref[...] += dot_nn(work_ref[...], jnp.concatenate([query, grad], 0))
    query_grad = dot_nn(key_t_ref[...], work_ref[:, :rows])
    query_grad = query_grad + extra[:HEAD_SIZE] + extra[HEAD_SIZE:PAIR]
    query_grad = (query_grad * SCALE).T.astype(jnp.bfloat16)
    half = rows // 2
    return jnp.concatenate([query_grad[:half], query_grad[half:]], 1)


def first_kernel(head_count, place_ref, keys_ref, key_t_ref, sent_ref, extra_ref, *refs):
    acc_ref, query_out, *scratch = refs[-5:]
    grad_refs = refs[:-5]
    rows = scratch[0].shape[2]
    offset = own_offset(head_count, place_ref)
    acc_ref[...] = jnp.zeros_like(acc_ref)
    for step, grad_ref in enumerate(grad_refs):
        query_out[step] = near_block(
            step * (rows // DILATION_RATE), offset, keys_ref, key_t_ref,
            queries_from(sent_ref, place_ref, step, rows), grad_ref, extra_ref,
            *[ref.at[step % 2] for ref in scratch], acc_ref,
        )


def second_kernel(
    head_count, steps, others, place_ref, keys_ref, key_t_ref, sent_ref, extra_ref, start_ref,
    query_ref, own_ref, *refs,
):
    back_refs, refs = refs[:others], refs[others:]
    grad_refs, refs = refs[:steps], refs[steps:]
    rows = query_ref.shape[1] * 2
    group = keys_ref.shape[0] // rows
    out_refs, refs = refs[:group], refs[group:]
    acc_ref, *scratch = refs
    count = extra_ref.shape[1]
    picked = count // group
    offset = own_offset(head_count, place_ref)
    acc_ref[...] = start_ref[...]
    for step, grad_ref in enumerate(grad_refs):
        place = group - steps + step
        out_refs[place][rows:, :] = near_block(
            place * picked, offset, keys_ref, key_t_ref,
            queries_from(sent_ref, place_ref, place, rows), grad_ref, extra_ref,
            *[ref.at[step % 2] for ref in scratch], acc_ref,
        )
    terms = own_ref[...]
    for back_ref in back_refs:
        terms = terms + back_ref[...]
    terms = jnp.concatenate(split_two(terms), 0)
    factor = jnp.where(left_half((rows, PAIR)), SCALE, 1.0)
    for place in range(group):
        spread = spread_matrix(offset, place * picked, count, rows, 1)
        placed = dot_nn(jnp.concatenate([spread, spread], 1), terms)
        summed = acc_ref[place * rows : (place + 1) * rows, :] * factor + placed
        out_refs[place][:rows, :] = summed.astype(jnp.bfloat16)
        if place < group - steps:
            out_refs[place][rows:, :] = query_ref[place]


def unpack_kernel(head_count, group, place_ref, *refs):
    near_refs, refs = refs[:group], refs[group:]
    query_out, key_out, value_out, stage_ref = refs
    rows = query_out.shape[0]
    half = rows // 2
    for step, near_ref in enumerate(near_refs):
        stage_ref[lax.bitwise_xor(place_ref[0], step)] = near_ref[...]
    for head in range(head_count):
        columns = slice(head * HEAD_SIZE, (head + 1) * HEAD_SIZE)
        key_out[:, columns] = stage_ref[head, :rows, :HEAD_SIZE]
        value_out[:, columns] = stage_ref[head, :rows, HEAD_SIZE:]
        query_out[:half, columns] = stage_ref[head, rows:, :HEAD_SIZE]
        query_out[half:, columns] = stage_ref[head, rows:, HEAD_SIZE:]


def call(kernel, name, out_shape, operands, scratch=(), flops=0, hbm=0):
    specs = [ANY] * hbm if hbm else [SMEM] + [VMEM] * (len(operands) - 1)
    return pl.pallas_call(
        kernel,
        out_shape=tuple(jax.ShapeDtypeStruct(*shape) for shape in out_shape),
        in_specs=specs,
        out_specs=tuple(VMEM for _ in out_shape),
        scratch_shapes=[pltpu.VMEM(*shape) if isinstance(shape, tuple) else shape for shape in scratch],
        compiler_params=pltpu.CompilerParams(vmem_limit_bytes=(60 if hbm else 40) * 1024 * 1024),
        cost_estimate=pl.CostEstimate(flops=flops, bytes_accessed=2**21, transcendentals=0),
        name=name,
    )(*operands)


def swap_order(group):
    return sorted(range(1, group), key=lambda step: (-(step >> 1).bit_count(), step & 1, step))


def body(upstream, out_weight, query_rows, key_rows, value_rows, head_offsets):
    rows, width = query_rows.shape
    head_count = width // HEAD_SIZE
    devices = lax.axis_size("context")
    shards = lax.axis_size("heads")
    group = FIRST_SEGMENT // rows
    others = devices // group - 1
    half = rows // 2
    picked = rows // DILATION_RATE
    count = group * picked
    near = group * rows
    place = jnp.stack([lax.rem(lax.axis_index("context"), group), lax.axis_index("heads")])
    place = jnp.concatenate([place.astype(jnp.int32), head_offsets])

    def swap(values):
        result = list(values)
        for step in swap_order(group):
            pairs = [(source, source ^ step) for source in range(devices)]
            result[step] = lax.ppermute(values[step], "context", pairs)
        return result

    def segment_shift(value, shift):
        pairs = [(source, (source + shift * group) % devices) for source in range(devices)]
        return lax.ppermute(value, "context", pairs)

    upstreams = [upstream]
    for step in range(1, shards):
        pairs = [(source, (source + step) % shards) for source in range(shards)]
        upstreams.append(lax.ppermute(upstream, "heads", pairs))

    bf16, f32 = jnp.bfloat16, jnp.float32
    (sent,) = call(
        functools.partial(pack_kernel, head_count), "pack_rows",
        [((group, rows + half, PAIR), bf16)],
        [query_rows, key_rows, value_rows],
        [((rows, width), bf16)] * 3 + [pltpu.SemaphoreType.DMA((3,))], hbm=3,
    )
    groups = [list(range(first, first + group)) for first in range(0, devices, group)]
    sent = lax.all_to_all(sent, "context", 0, 0, axis_index_groups=groups)
    grads = swap(
        call(
            functools.partial(project_kernel, head_count, group, shards), "project_pack",
            [((half, PAIR), bf16)] * group,
            [place, out_weight, *upstreams],
            [((rows, width), bf16), ((head_count, half, PAIR), bf16)],
            flops=2 * rows * width * upstream.shape[1],
        )
    )
    keys, key_t, picks = call(
        functools.partial(gather_kernel, head_count), "gather_keys",
        [((near, PAIR), bf16), ((HEAD_SIZE, near), bf16), ((count, PAIR), bf16)],
        [place, sent, grads[0]],
    )
    other_picks = [segment_shift(picks, shift) for shift in range(1, others + 1)]
    extra, own_terms, other_terms = call(
        functools.partial(far_kernel, head_count, group, others), "picked_rows",
        [
            ((PAIR + STAT_ROWS, count), bf16),
            ((count, PAIR), f32), ((others * count, PAIR), f32),
        ],
        [place, keys, sent, picks, *other_picks, *grads],
        [((near + count * (1 + others), PAIR), bf16)] + [((count, PAIR), bf16)] * 2,
        flops=8 * near * count * PAIR,
    )
    back = [
        segment_shift(other_terms[(shift - 1) * count : shift * count], -shift)
        for shift in range(1, others + 1)
    ]
    steps = group // 2
    scratch = [
        ((2, near, rows), f32), ((2, near, rows), f32), ((2, near, 2 * rows), bf16),
    ]
    half_flops = 10 * near * near // 2 * PAIR
    acc, query_half = call(
        functools.partial(first_kernel, head_count), "first_rows",
        [((near, PAIR), f32), ((steps, half, PAIR), bf16)],
        [place, keys, key_t, sent, extra, *grads[:steps]], scratch, half_flops,
    )
    near_send = call(
        functools.partial(second_kernel, head_count, group - steps, others), "second_rows",
        [((rows + half, PAIR), bf16)] * group,
        [place, keys, key_t, sent, extra, acc, query_half, own_terms, *back, *grads[steps:]],
        [((near, PAIR), f32)] + scratch, half_flops,
    )
    return tuple(
        call(
            functools.partial(unpack_kernel, head_count, group), "unpack",
            [((rows, width), bf16)] * 3,
            [place, *swap(near_send)],
            [((group, rows + half, PAIR), bf16)],
        )
    )


def solution(mesh):
    return jax.shard_map(
        body,
        mesh=mesh,
        in_specs=(
            P(("context", "heads"), None),
            P("heads", None),
            P("context", "heads"),
            P("context", "heads"),
            P("context", "heads"),
            P(),
        ),
        out_specs=(P("context", "heads"), P("context", "heads"), P("context", "heads")),
        check_vma=False,
    )
```

time: 74.1 us -> 73.1 us (0.987)
  local copies, waits for them, and re-layouts: 3.71 us -> 0.67 us
  Pallas kernels: 27.4 us -> 29.8 us
  starting transfers between devices: 27.1 us -> 26.1 us
    ppermute x1, waiting for transfers between devices: 0.01 us -> 6.43 us  [body(): upstreams.append(lax.ppermute(upstream, 'heads', pairs))]
    ppermute x21 -> x14, waiting for transfers between devices: 14.6 us -> 8.26 us  [swap(): result[step] = lax.ppermute(values[step], 'context', pairs)]
    all_to_all x0 -> x1, starting transfers between devices: none -> 5.4 us  [body(): sent = lax.all_to_all(sent, 'context', 0, 0, axis_index_groups=groups)]
    ppermute x21 -> x14, starting transfers between devices: 18.5 us -> 13.9 us  [swap(): result[step] = lax.ppermute(values[step], 'context', pairs)]
    unnamed x12 -> x6, local copies, waits for them, and re-layouts: 3.71 us -> 0.67 us
    pallas_call x6 -> x7, Pallas kernels: 27.4 us -> 29.8 us  [call(): pl.pallas_call(kernel, out_shape=tuple((jax.ShapeDtypeStruct(*shape) for...]
    ppermute x1, starting transfers between devices: 3 us -> 1.56 us  [body(): upstreams.append(lax.ppermute(upstream, 'heads', pairs))]
  transfers between devices with their start and end apart: 24 -> 18, of which waited for: 12 -> 6; matrix products, arithmetic and copies ran while one was open for 0% -> 0% of each run, Pallas kernels for 18% -> 18%
where the time goes in v3:
time: 73.1 us; the launch traced here: 72.9 us
  Pallas kernels  29.8 us (41%)
  starting transfers between devices  26.1 us (36%)
  waiting for transfers between devices  15.4 us (21%)
  between operations  0.75 us (1%)
    pallas_call x7, Pallas kernels, call(): pl.pallas_call(kernel, out_shape=tuple((jax.ShapeDtypeStruct(*shape) for...  29.8 us
    ppermute x14, starting transfers between devices, swap(): result[step] = lax.ppermute(values[step], 'context', pairs)  13.9 us
    ppermute x14, waiting for transfers between devices, swap(): result[step] = lax.ppermute(values[step], 'context', pairs)  8.26 us
    ppermute x1, waiting for transfers between devices, body(): upstreams.append(lax.ppermute(upstream, 'heads', pairs))  6.43 us
    all_to_all x1, starting transfers between devices, body(): sent = lax.all_to_all(sent, 'context', 0, 0, axis_index_groups=groups)  5.4 us
    ppermute x2, starting transfers between devices, segment_shift(): return lax.ppermute(value, 'context', pairs)  5.25 us
    ppermute x1, starting transfers between devices, body(): upstreams.append(lax.ppermute(upstream, 'heads', pairs))  1.56 us
  transfers between devices with their start and end apart: 18, of which 6 were waited for; matrix products, arithmetic and copies ran while one was open for 0% of the time, Pallas kernels for 18%

profile of v3, /device:TPU:0, one launch (start us, length us, event | category | flops | bytes accessed | tf_op | source)
XLA Modules:
  0.0 72.9 jit_solution(2958513380006601667)
XLA Ops:
  0.6 2.3 %pack_rows.1 = bf16[8,384,128]{2,1,0:T(8,128)(2,1)} custom-call(bf16[256,512]{1,0:T(8,128)(2,1)} %query_hbm.1, bf16[256,512]{1,0:T(8,128)(2,1)} %key_hbm.1, bf16[256,512]{1,0:T(8,128)(2,1)} %value_hbm.1), custom_call_target="tpu_custom_call" | custom-call | bytes 2097152 | tf_op jit(solution)/shard_map/pack_rows/pallas_call | solution.py:315
  2.9 0.0 copy-start.1
  2.9 0.0 copy-start
  3.0 5.4 %all-to-all-start = ((bf16[8,384,128]{2,1,0:T(8,128)(2,1)}), bf16[8,384,128]{2,1,0:T(8,128)(2,1)S(1)}, u32[]{:S(2)}, u32[]{:S(2)}) async-start(bf16[8,384,128]{2,1,0:T(8,128)(2,1)} %pack_rows.1), calls=%async_computation | async-start | bytes 1572864 | tf_op jit(solution)/shard_map/all_to_all | solution.py:369
  8.4 0.0 copy-done.1
  8.4 1.6 %collective-permute-start = (bf16[128,1024]{1,0:T(8,128)(2,1)S(1)}, bf16[128,1024]{1,0:T(8,128)(2,1)S(1)}, u32[]{:S(2)}, u32[]{:S(2)}) collective-permute-start(bf16[128,1024]{1,0:T(8,128)(2,1)S(1)} %copy-done.1), channel_id=1, source_target_pairs={{0,1},{1,0},{2,3},{3,2},{4,5},{5,4},{6,7},{7,6},{8,9},{9,8},{10,11... | collective-permute-start | bytes 786440 | tf_op jit(solution)/shard_map/ppermute | solution.py:359
  9.9 0.0 copy-start.2
  9.9 0.7 copy-done.2
  10.6 0.1 pad_add_fusion.place_ref
  10.6 6.4 %collective-permute-done.refs_1_ = bf16[128,1024]{1,0:T(8,128)(2,1)S(1)} collective-permute-done((bf16[128,1024]{1,0:T(8,128)(2,1)S(1)}, bf16[128,1024]{1,0:T(8,128)(2,1)S(1)}, u32[]{:S(2)}, u32[]{:S(2)}) %collective-permute-start) | collective-permute-done | bytes 262176 | tf_op jit(solution)/shard_map/ppermute | solution.py:359
  17.1 0.0 copy-done
  17.1 1.5 %project_pack.1 = (bf16[128,128]{1,0:T(8,128)(2,1)S(1)}, bf16[128,128]{1,0:T(8,128)(2,1)S(1)}, bf16[128,128]{1,0:T(8,128)(2,1)S(1)}, bf16[128,128]{1,0:T(8,128)(...) custom-call(s32[18]{0:T(128)S(1)} %pad_add_fusion.place_ref, ...), custom_call_target="tpu_custom_call" | custom-call | flops 268435456 | bytes 2097152 | tf_op jit(solution)/shard_map/project_pack/pallas_call | solution.py:315
  18.6 0.1 collective-permute-start.2
  18.7 1.7 %collective-permute-start.3 = (bf16[128,128]{1,0:T(8,128)(2,1)S(1)}, bf16[128,128]{1,0:T(8,128)(2,1)S(1)}, u32[]{:S(2)}, u32[]{:S(2)}) collective-permute-start(bf16[128,128]{1,0:T(8,128)(2,1)S(1)} %get-tuple-element.32), channel_id=1, source_target_pairs={{0,4},{2,6},{4,0},{6,2},{8,12},{10,14},{12,8},{14,10},{16,20},{18,... | collective-permute-start | bytes 98312 | tf_op jit(solution)/shard_map/ppermute | solution.py:349
  20.4 0.1 collective-permute-start.4
  20.6 1.7 %collective-permute-start.5 = (bf16[128,128]{1,0:T(8,128)(2,1)S(1)}, bf16[128,128]{1,0:T(8,128)(2,1)S(1)}, u32[]{:S(2)}, u32[]{:S(2)}) collective-permute-start(bf16[128,128]{1,0:T(8,128)(2,1)S(1)} %get-tuple-element.34), channel_id=1, source_target_pairs={{0,8},{2,10},{4,12},{6,14},{8,0},{10,2},{12,4},{14,6},{16,24},{18,... | collective-permute-start | bytes 98312 | tf_op jit(solution)/shard_map/ppermute | solution.py:349
  22.2 0.0 collective-permute-start.6
  22.3 0.0 all-to-all-done.sent_ref
  22.3 0.8 %gather_keys.1 = (bf16[2048,128]{1,0:T(8,128)(2,1)S(1)}, bf16[64,2048]{1,0:T(8,128)(2,1)S(1)}, bf16[128,128]{1,0:T(8,128)(2,1)S(1)}) custom-call(s32[18]{0:T(128)S(1)} %pad_add_fusion.place_ref, bf16[8,384,128]{2,1,0:T(8,128)(2,1)S(1)} %all-to-all-done.sent_ref, bf16[128,128]{1,0:T(8,128)(2,1)S(1)} %get-tuple-element.27.after_ref.refs_1_.refs_0_), custom_call_target="tpu_custom_call" | custom-call | bytes 2097152 | tf_op jit(solution)/shard_map/gather_keys/pallas_call | solution.py:315
  23.1 0.0 collective-permute-done.2.refs_2_.refs_1_
  23.1 2.6 %collective-permute-start.7 = (bf16[128,128]{1,0:T(8,128)(2,1)S(1)}, bf16[128,128]{1,0:T(8,128)(2,1)S(1)}, u32[]{:S(2)}, u32[]{:S(2)}) collective-permute-start(bf16[128,128]{1,0:T(8,128)(2,1)S(1)} %get-tuple-element.36), channel_id=1, source_target_pairs={{0,12},{2,14},{4,8},{6,10},{8,4},{10,6},{12,0},{14,2},{16,28},{18,... | collective-permute-start | bytes 98312 | tf_op jit(solution)/shard_map/ppermute | solution.py:349
  25.7 0.0 collective-permute-done.3.refs_3_.refs_2_
  25.7 0.1 collective-permute-start.8
  25.8 0.0 collective-permute-done.4.refs_4_.refs_3_
  25.8 2.6 %collective-permute-start.1 = (bf16[128,128]{1,0:T(8,128)(2,1)S(1)}, bf16[128,128]{1,0:T(8,128)(2,1)S(1)}, u32[]{:S(2)}, u32[]{:S(2)}) collective-permute-start(bf16[128,128]{1,0:T(8,128)(2,1)S(1)} %get-tuple-element.30.picks_ref), channel_id=1, source_target_pairs={{0,16},{2,18},{4,20},{6,22},{8,24},{10,26},{12,28},{14,30},{16,0},... | collective-permute-start | bytes 98312 | tf_op jit(solution)/shard_map/ppermute | solution.py:354
  28.4 0.0 collective-permute-done.5.refs_5_.refs_1_
  28.4 0.0 collective-permute-done.6.refs_6_.refs_2_
  28.4 0.0 collective-permute-done.7.refs_7_.refs_3_
  28.4 1.5 %collective-permute-done.8.refs_8_.refs_4_ = bf16[128,128]{1,0:T(8,128)(2,1)S(1)} collective-permute-done((bf16[128,128]{1,0:T(8,128)(2,1)S(1)}, bf16[128,128]{1,0:T(8,128)(2,1)S(1)}, u32[]{:S(2)}, u32[]{:S(2)}) %collective-permute-start.8) | collective-permute-done | bytes 32800 | tf_op jit(solution)/shard_map/ppermute | solution.py:349
  29.9 0.7 collective-permute-done.1.refs_0_
  30.7 1.9 %picked_rows.1 = (bf16[144,128]{1,0:T(8,128)(2,1)S(1)}, f32[128,128]{1,0:T(8,128)S(1)}, f32[128,128]{1,0:T(8,128)S(1)}) custom-call(s32[18]{0:T(128)S(1)} %pad_add_fusion.place_ref, bf16[2048,128]{1,0:T(8,128)(2,1)S(1)} %get-tuple-element.28.near_ref.keys_ref, bf16[8,384,128]{2,1,0:T(8,128)(2,1)S(1)} %all-to-all-done.sent_ref, ...), custom_call_target="tpu_custom_call" | custom-call | flops 268435456 | bytes 2097152 | tf_op jit(solution)/shard_map/picked_rows/pallas_call | solution.py:315
  32.5 2.7 %collective-permute-start.9 = (f32[128,128]{1,0:T(8,128)S(1)}, f32[128,128]{1,0:T(8,128)S(1)}, u32[]{:S(2)}, u32[]{:S(2)}) collective-permute-start(f32[128,128]{1,0:T(8,128)S(1)} %get-tuple-element.42), channel_id=1, source_target_pairs={{0,16},{2,18},{4,20},{6,22},{8,24},{10,26},{12,28},{14,30},{16,0},... | collective-permute-start | bytes 196616 | tf_op jit(solution)/shard_map/ppermute | solution.py:354
  35.2 10.6 %first_rows.1 = (f32[2048,128]{1,0:T(8,128)S(1)}, bf16[4,128,128]{2,1,0:T(8,128)(2,1)S(1)}) custom-call(s32[18]{0:T(128)S(1)} %pad_add_fusion.place_ref, bf16[2048,128]{1,0:T(8,128)(2,1)S(1)} %get-tuple-element.28.near_ref.keys_ref, bf16[64,2048]{1,0:T(8,128)(2,1)S(1)} %get-tuple-element.29.key_t_ref, bf16[8,384,128]{2,1,0:T(8,128)(2,1)S(1)} %all-to-all-done.sent_ref, ...), custom_call_target="tpu_custom_call" | custom-call | flops 2684354560 | bytes 2097152 | tf_op jit(solution)/shard_map/first_rows/pallas_call | solution.py:315
  45.8 0.0 collective-permute-done.9.refs_0_
  45.8 10.9 %second_rows.1 = (bf16[384,128]{1,0:T(8,128)(2,1)S(1)}, bf16[384,128]{1,0:T(8,128)(2,1)S(1)}, bf16[384,128]{1,0:T(8,128)(2,1)S(1)}, bf16[384,128]{1,0:T(8,128)(2...) custom-call(s32[18]{0:T(128)S(1)} %pad_add_fusion.place_ref, ...), custom_call_target="tpu_custom_call" | custom-call | flops 2684354560 | bytes 2097152 | tf_op jit(solution)/shard_map/second_rows/pallas_call | solution.py:315
  56.7 0.1 collective-permute-start.10
  56.7 1.7 %collective-permute-start.11 = (bf16[384,128]{1,0:T(8,128)(2,1)S(1)}, bf16[384,128]{1,0:T(8,128)(2,1)S(1)}, u32[]{:S(2)}, u32[]{:S(2)}) collective-permute-start(bf16[384,128]{1,0:T(8,128)(2,1)S(1)} %get-tuple-element.45), channel_id=1, source_target_pairs={{0,4},{2,6},{4,0},{6,2},{8,12},{10,14},{12,8},{14,10},{16,20},{18,... | collective-permute-start | bytes 294920 | tf_op jit(solution)/shard_map/ppermute | solution.py:349
  58.4 0.2 collective-permute-start.12
  58.6 1.9 %collective-permute-start.13 = (bf16[384,128]{1,0:T(8,128)(2,1)S(1)}, bf16[384,128]{1,0:T(8,128)(2,1)S(1)}, u32[]{:S(2)}, u32[]{:S(2)}) collective-permute-start(bf16[384,128]{1,0:T(8,128)(2,1)S(1)} %get-tuple-element.47), channel_id=1, source_target_pairs={{0,8},{2,10},{4,12},{6,14},{8,0},{10,2},{12,4},{14,6},{16,24},{18,... | collective-permute-start | bytes 294920 | tf_op jit(solution)/shard_map/ppermute | solution.py:349
  60.5 0.0 collective-permute-start.14
  60.5 0.0 collective-permute-done.10.refs_1_
  60.5 2.8 %collective-permute-start.15 = (bf16[384,128]{1,0:T(8,128)(2,1)S(1)}, bf16[384,128]{1,0:T(8,128)(2,1)S(1)}, u32[]{:S(2)}, u32[]{:S(2)}) collective-permute-start(bf16[384,128]{1,0:T(8,128)(2,1)S(1)} %get-tuple-element.49), channel_id=1, source_target_pairs={{0,12},{2,14},{4,8},{6,10},{8,4},{10,6},{12,0},{14,2},{16,28},{18,... | collective-permute-start | bytes 294920 | tf_op jit(solution)/shard_map/ppermute | solution.py:349
  63.3 0.0 collective-permute-done.11.refs_2_
  63.3 0.9 %collective-permute-start.16 = (bf16[384,128]{1,0:T(8,128)(2,1)S(1)}, bf16[384,128]{1,0:T(8,128)(2,1)S(1)}, u32[]{:S(2)}, u32[]{:S(2)}) collective-permute-start(bf16[384,128]{1,0:T(8,128)(2,1)S(1)} %get-tuple-element.50), channel_id=1, source_target_pairs={{0,14},{2,12},{4,10},{6,8},{8,6},{10,4},{12,2},{14,0},{16,30},{18,... | collective-permute-start | bytes 294920 | tf_op jit(solution)/shard_map/ppermute | solution.py:349
  64.2 0.0 collective-permute-done.12.refs_3_
  64.2 0.0 collective-permute-done.13.refs_4_
  64.2 1.6 %collective-permute-done.14.refs_5_ = bf16[384,128]{1,0:T(8,128)(2,1)S(1)} collective-permute-done((bf16[384,128]{1,0:T(8,128)(2,1)S(1)}, bf16[384,128]{1,0:T(8,128)(2,1)S(1)}, u32[]{:S(2)}, u32[]{:S(2)}) %collective-permute-start.14) | collective-permute-done | bytes 98336 | tf_op jit(solution)/shard_map/ppermute | solution.py:349
  65.7 3.6 %collective-permute-done.15.refs_6_ = bf16[384,128]{1,0:T(8,128)(2,1)S(1)} collective-permute-done((bf16[384,128]{1,0:T(8,128)(2,1)S(1)}, bf16[384,128]{1,0:T(8,128)(2,1)S(1)}, u32[]{:S(2)}, u32[]{:S(2)}) %collective-permute-start.15) | collective-permute-done | bytes 98336 | tf_op jit(solution)/shard_map/ppermute | solution.py:349
  69.3 1.6 %collective-permute-done.16.refs_7_ = bf16[384,128]{1,0:T(8,128)(2,1)S(1)} collective-permute-done((bf16[384,128]{1,0:T(8,128)(2,1)S(1)}, bf16[384,128]{1,0:T(8,128)(2,1)S(1)}, u32[]{:S(2)}, u32[]{:S(2)}) %collective-permute-start.16) | collective-permute-done | bytes 98336 | tf_op jit(solution)/shard_map/ppermute | solution.py:349
  70.9 1.9 %unpack.1 = (bf16[256,512]{1,0:T(8,128)(2,1)}, bf16[256,512]{1,0:T(8,128)(2,1)}, bf16[256,512]{1,0:T(8,128)(2,1)}) custom-call(s32[18]{0:T(128)S(1)} %pad_add_fusion.place_ref, bf16[384,128]{1,0:T(8,128)(2,1)S(1)} %get-tuple-element.43.refs_0_, bf16[384,128]{1,0:T(8,128)(2,1)S(1)} %collective-permute-done.10.refs_1_, ...), custom_call_target="tpu_custom_call" | custom-call | bytes 2097152 | tf_op jit(solution)/shard_map/unpack/pallas_call | solution.py:315
Async XLA Ops:
  2.9 5.4 %copy-start.1 = (bf16[128,1024]{1,0:T(8,128)(2,1)S(1)}, bf16[128,1024]{1,0:T(8,128)(2,1)}, u32[]{:S(2)}) copy-start(bf16[128,1024]{1,0:T(8,128)(2,1)} %refs_0_.1) | copy-start | bytes 786436
  2.9 14.1 %copy-start = (bf16[512,1024]{1,0:T(8,128)(2,1)S(1)}, bf16[512,1024]{1,0:T(8,128)(2,1)}, u32[]{:S(2)}) copy-start(bf16[512,1024]{1,0:T(8,128)(2,1)} %weight_ref.1) | copy-start | bytes 3145732
  3.0 19.3 %all-to-all-start = ((bf16[8,384,128]{2,1,0:T(8,128)(2,1)}), bf16[8,384,128]{2,1,0:T(8,128)(2,1)S(1)}, u32[]{:S(2)}, u32[]{:S(2)}) async-start(bf16[8,384,128]{2,1,0:T(8,128)(2,1)} %pack_rows.1), calls=%async_computation | async-start | bytes 1572864 | tf_op jit(solution)/shard_map/all_to_all | solution.py:369
  8.4 8.7 %collective-permute-start = (bf16[128,1024]{1,0:T(8,128)(2,1)S(1)}, bf16[128,1024]{1,0:T(8,128)(2,1)S(1)}, u32[]{:S(2)}, u32[]{:S(2)}) collective-permute-start(bf16[128,1024]{1,0:T(8,128)(2,1)S(1)} %copy-done.1), channel_id=1, source_target_pairs={{0,1},{1,0},{2,3},{3,2},{4,5},{5,4},{6,7},{7,6},{8,9},{9,8},{10,11... | collective-permute-start | bytes 786440 | tf_op jit(solution)/shard_map/ppermute | solution.py:359
  9.9 0.7 copy-start.2
  18.6 4.5 %collective-permute-start.2 = (bf16[128,128]{1,0:T(8,128)(2,1)S(1)}, bf16[128,128]{1,0:T(8,128)(2,1)S(1)}, u32[]{:S(2)}, u32[]{:S(2)}) collective-permute-start(bf16[128,128]{1,0:T(8,128)(2,1)S(1)} %get-tuple-element.31), channel_id=1, source_target_pairs={{0,2},{2,0},{4,6},{6,4},{8,10},{10,8},{12,14},{14,12},{16,18},{18,... | collective-permute-start | bytes 98312 | tf_op jit(solution)/shard_map/ppermute | solution.py:349
  18.7 7.0 %collective-permute-start.3 = (bf16[128,128]{1,0:T(8,128)(2,1)S(1)}, bf16[128,128]{1,0:T(8,128)(2,1)S(1)}, u32[]{:S(2)}, u32[]{:S(2)}) collective-permute-start(bf16[128,128]{1,0:T(8,128)(2,1)S(1)} %get-tuple-element.32), channel_id=1, source_target_pairs={{0,4},{2,6},{4,0},{6,2},{8,12},{10,14},{12,8},{14,10},{16,20},{18,... | collective-permute-start | bytes 98312 | tf_op jit(solution)/shard_map/ppermute | solution.py:349
  20.4 5.4 %collective-permute-start.4 = (bf16[128,128]{1,0:T(8,128)(2,1)S(1)}, bf16[128,128]{1,0:T(8,128)(2,1)S(1)}, u32[]{:S(2)}, u32[]{:S(2)}) collective-permute-start(bf16[128,128]{1,0:T(8,128)(2,1)S(1)} %get-tuple-element.33), channel_id=1, source_target_pairs={{0,6},{2,4},{4,2},{6,0},{8,14},{10,12},{12,10},{14,8},{16,22},{18,... | collective-permute-start | bytes 98312 | tf_op jit(solution)/shard_map/ppermute | solution.py:349
  20.6 7.9 %collective-permute-start.5 = (bf16[128,128]{1,0:T(8,128)(2,1)S(1)}, bf16[128,128]{1,0:T(8,128)(2,1)S(1)}, u32[]{:S(2)}, u32[]{:S(2)}) collective-permute-start(bf16[128,128]{1,0:T(8,128)(2,1)S(1)} %get-tuple-element.34), channel_id=1, source_target_pairs={{0,8},{2,10},{4,12},{6,14},{8,0},{10,2},{12,4},{14,6},{16,24},{18,... | collective-permute-start | bytes 98312 | tf_op jit(solution)/shard_map/ppermute | solution.py:349
  22.2 6.2 %collective-permute-start.6 = (bf16[128,128]{1,0:T(8,128)(2,1)S(1)}, bf16[128,128]{1,0:T(8,128)(2,1)S(1)}, u32[]{:S(2)}, u32[]{:S(2)}) collective-permute-start(bf16[128,128]{1,0:T(8,128)(2,1)S(1)} %get-tuple-element.35), channel_id=1, source_target_pairs={{0,10},{2,8},{4,14},{6,12},{8,2},{10,0},{12,6},{14,4},{16,26},{18,... | collective-permute-start | bytes 98312 | tf_op jit(solution)/shard_map/ppermute | solution.py:349
  23.1 5.4 %collective-permute-start.7 = (bf16[128,128]{1,0:T(8,128)(2,1)S(1)}, bf16[128,128]{1,0:T(8,128)(2,1)S(1)}, u32[]{:S(2)}, u32[]{:S(2)}) collective-permute-start(bf16[128,128]{1,0:T(8,128)(2,1)S(1)} %get-tuple-element.36), channel_id=1, source_target_pairs={{0,12},{2,14},{4,8},{6,10},{8,4},{10,6},{12,0},{14,2},{16,28},{18,... | collective-permute-start | bytes 98312 | tf_op jit(solution)/shard_map/ppermute | solution.py:349
  25.7 4.2 %collective-permute-start.8 = (bf16[128,128]{1,0:T(8,128)(2,1)S(1)}, bf16[128,128]{1,0:T(8,128)(2,1)S(1)}, u32[]{:S(2)}, u32[]{:S(2)}) collective-permute-start(bf16[128,128]{1,0:T(8,128)(2,1)S(1)} %get-tuple-element.37), channel_id=1, source_target_pairs={{0,14},{2,12},{4,10},{6,8},{8,6},{10,4},{12,2},{14,0},{16,30},{18,... | collective-permute-start | bytes 98312 | tf_op jit(solution)/shard_map/ppermute | solution.py:349
  25.8 4.8 %collective-permute-start.1 = (bf16[128,128]{1,0:T(8,128)(2,1)S(1)}, bf16[128,128]{1,0:T(8,128)(2,1)S(1)}, u32[]{:S(2)}, u32[]{:S(2)}) collective-permute-start(bf16[128,128]{1,0:T(8,128)(2,1)S(1)} %get-tuple-element.30.picks_ref), channel_id=1, source_target_pairs={{0,16},{2,18},{4,20},{6,22},{8,24},{10,26},{12,28},{14,30},{16,0},... | collective-permute-start | bytes 98312 | tf_op jit(solution)/shard_map/ppermute | solution.py:354
  32.5 13.2 %collective-permute-start.9 = (f32[128,128]{1,0:T(8,128)S(1)}, f32[128,128]{1,0:T(8,128)S(1)}, u32[]{:S(2)}, u32[]{:S(2)}) collective-permute-start(f32[128,128]{1,0:T(8,128)S(1)} %get-tuple-element.42), channel_id=1, source_target_pairs={{0,16},{2,18},{4,20},{6,22},{8,24},{10,26},{12,28},{14,30},{16,0},... | collective-permute-start | bytes 196616 | tf_op jit(solution)/shard_map/ppermute | solution.py:354
  56.7 3.9 %collective-permute-start.10 = (bf16[384,128]{1,0:T(8,128)(2,1)S(1)}, bf16[384,128]{1,0:T(8,128)(2,1)S(1)}, u32[]{:S(2)}, u32[]{:S(2)}) collective-permute-start(bf16[384,128]{1,0:T(8,128)(2,1)S(1)} %get-tuple-element.44), channel_id=1, source_target_pairs={{0,2},{2,0},{4,6},{6,4},{8,10},{10,8},{12,14},{14,12},{16,18},{18,... | collective-permute-start | bytes 294920 | tf_op jit(solution)/shard_map/ppermute | solution.py:349
  56.7 6.5 %collective-permute-start.11 = (bf16[384,128]{1,0:T(8,128)(2,1)S(1)}, bf16[384,128]{1,0:T(8,128)(2,1)S(1)}, u32[]{:S(2)}, u32[]{:S(2)}) collective-permute-start(bf16[384,128]{1,0:T(8,128)(2,1)S(1)} %get-tuple-element.45), channel_id=1, source_target_pairs={{0,4},{2,6},{4,0},{6,2},{8,12},{10,14},{12,8},{14,10},{16,20},{18,... | collective-permute-start | bytes 294920 | tf_op jit(solution)/shard_map/ppermute | solution.py:349
  58.4 5.7 %collective-permute-start.12 = (bf16[384,128]{1,0:T(8,128)(2,1)S(1)}, bf16[384,128]{1,0:T(8,128)(2,1)S(1)}, u32[]{:S(2)}, u32[]{:S(2)}) collective-permute-start(bf16[384,128]{1,0:T(8,128)(2,1)S(1)} %get-tuple-element.46), channel_id=1, source_target_pairs={{0,6},{2,4},{4,2},{6,0},{8,14},{10,12},{12,10},{14,8},{16,22},{18,... | collective-permute-start | bytes 294920 | tf_op jit(solution)/shard_map/ppermute | solution.py:349
  58.6 5.6 %collective-permute-start.13 = (bf16[384,128]{1,0:T(8,128)(2,1)S(1)}, bf16[384,128]{1,0:T(8,128)(2,1)S(1)}, u32[]{:S(2)}, u32[]{:S(2)}) collective-permute-start(bf16[384,128]{1,0:T(8,128)(2,1)S(1)} %get-tuple-element.47), channel_id=1, source_target_pairs={{0,8},{2,10},{4,12},{6,14},{8,0},{10,2},{12,4},{14,6},{16,24},{18,... | collective-permute-start | bytes 294920 | tf_op jit(solution)/shard_map/ppermute | solution.py:349
  60.5 5.2 %collective-permute-start.14 = (bf16[384,128]{1,0:T(8,128)(2,1)S(1)}, bf16[384,128]{1,0:T(8,128)(2,1)S(1)}, u32[]{:S(2)}, u32[]{:S(2)}) collective-permute-start(bf16[384,128]{1,0:T(8,128)(2,1)S(1)} %get-tuple-element.48), channel_id=1, source_target_pairs={{0,10},{2,8},{4,14},{6,12},{8,2},{10,0},{12,6},{14,4},{16,26},{18,... | collective-permute-start | bytes 294920 | tf_op jit(solution)/shard_map/ppermute | solution.py:349
  60.5 8.8 %collective-permute-start.15 = (bf16[384,128]{1,0:T(8,128)(2,1)S(1)}, bf16[384,128]{1,0:T(8,128)(2,1)S(1)}, u32[]{:S(2)}, u32[]{:S(2)}) collective-permute-start(bf16[384,128]{1,0:T(8,128)(2,1)S(1)} %get-tuple-element.49), channel_id=1, source_target_pairs={{0,12},{2,14},{4,8},{6,10},{8,4},{10,6},{12,0},{14,2},{16,28},{18,... | collective-permute-start | bytes 294920 | tf_op jit(solution)/shard_map/ppermute | solution.py:349
  63.3 7.7 %collective-permute-start.16 = (bf16[384,128]{1,0:T(8,128)(2,1)S(1)}, bf16[384,128]{1,0:T(8,128)(2,1)S(1)}, u32[]{:S(2)}, u32[]{:S(2)}) collective-permute-start(bf16[384,128]{1,0:T(8,128)(2,1)S(1)} %get-tuple-element.50), channel_id=1, source_target_pairs={{0,14},{2,12},{4,10},{6,8},{8,6},{10,4},{12,2},{14,0},{16,30},{18,... | collective-permute-start | bytes 294920 | tf_op jit(solution)/shard_map/ppermute | solution.py:349

commit v4 on v3

--- a/solution.py
+++ b/solution.py
@@ -81,8 +81,33 @@
     return jnp.concatenate([block[:half], block[half:]], 1)
 
 
-def pack_kernel(head_count, query_hbm, key_hbm, value_hbm, *refs):
-    out_ref, query_ref, key_ref, value_ref, sems = refs
+def swap_steps(group):
+    if group == 8:
+        return [(6, 6), (2, 4), (7, 1), (4, 2), (1, 7), (3, 5), (5, 3)]
+    return [(bits, bits) for bits in range(1, group)]
+
+
+def target_of(place, step):
+    return lax.bitwise_xor(place, jnp.where(lax.rem(place, 2) == 1, step[1], step[0]))
+
+
+def source_of(place, step):
+    odd = lax.rem(place + step[0], 2) == 1
+    return lax.bitwise_xor(place, jnp.where(odd, step[1], step[0]))
+
+
+def send_out(place, head_count, stage_ref, out_refs):
+    out_refs[0][...] = stage_ref[lax.rem(place, head_count)]
+    for step, out_ref in zip(swap_steps(len(out_refs)), out_refs[1:]):
+        out_ref[...] = stage_ref[lax.rem(target_of(place, step), head_count)]
+
+
+def places_of(place, group):
+    return [place] + [source_of(place, step) for step in swap_steps(group)]
+
+
+def pack_kernel(head_count, group, place_ref, query_hbm, key_hbm, value_hbm, *refs):
+    out_refs, (query_ref, key_ref, value_ref, stage_ref, sems) = refs[:group], refs[group:]
     rows = query_ref.shape[0]
     copies = [
         pltpu.make_async_copy(source, target, sems.at[index])
@@ -95,11 +120,11 @@
     for copy in copies:
         copy.wait()
     for head in range(head_count):
-        pair = jnp.concatenate([head_columns(key_ref, head), head_columns(value_ref, head)], 1)
-        query = side_by_side(head_columns(query_ref, head))
-        for place in range(head, out_ref.shape[0], head_count):
-            out_ref[place, :rows, :] = pair
-            out_ref[place, rows:, :] = query
+        stage_ref[head, :rows, :] = jnp.concatenate(
+            [head_columns(key_ref, head), head_columns(value_ref, head)], 1
+        )
+        stage_ref[head, rows:, :] = side_by_side(head_columns(query_ref, head))
+    send_out(place_ref[0], head_count, stage_ref, out_refs)
 
 
 def project_kernel(head_count, group, shards, place_ref, weight_ref, *refs):
@@ -114,30 +139,27 @@
         ).astype(jnp.bfloat16)
     for head in range(head_count):
         stage_ref[head] = side_by_side(head_columns(grad_ref, head))
-    for step, out_ref in enumerate(out_refs):
-        out_ref[...] = stage_ref[lax.rem(lax.bitwise_xor(place_ref[0], step), head_count)]
-
-
-def own_offset(head_count, place_ref):
-    return place_ref[2 + place_ref[1] * head_count + lax.rem(place_ref[0], head_count)]
-
-
-def gather_kernel(head_count, place_ref, sent_ref, after_ref, keys_out, key_t_out, picks_out):
-    group, sent_rows, _ = sent_ref.shape
+    send_out(place_ref[0], head_count, stage_ref, out_refs)
+
+
+def own_offset(head_count, place_ref, offset_ref):
+    return offset_ref[place_ref[1] * head_count + lax.rem(place_ref[0], head_count)]
+
+
+def gather_kernel(head_count, group, place_ref, offset_ref, *refs):
+    sent_refs, refs = refs[:group], refs[group + 1 :]
+    keys_out, key_t_out, queries_out, picks_out = refs
     rows = keys_out.shape[0] // group
     picked = rows // DILATION_RATE
-    pick = pick_matrix(own_offset(head_count, place_ref), picked, rows)
-    for step in range(group):
-        pair = sent_ref[lax.bitwise_xor(place_ref[0], step), :rows, :]
-        keys_out[step * rows : (step + 1) * rows, :] = pair
-        picks_out[step * picked : (step + 1) * picked, :] = dot_nn(pick, pair).astype(jnp.bfloat16)
-        key_t_out[:, step * rows : (step + 1) * rows] = (
-            pair.astype(jnp.float32).T[:HEAD_SIZE].astype(jnp.bfloat16)
-        )
-
-
-def queries_from(sent_ref, place_ref, step, rows):
-    return sent_ref.at[lax.bitwise_xor(place_ref[0], step), rows:]
+    pick = pick_matrix(own_offset(head_count, place_ref, offset_ref), picked, rows)
+    for place, sent_ref in zip(places_of(place_ref[0], group), sent_refs):
+        pair = sent_ref[:rows, :]
+        keys_out[pl.ds(pl.multiple_of(place * rows, rows), rows), :] = pair
+        picks_out[pl.ds(pl.multiple_of(place * picked, picked), picked), :] = dot_nn(
+            pick, pair
+        ).astype(jnp.bfloat16)
+        queries_out[place] = sent_ref[rows:, :]
+    key_t_out[...] = keys_out[...].astype(jnp.float32).T[:HEAD_SIZE].astype(jnp.bfloat16)
 
 
 def query_and_grad(query_ref, grad_ref):
@@ -159,21 +181,25 @@
     )
 
 
-def far_kernel(head_count, group, others, place_ref, near_ref, sent_ref, picks_ref, *refs):
+def far_kernel(
+    head_count, group, others, place_ref, offset_ref, near_ref, queries_ref, picks_ref, *refs
+):
     other_refs, refs = refs[:others], refs[others:]
     grad_refs, refs = refs[:group], refs[group:]
-    extra_out, own_out, other_out, keys_ref, query_ref, grad_ref = refs
+    extra_out, own_out, other_out, grads_out, keys_ref, query_ref, grad_ref = refs
     near = near_ref.shape[0]
     rows = near // group
     picked = rows // DILATION_RATE
     count = group * picked
     far = count * (1 + others)
-    pick = pick_matrix(own_offset(head_count, place_ref), picked, rows)
+    pick = pick_matrix(own_offset(head_count, place_ref, offset_ref), picked, rows)
     keys_ref[:near, :] = near_ref[...]
     for index, ref in enumerate([picks_ref, *other_refs]):
         keys_ref[near + index * count : near + (index + 1) * count, :] = ref[...]
+    for place, ref in zip(places_of(place_ref[0], group), grad_refs):
+        grads_out[place] = ref[...]
     for step in range(group):
-        query, grad = query_and_grad(queries_from(sent_ref, place_ref, step, rows), grad_refs[step])
+        query, grad = query_and_grad(queries_ref.at[step], grads_out.at[step])
         span = slice(step * picked, (step + 1) * picked)
         query_ref[span, :] = dot_nn(pick, query).astype(jnp.bfloat16)
         grad_ref[span, :] = dot_nn(pick, grad).astype(jnp.bfloat16)
@@ -246,40 +272,39 @@
     return jnp.concatenate([query_grad[:half], query_grad[half:]], 1)
 
 
-def first_kernel(head_count, place_ref, keys_ref, key_t_ref, sent_ref, extra_ref, *refs):
-    acc_ref, query_out, *scratch = refs[-5:]
-    grad_refs = refs[:-5]
+def first_kernel(
+    head_count, steps, place_ref, offset_ref, keys_ref, key_t_ref, queries_ref, grads_ref,
+    extra_ref, acc_ref, query_out, *scratch,
+):
     rows = scratch[0].shape[2]
-    offset = own_offset(head_count, place_ref)
+    offset = own_offset(head_count, place_ref, offset_ref)
     acc_ref[...] = jnp.zeros_like(acc_ref)
-    for step, grad_ref in enumerate(grad_refs):
+    for step in range(steps):
         query_out[step] = near_block(
             step * (rows // DILATION_RATE), offset, keys_ref, key_t_ref,
-            queries_from(sent_ref, place_ref, step, rows), grad_ref, extra_ref,
+            queries_ref.at[step], grads_ref.at[step], extra_ref,
             *[ref.at[step % 2] for ref in scratch], acc_ref,
         )
 
 
 def second_kernel(
-    head_count, steps, others, place_ref, keys_ref, key_t_ref, sent_ref, extra_ref, start_ref,
-    query_ref, own_ref, *refs,
+    head_count, steps, others, place_ref, offset_ref, keys_ref, key_t_ref, queries_ref, grads_ref,
+    extra_ref, start_ref, query_ref, own_ref, *refs,
 ):
     back_refs, refs = refs[:others], refs[others:]
-    grad_refs, refs = refs[:steps], refs[steps:]
     rows = query_ref.shape[1] * 2
     group = keys_ref.shape[0] // rows
     out_refs, refs = refs[:group], refs[group:]
-    acc_ref, *scratch = refs
+    acc_ref, stage_ref, *scratch = refs
     count = extra_ref.shape[1]
     picked = count // group
-    offset = own_offset(head_count, place_ref)
+    offset = own_offset(head_count, place_ref, offset_ref)
     acc_ref[...] = start_ref[...]
-    for step, grad_ref in enumerate(grad_refs):
-        place = group - steps + step
-        out_refs[place][rows:, :] = near_block(
+    for place in range(group - steps, group):
+        stage_ref[place, rows:, :] = near_block(
             place * picked, offset, keys_ref, key_t_ref,
-            queries_from(sent_ref, place_ref, place, rows), grad_ref, extra_ref,
-            *[ref.at[step % 2] for ref in scratch], acc_ref,
+            queries_ref.at[place], grads_ref.at[place], extra_ref,
+            *[ref.at[place % 2] for ref in scratch], acc_ref,
         )
     terms = own_ref[...]
     for back_ref in back_refs:
@@ -290,9 +315,10 @@
         spread = spread_matrix(offset, place * picked, count, rows, 1)
         placed = dot_nn(jnp.concatenate([spread, spread], 1), terms)
         summed = acc_ref[place * rows : (place + 1) * rows, :] * factor + placed
-        out_refs[place][:rows, :] = summed.astype(jnp.bfloat16)
+        stage_ref[place, :rows, :] = summed.astype(jnp.bfloat16)
         if place < group - steps:
-            out_refs[place][rows:, :] = query_ref[place]
+            stage_ref[place, rows:, :] = query_ref[place]
+    send_out(place_ref[0], group, stage_ref, out_refs)
 
 
 def unpack_kernel(head_count, group, place_ref, *refs):
@@ -300,8 +326,8 @@
     query_out, key_out, value_out, stage_ref = refs
     rows = query_out.shape[0]
     half = rows // 2
-    for step, near_ref in enumerate(near_refs):
-        stage_ref[lax.bitwise_xor(place_ref[0], step)] = near_ref[...]
+    for place, near_ref in zip(places_of(place_ref[0], group), near_refs):
+        stage_ref[place] = near_ref[...]
     for head in range(head_count):
         columns = slice(head * HEAD_SIZE, (head + 1) * HEAD_SIZE)
         key_out[:, columns] = stage_ref[head, :rows, :HEAD_SIZE]
@@ -310,22 +336,19 @@
         query_out[half:, columns] = stage_ref[head, rows:, HEAD_SIZE:]
 
 
-def call(kernel, name, out_shape, operands, scratch=(), flops=0, hbm=0):
-    specs = [ANY] * hbm if hbm else [SMEM] + [VMEM] * (len(operands) - 1)
+def call(kernel, name, out_shape, scalars, operands, scratch=(), flops=0, space=VMEM, limit=40):
     return pl.pallas_call(
         kernel,
         out_shape=tuple(jax.ShapeDtypeStruct(*shape) for shape in out_shape),
-        in_specs=specs,
+        in_specs=[SMEM] * len(scalars) + [space] * len(operands),
         out_specs=tuple(VMEM for _ in out_shape),
-        scratch_shapes=[pltpu.VMEM(*shape) if isinstance(shape, tuple) else shape for shape in scratch],
-        compiler_params=pltpu.CompilerParams(vmem_limit_bytes=(60 if hbm else 40) * 1024 * 1024),
+        scratch_shapes=[
+            pltpu.VMEM(*shape) if isinstance(shape, tuple) else shape for shape in scratch
+        ],
+        compiler_params=pltpu.CompilerParams(vmem_limit_bytes=limit * 1024 * 1024),
         cost_estimate=pl.CostEstimate(flops=flops, bytes_accessed=2**21, transcendentals=0),
         name=name,
-    )(*operands)
-
-
-def swap_order(group):
-    return sorted(range(1, group), key=lambda step: (-(step >> 1).bit_count(), step & 1, step))
+    )(*scalars, *operands)
 
 
 def body(upstream, out_weight, query_rows, key_rows, value_rows, head_offsets):
@@ -339,14 +362,16 @@
     picked = rows // DILATION_RATE
     count = group * picked
     near = group * rows
-    place = jnp.stack([lax.rem(lax.axis_index("context"), group), lax.axis_index("heads")])
-    place = jnp.concatenate([place.astype(jnp.int32), head_offsets])
+    place = jnp.stack(
+        [lax.rem(lax.axis_index("context"), group), lax.axis_index("heads")]
+    ).astype(jnp.int32)
+    scalars = [place, head_offsets]
 
     def swap(values):
-        result = list(values)
-        for step in swap_order(group):
-            pairs = [(source, source ^ step) for source in range(devices)]
-            result[step] = lax.ppermute(values[step], "context", pairs)
+        result = [values[0]]
+        for step, value in zip(swap_steps(group), values[1:]):
+            pairs = [(source, source ^ step[source % 2]) for source in range(devices)]
+            result.append(lax.ppermute(value, "context", pairs))
         return result
 
     def segment_shift(value, shift):
@@ -359,36 +384,41 @@
         upstreams.append(lax.ppermute(upstream, "heads", pairs))
 
     bf16, f32 = jnp.bfloat16, jnp.float32
-    (sent,) = call(
-        functools.partial(pack_kernel, head_count), "pack_rows",
-        [((group, rows + half, PAIR), bf16)],
-        [query_rows, key_rows, value_rows],
-        [((rows, width), bf16)] * 3 + [pltpu.SemaphoreType.DMA((3,))], hbm=3,
-    )
-    groups = [list(range(first, first + group)) for first in range(0, devices, group)]
-    sent = lax.all_to_all(sent, "context", 0, 0, axis_index_groups=groups)
+    sent = swap(
+        call(
+            functools.partial(pack_kernel, head_count, group), "pack_rows",
+            [((rows + half, PAIR), bf16)] * group,
+            [place], [query_rows, key_rows, value_rows],
+            [((rows, width), bf16)] * 3
+            + [((head_count, rows + half, PAIR), bf16), pltpu.SemaphoreType.DMA((3,))],
+            space=ANY, limit=60,
+        )
+    )
     grads = swap(
         call(
             functools.partial(project_kernel, head_count, group, shards), "project_pack",
             [((half, PAIR), bf16)] * group,
-            [place, out_weight, *upstreams],
+            [place], [out_weight, *upstreams],
             [((rows, width), bf16), ((head_count, half, PAIR), bf16)],
             flops=2 * rows * width * upstream.shape[1],
         )
     )
-    keys, key_t, picks = call(
-        functools.partial(gather_kernel, head_count), "gather_keys",
-        [((near, PAIR), bf16), ((HEAD_SIZE, near), bf16), ((count, PAIR), bf16)],
-        [place, sent, grads[0]],
+    keys, key_t, queries, picks = call(
+        functools.partial(gather_kernel, head_count, group), "gather_keys",
+        [
+            ((near, PAIR), bf16), ((HEAD_SIZE, near), bf16), ((group, half, PAIR), bf16),
+            ((count, PAIR), bf16),
+        ],
+        scalars, [*sent, grads[0]],
     )
     other_picks = [segment_shift(picks, shift) for shift in range(1, others + 1)]
-    extra, own_terms, other_terms = call(
+    extra, own_terms, other_terms, grads = call(
         functools.partial(far_kernel, head_count, group, others), "picked_rows",
         [
-            ((PAIR + STAT_ROWS, count), bf16),
-            ((count, PAIR), f32), ((others * count, PAIR), f32),
+            ((PAIR + STAT_ROWS, count), bf16), ((count, PAIR), f32),
+            ((others * count, PAIR), f32), ((group, half, PAIR), bf16),
         ],
-        [place, keys, sent, picks, *other_picks, *grads],
+        scalars, [keys, queries, picks, *other_picks, *grads],
         [((near + count * (1 + others), PAIR), bf16)] + [((count, PAIR), bf16)] * 2,
         flops=8 * near * count * PAIR,
     )
@@ -402,21 +432,21 @@
     ]
     half_flops = 10 * near * near // 2 * PAIR
     acc, query_half = call(
-        functools.partial(first_kernel, head_count), "first_rows",
+        functools.partial(first_kernel, head_count, steps), "first_rows",
         [((near, PAIR), f32), ((steps, half, PAIR), bf16)],
-        [place, keys, key_t, sent, extra, *grads[:steps]], scratch, half_flops,
+        scalars, [keys, key_t, queries, grads, extra], scratch, half_flops,
     )
     near_send = call(
         functools.partial(second_kernel, head_count, group - steps, others), "second_rows",
         [((rows + half, PAIR), bf16)] * group,
-        [place, keys, key_t, sent, extra, acc, query_half, own_terms, *back, *grads[steps:]],
-        [((near, PAIR), f32)] + scratch, half_flops,
+        scalars, [keys, key_t, queries, grads, extra, acc, query_half, own_terms, *back],
+        [((near, PAIR), f32), ((group, rows + half, PAIR), bf16)] + scratch, half_flops,
     )
     return tuple(
         call(
             functools.partial(unpack_kernel, head_count, group), "unpack",
             [((rows, width), bf16)] * 3,
-            [place, *swap(near_send)],
+            [place], swap(near_send),
             [((group, rows + half, PAIR), bf16)],
         )
     )

time: 73.1 us -> 76.8 us (1.051)
  waiting for transfers between devices: 15.4 us -> 19.1 us
  starting transfers between devices: 26.1 us -> 23.5 us
  local copies, waits for them, and re-layouts: 0.67 us -> 1.88 us
  Pallas kernels: 29.8 us -> 30.8 us
    ppermute x14 -> x21, waiting for transfers between devices: 8.26 us -> 16.5 us  [swap(): result.append(lax.ppermute(value, 'context', pairs))]
    ppermute x1, waiting for transfers between devices: 6.43 us -> 0.01 us  [body(): upstreams.append(lax.ppermute(upstream, 'heads', pairs))]
    all_to_all x1 -> x0, starting transfers between devices: 5.4 us -> none  [body(): sent = lax.all_to_all(sent, 'context', 0, 0, axis_index_groups=groups)]
    ppermute x14 -> x21, starting transfers between devices: 13.9 us -> 15.8 us  [swap(): result.append(lax.ppermute(value, 'context', pairs))]
    ppermute x2, waiting for transfers between devices: 0.72 us -> 2.56 us  [segment_shift(): return lax.ppermute(value, 'context', pairs)]
    ppermute x1, starting transfers between devices: 1.56 us -> 3 us  [body(): upstreams.append(lax.ppermute(upstream, 'heads', pairs))]
    unnamed x6 -> x10, local copies, waits for them, and re-layouts: 0.67 us -> 1.88 us
    pallas_call x7, Pallas kernels: 29.8 us -> 30.8 us  [call(): pl.pallas_call(kernel, out_shape=tuple((jax.ShapeDtypeStruct(*shape) for...]
  transfers between devices with their start and end apart: 18 -> 24, of which waited for: 6 -> 8; matrix products, arithmetic and copies ran while one was open for 0% -> 1% of each run, Pallas kernels for 18% -> 21%
where the time goes in v4:
time: 76.8 us; the launch traced here: 76.6 us
  Pallas kernels  30.8 us (40%)
  starting transfers between devices  23.5 us (31%)
  waiting for transfers between devices  19.1 us (25%)
  local copies, waits for them, and re-layouts  1.88 us (2%)
    pallas_call x7, Pallas kernels, call(): pl.pallas_call(kernel, out_shape=tuple((jax.ShapeDtypeStruct(*shape) for...  30.8 us
    ppermute x21, waiting for transfers between devices, swap(): result.append(lax.ppermute(value, 'context', pairs))  16.5 us
    ppermute x21, starting transfers between devices, swap(): result.append(lax.ppermute(value, 'context', pairs))  15.8 us
    ppermute x2, starting transfers between devices, segment_shift(): return lax.ppermute(value, 'context', pairs)  4.65 us
    ppermute x1, starting transfers between devices, body(): upstreams.append(lax.ppermute(upstream, 'heads', pairs))  3 us
    ppermute x2, waiting for transfers between devices, segment_shift(): return lax.ppermute(value, 'context', pairs)  2.56 us
    unnamed x10, local copies, waits for them, and re-layouts  1.88 us
  transfers between devices with their start and end apart: 24, of which 8 were waited for; matrix products, arithmetic and copies ran while one was open for 1% of the time, Pallas kernels for 21%

profile of v4, /device:TPU:0, one launch (start us, length us, event | category | flops | bytes accessed | tf_op | source)
XLA Modules:
  0.0 76.6 jit_solution(13027123326442660791)
XLA Ops:
  0.6 3.0 %collective-permute-start.7 = (bf16[128,1024]{1,0:T(8,128)(2,1)}, bf16[128,1024]{1,0:T(8,128)(2,1)S(1)}, u32[]{:S(2)}, u32[]{:S(2)}) collective-permute-start(bf16[128,1024]{1,0:T(8,128)(2,1)} %refs_0_.1), channel_id=1, source_target_pairs={{0,1},{1,0},{2,3},{3,2},{4,5},{5,4},{6,7},{7,6},{8,9},{9,8},{10,11... | collective-permute-start | bytes 786440 | tf_op jit(solution)/shard_map/ppermute | solution.py:384
  3.6 0.6 pad_add_fusion.place_ref
  4.2 0.0 copy-start.1
  4.2 3.1 %pack_rows.1 = (bf16[384,128]{1,0:T(8,128)(2,1)}, bf16[384,128]{1,0:T(8,128)(2,1)}, bf16[384,128]{1,0:T(8,128)(2,1)}, bf16[384,128]{1,0:T(8,128)(2,1)}, bf16[384...) custom-call(s32[2]{0:T(128)} %pad_add_fusion.place_ref, ...), custom_call_target="tpu_custom_call" | custom-call | bytes 2097152 | tf_op jit(solution)/shard_map/pack_rows/pallas_call | solution.py:340
  7.3 2.6 %collective-permute-start = (bf16[384,128]{1,0:T(8,128)(2,1)}, bf16[384,128]{1,0:T(8,128)(2,1)S(1)}, u32[]{:S(2)}, u32[]{:S(2)}) collective-permute-start(bf16[384,128]{1,0:T(8,128)(2,1)} %get-tuple-element.38), channel_id=1, source_target_pairs={{0,12},{2,14},{4,8},{6,10},{8,4},{10,6},{12,0},{14,2},{16,28},{18,... | collective-permute-start | bytes 294920 | tf_op jit(solution)/shard_map/ppermute | solution.py:374
  9.9 0.5 collective-permute-start.1
  10.4 0.1 collective-permute-start.2
  10.5 0.4 collective-permute-start.3
  10.9 3.2 %collective-permute-done.refs_1_ = bf16[384,128]{1,0:T(8,128)(2,1)S(1)} collective-permute-done((bf16[384,128]{1,0:T(8,128)(2,1)}, bf16[384,128]{1,0:T(8,128)(2,1)S(1)}, u32[]{:S(2)}, u32[]{:S(2)}) %collective-permute-start) | collective-permute-done | bytes 98336 | tf_op jit(solution)/shard_map/ppermute | solution.py:374
  14.1 0.0 collective-permute-start.4
  14.1 2.9 %collective-permute-done.1.refs_2_ = bf16[384,128]{1,0:T(8,128)(2,1)S(1)} collective-permute-done((bf16[384,128]{1,0:T(8,128)(2,1)}, bf16[384,128]{1,0:T(8,128)(2,1)S(1)}, u32[]{:S(2)}, u32[]{:S(2)}) %collective-permute-start.1) | collective-permute-done | bytes 98336 | tf_op jit(solution)/shard_map/ppermute | solution.py:374
  17.1 0.0 copy-start.3
  17.1 0.0 collective-permute-start.5
  17.1 0.0 collective-permute-done.7.refs_1_
  17.1 1.7 %collective-permute-start.6 = (bf16[384,128]{1,0:T(8,128)(2,1)}, bf16[384,128]{1,0:T(8,128)(2,1)S(1)}, u32[]{:S(2)}, u32[]{:S(2)}) collective-permute-start(bf16[384,128]{1,0:T(8,128)(2,1)} %get-tuple-element.44), channel_id=1, source_target_pairs={{0,10},{2,4},{4,14},{6,0},{8,2},{10,12},{12,6},{14,8},{16,26},{18,... | collective-permute-start | bytes 294920 | tf_op jit(solution)/shard_map/ppermute | solution.py:374
  18.8 0.0 copy-done.1
  18.8 0.0 copy-done.3
  18.8 0.0 copy-start
  18.8 1.2 %copy-done = bf16[512,1024]{1,0:T(8,128)(2,1)S(1)} copy-done((bf16[512,1024]{1,0:T(8,128)(2,1)S(1)}, bf16[512,1024]{1,0:T(8,128)(2,1)}, u32[]{:S(2)}) %copy-start) | copy-done | bytes 1048600
  20.0 1.5 %project_pack.1 = (bf16[128,128]{1,0:T(8,128)(2,1)S(1)}, bf16[128,128]{1,0:T(8,128)(2,1)S(1)}, bf16[128,128]{1,0:T(8,128)(2,1)S(1)}, bf16[128,128]{1,0:T(8,128)(...) custom-call(s32[2]{0:T(128)S(1)} %copy-done.3, ...), custom_call_target="tpu_custom_call" | custom-call | flops 268435456 | bytes 2097152 | tf_op jit(solution)/shard_map/project_pack/pallas_call | solution.py:340
  21.6 0.0 collective-permute-done.2.refs_3_
  21.6 0.8 %collective-permute-start.9 = (bf16[128,128]{1,0:T(8,128)(2,1)S(1)}, bf16[128,128]{1,0:T(8,128)(2,1)S(1)}, u32[]{:S(2)}, u32[]{:S(2)}) collective-permute-start(bf16[128,128]{1,0:T(8,128)(2,1)S(1)} %get-tuple-element.50), channel_id=1, source_target_pairs={{0,12},{2,14},{4,8},{6,10},{8,4},{10,6},{12,0},{14,2},{16,28},{18,... | collective-permute-start | bytes 98312 | tf_op jit(solution)/shard_map/ppermute | solution.py:374
  22.4 0.0 collective-permute-done.3.refs_4_
  22.4 1.8 %collective-permute-start.10 = (bf16[128,128]{1,0:T(8,128)(2,1)S(1)}, bf16[128,128]{1,0:T(8,128)(2,1)S(1)}, u32[]{:S(2)}, u32[]{:S(2)}) collective-permute-start(bf16[128,128]{1,0:T(8,128)(2,1)S(1)} %get-tuple-element.51), channel_id=1, source_target_pairs={{0,4},{2,10},{4,0},{6,14},{8,12},{10,2},{12,8},{14,6},{16,20},{18,... | collective-permute-start | bytes 98312 | tf_op jit(solution)/shard_map/ppermute | solution.py:374
  24.2 0.0 collective-permute-done.4.refs_5_
  24.2 0.0 collective-permute-start.11
  24.2 0.0 collective-permute-done.5.refs_6_
  24.2 1.0 %collective-permute-start.12 = (bf16[128,128]{1,0:T(8,128)(2,1)S(1)}, bf16[128,128]{1,0:T(8,128)(2,1)S(1)}, u32[]{:S(2)}, u32[]{:S(2)}) collective-permute-start(bf16[128,128]{1,0:T(8,128)(2,1)S(1)} %get-tuple-element.53), channel_id=1, source_target_pairs={{0,8},{2,6},{4,12},{6,2},{8,0},{10,14},{12,4},{14,10},{16,24},{18,... | collective-permute-start | bytes 98312 | tf_op jit(solution)/shard_map/ppermute | solution.py:374
  25.2 0.0 collective-permute-done.6.refs_7_
  25.2 0.0 collective-permute-start.13
  25.2 0.0 copy-done.2
  25.2 0.6 copy-done.4
  25.9 0.9 %gather_keys.1 = (bf16[2048,128]{1,0:T(8,128)(2,1)S(1)}, bf16[64,2048]{1,0:T(8,128)(2,1)S(1)}, bf16[8,128,128]{2,1,0:T(8,128)(2,1)S(1)}, bf16[128,128]{1,0:T(8,128)(2,1)S(1)}) custom-call(s32[2]{0:T(128)S(1)} %copy-done.3, s32[16]{0:T(128)S(1)} %copy-done.4, bf16[384,128]{1,0:T(8,128)(2,1)S(1)} %copy-done.2, ...), custom_call_target="tpu_custom_call" | custom-call | bytes 2097152 | tf_op jit(solution)/shard_map/gather_keys/pallas_call | solution.py:340
  26.8 0.0 collective-permute-done.9.refs_2_
  26.8 2.3 %collective-permute-start.14 = (bf16[128,128]{1,0:T(8,128)(2,1)S(1)}, bf16[128,128]{1,0:T(8,128)(2,1)S(1)}, u32[]{:S(2)}, u32[]{:S(2)}) collective-permute-start(bf16[128,128]{1,0:T(8,128)(2,1)S(1)} %get-tuple-element.55), channel_id=1, source_target_pairs={{0,6},{2,8},{4,2},{6,12},{8,14},{10,0},{12,10},{14,4},{16,22},{18,... | collective-permute-start | bytes 98312 | tf_op jit(solution)/shard_map/ppermute | solution.py:374
  29.1 0.0 collective-permute-done.10.refs_3_
  29.1 0.1 collective-permute-start.15
  29.2 0.0 collective-permute-done.11.refs_4_
  29.2 2.6 %collective-permute-start.8 = (bf16[128,128]{1,0:T(8,128)(2,1)S(1)}, bf16[128,128]{1,0:T(8,128)(2,1)S(1)}, u32[]{:S(2)}, u32[]{:S(2)}) collective-permute-start(bf16[128,128]{1,0:T(8,128)(2,1)S(1)} %get-tuple-element.49.picks_ref), channel_id=1, source_target_pairs={{0,16},{2,18},{4,20},{6,22},{8,24},{10,26},{12,28},{14,30},{16,0},... | collective-permute-start | bytes 98312 | tf_op jit(solution)/shard_map/ppermute | solution.py:379
  31.8 0.0 collective-permute-done.12.refs_5_
  31.8 0.0 collective-permute-done.13.refs_6_
  31.8 0.0 collective-permute-done.14.refs_7_
  31.8 0.6 collective-permute-done.15.refs_8_
  32.4 2.6 %collective-permute-done.8.refs_0_ = bf16[128,128]{1,0:T(8,128)(2,1)S(1)} collective-permute-done((bf16[128,128]{1,0:T(8,128)(2,1)S(1)}, bf16[128,128]{1,0:T(8,128)(2,1)S(1)}, u32[]{:S(2)}, u32[]{:S(2)}) %collective-permute-start.8) | collective-permute-done | bytes 32800 | tf_op jit(solution)/shard_map/ppermute | solution.py:379
  35.0 1.9 %picked_rows.1 = (bf16[144,128]{1,0:T(8,128)(2,1)S(1)}, f32[128,128]{1,0:T(8,128)S(1)}, f32[128,128]{1,0:T(8,128)S(1)}, bf16[8,128,128]{2,1,0:T(8,128)(2,1)S(1)}) custom-call(s32[2]{0:T(128)S(1)} %copy-done.3, s32[16]{0:T(128)S(1)} %copy-done.4, bf16[2048,128]{1,0:T(8,128)(2,1)S(1)} %get-tuple-element.46.near_ref.keys_ref, ...), custom_call_target="tpu_custom_call" | custom-call | flops 268435456 | bytes 2097152 | tf_op jit(solution)/shard_map/picked_rows/pallas_call | solution.py:340
  36.9 2.1 %collective-permute-start.16 = (f32[128,128]{1,0:T(8,128)S(1)}, f32[128,128]{1,0:T(8,128)S(1)}, u32[]{:S(2)}, u32[]{:S(2)}) collective-permute-start(f32[128,128]{1,0:T(8,128)S(1)} %get-tuple-element.62), channel_id=1, source_target_pairs={{0,16},{2,18},{4,20},{6,22},{8,24},{10,26},{12,28},{14,30},{16,0},... | collective-permute-start | bytes 196616 | tf_op jit(solution)/shard_map/ppermute | solution.py:379
  38.9 10.5 %first_rows.1 = (f32[2048,128]{1,0:T(8,128)S(1)}, bf16[4,128,128]{2,1,0:T(8,128)(2,1)S(1)}) custom-call(s32[2]{0:T(128)S(1)} %copy-done.3, s32[16]{0:T(128)S(1)} %copy-done.4, bf16[2048,128]{1,0:T(8,128)(2,1)S(1)} %get-tuple-element.46.near_ref.keys_ref, bf16[64,2048]{1,0:T(8,128)(2,1)S(1)} %get-tuple-element.47.key_t_ref, ...), custom_call_target="tpu_custom_call" | custom-call | flops 2684354560 | bytes 2097152 | tf_op jit(solution)/shard_map/first_rows/pallas_call | solution.py:340
  49.5 0.0 collective-permute-done.16.refs_0_
  49.5 10.9 %second_rows.1 = (bf16[384,128]{1,0:T(8,128)(2,1)S(1)}, bf16[384,128]{1,0:T(8,128)(2,1)S(1)}, bf16[384,128]{1,0:T(8,128)(2,1)S(1)}, bf16[384,128]{1,0:T(8,128)(2...) custom-call(s32[2]{0:T(128)S(1)} %copy-done.3, ...), custom_call_target="tpu_custom_call" | custom-call | flops 2684354560 | bytes 2097152 | tf_op jit(solution)/shard_map/second_rows/pallas_call | solution.py:340
  60.4 2.2 %collective-permute-start.17 = (bf16[384,128]{1,0:T(8,128)(2,1)S(1)}, bf16[384,128]{1,0:T(8,128)(2,1)S(1)}, u32[]{:S(2)}, u32[]{:S(2)}) collective-permute-start(bf16[384,128]{1,0:T(8,128)(2,1)S(1)} %get-tuple-element.64), channel_id=1, source_target_pairs={{0,12},{2,14},{4,8},{6,10},{8,4},{10,6},{12,0},{14,2},{16,28},{18,... | collective-permute-start | bytes 294920 | tf_op jit(solution)/shard_map/ppermute | solution.py:374
  62.6 0.9 %collective-permute-start.18 = (bf16[384,128]{1,0:T(8,128)(2,1)S(1)}, bf16[384,128]{1,0:T(8,128)(2,1)S(1)}, u32[]{:S(2)}, u32[]{:S(2)}) collective-permute-start(bf16[384,128]{1,0:T(8,128)(2,1)S(1)} %get-tuple-element.65), channel_id=1, source_target_pairs={{0,4},{2,10},{4,0},{6,14},{8,12},{10,2},{12,8},{14,6},{16,20},{18,... | collective-permute-start | bytes 294920 | tf_op jit(solution)/shard_map/ppermute | solution.py:374
  63.5 0.0 collective-permute-start.19
  63.5 0.6 collective-permute-start.20
  64.2 0.7 collective-permute-start.21
  64.9 2.0 %collective-permute-done.17.refs_1_ = bf16[384,128]{1,0:T(8,128)(2,1)S(1)} collective-permute-done((bf16[384,128]{1,0:T(8,128)(2,1)S(1)}, bf16[384,128]{1,0:T(8,128)(2,1)S(1)}, u32[]{:S(2)}, u32[]{:S(2)}) %collective-permute-start.17) | collective-permute-done | bytes 98336 | tf_op jit(solution)/shard_map/ppermute | solution.py:374
  66.9 0.0 collective-permute-start.22
  66.9 3.7 %collective-permute-done.18.refs_2_ = bf16[384,128]{1,0:T(8,128)(2,1)S(1)} collective-permute-done((bf16[384,128]{1,0:T(8,128)(2,1)S(1)}, bf16[384,128]{1,0:T(8,128)(2,1)S(1)}, u32[]{:S(2)}, u32[]{:S(2)}) %collective-permute-start.18) | collective-permute-done | bytes 98336 | tf_op jit(solution)/shard_map/ppermute | solution.py:374
  70.6 0.0 collective-permute-start.23
  70.6 0.0 collective-permute-done.19.refs_3_
  70.6 0.0 collective-permute-done.20.refs_4_
  70.6 0.0 collective-permute-done.21.refs_5_
  70.6 0.3 collective-permute-done.22.refs_6_
  71.0 3.7 %collective-permute-done.23.refs_7_ = bf16[384,128]{1,0:T(8,128)(2,1)S(1)} collective-permute-done((bf16[384,128]{1,0:T(8,128)(2,1)S(1)}, bf16[384,128]{1,0:T(8,128)(2,1)S(1)}, u32[]{:S(2)}, u32[]{:S(2)}) %collective-permute-start.23) | collective-permute-done | bytes 98336 | tf_op jit(solution)/shard_map/ppermute | solution.py:374
  74.7 1.9 %unpack.1 = (bf16[256,512]{1,0:T(8,128)(2,1)}, bf16[256,512]{1,0:T(8,128)(2,1)}, bf16[256,512]{1,0:T(8,128)(2,1)}) custom-call(s32[2]{0:T(128)S(1)} %copy-done.3, bf16[384,128]{1,0:T(8,128)(2,1)S(1)} %get-tuple-element.63.refs_0_, bf16[384,128]{1,0:T(8,128)(2,1)S(1)} %collective-permute-done.17.refs_1_, ...), custom_call_target="tpu_custom_call" | custom-call | bytes 2097152 | tf_op jit(solution)/shard_map/unpack/pallas_call | solution.py:340
  (2 shorter events, 0.0 us)
Async XLA Ops:
  0.6 16.4 %collective-permute-start.7 = (bf16[128,1024]{1,0:T(8,128)(2,1)}, bf16[128,1024]{1,0:T(8,128)(2,1)S(1)}, u32[]{:S(2)}, u32[]{:S(2)}) collective-permute-start(bf16[128,1024]{1,0:T(8,128)(2,1)} %refs_0_.1), channel_id=1, source_target_pairs={{0,1},{1,0},{2,3},{3,2},{4,5},{5,4},{6,7},{7,6},{8,9},{9,8},{10,11... | collective-permute-start | bytes 786440 | tf_op jit(solution)/shard_map/ppermute | solution.py:384
  4.2 14.6 %copy-start.1 = (bf16[128,1024]{1,0:T(8,128)(2,1)S(1)}, bf16[128,1024]{1,0:T(8,128)(2,1)}, u32[]{:S(2)}) copy-start(bf16[128,1024]{1,0:T(8,128)(2,1)} %refs_0_.1) | copy-start | bytes 786436
  7.3 6.8 %collective-permute-start = (bf16[384,128]{1,0:T(8,128)(2,1)}, bf16[384,128]{1,0:T(8,128)(2,1)S(1)}, u32[]{:S(2)}, u32[]{:S(2)}) collective-permute-start(bf16[384,128]{1,0:T(8,128)(2,1)} %get-tuple-element.38), channel_id=1, source_target_pairs={{0,12},{2,14},{4,8},{6,10},{8,4},{10,6},{12,0},{14,2},{16,28},{18,... | collective-permute-start | bytes 294920 | tf_op jit(solution)/shard_map/ppermute | solution.py:374
  9.9 7.1 %collective-permute-start.1 = (bf16[384,128]{1,0:T(8,128)(2,1)}, bf16[384,128]{1,0:T(8,128)(2,1)S(1)}, u32[]{:S(2)}, u32[]{:S(2)}) collective-permute-start(bf16[384,128]{1,0:T(8,128)(2,1)} %get-tuple-element.39), channel_id=1, source_target_pairs={{0,4},{2,10},{4,0},{6,14},{8,12},{10,2},{12,8},{14,6},{16,20},{18,... | collective-permute-start | bytes 294920 | tf_op jit(solution)/shard_map/ppermute | solution.py:374
  10.4 11.2 %collective-permute-start.2 = (bf16[384,128]{1,0:T(8,128)(2,1)}, bf16[384,128]{1,0:T(8,128)(2,1)S(1)}, u32[]{:S(2)}, u32[]{:S(2)}) collective-permute-start(bf16[384,128]{1,0:T(8,128)(2,1)} %get-tuple-element.40), channel_id=1, source_target_pairs={{0,14},{2,0},{4,10},{6,4},{8,6},{10,8},{12,2},{14,12},{16,30},{18,... | collective-permute-start | bytes 294920 | tf_op jit(solution)/shard_map/ppermute | solution.py:374
  10.5 11.9 %collective-permute-start.3 = (bf16[384,128]{1,0:T(8,128)(2,1)}, bf16[384,128]{1,0:T(8,128)(2,1)S(1)}, u32[]{:S(2)}, u32[]{:S(2)}) collective-permute-start(bf16[384,128]{1,0:T(8,128)(2,1)} %get-tuple-element.41), channel_id=1, source_target_pairs={{0,8},{2,6},{4,12},{6,2},{8,0},{10,14},{12,4},{14,10},{16,24},{18,... | collective-permute-start | bytes 294920 | tf_op jit(solution)/shard_map/ppermute | solution.py:374
  14.1 10.0 %collective-permute-start.4 = (bf16[384,128]{1,0:T(8,128)(2,1)}, bf16[384,128]{1,0:T(8,128)(2,1)S(1)}, u32[]{:S(2)}, u32[]{:S(2)}) collective-permute-start(bf16[384,128]{1,0:T(8,128)(2,1)} %get-tuple-element.42), channel_id=1, source_target_pairs={{0,2},{2,12},{4,6},{6,8},{8,10},{10,4},{12,14},{14,0},{16,18},{18,... | collective-permute-start | bytes 294920 | tf_op jit(solution)/shard_map/ppermute | solution.py:374
  17.1 1.8 %copy-start.3 = (s32[2]{0:T(128)S(1)}, s32[2]{0:T(128)}, u32[]{:S(2)}) copy-start(s32[2]{0:T(128)} %pad_add_fusion.place_ref) | copy-start | bytes 28
  17.1 7.1 %collective-permute-start.5 = (bf16[384,128]{1,0:T(8,128)(2,1)}, bf16[384,128]{1,0:T(8,128)(2,1)S(1)}, u32[]{:S(2)}, u32[]{:S(2)}) collective-permute-start(bf16[384,128]{1,0:T(8,128)(2,1)} %get-tuple-element.43), channel_id=1, source_target_pairs={{0,6},{2,8},{4,2},{6,12},{8,14},{10,0},{12,10},{14,4},{16,22},{18,... | collective-permute-start | bytes 294920 | tf_op jit(solution)/shard_map/ppermute | solution.py:374
  17.1 8.2 %collective-permute-start.6 = (bf16[384,128]{1,0:T(8,128)(2,1)}, bf16[384,128]{1,0:T(8,128)(2,1)S(1)}, u32[]{:S(2)}, u32[]{:S(2)}) collective-permute-start(bf16[384,128]{1,0:T(8,128)(2,1)} %get-tuple-element.44), channel_id=1, source_target_pairs={{0,10},{2,4},{4,14},{6,0},{8,2},{10,12},{12,6},{14,8},{16,26},{18,... | collective-permute-start | bytes 294920 | tf_op jit(solution)/shard_map/ppermute | solution.py:374
  18.8 1.2 %copy-start = (bf16[512,1024]{1,0:T(8,128)(2,1)S(1)}, bf16[512,1024]{1,0:T(8,128)(2,1)}, u32[]{:S(2)}) copy-start(bf16[512,1024]{1,0:T(8,128)(2,1)} %weight_ref.1) | copy-start | bytes 3145732
  20.0 5.2 %copy-start.2 = (bf16[384,128]{1,0:T(8,128)(2,1)S(1)}, bf16[384,128]{1,0:T(8,128)(2,1)}, u32[]{:S(2)}) copy-start(bf16[384,128]{1,0:T(8,128)(2,1)} %get-tuple-element.37.refs_0_) | copy-start | bytes 294916
  21.6 5.2 %collective-permute-start.9 = (bf16[128,128]{1,0:T(8,128)(2,1)S(1)}, bf16[128,128]{1,0:T(8,128)(2,1)S(1)}, u32[]{:S(2)}, u32[]{:S(2)}) collective-permute-start(bf16[128,128]{1,0:T(8,128)(2,1)S(1)} %get-tuple-element.50), channel_id=1, source_target_pairs={{0,12},{2,14},{4,8},{6,10},{8,4},{10,6},{12,0},{14,2},{16,28},{18,... | collective-permute-start | bytes 98312 | tf_op jit(solution)/shard_map/ppermute | solution.py:374
  22.4 6.7 %collective-permute-start.10 = (bf16[128,128]{1,0:T(8,128)(2,1)S(1)}, bf16[128,128]{1,0:T(8,128)(2,1)S(1)}, u32[]{:S(2)}, u32[]{:S(2)}) collective-permute-start(bf16[128,128]{1,0:T(8,128)(2,1)S(1)} %get-tuple-element.51), channel_id=1, source_target_pairs={{0,4},{2,10},{4,0},{6,14},{8,12},{10,2},{12,8},{14,6},{16,20},{18,... | collective-permute-start | bytes 98312 | tf_op jit(solution)/shard_map/ppermute | solution.py:374
  24.2 5.0 %collective-permute-start.11 = (bf16[128,128]{1,0:T(8,128)(2,1)S(1)}, bf16[128,128]{1,0:T(8,128)(2,1)S(1)}, u32[]{:S(2)}, u32[]{:S(2)}) collective-permute-start(bf16[128,128]{1,0:T(8,128)(2,1)S(1)} %get-tuple-element.52), channel_id=1, source_target_pairs={{0,14},{2,0},{4,10},{6,4},{8,6},{10,8},{12,2},{14,12},{16,30},{18,... | collective-permute-start | bytes 98312 | tf_op jit(solution)/shard_map/ppermute | solution.py:374
  24.2 7.6 %collective-permute-start.12 = (bf16[128,128]{1,0:T(8,128)(2,1)S(1)}, bf16[128,128]{1,0:T(8,128)(2,1)S(1)}, u32[]{:S(2)}, u32[]{:S(2)}) collective-permute-start(bf16[128,128]{1,0:T(8,128)(2,1)S(1)} %get-tuple-element.53), channel_id=1, source_target_pairs={{0,8},{2,6},{4,12},{6,2},{8,0},{10,14},{12,4},{14,10},{16,24},{18,... | collective-permute-start | bytes 98312 | tf_op jit(solution)/shard_map/ppermute | solution.py:374
  25.2 6.5 %collective-permute-start.13 = (bf16[128,128]{1,0:T(8,128)(2,1)S(1)}, bf16[128,128]{1,0:T(8,128)(2,1)S(1)}, u32[]{:S(2)}, u32[]{:S(2)}) collective-permute-start(bf16[128,128]{1,0:T(8,128)(2,1)S(1)} %get-tuple-element.54), channel_id=1, source_target_pairs={{0,2},{2,12},{4,6},{6,8},{8,10},{10,4},{12,14},{14,0},{16,18},{18,... | collective-permute-start | bytes 98312 | tf_op jit(solution)/shard_map/ppermute | solution.py:374
  25.2 0.7 copy-start.4
  26.8 5.0 %collective-permute-start.14 = (bf16[128,128]{1,0:T(8,128)(2,1)S(1)}, bf16[128,128]{1,0:T(8,128)(2,1)S(1)}, u32[]{:S(2)}, u32[]{:S(2)}) collective-permute-start(bf16[128,128]{1,0:T(8,128)(2,1)S(1)} %get-tuple-element.55), channel_id=1, source_target_pairs={{0,6},{2,8},{4,2},{6,12},{8,14},{10,0},{12,10},{14,4},{16,22},{18,... | collective-permute-start | bytes 98312 | tf_op jit(solution)/shard_map/ppermute | solution.py:374
  29.1 3.3 %collective-permute-start.15 = (bf16[128,128]{1,0:T(8,128)(2,1)S(1)}, bf16[128,128]{1,0:T(8,128)(2,1)S(1)}, u32[]{:S(2)}, u32[]{:S(2)}) collective-permute-start(bf16[128,128]{1,0:T(8,128)(2,1)S(1)} %get-tuple-element.56), channel_id=1, source_target_pairs={{0,10},{2,4},{4,14},{6,0},{8,2},{10,12},{12,6},{14,8},{16,26},{18,... | collective-permute-start | bytes 98312 | tf_op jit(solution)/shard_map/ppermute | solution.py:374
  29.2 5.8 %collective-permute-start.8 = (bf16[128,128]{1,0:T(8,128)(2,1)S(1)}, bf16[128,128]{1,0:T(8,128)(2,1)S(1)}, u32[]{:S(2)}, u32[]{:S(2)}) collective-permute-start(bf16[128,128]{1,0:T(8,128)(2,1)S(1)} %get-tuple-element.49.picks_ref), channel_id=1, source_target_pairs={{0,16},{2,18},{4,20},{6,22},{8,24},{10,26},{12,28},{14,30},{16,0},... | collective-permute-start | bytes 98312 | tf_op jit(solution)/shard_map/ppermute | solution.py:379
  36.9 12.6 %collective-permute-start.16 = (f32[128,128]{1,0:T(8,128)S(1)}, f32[128,128]{1,0:T(8,128)S(1)}, u32[]{:S(2)}, u32[]{:S(2)}) collective-permute-start(f32[128,128]{1,0:T(8,128)S(1)} %get-tuple-element.62), channel_id=1, source_target_pairs={{0,16},{2,18},{4,20},{6,22},{8,24},{10,26},{12,28},{14,30},{16,0},... | collective-permute-start | bytes 196616 | tf_op jit(solution)/shard_map/ppermute | solution.py:379
  60.4 6.5 %collective-permute-start.17 = (bf16[384,128]{1,0:T(8,128)(2,1)S(1)}, bf16[384,128]{1,0:T(8,128)(2,1)S(1)}, u32[]{:S(2)}, u32[]{:S(2)}) collective-permute-start(bf16[384,128]{1,0:T(8,128)(2,1)S(1)} %get-tuple-element.64), channel_id=1, source_target_pairs={{0,12},{2,14},{4,8},{6,10},{8,4},{10,6},{12,0},{14,2},{16,28},{18,... | collective-permute-start | bytes 294920 | tf_op jit(solution)/shard_map/ppermute | solution.py:374
  62.6 8.0 %collective-permute-start.18 = (bf16[384,128]{1,0:T(8,128)(2,1)S(1)}, bf16[384,128]{1,0:T(8,128)(2,1)S(1)}, u32[]{:S(2)}, u32[]{:S(2)}) collective-permute-start(bf16[384,128]{1,0:T(8,128)(2,1)S(1)} %get-tuple-element.65), channel_id=1, source_target_pairs={{0,4},{2,10},{4,0},{6,14},{8,12},{10,2},{12,8},{14,6},{16,20},{18,... | collective-permute-start | bytes 294920 | tf_op jit(solution)/shard_map/ppermute | solution.py:374
  63.5 7.1 %collective-permute-start.19 = (bf16[384,128]{1,0:T(8,128)(2,1)S(1)}, bf16[384,128]{1,0:T(8,128)(2,1)S(1)}, u32[]{:S(2)}, u32[]{:S(2)}) collective-permute-start(bf16[384,128]{1,0:T(8,128)(2,1)S(1)} %get-tuple-element.66), channel_id=1, source_target_pairs={{0,14},{2,0},{4,10},{6,4},{8,6},{10,8},{12,2},{14,12},{16,30},{18,... | collective-permute-start | bytes 294920 | tf_op jit(solution)/shard_map/ppermute | solution.py:374
  63.5 7.1 %collective-permute-start.20 = (bf16[384,128]{1,0:T(8,128)(2,1)S(1)}, bf16[384,128]{1,0:T(8,128)(2,1)S(1)}, u32[]{:S(2)}, u32[]{:S(2)}) collective-permute-start(bf16[384,128]{1,0:T(8,128)(2,1)S(1)} %get-tuple-element.67), channel_id=1, source_target_pairs={{0,8},{2,6},{4,12},{6,2},{8,0},{10,14},{12,4},{14,10},{16,24},{18,... | collective-permute-start | bytes 294920 | tf_op jit(solution)/shard_map/ppermute | solution.py:374
  64.2 6.5 %collective-permute-start.21 = (bf16[384,128]{1,0:T(8,128)(2,1)S(1)}, bf16[384,128]{1,0:T(8,128)(2,1)S(1)}, u32[]{:S(2)}, u32[]{:S(2)}) collective-permute-start(bf16[384,128]{1,0:T(8,128)(2,1)S(1)} %get-tuple-element.68), channel_id=1, source_target_pairs={{0,2},{2,12},{4,6},{6,8},{8,10},{10,4},{12,14},{14,0},{16,18},{18,... | collective-permute-start | bytes 294920 | tf_op jit(solution)/shard_map/ppermute | solution.py:374
  66.9 4.0 %collective-permute-start.22 = (bf16[384,128]{1,0:T(8,128)(2,1)S(1)}, bf16[384,128]{1,0:T(8,128)(2,1)S(1)}, u32[]{:S(2)}, u32[]{:S(2)}) collective-permute-start(bf16[384,128]{1,0:T(8,128)(2,1)S(1)} %get-tuple-element.69), channel_id=1, source_target_pairs={{0,6},{2,8},{4,2},{6,12},{8,14},{10,0},{12,10},{14,4},{16,22},{18,... | collective-permute-start | bytes 294920 | tf_op jit(solution)/shard_map/ppermute | solution.py:374
  70.6 4.0 %collective-permute-start.23 = (bf16[384,128]{1,0:T(8,128)(2,1)S(1)}, bf16[384,128]{1,0:T(8,128)(2,1)S(1)}, u32[]{:S(2)}, u32[]{:S(2)}) collective-permute-start(bf16[384,128]{1,0:T(8,128)(2,1)S(1)} %get-tuple-element.70), channel_id=1, source_target_pairs={{0,10},{2,4},{4,14},{6,0},{8,2},{10,12},{12,6},{14,8},{16,26},{18,... | collective-permute-start | bytes 294920 | tf_op jit(solution)/shard_map/ppermute | solution.py:374

commit v5 on v4

--- a/solution.py
+++ b/solution.py
@@ -81,33 +81,13 @@
     return jnp.concatenate([block[:half], block[half:]], 1)
 
 
-def swap_steps(group):
-    if group == 8:
-        return [(6, 6), (2, 4), (7, 1), (4, 2), (1, 7), (3, 5), (5, 3)]
-    return [(bits, bits) for bits in range(1, group)]
-
-
-def target_of(place, step):
-    return lax.bitwise_xor(place, jnp.where(lax.rem(place, 2) == 1, step[1], step[0]))
-
-
-def source_of(place, step):
-    odd = lax.rem(place + step[0], 2) == 1
-    return lax.bitwise_xor(place, jnp.where(odd, step[1], step[0]))
-
-
-def send_out(place, head_count, stage_ref, out_refs):
-    out_refs[0][...] = stage_ref[lax.rem(place, head_count)]
-    for step, out_ref in zip(swap_steps(len(out_refs)), out_refs[1:]):
-        out_ref[...] = stage_ref[lax.rem(target_of(place, step), head_count)]
-
-
-def places_of(place, group):
-    return [place] + [source_of(place, step) for step in swap_steps(group)]
-
-
-def pack_kernel(head_count, group, place_ref, query_hbm, key_hbm, value_hbm, *refs):
-    out_refs, (query_ref, key_ref, value_ref, stage_ref, sems) = refs[:group], refs[group:]
+def send_out(place, stage_ref, out_refs):
+    for bits, out_ref in enumerate(out_refs):
+        out_ref[...] = stage_ref[lax.bitwise_xor(place, bits)]
+
+
+def pack_kernel(head_count, query_hbm, key_hbm, value_hbm, *refs):
+    out_ref, query_ref, key_ref, value_ref, sems = refs
     rows = query_ref.shape[0]
     copies = [
         pltpu.make_async_copy(source, target, sems.at[index])
@@ -120,16 +100,15 @@
     for copy in copies:
         copy.wait()
     for head in range(head_count):
-        stage_ref[head, :rows, :] = jnp.concatenate(
-            [head_columns(key_ref, head), head_columns(value_ref, head)], 1
-        )
-        stage_ref[head, rows:, :] = side_by_side(head_columns(query_ref, head))
-    send_out(place_ref[0], head_count, stage_ref, out_refs)
-
-
-def project_kernel(head_count, group, shards, place_ref, weight_ref, *refs):
-    upstream_refs, refs = refs[:shards], refs[shards:]
-    out_refs, grad_ref, stage_ref = refs[:group], refs[group], refs[group + 1]
+        pair = jnp.concatenate([head_columns(key_ref, head), head_columns(value_ref, head)], 1)
+        query = side_by_side(head_columns(query_ref, head))
+        for place in range(head, out_ref.shape[0], head_count):
+            out_ref[place, :rows, :] = pair
+            out_ref[place, rows:, :] = query
+
+
+def project_kernel(head_count, shards, place_ref, weight_ref, *refs):
+    upstream_refs, (out_ref, grad_ref) = refs[:shards], refs[shards:]
     shard_rows = upstream_refs[0].shape[0]
     for step, upstream_ref in enumerate(upstream_refs):
         owner = lax.rem(place_ref[1] + (shards - step), shards)
@@ -138,27 +117,30 @@
             upstream_ref[...], weight_ref[...]
         ).astype(jnp.bfloat16)
     for head in range(head_count):
-        stage_ref[head] = side_by_side(head_columns(grad_ref, head))
-    send_out(place_ref[0], head_count, stage_ref, out_refs)
+        grad = side_by_side(head_columns(grad_ref, head))
+        for place in range(head, out_ref.shape[0], head_count):
+            out_ref[place] = grad
 
 
 def own_offset(head_count, place_ref, offset_ref):
     return offset_ref[place_ref[1] * head_count + lax.rem(place_ref[0], head_count)]
 
 
-def gather_kernel(head_count, group, place_ref, offset_ref, *refs):
-    sent_refs, refs = refs[:group], refs[group + 1 :]
-    keys_out, key_t_out, queries_out, picks_out = refs
+def gather_kernel(
+    head_count, place_ref, offset_ref, sent_ref, after_ref, keys_out, key_t_out, queries_out,
+    picks_out,
+):
+    group = sent_ref.shape[0]
     rows = keys_out.shape[0] // group
     picked = rows // DILATION_RATE
     pick = pick_matrix(own_offset(head_count, place_ref, offset_ref), picked, rows)
-    for place, sent_ref in zip(places_of(place_ref[0], group), sent_refs):
-        pair = sent_ref[:rows, :]
-        keys_out[pl.ds(pl.multiple_of(place * rows, rows), rows), :] = pair
-        picks_out[pl.ds(pl.multiple_of(place * picked, picked), picked), :] = dot_nn(
-            pick, pair
-        ).astype(jnp.bfloat16)
-        queries_out[place] = sent_ref[rows:, :]
+    for place in range(group):
+        pair = sent_ref[place, :rows, :]
+        keys_out[place * rows : (place + 1) * rows, :] = pair
+        picks_out[place * picked : (place + 1) * picked, :] = dot_nn(pick, pair).astype(
+            jnp.bfloat16
+        )
+        queries_out[place] = sent_ref[place, rows:, :]
     key_t_out[...] = keys_out[...].astype(jnp.float32).T[:HEAD_SIZE].astype(jnp.bfloat16)
 
 
@@ -182,11 +164,11 @@
 
 
 def far_kernel(
-    head_count, group, others, place_ref, offset_ref, near_ref, queries_ref, picks_ref, *refs
+    head_count, group, others, place_ref, offset_ref, near_ref, queries_ref, grads_ref, picks_ref,
+    *refs,
 ):
     other_refs, refs = refs[:others], refs[others:]
-    grad_refs, refs = refs[:group], refs[group:]
-    extra_out, own_out, other_out, grads_out, keys_ref, query_ref, grad_ref = refs
+    extra_out, own_out, other_out, keys_ref, query_ref, grad_ref = refs
     near = near_ref.shape[0]
     rows = near // group
     picked = rows // DILATION_RATE
@@ -196,10 +178,8 @@
     keys_ref[:near, :] = near_ref[...]
     for index, ref in enumerate([picks_ref, *other_refs]):
         keys_ref[near + index * count : near + (index + 1) * count, :] = ref[...]
-    for place, ref in zip(places_of(place_ref[0], group), grad_refs):
-        grads_out[place] = ref[...]
     for step in range(group):
-        query, grad = query_and_grad(queries_ref.at[step], grads_out.at[step])
+        query, grad = query_and_grad(queries_ref.at[step], grads_ref.at[step])
         span = slice(step * picked, (step + 1) * picked)
         query_ref[span, :] = dot_nn(pick, query).astype(jnp.bfloat16)
         grad_ref[span, :] = dot_nn(pick, grad).astype(jnp.bfloat16)
@@ -318,7 +298,7 @@
         stage_ref[place, :rows, :] = summed.astype(jnp.bfloat16)
         if place < group - steps:
             stage_ref[place, rows:, :] = query_ref[place]
-    send_out(place_ref[0], group, stage_ref, out_refs)
+    send_out(place_ref[0], stage_ref, out_refs)
 
 
 def unpack_kernel(head_count, group, place_ref, *refs):
@@ -326,8 +306,8 @@
     query_out, key_out, value_out, stage_ref = refs
     rows = query_out.shape[0]
     half = rows // 2
-    for place, near_ref in zip(places_of(place_ref[0], group), near_refs):
-        stage_ref[place] = near_ref[...]
+    for bits, near_ref in enumerate(near_refs):
+        stage_ref[lax.bitwise_xor(place_ref[0], bits)] = near_ref[...]
     for head in range(head_count):
         columns = slice(head * HEAD_SIZE, (head + 1) * HEAD_SIZE)
         key_out[:, columns] = stage_ref[head, :rows, :HEAD_SIZE]
@@ -368,11 +348,14 @@
     scalars = [place, head_offsets]
 
     def swap(values):
-        result = [values[0]]
-        for step, value in zip(swap_steps(group), values[1:]):
-            pairs = [(source, source ^ step[source % 2]) for source in range(devices)]
-            result.append(lax.ppermute(value, "context", pairs))
-        return result
+        pairs = [[(source, source ^ bits) for source in range(devices)] for bits in range(group)]
+        return [values[0]] + [
+            lax.ppermute(values[bits], "context", pairs[bits]) for bits in range(1, group)
+        ]
+
+    def exchange(value):
+        groups = [list(range(first, first + group)) for first in range(0, devices, group)]
+        return lax.all_to_all(value, "context", 0, 0, axis_index_groups=groups)
 
     def segment_shift(value, shift):
         pairs = [(source, (source + shift * group) % devices) for source in range(devices)]
@@ -384,41 +367,38 @@
         upstreams.append(lax.ppermute(upstream, "heads", pairs))
 
     bf16, f32 = jnp.bfloat16, jnp.float32
-    sent = swap(
-        call(
-            functools.partial(pack_kernel, head_count, group), "pack_rows",
-            [((rows + half, PAIR), bf16)] * group,
-            [place], [query_rows, key_rows, value_rows],
-            [((rows, width), bf16)] * 3
-            + [((head_count, rows + half, PAIR), bf16), pltpu.SemaphoreType.DMA((3,))],
-            space=ANY, limit=60,
-        )
-    )
-    grads = swap(
-        call(
-            functools.partial(project_kernel, head_count, group, shards), "project_pack",
-            [((half, PAIR), bf16)] * group,
-            [place], [out_weight, *upstreams],
-            [((rows, width), bf16), ((head_count, half, PAIR), bf16)],
-            flops=2 * rows * width * upstream.shape[1],
-        )
-    )
+    (sent,) = call(
+        functools.partial(pack_kernel, head_count), "pack_rows",
+        [((group, rows + half, PAIR), bf16)],
+        [], [query_rows, key_rows, value_rows],
+        [((rows, width), bf16)] * 3 + [pltpu.SemaphoreType.DMA((3,))],
+        flops=2**31, space=ANY, limit=60,
+    )
+    sent = exchange(sent)
+    (grads_send,) = call(
+        functools.partial(project_kernel, head_count, shards), "project_pack",
+        [((group, half, PAIR), bf16)],
+        [place], [out_weight, *upstreams],
+        [((rows, width), bf16)],
+        flops=2 * rows * width * upstream.shape[1],
+    )
+    grads = exchange(grads_send)
     keys, key_t, queries, picks = call(
-        functools.partial(gather_kernel, head_count, group), "gather_keys",
+        functools.partial(gather_kernel, head_count), "gather_keys",
         [
             ((near, PAIR), bf16), ((HEAD_SIZE, near), bf16), ((group, half, PAIR), bf16),
             ((count, PAIR), bf16),
         ],
-        scalars, [*sent, grads[0]],
+        scalars, [sent, grads_send],
     )
     other_picks = [segment_shift(picks, shift) for shift in range(1, others + 1)]
-    extra, own_terms, other_terms, grads = call(
+    extra, own_terms, other_terms = call(
         functools.partial(far_kernel, head_count, group, others), "picked_rows",
         [
             ((PAIR + STAT_ROWS, count), bf16), ((count, PAIR), f32),
-            ((others * count, PAIR), f32), ((group, half, PAIR), bf16),
+            ((others * count, PAIR), f32),
         ],
-        scalars, [keys, queries, picks, *other_picks, *grads],
+        scalars, [keys, queries, grads, picks, *other_picks],
         [((near + count * (1 + others), PAIR), bf16)] + [((count, PAIR), bf16)] * 2,
         flops=8 * near * count * PAIR,
     )

time: 76.8 us -> 72.3 us (0.941)
  local copies, waits for them, and re-layouts: 1.88 us -> 0.02 us
  waiting for transfers between devices: 19.1 us -> 17.3 us
    ppermute x21 -> x7, waiting for transfers between devices: 16.5 us -> 6.74 us  [swap(): lax.ppermute(values[bits], 'context', pairs[bits])]
    all_to_all x0 -> x2, starting transfers between devices: none -> 8.81 us  [exchange(): return lax.all_to_all(value, 'context', 0, 0, axis_index_groups=groups)]
    ppermute x21 -> x7, starting transfers between devices: 15.8 us -> 7.52 us  [swap(): lax.ppermute(values[bits], 'context', pairs[bits])]
    ppermute x1, waiting for transfers between devices: 0.01 us -> 7.08 us  [body(): upstreams.append(lax.ppermute(upstream, 'heads', pairs))]
    all_to_all x0 -> x2, waiting for transfers between devices: none -> 3.43 us  [exchange(): return lax.all_to_all(value, 'context', 0, 0, axis_index_groups=groups)]
    ppermute x2, waiting for transfers between devices: 2.56 us -> 0.01 us  [segment_shift(): return lax.ppermute(value, 'context', pairs)]
    unnamed x10 -> x6, local copies, waits for them, and re-layouts: 1.88 us -> 0.02 us
    ppermute x1, starting transfers between devices: 3 us -> 1.56 us  [body(): upstreams.append(lax.ppermute(upstream, 'heads', pairs))]
  transfers between devices with their start and end apart: 24 -> 12, of which waited for: 8 -> 6; matrix products, arithmetic and copies ran while one was open for 1% -> 0% of each run, Pallas kernels for 21% -> 19%
where the time goes in v5:
time: 72.3 us; the launch traced here: 72 us
  Pallas kernels  31 us (43%)
  starting transfers between devices  22.9 us (32%)
  waiting for transfers between devices  17.3 us (24%)
  between operations  0.73 us (1%)
    pallas_call x7, Pallas kernels, call(): pl.pallas_call(kernel, out_shape=tuple((jax.ShapeDtypeStruct(*shape) for...  31 us
    all_to_all x2, starting transfers between devices, exchange(): return lax.all_to_all(value, 'context', 0, 0, axis_index_groups=groups)  8.81 us
    ppermute x7, starting transfers between devices, swap(): lax.ppermute(values[bits], 'context', pairs[bits])  7.52 us
    ppermute x1, waiting for transfers between devices, body(): upstreams.append(lax.ppermute(upstream, 'heads', pairs))  7.08 us
    ppermute x7, waiting for transfers between devices, swap(): lax.ppermute(values[bits], 'context', pairs[bits])  6.74 us
    ppermute x2, starting transfers between devices, segment_shift(): return lax.ppermute(value, 'context', pairs)  4.98 us
    all_to_all x2, waiting for transfers between devices, exchange(): return lax.all_to_all(value, 'context', 0, 0, axis_index_groups=groups)  3.43 us
    ppermute x1, starting transfers between devices, body(): upstreams.append(lax.ppermute(upstream, 'heads', pairs))  1.56 us
  transfers between devices with their start and end apart: 12, of which 6 were waited for; matrix products, arithmetic and copies ran while one was open for 0% of the time, Pallas kernels for 19%

profile of v5, /device:TPU:0, one launch (start us, length us, event | category | flops | bytes accessed | tf_op | source)
XLA Modules:
  0.0 72.0 jit_solution(7297251390711713875)
XLA Ops:
  0.6 2.3 %pack_rows.1 = bf16[8,384,128]{2,1,0:T(8,128)(2,1)} custom-call(bf16[256,512]{1,0:T(8,128)(2,1)} %query_hbm.1, bf16[256,512]{1,0:T(8,128)(2,1)} %key_hbm.1, bf16[256,512]{1,0:T(8,128)(2,1)} %value_hbm.1), custom_call_target="tpu_custom_call" | custom-call | flops 2147483648 | bytes 2097152 | tf_op jit(solution)/shard_map/pack_rows/pallas_call | solution.py:320
  2.9 0.0 copy-start.1
  2.9 0.0 copy-start
  2.9 5.4 %all-to-all-start = ((bf16[8,384,128]{2,1,0:T(8,128)(2,1)}), bf16[8,384,128]{2,1,0:T(8,128)(2,1)S(1)}, u32[]{:S(2)}, u32[]{:S(2)}) async-start(bf16[8,384,128]{2,1,0:T(8,128)(2,1)} %pack_rows.1), calls=%async_computation | async-start | bytes 1572864 | tf_op jit(solution)/shard_map/all_to_all | solution.py:358
  8.3 0.0 copy-done.1
  8.4 1.6 %collective-permute-start = (bf16[128,1024]{1,0:T(8,128)(2,1)S(1)}, bf16[128,1024]{1,0:T(8,128)(2,1)S(1)}, u32[]{:S(2)}, u32[]{:S(2)}) collective-permute-start(bf16[128,1024]{1,0:T(8,128)(2,1)S(1)} %copy-done.1), channel_id=1, source_target_pairs={{0,1},{1,0},{2,3},{3,2},{4,5},{5,4},{6,7},{7,6},{8,9},{9,8},{10,11... | collective-permute-start | bytes 786440 | tf_op jit(solution)/shard_map/ppermute | solution.py:367
  9.9 0.1 pad_add_fusion.place_ref
  10.0 7.1 %collective-permute-done.refs_1_ = bf16[128,1024]{1,0:T(8,128)(2,1)S(1)} collective-permute-done((bf16[128,1024]{1,0:T(8,128)(2,1)S(1)}, bf16[128,1024]{1,0:T(8,128)(2,1)S(1)}, u32[]{:S(2)}, u32[]{:S(2)}) %collective-permute-start) | collective-permute-done | bytes 262176 | tf_op jit(solution)/shard_map/ppermute | solution.py:367
  17.1 0.0 copy-done
  17.1 2.2 %project_pack.1.after_ref = bf16[8,128,128]{2,1,0:T(8,128)(2,1)} custom-call(s32[2]{0:T(128)S(1)} %pad_add_fusion.place_ref, bf16[512,1024]{1,0:T(8,128)(2,1)S(1)} %copy-done, bf16[128,1024]{1,0:T(8,128)(2,1)S(1)} %copy-done.1, bf16[128,1024]{1,0:T(8,128)(2,1)S(1)} %collective-permute-done.refs_1_), custom_call_target="tpu_custom_call" | custom-call | flops 268435456 | bytes 2097152 | tf_op jit(solution)/shard_map/project_pack/pallas_call | solution.py:320
  19.3 0.0 copy-start.2
  19.3 0.7 all-to-all-done.sent_ref
  20.0 3.4 %all-to-all-start.1 = ((bf16[8,128,128]{2,1,0:T(8,128)(2,1)}), bf16[8,128,128]{2,1,0:T(8,128)(2,1)S(1)}, u32[]{:S(2)}, u32[]{:S(2)}) async-start(bf16[8,128,128]{2,1,0:T(8,128)(2,1)} %project_pack.1.after_ref), calls=%async_computation.1 | async-start | bytes 524288 | tf_op jit(solution)/shard_map/all_to_all | solution.py:358
  23.4 0.0 copy-done.2
  23.4 1.2 %gather_keys.1 = (bf16[2048,128]{1,0:T(8,128)(2,1)S(1)}, bf16[64,2048]{1,0:T(8,128)(2,1)S(1)}, bf16[8,128,128]{2,1,0:T(8,128)(2,1)S(1)}, bf16[128,128]{1,0:T(8,128)(2,1)S(1)}) custom-call(s32[2]{0:T(128)S(1)} %pad_add_fusion.place_ref, s32[16]{0:T(128)S(1)} %copy-done.2, bf16[8,384,128]{2,1,0:T(8,128)(2,1)S(1)} %all-to-all-done.sent_ref, ...), custom_call_target="tpu_custom_call" | custom-call | bytes 2097152 | tf_op jit(solution)/shard_map/gather_keys/pallas_call | solution.py:320
  24.7 2.7 %collective-permute-start.1 = (bf16[128,128]{1,0:T(8,128)(2,1)S(1)}, bf16[128,128]{1,0:T(8,128)(2,1)S(1)}, u32[]{:S(2)}, u32[]{:S(2)}) collective-permute-start(bf16[128,128]{1,0:T(8,128)(2,1)S(1)} %get-tuple-element.23.picks_ref), channel_id=1, source_target_pairs={{0,16},{2,18},{4,20},{6,22},{8,24},{10,26},{12,28},{14,30},{16,0},... | collective-permute-start | bytes 98312 | tf_op jit(solution)/shard_map/ppermute | solution.py:362
  27.4 2.7 %all-to-all-done.1.grads_ref = bf16[8,128,128]{2,1,0:T(8,128)(2,1)S(1)} async-done(((bf16[8,128,128]{2,1,0:T(8,128)(2,1)}), bf16[8,128,128]{2,1,0:T(8,128)(2,1)S(1)}, u32[]{:S(2)}, u32[]{:S(2)}) %all-to-all-start.1) | async-done | bytes 262176 | tf_op jit(solution)/shard_map/all_to_all | solution.py:358
  30.1 0.0 collective-permute-done.1.refs_0_
  30.1 1.9 %picked_rows.1 = (bf16[144,128]{1,0:T(8,128)(2,1)S(1)}, f32[128,128]{1,0:T(8,128)S(1)}, f32[128,128]{1,0:T(8,128)S(1)}) custom-call(s32[2]{0:T(128)S(1)} %pad_add_fusion.place_ref, s32[16]{0:T(128)S(1)} %copy-done.2, bf16[2048,128]{1,0:T(8,128)(2,1)S(1)} %get-tuple-element.20.near_ref.keys_ref, bf16[8,128,128]{2,1,0:T(8,128)(2,1)S(1)} %get-tuple-element.22.queries_ref, ...), custom_call_target="tpu_custom_call" | custom-call | flops 268435456 | bytes 2097152 | tf_op jit(solution)/shard_map/picked_rows/pallas_call | solution.py:320
  32.0 2.3 %collective-permute-start.2 = (f32[128,128]{1,0:T(8,128)S(1)}, f32[128,128]{1,0:T(8,128)S(1)}, u32[]{:S(2)}, u32[]{:S(2)}) collective-permute-start(f32[128,128]{1,0:T(8,128)S(1)} %get-tuple-element.28), channel_id=1, source_target_pairs={{0,16},{2,18},{4,20},{6,22},{8,24},{10,26},{12,28},{14,30},{16,0},... | collective-permute-start | bytes 196616 | tf_op jit(solution)/shard_map/ppermute | solution.py:362
  34.3 10.6 %first_rows.1 = (f32[2048,128]{1,0:T(8,128)S(1)}, bf16[4,128,128]{2,1,0:T(8,128)(2,1)S(1)}) custom-call(s32[2]{0:T(128)S(1)} %pad_add_fusion.place_ref, s32[16]{0:T(128)S(1)} %copy-done.2, bf16[2048,128]{1,0:T(8,128)(2,1)S(1)} %get-tuple-element.20.near_ref.keys_ref, bf16[64,2048]{1,0:T(8,128)(2,1)S(1)} %get-tuple-element.21.key_t_ref, ...), custom_call_target="tpu_custom_call" | custom-call | flops 2684354560 | bytes 2097152 | tf_op jit(solution)/shard_map/first_rows/pallas_call | solution.py:320
  44.9 0.0 collective-permute-done.2.refs_0_
  44.9 10.9 %second_rows.1 = (bf16[384,128]{1,0:T(8,128)(2,1)S(1)}, bf16[384,128]{1,0:T(8,128)(2,1)S(1)}, bf16[384,128]{1,0:T(8,128)(2,1)S(1)}, bf16[384,128]{1,0:T(8,128)(2...) custom-call(s32[2]{0:T(128)S(1)} %pad_add_fusion.place_ref, ...), custom_call_target="tpu_custom_call" | custom-call | flops 2684354560 | bytes 2097152 | tf_op jit(solution)/shard_map/second_rows/pallas_call | solution.py:320
  55.8 0.1 collective-permute-start.3
  55.9 1.8 %collective-permute-start.4 = (bf16[384,128]{1,0:T(8,128)(2,1)S(1)}, bf16[384,128]{1,0:T(8,128)(2,1)S(1)}, u32[]{:S(2)}, u32[]{:S(2)}) collective-permute-start(bf16[384,128]{1,0:T(8,128)(2,1)S(1)} %get-tuple-element.31), channel_id=1, source_target_pairs={{0,4},{2,6},{4,0},{6,2},{8,12},{10,14},{12,8},{14,10},{16,20},{18,... | collective-permute-start | bytes 294920 | tf_op jit(solution)/shard_map/ppermute | solution.py:353
  57.7 0.1 collective-permute-start.5
  57.8 1.8 %collective-permute-start.6 = (bf16[384,128]{1,0:T(8,128)(2,1)S(1)}, bf16[384,128]{1,0:T(8,128)(2,1)S(1)}, u32[]{:S(2)}, u32[]{:S(2)}) collective-permute-start(bf16[384,128]{1,0:T(8,128)(2,1)S(1)} %get-tuple-element.33), channel_id=1, source_target_pairs={{0,8},{2,10},{4,12},{6,14},{8,0},{10,2},{12,4},{14,6},{16,24},{18,... | collective-permute-start | bytes 294920 | tf_op jit(solution)/shard_map/ppermute | solution.py:353
  59.6 0.0 collective-permute-start.7
  59.6 0.0 collective-permute-done.3.refs_1_
  59.6 2.9 %collective-permute-start.8 = (bf16[384,128]{1,0:T(8,128)(2,1)S(1)}, bf16[384,128]{1,0:T(8,128)(2,1)S(1)}, u32[]{:S(2)}, u32[]{:S(2)}) collective-permute-start(bf16[384,128]{1,0:T(8,128)(2,1)S(1)} %get-tuple-element.35), channel_id=1, source_target_pairs={{0,12},{2,14},{4,8},{6,10},{8,4},{10,6},{12,0},{14,2},{16,28},{18,... | collective-permute-start | bytes 294920 | tf_op jit(solution)/shard_map/ppermute | solution.py:353
  62.4 0.0 collective-permute-done.4.refs_2_
  62.4 0.9 %collective-permute-start.9 = (bf16[384,128]{1,0:T(8,128)(2,1)S(1)}, bf16[384,128]{1,0:T(8,128)(2,1)S(1)}, u32[]{:S(2)}, u32[]{:S(2)}) collective-permute-start(bf16[384,128]{1,0:T(8,128)(2,1)S(1)} %get-tuple-element.36), channel_id=1, source_target_pairs={{0,14},{2,12},{4,10},{6,8},{8,6},{10,4},{12,2},{14,0},{16,30},{18,... | collective-permute-start | bytes 294920 | tf_op jit(solution)/shard_map/ppermute | solution.py:353
  63.3 0.0 collective-permute-done.5.refs_3_
  63.3 0.0 collective-permute-done.6.refs_4_
  63.3 1.5 %collective-permute-done.7.refs_5_ = bf16[384,128]{1,0:T(8,128)(2,1)S(1)} collective-permute-done((bf16[384,128]{1,0:T(8,128)(2,1)S(1)}, bf16[384,128]{1,0:T(8,128)(2,1)S(1)}, u32[]{:S(2)}, u32[]{:S(2)}) %collective-permute-start.7) | collective-permute-done | bytes 98336 | tf_op jit(solution)/shard_map/ppermute | solution.py:353
  64.8 3.7 %collective-permute-done.8.refs_6_ = bf16[384,128]{1,0:T(8,128)(2,1)S(1)} collective-permute-done((bf16[384,128]{1,0:T(8,128)(2,1)S(1)}, bf16[384,128]{1,0:T(8,128)(2,1)S(1)}, u32[]{:S(2)}, u32[]{:S(2)}) %collective-permute-start.8) | collective-permute-done | bytes 98336 | tf_op jit(solution)/shard_map/ppermute | solution.py:353
  68.5 1.6 %collective-permute-done.9.refs_7_ = bf16[384,128]{1,0:T(8,128)(2,1)S(1)} collective-permute-done((bf16[384,128]{1,0:T(8,128)(2,1)S(1)}, bf16[384,128]{1,0:T(8,128)(2,1)S(1)}, u32[]{:S(2)}, u32[]{:S(2)}) %collective-permute-start.9) | collective-permute-done | bytes 98336 | tf_op jit(solution)/shard_map/ppermute | solution.py:353
  70.1 1.9 %unpack.1 = (bf16[256,512]{1,0:T(8,128)(2,1)}, bf16[256,512]{1,0:T(8,128)(2,1)}, bf16[256,512]{1,0:T(8,128)(2,1)}) custom-call(s32[2]{0:T(128)S(1)} %pad_add_fusion.place_ref, bf16[384,128]{1,0:T(8,128)(2,1)S(1)} %get-tuple-element.29.refs_0_, bf16[384,128]{1,0:T(8,128)(2,1)S(1)} %collective-permute-done.3.refs_1_, ...), custom_call_target="tpu_custom_call" | custom-call | bytes 2097152 | tf_op jit(solution)/shard_map/unpack/pallas_call | solution.py:320
Async XLA Ops:
  2.9 5.4 %copy-start.1 = (bf16[128,1024]{1,0:T(8,128)(2,1)S(1)}, bf16[128,1024]{1,0:T(8,128)(2,1)}, u32[]{:S(2)}) copy-start(bf16[128,1024]{1,0:T(8,128)(2,1)} %refs_0_.1) | copy-start | bytes 786436
  2.9 14.1 %copy-start = (bf16[512,1024]{1,0:T(8,128)(2,1)S(1)}, bf16[512,1024]{1,0:T(8,128)(2,1)}, u32[]{:S(2)}) copy-start(bf16[512,1024]{1,0:T(8,128)(2,1)} %weight_ref.1) | copy-start | bytes 3145732
  2.9 17.1 %all-to-all-start = ((bf16[8,384,128]{2,1,0:T(8,128)(2,1)}), bf16[8,384,128]{2,1,0:T(8,128)(2,1)S(1)}, u32[]{:S(2)}, u32[]{:S(2)}) async-start(bf16[8,384,128]{2,1,0:T(8,128)(2,1)} %pack_rows.1), calls=%async_computation | async-start | bytes 1572864 | tf_op jit(solution)/shard_map/all_to_all | solution.py:358
  8.4 8.7 %collective-permute-start = (bf16[128,1024]{1,0:T(8,128)(2,1)S(1)}, bf16[128,1024]{1,0:T(8,128)(2,1)S(1)}, u32[]{:S(2)}, u32[]{:S(2)}) collective-permute-start(bf16[128,1024]{1,0:T(8,128)(2,1)S(1)} %copy-done.1), channel_id=1, source_target_pairs={{0,1},{1,0},{2,3},{3,2},{4,5},{5,4},{6,7},{7,6},{8,9},{9,8},{10,11... | collective-permute-start | bytes 786440 | tf_op jit(solution)/shard_map/ppermute | solution.py:367
  19.3 4.1 %copy-start.2 = (s32[16]{0:T(128)S(1)}, s32[16]{0:T(128)}, u32[]{:S(2)}) copy-start(s32[16]{0:T(128)} %offset_ref.7) | copy-start | bytes 196
  20.0 10.1 %all-to-all-start.1 = ((bf16[8,128,128]{2,1,0:T(8,128)(2,1)}), bf16[8,128,128]{2,1,0:T(8,128)(2,1)S(1)}, u32[]{:S(2)}, u32[]{:S(2)}) async-start(bf16[8,128,128]{2,1,0:T(8,128)(2,1)} %project_pack.1.after_ref), calls=%async_computation.1 | async-start | bytes 524288 | tf_op jit(solution)/shard_map/all_to_all | solution.py:358
  24.7 5.4 %collective-permute-start.1 = (bf16[128,128]{1,0:T(8,128)(2,1)S(1)}, bf16[128,128]{1,0:T(8,128)(2,1)S(1)}, u32[]{:S(2)}, u32[]{:S(2)}) collective-permute-start(bf16[128,128]{1,0:T(8,128)(2,1)S(1)} %get-tuple-element.23.picks_ref), channel_id=1, source_target_pairs={{0,16},{2,18},{4,20},{6,22},{8,24},{10,26},{12,28},{14,30},{16,0},... | collective-permute-start | bytes 98312 | tf_op jit(solution)/shard_map/ppermute | solution.py:362
  32.0 12.9 %collective-permute-start.2 = (f32[128,128]{1,0:T(8,128)S(1)}, f32[128,128]{1,0:T(8,128)S(1)}, u32[]{:S(2)}, u32[]{:S(2)}) collective-permute-start(f32[128,128]{1,0:T(8,128)S(1)} %get-tuple-element.28), channel_id=1, source_target_pairs={{0,16},{2,18},{4,20},{6,22},{8,24},{10,26},{12,28},{14,30},{16,0},... | collective-permute-start | bytes 196616 | tf_op jit(solution)/shard_map/ppermute | solution.py:362
  55.8 3.8 %collective-permute-start.3 = (bf16[384,128]{1,0:T(8,128)(2,1)S(1)}, bf16[384,128]{1,0:T(8,128)(2,1)S(1)}, u32[]{:S(2)}, u32[]{:S(2)}) collective-permute-start(bf16[384,128]{1,0:T(8,128)(2,1)S(1)} %get-tuple-element.30), channel_id=1, source_target_pairs={{0,2},{2,0},{4,6},{6,4},{8,10},{10,8},{12,14},{14,12},{16,18},{18,... | collective-permute-start | bytes 294920 | tf_op jit(solution)/shard_map/ppermute | solution.py:353
  55.9 6.5 %collective-permute-start.4 = (bf16[384,128]{1,0:T(8,128)(2,1)S(1)}, bf16[384,128]{1,0:T(8,128)(2,1)S(1)}, u32[]{:S(2)}, u32[]{:S(2)}) collective-permute-start(bf16[384,128]{1,0:T(8,128)(2,1)S(1)} %get-tuple-element.31), channel_id=1, source_target_pairs={{0,4},{2,6},{4,0},{6,2},{8,12},{10,14},{12,8},{14,10},{16,20},{18,... | collective-permute-start | bytes 294920 | tf_op jit(solution)/shard_map/ppermute | solution.py:353
  57.7 5.7 %collective-permute-start.5 = (bf16[384,128]{1,0:T(8,128)(2,1)S(1)}, bf16[384,128]{1,0:T(8,128)(2,1)S(1)}, u32[]{:S(2)}, u32[]{:S(2)}) collective-permute-start(bf16[384,128]{1,0:T(8,128)(2,1)S(1)} %get-tuple-element.32), channel_id=1, source_target_pairs={{0,6},{2,4},{4,2},{6,0},{8,14},{10,12},{12,10},{14,8},{16,22},{18,... | collective-permute-start | bytes 294920 | tf_op jit(solution)/shard_map/ppermute | solution.py:353
  57.8 5.6 %collective-permute-start.6 = (bf16[384,128]{1,0:T(8,128)(2,1)S(1)}, bf16[384,128]{1,0:T(8,128)(2,1)S(1)}, u32[]{:S(2)}, u32[]{:S(2)}) collective-permute-start(bf16[384,128]{1,0:T(8,128)(2,1)S(1)} %get-tuple-element.33), channel_id=1, source_target_pairs={{0,8},{2,10},{4,12},{6,14},{8,0},{10,2},{12,4},{14,6},{16,24},{18,... | collective-permute-start | bytes 294920 | tf_op jit(solution)/shard_map/ppermute | solution.py:353
  59.6 5.3 %collective-permute-start.7 = (bf16[384,128]{1,0:T(8,128)(2,1)S(1)}, bf16[384,128]{1,0:T(8,128)(2,1)S(1)}, u32[]{:S(2)}, u32[]{:S(2)}) collective-permute-start(bf16[384,128]{1,0:T(8,128)(2,1)S(1)} %get-tuple-element.34), channel_id=1, source_target_pairs={{0,10},{2,8},{4,14},{6,12},{8,2},{10,0},{12,6},{14,4},{16,26},{18,... | collective-permute-start | bytes 294920 | tf_op jit(solution)/shard_map/ppermute | solution.py:353
  59.6 8.9 %collective-permute-start.8 = (bf16[384,128]{1,0:T(8,128)(2,1)S(1)}, bf16[384,128]{1,0:T(8,128)(2,1)S(1)}, u32[]{:S(2)}, u32[]{:S(2)}) collective-permute-start(bf16[384,128]{1,0:T(8,128)(2,1)S(1)} %get-tuple-element.35), channel_id=1, source_target_pairs={{0,12},{2,14},{4,8},{6,10},{8,4},{10,6},{12,0},{14,2},{16,28},{18,... | collective-permute-start | bytes 294920 | tf_op jit(solution)/shard_map/ppermute | solution.py:353
  62.4 7.6 %collective-permute-start.9 = (bf16[384,128]{1,0:T(8,128)(2,1)S(1)}, bf16[384,128]{1,0:T(8,128)(2,1)S(1)}, u32[]{:S(2)}, u32[]{:S(2)}) collective-permute-start(bf16[384,128]{1,0:T(8,128)(2,1)S(1)} %get-tuple-element.36), channel_id=1, source_target_pairs={{0,14},{2,12},{4,10},{6,8},{8,6},{10,4},{12,2},{14,0},{16,30},{18,... | collective-permute-start | bytes 294920 | tf_op jit(solution)/shard_map/ppermute | solution.py:353

commit v6 on v5

--- a/solution.py
+++ b/solution.py
@@ -16,6 +16,8 @@
 LOG2E = math.log2(math.e)
 SCORE_FACTOR = SCALE * LOG2E
 STRIP = 64
+PIECE = 512
+BUSY = 2**35
 STAT_ROWS = 16
 
 SMEM = pl.BlockSpec(memory_space=pltpu.SMEM)
@@ -207,64 +209,94 @@
     extra_out[PAIR:, :] = jnp.concatenate([*split_three(lse), *split_three(delta), blank], 0)
 
 
-def near_block(
-    first, offset, keys_ref, key_t_ref, query_ref, grad_ref, extra_ref, score_ref, dprob_ref,
-    work_ref, acc_ref,
+def near_blocks(
+    places, offset, keys_ref, key_t_ref, queries_ref, grads_ref, extra_ref,
+    score_ref, dprob_ref, work_ref, acc_ref, emit,
 ):
     near = keys_ref.shape[0]
-    rows = score_ref.shape[1]
+    rows = score_ref.shape[2]
+    half = rows // 2
     count = extra_ref.shape[1]
-    query, grad = query_and_grad(query_ref, grad_ref)
-    score_ref[...] = dot_nt(keys_ref[...], query)
-    dprob_ref[...] = dot_nt(keys_ref[...], grad)
-    extra = dot_nn(extra_ref[...], spread_matrix(offset, first, count, rows, 0))
+    pieces = [slice(start, start + PIECE) for start in range(0, near, PIECE)]
     row_lane = lax.broadcasted_iota(jnp.int32, (1, rows), 1)
     picked = lax.rem(row_lane, DILATION_RATE) == offset
-    lse_picked = extra[PAIR : PAIR + 1] + extra[PAIR + 1 : PAIR + 2] + extra[PAIR + 2 : PAIR + 3]
-    delta_picked = (
-        extra[PAIR + 3 : PAIR + 4] + extra[PAIR + 4 : PAIR + 5] + extra[PAIR + 5 : PAIR + 6]
-    )
-    strips = [slice(start, start + STRIP) for start in range(0, near, STRIP)]
+
+    def strips(piece):
+        return [slice(start, start + STRIP) for start in range(piece.start, piece.stop, STRIP)]
+
+    def first_matmuls(index, weights, piece):
+        query, grad = weights
+        score_ref[index % 2, piece, :] = dot_nt(keys_ref[piece, :], query)
+        dprob_ref[index % 2, piece, :] = dot_nt(keys_ref[piece, :], grad)
+
+    def maximum(index, top, piece):
+        for strip in strips(piece):
+            part = fold(score_ref[index % 2, strip, :], jnp.maximum)
+            top = part if top is None else jnp.maximum(top, part)
+        return top
+
+    def weights_of(index):
+        return query_and_grad(queries_ref.at[places[index]], grads_ref.at[places[index]])
+
+    weights = weights_of(0)
     top = None
-    for strip in strips:
-        part = fold(score_ref[strip, :], jnp.maximum)
-        top = part if top is None else jnp.maximum(top, part)
-    top = jnp.max(top, 0, keepdims=True) * SCORE_FACTOR
-    top = jnp.where(picked, lse_picked, top)
-    total = jnp.zeros((8, rows), jnp.float32)
-    delta = jnp.zeros((8, rows), jnp.float32)
-    for strip in strips:
-        prob = jnp.exp2(score_ref[strip, :] * SCORE_FACTOR - top)
-        total = total + fold(prob, jnp.add)
-        delta = delta + fold(prob * dprob_ref[strip, :], jnp.add)
-        score_ref[strip, :] = prob
-    inverse = jnp.where(picked, 1.0, 1.0 / jnp.sum(total, 0, keepdims=True))
-    delta = jnp.where(picked, delta_picked, jnp.sum(delta, 0, keepdims=True) * inverse)
-    for strip in strips:
-        prob = score_ref[strip, :] * inverse
-        work_ref[strip, :rows] = (prob * (dprob_ref[strip, :] - delta)).astype(jnp.bfloat16)
-        work_ref[strip, rows:] = prob.astype(jnp.bfloat16)
-    acc_ref[...] += dot_nn(work_ref[...], jnp.concatenate([query, grad], 0))
-    query_grad = dot_nn(key_t_ref[...], work_ref[:, :rows])
-    query_grad = query_grad + extra[:HEAD_SIZE] + extra[HEAD_SIZE:PAIR]
-    query_grad = (query_grad * SCALE).T.astype(jnp.bfloat16)
-    half = rows // 2
-    return jnp.concatenate([query_grad[:half], query_grad[half:]], 1)
+    for piece in pieces:
+        first_matmuls(0, weights, piece)
+        top = maximum(0, top, piece)
+    for index, place in enumerate(places):
+        slot = index % 2
+        last = index + 1 == len(places)
+        first = place * (rows // DILATION_RATE)
+        extra = dot_nn(extra_ref[...], spread_matrix(offset, first, count, rows, 0))
+        stats = [extra[PAIR + row : PAIR + row + 1] for row in range(6)]
+        top = jnp.max(top, 0, keepdims=True) * SCORE_FACTOR
+        top = jnp.where(picked, stats[0] + stats[1] + stats[2], top)
+        total = jnp.zeros((8, rows), jnp.float32)
+        delta = jnp.zeros((8, rows), jnp.float32)
+        after = None if last else weights_of(index + 1)
+        for piece in pieces:
+            if not last:
+                first_matmuls(index + 1, after, piece)
+            for strip in strips(piece):
+                prob = jnp.exp2(score_ref[slot, strip, :] * SCORE_FACTOR - top)
+                total = total + fold(prob, jnp.add)
+                delta = delta + fold(prob * dprob_ref[slot, strip, :], jnp.add)
+                score_ref[slot, strip, :] = prob
+        inverse = jnp.where(picked, 1.0, 1.0 / jnp.sum(total, 0, keepdims=True))
+        delta = jnp.sum(delta, 0, keepdims=True) * inverse
+        delta = jnp.where(picked, stats[3] + stats[4] + stats[5], delta)
+        both = jnp.concatenate(weights, 0)
+        query_grad = extra[:HEAD_SIZE] + extra[HEAD_SIZE:PAIR]
+        top = None
+        for piece in pieces:
+            for strip in strips(piece):
+                prob = score_ref[slot, strip, :] * inverse
+                dscore = prob * (dprob_ref[slot, strip, :] - delta)
+                work_ref[slot, strip, :rows] = dscore.astype(jnp.bfloat16)
+                work_ref[slot, strip, rows:] = prob.astype(jnp.bfloat16)
+            acc_ref[piece, :] += dot_nn(work_ref[slot, piece, :], both)
+            query_grad = query_grad + dot_nn(key_t_ref[:, piece], work_ref[slot, piece, :rows])
+            if not last:
+                top = maximum(index + 1, top, piece)
+        query_grad = (query_grad * SCALE).T.astype(jnp.bfloat16)
+        emit(place, jnp.concatenate([query_grad[:half], query_grad[half:]], 1))
+        weights = after
 
 
 def first_kernel(
     head_count, steps, place_ref, offset_ref, keys_ref, key_t_ref, queries_ref, grads_ref,
     extra_ref, acc_ref, query_out, *scratch,
 ):
-    rows = scratch[0].shape[2]
     offset = own_offset(head_count, place_ref, offset_ref)
     acc_ref[...] = jnp.zeros_like(acc_ref)
-    for step in range(steps):
-        query_out[step] = near_block(
-            step * (rows // DILATION_RATE), offset, keys_ref, key_t_ref,
-            queries_ref.at[step], grads_ref.at[step], extra_ref,
-            *[ref.at[step % 2] for ref in scratch], acc_ref,
-        )
+
+    def emit(place, query_grad):
+        query_out[place] = query_grad
+
+    near_blocks(
+        range(steps), offset, keys_ref, key_t_ref, queries_ref, grads_ref, extra_ref,
+        *scratch, acc_ref, emit,
+    )
 
 
 def second_kernel(
@@ -280,12 +312,14 @@
     picked = count // group
     offset = own_offset(head_count, place_ref, offset_ref)
     acc_ref[...] = start_ref[...]
-    for place in range(group - steps, group):
-        stage_ref[place, rows:, :] = near_block(
-            place * picked, offset, keys_ref, key_t_ref,
-            queries_ref.at[place], grads_ref.at[place], extra_ref,
-            *[ref.at[place % 2] for ref in scratch], acc_ref,
-        )
+
+    def emit(place, query_grad):
+        stage_ref[place, rows:, :] = query_grad
+
+    near_blocks(
+        range(group - steps, group), offset, keys_ref, key_t_ref, queries_ref, grads_ref, extra_ref,
+        *scratch, acc_ref, emit,
+    )
     terms = own_ref[...]
     for back_ref in back_refs:
         terms = terms + back_ref[...]
@@ -380,7 +414,7 @@
         [((group, half, PAIR), bf16)],
         [place], [out_weight, *upstreams],
         [((rows, width), bf16)],
-        flops=2 * rows * width * upstream.shape[1],
+        flops=BUSY,
     )
     grads = exchange(grads_send)
     keys, key_t, queries, picks = call(

time: 72.3 us -> 70.4 us (0.974)
  Pallas kernels: 31 us -> 27.5 us
  waiting for transfers between devices: 17.3 us -> 18.8 us
    all_to_all x2, waiting for transfers between devices: 3.43 us -> 11.9 us  [exchange(): return lax.all_to_all(value, 'context', 0, 0, axis_index_groups=groups)]
    ppermute x1, waiting for transfers between devices: 7.08 us -> 0.17 us  [body(): upstreams.append(lax.ppermute(upstream, 'heads', pairs))]
    pallas_call x7, Pallas kernels: 31 us -> 27.5 us  [call(): pl.pallas_call(kernel, out_shape=tuple((jax.ShapeDtypeStruct(*shape) for...]
    ppermute x1, starting transfers between devices: 1.56 us -> 3 us  [body(): upstreams.append(lax.ppermute(upstream, 'heads', pairs))]
    all_to_all x2, starting transfers between devices: 8.81 us -> 7.37 us  [exchange(): return lax.all_to_all(value, 'context', 0, 0, axis_index_groups=groups)]
  transfers between devices with their start and end apart: 12 -> 12, of which waited for: 6 -> 6; matrix products, arithmetic and copies ran while one was open for 0% -> 0% of each run, Pallas kernels for 19% -> 21%
where the time goes in v6:
time: 70.4 us; the launch traced here: 70 us
  Pallas kernels  27.5 us (39%)
  starting transfers between devices  22.9 us (33%)
  waiting for transfers between devices  18.8 us (27%)
  between operations  0.72 us (1%)
    pallas_call x7, Pallas kernels, call(): pl.pallas_call(kernel, out_shape=tuple((jax.ShapeDtypeStruct(*shape) for...  27.5 us
    all_to_all x2, waiting for transfers between devices, exchange(): return lax.all_to_all(value, 'context', 0, 0, axis_index_groups=groups)  11.9 us
    ppermute x7, starting transfers between devices, swap(): lax.ppermute(values[bits], 'context', pairs[bits])  7.53 us
    all_to_all x2, starting transfers between devices, exchange(): return lax.all_to_all(value, 'context', 0, 0, axis_index_groups=groups)  7.37 us
    ppermute x7, waiting for transfers between devices, swap(): lax.ppermute(values[bits], 'context', pairs[bits])  6.74 us
    ppermute x2, starting transfers between devices, segment_shift(): return lax.ppermute(value, 'context', pairs)  4.98 us
    ppermute x1, starting transfers between devices, body(): upstreams.append(lax.ppermute(upstream, 'heads', pairs))  3 us
  transfers between devices with their start and end apart: 12, of which 6 were waited for; matrix products, arithmetic and copies ran while one was open for 0% of the time, Pallas kernels for 21%

profile of v6, /device:TPU:0, one launch (start us, length us, event | category | flops | bytes accessed | tf_op | source)
XLA Modules:
  0.0 70.0 jit_solution(16482354672649423138)
XLA Ops:
  0.6 3.0 %collective-permute-start = (bf16[128,1024]{1,0:T(8,128)(2,1)}, bf16[128,1024]{1,0:T(8,128)(2,1)S(1)}, u32[]{:S(2)}, u32[]{:S(2)}) collective-permute-start(bf16[128,1024]{1,0:T(8,128)(2,1)} %refs_0_.1), channel_id=1, source_target_pairs={{0,1},{1,0},{2,3},{3,2},{4,5},{5,4},{6,7},{7,6},{8,9},{9,8},{10,11... | collective-permute-start | bytes 786440 | tf_op jit(solution)/shard_map/ppermute | solution.py:401
  3.6 2.3 %pack_rows.1 = bf16[8,384,128]{2,1,0:T(8,128)(2,1)} custom-call(bf16[256,512]{1,0:T(8,128)(2,1)} %query_hbm.1, bf16[256,512]{1,0:T(8,128)(2,1)} %key_hbm.1, bf16[256,512]{1,0:T(8,128)(2,1)} %value_hbm.1), custom_call_target="tpu_custom_call" | custom-call | flops 2147483648 | bytes 2097152 | tf_op jit(solution)/shard_map/pack_rows/pallas_call | solution.py:354
  5.9 0.0 copy-start.1
  5.9 0.0 copy-start.2
  6.0 4.0 %all-to-all-start = ((bf16[8,384,128]{2,1,0:T(8,128)(2,1)}), bf16[8,384,128]{2,1,0:T(8,128)(2,1)S(1)}, u32[]{:S(2)}, u32[]{:S(2)}) async-start(bf16[8,384,128]{2,1,0:T(8,128)(2,1)} %pack_rows.1), calls=%async_computation | async-start | bytes 1572864 | tf_op jit(solution)/shard_map/all_to_all | solution.py:392
  9.9 0.1 pad_add_fusion.place_ref
  10.0 0.2 collective-permute-done.refs_1_
  10.2 0.0 copy-done.1
  10.2 0.0 copy-done.2
  10.2 2.2 %project_pack.1.after_ref = bf16[8,128,128]{2,1,0:T(8,128)(2,1)} custom-call(s32[2]{0:T(128)S(1)} %pad_add_fusion.place_ref, bf16[512,1024]{1,0:T(8,128)(2,1)S(1)} %copy-done.1, bf16[128,1024]{1,0:T(8,128)(2,1)S(1)} %copy-done.2, bf16[128,1024]{1,0:T(8,128)(2,1)S(1)} %collective-permute-done.refs_1_), custom_call_target="tpu_custom_call" | custom-call | flops 34359738368 | bytes 2097152 | tf_op jit(solution)/shard_map/project_pack/pallas_call | solution.py:354
  12.4 0.0 copy-start
  12.4 9.2 %all-to-all-done.sent_ref = bf16[8,384,128]{2,1,0:T(8,128)(2,1)S(1)} async-done(((bf16[8,384,128]{2,1,0:T(8,128)(2,1)}), bf16[8,384,128]{2,1,0:T(8,128)(2,1)S(1)}, u32[]{:S(2)}, u32[]{:S(2)}) %all-to-all-start) | async-done | bytes 786464 | tf_op jit(solution)/shard_map/all_to_all | solution.py:392
  21.6 3.4 %all-to-all-start.1 = ((bf16[8,128,128]{2,1,0:T(8,128)(2,1)}), bf16[8,128,128]{2,1,0:T(8,128)(2,1)S(1)}, u32[]{:S(2)}, u32[]{:S(2)}) async-start(bf16[8,128,128]{2,1,0:T(8,128)(2,1)} %project_pack.1.after_ref), calls=%async_computation.1 | async-start | bytes 524288 | tf_op jit(solution)/shard_map/all_to_all | solution.py:392
  25.0 0.0 copy-done
  25.0 1.2 %gather_keys.1 = (bf16[2048,128]{1,0:T(8,128)(2,1)S(1)}, bf16[64,2048]{1,0:T(8,128)(2,1)S(1)}, bf16[8,128,128]{2,1,0:T(8,128)(2,1)S(1)}, bf16[128,128]{1,0:T(8,128)(2,1)S(1)}) custom-call(s32[2]{0:T(128)S(1)} %pad_add_fusion.place_ref, s32[16]{0:T(128)S(1)} %copy-done, bf16[8,384,128]{2,1,0:T(8,128)(2,1)S(1)} %all-to-all-done.sent_ref, ...), custom_call_target="tpu_custom_call" | custom-call | bytes 2097152 | tf_op jit(solution)/shard_map/gather_keys/pallas_call | solution.py:354
  26.2 2.7 %collective-permute-start.1 = (bf16[128,128]{1,0:T(8,128)(2,1)S(1)}, bf16[128,128]{1,0:T(8,128)(2,1)S(1)}, u32[]{:S(2)}, u32[]{:S(2)}) collective-permute-start(bf16[128,128]{1,0:T(8,128)(2,1)S(1)} %get-tuple-element.23.picks_ref), channel_id=1, source_target_pairs={{0,16},{2,18},{4,20},{6,22},{8,24},{10,26},{12,28},{14,30},{16,0},... | collective-permute-start | bytes 98312 | tf_op jit(solution)/shard_map/ppermute | solution.py:396
  28.9 2.7 %all-to-all-done.1.grads_ref = bf16[8,128,128]{2,1,0:T(8,128)(2,1)S(1)} async-done(((bf16[8,128,128]{2,1,0:T(8,128)(2,1)}), bf16[8,128,128]{2,1,0:T(8,128)(2,1)S(1)}, u32[]{:S(2)}, u32[]{:S(2)}) %all-to-all-start.1) | async-done | bytes 262176 | tf_op jit(solution)/shard_map/all_to_all | solution.py:392
  31.6 0.0 collective-permute-done.1.refs_0_
  31.6 1.9 %picked_rows.1 = (bf16[144,128]{1,0:T(8,128)(2,1)S(1)}, f32[128,128]{1,0:T(8,128)S(1)}, f32[128,128]{1,0:T(8,128)S(1)}) custom-call(s32[2]{0:T(128)S(1)} %pad_add_fusion.place_ref, s32[16]{0:T(128)S(1)} %copy-done, bf16[2048,128]{1,0:T(8,128)(2,1)S(1)} %get-tuple-element.20.near_ref.keys_ref, bf16[8,128,128]{2,1,0:T(8,128)(2,1)S(1)} %get-tuple-element.22.queries_ref, ...), custom_call_target="tpu_custom_call" | custom-call | flops 268435456 | bytes 2097152 | tf_op jit(solution)/shard_map/picked_rows/pallas_call | solution.py:354
  33.5 2.3 %collective-permute-start.2 = (f32[128,128]{1,0:T(8,128)S(1)}, f32[128,128]{1,0:T(8,128)S(1)}, u32[]{:S(2)}, u32[]{:S(2)}) collective-permute-start(f32[128,128]{1,0:T(8,128)S(1)} %get-tuple-element.28), channel_id=1, source_target_pairs={{0,16},{2,18},{4,20},{6,22},{8,24},{10,26},{12,28},{14,30},{16,0},... | collective-permute-start | bytes 196616 | tf_op jit(solution)/shard_map/ppermute | solution.py:396
  35.8 8.8 %first_rows.1 = (f32[2048,128]{1,0:T(8,128)S(1)}, bf16[4,128,128]{2,1,0:T(8,128)(2,1)S(1)}) custom-call(s32[2]{0:T(128)S(1)} %pad_add_fusion.place_ref, s32[16]{0:T(128)S(1)} %copy-done, bf16[2048,128]{1,0:T(8,128)(2,1)S(1)} %get-tuple-element.20.near_ref.keys_ref, bf16[64,2048]{1,0:T(8,128)(2,1)S(1)} %get-tuple-element.21.key_t_ref, ...), custom_call_target="tpu_custom_call" | custom-call | flops 2684354560 | bytes 2097152 | tf_op jit(solution)/shard_map/first_rows/pallas_call | solution.py:354
  44.6 0.0 collective-permute-done.2.refs_0_
  44.6 9.2 %second_rows.1 = (bf16[384,128]{1,0:T(8,128)(2,1)S(1)}, bf16[384,128]{1,0:T(8,128)(2,1)S(1)}, bf16[384,128]{1,0:T(8,128)(2,1)S(1)}, bf16[384,128]{1,0:T(8,128)(2...) custom-call(s32[2]{0:T(128)S(1)} %pad_add_fusion.place_ref, ...), custom_call_target="tpu_custom_call" | custom-call | flops 2684354560 | bytes 2097152 | tf_op jit(solution)/shard_map/second_rows/pallas_call | solution.py:354
  53.8 0.1 collective-permute-start.3
  53.9 1.8 %collective-permute-start.4 = (bf16[384,128]{1,0:T(8,128)(2,1)S(1)}, bf16[384,128]{1,0:T(8,128)(2,1)S(1)}, u32[]{:S(2)}, u32[]{:S(2)}) collective-permute-start(bf16[384,128]{1,0:T(8,128)(2,1)S(1)} %get-tuple-element.31), channel_id=1, source_target_pairs={{0,4},{2,6},{4,0},{6,2},{8,12},{10,14},{12,8},{14,10},{16,20},{18,... | collective-permute-start | bytes 294920 | tf_op jit(solution)/shard_map/ppermute | solution.py:387
  55.7 0.1 collective-permute-start.5
  55.8 1.8 %collective-permute-start.6 = (bf16[384,128]{1,0:T(8,128)(2,1)S(1)}, bf16[384,128]{1,0:T(8,128)(2,1)S(1)}, u32[]{:S(2)}, u32[]{:S(2)}) collective-permute-start(bf16[384,128]{1,0:T(8,128)(2,1)S(1)} %get-tuple-element.33), channel_id=1, source_target_pairs={{0,8},{2,10},{4,12},{6,14},{8,0},{10,2},{12,4},{14,6},{16,24},{18,... | collective-permute-start | bytes 294920 | tf_op jit(solution)/shard_map/ppermute | solution.py:387
  57.6 0.0 collective-permute-start.7
  57.6 0.0 collective-permute-done.3.refs_1_
  57.6 2.9 %collective-permute-start.8 = (bf16[384,128]{1,0:T(8,128)(2,1)S(1)}, bf16[384,128]{1,0:T(8,128)(2,1)S(1)}, u32[]{:S(2)}, u32[]{:S(2)}) collective-permute-start(bf16[384,128]{1,0:T(8,128)(2,1)S(1)} %get-tuple-element.35), channel_id=1, source_target_pairs={{0,12},{2,14},{4,8},{6,10},{8,4},{10,6},{12,0},{14,2},{16,28},{18,... | collective-permute-start | bytes 294920 | tf_op jit(solution)/shard_map/ppermute | solution.py:387
  60.5 0.0 collective-permute-done.4.refs_2_
  60.5 0.9 %collective-permute-start.9 = (bf16[384,128]{1,0:T(8,128)(2,1)S(1)}, bf16[384,128]{1,0:T(8,128)(2,1)S(1)}, u32[]{:S(2)}, u32[]{:S(2)}) collective-permute-start(bf16[384,128]{1,0:T(8,128)(2,1)S(1)} %get-tuple-element.36), channel_id=1, source_target_pairs={{0,14},{2,12},{4,10},{6,8},{8,6},{10,4},{12,2},{14,0},{16,30},{18,... | collective-permute-start | bytes 294920 | tf_op jit(solution)/shard_map/ppermute | solution.py:387
  61.4 0.0 collective-permute-done.5.refs_3_
  61.4 0.0 collective-permute-done.6.refs_4_
  61.4 1.5 %collective-permute-done.7.refs_5_ = bf16[384,128]{1,0:T(8,128)(2,1)S(1)} collective-permute-done((bf16[384,128]{1,0:T(8,128)(2,1)S(1)}, bf16[384,128]{1,0:T(8,128)(2,1)S(1)}, u32[]{:S(2)}, u32[]{:S(2)}) %collective-permute-start.7) | collective-permute-done | bytes 98336 | tf_op jit(solution)/shard_map/ppermute | solution.py:387
  62.8 3.7 %collective-permute-done.8.refs_6_ = bf16[384,128]{1,0:T(8,128)(2,1)S(1)} collective-permute-done((bf16[384,128]{1,0:T(8,128)(2,1)S(1)}, bf16[384,128]{1,0:T(8,128)(2,1)S(1)}, u32[]{:S(2)}, u32[]{:S(2)}) %collective-permute-start.8) | collective-permute-done | bytes 98336 | tf_op jit(solution)/shard_map/ppermute | solution.py:387
  66.5 1.6 %collective-permute-done.9.refs_7_ = bf16[384,128]{1,0:T(8,128)(2,1)S(1)} collective-permute-done((bf16[384,128]{1,0:T(8,128)(2,1)S(1)}, bf16[384,128]{1,0:T(8,128)(2,1)S(1)}, u32[]{:S(2)}, u32[]{:S(2)}) %collective-permute-start.9) | collective-permute-done | bytes 98336 | tf_op jit(solution)/shard_map/ppermute | solution.py:387
  68.1 1.9 %unpack.1 = (bf16[256,512]{1,0:T(8,128)(2,1)}, bf16[256,512]{1,0:T(8,128)(2,1)}, bf16[256,512]{1,0:T(8,128)(2,1)}) custom-call(s32[2]{0:T(128)S(1)} %pad_add_fusion.place_ref, bf16[384,128]{1,0:T(8,128)(2,1)S(1)} %get-tuple-element.29.refs_0_, bf16[384,128]{1,0:T(8,128)(2,1)S(1)} %collective-permute-done.3.refs_1_, ...), custom_call_target="tpu_custom_call" | custom-call | bytes 2097152 | tf_op jit(solution)/shard_map/unpack/pallas_call | solution.py:354
Async XLA Ops:
  0.6 9.5 %collective-permute-start = (bf16[128,1024]{1,0:T(8,128)(2,1)}, bf16[128,1024]{1,0:T(8,128)(2,1)S(1)}, u32[]{:S(2)}, u32[]{:S(2)}) collective-permute-start(bf16[128,1024]{1,0:T(8,128)(2,1)} %refs_0_.1), channel_id=1, source_target_pairs={{0,1},{1,0},{2,3},{3,2},{4,5},{5,4},{6,7},{7,6},{8,9},{9,8},{10,11... | collective-permute-start | bytes 786440 | tf_op jit(solution)/shard_map/ppermute | solution.py:401
  5.9 4.2 %copy-start.1 = (bf16[512,1024]{1,0:T(8,128)(2,1)S(1)}, bf16[512,1024]{1,0:T(8,128)(2,1)}, u32[]{:S(2)}) copy-start(bf16[512,1024]{1,0:T(8,128)(2,1)} %weight_ref.1) | copy-start | bytes 3145732
  5.9 4.2 %copy-start.2 = (bf16[128,1024]{1,0:T(8,128)(2,1)S(1)}, bf16[128,1024]{1,0:T(8,128)(2,1)}, u32[]{:S(2)}) copy-start(bf16[128,1024]{1,0:T(8,128)(2,1)} %refs_0_.1) | copy-start | bytes 786436
  6.0 15.6 %all-to-all-start = ((bf16[8,384,128]{2,1,0:T(8,128)(2,1)}), bf16[8,384,128]{2,1,0:T(8,128)(2,1)S(1)}, u32[]{:S(2)}, u32[]{:S(2)}) async-start(bf16[8,384,128]{2,1,0:T(8,128)(2,1)} %pack_rows.1), calls=%async_computation | async-start | bytes 1572864 | tf_op jit(solution)/shard_map/all_to_all | solution.py:392
  12.4 12.6 %copy-start = (s32[16]{0:T(128)S(1)}, s32[16]{0:T(128)}, u32[]{:S(2)}) copy-start(s32[16]{0:T(128)} %offset_ref.7) | copy-start | bytes 196
  21.6 10.1 %all-to-all-start.1 = ((bf16[8,128,128]{2,1,0:T(8,128)(2,1)}), bf16[8,128,128]{2,1,0:T(8,128)(2,1)S(1)}, u32[]{:S(2)}, u32[]{:S(2)}) async-start(bf16[8,128,128]{2,1,0:T(8,128)(2,1)} %project_pack.1.after_ref), calls=%async_computation.1 | async-start | bytes 524288 | tf_op jit(solution)/shard_map/all_to_all | solution.py:392
  26.2 5.4 %collective-permute-start.1 = (bf16[128,128]{1,0:T(8,128)(2,1)S(1)}, bf16[128,128]{1,0:T(8,128)(2,1)S(1)}, u32[]{:S(2)}, u32[]{:S(2)}) collective-permute-start(bf16[128,128]{1,0:T(8,128)(2,1)S(1)} %get-tuple-element.23.picks_ref), channel_id=1, source_target_pairs={{0,16},{2,18},{4,20},{6,22},{8,24},{10,26},{12,28},{14,30},{16,0},... | collective-permute-start | bytes 98312 | tf_op jit(solution)/shard_map/ppermute | solution.py:396
  33.5 11.1 %collective-permute-start.2 = (f32[128,128]{1,0:T(8,128)S(1)}, f32[128,128]{1,0:T(8,128)S(1)}, u32[]{:S(2)}, u32[]{:S(2)}) collective-permute-start(f32[128,128]{1,0:T(8,128)S(1)} %get-tuple-element.28), channel_id=1, source_target_pairs={{0,16},{2,18},{4,20},{6,22},{8,24},{10,26},{12,28},{14,30},{16,0},... | collective-permute-start | bytes 196616 | tf_op jit(solution)/shard_map/ppermute | solution.py:396
  53.8 3.8 %collective-permute-start.3 = (bf16[384,128]{1,0:T(8,128)(2,1)S(1)}, bf16[384,128]{1,0:T(8,128)(2,1)S(1)}, u32[]{:S(2)}, u32[]{:S(2)}) collective-permute-start(bf16[384,128]{1,0:T(8,128)(2,1)S(1)} %get-tuple-element.30), channel_id=1, source_target_pairs={{0,2},{2,0},{4,6},{6,4},{8,10},{10,8},{12,14},{14,12},{16,18},{18,... | collective-permute-start | bytes 294920 | tf_op jit(solution)/shard_map/ppermute | solution.py:387
  53.9 6.6 %collective-permute-start.4 = (bf16[384,128]{1,0:T(8,128)(2,1)S(1)}, bf16[384,128]{1,0:T(8,128)(2,1)S(1)}, u32[]{:S(2)}, u32[]{:S(2)}) collective-permute-start(bf16[384,128]{1,0:T(8,128)(2,1)S(1)} %get-tuple-element.31), channel_id=1, source_target_pairs={{0,4},{2,6},{4,0},{6,2},{8,12},{10,14},{12,8},{14,10},{16,20},{18,... | collective-permute-start | bytes 294920 | tf_op jit(solution)/shard_map/ppermute | solution.py:387
  55.7 5.7 %collective-permute-start.5 = (bf16[384,128]{1,0:T(8,128)(2,1)S(1)}, bf16[384,128]{1,0:T(8,128)(2,1)S(1)}, u32[]{:S(2)}, u32[]{:S(2)}) collective-permute-start(bf16[384,128]{1,0:T(8,128)(2,1)S(1)} %get-tuple-element.32), channel_id=1, source_target_pairs={{0,6},{2,4},{4,2},{6,0},{8,14},{10,12},{12,10},{14,8},{16,22},{18,... | collective-permute-start | bytes 294920 | tf_op jit(solution)/shard_map/ppermute | solution.py:387
  55.8 5.6 %collective-permute-start.6 = (bf16[384,128]{1,0:T(8,128)(2,1)S(1)}, bf16[384,128]{1,0:T(8,128)(2,1)S(1)}, u32[]{:S(2)}, u32[]{:S(2)}) collective-permute-start(bf16[384,128]{1,0:T(8,128)(2,1)S(1)} %get-tuple-element.33), channel_id=1, source_target_pairs={{0,8},{2,10},{4,12},{6,14},{8,0},{10,2},{12,4},{14,6},{16,24},{18,... | collective-permute-start | bytes 294920 | tf_op jit(solution)/shard_map/ppermute | solution.py:387
  57.6 5.2 %collective-permute-start.7 = (bf16[384,128]{1,0:T(8,128)(2,1)S(1)}, bf16[384,128]{1,0:T(8,128)(2,1)S(1)}, u32[]{:S(2)}, u32[]{:S(2)}) collective-permute-start(bf16[384,128]{1,0:T(8,128)(2,1)S(1)} %get-tuple-element.34), channel_id=1, source_target_pairs={{0,10},{2,8},{4,14},{6,12},{8,2},{10,0},{12,6},{14,4},{16,26},{18,... | collective-permute-start | bytes 294920 | tf_op jit(solution)/shard_map/ppermute | solution.py:387
  57.6 8.9 %collective-permute-start.8 = (bf16[384,128]{1,0:T(8,128)(2,1)S(1)}, bf16[384,128]{1,0:T(8,128)(2,1)S(1)}, u32[]{:S(2)}, u32[]{:S(2)}) collective-permute-start(bf16[384,128]{1,0:T(8,128)(2,1)S(1)} %get-tuple-element.35), channel_id=1, source_target_pairs={{0,12},{2,14},{4,8},{6,10},{8,4},{10,6},{12,0},{14,2},{16,28},{18,... | collective-permute-start | bytes 294920 | tf_op jit(solution)/shard_map/ppermute | solution.py:387
  60.5 7.6 %collective-permute-start.9 = (bf16[384,128]{1,0:T(8,128)(2,1)S(1)}, bf16[384,128]{1,0:T(8,128)(2,1)S(1)}, u32[]{:S(2)}, u32[]{:S(2)}) collective-permute-start(bf16[384,128]{1,0:T(8,128)(2,1)S(1)} %get-tuple-element.36), channel_id=1, source_target_pairs={{0,14},{2,12},{4,10},{6,8},{8,6},{10,4},{12,2},{14,0},{16,30},{18,... | collective-permute-start | bytes 294920 | tf_op jit(solution)/shard_map/ppermute | solution.py:387

commit v7 on v6

--- a/solution.py
+++ b/solution.py
@@ -16,7 +16,7 @@
 LOG2E = math.log2(math.e)
 SCORE_FACTOR = SCALE * LOG2E
 STRIP = 64
-PIECE = 512
+PIECE = 256
 BUSY = 2**35
 STAT_ROWS = 16
 
@@ -109,8 +109,9 @@
             out_ref[place, rows:, :] = query
 
 
-def project_kernel(head_count, shards, place_ref, weight_ref, *refs):
-    upstream_refs, (out_ref, grad_ref) = refs[:shards], refs[shards:]
+def project_kernel(head_count, group, shards, place_ref, weight_ref, *refs):
+    upstream_refs, refs = refs[:shards], refs[shards:]
+    out_refs, (grad_ref, stage_ref) = refs[:group], refs[group:]
     shard_rows = upstream_refs[0].shape[0]
     for step, upstream_ref in enumerate(upstream_refs):
         owner = lax.rem(place_ref[1] + (shards - step), shards)
@@ -120,8 +121,9 @@
         ).astype(jnp.bfloat16)
     for head in range(head_count):
         grad = side_by_side(head_columns(grad_ref, head))
-        for place in range(head, out_ref.shape[0], head_count):
-            out_ref[place] = grad
+        for place in range(head, group, head_count):
+            stage_ref[place] = grad
+    send_out(place_ref[0], stage_ref, out_refs)
 
 
 def own_offset(head_count, place_ref, offset_ref):
@@ -166,11 +168,11 @@
 
 
 def far_kernel(
-    head_count, group, others, place_ref, offset_ref, near_ref, queries_ref, grads_ref, picks_ref,
-    *refs,
+    head_count, group, others, place_ref, offset_ref, near_ref, queries_ref, picks_ref, *refs
 ):
     other_refs, refs = refs[:others], refs[others:]
-    extra_out, own_out, other_out, keys_ref, query_ref, grad_ref = refs
+    grad_refs, refs = refs[:group], refs[group:]
+    extra_out, own_out, other_out, grads_out, keys_ref, query_ref, grad_ref = refs
     near = near_ref.shape[0]
     rows = near // group
     picked = rows // DILATION_RATE
@@ -180,8 +182,10 @@
     keys_ref[:near, :] = near_ref[...]
     for index, ref in enumerate([picks_ref, *other_refs]):
         keys_ref[near + index * count : near + (index + 1) * count, :] = ref[...]
+    for bits, ref in enumerate(grad_refs):
+        grads_out[lax.bitwise_xor(place_ref[0], bits)] = ref[...]
     for step in range(group):
-        query, grad = query_and_grad(queries_ref.at[step], grads_ref.at[step])
+        query, grad = query_and_grad(queries_ref.at[step], grads_out.at[step])
         span = slice(step * picked, (step + 1) * picked)
         query_ref[span, :] = dot_nn(pick, query).astype(jnp.bfloat16)
         grad_ref[span, :] = dot_nn(pick, grad).astype(jnp.bfloat16)
@@ -211,76 +215,86 @@
 
 def near_blocks(
     places, offset, keys_ref, key_t_ref, queries_ref, grads_ref, extra_ref,
-    score_ref, dprob_ref, work_ref, acc_ref, emit,
+    prob_ref, dprob_ref, work_ref, top_ref, acc_ref, emit,
 ):
     near = keys_ref.shape[0]
-    rows = score_ref.shape[2]
+    rows = prob_ref.shape[2]
     half = rows // 2
     count = extra_ref.shape[1]
-    pieces = [slice(start, start + PIECE) for start in range(0, near, PIECE)]
     row_lane = lax.broadcasted_iota(jnp.int32, (1, rows), 1)
     picked = lax.rem(row_lane, DILATION_RATE) == offset
 
-    def strips(piece):
-        return [slice(start, start + STRIP) for start in range(piece.start, piece.stop, STRIP)]
-
-    def first_matmuls(index, weights, piece):
-        query, grad = weights
-        score_ref[index % 2, piece, :] = dot_nt(keys_ref[piece, :], query)
-        dprob_ref[index % 2, piece, :] = dot_nt(keys_ref[piece, :], grad)
-
-    def maximum(index, top, piece):
-        for strip in strips(piece):
-            part = fold(score_ref[index % 2, strip, :], jnp.maximum)
-            top = part if top is None else jnp.maximum(top, part)
-        return top
+    def by_eight(value):
+        return value.reshape(value.shape[0] // 8, 8, rows)
 
     def weights_of(index):
         return query_and_grad(queries_ref.at[places[index]], grads_ref.at[places[index]])
 
+    def first_pass(index, weights, start, state):
+        top, total, delta = state
+        slot = index % 2
+        query, grad = weights
+        keys = keys_ref[start : start + PIECE, :]
+        scores, dprobs = dot_nt(keys, query), dot_nt(keys, grad)
+        for inner in range(0, PIECE, STRIP):
+            strip = slice(start + inner, start + inner + STRIP)
+            score, dprob = scores[inner : inner + STRIP], dprobs[inner : inner + STRIP]
+            part = fold(score, jnp.maximum) * SCORE_FACTOR
+            raised = part if top is None else jnp.maximum(top, part)
+            prob = jnp.exp2(by_eight(score) * SCORE_FACTOR - raised[None])
+            part_total = jnp.sum(prob, 0)
+            part_delta = jnp.sum(prob * by_eight(dprob), 0)
+            if top is None:
+                total, delta = part_total, part_delta
+            else:
+                shrink = jnp.exp2(top - raised)
+                total, delta = total * shrink + part_total, delta * shrink + part_delta
+            top = raised
+            prob_ref[slot, strip, :] = prob.reshape(STRIP, rows)
+            dprob_ref[slot, strip, :] = dprob
+            top_ref[slot, strip.start // STRIP] = raised
+        return top, total, delta
+
+    def last_pass(index, lse, delta, both, start, query_grad):
+        slot = index % 2
+        piece = slice(start, start + PIECE)
+        for inner in range(0, PIECE, STRIP):
+            strip = slice(start + inner, start + inner + STRIP)
+            factor = jnp.exp2(top_ref[slot, strip.start // STRIP] - lse)
+            prob = by_eight(prob_ref[slot, strip, :]) * factor[None]
+            dscore = prob * (by_eight(dprob_ref[slot, strip, :]) - delta)
+            work_ref[slot, strip, :rows] = dscore.reshape(STRIP, rows).astype(jnp.bfloat16)
+            work_ref[slot, strip, rows:] = prob.reshape(STRIP, rows).astype(jnp.bfloat16)
+        acc_ref[piece, :] += dot_nn(work_ref[slot, piece, :], both)
+        return query_grad + dot_nn(key_t_ref[:, piece], work_ref[slot, piece, :rows])
+
+    starts = range(0, near, PIECE)
     weights = weights_of(0)
-    top = None
-    for piece in pieces:
-        first_matmuls(0, weights, piece)
-        top = maximum(0, top, piece)
+    state = (None, None, None)
+    for start in starts:
+        state = first_pass(0, weights, start, state)
     for index, place in enumerate(places):
-        slot = index % 2
         last = index + 1 == len(places)
         first = place * (rows // DILATION_RATE)
         extra = dot_nn(extra_ref[...], spread_matrix(offset, first, count, rows, 0))
         stats = [extra[PAIR + row : PAIR + row + 1] for row in range(6)]
-        top = jnp.max(top, 0, keepdims=True) * SCORE_FACTOR
-        top = jnp.where(picked, stats[0] + stats[1] + stats[2], top)
-        total = jnp.zeros((8, rows), jnp.float32)
-        delta = jnp.zeros((8, rows), jnp.float32)
-        after = None if last else weights_of(index + 1)
-        for piece in pieces:
-            if not last:
-                first_matmuls(index + 1, after, piece)
-            for strip in strips(piece):
-                prob = jnp.exp2(score_ref[slot, strip, :] * SCORE_FACTOR - top)
-                total = total + fold(prob, jnp.add)
-                delta = delta + fold(prob * dprob_ref[slot, strip, :], jnp.add)
-                score_ref[slot, strip, :] = prob
-        inverse = jnp.where(picked, 1.0, 1.0 / jnp.sum(total, 0, keepdims=True))
-        delta = jnp.sum(delta, 0, keepdims=True) * inverse
+        top, total, delta = state
+        highest = jnp.max(top, 0, keepdims=True)
+        shrink = jnp.exp2(top - highest)
+        total = jnp.sum(total * shrink, 0, keepdims=True)
+        delta = jnp.sum(delta * shrink, 0, keepdims=True) / total
+        lse = jnp.where(picked, stats[0] + stats[1] + stats[2], highest + jnp.log2(total))
         delta = jnp.where(picked, stats[3] + stats[4] + stats[5], delta)
         both = jnp.concatenate(weights, 0)
         query_grad = extra[:HEAD_SIZE] + extra[HEAD_SIZE:PAIR]
-        top = None
-        for piece in pieces:
-            for strip in strips(piece):
-                prob = score_ref[slot, strip, :] * inverse
-                dscore = prob * (dprob_ref[slot, strip, :] - delta)
-                work_ref[slot, strip, :rows] = dscore.astype(jnp.bfloat16)
-                work_ref[slot, strip, rows:] = prob.astype(jnp.bfloat16)
-            acc_ref[piece, :] += dot_nn(work_ref[slot, piece, :], both)
-            query_grad = query_grad + dot_nn(key_t_ref[:, piece], work_ref[slot, piece, :rows])
+        weights = None if last else weights_of(index + 1)
+        state = (None, None, None)
+        for start in starts:
             if not last:
-                top = maximum(index + 1, top, piece)
+                state = first_pass(index + 1, weights, start, state)
+            query_grad = last_pass(index, lse, delta, both, start, query_grad)
         query_grad = (query_grad * SCALE).T.astype(jnp.bfloat16)
         emit(place, jnp.concatenate([query_grad[:half], query_grad[half:]], 1))
-        weights = after
 
 
 def first_kernel(
@@ -409,30 +423,30 @@
         flops=2**31, space=ANY, limit=60,
     )
     sent = exchange(sent)
-    (grads_send,) = call(
-        functools.partial(project_kernel, head_count, shards), "project_pack",
-        [((group, half, PAIR), bf16)],
+    grads_send = call(
+        functools.partial(project_kernel, head_count, group, shards), "project_pack",
+        [((half, PAIR), bf16)] * group,
         [place], [out_weight, *upstreams],
-        [((rows, width), bf16)],
+        [((rows, width), bf16), ((group, half, PAIR), bf16)],
         flops=BUSY,
     )
-    grads = exchange(grads_send)
+    grads = swap(grads_send)
     keys, key_t, queries, picks = call(
         functools.partial(gather_kernel, head_count), "gather_keys",
         [
             ((near, PAIR), bf16), ((HEAD_SIZE, near), bf16), ((group, half, PAIR), bf16),
             ((count, PAIR), bf16),
         ],
-        scalars, [sent, grads_send],
+        scalars, [sent, grads_send[0]],
     )
     other_picks = [segment_shift(picks, shift) for shift in range(1, others + 1)]
-    extra, own_terms, other_terms = call(
+    extra, own_terms, other_terms, grads = call(
         functools.partial(far_kernel, head_count, group, others), "picked_rows",
         [
             ((PAIR + STAT_ROWS, count), bf16), ((count, PAIR), f32),
-            ((others * count, PAIR), f32),
+            ((others * count, PAIR), f32), ((group, half, PAIR), bf16),
         ],
-        scalars, [keys, queries, grads, picks, *other_picks],
+        scalars, [keys, queries, picks, *other_picks, *grads],
         [((near + count * (1 + others), PAIR), bf16)] + [((count, PAIR), bf16)] * 2,
         flops=8 * near * count * PAIR,
     )
@@ -443,6 +457,7 @@
     steps = group // 2
     scratch = [
         ((2, near, rows), f32), ((2, near, rows), f32), ((2, near, 2 * rows), bf16),
+        ((2, near // STRIP, 8, rows), f32),
     ]
     half_flops = 10 * near * near // 2 * PAIR
     acc, query_half = call(

time: 70.4 us -> 65.2 us (0.926)
  Pallas kernels: 27.5 us -> 24 us
  waiting for transfers between devices: 18.8 us -> 16 us
  starting transfers between devices: 22.9 us -> 24.2 us
    all_to_all x2 -> x1, waiting for transfers between devices: 11.9 us -> 6.43 us  [exchange(): return lax.all_to_all(value, 'context', 0, 0, axis_index_groups=groups)]
    ppermute x7 -> x14, starting transfers between devices: 7.53 us -> 11.9 us  [swap(): lax.ppermute(values[bits], 'context', pairs[bits])]
    pallas_call x7, Pallas kernels: 27.5 us -> 24 us  [call(): pl.pallas_call(kernel, out_shape=tuple((jax.ShapeDtypeStruct(*shape) for...]
    all_to_all x2 -> x1, starting transfers between devices: 7.37 us -> 3.95 us  [exchange(): return lax.all_to_all(value, 'context', 0, 0, axis_index_groups=groups)]
    ppermute x7 -> x14, waiting for transfers between devices: 6.74 us -> 8.74 us  [swap(): lax.ppermute(values[bits], 'context', pairs[bits])]
  transfers between devices with their start and end apart: 12 -> 18, of which waited for: 6 -> 11; matrix products, arithmetic and copies ran while one was open for 0% -> 0% of each run, Pallas kernels for 21% -> 19%
where the time goes in v7:
time: 65.2 us; the launch traced here: 65 us
  starting transfers between devices  24.2 us (37%)
  Pallas kernels  24 us (37%)
  waiting for transfers between devices  16 us (25%)
  between operations  0.72 us (1%)
    pallas_call x7, Pallas kernels, call(): pl.pallas_call(kernel, out_shape=tuple((jax.ShapeDtypeStruct(*shape) for...  24 us
    ppermute x14, starting transfers between devices, swap(): lax.ppermute(values[bits], 'context', pairs[bits])  11.9 us
    ppermute x14, waiting for transfers between devices, swap(): lax.ppermute(values[bits], 'context', pairs[bits])  8.74 us
    all_to_all x1, waiting for transfers between devices, exchange(): return lax.all_to_all(value, 'context', 0, 0, axis_index_groups=groups)  6.43 us
    ppermute x2, starting transfers between devices, segment_shift(): return lax.ppermute(value, 'context', pairs)  5.35 us
    all_to_all x1, starting transfers between devices, exchange(): return lax.all_to_all(value, 'context', 0, 0, axis_index_groups=groups)  3.95 us
    ppermute x1, starting transfers between devices, body(): upstreams.append(lax.ppermute(upstream, 'heads', pairs))  3 us
  transfers between devices with their start and end apart: 18, of which 11 were waited for; matrix products, arithmetic and copies ran while one was open for 0% of the time, Pallas kernels for 19%

profile of v7, /device:TPU:0, one launch (start us, length us, event | category | flops | bytes accessed | tf_op | source)
XLA Modules:
  0.0 65.0 jit_solution(5744683371766177290)
XLA Ops:
  0.6 3.0 %collective-permute-start = (bf16[128,1024]{1,0:T(8,128)(2,1)}, bf16[128,1024]{1,0:T(8,128)(2,1)S(1)}, u32[]{:S(2)}, u32[]{:S(2)}) collective-permute-start(bf16[128,1024]{1,0:T(8,128)(2,1)} %refs_0_.1), channel_id=1, source_target_pairs={{0,1},{1,0},{2,3},{3,2},{4,5},{5,4},{6,7},{7,6},{8,9},{9,8},{10,11... | collective-permute-start | bytes 786440 | tf_op jit(solution)/shard_map/ppermute | solution.py:415
  3.6 2.3 %pack_rows.1 = bf16[8,384,128]{2,1,0:T(8,128)(2,1)} custom-call(bf16[256,512]{1,0:T(8,128)(2,1)} %query_hbm.1, bf16[256,512]{1,0:T(8,128)(2,1)} %key_hbm.1, bf16[256,512]{1,0:T(8,128)(2,1)} %value_hbm.1), custom_call_target="tpu_custom_call" | custom-call | flops 2147483648 | bytes 2097152 | tf_op jit(solution)/shard_map/pack_rows/pallas_call | solution.py:368
  5.9 0.0 copy-start.1
  5.9 0.0 copy-start.2
  6.0 4.0 %all-to-all-start = ((bf16[8,384,128]{2,1,0:T(8,128)(2,1)}), bf16[8,384,128]{2,1,0:T(8,128)(2,1)S(1)}, u32[]{:S(2)}, u32[]{:S(2)}) async-start(bf16[8,384,128]{2,1,0:T(8,128)(2,1)} %pack_rows.1), calls=%async_computation | async-start | bytes 1572864 | tf_op jit(solution)/shard_map/all_to_all | solution.py:406
  9.9 0.1 pad_add_fusion.place_ref
  10.0 0.2 collective-permute-done.refs_1_
  10.2 0.0 copy-done.1
  10.2 0.0 copy-done.2
  10.2 1.5 %project_pack.1 = (bf16[128,128]{1,0:T(8,128)(2,1)S(1)}, bf16[128,128]{1,0:T(8,128)(2,1)S(1)}, bf16[128,128]{1,0:T(8,128)(2,1)S(1)}, bf16[128,128]{1,0:T(8,128)(...) custom-call(s32[2]{0:T(128)S(1)} %pad_add_fusion.place_ref, ...), custom_call_target="tpu_custom_call" | custom-call | flops 34359738368 | bytes 2097152 | tf_op jit(solution)/shard_map/project_pack/pallas_call | solution.py:368
  11.7 0.4 collective-permute-start.2
  12.1 1.7 %collective-permute-start.3 = (bf16[128,128]{1,0:T(8,128)(2,1)S(1)}, bf16[128,128]{1,0:T(8,128)(2,1)S(1)}, u32[]{:S(2)}, u32[]{:S(2)}) collective-permute-start(bf16[128,128]{1,0:T(8,128)(2,1)S(1)} %get-tuple-element.35), channel_id=1, source_target_pairs={{0,4},{2,6},{4,0},{6,2},{8,12},{10,14},{12,8},{14,10},{16,20},{18,... | collective-permute-start | bytes 98312 | tf_op jit(solution)/shard_map/ppermute | solution.py:401
  13.8 0.0 collective-permute-start.4
  13.8 1.7 %collective-permute-start.5 = (bf16[128,128]{1,0:T(8,128)(2,1)S(1)}, bf16[128,128]{1,0:T(8,128)(2,1)S(1)}, u32[]{:S(2)}, u32[]{:S(2)}) collective-permute-start(bf16[128,128]{1,0:T(8,128)(2,1)S(1)} %get-tuple-element.37), channel_id=1, source_target_pairs={{0,8},{2,10},{4,12},{6,14},{8,0},{10,2},{12,4},{14,6},{16,24},{18,... | collective-permute-start | bytes 98312 | tf_op jit(solution)/shard_map/ppermute | solution.py:401
  15.5 0.0 copy-start
  15.5 0.1 collective-permute-start.6
  15.6 6.4 %all-to-all-done.sent_ref = bf16[8,384,128]{2,1,0:T(8,128)(2,1)S(1)} async-done(((bf16[8,384,128]{2,1,0:T(8,128)(2,1)}), bf16[8,384,128]{2,1,0:T(8,128)(2,1)S(1)}, u32[]{:S(2)}, u32[]{:S(2)}) %all-to-all-start) | async-done | bytes 786464 | tf_op jit(solution)/shard_map/all_to_all | solution.py:406
  22.0 0.0 copy-done
  22.0 0.8 %gather_keys.1 = (bf16[2048,128]{1,0:T(8,128)(2,1)S(1)}, bf16[64,2048]{1,0:T(8,128)(2,1)S(1)}, bf16[8,128,128]{2,1,0:T(8,128)(2,1)S(1)}, bf16[128,128]{1,0:T(8,128)(2,1)S(1)}) custom-call(s32[2]{0:T(128)S(1)} %pad_add_fusion.place_ref, s32[16]{0:T(128)S(1)} %copy-done, bf16[8,384,128]{2,1,0:T(8,128)(2,1)S(1)} %all-to-all-done.sent_ref, ...), custom_call_target="tpu_custom_call" | custom-call | bytes 2097152 | tf_op jit(solution)/shard_map/gather_keys/pallas_call | solution.py:368
  22.8 0.0 collective-permute-done.2.refs_2_
  22.8 1.5 %collective-permute-start.7 = (bf16[128,128]{1,0:T(8,128)(2,1)S(1)}, bf16[128,128]{1,0:T(8,128)(2,1)S(1)}, u32[]{:S(2)}, u32[]{:S(2)}) collective-permute-start(bf16[128,128]{1,0:T(8,128)(2,1)S(1)} %get-tuple-element.39), channel_id=1, source_target_pairs={{0,12},{2,14},{4,8},{6,10},{8,4},{10,6},{12,0},{14,2},{16,28},{18,... | collective-permute-start | bytes 98312 | tf_op jit(solution)/shard_map/ppermute | solution.py:401
  24.4 0.0 collective-permute-done.3.refs_3_
  24.4 0.0 collective-permute-start.8
  24.4 0.0 collective-permute-done.4.refs_4_
  24.4 2.7 %collective-permute-start.1 = (bf16[128,128]{1,0:T(8,128)(2,1)S(1)}, bf16[128,128]{1,0:T(8,128)(2,1)S(1)}, u32[]{:S(2)}, u32[]{:S(2)}) collective-permute-start(bf16[128,128]{1,0:T(8,128)(2,1)S(1)} %get-tuple-element.33.picks_ref), channel_id=1, source_target_pairs={{0,16},{2,18},{4,20},{6,22},{8,24},{10,26},{12,28},{14,30},{16,0},... | collective-permute-start | bytes 98312 | tf_op jit(solution)/shard_map/ppermute | solution.py:410
  27.0 0.0 collective-permute-done.5.refs_5_
  27.0 0.0 collective-permute-done.6.refs_6_
  27.0 0.7 %collective-permute-done.7.refs_7_ = bf16[128,128]{1,0:T(8,128)(2,1)S(1)} collective-permute-done((bf16[128,128]{1,0:T(8,128)(2,1)S(1)}, bf16[128,128]{1,0:T(8,128)(2,1)S(1)}, u32[]{:S(2)}, u32[]{:S(2)}) %collective-permute-start.7) | collective-permute-done | bytes 32800 | tf_op jit(solution)/shard_map/ppermute | solution.py:401
  27.7 0.9 %collective-permute-done.8.refs_8_ = bf16[128,128]{1,0:T(8,128)(2,1)S(1)} collective-permute-done((bf16[128,128]{1,0:T(8,128)(2,1)S(1)}, bf16[128,128]{1,0:T(8,128)(2,1)S(1)}, u32[]{:S(2)}, u32[]{:S(2)}) %collective-permute-start.8) | collective-permute-done | bytes 32800 | tf_op jit(solution)/shard_map/ppermute | solution.py:401
  28.6 0.6 collective-permute-done.1.refs_0_
  29.3 1.9 %picked_rows.1 = (bf16[144,128]{1,0:T(8,128)(2,1)S(1)}, f32[128,128]{1,0:T(8,128)S(1)}, f32[128,128]{1,0:T(8,128)S(1)}, bf16[8,128,128]{2,1,0:T(8,128)(2,1)S(1)}) custom-call(s32[2]{0:T(128)S(1)} %pad_add_fusion.place_ref, s32[16]{0:T(128)S(1)} %copy-done, bf16[2048,128]{1,0:T(8,128)(2,1)S(1)} %get-tuple-element.30.near_ref.keys_ref, ...), custom_call_target="tpu_custom_call" | custom-call | flops 268435456 | bytes 2097152 | tf_op jit(solution)/shard_map/picked_rows/pallas_call | solution.py:368
  31.1 2.7 %collective-permute-start.9 = (f32[128,128]{1,0:T(8,128)S(1)}, f32[128,128]{1,0:T(8,128)S(1)}, u32[]{:S(2)}, u32[]{:S(2)}) collective-permute-start(f32[128,128]{1,0:T(8,128)S(1)} %get-tuple-element.46), channel_id=1, source_target_pairs={{0,16},{2,18},{4,20},{6,22},{8,24},{10,26},{12,28},{14,30},{16,0},... | collective-permute-start | bytes 196616 | tf_op jit(solution)/shard_map/ppermute | solution.py:410
  33.8 7.7 %first_rows.1 = (f32[2048,128]{1,0:T(8,128)S(1)}, bf16[4,128,128]{2,1,0:T(8,128)(2,1)S(1)}) custom-call(s32[2]{0:T(128)S(1)} %pad_add_fusion.place_ref, s32[16]{0:T(128)S(1)} %copy-done, bf16[2048,128]{1,0:T(8,128)(2,1)S(1)} %get-tuple-element.30.near_ref.keys_ref, bf16[64,2048]{1,0:T(8,128)(2,1)S(1)} %get-tuple-element.31.key_t_ref, ...), custom_call_target="tpu_custom_call" | custom-call | flops 2684354560 | bytes 2097152 | tf_op jit(solution)/shard_map/first_rows/pallas_call | solution.py:368
  41.5 0.0 collective-permute-done.9.refs_0_
  41.5 8.0 %second_rows.1 = (bf16[384,128]{1,0:T(8,128)(2,1)S(1)}, bf16[384,128]{1,0:T(8,128)(2,1)S(1)}, bf16[384,128]{1,0:T(8,128)(2,1)S(1)}, bf16[384,128]{1,0:T(8,128)(2...) custom-call(s32[2]{0:T(128)S(1)} %pad_add_fusion.place_ref, ...), custom_call_target="tpu_custom_call" | custom-call | flops 2684354560 | bytes 2097152 | tf_op jit(solution)/shard_map/second_rows/pallas_call | solution.py:368
  49.5 0.1 collective-permute-start.10
  49.6 1.5 %collective-permute-start.11 = (bf16[384,128]{1,0:T(8,128)(2,1)S(1)}, bf16[384,128]{1,0:T(8,128)(2,1)S(1)}, u32[]{:S(2)}, u32[]{:S(2)}) collective-permute-start(bf16[384,128]{1,0:T(8,128)(2,1)S(1)} %get-tuple-element.49), channel_id=1, source_target_pairs={{0,4},{2,6},{4,0},{6,2},{8,12},{10,14},{12,8},{14,10},{16,20},{18,... | collective-permute-start | bytes 294920 | tf_op jit(solution)/shard_map/ppermute | solution.py:401
  51.1 0.4 collective-permute-start.12
  51.4 2.3 %collective-permute-start.13 = (bf16[384,128]{1,0:T(8,128)(2,1)S(1)}, bf16[384,128]{1,0:T(8,128)(2,1)S(1)}, u32[]{:S(2)}, u32[]{:S(2)}) collective-permute-start(bf16[384,128]{1,0:T(8,128)(2,1)S(1)} %get-tuple-element.51), channel_id=1, source_target_pairs={{0,8},{2,10},{4,12},{6,14},{8,0},{10,2},{12,4},{14,6},{16,24},{18,... | collective-permute-start | bytes 294920 | tf_op jit(solution)/shard_map/ppermute | solution.py:401
  53.7 0.0 collective-permute-start.14
  53.7 0.0 collective-permute-done.10.refs_1_
  53.7 1.2 %collective-permute-start.15 = (bf16[384,128]{1,0:T(8,128)(2,1)S(1)}, bf16[384,128]{1,0:T(8,128)(2,1)S(1)}, u32[]{:S(2)}, u32[]{:S(2)}) collective-permute-start(bf16[384,128]{1,0:T(8,128)(2,1)S(1)} %get-tuple-element.53), channel_id=1, source_target_pairs={{0,12},{2,14},{4,8},{6,10},{8,4},{10,6},{12,0},{14,2},{16,28},{18,... | collective-permute-start | bytes 294920 | tf_op jit(solution)/shard_map/ppermute | solution.py:401
  54.9 0.3 collective-permute-done.11.refs_2_
  55.2 1.0 %collective-permute-start.16 = (bf16[384,128]{1,0:T(8,128)(2,1)S(1)}, bf16[384,128]{1,0:T(8,128)(2,1)S(1)}, u32[]{:S(2)}, u32[]{:S(2)}) collective-permute-start(bf16[384,128]{1,0:T(8,128)(2,1)S(1)} %get-tuple-element.54), channel_id=1, source_target_pairs={{0,14},{2,12},{4,10},{6,8},{8,6},{10,4},{12,2},{14,0},{16,30},{18,... | collective-permute-start | bytes 294920 | tf_op jit(solution)/shard_map/ppermute | solution.py:401
  56.2 0.2 collective-permute-done.12.refs_3_
  56.4 0.8 %collective-permute-done.13.refs_4_ = bf16[384,128]{1,0:T(8,128)(2,1)S(1)} collective-permute-done((bf16[384,128]{1,0:T(8,128)(2,1)S(1)}, bf16[384,128]{1,0:T(8,128)(2,1)S(1)}, u32[]{:S(2)}, u32[]{:S(2)}) %collective-permute-start.13) | collective-permute-done | bytes 98336 | tf_op jit(solution)/shard_map/ppermute | solution.py:401
  57.3 1.7 %collective-permute-done.14.refs_5_ = bf16[384,128]{1,0:T(8,128)(2,1)S(1)} collective-permute-done((bf16[384,128]{1,0:T(8,128)(2,1)S(1)}, bf16[384,128]{1,0:T(8,128)(2,1)S(1)}, u32[]{:S(2)}, u32[]{:S(2)}) %collective-permute-start.14) | collective-permute-done | bytes 98336 | tf_op jit(solution)/shard_map/ppermute | solution.py:401
  59.0 3.2 %collective-permute-done.15.refs_6_ = bf16[384,128]{1,0:T(8,128)(2,1)S(1)} collective-permute-done((bf16[384,128]{1,0:T(8,128)(2,1)S(1)}, bf16[384,128]{1,0:T(8,128)(2,1)S(1)}, u32[]{:S(2)}, u32[]{:S(2)}) %collective-permute-start.15) | collective-permute-done | bytes 98336 | tf_op jit(solution)/shard_map/ppermute | solution.py:401
  62.1 1.0 %collective-permute-done.16.refs_7_ = bf16[384,128]{1,0:T(8,128)(2,1)S(1)} collective-permute-done((bf16[384,128]{1,0:T(8,128)(2,1)S(1)}, bf16[384,128]{1,0:T(8,128)(2,1)S(1)}, u32[]{:S(2)}, u32[]{:S(2)}) %collective-permute-start.16) | collective-permute-done | bytes 98336 | tf_op jit(solution)/shard_map/ppermute | solution.py:401
  63.1 1.9 %unpack.1 = (bf16[256,512]{1,0:T(8,128)(2,1)}, bf16[256,512]{1,0:T(8,128)(2,1)}, bf16[256,512]{1,0:T(8,128)(2,1)}) custom-call(s32[2]{0:T(128)S(1)} %pad_add_fusion.place_ref, bf16[384,128]{1,0:T(8,128)(2,1)S(1)} %get-tuple-element.47.refs_0_, bf16[384,128]{1,0:T(8,128)(2,1)S(1)} %collective-permute-done.10.refs_1_, ...), custom_call_target="tpu_custom_call" | custom-call | bytes 2097152 | tf_op jit(solution)/shard_map/unpack/pallas_call | solution.py:368
Async XLA Ops:
  0.6 9.5 %collective-permute-start = (bf16[128,1024]{1,0:T(8,128)(2,1)}, bf16[128,1024]{1,0:T(8,128)(2,1)S(1)}, u32[]{:S(2)}, u32[]{:S(2)}) collective-permute-start(bf16[128,1024]{1,0:T(8,128)(2,1)} %refs_0_.1), channel_id=1, source_target_pairs={{0,1},{1,0},{2,3},{3,2},{4,5},{5,4},{6,7},{7,6},{8,9},{9,8},{10,11... | collective-permute-start | bytes 786440 | tf_op jit(solution)/shard_map/ppermute | solution.py:415
  5.9 4.2 %copy-start.1 = (bf16[512,1024]{1,0:T(8,128)(2,1)S(1)}, bf16[512,1024]{1,0:T(8,128)(2,1)}, u32[]{:S(2)}) copy-start(bf16[512,1024]{1,0:T(8,128)(2,1)} %weight_ref.1) | copy-start | bytes 3145732
  5.9 4.2 %copy-start.2 = (bf16[128,1024]{1,0:T(8,128)(2,1)S(1)}, bf16[128,1024]{1,0:T(8,128)(2,1)}, u32[]{:S(2)}) copy-start(bf16[128,1024]{1,0:T(8,128)(2,1)} %refs_0_.1) | copy-start | bytes 786436
  6.0 16.1 %all-to-all-start = ((bf16[8,384,128]{2,1,0:T(8,128)(2,1)}), bf16[8,384,128]{2,1,0:T(8,128)(2,1)S(1)}, u32[]{:S(2)}, u32[]{:S(2)}) async-start(bf16[8,384,128]{2,1,0:T(8,128)(2,1)} %pack_rows.1), calls=%async_computation | async-start | bytes 1572864 | tf_op jit(solution)/shard_map/all_to_all | solution.py:406
  11.7 11.1 %collective-permute-start.2 = (bf16[128,128]{1,0:T(8,128)(2,1)S(1)}, bf16[128,128]{1,0:T(8,128)(2,1)S(1)}, u32[]{:S(2)}, u32[]{:S(2)}) collective-permute-start(bf16[128,128]{1,0:T(8,128)(2,1)S(1)} %get-tuple-element.34), channel_id=1, source_target_pairs={{0,2},{2,0},{4,6},{6,4},{8,10},{10,8},{12,14},{14,12},{16,18},{18,... | collective-permute-start | bytes 98312 | tf_op jit(solution)/shard_map/ppermute | solution.py:401
  12.1 12.3 %collective-permute-start.3 = (bf16[128,128]{1,0:T(8,128)(2,1)S(1)}, bf16[128,128]{1,0:T(8,128)(2,1)S(1)}, u32[]{:S(2)}, u32[]{:S(2)}) collective-permute-start(bf16[128,128]{1,0:T(8,128)(2,1)S(1)} %get-tuple-element.35), channel_id=1, source_target_pairs={{0,4},{2,6},{4,0},{6,2},{8,12},{10,14},{12,8},{14,10},{16,20},{18,... | collective-permute-start | bytes 98312 | tf_op jit(solution)/shard_map/ppermute | solution.py:401
  13.8 10.6 %collective-permute-start.4 = (bf16[128,128]{1,0:T(8,128)(2,1)S(1)}, bf16[128,128]{1,0:T(8,128)(2,1)S(1)}, u32[]{:S(2)}, u32[]{:S(2)}) collective-permute-start(bf16[128,128]{1,0:T(8,128)(2,1)S(1)} %get-tuple-element.36), channel_id=1, source_target_pairs={{0,6},{2,4},{4,2},{6,0},{8,14},{10,12},{12,10},{14,8},{16,22},{18,... | collective-permute-start | bytes 98312 | tf_op jit(solution)/shard_map/ppermute | solution.py:401
  13.8 13.2 %collective-permute-start.5 = (bf16[128,128]{1,0:T(8,128)(2,1)S(1)}, bf16[128,128]{1,0:T(8,128)(2,1)S(1)}, u32[]{:S(2)}, u32[]{:S(2)}) collective-permute-start(bf16[128,128]{1,0:T(8,128)(2,1)S(1)} %get-tuple-element.37), channel_id=1, source_target_pairs={{0,8},{2,10},{4,12},{6,14},{8,0},{10,2},{12,4},{14,6},{16,24},{18,... | collective-permute-start | bytes 98312 | tf_op jit(solution)/shard_map/ppermute | solution.py:401
  15.5 6.6 %copy-start = (s32[16]{0:T(128)S(1)}, s32[16]{0:T(128)}, u32[]{:S(2)}) copy-start(s32[16]{0:T(128)} %offset_ref.7) | copy-start | bytes 196
  15.5 11.6 %collective-permute-start.6 = (bf16[128,128]{1,0:T(8,128)(2,1)S(1)}, bf16[128,128]{1,0:T(8,128)(2,1)S(1)}, u32[]{:S(2)}, u32[]{:S(2)}) collective-permute-start(bf16[128,128]{1,0:T(8,128)(2,1)S(1)} %get-tuple-element.38), channel_id=1, source_target_pairs={{0,10},{2,8},{4,14},{6,12},{8,2},{10,0},{12,6},{14,4},{16,26},{18,... | collective-permute-start | bytes 98312 | tf_op jit(solution)/shard_map/ppermute | solution.py:401
  22.8 4.9 %collective-permute-start.7 = (bf16[128,128]{1,0:T(8,128)(2,1)S(1)}, bf16[128,128]{1,0:T(8,128)(2,1)S(1)}, u32[]{:S(2)}, u32[]{:S(2)}) collective-permute-start(bf16[128,128]{1,0:T(8,128)(2,1)S(1)} %get-tuple-element.39), channel_id=1, source_target_pairs={{0,12},{2,14},{4,8},{6,10},{8,4},{10,6},{12,0},{14,2},{16,28},{18,... | collective-permute-start | bytes 98312 | tf_op jit(solution)/shard_map/ppermute | solution.py:401
  24.4 4.2 %collective-permute-start.8 = (bf16[128,128]{1,0:T(8,128)(2,1)S(1)}, bf16[128,128]{1,0:T(8,128)(2,1)S(1)}, u32[]{:S(2)}, u32[]{:S(2)}) collective-permute-start(bf16[128,128]{1,0:T(8,128)(2,1)S(1)} %get-tuple-element.40), channel_id=1, source_target_pairs={{0,14},{2,12},{4,10},{6,8},{8,6},{10,4},{12,2},{14,0},{16,30},{18,... | collective-permute-start | bytes 98312 | tf_op jit(solution)/shard_map/ppermute | solution.py:401
  24.4 4.9 %collective-permute-start.1 = (bf16[128,128]{1,0:T(8,128)(2,1)S(1)}, bf16[128,128]{1,0:T(8,128)(2,1)S(1)}, u32[]{:S(2)}, u32[]{:S(2)}) collective-permute-start(bf16[128,128]{1,0:T(8,128)(2,1)S(1)} %get-tuple-element.33.picks_ref), channel_id=1, source_target_pairs={{0,16},{2,18},{4,20},{6,22},{8,24},{10,26},{12,28},{14,30},{16,0},... | collective-permute-start | bytes 98312 | tf_op jit(solution)/shard_map/ppermute | solution.py:410
  31.1 10.4 %collective-permute-start.9 = (f32[128,128]{1,0:T(8,128)S(1)}, f32[128,128]{1,0:T(8,128)S(1)}, u32[]{:S(2)}, u32[]{:S(2)}) collective-permute-start(f32[128,128]{1,0:T(8,128)S(1)} %get-tuple-element.46), channel_id=1, source_target_pairs={{0,16},{2,18},{4,20},{6,22},{8,24},{10,26},{12,28},{14,30},{16,0},... | collective-permute-start | bytes 196616 | tf_op jit(solution)/shard_map/ppermute | solution.py:410
  49.5 4.2 %collective-permute-start.10 = (bf16[384,128]{1,0:T(8,128)(2,1)S(1)}, bf16[384,128]{1,0:T(8,128)(2,1)S(1)}, u32[]{:S(2)}, u32[]{:S(2)}) collective-permute-start(bf16[384,128]{1,0:T(8,128)(2,1)S(1)} %get-tuple-element.48), channel_id=1, source_target_pairs={{0,2},{2,0},{4,6},{6,4},{8,10},{10,8},{12,14},{14,12},{16,18},{18,... | collective-permute-start | bytes 294920 | tf_op jit(solution)/shard_map/ppermute | solution.py:401
  49.6 5.6 %collective-permute-start.11 = (bf16[384,128]{1,0:T(8,128)(2,1)S(1)}, bf16[384,128]{1,0:T(8,128)(2,1)S(1)}, u32[]{:S(2)}, u32[]{:S(2)}) collective-permute-start(bf16[384,128]{1,0:T(8,128)(2,1)S(1)} %get-tuple-element.49), channel_id=1, source_target_pairs={{0,4},{2,6},{4,0},{6,2},{8,12},{10,14},{12,8},{14,10},{16,20},{18,... | collective-permute-start | bytes 294920 | tf_op jit(solution)/shard_map/ppermute | solution.py:401
  51.1 5.4 %collective-permute-start.12 = (bf16[384,128]{1,0:T(8,128)(2,1)S(1)}, bf16[384,128]{1,0:T(8,128)(2,1)S(1)}, u32[]{:S(2)}, u32[]{:S(2)}) collective-permute-start(bf16[384,128]{1,0:T(8,128)(2,1)S(1)} %get-tuple-element.50), channel_id=1, source_target_pairs={{0,6},{2,4},{4,2},{6,0},{8,14},{10,12},{12,10},{14,8},{16,22},{18,... | collective-permute-start | bytes 294920 | tf_op jit(solution)/shard_map/ppermute | solution.py:401
  51.4 5.8 %collective-permute-start.13 = (bf16[384,128]{1,0:T(8,128)(2,1)S(1)}, bf16[384,128]{1,0:T(8,128)(2,1)S(1)}, u32[]{:S(2)}, u32[]{:S(2)}) collective-permute-start(bf16[384,128]{1,0:T(8,128)(2,1)S(1)} %get-tuple-element.51), channel_id=1, source_target_pairs={{0,8},{2,10},{4,12},{6,14},{8,0},{10,2},{12,4},{14,6},{16,24},{18,... | collective-permute-start | bytes 294920 | tf_op jit(solution)/shard_map/ppermute | solution.py:401
  53.7 5.2 %collective-permute-start.14 = (bf16[384,128]{1,0:T(8,128)(2,1)S(1)}, bf16[384,128]{1,0:T(8,128)(2,1)S(1)}, u32[]{:S(2)}, u32[]{:S(2)}) collective-permute-start(bf16[384,128]{1,0:T(8,128)(2,1)S(1)} %get-tuple-element.52), channel_id=1, source_target_pairs={{0,10},{2,8},{4,14},{6,12},{8,2},{10,0},{12,6},{14,4},{16,26},{18,... | collective-permute-start | bytes 294920 | tf_op jit(solution)/shard_map/ppermute | solution.py:401
  53.7 8.4 %collective-permute-start.15 = (bf16[384,128]{1,0:T(8,128)(2,1)S(1)}, bf16[384,128]{1,0:T(8,128)(2,1)S(1)}, u32[]{:S(2)}, u32[]{:S(2)}) collective-permute-start(bf16[384,128]{1,0:T(8,128)(2,1)S(1)} %get-tuple-element.53), channel_id=1, source_target_pairs={{0,12},{2,14},{4,8},{6,10},{8,4},{10,6},{12,0},{14,2},{16,28},{18,... | collective-permute-start | bytes 294920 | tf_op jit(solution)/shard_map/ppermute | solution.py:401
  55.2 7.9 %collective-permute-start.16 = (bf16[384,128]{1,0:T(8,128)(2,1)S(1)}, bf16[384,128]{1,0:T(8,128)(2,1)S(1)}, u32[]{:S(2)}, u32[]{:S(2)}) collective-permute-start(bf16[384,128]{1,0:T(8,128)(2,1)S(1)} %get-tuple-element.54), channel_id=1, source_target_pairs={{0,14},{2,12},{4,10},{6,8},{8,6},{10,4},{12,2},{14,0},{16,30},{18,... | collective-permute-start | bytes 294920 | tf_op jit(solution)/shard_map/ppermute | solution.py:401

commit v8 on v7

--- a/solution.py
+++ b/solution.py
@@ -88,14 +88,18 @@
         out_ref[...] = stage_ref[lax.bitwise_xor(place, bits)]
 
 
-def pack_kernel(head_count, query_hbm, key_hbm, value_hbm, *refs):
-    out_ref, query_ref, key_ref, value_ref, sems = refs
+def pack_kernel(head_count, query_hbm, key_hbm, value_hbm, offset_hbm, *refs):
+    out_ref, picks_ref, query_ref, key_ref, value_ref, offset_ref, sems = refs
     rows = query_ref.shape[0]
+    picked = picks_ref.shape[1]
+    shard = lax.axis_index("heads")
+    loads = [
+        (offset_hbm, offset_ref), (key_hbm, key_ref), (value_hbm, value_ref),
+        (query_hbm, query_ref),
+    ]
     copies = [
         pltpu.make_async_copy(source, target, sems.at[index])
-        for index, (source, target) in enumerate(
-            [(key_hbm, key_ref), (value_hbm, value_ref), (query_hbm, query_ref)]
-        )
+        for index, (source, target) in enumerate(loads)
     ]
     for copy in copies:
         copy.start()
@@ -107,10 +111,13 @@
         for place in range(head, out_ref.shape[0], head_count):
             out_ref[place, :rows, :] = pair
             out_ref[place, rows:, :] = query
+        pick = pick_matrix(offset_ref[shard * head_count + head], picked, rows)
+        picks_ref[head] = dot_nn(pick, pair).astype(jnp.bfloat16)
 
 
 def project_kernel(head_count, group, shards, place_ref, weight_ref, *refs):
     upstream_refs, refs = refs[:shards], refs[shards:]
+    far_refs, refs = refs[: -group - 2], refs[-group - 2 :]
     out_refs, (grad_ref, stage_ref) = refs[:group], refs[group:]
     shard_rows = upstream_refs[0].shape[0]
     for step, upstream_ref in enumerate(upstream_refs):
@@ -122,30 +129,15 @@
     for head in range(head_count):
         grad = side_by_side(head_columns(grad_ref, head))
         for place in range(head, group, head_count):
-            stage_ref[place] = grad
+            stage_ref[place, : grad.shape[0], :] = grad
+            for other, far_ref in enumerate(far_refs):
+                first = grad.shape[0] + other * far_ref.shape[1]
+                stage_ref[place, first : first + far_ref.shape[1], :] = far_ref[head]
     send_out(place_ref[0], stage_ref, out_refs)
 
 
 def own_offset(head_count, place_ref, offset_ref):
     return offset_ref[place_ref[1] * head_count + lax.rem(place_ref[0], head_count)]
-
-
-def gather_kernel(
-    head_count, place_ref, offset_ref, sent_ref, after_ref, keys_out, key_t_out, queries_out,
-    picks_out,
-):
-    group = sent_ref.shape[0]
-    rows = keys_out.shape[0] // group
-    picked = rows // DILATION_RATE
-    pick = pick_matrix(own_offset(head_count, place_ref, offset_ref), picked, rows)
-    for place in range(group):
-        pair = sent_ref[place, :rows, :]
-        keys_out[place * rows : (place + 1) * rows, :] = pair
-        picks_out[place * picked : (place + 1) * picked, :] = dot_nn(pick, pair).astype(
-            jnp.bfloat16
-        )
-        queries_out[place] = sent_ref[place, rows:, :]
-    key_t_out[...] = keys_out[...].astype(jnp.float32).T[:HEAD_SIZE].astype(jnp.bfloat16)
 
 
 def query_and_grad(query_ref, grad_ref):
@@ -167,28 +159,36 @@
     )
 
 
-def far_kernel(
-    head_count, group, others, place_ref, offset_ref, near_ref, queries_ref, picks_ref, *refs
-):
-    other_refs, refs = refs[:others], refs[others:]
+def far_kernel(head_count, others, place_ref, offset_ref, sent_ref, *refs):
+    group = sent_ref.shape[0]
     grad_refs, refs = refs[:group], refs[group:]
-    extra_out, own_out, other_out, grads_out, keys_ref, query_ref, grad_ref = refs
-    near = near_ref.shape[0]
+    keys_out, key_t_out, queries_out, grads_out, *refs = refs
+    extra_out, own_out, other_out, keys_ref, query_ref, grad_ref = refs
+    near = keys_out.shape[0]
     rows = near // group
+    half = rows // 2
     picked = rows // DILATION_RATE
     count = group * picked
     far = count * (1 + others)
     pick = pick_matrix(own_offset(head_count, place_ref, offset_ref), picked, rows)
-    keys_ref[:near, :] = near_ref[...]
-    for index, ref in enumerate([picks_ref, *other_refs]):
-        keys_ref[near + index * count : near + (index + 1) * count, :] = ref[...]
     for bits, ref in enumerate(grad_refs):
-        grads_out[lax.bitwise_xor(place_ref[0], bits)] = ref[...]
-    for step in range(group):
-        query, grad = query_and_grad(queries_ref.at[step], grads_out.at[step])
-        span = slice(step * picked, (step + 1) * picked)
+        place = lax.bitwise_xor(place_ref[0], bits)
+        grads_out[place] = ref[:half, :]
+        for other in range(others):
+            start = pl.multiple_of(near + (1 + other) * count + place * picked, picked)
+            source = half + other * picked
+            keys_ref[pl.ds(start, picked), :] = ref[source : source + picked, :]
+    for place in range(group):
+        pair = sent_ref[place, :rows, :]
+        span = slice(place * picked, (place + 1) * picked)
+        keys_ref[place * rows : (place + 1) * rows, :] = pair
+        keys_ref[near + span.start : near + span.stop, :] = dot_nn(pick, pair).astype(jnp.bfloat16)
+        queries_out[place] = sent_ref[place, rows:, :]
+        query, grad = query_and_grad(queries_out.at[place], grads_out.at[place])
         query_ref[span, :] = dot_nn(pick, query).astype(jnp.bfloat16)
         grad_ref[span, :] = dot_nn(pick, grad).astype(jnp.bfloat16)
+    keys_out[...] = keys_ref[:near, :]
+    key_t_out[...] = keys_out[...].astype(jnp.float32).T[:HEAD_SIZE].astype(jnp.bfloat16)
     far_t = keys_ref[near:, :].astype(jnp.float32).T[:HEAD_SIZE].astype(jnp.bfloat16)
     query, grad = query_ref[...], grad_ref[...]
     score = dot_nt(keys_ref[...], query)
@@ -401,10 +401,6 @@
             lax.ppermute(values[bits], "context", pairs[bits]) for bits in range(1, group)
         ]
 
-    def exchange(value):
-        groups = [list(range(first, first + group)) for first in range(0, devices, group)]
-        return lax.all_to_all(value, "context", 0, 0, axis_index_groups=groups)
-
     def segment_shift(value, shift):
         pairs = [(source, (source + shift * group) % devices) for source in range(devices)]
         return lax.ppermute(value, "context", pairs)
@@ -415,38 +411,35 @@
         upstreams.append(lax.ppermute(upstream, "heads", pairs))
 
     bf16, f32 = jnp.bfloat16, jnp.float32
-    (sent,) = call(
+    sent, far_send = call(
         functools.partial(pack_kernel, head_count), "pack_rows",
-        [((group, rows + half, PAIR), bf16)],
-        [], [query_rows, key_rows, value_rows],
-        [((rows, width), bf16)] * 3 + [pltpu.SemaphoreType.DMA((3,))],
+        [((group, rows + half, PAIR), bf16), ((head_count, picked, PAIR), bf16)],
+        [], [query_rows, key_rows, value_rows, head_offsets],
+        [((rows, width), bf16)] * 3
+        + [pltpu.SMEM(head_offsets.shape, jnp.int32), pltpu.SemaphoreType.DMA((4,))],
         flops=2**31, space=ANY, limit=60,
     )
-    sent = exchange(sent)
-    grads_send = call(
-        functools.partial(project_kernel, head_count, group, shards), "project_pack",
-        [((half, PAIR), bf16)] * group,
-        [place], [out_weight, *upstreams],
-        [((rows, width), bf16), ((group, half, PAIR), bf16)],
-        flops=BUSY,
-    )
-    grads = swap(grads_send)
-    keys, key_t, queries, picks = call(
-        functools.partial(gather_kernel, head_count), "gather_keys",
+    groups = [list(range(first, first + group)) for first in range(0, devices, group)]
+    sent = lax.all_to_all(sent, "context", 0, 0, axis_index_groups=groups)
+    far_in = [segment_shift(far_send, shift) for shift in range(1, others + 1)]
+    sent_rows = half + others * picked
+    grads = swap(
+        call(
+            functools.partial(project_kernel, head_count, group, shards), "project_pack",
+            [((sent_rows, PAIR), bf16)] * group,
+            [place], [out_weight, *upstreams, *far_in],
+            [((rows, width), bf16), ((group, sent_rows, PAIR), bf16)],
+            flops=BUSY,
+        )
+    )
+    keys, key_t, queries, grads, extra, own_terms, other_terms = call(
+        functools.partial(far_kernel, head_count, others), "picked_rows",
         [
             ((near, PAIR), bf16), ((HEAD_SIZE, near), bf16), ((group, half, PAIR), bf16),
-            ((count, PAIR), bf16),
+            ((group, half, PAIR), bf16), ((PAIR + STAT_ROWS, count), bf16),
+            ((count, PAIR), f32), ((others * count, PAIR), f32),
         ],
-        scalars, [sent, grads_send[0]],
-    )
-    other_picks = [segment_shift(picks, shift) for shift in range(1, others + 1)]
-    extra, own_terms, other_terms, grads = call(
-        functools.partial(far_kernel, head_count, group, others), "picked_rows",
-        [
-            ((PAIR + STAT_ROWS, count), bf16), ((count, PAIR), f32),
-            ((others * count, PAIR), f32), ((group, half, PAIR), bf16),
-        ],
-        scalars, [keys, queries, picks, *other_picks, *grads],
+        scalars, [sent, *grads],
         [((near + count * (1 + others), PAIR), bf16)] + [((count, PAIR), bf16)] * 2,
         flops=8 * near * count * PAIR,
     )

time: 65.2 us -> 68.3 us (1.048)
  waiting for transfers between devices: 16 us -> 19.3 us
    ppermute x2, waiting for transfers between devices: 0.65 us -> 7.55 us  [segment_shift(): return lax.ppermute(value, 'context', pairs)]
    all_to_all x1, waiting for transfers between devices: 6.43 us -> 0.01 us  [body(): sent = lax.all_to_all(sent, 'context', 0, 0, axis_index_groups=groups)]
    ppermute x14, waiting for transfers between devices: 8.74 us -> 11.8 us  [swap(): lax.ppermute(values[bits], 'context', pairs[bits])]
    ppermute x14, starting transfers between devices: 11.9 us -> 14.7 us  [swap(): lax.ppermute(values[bits], 'context', pairs[bits])]
    ppermute x2, starting transfers between devices: 5.35 us -> 2.73 us  [segment_shift(): return lax.ppermute(value, 'context', pairs)]
    pallas_call x7 -> x6, Pallas kernels: 24 us -> 23.5 us  [call(): pl.pallas_call(kernel, out_shape=tuple((jax.ShapeDtypeStruct(*shape) for...]
  transfers between devices with their start and end apart: 18 -> 18, of which waited for: 11 -> 10; matrix products, arithmetic and copies ran while one was open for 0% -> 0% of each run, Pallas kernels for 19% -> 17%
where the time goes in v8:
time: 68.3 us; the launch traced here: 68.1 us
  starting transfers between devices  24.4 us (36%)
  Pallas kernels  23.5 us (34%)
  waiting for transfers between devices  19.3 us (28%)
  between operations  0.73 us (1%)
    pallas_call x6, Pallas kernels, call(): pl.pallas_call(kernel, out_shape=tuple((jax.ShapeDtypeStruct(*shape) for...  23.5 us
    ppermute x14, starting transfers between devices, swap(): lax.ppermute(values[bits], 'context', pairs[bits])  14.7 us
    ppermute x14, waiting for transfers between devices, swap(): lax.ppermute(values[bits], 'context', pairs[bits])  11.8 us
    ppermute x2, waiting for transfers between devices, segment_shift(): return lax.ppermute(value, 'context', pairs)  7.55 us
    all_to_all x1, starting transfers between devices, body(): sent = lax.all_to_all(sent, 'context', 0, 0, axis_index_groups=groups)  3.95 us
    ppermute x1, starting transfers between devices, body(): upstreams.append(lax.ppermute(upstream, 'heads', pairs))  3 us
    ppermute x2, starting transfers between devices, segment_shift(): return lax.ppermute(value, 'context', pairs)  2.73 us
  transfers between devices with their start and end apart: 18, of which 10 were waited for; matrix products, arithmetic and copies ran while one was open for 0% of the time, Pallas kernels for 17%

profile of v8, /device:TPU:0, one launch (start us, length us, event | category | flops | bytes accessed | tf_op | source)
XLA Modules:
  0.0 68.1 jit_solution(18200191165620846013)
XLA Ops:
  0.6 3.0 %collective-permute-start = (bf16[128,1024]{1,0:T(8,128)(2,1)}, bf16[128,1024]{1,0:T(8,128)(2,1)S(1)}, u32[]{:S(2)}, u32[]{:S(2)}) collective-permute-start(bf16[128,1024]{1,0:T(8,128)(2,1)} %refs_0_.1), channel_id=1, source_target_pairs={{0,1},{1,0},{2,3},{3,2},{4,5},{5,4},{6,7},{7,6},{8,9},{9,8},{10,11... | collective-permute-start | bytes 786440 | tf_op jit(solution)/shard_map/ppermute | solution.py:411
  3.6 2.3 %pack_rows.1 = (bf16[8,384,128]{2,1,0:T(8,128)(2,1)}, bf16[8,16,128]{2,1,0:T(8,128)(2,1)}) custom-call(bf16[256,512]{1,0:T(8,128)(2,1)} %query_hbm.1, bf16[256,512]{1,0:T(8,128)(2,1)} %key_hbm.1, bf16[256,512]{1,0:T(8,128)(2,1)} %value_hbm.1, s32[16]{0:T(128)} %offset_ref.5), custom_call_target="tpu_custom_call" | custom-call | flops 2147483648 | bytes 2097152 | tf_op jit(solution)/shard_map/pack_rows/pallas_call | solution.py:368
  5.9 0.0 copy-start.1
  6.0 0.0 copy-start.3
  6.0 0.0 copy-start.2
  6.0 4.0 %all-to-all-start = ((bf16[8,384,128]{2,1,0:T(8,128)(2,1)}), bf16[8,384,128]{2,1,0:T(8,128)(2,1)S(1)}, u32[]{:S(2)}, u32[]{:S(2)}) async-start(bf16[8,384,128]{2,1,0:T(8,128)(2,1)} %get-tuple-element.30), calls=%async_computation | async-start | bytes 1572864 | tf_op jit(solution)/shard_map/all_to_all | solution.py:423
  9.9 0.0 copy-done.3
  9.9 2.7 %collective-permute-start.1 = (bf16[8,16,128]{2,1,0:T(8,128)(2,1)S(1)}, bf16[8,16,128]{2,1,0:T(8,128)(2,1)S(1)}, u32[]{:S(2)}, u32[]{:S(2)}) collective-permute-start(bf16[8,16,128]{2,1,0:T(8,128)(2,1)S(1)} %copy-done.3), channel_id=1, source_target_pairs={{0,16},{2,18},{4,20},{6,22},{8,24},{10,26},{12,28},{14,30},{16,0},... | collective-permute-start | bytes 98312 | tf_op jit(solution)/shard_map/ppermute | solution.py:406
  12.6 0.1 pad_add_fusion.place_ref
  12.7 7.5 %collective-permute-done.1.refs_2_ = bf16[8,16,128]{2,1,0:T(8,128)(2,1)S(1)} collective-permute-done((bf16[8,16,128]{2,1,0:T(8,128)(2,1)S(1)}, bf16[8,16,128]{2,1,0:T(8,128)(2,1)S(1)}, u32[]{:S(2)}, u32[]{:S(2)}) %collective-permute-start.1) | collective-permute-done | bytes 32800 | tf_op jit(solution)/shard_map/ppermute | solution.py:406
  20.2 0.0 collective-permute-done.refs_1_
  20.2 0.0 copy-done.1
  20.2 0.0 copy-done.2
  20.2 1.5 %project_pack.1 = (bf16[144,128]{1,0:T(8,128)(2,1)S(1)}, bf16[144,128]{1,0:T(8,128)(2,1)S(1)}, bf16[144,128]{1,0:T(8,128)(2,1)S(1)}, bf16[144,128]{1,0:T(8,128)(...) custom-call(s32[2]{0:T(128)S(1)} %pad_add_fusion.place_ref, ...), custom_call_target="tpu_custom_call" | custom-call | flops 34359738368 | bytes 2097152 | tf_op jit(solution)/shard_map/project_pack/pallas_call | solution.py:368
  21.8 0.1 collective-permute-start.2
  21.8 1.7 %collective-permute-start.3 = (bf16[144,128]{1,0:T(8,128)(2,1)S(1)}, bf16[144,128]{1,0:T(8,128)(2,1)S(1)}, u32[]{:S(2)}, u32[]{:S(2)}) collective-permute-start(bf16[144,128]{1,0:T(8,128)(2,1)S(1)} %get-tuple-element.34), channel_id=1, source_target_pairs={{0,4},{2,6},{4,0},{6,2},{8,12},{10,14},{12,8},{14,10},{16,20},{18,... | collective-permute-start | bytes 110600 | tf_op jit(solution)/shard_map/ppermute | solution.py:401
  23.5 0.2 collective-permute-start.4
  23.7 4.7 %collective-permute-start.5 = (bf16[144,128]{1,0:T(8,128)(2,1)S(1)}, bf16[144,128]{1,0:T(8,128)(2,1)S(1)}, u32[]{:S(2)}, u32[]{:S(2)}) collective-permute-start(bf16[144,128]{1,0:T(8,128)(2,1)S(1)} %get-tuple-element.36), channel_id=1, source_target_pairs={{0,8},{2,10},{4,12},{6,14},{8,0},{10,2},{12,4},{14,6},{16,24},{18,... | collective-permute-start | bytes 110600 | tf_op jit(solution)/shard_map/ppermute | solution.py:401
  28.4 0.0 collective-permute-start.6
  28.4 0.0 collective-permute-done.2.refs_1_
  28.4 2.6 %collective-permute-start.7 = (bf16[144,128]{1,0:T(8,128)(2,1)S(1)}, bf16[144,128]{1,0:T(8,128)(2,1)S(1)}, u32[]{:S(2)}, u32[]{:S(2)}) collective-permute-start(bf16[144,128]{1,0:T(8,128)(2,1)S(1)} %get-tuple-element.38), channel_id=1, source_target_pairs={{0,12},{2,14},{4,8},{6,10},{8,4},{10,6},{12,0},{14,2},{16,28},{18,... | collective-permute-start | bytes 110600 | tf_op jit(solution)/shard_map/ppermute | solution.py:401
  31.0 0.0 collective-permute-done.3.refs_2_
  31.0 0.0 copy-start
  31.0 0.1 collective-permute-start.8
  31.1 0.0 collective-permute-done.4.refs_3_
  31.1 0.0 collective-permute-done.5.refs_4_
  31.1 0.8 %collective-permute-done.6.refs_5_ = bf16[144,128]{1,0:T(8,128)(2,1)S(1)} collective-permute-done((bf16[144,128]{1,0:T(8,128)(2,1)S(1)}, bf16[144,128]{1,0:T(8,128)(2,1)S(1)}, u32[]{:S(2)}, u32[]{:S(2)}) %collective-permute-start.6) | collective-permute-done | bytes 36896 | tf_op jit(solution)/shard_map/ppermute | solution.py:401
  31.9 1.9 %collective-permute-done.7.refs_6_ = bf16[144,128]{1,0:T(8,128)(2,1)S(1)} collective-permute-done((bf16[144,128]{1,0:T(8,128)(2,1)S(1)}, bf16[144,128]{1,0:T(8,128)(2,1)S(1)}, u32[]{:S(2)}, u32[]{:S(2)}) %collective-permute-start.7) | collective-permute-done | bytes 36896 | tf_op jit(solution)/shard_map/ppermute | solution.py:401
  33.9 1.5 %collective-permute-done.8.refs_7_ = bf16[144,128]{1,0:T(8,128)(2,1)S(1)} collective-permute-done((bf16[144,128]{1,0:T(8,128)(2,1)S(1)}, bf16[144,128]{1,0:T(8,128)(2,1)S(1)}, u32[]{:S(2)}, u32[]{:S(2)}) %collective-permute-start.8) | collective-permute-done | bytes 36896 | tf_op jit(solution)/shard_map/ppermute | solution.py:401
  35.4 0.0 all-to-all-done.sent_ref
  35.4 0.0 copy-done
  35.4 2.1 %picked_rows.1 = (bf16[2048,128]{1,0:T(8,128)(2,1)S(1)}, bf16[64,2048]{1,0:T(8,128)(2,1)S(1)}, bf16[8,128,128]{2,1,0:T(8,128)(2,1)S(1)}, bf16[8,128,128]{2,1,0:T...) custom-call(s32[2]{0:T(128)S(1)} %pad_add_fusion.place_ref, ...), custom_call_target="tpu_custom_call" | custom-call | flops 268435456 | bytes 2097152 | tf_op jit(solution)/shard_map/picked_rows/pallas_call | solution.py:368
  37.5 0.1 collective-permute-start.9
  37.6 7.7 %first_rows.1 = (f32[2048,128]{1,0:T(8,128)S(1)}, bf16[4,128,128]{2,1,0:T(8,128)(2,1)S(1)}) custom-call(s32[2]{0:T(128)S(1)} %pad_add_fusion.place_ref, s32[16]{0:T(128)S(1)} %copy-done, bf16[2048,128]{1,0:T(8,128)(2,1)S(1)} %get-tuple-element.40.keys_ref, bf16[64,2048]{1,0:T(8,128)(2,1)S(1)} %get-tuple-element.41.key_t_ref, ...), custom_call_target="tpu_custom_call" | custom-call | flops 2684354560 | bytes 2097152 | tf_op jit(solution)/shard_map/first_rows/pallas_call | solution.py:368
  45.2 0.0 collective-permute-done.9.refs_0_
  45.2 8.0 %second_rows.1 = (bf16[384,128]{1,0:T(8,128)(2,1)S(1)}, bf16[384,128]{1,0:T(8,128)(2,1)S(1)}, bf16[384,128]{1,0:T(8,128)(2,1)S(1)}, bf16[384,128]{1,0:T(8,128)(2...) custom-call(s32[2]{0:T(128)S(1)} %pad_add_fusion.place_ref, ...), custom_call_target="tpu_custom_call" | custom-call | flops 2684354560 | bytes 2097152 | tf_op jit(solution)/shard_map/second_rows/pallas_call | solution.py:368
  53.2 0.2 collective-permute-start.10
  53.4 0.6 collective-permute-start.11
  54.0 1.2 %collective-permute-start.12 = (bf16[384,128]{1,0:T(8,128)(2,1)S(1)}, bf16[384,128]{1,0:T(8,128)(2,1)S(1)}, u32[]{:S(2)}, u32[]{:S(2)}) collective-permute-start(bf16[384,128]{1,0:T(8,128)(2,1)S(1)} %get-tuple-element.52), channel_id=1, source_target_pairs={{0,6},{2,4},{4,2},{6,0},{8,14},{10,12},{12,10},{14,8},{16,22},{18,... | collective-permute-start | bytes 294920 | tf_op jit(solution)/shard_map/ppermute | solution.py:401
  55.2 0.8 %collective-permute-start.13 = (bf16[384,128]{1,0:T(8,128)(2,1)S(1)}, bf16[384,128]{1,0:T(8,128)(2,1)S(1)}, u32[]{:S(2)}, u32[]{:S(2)}) collective-permute-start(bf16[384,128]{1,0:T(8,128)(2,1)S(1)} %get-tuple-element.53), channel_id=1, source_target_pairs={{0,8},{2,10},{4,12},{6,14},{8,0},{10,2},{12,4},{14,6},{16,24},{18,... | collective-permute-start | bytes 294920 | tf_op jit(solution)/shard_map/ppermute | solution.py:401
  56.0 0.9 %collective-permute-start.14 = (bf16[384,128]{1,0:T(8,128)(2,1)S(1)}, bf16[384,128]{1,0:T(8,128)(2,1)S(1)}, u32[]{:S(2)}, u32[]{:S(2)}) collective-permute-start(bf16[384,128]{1,0:T(8,128)(2,1)S(1)} %get-tuple-element.54), channel_id=1, source_target_pairs={{0,10},{2,8},{4,14},{6,12},{8,2},{10,0},{12,6},{14,4},{16,26},{18,... | collective-permute-start | bytes 294920 | tf_op jit(solution)/shard_map/ppermute | solution.py:401
  56.9 0.0 collective-permute-done.10.refs_1_
  56.9 1.1 %collective-permute-start.15 = (bf16[384,128]{1,0:T(8,128)(2,1)S(1)}, bf16[384,128]{1,0:T(8,128)(2,1)S(1)}, u32[]{:S(2)}, u32[]{:S(2)}) collective-permute-start(bf16[384,128]{1,0:T(8,128)(2,1)S(1)} %get-tuple-element.55), channel_id=1, source_target_pairs={{0,12},{2,14},{4,8},{6,10},{8,4},{10,6},{12,0},{14,2},{16,28},{18,... | collective-permute-start | bytes 294920 | tf_op jit(solution)/shard_map/ppermute | solution.py:401
  58.0 1.0 %collective-permute-done.11.refs_2_ = bf16[384,128]{1,0:T(8,128)(2,1)S(1)} collective-permute-done((bf16[384,128]{1,0:T(8,128)(2,1)S(1)}, bf16[384,128]{1,0:T(8,128)(2,1)S(1)}, u32[]{:S(2)}, u32[]{:S(2)}) %collective-permute-start.11) | collective-permute-done | bytes 98336 | tf_op jit(solution)/shard_map/ppermute | solution.py:401
  59.0 0.6 collective-permute-start.16
  59.6 0.6 collective-permute-done.12.refs_3_
  60.2 0.6 collective-permute-done.13.refs_4_
  60.8 1.0 %collective-permute-done.14.refs_5_ = bf16[384,128]{1,0:T(8,128)(2,1)S(1)} collective-permute-done((bf16[384,128]{1,0:T(8,128)(2,1)S(1)}, bf16[384,128]{1,0:T(8,128)(2,1)S(1)}, u32[]{:S(2)}, u32[]{:S(2)}) %collective-permute-start.14) | collective-permute-done | bytes 98336 | tf_op jit(solution)/shard_map/ppermute | solution.py:401
  61.8 3.2 %collective-permute-done.15.refs_6_ = bf16[384,128]{1,0:T(8,128)(2,1)S(1)} collective-permute-done((bf16[384,128]{1,0:T(8,128)(2,1)S(1)}, bf16[384,128]{1,0:T(8,128)(2,1)S(1)}, u32[]{:S(2)}, u32[]{:S(2)}) %collective-permute-start.15) | collective-permute-done | bytes 98336 | tf_op jit(solution)/shard_map/ppermute | solution.py:401
  65.0 1.2 %collective-permute-done.16.refs_7_ = bf16[384,128]{1,0:T(8,128)(2,1)S(1)} collective-permute-done((bf16[384,128]{1,0:T(8,128)(2,1)S(1)}, bf16[384,128]{1,0:T(8,128)(2,1)S(1)}, u32[]{:S(2)}, u32[]{:S(2)}) %collective-permute-start.16) | collective-permute-done | bytes 98336 | tf_op jit(solution)/shard_map/ppermute | solution.py:401
  66.1 1.9 %unpack.1 = (bf16[256,512]{1,0:T(8,128)(2,1)}, bf16[256,512]{1,0:T(8,128)(2,1)}, bf16[256,512]{1,0:T(8,128)(2,1)}) custom-call(s32[2]{0:T(128)S(1)} %pad_add_fusion.place_ref, bf16[384,128]{1,0:T(8,128)(2,1)S(1)} %get-tuple-element.49.refs_0_, bf16[384,128]{1,0:T(8,128)(2,1)S(1)} %collective-permute-done.10.refs_1_, ...), custom_call_target="tpu_custom_call" | custom-call | bytes 2097152 | tf_op jit(solution)/shard_map/unpack/pallas_call | solution.py:368
Async XLA Ops:
  0.6 19.6 %collective-permute-start = (bf16[128,1024]{1,0:T(8,128)(2,1)}, bf16[128,1024]{1,0:T(8,128)(2,1)S(1)}, u32[]{:S(2)}, u32[]{:S(2)}) collective-permute-start(bf16[128,1024]{1,0:T(8,128)(2,1)} %refs_0_.1), channel_id=1, source_target_pairs={{0,1},{1,0},{2,3},{3,2},{4,5},{5,4},{6,7},{7,6},{8,9},{9,8},{10,11... | collective-permute-start | bytes 786440 | tf_op jit(solution)/shard_map/ppermute | solution.py:411
  5.9 14.3 %copy-start.1 = (bf16[512,1024]{1,0:T(8,128)(2,1)S(1)}, bf16[512,1024]{1,0:T(8,128)(2,1)}, u32[]{:S(2)}) copy-start(bf16[512,1024]{1,0:T(8,128)(2,1)} %weight_ref.1) | copy-start | bytes 3145732
  6.0 4.0 %copy-start.3 = (bf16[8,16,128]{2,1,0:T(8,128)(2,1)S(1)}, bf16[8,16,128]{2,1,0:T(8,128)(2,1)}, u32[]{:S(2)}) copy-start(bf16[8,16,128]{2,1,0:T(8,128)(2,1)} %get-tuple-element.31) | copy-start | bytes 98308
  6.0 14.3 %copy-start.2 = (bf16[128,1024]{1,0:T(8,128)(2,1)S(1)}, bf16[128,1024]{1,0:T(8,128)(2,1)}, u32[]{:S(2)}) copy-start(bf16[128,1024]{1,0:T(8,128)(2,1)} %refs_0_.1) | copy-start | bytes 786436
  6.0 29.4 %all-to-all-start = ((bf16[8,384,128]{2,1,0:T(8,128)(2,1)}), bf16[8,384,128]{2,1,0:T(8,128)(2,1)S(1)}, u32[]{:S(2)}, u32[]{:S(2)}) async-start(bf16[8,384,128]{2,1,0:T(8,128)(2,1)} %get-tuple-element.30), calls=%async_computation | async-start | bytes 1572864 | tf_op jit(solution)/shard_map/all_to_all | solution.py:423
  9.9 10.3 %collective-permute-start.1 = (bf16[8,16,128]{2,1,0:T(8,128)(2,1)S(1)}, bf16[8,16,128]{2,1,0:T(8,128)(2,1)S(1)}, u32[]{:S(2)}, u32[]{:S(2)}) collective-permute-start(bf16[8,16,128]{2,1,0:T(8,128)(2,1)S(1)} %copy-done.3), channel_id=1, source_target_pairs={{0,16},{2,18},{4,20},{6,22},{8,24},{10,26},{12,28},{14,30},{16,0},... | collective-permute-start | bytes 98312 | tf_op jit(solution)/shard_map/ppermute | solution.py:406
  21.8 6.6 %collective-permute-start.2 = (bf16[144,128]{1,0:T(8,128)(2,1)S(1)}, bf16[144,128]{1,0:T(8,128)(2,1)S(1)}, u32[]{:S(2)}, u32[]{:S(2)}) collective-permute-start(bf16[144,128]{1,0:T(8,128)(2,1)S(1)} %get-tuple-element.33), channel_id=1, source_target_pairs={{0,2},{2,0},{4,6},{6,4},{8,10},{10,8},{12,14},{14,12},{16,18},{18,... | collective-permute-start | bytes 110600 | tf_op jit(solution)/shard_map/ppermute | solution.py:401
  21.8 9.1 %collective-permute-start.3 = (bf16[144,128]{1,0:T(8,128)(2,1)S(1)}, bf16[144,128]{1,0:T(8,128)(2,1)S(1)}, u32[]{:S(2)}, u32[]{:S(2)}) collective-permute-start(bf16[144,128]{1,0:T(8,128)(2,1)S(1)} %get-tuple-element.34), channel_id=1, source_target_pairs={{0,4},{2,6},{4,0},{6,2},{8,12},{10,14},{12,8},{14,10},{16,20},{18,... | collective-permute-start | bytes 110600 | tf_op jit(solution)/shard_map/ppermute | solution.py:401
  23.5 7.6 %collective-permute-start.4 = (bf16[144,128]{1,0:T(8,128)(2,1)S(1)}, bf16[144,128]{1,0:T(8,128)(2,1)S(1)}, u32[]{:S(2)}, u32[]{:S(2)}) collective-permute-start(bf16[144,128]{1,0:T(8,128)(2,1)S(1)} %get-tuple-element.35), channel_id=1, source_target_pairs={{0,6},{2,4},{4,2},{6,0},{8,14},{10,12},{12,10},{14,8},{16,22},{18,... | collective-permute-start | bytes 110600 | tf_op jit(solution)/shard_map/ppermute | solution.py:401
  23.7 7.4 %collective-permute-start.5 = (bf16[144,128]{1,0:T(8,128)(2,1)S(1)}, bf16[144,128]{1,0:T(8,128)(2,1)S(1)}, u32[]{:S(2)}, u32[]{:S(2)}) collective-permute-start(bf16[144,128]{1,0:T(8,128)(2,1)S(1)} %get-tuple-element.36), channel_id=1, source_target_pairs={{0,8},{2,10},{4,12},{6,14},{8,0},{10,2},{12,4},{14,6},{16,24},{18,... | collective-permute-start | bytes 110600 | tf_op jit(solution)/shard_map/ppermute | solution.py:401
  28.4 3.5 %collective-permute-start.6 = (bf16[144,128]{1,0:T(8,128)(2,1)S(1)}, bf16[144,128]{1,0:T(8,128)(2,1)S(1)}, u32[]{:S(2)}, u32[]{:S(2)}) collective-permute-start(bf16[144,128]{1,0:T(8,128)(2,1)S(1)} %get-tuple-element.37), channel_id=1, source_target_pairs={{0,10},{2,8},{4,14},{6,12},{8,2},{10,0},{12,6},{14,4},{16,26},{18,... | collective-permute-start | bytes 110600 | tf_op jit(solution)/shard_map/ppermute | solution.py:401
  28.4 5.5 %collective-permute-start.7 = (bf16[144,128]{1,0:T(8,128)(2,1)S(1)}, bf16[144,128]{1,0:T(8,128)(2,1)S(1)}, u32[]{:S(2)}, u32[]{:S(2)}) collective-permute-start(bf16[144,128]{1,0:T(8,128)(2,1)S(1)} %get-tuple-element.38), channel_id=1, source_target_pairs={{0,12},{2,14},{4,8},{6,10},{8,4},{10,6},{12,0},{14,2},{16,28},{18,... | collective-permute-start | bytes 110600 | tf_op jit(solution)/shard_map/ppermute | solution.py:401
  31.0 4.4 %copy-start = (s32[16]{0:T(128)S(1)}, s32[16]{0:T(128)}, u32[]{:S(2)}) copy-start(s32[16]{0:T(128)} %offset_ref.5) | copy-start | bytes 196
  31.0 4.4 %collective-permute-start.8 = (bf16[144,128]{1,0:T(8,128)(2,1)S(1)}, bf16[144,128]{1,0:T(8,128)(2,1)S(1)}, u32[]{:S(2)}, u32[]{:S(2)}) collective-permute-start(bf16[144,128]{1,0:T(8,128)(2,1)S(1)} %get-tuple-element.39), channel_id=1, source_target_pairs={{0,14},{2,12},{4,10},{6,8},{8,6},{10,4},{12,2},{14,0},{16,30},{18,... | collective-permute-start | bytes 110600 | tf_op jit(solution)/shard_map/ppermute | solution.py:401
  37.5 7.7 %collective-permute-start.9 = (f32[128,128]{1,0:T(8,128)S(1)}, f32[128,128]{1,0:T(8,128)S(1)}, u32[]{:S(2)}, u32[]{:S(2)}) collective-permute-start(f32[128,128]{1,0:T(8,128)S(1)} %get-tuple-element.48), channel_id=1, source_target_pairs={{0,16},{2,18},{4,20},{6,22},{8,24},{10,26},{12,28},{14,30},{16,0},... | collective-permute-start | bytes 196616 | tf_op jit(solution)/shard_map/ppermute | solution.py:406
  53.2 3.7 %collective-permute-start.10 = (bf16[384,128]{1,0:T(8,128)(2,1)S(1)}, bf16[384,128]{1,0:T(8,128)(2,1)S(1)}, u32[]{:S(2)}, u32[]{:S(2)}) collective-permute-start(bf16[384,128]{1,0:T(8,128)(2,1)S(1)} %get-tuple-element.50), channel_id=1, source_target_pairs={{0,2},{2,0},{4,6},{6,4},{8,10},{10,8},{12,14},{14,12},{16,18},{18,... | collective-permute-start | bytes 294920 | tf_op jit(solution)/shard_map/ppermute | solution.py:401
  53.4 5.6 %collective-permute-start.11 = (bf16[384,128]{1,0:T(8,128)(2,1)S(1)}, bf16[384,128]{1,0:T(8,128)(2,1)S(1)}, u32[]{:S(2)}, u32[]{:S(2)}) collective-permute-start(bf16[384,128]{1,0:T(8,128)(2,1)S(1)} %get-tuple-element.51), channel_id=1, source_target_pairs={{0,4},{2,6},{4,0},{6,2},{8,12},{10,14},{12,8},{14,10},{16,20},{18,... | collective-permute-start | bytes 294920 | tf_op jit(solution)/shard_map/ppermute | solution.py:401
  54.0 6.2 %collective-permute-start.12 = (bf16[384,128]{1,0:T(8,128)(2,1)S(1)}, bf16[384,128]{1,0:T(8,128)(2,1)S(1)}, u32[]{:S(2)}, u32[]{:S(2)}) collective-permute-start(bf16[384,128]{1,0:T(8,128)(2,1)S(1)} %get-tuple-element.52), channel_id=1, source_target_pairs={{0,6},{2,4},{4,2},{6,0},{8,14},{10,12},{12,10},{14,8},{16,22},{18,... | collective-permute-start | bytes 294920 | tf_op jit(solution)/shard_map/ppermute | solution.py:401
  55.2 5.6 %collective-permute-start.13 = (bf16[384,128]{1,0:T(8,128)(2,1)S(1)}, bf16[384,128]{1,0:T(8,128)(2,1)S(1)}, u32[]{:S(2)}, u32[]{:S(2)}) collective-permute-start(bf16[384,128]{1,0:T(8,128)(2,1)S(1)} %get-tuple-element.53), channel_id=1, source_target_pairs={{0,8},{2,10},{4,12},{6,14},{8,0},{10,2},{12,4},{14,6},{16,24},{18,... | collective-permute-start | bytes 294920 | tf_op jit(solution)/shard_map/ppermute | solution.py:401
  56.0 5.8 %collective-permute-start.14 = (bf16[384,128]{1,0:T(8,128)(2,1)S(1)}, bf16[384,128]{1,0:T(8,128)(2,1)S(1)}, u32[]{:S(2)}, u32[]{:S(2)}) collective-permute-start(bf16[384,128]{1,0:T(8,128)(2,1)S(1)} %get-tuple-element.54), channel_id=1, source_target_pairs={{0,10},{2,8},{4,14},{6,12},{8,2},{10,0},{12,6},{14,4},{16,26},{18,... | collective-permute-start | bytes 294920 | tf_op jit(solution)/shard_map/ppermute | solution.py:401
  56.9 8.0 %collective-permute-start.15 = (bf16[384,128]{1,0:T(8,128)(2,1)S(1)}, bf16[384,128]{1,0:T(8,128)(2,1)S(1)}, u32[]{:S(2)}, u32[]{:S(2)}) collective-permute-start(bf16[384,128]{1,0:T(8,128)(2,1)S(1)} %get-tuple-element.55), channel_id=1, source_target_pairs={{0,12},{2,14},{4,8},{6,10},{8,4},{10,6},{12,0},{14,2},{16,28},{18,... | collective-permute-start | bytes 294920 | tf_op jit(solution)/shard_map/ppermute | solution.py:401
  59.0 7.1 %collective-permute-start.16 = (bf16[384,128]{1,0:T(8,128)(2,1)S(1)}, bf16[384,128]{1,0:T(8,128)(2,1)S(1)}, u32[]{:S(2)}, u32[]{:S(2)}) collective-permute-start(bf16[384,128]{1,0:T(8,128)(2,1)S(1)} %get-tuple-element.56), channel_id=1, source_target_pairs={{0,14},{2,12},{4,10},{6,8},{8,6},{10,4},{12,2},{14,0},{16,30},{18,... | collective-permute-start | bytes 294920 | tf_op jit(solution)/shard_map/ppermute | solution.py:401

commit v9 on v7

--- a/solution.py
+++ b/solution.py
@@ -16,7 +16,7 @@
 LOG2E = math.log2(math.e)
 SCORE_FACTOR = SCALE * LOG2E
 STRIP = 64
-PIECE = 256
+PIECE = 1024
 BUSY = 2**35
 STAT_ROWS = 16
 
@@ -230,12 +230,22 @@
     def weights_of(index):
         return query_and_grad(queries_ref.at[places[index]], grads_ref.at[places[index]])
 
+    def columns_of(ref):
+        packed = ref[...].astype(jnp.float32).T
+        return jnp.concatenate([packed[:HEAD_SIZE], packed[HEAD_SIZE:]], 1).astype(jnp.bfloat16)
+
+    def transposed_of(index):
+        zero = jnp.zeros((HEAD_SIZE, rows), jnp.bfloat16)
+        query = columns_of(queries_ref.at[places[index]])
+        grad = columns_of(grads_ref.at[places[index]])
+        return jnp.concatenate([query, zero], 0), jnp.concatenate([zero, grad], 0)
+
     def first_pass(index, weights, start, state):
         top, total, delta = state
         slot = index % 2
         query, grad = weights
         keys = keys_ref[start : start + PIECE, :]
-        scores, dprobs = dot_nt(keys, query), dot_nt(keys, grad)
+        scores, dprobs = dot_nn(keys, query), dot_nn(keys, grad)
         for inner in range(0, PIECE, STRIP):
             strip = slice(start + inner, start + inner + STRIP)
             score, dprob = scores[inner : inner + STRIP], dprobs[inner : inner + STRIP]
@@ -269,7 +279,7 @@
         return query_grad + dot_nn(key_t_ref[:, piece], work_ref[slot, piece, :rows])
 
     starts = range(0, near, PIECE)
-    weights = weights_of(0)
+    weights = transposed_of(0)
     state = (None, None, None)
     for start in starts:
         state = first_pass(0, weights, start, state)
@@ -285,9 +295,9 @@
         delta = jnp.sum(delta * shrink, 0, keepdims=True) / total
         lse = jnp.where(picked, stats[0] + stats[1] + stats[2], highest + jnp.log2(total))
         delta = jnp.where(picked, stats[3] + stats[4] + stats[5], delta)
-        both = jnp.concatenate(weights, 0)
+        both = jnp.concatenate(weights_of(index), 0)
         query_grad = extra[:HEAD_SIZE] + extra[HEAD_SIZE:PAIR]
-        weights = None if last else weights_of(index + 1)
+        weights = None if last else transposed_of(index + 1)
         state = (None, None, None)
         for start in starts:
             if not last:

time: 65.2 us -> 66.2 us (1.015)
  Pallas kernels: 24 us -> 25 us
    pallas_call x7, Pallas kernels: 24 us -> 25 us  [call(): pl.pallas_call(kernel, out_shape=tuple((jax.ShapeDtypeStruct(*shape) for...]
  transfers between devices with their start and end apart: 18 -> 18, of which waited for: 11 -> 11; matrix products, arithmetic and copies ran while one was open for 0% -> 0% of each run, Pallas kernels for 19% -> 20%
where the time goes in v9:
time: 66.2 us; the launch traced here: 66 us
  Pallas kernels  25 us (38%)
  starting transfers between devices  24.2 us (37%)
  waiting for transfers between devices  16 us (24%)
  between operations  0.72 us (1%)
    pallas_call x7, Pallas kernels, call(): pl.pallas_call(kernel, out_shape=tuple((jax.ShapeDtypeStruct(*shape) for...  25 us
    ppermute x14, starting transfers between devices, swap(): lax.ppermute(values[bits], 'context', pairs[bits])  11.9 us
    ppermute x14, waiting for transfers between devices, swap(): lax.ppermute(values[bits], 'context', pairs[bits])  8.74 us
    all_to_all x1, waiting for transfers between devices, exchange(): return lax.all_to_all(value, 'context', 0, 0, axis_index_groups=groups)  6.43 us
    ppermute x2, starting transfers between devices, segment_shift(): return lax.ppermute(value, 'context', pairs)  5.35 us
    all_to_all x1, starting transfers between devices, exchange(): return lax.all_to_all(value, 'context', 0, 0, axis_index_groups=groups)  3.95 us
    ppermute x1, starting transfers between devices, body(): upstreams.append(lax.ppermute(upstream, 'heads', pairs))  3 us
  transfers between devices with their start and end apart: 18, of which 11 were waited for; matrix products, arithmetic and copies ran while one was open for 0% of the time, Pallas kernels for 20%

profile of v9, /device:TPU:0, one launch (start us, length us, event | category | flops | bytes accessed | tf_op | source)
XLA Modules:
  0.0 66.0 jit_solution(2529830200633284979)
XLA Ops:
  0.6 3.0 %collective-permute-start = (bf16[128,1024]{1,0:T(8,128)(2,1)}, bf16[128,1024]{1,0:T(8,128)(2,1)S(1)}, u32[]{:S(2)}, u32[]{:S(2)}) collective-permute-start(bf16[128,1024]{1,0:T(8,128)(2,1)} %refs_0_.1), channel_id=1, source_target_pairs={{0,1},{1,0},{2,3},{3,2},{4,5},{5,4},{6,7},{7,6},{8,9},{9,8},{10,11... | collective-permute-start | bytes 786440 | tf_op jit(solution)/shard_map/ppermute | solution.py:425
  3.6 2.3 %pack_rows.1 = bf16[8,384,128]{2,1,0:T(8,128)(2,1)} custom-call(bf16[256,512]{1,0:T(8,128)(2,1)} %query_hbm.1, bf16[256,512]{1,0:T(8,128)(2,1)} %key_hbm.1, bf16[256,512]{1,0:T(8,128)(2,1)} %value_hbm.1), custom_call_target="tpu_custom_call" | custom-call | flops 2147483648 | bytes 2097152 | tf_op jit(solution)/shard_map/pack_rows/pallas_call | solution.py:378
  5.9 0.0 copy-start.1
  5.9 0.0 copy-start.2
  6.0 4.0 %all-to-all-start = ((bf16[8,384,128]{2,1,0:T(8,128)(2,1)}), bf16[8,384,128]{2,1,0:T(8,128)(2,1)S(1)}, u32[]{:S(2)}, u32[]{:S(2)}) async-start(bf16[8,384,128]{2,1,0:T(8,128)(2,1)} %pack_rows.1), calls=%async_computation | async-start | bytes 1572864 | tf_op jit(solution)/shard_map/all_to_all | solution.py:416
  9.9 0.1 pad_add_fusion.place_ref
  10.0 0.2 collective-permute-done.refs_1_
  10.2 0.0 copy-done.1
  10.2 0.0 copy-done.2
  10.2 1.5 %project_pack.1 = (bf16[128,128]{1,0:T(8,128)(2,1)S(1)}, bf16[128,128]{1,0:T(8,128)(2,1)S(1)}, bf16[128,128]{1,0:T(8,128)(2,1)S(1)}, bf16[128,128]{1,0:T(8,128)(...) custom-call(s32[2]{0:T(128)S(1)} %pad_add_fusion.place_ref, ...), custom_call_target="tpu_custom_call" | custom-call | flops 34359738368 | bytes 2097152 | tf_op jit(solution)/shard_map/project_pack/pallas_call | solution.py:378
  11.7 0.4 collective-permute-start.2
  12.1 1.7 %collective-permute-start.3 = (bf16[128,128]{1,0:T(8,128)(2,1)S(1)}, bf16[128,128]{1,0:T(8,128)(2,1)S(1)}, u32[]{:S(2)}, u32[]{:S(2)}) collective-permute-start(bf16[128,128]{1,0:T(8,128)(2,1)S(1)} %get-tuple-element.35), channel_id=1, source_target_pairs={{0,4},{2,6},{4,0},{6,2},{8,12},{10,14},{12,8},{14,10},{16,20},{18,... | collective-permute-start | bytes 98312 | tf_op jit(solution)/shard_map/ppermute | solution.py:411
  13.8 0.0 collective-permute-start.4
  13.8 1.7 %collective-permute-start.5 = (bf16[128,128]{1,0:T(8,128)(2,1)S(1)}, bf16[128,128]{1,0:T(8,128)(2,1)S(1)}, u32[]{:S(2)}, u32[]{:S(2)}) collective-permute-start(bf16[128,128]{1,0:T(8,128)(2,1)S(1)} %get-tuple-element.37), channel_id=1, source_target_pairs={{0,8},{2,10},{4,12},{6,14},{8,0},{10,2},{12,4},{14,6},{16,24},{18,... | collective-permute-start | bytes 98312 | tf_op jit(solution)/shard_map/ppermute | solution.py:411
  15.5 0.0 copy-start
  15.5 0.1 collective-permute-start.6
  15.6 6.4 %all-to-all-done.sent_ref = bf16[8,384,128]{2,1,0:T(8,128)(2,1)S(1)} async-done(((bf16[8,384,128]{2,1,0:T(8,128)(2,1)}), bf16[8,384,128]{2,1,0:T(8,128)(2,1)S(1)}, u32[]{:S(2)}, u32[]{:S(2)}) %all-to-all-start) | async-done | bytes 786464 | tf_op jit(solution)/shard_map/all_to_all | solution.py:416
  22.0 0.0 copy-done
  22.0 0.8 %gather_keys.1 = (bf16[2048,128]{1,0:T(8,128)(2,1)S(1)}, bf16[64,2048]{1,0:T(8,128)(2,1)S(1)}, bf16[8,128,128]{2,1,0:T(8,128)(2,1)S(1)}, bf16[128,128]{1,0:T(8,128)(2,1)S(1)}) custom-call(s32[2]{0:T(128)S(1)} %pad_add_fusion.place_ref, s32[16]{0:T(128)S(1)} %copy-done, bf16[8,384,128]{2,1,0:T(8,128)(2,1)S(1)} %all-to-all-done.sent_ref, ...), custom_call_target="tpu_custom_call" | custom-call | bytes 2097152 | tf_op jit(solution)/shard_map/gather_keys/pallas_call | solution.py:378
  22.8 0.0 collective-permute-done.2.refs_2_
  22.8 1.5 %collective-permute-start.7 = (bf16[128,128]{1,0:T(8,128)(2,1)S(1)}, bf16[128,128]{1,0:T(8,128)(2,1)S(1)}, u32[]{:S(2)}, u32[]{:S(2)}) collective-permute-start(bf16[128,128]{1,0:T(8,128)(2,1)S(1)} %get-tuple-element.39), channel_id=1, source_target_pairs={{0,12},{2,14},{4,8},{6,10},{8,4},{10,6},{12,0},{14,2},{16,28},{18,... | collective-permute-start | bytes 98312 | tf_op jit(solution)/shard_map/ppermute | solution.py:411
  24.4 0.0 collective-permute-done.3.refs_3_
  24.4 0.0 collective-permute-start.8
  24.4 0.0 collective-permute-done.4.refs_4_
  24.4 2.7 %collective-permute-start.1 = (bf16[128,128]{1,0:T(8,128)(2,1)S(1)}, bf16[128,128]{1,0:T(8,128)(2,1)S(1)}, u32[]{:S(2)}, u32[]{:S(2)}) collective-permute-start(bf16[128,128]{1,0:T(8,128)(2,1)S(1)} %get-tuple-element.33.picks_ref), channel_id=1, source_target_pairs={{0,16},{2,18},{4,20},{6,22},{8,24},{10,26},{12,28},{14,30},{16,0},... | collective-permute-start | bytes 98312 | tf_op jit(solution)/shard_map/ppermute | solution.py:420
  27.0 0.0 collective-permute-done.5.refs_5_
  27.0 0.0 collective-permute-done.6.refs_6_
  27.0 0.7 %collective-permute-done.7.refs_7_ = bf16[128,128]{1,0:T(8,128)(2,1)S(1)} collective-permute-done((bf16[128,128]{1,0:T(8,128)(2,1)S(1)}, bf16[128,128]{1,0:T(8,128)(2,1)S(1)}, u32[]{:S(2)}, u32[]{:S(2)}) %collective-permute-start.7) | collective-permute-done | bytes 32800 | tf_op jit(solution)/shard_map/ppermute | solution.py:411
  27.7 0.9 %collective-permute-done.8.refs_8_ = bf16[128,128]{1,0:T(8,128)(2,1)S(1)} collective-permute-done((bf16[128,128]{1,0:T(8,128)(2,1)S(1)}, bf16[128,128]{1,0:T(8,128)(2,1)S(1)}, u32[]{:S(2)}, u32[]{:S(2)}) %collective-permute-start.8) | collective-permute-done | bytes 32800 | tf_op jit(solution)/shard_map/ppermute | solution.py:411
  28.6 0.6 collective-permute-done.1.refs_0_
  29.3 1.9 %picked_rows.1 = (bf16[144,128]{1,0:T(8,128)(2,1)S(1)}, f32[128,128]{1,0:T(8,128)S(1)}, f32[128,128]{1,0:T(8,128)S(1)}, bf16[8,128,128]{2,1,0:T(8,128)(2,1)S(1)}) custom-call(s32[2]{0:T(128)S(1)} %pad_add_fusion.place_ref, s32[16]{0:T(128)S(1)} %copy-done, bf16[2048,128]{1,0:T(8,128)(2,1)S(1)} %get-tuple-element.30.near_ref.keys_ref, ...), custom_call_target="tpu_custom_call" | custom-call | flops 268435456 | bytes 2097152 | tf_op jit(solution)/shard_map/picked_rows/pallas_call | solution.py:378
  31.1 2.7 %collective-permute-start.9 = (f32[128,128]{1,0:T(8,128)S(1)}, f32[128,128]{1,0:T(8,128)S(1)}, u32[]{:S(2)}, u32[]{:S(2)}) collective-permute-start(f32[128,128]{1,0:T(8,128)S(1)} %get-tuple-element.46), channel_id=1, source_target_pairs={{0,16},{2,18},{4,20},{6,22},{8,24},{10,26},{12,28},{14,30},{16,0},... | collective-permute-start | bytes 196616 | tf_op jit(solution)/shard_map/ppermute | solution.py:420
  33.8 8.3 %first_rows.1 = (f32[2048,128]{1,0:T(8,128)S(1)}, bf16[4,128,128]{2,1,0:T(8,128)(2,1)S(1)}) custom-call(s32[2]{0:T(128)S(1)} %pad_add_fusion.place_ref, s32[16]{0:T(128)S(1)} %copy-done, bf16[2048,128]{1,0:T(8,128)(2,1)S(1)} %get-tuple-element.30.near_ref.keys_ref, bf16[64,2048]{1,0:T(8,128)(2,1)S(1)} %get-tuple-element.31.key_t_ref, ...), custom_call_target="tpu_custom_call" | custom-call | flops 2684354560 | bytes 2097152 | tf_op jit(solution)/shard_map/first_rows/pallas_call | solution.py:378
  42.2 0.0 collective-permute-done.9.refs_0_
  42.2 8.3 %second_rows.1 = (bf16[384,128]{1,0:T(8,128)(2,1)S(1)}, bf16[384,128]{1,0:T(8,128)(2,1)S(1)}, bf16[384,128]{1,0:T(8,128)(2,1)S(1)}, bf16[384,128]{1,0:T(8,128)(2...) custom-call(s32[2]{0:T(128)S(1)} %pad_add_fusion.place_ref, ...), custom_call_target="tpu_custom_call" | custom-call | flops 2684354560 | bytes 2097152 | tf_op jit(solution)/shard_map/second_rows/pallas_call | solution.py:378
  50.5 0.1 collective-permute-start.10
  50.6 1.5 %collective-permute-start.11 = (bf16[384,128]{1,0:T(8,128)(2,1)S(1)}, bf16[384,128]{1,0:T(8,128)(2,1)S(1)}, u32[]{:S(2)}, u32[]{:S(2)}) collective-permute-start(bf16[384,128]{1,0:T(8,128)(2,1)S(1)} %get-tuple-element.49), channel_id=1, source_target_pairs={{0,4},{2,6},{4,0},{6,2},{8,12},{10,14},{12,8},{14,10},{16,20},{18,... | collective-permute-start | bytes 294920 | tf_op jit(solution)/shard_map/ppermute | solution.py:411
  52.0 0.4 collective-permute-start.12
  52.4 2.3 %collective-permute-start.13 = (bf16[384,128]{1,0:T(8,128)(2,1)S(1)}, bf16[384,128]{1,0:T(8,128)(2,1)S(1)}, u32[]{:S(2)}, u32[]{:S(2)}) collective-permute-start(bf16[384,128]{1,0:T(8,128)(2,1)S(1)} %get-tuple-element.51), channel_id=1, source_target_pairs={{0,8},{2,10},{4,12},{6,14},{8,0},{10,2},{12,4},{14,6},{16,24},{18,... | collective-permute-start | bytes 294920 | tf_op jit(solution)/shard_map/ppermute | solution.py:411
  54.7 0.0 collective-permute-start.14
  54.7 0.0 collective-permute-done.10.refs_1_
  54.7 1.2 %collective-permute-start.15 = (bf16[384,128]{1,0:T(8,128)(2,1)S(1)}, bf16[384,128]{1,0:T(8,128)(2,1)S(1)}, u32[]{:S(2)}, u32[]{:S(2)}) collective-permute-start(bf16[384,128]{1,0:T(8,128)(2,1)S(1)} %get-tuple-element.53), channel_id=1, source_target_pairs={{0,12},{2,14},{4,8},{6,10},{8,4},{10,6},{12,0},{14,2},{16,28},{18,... | collective-permute-start | bytes 294920 | tf_op jit(solution)/shard_map/ppermute | solution.py:411
  55.9 0.3 collective-permute-done.11.refs_2_
  56.2 1.0 %collective-permute-start.16 = (bf16[384,128]{1,0:T(8,128)(2,1)S(1)}, bf16[384,128]{1,0:T(8,128)(2,1)S(1)}, u32[]{:S(2)}, u32[]{:S(2)}) collective-permute-start(bf16[384,128]{1,0:T(8,128)(2,1)S(1)} %get-tuple-element.54), channel_id=1, source_target_pairs={{0,14},{2,12},{4,10},{6,8},{8,6},{10,4},{12,2},{14,0},{16,30},{18,... | collective-permute-start | bytes 294920 | tf_op jit(solution)/shard_map/ppermute | solution.py:411
  57.2 0.2 collective-permute-done.12.refs_3_
  57.4 0.8 %collective-permute-done.13.refs_4_ = bf16[384,128]{1,0:T(8,128)(2,1)S(1)} collective-permute-done((bf16[384,128]{1,0:T(8,128)(2,1)S(1)}, bf16[384,128]{1,0:T(8,128)(2,1)S(1)}, u32[]{:S(2)}, u32[]{:S(2)}) %collective-permute-start.13) | collective-permute-done | bytes 98336 | tf_op jit(solution)/shard_map/ppermute | solution.py:411
  58.2 1.7 %collective-permute-done.14.refs_5_ = bf16[384,128]{1,0:T(8,128)(2,1)S(1)} collective-permute-done((bf16[384,128]{1,0:T(8,128)(2,1)S(1)}, bf16[384,128]{1,0:T(8,128)(2,1)S(1)}, u32[]{:S(2)}, u32[]{:S(2)}) %collective-permute-start.14) | collective-permute-done | bytes 98336 | tf_op jit(solution)/shard_map/ppermute | solution.py:411
  59.9 3.2 %collective-permute-done.15.refs_6_ = bf16[384,128]{1,0:T(8,128)(2,1)S(1)} collective-permute-done((bf16[384,128]{1,0:T(8,128)(2,1)S(1)}, bf16[384,128]{1,0:T(8,128)(2,1)S(1)}, u32[]{:S(2)}, u32[]{:S(2)}) %collective-permute-start.15) | collective-permute-done | bytes 98336 | tf_op jit(solution)/shard_map/ppermute | solution.py:411
  63.1 1.0 %collective-permute-done.16.refs_7_ = bf16[384,128]{1,0:T(8,128)(2,1)S(1)} collective-permute-done((bf16[384,128]{1,0:T(8,128)(2,1)S(1)}, bf16[384,128]{1,0:T(8,128)(2,1)S(1)}, u32[]{:S(2)}, u32[]{:S(2)}) %collective-permute-start.16) | collective-permute-done | bytes 98336 | tf_op jit(solution)/shard_map/ppermute | solution.py:411
  64.1 1.9 %unpack.1 = (bf16[256,512]{1,0:T(8,128)(2,1)}, bf16[256,512]{1,0:T(8,128)(2,1)}, bf16[256,512]{1,0:T(8,128)(2,1)}) custom-call(s32[2]{0:T(128)S(1)} %pad_add_fusion.place_ref, bf16[384,128]{1,0:T(8,128)(2,1)S(1)} %get-tuple-element.47.refs_0_, bf16[384,128]{1,0:T(8,128)(2,1)S(1)} %collective-permute-done.10.refs_1_, ...), custom_call_target="tpu_custom_call" | custom-call | bytes 2097152 | tf_op jit(solution)/shard_map/unpack/pallas_call | solution.py:378
Async XLA Ops:
  0.6 9.5 %collective-permute-start = (bf16[128,1024]{1,0:T(8,128)(2,1)}, bf16[128,1024]{1,0:T(8,128)(2,1)S(1)}, u32[]{:S(2)}, u32[]{:S(2)}) collective-permute-start(bf16[128,1024]{1,0:T(8,128)(2,1)} %refs_0_.1), channel_id=1, source_target_pairs={{0,1},{1,0},{2,3},{3,2},{4,5},{5,4},{6,7},{7,6},{8,9},{9,8},{10,11... | collective-permute-start | bytes 786440 | tf_op jit(solution)/shard_map/ppermute | solution.py:425
  5.9 4.2 %copy-start.1 = (bf16[512,1024]{1,0:T(8,128)(2,1)S(1)}, bf16[512,1024]{1,0:T(8,128)(2,1)}, u32[]{:S(2)}) copy-start(bf16[512,1024]{1,0:T(8,128)(2,1)} %weight_ref.1) | copy-start | bytes 3145732
  5.9 4.2 %copy-start.2 = (bf16[128,1024]{1,0:T(8,128)(2,1)S(1)}, bf16[128,1024]{1,0:T(8,128)(2,1)}, u32[]{:S(2)}) copy-start(bf16[128,1024]{1,0:T(8,128)(2,1)} %refs_0_.1) | copy-start | bytes 786436
  6.0 16.1 %all-to-all-start = ((bf16[8,384,128]{2,1,0:T(8,128)(2,1)}), bf16[8,384,128]{2,1,0:T(8,128)(2,1)S(1)}, u32[]{:S(2)}, u32[]{:S(2)}) async-start(bf16[8,384,128]{2,1,0:T(8,128)(2,1)} %pack_rows.1), calls=%async_computation | async-start | bytes 1572864 | tf_op jit(solution)/shard_map/all_to_all | solution.py:416
  11.7 11.1 %collective-permute-start.2 = (bf16[128,128]{1,0:T(8,128)(2,1)S(1)}, bf16[128,128]{1,0:T(8,128)(2,1)S(1)}, u32[]{:S(2)}, u32[]{:S(2)}) collective-permute-start(bf16[128,128]{1,0:T(8,128)(2,1)S(1)} %get-tuple-element.34), channel_id=1, source_target_pairs={{0,2},{2,0},{4,6},{6,4},{8,10},{10,8},{12,14},{14,12},{16,18},{18,... | collective-permute-start | bytes 98312 | tf_op jit(solution)/shard_map/ppermute | solution.py:411
  12.1 12.3 %collective-permute-start.3 = (bf16[128,128]{1,0:T(8,128)(2,1)S(1)}, bf16[128,128]{1,0:T(8,128)(2,1)S(1)}, u32[]{:S(2)}, u32[]{:S(2)}) collective-permute-start(bf16[128,128]{1,0:T(8,128)(2,1)S(1)} %get-tuple-element.35), channel_id=1, source_target_pairs={{0,4},{2,6},{4,0},{6,2},{8,12},{10,14},{12,8},{14,10},{16,20},{18,... | collective-permute-start | bytes 98312 | tf_op jit(solution)/shard_map/ppermute | solution.py:411
  13.8 10.6 %collective-permute-start.4 = (bf16[128,128]{1,0:T(8,128)(2,1)S(1)}, bf16[128,128]{1,0:T(8,128)(2,1)S(1)}, u32[]{:S(2)}, u32[]{:S(2)}) collective-permute-start(bf16[128,128]{1,0:T(8,128)(2,1)S(1)} %get-tuple-element.36), channel_id=1, source_target_pairs={{0,6},{2,4},{4,2},{6,0},{8,14},{10,12},{12,10},{14,8},{16,22},{18,... | collective-permute-start | bytes 98312 | tf_op jit(solution)/shard_map/ppermute | solution.py:411
  13.8 13.2 %collective-permute-start.5 = (bf16[128,128]{1,0:T(8,128)(2,1)S(1)}, bf16[128,128]{1,0:T(8,128)(2,1)S(1)}, u32[]{:S(2)}, u32[]{:S(2)}) collective-permute-start(bf16[128,128]{1,0:T(8,128)(2,1)S(1)} %get-tuple-element.37), channel_id=1, source_target_pairs={{0,8},{2,10},{4,12},{6,14},{8,0},{10,2},{12,4},{14,6},{16,24},{18,... | collective-permute-start | bytes 98312 | tf_op jit(solution)/shard_map/ppermute | solution.py:411
  15.5 6.6 %copy-start = (s32[16]{0:T(128)S(1)}, s32[16]{0:T(128)}, u32[]{:S(2)}) copy-start(s32[16]{0:T(128)} %offset_ref.7) | copy-start | bytes 196
  15.5 11.6 %collective-permute-start.6 = (bf16[128,128]{1,0:T(8,128)(2,1)S(1)}, bf16[128,128]{1,0:T(8,128)(2,1)S(1)}, u32[]{:S(2)}, u32[]{:S(2)}) collective-permute-start(bf16[128,128]{1,0:T(8,128)(2,1)S(1)} %get-tuple-element.38), channel_id=1, source_target_pairs={{0,10},{2,8},{4,14},{6,12},{8,2},{10,0},{12,6},{14,4},{16,26},{18,... | collective-permute-start | bytes 98312 | tf_op jit(solution)/shard_map/ppermute | solution.py:411
  22.8 4.9 %collective-permute-start.7 = (bf16[128,128]{1,0:T(8,128)(2,1)S(1)}, bf16[128,128]{1,0:T(8,128)(2,1)S(1)}, u32[]{:S(2)}, u32[]{:S(2)}) collective-permute-start(bf16[128,128]{1,0:T(8,128)(2,1)S(1)} %get-tuple-element.39), channel_id=1, source_target_pairs={{0,12},{2,14},{4,8},{6,10},{8,4},{10,6},{12,0},{14,2},{16,28},{18,... | collective-permute-start | bytes 98312 | tf_op jit(solution)/shard_map/ppermute | solution.py:411
  24.4 4.2 %collective-permute-start.8 = (bf16[128,128]{1,0:T(8,128)(2,1)S(1)}, bf16[128,128]{1,0:T(8,128)(2,1)S(1)}, u32[]{:S(2)}, u32[]{:S(2)}) collective-permute-start(bf16[128,128]{1,0:T(8,128)(2,1)S(1)} %get-tuple-element.40), channel_id=1, source_target_pairs={{0,14},{2,12},{4,10},{6,8},{8,6},{10,4},{12,2},{14,0},{16,30},{18,... | collective-permute-start | bytes 98312 | tf_op jit(solution)/shard_map/ppermute | solution.py:411
  24.4 4.9 %collective-permute-start.1 = (bf16[128,128]{1,0:T(8,128)(2,1)S(1)}, bf16[128,128]{1,0:T(8,128)(2,1)S(1)}, u32[]{:S(2)}, u32[]{:S(2)}) collective-permute-start(bf16[128,128]{1,0:T(8,128)(2,1)S(1)} %get-tuple-element.33.picks_ref), channel_id=1, source_target_pairs={{0,16},{2,18},{4,20},{6,22},{8,24},{10,26},{12,28},{14,30},{16,0},... | collective-permute-start | bytes 98312 | tf_op jit(solution)/shard_map/ppermute | solution.py:420
  31.1 11.0 %collective-permute-start.9 = (f32[128,128]{1,0:T(8,128)S(1)}, f32[128,128]{1,0:T(8,128)S(1)}, u32[]{:S(2)}, u32[]{:S(2)}) collective-permute-start(f32[128,128]{1,0:T(8,128)S(1)} %get-tuple-element.46), channel_id=1, source_target_pairs={{0,16},{2,18},{4,20},{6,22},{8,24},{10,26},{12,28},{14,30},{16,0},... | collective-permute-start | bytes 196616 | tf_op jit(solution)/shard_map/ppermute | solution.py:420
  50.5 4.2 %collective-permute-start.10 = (bf16[384,128]{1,0:T(8,128)(2,1)S(1)}, bf16[384,128]{1,0:T(8,128)(2,1)S(1)}, u32[]{:S(2)}, u32[]{:S(2)}) collective-permute-start(bf16[384,128]{1,0:T(8,128)(2,1)S(1)} %get-tuple-element.48), channel_id=1, source_target_pairs={{0,2},{2,0},{4,6},{6,4},{8,10},{10,8},{12,14},{14,12},{16,18},{18,... | collective-permute-start | bytes 294920 | tf_op jit(solution)/shard_map/ppermute | solution.py:411
  50.6 5.6 %collective-permute-start.11 = (bf16[384,128]{1,0:T(8,128)(2,1)S(1)}, bf16[384,128]{1,0:T(8,128)(2,1)S(1)}, u32[]{:S(2)}, u32[]{:S(2)}) collective-permute-start(bf16[384,128]{1,0:T(8,128)(2,1)S(1)} %get-tuple-element.49), channel_id=1, source_target_pairs={{0,4},{2,6},{4,0},{6,2},{8,12},{10,14},{12,8},{14,10},{16,20},{18,... | collective-permute-start | bytes 294920 | tf_op jit(solution)/shard_map/ppermute | solution.py:411
  52.0 5.4 %collective-permute-start.12 = (bf16[384,128]{1,0:T(8,128)(2,1)S(1)}, bf16[384,128]{1,0:T(8,128)(2,1)S(1)}, u32[]{:S(2)}, u32[]{:S(2)}) collective-permute-start(bf16[384,128]{1,0:T(8,128)(2,1)S(1)} %get-tuple-element.50), channel_id=1, source_target_pairs={{0,6},{2,4},{4,2},{6,0},{8,14},{10,12},{12,10},{14,8},{16,22},{18,... | collective-permute-start | bytes 294920 | tf_op jit(solution)/shard_map/ppermute | solution.py:411
  52.4 5.8 %collective-permute-start.13 = (bf16[384,128]{1,0:T(8,128)(2,1)S(1)}, bf16[384,128]{1,0:T(8,128)(2,1)S(1)}, u32[]{:S(2)}, u32[]{:S(2)}) collective-permute-start(bf16[384,128]{1,0:T(8,128)(2,1)S(1)} %get-tuple-element.51), channel_id=1, source_target_pairs={{0,8},{2,10},{4,12},{6,14},{8,0},{10,2},{12,4},{14,6},{16,24},{18,... | collective-permute-start | bytes 294920 | tf_op jit(solution)/shard_map/ppermute | solution.py:411
  54.7 5.2 %collective-permute-start.14 = (bf16[384,128]{1,0:T(8,128)(2,1)S(1)}, bf16[384,128]{1,0:T(8,128)(2,1)S(1)}, u32[]{:S(2)}, u32[]{:S(2)}) collective-permute-start(bf16[384,128]{1,0:T(8,128)(2,1)S(1)} %get-tuple-element.52), channel_id=1, source_target_pairs={{0,10},{2,8},{4,14},{6,12},{8,2},{10,0},{12,6},{14,4},{16,26},{18,... | collective-permute-start | bytes 294920 | tf_op jit(solution)/shard_map/ppermute | solution.py:411
  54.7 8.4 %collective-permute-start.15 = (bf16[384,128]{1,0:T(8,128)(2,1)S(1)}, bf16[384,128]{1,0:T(8,128)(2,1)S(1)}, u32[]{:S(2)}, u32[]{:S(2)}) collective-permute-start(bf16[384,128]{1,0:T(8,128)(2,1)S(1)} %get-tuple-element.53), channel_id=1, source_target_pairs={{0,12},{2,14},{4,8},{6,10},{8,4},{10,6},{12,0},{14,2},{16,28},{18,... | collective-permute-start | bytes 294920 | tf_op jit(solution)/shard_map/ppermute | solution.py:411
  56.2 7.9 %collective-permute-start.16 = (bf16[384,128]{1,0:T(8,128)(2,1)S(1)}, bf16[384,128]{1,0:T(8,128)(2,1)S(1)}, u32[]{:S(2)}, u32[]{:S(2)}) collective-permute-start(bf16[384,128]{1,0:T(8,128)(2,1)S(1)} %get-tuple-element.54), channel_id=1, source_target_pairs={{0,14},{2,12},{4,10},{6,8},{8,6},{10,4},{12,2},{14,0},{16,30},{18,... | collective-permute-start | bytes 294920 | tf_op jit(solution)/shard_map/ppermute | solution.py:411

commit v10 on v9

--- a/solution.py
+++ b/solution.py
@@ -16,7 +16,7 @@
 LOG2E = math.log2(math.e)
 SCORE_FACTOR = SCALE * LOG2E
 STRIP = 64
-PIECE = 1024
+PIECE = 128
 BUSY = 2**35
 STAT_ROWS = 16
 

time: 66.2 us -> 65.7 us (level)
  transfers between devices with their start and end apart: 18 -> 18, of which waited for: 11 -> 11; matrix products, arithmetic and copies ran while one was open for 0% -> 0% of each run, Pallas kernels for 20% -> 19%
where the time goes in v10:
time: 65.7 us; the launch traced here: 65.5 us
  Pallas kernels  24.5 us (37%)
  starting transfers between devices  24.2 us (37%)
  waiting for transfers between devices  16 us (24%)
  between operations  0.73 us (1%)
    pallas_call x7, Pallas kernels, call(): pl.pallas_call(kernel, out_shape=tuple((jax.ShapeDtypeStruct(*shape) for...  24.5 us
    ppermute x14, starting transfers between devices, swap(): lax.ppermute(values[bits], 'context', pairs[bits])  11.9 us
    ppermute x14, waiting for transfers between devices, swap(): lax.ppermute(values[bits], 'context', pairs[bits])  8.76 us
    all_to_all x1, waiting for transfers between devices, exchange(): return lax.all_to_all(value, 'context', 0, 0, axis_index_groups=groups)  6.43 us
    ppermute x2, starting transfers between devices, segment_shift(): return lax.ppermute(value, 'context', pairs)  5.35 us
    all_to_all x1, starting transfers between devices, exchange(): return lax.all_to_all(value, 'context', 0, 0, axis_index_groups=groups)  3.95 us
    ppermute x1, starting transfers between devices, body(): upstreams.append(lax.ppermute(upstream, 'heads', pairs))  3 us
  transfers between devices with their start and end apart: 18, of which 11 were waited for; matrix products, arithmetic and copies ran while one was open for 0% of the time, Pallas kernels for 19%

profile of v10, /device:TPU:0, one launch (start us, length us, event | category | flops | bytes accessed | tf_op | source)
XLA Modules:
  0.0 65.5 jit_solution(12640172568608683726)
XLA Ops:
  0.6 3.0 %collective-permute-start = (bf16[128,1024]{1,0:T(8,128)(2,1)}, bf16[128,1024]{1,0:T(8,128)(2,1)S(1)}, u32[]{:S(2)}, u32[]{:S(2)}) collective-permute-start(bf16[128,1024]{1,0:T(8,128)(2,1)} %refs_0_.1), channel_id=1, source_target_pairs={{0,1},{1,0},{2,3},{3,2},{4,5},{5,4},{6,7},{7,6},{8,9},{9,8},{10,11... | collective-permute-start | bytes 786440 | tf_op jit(solution)/shard_map/ppermute | solution.py:425
  3.6 2.3 %pack_rows.1 = bf16[8,384,128]{2,1,0:T(8,128)(2,1)} custom-call(bf16[256,512]{1,0:T(8,128)(2,1)} %query_hbm.1, bf16[256,512]{1,0:T(8,128)(2,1)} %key_hbm.1, bf16[256,512]{1,0:T(8,128)(2,1)} %value_hbm.1), custom_call_target="tpu_custom_call" | custom-call | flops 2147483648 | bytes 2097152 | tf_op jit(solution)/shard_map/pack_rows/pallas_call | solution.py:378
  5.9 0.0 copy-start.1
  5.9 0.0 copy-start.2
  6.0 4.0 %all-to-all-start = ((bf16[8,384,128]{2,1,0:T(8,128)(2,1)}), bf16[8,384,128]{2,1,0:T(8,128)(2,1)S(1)}, u32[]{:S(2)}, u32[]{:S(2)}) async-start(bf16[8,384,128]{2,1,0:T(8,128)(2,1)} %pack_rows.1), calls=%async_computation | async-start | bytes 1572864 | tf_op jit(solution)/shard_map/all_to_all | solution.py:416
  9.9 0.1 pad_add_fusion.place_ref
  10.0 0.2 collective-permute-done.refs_1_
  10.2 0.0 copy-done.1
  10.2 0.0 copy-done.2
  10.2 1.5 %project_pack.1 = (bf16[128,128]{1,0:T(8,128)(2,1)S(1)}, bf16[128,128]{1,0:T(8,128)(2,1)S(1)}, bf16[128,128]{1,0:T(8,128)(2,1)S(1)}, bf16[128,128]{1,0:T(8,128)(...) custom-call(s32[2]{0:T(128)S(1)} %pad_add_fusion.place_ref, ...), custom_call_target="tpu_custom_call" | custom-call | flops 34359738368 | bytes 2097152 | tf_op jit(solution)/shard_map/project_pack/pallas_call | solution.py:378
  11.7 0.4 collective-permute-start.2
  12.1 1.7 %collective-permute-start.3 = (bf16[128,128]{1,0:T(8,128)(2,1)S(1)}, bf16[128,128]{1,0:T(8,128)(2,1)S(1)}, u32[]{:S(2)}, u32[]{:S(2)}) collective-permute-start(bf16[128,128]{1,0:T(8,128)(2,1)S(1)} %get-tuple-element.35), channel_id=1, source_target_pairs={{0,4},{2,6},{4,0},{6,2},{8,12},{10,14},{12,8},{14,10},{16,20},{18,... | collective-permute-start | bytes 98312 | tf_op jit(solution)/shard_map/ppermute | solution.py:411
  13.8 0.0 collective-permute-start.4
  13.8 1.7 %collective-permute-start.5 = (bf16[128,128]{1,0:T(8,128)(2,1)S(1)}, bf16[128,128]{1,0:T(8,128)(2,1)S(1)}, u32[]{:S(2)}, u32[]{:S(2)}) collective-permute-start(bf16[128,128]{1,0:T(8,128)(2,1)S(1)} %get-tuple-element.37), channel_id=1, source_target_pairs={{0,8},{2,10},{4,12},{6,14},{8,0},{10,2},{12,4},{14,6},{16,24},{18,... | collective-permute-start | bytes 98312 | tf_op jit(solution)/shard_map/ppermute | solution.py:411
  15.5 0.0 copy-start
  15.5 0.1 collective-permute-start.6
  15.6 6.4 %all-to-all-done.sent_ref = bf16[8,384,128]{2,1,0:T(8,128)(2,1)S(1)} async-done(((bf16[8,384,128]{2,1,0:T(8,128)(2,1)}), bf16[8,384,128]{2,1,0:T(8,128)(2,1)S(1)}, u32[]{:S(2)}, u32[]{:S(2)}) %all-to-all-start) | async-done | bytes 786464 | tf_op jit(solution)/shard_map/all_to_all | solution.py:416
  22.0 0.0 copy-done
  22.0 0.8 %gather_keys.1 = (bf16[2048,128]{1,0:T(8,128)(2,1)S(1)}, bf16[64,2048]{1,0:T(8,128)(2,1)S(1)}, bf16[8,128,128]{2,1,0:T(8,128)(2,1)S(1)}, bf16[128,128]{1,0:T(8,128)(2,1)S(1)}) custom-call(s32[2]{0:T(128)S(1)} %pad_add_fusion.place_ref, s32[16]{0:T(128)S(1)} %copy-done, bf16[8,384,128]{2,1,0:T(8,128)(2,1)S(1)} %all-to-all-done.sent_ref, ...), custom_call_target="tpu_custom_call" | custom-call | bytes 2097152 | tf_op jit(solution)/shard_map/gather_keys/pallas_call | solution.py:378
  22.8 0.0 collective-permute-done.2.refs_2_
  22.8 1.5 %collective-permute-start.7 = (bf16[128,128]{1,0:T(8,128)(2,1)S(1)}, bf16[128,128]{1,0:T(8,128)(2,1)S(1)}, u32[]{:S(2)}, u32[]{:S(2)}) collective-permute-start(bf16[128,128]{1,0:T(8,128)(2,1)S(1)} %get-tuple-element.39), channel_id=1, source_target_pairs={{0,12},{2,14},{4,8},{6,10},{8,4},{10,6},{12,0},{14,2},{16,28},{18,... | collective-permute-start | bytes 98312 | tf_op jit(solution)/shard_map/ppermute | solution.py:411
  24.4 0.0 collective-permute-done.3.refs_3_
  24.4 0.0 collective-permute-start.8
  24.4 0.0 collective-permute-done.4.refs_4_
  24.4 2.7 %collective-permute-start.1 = (bf16[128,128]{1,0:T(8,128)(2,1)S(1)}, bf16[128,128]{1,0:T(8,128)(2,1)S(1)}, u32[]{:S(2)}, u32[]{:S(2)}) collective-permute-start(bf16[128,128]{1,0:T(8,128)(2,1)S(1)} %get-tuple-element.33.picks_ref), channel_id=1, source_target_pairs={{0,16},{2,18},{4,20},{6,22},{8,24},{10,26},{12,28},{14,30},{16,0},... | collective-permute-start | bytes 98312 | tf_op jit(solution)/shard_map/ppermute | solution.py:420
  27.0 0.0 collective-permute-done.5.refs_5_
  27.0 0.0 collective-permute-done.6.refs_6_
  27.0 0.7 %collective-permute-done.7.refs_7_ = bf16[128,128]{1,0:T(8,128)(2,1)S(1)} collective-permute-done((bf16[128,128]{1,0:T(8,128)(2,1)S(1)}, bf16[128,128]{1,0:T(8,128)(2,1)S(1)}, u32[]{:S(2)}, u32[]{:S(2)}) %collective-permute-start.7) | collective-permute-done | bytes 32800 | tf_op jit(solution)/shard_map/ppermute | solution.py:411
  27.7 0.9 %collective-permute-done.8.refs_8_ = bf16[128,128]{1,0:T(8,128)(2,1)S(1)} collective-permute-done((bf16[128,128]{1,0:T(8,128)(2,1)S(1)}, bf16[128,128]{1,0:T(8,128)(2,1)S(1)}, u32[]{:S(2)}, u32[]{:S(2)}) %collective-permute-start.8) | collective-permute-done | bytes 32800 | tf_op jit(solution)/shard_map/ppermute | solution.py:411
  28.6 0.6 collective-permute-done.1.refs_0_
  29.3 1.9 %picked_rows.1 = (bf16[144,128]{1,0:T(8,128)(2,1)S(1)}, f32[128,128]{1,0:T(8,128)S(1)}, f32[128,128]{1,0:T(8,128)S(1)}, bf16[8,128,128]{2,1,0:T(8,128)(2,1)S(1)}) custom-call(s32[2]{0:T(128)S(1)} %pad_add_fusion.place_ref, s32[16]{0:T(128)S(1)} %copy-done, bf16[2048,128]{1,0:T(8,128)(2,1)S(1)} %get-tuple-element.30.near_ref.keys_ref, ...), custom_call_target="tpu_custom_call" | custom-call | flops 268435456 | bytes 2097152 | tf_op jit(solution)/shard_map/picked_rows/pallas_call | solution.py:378
  31.1 2.7 %collective-permute-start.9 = (f32[128,128]{1,0:T(8,128)S(1)}, f32[128,128]{1,0:T(8,128)S(1)}, u32[]{:S(2)}, u32[]{:S(2)}) collective-permute-start(f32[128,128]{1,0:T(8,128)S(1)} %get-tuple-element.46), channel_id=1, source_target_pairs={{0,16},{2,18},{4,20},{6,22},{8,24},{10,26},{12,28},{14,30},{16,0},... | collective-permute-start | bytes 196616 | tf_op jit(solution)/shard_map/ppermute | solution.py:420
  33.8 7.9 %first_rows.1 = (f32[2048,128]{1,0:T(8,128)S(1)}, bf16[4,128,128]{2,1,0:T(8,128)(2,1)S(1)}) custom-call(s32[2]{0:T(128)S(1)} %pad_add_fusion.place_ref, s32[16]{0:T(128)S(1)} %copy-done, bf16[2048,128]{1,0:T(8,128)(2,1)S(1)} %get-tuple-element.30.near_ref.keys_ref, bf16[64,2048]{1,0:T(8,128)(2,1)S(1)} %get-tuple-element.31.key_t_ref, ...), custom_call_target="tpu_custom_call" | custom-call | flops 2684354560 | bytes 2097152 | tf_op jit(solution)/shard_map/first_rows/pallas_call | solution.py:378
  41.7 0.0 collective-permute-done.9.refs_0_
  41.7 8.2 %second_rows.1 = (bf16[384,128]{1,0:T(8,128)(2,1)S(1)}, bf16[384,128]{1,0:T(8,128)(2,1)S(1)}, bf16[384,128]{1,0:T(8,128)(2,1)S(1)}, bf16[384,128]{1,0:T(8,128)(2...) custom-call(s32[2]{0:T(128)S(1)} %pad_add_fusion.place_ref, ...), custom_call_target="tpu_custom_call" | custom-call | flops 2684354560 | bytes 2097152 | tf_op jit(solution)/shard_map/second_rows/pallas_call | solution.py:378
  49.9 0.1 collective-permute-start.10
  50.1 1.5 %collective-permute-start.11 = (bf16[384,128]{1,0:T(8,128)(2,1)S(1)}, bf16[384,128]{1,0:T(8,128)(2,1)S(1)}, u32[]{:S(2)}, u32[]{:S(2)}) collective-permute-start(bf16[384,128]{1,0:T(8,128)(2,1)S(1)} %get-tuple-element.49), channel_id=1, source_target_pairs={{0,4},{2,6},{4,0},{6,2},{8,12},{10,14},{12,8},{14,10},{16,20},{18,... | collective-permute-start | bytes 294920 | tf_op jit(solution)/shard_map/ppermute | solution.py:411
  51.5 0.4 collective-permute-start.12
  51.9 2.3 %collective-permute-start.13 = (bf16[384,128]{1,0:T(8,128)(2,1)S(1)}, bf16[384,128]{1,0:T(8,128)(2,1)S(1)}, u32[]{:S(2)}, u32[]{:S(2)}) collective-permute-start(bf16[384,128]{1,0:T(8,128)(2,1)S(1)} %get-tuple-element.51), channel_id=1, source_target_pairs={{0,8},{2,10},{4,12},{6,14},{8,0},{10,2},{12,4},{14,6},{16,24},{18,... | collective-permute-start | bytes 294920 | tf_op jit(solution)/shard_map/ppermute | solution.py:411
  54.2 0.0 collective-permute-start.14
  54.2 0.0 collective-permute-done.10.refs_1_
  54.2 1.2 %collective-permute-start.15 = (bf16[384,128]{1,0:T(8,128)(2,1)S(1)}, bf16[384,128]{1,0:T(8,128)(2,1)S(1)}, u32[]{:S(2)}, u32[]{:S(2)}) collective-permute-start(bf16[384,128]{1,0:T(8,128)(2,1)S(1)} %get-tuple-element.53), channel_id=1, source_target_pairs={{0,12},{2,14},{4,8},{6,10},{8,4},{10,6},{12,0},{14,2},{16,28},{18,... | collective-permute-start | bytes 294920 | tf_op jit(solution)/shard_map/ppermute | solution.py:411
  55.4 0.3 collective-permute-done.11.refs_2_
  55.7 1.0 %collective-permute-start.16 = (bf16[384,128]{1,0:T(8,128)(2,1)S(1)}, bf16[384,128]{1,0:T(8,128)(2,1)S(1)}, u32[]{:S(2)}, u32[]{:S(2)}) collective-permute-start(bf16[384,128]{1,0:T(8,128)(2,1)S(1)} %get-tuple-element.54), channel_id=1, source_target_pairs={{0,14},{2,12},{4,10},{6,8},{8,6},{10,4},{12,2},{14,0},{16,30},{18,... | collective-permute-start | bytes 294920 | tf_op jit(solution)/shard_map/ppermute | solution.py:411
  56.7 0.2 collective-permute-done.12.refs_3_
  56.9 0.8 %collective-permute-done.13.refs_4_ = bf16[384,128]{1,0:T(8,128)(2,1)S(1)} collective-permute-done((bf16[384,128]{1,0:T(8,128)(2,1)S(1)}, bf16[384,128]{1,0:T(8,128)(2,1)S(1)}, u32[]{:S(2)}, u32[]{:S(2)}) %collective-permute-start.13) | collective-permute-done | bytes 98336 | tf_op jit(solution)/shard_map/ppermute | solution.py:411
  57.7 1.7 %collective-permute-done.14.refs_5_ = bf16[384,128]{1,0:T(8,128)(2,1)S(1)} collective-permute-done((bf16[384,128]{1,0:T(8,128)(2,1)S(1)}, bf16[384,128]{1,0:T(8,128)(2,1)S(1)}, u32[]{:S(2)}, u32[]{:S(2)}) %collective-permute-start.14) | collective-permute-done | bytes 98336 | tf_op jit(solution)/shard_map/ppermute | solution.py:411
  59.4 3.2 %collective-permute-done.15.refs_6_ = bf16[384,128]{1,0:T(8,128)(2,1)S(1)} collective-permute-done((bf16[384,128]{1,0:T(8,128)(2,1)S(1)}, bf16[384,128]{1,0:T(8,128)(2,1)S(1)}, u32[]{:S(2)}, u32[]{:S(2)}) %collective-permute-start.15) | collective-permute-done | bytes 98336 | tf_op jit(solution)/shard_map/ppermute | solution.py:411
  62.6 1.0 %collective-permute-done.16.refs_7_ = bf16[384,128]{1,0:T(8,128)(2,1)S(1)} collective-permute-done((bf16[384,128]{1,0:T(8,128)(2,1)S(1)}, bf16[384,128]{1,0:T(8,128)(2,1)S(1)}, u32[]{:S(2)}, u32[]{:S(2)}) %collective-permute-start.16) | collective-permute-done | bytes 98336 | tf_op jit(solution)/shard_map/ppermute | solution.py:411
  63.6 1.9 %unpack.1 = (bf16[256,512]{1,0:T(8,128)(2,1)}, bf16[256,512]{1,0:T(8,128)(2,1)}, bf16[256,512]{1,0:T(8,128)(2,1)}) custom-call(s32[2]{0:T(128)S(1)} %pad_add_fusion.place_ref, bf16[384,128]{1,0:T(8,128)(2,1)S(1)} %get-tuple-element.47.refs_0_, bf16[384,128]{1,0:T(8,128)(2,1)S(1)} %collective-permute-done.10.refs_1_, ...), custom_call_target="tpu_custom_call" | custom-call | bytes 2097152 | tf_op jit(solution)/shard_map/unpack/pallas_call | solution.py:378
Async XLA Ops:
  0.6 9.5 %collective-permute-start = (bf16[128,1024]{1,0:T(8,128)(2,1)}, bf16[128,1024]{1,0:T(8,128)(2,1)S(1)}, u32[]{:S(2)}, u32[]{:S(2)}) collective-permute-start(bf16[128,1024]{1,0:T(8,128)(2,1)} %refs_0_.1), channel_id=1, source_target_pairs={{0,1},{1,0},{2,3},{3,2},{4,5},{5,4},{6,7},{7,6},{8,9},{9,8},{10,11... | collective-permute-start | bytes 786440 | tf_op jit(solution)/shard_map/ppermute | solution.py:425
  5.9 4.2 %copy-start.1 = (bf16[512,1024]{1,0:T(8,128)(2,1)S(1)}, bf16[512,1024]{1,0:T(8,128)(2,1)}, u32[]{:S(2)}) copy-start(bf16[512,1024]{1,0:T(8,128)(2,1)} %weight_ref.1) | copy-start | bytes 3145732
  5.9 4.2 %copy-start.2 = (bf16[128,1024]{1,0:T(8,128)(2,1)S(1)}, bf16[128,1024]{1,0:T(8,128)(2,1)}, u32[]{:S(2)}) copy-start(bf16[128,1024]{1,0:T(8,128)(2,1)} %refs_0_.1) | copy-start | bytes 786436
  6.0 16.1 %all-to-all-start = ((bf16[8,384,128]{2,1,0:T(8,128)(2,1)}), bf16[8,384,128]{2,1,0:T(8,128)(2,1)S(1)}, u32[]{:S(2)}, u32[]{:S(2)}) async-start(bf16[8,384,128]{2,1,0:T(8,128)(2,1)} %pack_rows.1), calls=%async_computation | async-start | bytes 1572864 | tf_op jit(solution)/shard_map/all_to_all | solution.py:416
  11.7 11.1 %collective-permute-start.2 = (bf16[128,128]{1,0:T(8,128)(2,1)S(1)}, bf16[128,128]{1,0:T(8,128)(2,1)S(1)}, u32[]{:S(2)}, u32[]{:S(2)}) collective-permute-start(bf16[128,128]{1,0:T(8,128)(2,1)S(1)} %get-tuple-element.34), channel_id=1, source_target_pairs={{0,2},{2,0},{4,6},{6,4},{8,10},{10,8},{12,14},{14,12},{16,18},{18,... | collective-permute-start | bytes 98312 | tf_op jit(solution)/shard_map/ppermute | solution.py:411
  12.1 12.3 %collective-permute-start.3 = (bf16[128,128]{1,0:T(8,128)(2,1)S(1)}, bf16[128,128]{1,0:T(8,128)(2,1)S(1)}, u32[]{:S(2)}, u32[]{:S(2)}) collective-permute-start(bf16[128,128]{1,0:T(8,128)(2,1)S(1)} %get-tuple-element.35), channel_id=1, source_target_pairs={{0,4},{2,6},{4,0},{6,2},{8,12},{10,14},{12,8},{14,10},{16,20},{18,... | collective-permute-start | bytes 98312 | tf_op jit(solution)/shard_map/ppermute | solution.py:411
  13.8 10.6 %collective-permute-start.4 = (bf16[128,128]{1,0:T(8,128)(2,1)S(1)}, bf16[128,128]{1,0:T(8,128)(2,1)S(1)}, u32[]{:S(2)}, u32[]{:S(2)}) collective-permute-start(bf16[128,128]{1,0:T(8,128)(2,1)S(1)} %get-tuple-element.36), channel_id=1, source_target_pairs={{0,6},{2,4},{4,2},{6,0},{8,14},{10,12},{12,10},{14,8},{16,22},{18,... | collective-permute-start | bytes 98312 | tf_op jit(solution)/shard_map/ppermute | solution.py:411
  13.8 13.2 %collective-permute-start.5 = (bf16[128,128]{1,0:T(8,128)(2,1)S(1)}, bf16[128,128]{1,0:T(8,128)(2,1)S(1)}, u32[]{:S(2)}, u32[]{:S(2)}) collective-permute-start(bf16[128,128]{1,0:T(8,128)(2,1)S(1)} %get-tuple-element.37), channel_id=1, source_target_pairs={{0,8},{2,10},{4,12},{6,14},{8,0},{10,2},{12,4},{14,6},{16,24},{18,... | collective-permute-start | bytes 98312 | tf_op jit(solution)/shard_map/ppermute | solution.py:411
  15.5 6.6 %copy-start = (s32[16]{0:T(128)S(1)}, s32[16]{0:T(128)}, u32[]{:S(2)}) copy-start(s32[16]{0:T(128)} %offset_ref.7) | copy-start | bytes 196
  15.5 11.6 %collective-permute-start.6 = (bf16[128,128]{1,0:T(8,128)(2,1)S(1)}, bf16[128,128]{1,0:T(8,128)(2,1)S(1)}, u32[]{:S(2)}, u32[]{:S(2)}) collective-permute-start(bf16[128,128]{1,0:T(8,128)(2,1)S(1)} %get-tuple-element.38), channel_id=1, source_target_pairs={{0,10},{2,8},{4,14},{6,12},{8,2},{10,0},{12,6},{14,4},{16,26},{18,... | collective-permute-start | bytes 98312 | tf_op jit(solution)/shard_map/ppermute | solution.py:411
  22.8 4.9 %collective-permute-start.7 = (bf16[128,128]{1,0:T(8,128)(2,1)S(1)}, bf16[128,128]{1,0:T(8,128)(2,1)S(1)}, u32[]{:S(2)}, u32[]{:S(2)}) collective-permute-start(bf16[128,128]{1,0:T(8,128)(2,1)S(1)} %get-tuple-element.39), channel_id=1, source_target_pairs={{0,12},{2,14},{4,8},{6,10},{8,4},{10,6},{12,0},{14,2},{16,28},{18,... | collective-permute-start | bytes 98312 | tf_op jit(solution)/shard_map/ppermute | solution.py:411
  24.4 4.2 %collective-permute-start.8 = (bf16[128,128]{1,0:T(8,128)(2,1)S(1)}, bf16[128,128]{1,0:T(8,128)(2,1)S(1)}, u32[]{:S(2)}, u32[]{:S(2)}) collective-permute-start(bf16[128,128]{1,0:T(8,128)(2,1)S(1)} %get-tuple-element.40), channel_id=1, source_target_pairs={{0,14},{2,12},{4,10},{6,8},{8,6},{10,4},{12,2},{14,0},{16,30},{18,... | collective-permute-start | bytes 98312 | tf_op jit(solution)/shard_map/ppermute | solution.py:411
  24.4 4.9 %collective-permute-start.1 = (bf16[128,128]{1,0:T(8,128)(2,1)S(1)}, bf16[128,128]{1,0:T(8,128)(2,1)S(1)}, u32[]{:S(2)}, u32[]{:S(2)}) collective-permute-start(bf16[128,128]{1,0:T(8,128)(2,1)S(1)} %get-tuple-element.33.picks_ref), channel_id=1, source_target_pairs={{0,16},{2,18},{4,20},{6,22},{8,24},{10,26},{12,28},{14,30},{16,0},... | collective-permute-start | bytes 98312 | tf_op jit(solution)/shard_map/ppermute | solution.py:420
  31.1 10.6 %collective-permute-start.9 = (f32[128,128]{1,0:T(8,128)S(1)}, f32[128,128]{1,0:T(8,128)S(1)}, u32[]{:S(2)}, u32[]{:S(2)}) collective-permute-start(f32[128,128]{1,0:T(8,128)S(1)} %get-tuple-element.46), channel_id=1, source_target_pairs={{0,16},{2,18},{4,20},{6,22},{8,24},{10,26},{12,28},{14,30},{16,0},... | collective-permute-start | bytes 196616 | tf_op jit(solution)/shard_map/ppermute | solution.py:420
  49.9 4.2 %collective-permute-start.10 = (bf16[384,128]{1,0:T(8,128)(2,1)S(1)}, bf16[384,128]{1,0:T(8,128)(2,1)S(1)}, u32[]{:S(2)}, u32[]{:S(2)}) collective-permute-start(bf16[384,128]{1,0:T(8,128)(2,1)S(1)} %get-tuple-element.48), channel_id=1, source_target_pairs={{0,2},{2,0},{4,6},{6,4},{8,10},{10,8},{12,14},{14,12},{16,18},{18,... | collective-permute-start | bytes 294920 | tf_op jit(solution)/shard_map/ppermute | solution.py:411
  50.1 5.6 %collective-permute-start.11 = (bf16[384,128]{1,0:T(8,128)(2,1)S(1)}, bf16[384,128]{1,0:T(8,128)(2,1)S(1)}, u32[]{:S(2)}, u32[]{:S(2)}) collective-permute-start(bf16[384,128]{1,0:T(8,128)(2,1)S(1)} %get-tuple-element.49), channel_id=1, source_target_pairs={{0,4},{2,6},{4,0},{6,2},{8,12},{10,14},{12,8},{14,10},{16,20},{18,... | collective-permute-start | bytes 294920 | tf_op jit(solution)/shard_map/ppermute | solution.py:411
  51.5 5.4 %collective-permute-start.12 = (bf16[384,128]{1,0:T(8,128)(2,1)S(1)}, bf16[384,128]{1,0:T(8,128)(2,1)S(1)}, u32[]{:S(2)}, u32[]{:S(2)}) collective-permute-start(bf16[384,128]{1,0:T(8,128)(2,1)S(1)} %get-tuple-element.50), channel_id=1, source_target_pairs={{0,6},{2,4},{4,2},{6,0},{8,14},{10,12},{12,10},{14,8},{16,22},{18,... | collective-permute-start | bytes 294920 | tf_op jit(solution)/shard_map/ppermute | solution.py:411
  51.9 5.8 %collective-permute-start.13 = (bf16[384,128]{1,0:T(8,128)(2,1)S(1)}, bf16[384,128]{1,0:T(8,128)(2,1)S(1)}, u32[]{:S(2)}, u32[]{:S(2)}) collective-permute-start(bf16[384,128]{1,0:T(8,128)(2,1)S(1)} %get-tuple-element.51), channel_id=1, source_target_pairs={{0,8},{2,10},{4,12},{6,14},{8,0},{10,2},{12,4},{14,6},{16,24},{18,... | collective-permute-start | bytes 294920 | tf_op jit(solution)/shard_map/ppermute | solution.py:411
  54.2 5.2 %collective-permute-start.14 = (bf16[384,128]{1,0:T(8,128)(2,1)S(1)}, bf16[384,128]{1,0:T(8,128)(2,1)S(1)}, u32[]{:S(2)}, u32[]{:S(2)}) collective-permute-start(bf16[384,128]{1,0:T(8,128)(2,1)S(1)} %get-tuple-element.52), channel_id=1, source_target_pairs={{0,10},{2,8},{4,14},{6,12},{8,2},{10,0},{12,6},{14,4},{16,26},{18,... | collective-permute-start | bytes 294920 | tf_op jit(solution)/shard_map/ppermute | solution.py:411
  54.2 8.4 %collective-permute-start.15 = (bf16[384,128]{1,0:T(8,128)(2,1)S(1)}, bf16[384,128]{1,0:T(8,128)(2,1)S(1)}, u32[]{:S(2)}, u32[]{:S(2)}) collective-permute-start(bf16[384,128]{1,0:T(8,128)(2,1)S(1)} %get-tuple-element.53), channel_id=1, source_target_pairs={{0,12},{2,14},{4,8},{6,10},{8,4},{10,6},{12,0},{14,2},{16,28},{18,... | collective-permute-start | bytes 294920 | tf_op jit(solution)/shard_map/ppermute | solution.py:411
  55.7 7.9 %collective-permute-start.16 = (bf16[384,128]{1,0:T(8,128)(2,1)S(1)}, bf16[384,128]{1,0:T(8,128)(2,1)S(1)}, u32[]{:S(2)}, u32[]{:S(2)}) collective-permute-start(bf16[384,128]{1,0:T(8,128)(2,1)S(1)} %get-tuple-element.54), channel_id=1, source_target_pairs={{0,14},{2,12},{4,10},{6,8},{8,6},{10,4},{12,2},{14,0},{16,30},{18,... | collective-permute-start | bytes 294920 | tf_op jit(solution)/shard_map/ppermute | solution.py:411

commit v11 on v10

--- a/solution.py
+++ b/solution.py
@@ -16,7 +16,7 @@
 LOG2E = math.log2(math.e)
 SCORE_FACTOR = SCALE * LOG2E
 STRIP = 64
-PIECE = 128
+PIECE = 256
 BUSY = 2**35
 STAT_ROWS = 16
 
@@ -145,7 +145,8 @@
             jnp.bfloat16
         )
         queries_out[place] = sent_ref[place, rows:, :]
-    key_t_out[...] = keys_out[...].astype(jnp.float32).T[:HEAD_SIZE].astype(jnp.bfloat16)
+    key_t_out[:PAIR, :] = keys_out[...].astype(jnp.float32).T.astype(jnp.bfloat16)
+    key_t_out[PAIR:, :] = jnp.ones((STAT_ROWS, keys_out.shape[0]), jnp.bfloat16)
 
 
 def query_and_grad(query_ref, grad_ref):
@@ -224,9 +225,6 @@
     row_lane = lax.broadcasted_iota(jnp.int32, (1, rows), 1)
     picked = lax.rem(row_lane, DILATION_RATE) == offset
 
-    def by_eight(value):
-        return value.reshape(value.shape[0] // 8, 8, rows)
-
     def weights_of(index):
         return query_and_grad(queries_ref.at[places[index]], grads_ref.at[places[index]])
 
@@ -235,73 +233,65 @@
         return jnp.concatenate([packed[:HEAD_SIZE], packed[HEAD_SIZE:]], 1).astype(jnp.bfloat16)
 
     def transposed_of(index):
-        zero = jnp.zeros((HEAD_SIZE, rows), jnp.bfloat16)
-        query = columns_of(queries_ref.at[places[index]])
-        grad = columns_of(grads_ref.at[places[index]])
-        return jnp.concatenate([query, zero], 0), jnp.concatenate([zero, grad], 0)
-
-    def first_pass(index, weights, start, state):
-        top, total, delta = state
+        return columns_of(queries_ref.at[places[index]]), columns_of(grads_ref.at[places[index]])
+
+    def first_pass(index, columns, start, state):
         slot = index % 2
-        query, grad = weights
-        keys = keys_ref[start : start + PIECE, :]
-        scores, dprobs = dot_nn(keys, query), dot_nn(keys, grad)
+        piece = slice(start, start + PIECE)
+        query, grad = columns
+        zero = jnp.zeros_like(query)
+        keys = keys_ref[piece, :]
+        score = dot_nn(keys, jnp.concatenate([query, zero], 0))
+        dprob_ref[slot, piece, :] = dot_nn(keys, jnp.concatenate([zero, grad], 0))
+        raised = jnp.max(fold(score, jnp.maximum), 0, keepdims=True) * SCORE_FACTOR
+        if state is not None:
+            raised = jnp.maximum(raised, state[0])
         for inner in range(0, PIECE, STRIP):
-            strip = slice(start + inner, start + inner + STRIP)
-            score, dprob = scores[inner : inner + STRIP], dprobs[inner : inner + STRIP]
-            part = fold(score, jnp.maximum) * SCORE_FACTOR
-            raised = part if top is None else jnp.maximum(top, part)
-            prob = jnp.exp2(by_eight(score) * SCORE_FACTOR - raised[None])
-            part_total = jnp.sum(prob, 0)
-            part_delta = jnp.sum(prob * by_eight(dprob), 0)
-            if top is None:
-                total, delta = part_total, part_delta
-            else:
-                shrink = jnp.exp2(top - raised)
-                total, delta = total * shrink + part_total, delta * shrink + part_delta
-            top = raised
-            prob_ref[slot, strip, :] = prob.reshape(STRIP, rows)
-            dprob_ref[slot, strip, :] = dprob
-            top_ref[slot, strip.start // STRIP] = raised
-        return top, total, delta
+            prob = jnp.exp2(score[inner : inner + STRIP] * SCORE_FACTOR - raised)
+            prob_ref[slot, start + inner : start + inner + STRIP, :] = prob.astype(jnp.bfloat16)
+        sums = dot_nn(key_t_ref[HEAD_SIZE:, piece], prob_ref[slot, piece, :])
+        if state is not None:
+            sums = sums + state[1] * jnp.exp2(state[0] - raised)
+        top_ref[slot, start // PIECE] = raised
+        return raised, sums
 
     def last_pass(index, lse, delta, both, start, query_grad):
         slot = index % 2
         piece = slice(start, start + PIECE)
+        factor = jnp.exp2(top_ref[slot, start // PIECE] - lse)
+        factor = jnp.broadcast_to(factor, (16, rows)).astype(jnp.bfloat16)[None]
         for inner in range(0, PIECE, STRIP):
             strip = slice(start + inner, start + inner + STRIP)
-            factor = jnp.exp2(top_ref[slot, strip.start // STRIP] - lse)
-            prob = by_eight(prob_ref[slot, strip, :]) * factor[None]
-            dscore = prob * (by_eight(dprob_ref[slot, strip, :]) - delta)
-            work_ref[slot, strip, :rows] = dscore.reshape(STRIP, rows).astype(jnp.bfloat16)
-            work_ref[slot, strip, rows:] = prob.reshape(STRIP, rows).astype(jnp.bfloat16)
+            prob = prob_ref[slot, strip, :].reshape(STRIP // 16, 16, rows) * factor
+            prob = prob.reshape(STRIP, rows)
+            centred = (dprob_ref[slot, strip, :] - delta).astype(jnp.bfloat16)
+            work_ref[slot, strip, :rows] = prob * centred
+            work_ref[slot, strip, rows:] = prob
         acc_ref[piece, :] += dot_nn(work_ref[slot, piece, :], both)
-        return query_grad + dot_nn(key_t_ref[:, piece], work_ref[slot, piece, :rows])
+        return query_grad + dot_nn(key_t_ref[:HEAD_SIZE, piece], work_ref[slot, piece, :rows])
 
     starts = range(0, near, PIECE)
-    weights = transposed_of(0)
-    state = (None, None, None)
+    columns = transposed_of(0)
+    state = None
     for start in starts:
-        state = first_pass(0, weights, start, state)
+        state = first_pass(0, columns, start, state)
     for index, place in enumerate(places):
         last = index + 1 == len(places)
         first = place * (rows // DILATION_RATE)
         extra = dot_nn(extra_ref[...], spread_matrix(offset, first, count, rows, 0))
         stats = [extra[PAIR + row : PAIR + row + 1] for row in range(6)]
-        top, total, delta = state
-        highest = jnp.max(top, 0, keepdims=True)
-        shrink = jnp.exp2(top - highest)
-        total = jnp.sum(total * shrink, 0, keepdims=True)
-        delta = jnp.sum(delta * shrink, 0, keepdims=True) / total
-        lse = jnp.where(picked, stats[0] + stats[1] + stats[2], highest + jnp.log2(total))
+        top, sums = state
+        total = sums[HEAD_SIZE : HEAD_SIZE + 1]
+        delta = jnp.sum(sums[:HEAD_SIZE] * columns[1].astype(jnp.float32), 0, keepdims=True) / total
+        lse = jnp.where(picked, stats[0] + stats[1] + stats[2], top + jnp.log2(total))
         delta = jnp.where(picked, stats[3] + stats[4] + stats[5], delta)
         both = jnp.concatenate(weights_of(index), 0)
         query_grad = extra[:HEAD_SIZE] + extra[HEAD_SIZE:PAIR]
-        weights = None if last else transposed_of(index + 1)
-        state = (None, None, None)
+        state = None
+        columns = None if last else transposed_of(index + 1)
         for start in starts:
             if not last:
-                state = first_pass(index + 1, weights, start, state)
+                state = first_pass(index + 1, columns, start, state)
             query_grad = last_pass(index, lse, delta, both, start, query_grad)
         query_grad = (query_grad * SCALE).T.astype(jnp.bfloat16)
         emit(place, jnp.concatenate([query_grad[:half], query_grad[half:]], 1))
@@ -444,7 +434,7 @@
     keys, key_t, queries, picks = call(
         functools.partial(gather_kernel, head_count), "gather_keys",
         [
-            ((near, PAIR), bf16), ((HEAD_SIZE, near), bf16), ((group, half, PAIR), bf16),
+            ((near, PAIR), bf16), ((PAIR + STAT_ROWS, near), bf16), ((group, half, PAIR), bf16),
             ((count, PAIR), bf16),
         ],
         scalars, [sent, grads_send[0]],
@@ -466,8 +456,8 @@
     ]
     steps = group // 2
     scratch = [
-        ((2, near, rows), f32), ((2, near, rows), f32), ((2, near, 2 * rows), bf16),
-        ((2, near // STRIP, 8, rows), f32),
+        ((2, near, rows), bf16), ((2, near, rows), f32), ((2, near, 2 * rows), bf16),
+        ((2, near // PIECE, 1, rows), f32),
     ]
     half_flops = 10 * near * near // 2 * PAIR
     acc, query_half = call(

time: 65.7 us -> 73.5 us (1.12)
  Pallas kernels: 24.5 us -> 32.3 us
    pallas_call x7, Pallas kernels: 24.5 us -> 32.3 us  [call(): pl.pallas_call(kernel, out_shape=tuple((jax.ShapeDtypeStruct(*shape) for...]
  transfers between devices with their start and end apart: 18 -> 18, of which waited for: 11 -> 11; matrix products, arithmetic and copies ran while one was open for 0% -> 0% of each run, Pallas kernels for 19% -> 23%
where the time goes in v11:
time: 73.5 us; the launch traced here: 73.3 us
  Pallas kernels  32.3 us (44%)
  starting transfers between devices  24.2 us (33%)
  waiting for transfers between devices  16 us (22%)
    pallas_call x7, Pallas kernels, call(): pl.pallas_call(kernel, out_shape=tuple((jax.ShapeDtypeStruct(*shape) for...  32.3 us
    ppermute x14, starting transfers between devices, swap(): lax.ppermute(values[bits], 'context', pairs[bits])  11.9 us
    ppermute x14, waiting for transfers between devices, swap(): lax.ppermute(values[bits], 'context', pairs[bits])  8.74 us
    all_to_all x1, waiting for transfers between devices, exchange(): return lax.all_to_all(value, 'context', 0, 0, axis_index_groups=groups)  6.43 us
    ppermute x2, starting transfers between devices, segment_shift(): return lax.ppermute(value, 'context', pairs)  5.33 us
    all_to_all x1, starting transfers between devices, exchange(): return lax.all_to_all(value, 'context', 0, 0, axis_index_groups=groups)  3.95 us
    ppermute x1, starting transfers between devices, body(): upstreams.append(lax.ppermute(upstream, 'heads', pairs))  3 us
  transfers between devices with their start and end apart: 18, of which 11 were waited for; matrix products, arithmetic and copies ran while one was open for 0% of the time, Pallas kernels for 23%

profile of v11, /device:TPU:0, one launch (start us, length us, event | category | flops | bytes accessed | tf_op | source)
XLA Modules:
  0.0 73.3 jit_solution(13718884927906930186)
XLA Ops:
  0.6 3.0 %collective-permute-start = (bf16[128,1024]{1,0:T(8,128)(2,1)}, bf16[128,1024]{1,0:T(8,128)(2,1)S(1)}, u32[]{:S(2)}, u32[]{:S(2)}) collective-permute-start(bf16[128,1024]{1,0:T(8,128)(2,1)} %refs_0_.1), channel_id=1, source_target_pairs={{0,1},{1,0},{2,3},{3,2},{4,5},{5,4},{6,7},{7,6},{8,9},{9,8},{10,11... | collective-permute-start | bytes 786440 | tf_op jit(solution)/shard_map/ppermute | solution.py:415
  3.6 2.3 %pack_rows.1 = bf16[8,384,128]{2,1,0:T(8,128)(2,1)} custom-call(bf16[256,512]{1,0:T(8,128)(2,1)} %query_hbm.1, bf16[256,512]{1,0:T(8,128)(2,1)} %key_hbm.1, bf16[256,512]{1,0:T(8,128)(2,1)} %value_hbm.1), custom_call_target="tpu_custom_call" | custom-call | flops 2147483648 | bytes 2097152 | tf_op jit(solution)/shard_map/pack_rows/pallas_call | solution.py:368
  5.9 0.0 copy-start.1
  5.9 0.0 copy-start.2
  6.0 4.0 %all-to-all-start = ((bf16[8,384,128]{2,1,0:T(8,128)(2,1)}), bf16[8,384,128]{2,1,0:T(8,128)(2,1)S(1)}, u32[]{:S(2)}, u32[]{:S(2)}) async-start(bf16[8,384,128]{2,1,0:T(8,128)(2,1)} %pack_rows.1), calls=%async_computation | async-start | bytes 1572864 | tf_op jit(solution)/shard_map/all_to_all | solution.py:406
  9.9 0.1 pad_add_fusion.place_ref
  10.0 0.2 collective-permute-done.refs_1_
  10.2 0.0 copy-done.1
  10.2 0.0 copy-done.2
  10.2 1.5 %project_pack.1 = (bf16[128,128]{1,0:T(8,128)(2,1)S(1)}, bf16[128,128]{1,0:T(8,128)(2,1)S(1)}, bf16[128,128]{1,0:T(8,128)(2,1)S(1)}, bf16[128,128]{1,0:T(8,128)(...) custom-call(s32[2]{0:T(128)S(1)} %pad_add_fusion.place_ref, ...), custom_call_target="tpu_custom_call" | custom-call | flops 34359738368 | bytes 2097152 | tf_op jit(solution)/shard_map/project_pack/pallas_call | solution.py:368
  11.7 0.4 collective-permute-start.2
  12.1 1.7 %collective-permute-start.3 = (bf16[128,128]{1,0:T(8,128)(2,1)S(1)}, bf16[128,128]{1,0:T(8,128)(2,1)S(1)}, u32[]{:S(2)}, u32[]{:S(2)}) collective-permute-start(bf16[128,128]{1,0:T(8,128)(2,1)S(1)} %get-tuple-element.35), channel_id=1, source_target_pairs={{0,4},{2,6},{4,0},{6,2},{8,12},{10,14},{12,8},{14,10},{16,20},{18,... | collective-permute-start | bytes 98312 | tf_op jit(solution)/shard_map/ppermute | solution.py:401
  13.8 0.0 collective-permute-start.4
  13.8 1.7 %collective-permute-start.5 = (bf16[128,128]{1,0:T(8,128)(2,1)S(1)}, bf16[128,128]{1,0:T(8,128)(2,1)S(1)}, u32[]{:S(2)}, u32[]{:S(2)}) collective-permute-start(bf16[128,128]{1,0:T(8,128)(2,1)S(1)} %get-tuple-element.37), channel_id=1, source_target_pairs={{0,8},{2,10},{4,12},{6,14},{8,0},{10,2},{12,4},{14,6},{16,24},{18,... | collective-permute-start | bytes 98312 | tf_op jit(solution)/shard_map/ppermute | solution.py:401
  15.5 0.0 copy-start
  15.5 0.1 collective-permute-start.6
  15.6 6.4 %all-to-all-done.sent_ref = bf16[8,384,128]{2,1,0:T(8,128)(2,1)S(1)} async-done(((bf16[8,384,128]{2,1,0:T(8,128)(2,1)}), bf16[8,384,128]{2,1,0:T(8,128)(2,1)S(1)}, u32[]{:S(2)}, u32[]{:S(2)}) %all-to-all-start) | async-done | bytes 786464 | tf_op jit(solution)/shard_map/all_to_all | solution.py:406
  22.0 0.0 copy-done
  22.0 0.8 %gather_keys.1 = (bf16[2048,128]{1,0:T(8,128)(2,1)S(1)}, bf16[144,2048]{1,0:T(8,128)(2,1)S(1)}, bf16[8,128,128]{2,1,0:T(8,128)(2,1)S(1)}, bf16[128,128]{1,0:T(8,128)(2,1)S(1)}) custom-call(s32[2]{0:T(128)S(1)} %pad_add_fusion.place_ref, s32[16]{0:T(128)S(1)} %copy-done, bf16[8,384,128]{2,1,0:T(8,128)(2,1)S(1)} %all-to-all-done.sent_ref, ...), custom_call_target="tpu_custom_call" | custom-call | bytes 2097152 | tf_op jit(solution)/shard_map/gather_keys/pallas_call | solution.py:368
  22.8 0.0 collective-permute-done.2.refs_2_
  22.9 1.5 %collective-permute-start.7 = (bf16[128,128]{1,0:T(8,128)(2,1)S(1)}, bf16[128,128]{1,0:T(8,128)(2,1)S(1)}, u32[]{:S(2)}, u32[]{:S(2)}) collective-permute-start(bf16[128,128]{1,0:T(8,128)(2,1)S(1)} %get-tuple-element.39), channel_id=1, source_target_pairs={{0,12},{2,14},{4,8},{6,10},{8,4},{10,6},{12,0},{14,2},{16,28},{18,... | collective-permute-start | bytes 98312 | tf_op jit(solution)/shard_map/ppermute | solution.py:401
  24.4 0.0 collective-permute-done.3.refs_3_
  24.4 0.0 collective-permute-start.8
  24.4 0.0 collective-permute-done.4.refs_4_
  24.4 2.7 %collective-permute-start.1 = (bf16[128,128]{1,0:T(8,128)(2,1)S(1)}, bf16[128,128]{1,0:T(8,128)(2,1)S(1)}, u32[]{:S(2)}, u32[]{:S(2)}) collective-permute-start(bf16[128,128]{1,0:T(8,128)(2,1)S(1)} %get-tuple-element.33.picks_ref), channel_id=1, source_target_pairs={{0,16},{2,18},{4,20},{6,22},{8,24},{10,26},{12,28},{14,30},{16,0},... | collective-permute-start | bytes 98312 | tf_op jit(solution)/shard_map/ppermute | solution.py:410
  27.0 0.0 collective-permute-done.5.refs_5_
  27.1 0.0 collective-permute-done.6.refs_6_
  27.1 0.7 collective-permute-done.7.refs_7_
  27.7 0.9 %collective-permute-done.8.refs_8_ = bf16[128,128]{1,0:T(8,128)(2,1)S(1)} collective-permute-done((bf16[128,128]{1,0:T(8,128)(2,1)S(1)}, bf16[128,128]{1,0:T(8,128)(2,1)S(1)}, u32[]{:S(2)}, u32[]{:S(2)}) %collective-permute-start.8) | collective-permute-done | bytes 32800 | tf_op jit(solution)/shard_map/ppermute | solution.py:401
  28.6 0.6 collective-permute-done.1.refs_0_
  29.3 1.9 %picked_rows.1 = (bf16[144,128]{1,0:T(8,128)(2,1)S(1)}, f32[128,128]{1,0:T(8,128)S(1)}, f32[128,128]{1,0:T(8,128)S(1)}, bf16[8,128,128]{2,1,0:T(8,128)(2,1)S(1)}) custom-call(s32[2]{0:T(128)S(1)} %pad_add_fusion.place_ref, s32[16]{0:T(128)S(1)} %copy-done, bf16[2048,128]{1,0:T(8,128)(2,1)S(1)} %get-tuple-element.30.near_ref.keys_ref, ...), custom_call_target="tpu_custom_call" | custom-call | flops 268435456 | bytes 2097152 | tf_op jit(solution)/shard_map/picked_rows/pallas_call | solution.py:368
  31.2 2.7 %collective-permute-start.9 = (f32[128,128]{1,0:T(8,128)S(1)}, f32[128,128]{1,0:T(8,128)S(1)}, u32[]{:S(2)}, u32[]{:S(2)}) collective-permute-start(f32[128,128]{1,0:T(8,128)S(1)} %get-tuple-element.46), channel_id=1, source_target_pairs={{0,16},{2,18},{4,20},{6,22},{8,24},{10,26},{12,28},{14,30},{16,0},... | collective-permute-start | bytes 196616 | tf_op jit(solution)/shard_map/ppermute | solution.py:410
  33.8 12.0 %first_rows.1 = (f32[2048,128]{1,0:T(8,128)S(1)}, bf16[4,128,128]{2,1,0:T(8,128)(2,1)S(1)}) custom-call(s32[2]{0:T(128)S(1)} %pad_add_fusion.place_ref, s32[16]{0:T(128)S(1)} %copy-done, bf16[2048,128]{1,0:T(8,128)(2,1)S(1)} %get-tuple-element.30.near_ref.keys_ref, bf16[144,2048]{1,0:T(8,128)(2,1)S(1)} %get-tuple-element.31.key_t_ref, ...), custom_call_target="tpu_custom_call" | custom-call | flops 2684354560 | bytes 2097152 | tf_op jit(solution)/shard_map/first_rows/pallas_call | solution.py:368
  45.8 0.0 collective-permute-done.9.refs_0_
  45.8 11.9 %second_rows.1 = (bf16[384,128]{1,0:T(8,128)(2,1)S(1)}, bf16[384,128]{1,0:T(8,128)(2,1)S(1)}, bf16[384,128]{1,0:T(8,128)(2,1)S(1)}, bf16[384,128]{1,0:T(8,128)(2...) custom-call(s32[2]{0:T(128)S(1)} %pad_add_fusion.place_ref, ...), custom_call_target="tpu_custom_call" | custom-call | flops 2684354560 | bytes 2097152 | tf_op jit(solution)/shard_map/second_rows/pallas_call | solution.py:368
  57.7 0.1 collective-permute-start.10
  57.8 1.5 %collective-permute-start.11 = (bf16[384,128]{1,0:T(8,128)(2,1)S(1)}, bf16[384,128]{1,0:T(8,128)(2,1)S(1)}, u32[]{:S(2)}, u32[]{:S(2)}) collective-permute-start(bf16[384,128]{1,0:T(8,128)(2,1)S(1)} %get-tuple-element.49), channel_id=1, source_target_pairs={{0,4},{2,6},{4,0},{6,2},{8,12},{10,14},{12,8},{14,10},{16,20},{18,... | collective-permute-start | bytes 294920 | tf_op jit(solution)/shard_map/ppermute | solution.py:401
  59.3 0.3 collective-permute-start.12
  59.6 2.3 %collective-permute-start.13 = (bf16[384,128]{1,0:T(8,128)(2,1)S(1)}, bf16[384,128]{1,0:T(8,128)(2,1)S(1)}, u32[]{:S(2)}, u32[]{:S(2)}) collective-permute-start(bf16[384,128]{1,0:T(8,128)(2,1)S(1)} %get-tuple-element.51), channel_id=1, source_target_pairs={{0,8},{2,10},{4,12},{6,14},{8,0},{10,2},{12,4},{14,6},{16,24},{18,... | collective-permute-start | bytes 294920 | tf_op jit(solution)/shard_map/ppermute | solution.py:401
  62.0 0.0 collective-permute-start.14
  62.0 0.0 collective-permute-done.10.refs_1_
  62.0 1.2 %collective-permute-start.15 = (bf16[384,128]{1,0:T(8,128)(2,1)S(1)}, bf16[384,128]{1,0:T(8,128)(2,1)S(1)}, u32[]{:S(2)}, u32[]{:S(2)}) collective-permute-start(bf16[384,128]{1,0:T(8,128)(2,1)S(1)} %get-tuple-element.53), channel_id=1, source_target_pairs={{0,12},{2,14},{4,8},{6,10},{8,4},{10,6},{12,0},{14,2},{16,28},{18,... | collective-permute-start | bytes 294920 | tf_op jit(solution)/shard_map/ppermute | solution.py:401
  63.2 0.3 collective-permute-done.11.refs_2_
  63.4 1.0 %collective-permute-start.16 = (bf16[384,128]{1,0:T(8,128)(2,1)S(1)}, bf16[384,128]{1,0:T(8,128)(2,1)S(1)}, u32[]{:S(2)}, u32[]{:S(2)}) collective-permute-start(bf16[384,128]{1,0:T(8,128)(2,1)S(1)} %get-tuple-element.54), channel_id=1, source_target_pairs={{0,14},{2,12},{4,10},{6,8},{8,6},{10,4},{12,2},{14,0},{16,30},{18,... | collective-permute-start | bytes 294920 | tf_op jit(solution)/shard_map/ppermute | solution.py:401
  64.5 0.2 collective-permute-done.12.refs_3_
  64.6 0.8 %collective-permute-done.13.refs_4_ = bf16[384,128]{1,0:T(8,128)(2,1)S(1)} collective-permute-done((bf16[384,128]{1,0:T(8,128)(2,1)S(1)}, bf16[384,128]{1,0:T(8,128)(2,1)S(1)}, u32[]{:S(2)}, u32[]{:S(2)}) %collective-permute-start.13) | collective-permute-done | bytes 98336 | tf_op jit(solution)/shard_map/ppermute | solution.py:401
  65.5 1.7 %collective-permute-done.14.refs_5_ = bf16[384,128]{1,0:T(8,128)(2,1)S(1)} collective-permute-done((bf16[384,128]{1,0:T(8,128)(2,1)S(1)}, bf16[384,128]{1,0:T(8,128)(2,1)S(1)}, u32[]{:S(2)}, u32[]{:S(2)}) %collective-permute-start.14) | collective-permute-done | bytes 98336 | tf_op jit(solution)/shard_map/ppermute | solution.py:401
  67.2 3.2 %collective-permute-done.15.refs_6_ = bf16[384,128]{1,0:T(8,128)(2,1)S(1)} collective-permute-done((bf16[384,128]{1,0:T(8,128)(2,1)S(1)}, bf16[384,128]{1,0:T(8,128)(2,1)S(1)}, u32[]{:S(2)}, u32[]{:S(2)}) %collective-permute-start.15) | collective-permute-done | bytes 98336 | tf_op jit(solution)/shard_map/ppermute | solution.py:401
  70.4 1.0 %collective-permute-done.16.refs_7_ = bf16[384,128]{1,0:T(8,128)(2,1)S(1)} collective-permute-done((bf16[384,128]{1,0:T(8,128)(2,1)S(1)}, bf16[384,128]{1,0:T(8,128)(2,1)S(1)}, u32[]{:S(2)}, u32[]{:S(2)}) %collective-permute-start.16) | collective-permute-done | bytes 98336 | tf_op jit(solution)/shard_map/ppermute | solution.py:401
  71.3 1.9 %unpack.1 = (bf16[256,512]{1,0:T(8,128)(2,1)}, bf16[256,512]{1,0:T(8,128)(2,1)}, bf16[256,512]{1,0:T(8,128)(2,1)}) custom-call(s32[2]{0:T(128)S(1)} %pad_add_fusion.place_ref, bf16[384,128]{1,0:T(8,128)(2,1)S(1)} %get-tuple-element.47.refs_0_, bf16[384,128]{1,0:T(8,128)(2,1)S(1)} %collective-permute-done.10.refs_1_, ...), custom_call_target="tpu_custom_call" | custom-call | bytes 2097152 | tf_op jit(solution)/shard_map/unpack/pallas_call | solution.py:368
Async XLA Ops:
  0.6 9.5 %collective-permute-start = (bf16[128,1024]{1,0:T(8,128)(2,1)}, bf16[128,1024]{1,0:T(8,128)(2,1)S(1)}, u32[]{:S(2)}, u32[]{:S(2)}) collective-permute-start(bf16[128,1024]{1,0:T(8,128)(2,1)} %refs_0_.1), channel_id=1, source_target_pairs={{0,1},{1,0},{2,3},{3,2},{4,5},{5,4},{6,7},{7,6},{8,9},{9,8},{10,11... | collective-permute-start | bytes 786440 | tf_op jit(solution)/shard_map/ppermute | solution.py:415
  5.9 4.2 %copy-start.1 = (bf16[512,1024]{1,0:T(8,128)(2,1)S(1)}, bf16[512,1024]{1,0:T(8,128)(2,1)}, u32[]{:S(2)}) copy-start(bf16[512,1024]{1,0:T(8,128)(2,1)} %weight_ref.1) | copy-start | bytes 3145732
  5.9 4.2 %copy-start.2 = (bf16[128,1024]{1,0:T(8,128)(2,1)S(1)}, bf16[128,1024]{1,0:T(8,128)(2,1)}, u32[]{:S(2)}) copy-start(bf16[128,1024]{1,0:T(8,128)(2,1)} %refs_0_.1) | copy-start | bytes 786436
  6.0 16.1 %all-to-all-start = ((bf16[8,384,128]{2,1,0:T(8,128)(2,1)}), bf16[8,384,128]{2,1,0:T(8,128)(2,1)S(1)}, u32[]{:S(2)}, u32[]{:S(2)}) async-start(bf16[8,384,128]{2,1,0:T(8,128)(2,1)} %pack_rows.1), calls=%async_computation | async-start | bytes 1572864 | tf_op jit(solution)/shard_map/all_to_all | solution.py:406
  11.7 11.1 %collective-permute-start.2 = (bf16[128,128]{1,0:T(8,128)(2,1)S(1)}, bf16[128,128]{1,0:T(8,128)(2,1)S(1)}, u32[]{:S(2)}, u32[]{:S(2)}) collective-permute-start(bf16[128,128]{1,0:T(8,128)(2,1)S(1)} %get-tuple-element.34), channel_id=1, source_target_pairs={{0,2},{2,0},{4,6},{6,4},{8,10},{10,8},{12,14},{14,12},{16,18},{18,... | collective-permute-start | bytes 98312 | tf_op jit(solution)/shard_map/ppermute | solution.py:401
  12.1 12.3 %collective-permute-start.3 = (bf16[128,128]{1,0:T(8,128)(2,1)S(1)}, bf16[128,128]{1,0:T(8,128)(2,1)S(1)}, u32[]{:S(2)}, u32[]{:S(2)}) collective-permute-start(bf16[128,128]{1,0:T(8,128)(2,1)S(1)} %get-tuple-element.35), channel_id=1, source_target_pairs={{0,4},{2,6},{4,0},{6,2},{8,12},{10,14},{12,8},{14,10},{16,20},{18,... | collective-permute-start | bytes 98312 | tf_op jit(solution)/shard_map/ppermute | solution.py:401
  13.8 10.6 %collective-permute-start.4 = (bf16[128,128]{1,0:T(8,128)(2,1)S(1)}, bf16[128,128]{1,0:T(8,128)(2,1)S(1)}, u32[]{:S(2)}, u32[]{:S(2)}) collective-permute-start(bf16[128,128]{1,0:T(8,128)(2,1)S(1)} %get-tuple-element.36), channel_id=1, source_target_pairs={{0,6},{2,4},{4,2},{6,0},{8,14},{10,12},{12,10},{14,8},{16,22},{18,... | collective-permute-start | bytes 98312 | tf_op jit(solution)/shard_map/ppermute | solution.py:401
  13.8 13.3 %collective-permute-start.5 = (bf16[128,128]{1,0:T(8,128)(2,1)S(1)}, bf16[128,128]{1,0:T(8,128)(2,1)S(1)}, u32[]{:S(2)}, u32[]{:S(2)}) collective-permute-start(bf16[128,128]{1,0:T(8,128)(2,1)S(1)} %get-tuple-element.37), channel_id=1, source_target_pairs={{0,8},{2,10},{4,12},{6,14},{8,0},{10,2},{12,4},{14,6},{16,24},{18,... | collective-permute-start | bytes 98312 | tf_op jit(solution)/shard_map/ppermute | solution.py:401
  15.5 6.6 %copy-start = (s32[16]{0:T(128)S(1)}, s32[16]{0:T(128)}, u32[]{:S(2)}) copy-start(s32[16]{0:T(128)} %offset_ref.7) | copy-start | bytes 196
  15.5 11.6 %collective-permute-start.6 = (bf16[128,128]{1,0:T(8,128)(2,1)S(1)}, bf16[128,128]{1,0:T(8,128)(2,1)S(1)}, u32[]{:S(2)}, u32[]{:S(2)}) collective-permute-start(bf16[128,128]{1,0:T(8,128)(2,1)S(1)} %get-tuple-element.38), channel_id=1, source_target_pairs={{0,10},{2,8},{4,14},{6,12},{8,2},{10,0},{12,6},{14,4},{16,26},{18,... | collective-permute-start | bytes 98312 | tf_op jit(solution)/shard_map/ppermute | solution.py:401
  22.9 4.9 %collective-permute-start.7 = (bf16[128,128]{1,0:T(8,128)(2,1)S(1)}, bf16[128,128]{1,0:T(8,128)(2,1)S(1)}, u32[]{:S(2)}, u32[]{:S(2)}) collective-permute-start(bf16[128,128]{1,0:T(8,128)(2,1)S(1)} %get-tuple-element.39), channel_id=1, source_target_pairs={{0,12},{2,14},{4,8},{6,10},{8,4},{10,6},{12,0},{14,2},{16,28},{18,... | collective-permute-start | bytes 98312 | tf_op jit(solution)/shard_map/ppermute | solution.py:401
  24.4 4.2 %collective-permute-start.8 = (bf16[128,128]{1,0:T(8,128)(2,1)S(1)}, bf16[128,128]{1,0:T(8,128)(2,1)S(1)}, u32[]{:S(2)}, u32[]{:S(2)}) collective-permute-start(bf16[128,128]{1,0:T(8,128)(2,1)S(1)} %get-tuple-element.40), channel_id=1, source_target_pairs={{0,14},{2,12},{4,10},{6,8},{8,6},{10,4},{12,2},{14,0},{16,30},{18,... | collective-permute-start | bytes 98312 | tf_op jit(solution)/shard_map/ppermute | solution.py:401
  24.4 4.9 %collective-permute-start.1 = (bf16[128,128]{1,0:T(8,128)(2,1)S(1)}, bf16[128,128]{1,0:T(8,128)(2,1)S(1)}, u32[]{:S(2)}, u32[]{:S(2)}) collective-permute-start(bf16[128,128]{1,0:T(8,128)(2,1)S(1)} %get-tuple-element.33.picks_ref), channel_id=1, source_target_pairs={{0,16},{2,18},{4,20},{6,22},{8,24},{10,26},{12,28},{14,30},{16,0},... | collective-permute-start | bytes 98312 | tf_op jit(solution)/shard_map/ppermute | solution.py:410
  31.2 14.6 %collective-permute-start.9 = (f32[128,128]{1,0:T(8,128)S(1)}, f32[128,128]{1,0:T(8,128)S(1)}, u32[]{:S(2)}, u32[]{:S(2)}) collective-permute-start(f32[128,128]{1,0:T(8,128)S(1)} %get-tuple-element.46), channel_id=1, source_target_pairs={{0,16},{2,18},{4,20},{6,22},{8,24},{10,26},{12,28},{14,30},{16,0},... | collective-permute-start | bytes 196616 | tf_op jit(solution)/shard_map/ppermute | solution.py:410
  57.7 4.3 %collective-permute-start.10 = (bf16[384,128]{1,0:T(8,128)(2,1)S(1)}, bf16[384,128]{1,0:T(8,128)(2,1)S(1)}, u32[]{:S(2)}, u32[]{:S(2)}) collective-permute-start(bf16[384,128]{1,0:T(8,128)(2,1)S(1)} %get-tuple-element.48), channel_id=1, source_target_pairs={{0,2},{2,0},{4,6},{6,4},{8,10},{10,8},{12,14},{14,12},{16,18},{18,... | collective-permute-start | bytes 294920 | tf_op jit(solution)/shard_map/ppermute | solution.py:401
  57.8 5.6 %collective-permute-start.11 = (bf16[384,128]{1,0:T(8,128)(2,1)S(1)}, bf16[384,128]{1,0:T(8,128)(2,1)S(1)}, u32[]{:S(2)}, u32[]{:S(2)}) collective-permute-start(bf16[384,128]{1,0:T(8,128)(2,1)S(1)} %get-tuple-element.49), channel_id=1, source_target_pairs={{0,4},{2,6},{4,0},{6,2},{8,12},{10,14},{12,8},{14,10},{16,20},{18,... | collective-permute-start | bytes 294920 | tf_op jit(solution)/shard_map/ppermute | solution.py:401
  59.3 5.3 %collective-permute-start.12 = (bf16[384,128]{1,0:T(8,128)(2,1)S(1)}, bf16[384,128]{1,0:T(8,128)(2,1)S(1)}, u32[]{:S(2)}, u32[]{:S(2)}) collective-permute-start(bf16[384,128]{1,0:T(8,128)(2,1)S(1)} %get-tuple-element.50), channel_id=1, source_target_pairs={{0,6},{2,4},{4,2},{6,0},{8,14},{10,12},{12,10},{14,8},{16,22},{18,... | collective-permute-start | bytes 294920 | tf_op jit(solution)/shard_map/ppermute | solution.py:401
  59.6 5.8 %collective-permute-start.13 = (bf16[384,128]{1,0:T(8,128)(2,1)S(1)}, bf16[384,128]{1,0:T(8,128)(2,1)S(1)}, u32[]{:S(2)}, u32[]{:S(2)}) collective-permute-start(bf16[384,128]{1,0:T(8,128)(2,1)S(1)} %get-tuple-element.51), channel_id=1, source_target_pairs={{0,8},{2,10},{4,12},{6,14},{8,0},{10,2},{12,4},{14,6},{16,24},{18,... | collective-permute-start | bytes 294920 | tf_op jit(solution)/shard_map/ppermute | solution.py:401
  62.0 5.2 %collective-permute-start.14 = (bf16[384,128]{1,0:T(8,128)(2,1)S(1)}, bf16[384,128]{1,0:T(8,128)(2,1)S(1)}, u32[]{:S(2)}, u32[]{:S(2)}) collective-permute-start(bf16[384,128]{1,0:T(8,128)(2,1)S(1)} %get-tuple-element.52), channel_id=1, source_target_pairs={{0,10},{2,8},{4,14},{6,12},{8,2},{10,0},{12,6},{14,4},{16,26},{18,... | collective-permute-start | bytes 294920 | tf_op jit(solution)/shard_map/ppermute | solution.py:401
  62.0 8.4 %collective-permute-start.15 = (bf16[384,128]{1,0:T(8,128)(2,1)S(1)}, bf16[384,128]{1,0:T(8,128)(2,1)S(1)}, u32[]{:S(2)}, u32[]{:S(2)}) collective-permute-start(bf16[384,128]{1,0:T(8,128)(2,1)S(1)} %get-tuple-element.53), channel_id=1, source_target_pairs={{0,12},{2,14},{4,8},{6,10},{8,4},{10,6},{12,0},{14,2},{16,28},{18,... | collective-permute-start | bytes 294920 | tf_op jit(solution)/shard_map/ppermute | solution.py:401
  63.4 7.9 %collective-permute-start.16 = (bf16[384,128]{1,0:T(8,128)(2,1)S(1)}, bf16[384,128]{1,0:T(8,128)(2,1)S(1)}, u32[]{:S(2)}, u32[]{:S(2)}) collective-permute-start(bf16[384,128]{1,0:T(8,128)(2,1)S(1)} %get-tuple-element.54), channel_id=1, source_target_pairs={{0,14},{2,12},{4,10},{6,8},{8,6},{10,4},{12,2},{14,0},{16,30},{18,... | collective-permute-start | bytes 294920 | tf_op jit(solution)/shard_map/ppermute | solution.py:401

commit v12 on v10

--- a/solution.py
+++ b/solution.py
@@ -16,7 +16,7 @@
 LOG2E = math.log2(math.e)
 SCORE_FACTOR = SCALE * LOG2E
 STRIP = 64
-PIECE = 128
+PIECE = 256
 BUSY = 2**35
 STAT_ROWS = 16
 
@@ -33,6 +33,12 @@
 
 def dot_nn(left, right):
     return jnp.dot(left, right, preferred_element_type=jnp.float32)
+
+
+def dot_tn(left, right):
+    return lax.dot_general(
+        left, right, (((0,), (0,)), ((), ())), preferred_element_type=jnp.float32
+    )
 
 
 def head_columns(ref, head):
@@ -276,7 +282,7 @@
             work_ref[slot, strip, :rows] = dscore.reshape(STRIP, rows).astype(jnp.bfloat16)
             work_ref[slot, strip, rows:] = prob.reshape(STRIP, rows).astype(jnp.bfloat16)
         acc_ref[piece, :] += dot_nn(work_ref[slot, piece, :], both)
-        return query_grad + dot_nn(key_t_ref[:, piece], work_ref[slot, piece, :rows])
+        return query_grad + dot_tn(work_ref[slot, piece, :rows], keys_ref[piece, :])
 
     starts = range(0, near, PIECE)
     weights = transposed_of(0)
@@ -286,8 +292,9 @@
     for index, place in enumerate(places):
         last = index + 1 == len(places)
         first = place * (rows // DILATION_RATE)
-        extra = dot_nn(extra_ref[...], spread_matrix(offset, first, count, rows, 0))
-        stats = [extra[PAIR + row : PAIR + row + 1] for row in range(6)]
+        spread = spread_matrix(offset, first, count, rows, 0)
+        extra = dot_nn(extra_ref[PAIR:, :], spread)
+        stats = [extra[row : row + 1] for row in range(6)]
         top, total, delta = state
         highest = jnp.max(top, 0, keepdims=True)
         shrink = jnp.exp2(top - highest)
@@ -296,14 +303,16 @@
         lse = jnp.where(picked, stats[0] + stats[1] + stats[2], highest + jnp.log2(total))
         delta = jnp.where(picked, stats[3] + stats[4] + stats[5], delta)
         both = jnp.concatenate(weights_of(index), 0)
-        query_grad = extra[:HEAD_SIZE] + extra[HEAD_SIZE:PAIR]
+        spread = spread_matrix(offset, first, count, rows, 1)
+        query_grad = dot_nt(spread, extra_ref[:PAIR, :])
+        query_grad = query_grad + pltpu.roll(query_grad, HEAD_SIZE, 1)
         weights = None if last else transposed_of(index + 1)
         state = (None, None, None)
         for start in starts:
             if not last:
                 state = first_pass(index + 1, weights, start, state)
             query_grad = last_pass(index, lse, delta, both, start, query_grad)
-        query_grad = (query_grad * SCALE).T.astype(jnp.bfloat16)
+        query_grad = (query_grad[:, :HEAD_SIZE] * SCALE).astype(jnp.bfloat16)
         emit(place, jnp.concatenate([query_grad[:half], query_grad[half:]], 1))
 
 

time: 65.7 us -> 66.5 us (1.012)
  Pallas kernels: 24.5 us -> 25.3 us
    pallas_call x7, Pallas kernels: 24.5 us -> 25.3 us  [call(): pl.pallas_call(kernel, out_shape=tuple((jax.ShapeDtypeStruct(*shape) for...]
where the time goes in v12:
time: 66.5 us; the launch traced here: 66.3 us
  Pallas kernels  25.3 us (38%)
  starting transfers between devices  24.2 us (36%)
  waiting for transfers between devices  16 us (24%)
  between operations  0.72 us (1%)
    pallas_call x7, Pallas kernels, call(): pl.pallas_call(kernel, out_shape=tuple((jax.ShapeDtypeStruct(*shape) for...  25.3 us
    ppermute x14, starting transfers between devices, swap(): lax.ppermute(values[bits], 'context', pairs[bits])  11.9 us
    ppermute x14, waiting for transfers between devices, swap(): lax.ppermute(values[bits], 'context', pairs[bits])  8.73 us
    all_to_all x1, waiting for transfers between devices, exchange(): return lax.all_to_all(value, 'context', 0, 0, axis_index_groups=groups)  6.43 us
    ppermute x2, starting transfers between devices, segment_shift(): return lax.ppermute(value, 'context', pairs)  5.35 us
    all_to_all x1, starting transfers between devices, exchange(): return lax.all_to_all(value, 'context', 0, 0, axis_index_groups=groups)  3.95 us
    ppermute x1, starting transfers between devices, body(): upstreams.append(lax.ppermute(upstream, 'heads', pairs))  3 us
  transfers between devices with their start and end apart: 18, of which 11 were waited for; matrix products, arithmetic and copies ran while one was open for 0% of the time, Pallas kernels for 19%

profile of v12, /device:TPU:0, one launch (start us, length us, event | category | flops | bytes accessed | tf_op | source)
XLA Modules:
  0.0 66.3 jit_solution(14012168197474230372)
XLA Ops:
  0.6 3.0 %collective-permute-start = (bf16[128,1024]{1,0:T(8,128)(2,1)}, bf16[128,1024]{1,0:T(8,128)(2,1)S(1)}, u32[]{:S(2)}, u32[]{:S(2)}) collective-permute-start(bf16[128,1024]{1,0:T(8,128)(2,1)} %refs_0_.1), channel_id=1, source_target_pairs={{0,1},{1,0},{2,3},{3,2},{4,5},{5,4},{6,7},{7,6},{8,9},{9,8},{10,11... | collective-permute-start | bytes 786440 | tf_op jit(solution)/shard_map/ppermute | solution.py:434
  3.6 2.3 %pack_rows.1 = bf16[8,384,128]{2,1,0:T(8,128)(2,1)} custom-call(bf16[256,512]{1,0:T(8,128)(2,1)} %query_hbm.1, bf16[256,512]{1,0:T(8,128)(2,1)} %key_hbm.1, bf16[256,512]{1,0:T(8,128)(2,1)} %value_hbm.1), custom_call_target="tpu_custom_call" | custom-call | flops 2147483648 | bytes 2097152 | tf_op jit(solution)/shard_map/pack_rows/pallas_call | solution.py:387
  5.9 0.0 copy-start.1
  5.9 0.0 copy-start.2
  6.0 4.0 %all-to-all-start = ((bf16[8,384,128]{2,1,0:T(8,128)(2,1)}), bf16[8,384,128]{2,1,0:T(8,128)(2,1)S(1)}, u32[]{:S(2)}, u32[]{:S(2)}) async-start(bf16[8,384,128]{2,1,0:T(8,128)(2,1)} %pack_rows.1), calls=%async_computation | async-start | bytes 1572864 | tf_op jit(solution)/shard_map/all_to_all | solution.py:425
  9.9 0.1 pad_add_fusion.place_ref
  10.0 0.2 collective-permute-done.refs_1_
  10.2 0.0 copy-done.1
  10.2 0.0 copy-done.2
  10.2 1.5 %project_pack.1 = (bf16[128,128]{1,0:T(8,128)(2,1)S(1)}, bf16[128,128]{1,0:T(8,128)(2,1)S(1)}, bf16[128,128]{1,0:T(8,128)(2,1)S(1)}, bf16[128,128]{1,0:T(8,128)(...) custom-call(s32[2]{0:T(128)S(1)} %pad_add_fusion.place_ref, ...), custom_call_target="tpu_custom_call" | custom-call | flops 34359738368 | bytes 2097152 | tf_op jit(solution)/shard_map/project_pack/pallas_call | solution.py:387
  11.7 0.4 collective-permute-start.2
  12.1 1.7 %collective-permute-start.3 = (bf16[128,128]{1,0:T(8,128)(2,1)S(1)}, bf16[128,128]{1,0:T(8,128)(2,1)S(1)}, u32[]{:S(2)}, u32[]{:S(2)}) collective-permute-start(bf16[128,128]{1,0:T(8,128)(2,1)S(1)} %get-tuple-element.35), channel_id=1, source_target_pairs={{0,4},{2,6},{4,0},{6,2},{8,12},{10,14},{12,8},{14,10},{16,20},{18,... | collective-permute-start | bytes 98312 | tf_op jit(solution)/shard_map/ppermute | solution.py:420
  13.8 0.0 collective-permute-start.4
  13.8 1.7 %collective-permute-start.5 = (bf16[128,128]{1,0:T(8,128)(2,1)S(1)}, bf16[128,128]{1,0:T(8,128)(2,1)S(1)}, u32[]{:S(2)}, u32[]{:S(2)}) collective-permute-start(bf16[128,128]{1,0:T(8,128)(2,1)S(1)} %get-tuple-element.37), channel_id=1, source_target_pairs={{0,8},{2,10},{4,12},{6,14},{8,0},{10,2},{12,4},{14,6},{16,24},{18,... | collective-permute-start | bytes 98312 | tf_op jit(solution)/shard_map/ppermute | solution.py:420
  15.5 0.0 copy-start
  15.5 0.1 collective-permute-start.6
  15.6 6.4 %all-to-all-done.sent_ref = bf16[8,384,128]{2,1,0:T(8,128)(2,1)S(1)} async-done(((bf16[8,384,128]{2,1,0:T(8,128)(2,1)}), bf16[8,384,128]{2,1,0:T(8,128)(2,1)S(1)}, u32[]{:S(2)}, u32[]{:S(2)}) %all-to-all-start) | async-done | bytes 786464 | tf_op jit(solution)/shard_map/all_to_all | solution.py:425
  22.0 0.0 copy-done
  22.0 0.8 %gather_keys.1 = (bf16[2048,128]{1,0:T(8,128)(2,1)S(1)}, bf16[64,2048]{1,0:T(8,128)(2,1)S(1)}, bf16[8,128,128]{2,1,0:T(8,128)(2,1)S(1)}, bf16[128,128]{1,0:T(8,128)(2,1)S(1)}) custom-call(s32[2]{0:T(128)S(1)} %pad_add_fusion.place_ref, s32[16]{0:T(128)S(1)} %copy-done, bf16[8,384,128]{2,1,0:T(8,128)(2,1)S(1)} %all-to-all-done.sent_ref, ...), custom_call_target="tpu_custom_call" | custom-call | bytes 2097152 | tf_op jit(solution)/shard_map/gather_keys/pallas_call | solution.py:387
  22.8 0.0 collective-permute-done.2.refs_2_
  22.8 1.5 %collective-permute-start.7 = (bf16[128,128]{1,0:T(8,128)(2,1)S(1)}, bf16[128,128]{1,0:T(8,128)(2,1)S(1)}, u32[]{:S(2)}, u32[]{:S(2)}) collective-permute-start(bf16[128,128]{1,0:T(8,128)(2,1)S(1)} %get-tuple-element.39), channel_id=1, source_target_pairs={{0,12},{2,14},{4,8},{6,10},{8,4},{10,6},{12,0},{14,2},{16,28},{18,... | collective-permute-start | bytes 98312 | tf_op jit(solution)/shard_map/ppermute | solution.py:420
  24.4 0.0 collective-permute-done.3.refs_3_
  24.4 0.0 collective-permute-start.8
  24.4 0.0 collective-permute-done.4.refs_4_
  24.4 2.7 %collective-permute-start.1 = (bf16[128,128]{1,0:T(8,128)(2,1)S(1)}, bf16[128,128]{1,0:T(8,128)(2,1)S(1)}, u32[]{:S(2)}, u32[]{:S(2)}) collective-permute-start(bf16[128,128]{1,0:T(8,128)(2,1)S(1)} %get-tuple-element.33.picks_ref), channel_id=1, source_target_pairs={{0,16},{2,18},{4,20},{6,22},{8,24},{10,26},{12,28},{14,30},{16,0},... | collective-permute-start | bytes 98312 | tf_op jit(solution)/shard_map/ppermute | solution.py:429
  27.0 0.0 collective-permute-done.5.refs_5_
  27.0 0.0 collective-permute-done.6.refs_6_
  27.0 0.7 %collective-permute-done.7.refs_7_ = bf16[128,128]{1,0:T(8,128)(2,1)S(1)} collective-permute-done((bf16[128,128]{1,0:T(8,128)(2,1)S(1)}, bf16[128,128]{1,0:T(8,128)(2,1)S(1)}, u32[]{:S(2)}, u32[]{:S(2)}) %collective-permute-start.7) | collective-permute-done | bytes 32800 | tf_op jit(solution)/shard_map/ppermute | solution.py:420
  27.7 0.9 %collective-permute-done.8.refs_8_ = bf16[128,128]{1,0:T(8,128)(2,1)S(1)} collective-permute-done((bf16[128,128]{1,0:T(8,128)(2,1)S(1)}, bf16[128,128]{1,0:T(8,128)(2,1)S(1)}, u32[]{:S(2)}, u32[]{:S(2)}) %collective-permute-start.8) | collective-permute-done | bytes 32800 | tf_op jit(solution)/shard_map/ppermute | solution.py:420
  28.6 0.6 collective-permute-done.1.refs_0_
  29.3 1.9 %picked_rows.1 = (bf16[144,128]{1,0:T(8,128)(2,1)S(1)}, f32[128,128]{1,0:T(8,128)S(1)}, f32[128,128]{1,0:T(8,128)S(1)}, bf16[8,128,128]{2,1,0:T(8,128)(2,1)S(1)}) custom-call(s32[2]{0:T(128)S(1)} %pad_add_fusion.place_ref, s32[16]{0:T(128)S(1)} %copy-done, bf16[2048,128]{1,0:T(8,128)(2,1)S(1)} %get-tuple-element.30.near_ref.keys_ref, ...), custom_call_target="tpu_custom_call" | custom-call | flops 268435456 | bytes 2097152 | tf_op jit(solution)/shard_map/picked_rows/pallas_call | solution.py:387
  31.1 2.7 %collective-permute-start.9 = (f32[128,128]{1,0:T(8,128)S(1)}, f32[128,128]{1,0:T(8,128)S(1)}, u32[]{:S(2)}, u32[]{:S(2)}) collective-permute-start(f32[128,128]{1,0:T(8,128)S(1)} %get-tuple-element.46), channel_id=1, source_target_pairs={{0,16},{2,18},{4,20},{6,22},{8,24},{10,26},{12,28},{14,30},{16,0},... | collective-permute-start | bytes 196616 | tf_op jit(solution)/shard_map/ppermute | solution.py:429
  33.8 8.2 %first_rows.1 = (f32[2048,128]{1,0:T(8,128)S(1)}, bf16[4,128,128]{2,1,0:T(8,128)(2,1)S(1)}) custom-call(s32[2]{0:T(128)S(1)} %pad_add_fusion.place_ref, s32[16]{0:T(128)S(1)} %copy-done, bf16[2048,128]{1,0:T(8,128)(2,1)S(1)} %get-tuple-element.30.near_ref.keys_ref, bf16[64,2048]{1,0:T(8,128)(2,1)S(1)} %get-tuple-element.31.key_t_ref, ...), custom_call_target="tpu_custom_call" | custom-call | flops 2684354560 | bytes 2097152 | tf_op jit(solution)/shard_map/first_rows/pallas_call | solution.py:387
  42.0 0.0 collective-permute-done.9.refs_0_
  42.0 8.7 %second_rows.1 = (bf16[384,128]{1,0:T(8,128)(2,1)S(1)}, bf16[384,128]{1,0:T(8,128)(2,1)S(1)}, bf16[384,128]{1,0:T(8,128)(2,1)S(1)}, bf16[384,128]{1,0:T(8,128)(2...) custom-call(s32[2]{0:T(128)S(1)} %pad_add_fusion.place_ref, ...), custom_call_target="tpu_custom_call" | custom-call | flops 2684354560 | bytes 2097152 | tf_op jit(solution)/shard_map/second_rows/pallas_call | solution.py:387
  50.7 0.1 collective-permute-start.10
  50.8 1.5 %collective-permute-start.11 = (bf16[384,128]{1,0:T(8,128)(2,1)S(1)}, bf16[384,128]{1,0:T(8,128)(2,1)S(1)}, u32[]{:S(2)}, u32[]{:S(2)}) collective-permute-start(bf16[384,128]{1,0:T(8,128)(2,1)S(1)} %get-tuple-element.49), channel_id=1, source_target_pairs={{0,4},{2,6},{4,0},{6,2},{8,12},{10,14},{12,8},{14,10},{16,20},{18,... | collective-permute-start | bytes 294920 | tf_op jit(solution)/shard_map/ppermute | solution.py:420
  52.3 0.4 collective-permute-start.12
  52.7 2.3 %collective-permute-start.13 = (bf16[384,128]{1,0:T(8,128)(2,1)S(1)}, bf16[384,128]{1,0:T(8,128)(2,1)S(1)}, u32[]{:S(2)}, u32[]{:S(2)}) collective-permute-start(bf16[384,128]{1,0:T(8,128)(2,1)S(1)} %get-tuple-element.51), channel_id=1, source_target_pairs={{0,8},{2,10},{4,12},{6,14},{8,0},{10,2},{12,4},{14,6},{16,24},{18,... | collective-permute-start | bytes 294920 | tf_op jit(solution)/shard_map/ppermute | solution.py:420
  55.0 0.0 collective-permute-start.14
  55.0 0.0 collective-permute-done.10.refs_1_
  55.0 1.2 %collective-permute-start.15 = (bf16[384,128]{1,0:T(8,128)(2,1)S(1)}, bf16[384,128]{1,0:T(8,128)(2,1)S(1)}, u32[]{:S(2)}, u32[]{:S(2)}) collective-permute-start(bf16[384,128]{1,0:T(8,128)(2,1)S(1)} %get-tuple-element.53), channel_id=1, source_target_pairs={{0,12},{2,14},{4,8},{6,10},{8,4},{10,6},{12,0},{14,2},{16,28},{18,... | collective-permute-start | bytes 294920 | tf_op jit(solution)/shard_map/ppermute | solution.py:420
  56.2 0.3 collective-permute-done.11.refs_2_
  56.5 1.0 %collective-permute-start.16 = (bf16[384,128]{1,0:T(8,128)(2,1)S(1)}, bf16[384,128]{1,0:T(8,128)(2,1)S(1)}, u32[]{:S(2)}, u32[]{:S(2)}) collective-permute-start(bf16[384,128]{1,0:T(8,128)(2,1)S(1)} %get-tuple-element.54), channel_id=1, source_target_pairs={{0,14},{2,12},{4,10},{6,8},{8,6},{10,4},{12,2},{14,0},{16,30},{18,... | collective-permute-start | bytes 294920 | tf_op jit(solution)/shard_map/ppermute | solution.py:420
  57.5 0.2 collective-permute-done.12.refs_3_
  57.7 0.8 %collective-permute-done.13.refs_4_ = bf16[384,128]{1,0:T(8,128)(2,1)S(1)} collective-permute-done((bf16[384,128]{1,0:T(8,128)(2,1)S(1)}, bf16[384,128]{1,0:T(8,128)(2,1)S(1)}, u32[]{:S(2)}, u32[]{:S(2)}) %collective-permute-start.13) | collective-permute-done | bytes 98336 | tf_op jit(solution)/shard_map/ppermute | solution.py:420
  58.5 1.7 %collective-permute-done.14.refs_5_ = bf16[384,128]{1,0:T(8,128)(2,1)S(1)} collective-permute-done((bf16[384,128]{1,0:T(8,128)(2,1)S(1)}, bf16[384,128]{1,0:T(8,128)(2,1)S(1)}, u32[]{:S(2)}, u32[]{:S(2)}) %collective-permute-start.14) | collective-permute-done | bytes 98336 | tf_op jit(solution)/shard_map/ppermute | solution.py:420
  60.2 3.2 %collective-permute-done.15.refs_6_ = bf16[384,128]{1,0:T(8,128)(2,1)S(1)} collective-permute-done((bf16[384,128]{1,0:T(8,128)(2,1)S(1)}, bf16[384,128]{1,0:T(8,128)(2,1)S(1)}, u32[]{:S(2)}, u32[]{:S(2)}) %collective-permute-start.15) | collective-permute-done | bytes 98336 | tf_op jit(solution)/shard_map/ppermute | solution.py:420
  63.4 1.0 %collective-permute-done.16.refs_7_ = bf16[384,128]{1,0:T(8,128)(2,1)S(1)} collective-permute-done((bf16[384,128]{1,0:T(8,128)(2,1)S(1)}, bf16[384,128]{1,0:T(8,128)(2,1)S(1)}, u32[]{:S(2)}, u32[]{:S(2)}) %collective-permute-start.16) | collective-permute-done | bytes 98336 | tf_op jit(solution)/shard_map/ppermute | solution.py:420
  64.3 1.9 %unpack.1 = (bf16[256,512]{1,0:T(8,128)(2,1)}, bf16[256,512]{1,0:T(8,128)(2,1)}, bf16[256,512]{1,0:T(8,128)(2,1)}) custom-call(s32[2]{0:T(128)S(1)} %pad_add_fusion.place_ref, bf16[384,128]{1,0:T(8,128)(2,1)S(1)} %get-tuple-element.47.refs_0_, bf16[384,128]{1,0:T(8,128)(2,1)S(1)} %collective-permute-done.10.refs_1_, ...), custom_call_target="tpu_custom_call" | custom-call | bytes 2097152 | tf_op jit(solution)/shard_map/unpack/pallas_call | solution.py:387
Async XLA Ops:
  0.6 9.5 %collective-permute-start = (bf16[128,1024]{1,0:T(8,128)(2,1)}, bf16[128,1024]{1,0:T(8,128)(2,1)S(1)}, u32[]{:S(2)}, u32[]{:S(2)}) collective-permute-start(bf16[128,1024]{1,0:T(8,128)(2,1)} %refs_0_.1), channel_id=1, source_target_pairs={{0,1},{1,0},{2,3},{3,2},{4,5},{5,4},{6,7},{7,6},{8,9},{9,8},{10,11... | collective-permute-start | bytes 786440 | tf_op jit(solution)/shard_map/ppermute | solution.py:434
  5.9 4.2 %copy-start.1 = (bf16[512,1024]{1,0:T(8,128)(2,1)S(1)}, bf16[512,1024]{1,0:T(8,128)(2,1)}, u32[]{:S(2)}) copy-start(bf16[512,1024]{1,0:T(8,128)(2,1)} %weight_ref.1) | copy-start | bytes 3145732
  5.9 4.2 %copy-start.2 = (bf16[128,1024]{1,0:T(8,128)(2,1)S(1)}, bf16[128,1024]{1,0:T(8,128)(2,1)}, u32[]{:S(2)}) copy-start(bf16[128,1024]{1,0:T(8,128)(2,1)} %refs_0_.1) | copy-start | bytes 786436
  6.0 16.1 %all-to-all-start = ((bf16[8,384,128]{2,1,0:T(8,128)(2,1)}), bf16[8,384,128]{2,1,0:T(8,128)(2,1)S(1)}, u32[]{:S(2)}, u32[]{:S(2)}) async-start(bf16[8,384,128]{2,1,0:T(8,128)(2,1)} %pack_rows.1), calls=%async_computation | async-start | bytes 1572864 | tf_op jit(solution)/shard_map/all_to_all | solution.py:425
  11.7 11.1 %collective-permute-start.2 = (bf16[128,128]{1,0:T(8,128)(2,1)S(1)}, bf16[128,128]{1,0:T(8,128)(2,1)S(1)}, u32[]{:S(2)}, u32[]{:S(2)}) collective-permute-start(bf16[128,128]{1,0:T(8,128)(2,1)S(1)} %get-tuple-element.34), channel_id=1, source_target_pairs={{0,2},{2,0},{4,6},{6,4},{8,10},{10,8},{12,14},{14,12},{16,18},{18,... | collective-permute-start | bytes 98312 | tf_op jit(solution)/shard_map/ppermute | solution.py:420
  12.1 12.3 %collective-permute-start.3 = (bf16[128,128]{1,0:T(8,128)(2,1)S(1)}, bf16[128,128]{1,0:T(8,128)(2,1)S(1)}, u32[]{:S(2)}, u32[]{:S(2)}) collective-permute-start(bf16[128,128]{1,0:T(8,128)(2,1)S(1)} %get-tuple-element.35), channel_id=1, source_target_pairs={{0,4},{2,6},{4,0},{6,2},{8,12},{10,14},{12,8},{14,10},{16,20},{18,... | collective-permute-start | bytes 98312 | tf_op jit(solution)/shard_map/ppermute | solution.py:420
  13.8 10.6 %collective-permute-start.4 = (bf16[128,128]{1,0:T(8,128)(2,1)S(1)}, bf16[128,128]{1,0:T(8,128)(2,1)S(1)}, u32[]{:S(2)}, u32[]{:S(2)}) collective-permute-start(bf16[128,128]{1,0:T(8,128)(2,1)S(1)} %get-tuple-element.36), channel_id=1, source_target_pairs={{0,6},{2,4},{4,2},{6,0},{8,14},{10,12},{12,10},{14,8},{16,22},{18,... | collective-permute-start | bytes 98312 | tf_op jit(solution)/shard_map/ppermute | solution.py:420
  13.8 13.2 %collective-permute-start.5 = (bf16[128,128]{1,0:T(8,128)(2,1)S(1)}, bf16[128,128]{1,0:T(8,128)(2,1)S(1)}, u32[]{:S(2)}, u32[]{:S(2)}) collective-permute-start(bf16[128,128]{1,0:T(8,128)(2,1)S(1)} %get-tuple-element.37), channel_id=1, source_target_pairs={{0,8},{2,10},{4,12},{6,14},{8,0},{10,2},{12,4},{14,6},{16,24},{18,... | collective-permute-start | bytes 98312 | tf_op jit(solution)/shard_map/ppermute | solution.py:420
  15.5 6.6 %copy-start = (s32[16]{0:T(128)S(1)}, s32[16]{0:T(128)}, u32[]{:S(2)}) copy-start(s32[16]{0:T(128)} %offset_ref.7) | copy-start | bytes 196
  15.5 11.6 %collective-permute-start.6 = (bf16[128,128]{1,0:T(8,128)(2,1)S(1)}, bf16[128,128]{1,0:T(8,128)(2,1)S(1)}, u32[]{:S(2)}, u32[]{:S(2)}) collective-permute-start(bf16[128,128]{1,0:T(8,128)(2,1)S(1)} %get-tuple-element.38), channel_id=1, source_target_pairs={{0,10},{2,8},{4,14},{6,12},{8,2},{10,0},{12,6},{14,4},{16,26},{18,... | collective-permute-start | bytes 98312 | tf_op jit(solution)/shard_map/ppermute | solution.py:420
  22.8 4.9 %collective-permute-start.7 = (bf16[128,128]{1,0:T(8,128)(2,1)S(1)}, bf16[128,128]{1,0:T(8,128)(2,1)S(1)}, u32[]{:S(2)}, u32[]{:S(2)}) collective-permute-start(bf16[128,128]{1,0:T(8,128)(2,1)S(1)} %get-tuple-element.39), channel_id=1, source_target_pairs={{0,12},{2,14},{4,8},{6,10},{8,4},{10,6},{12,0},{14,2},{16,28},{18,... | collective-permute-start | bytes 98312 | tf_op jit(solution)/shard_map/ppermute | solution.py:420
  24.4 4.2 %collective-permute-start.8 = (bf16[128,128]{1,0:T(8,128)(2,1)S(1)}, bf16[128,128]{1,0:T(8,128)(2,1)S(1)}, u32[]{:S(2)}, u32[]{:S(2)}) collective-permute-start(bf16[128,128]{1,0:T(8,128)(2,1)S(1)} %get-tuple-element.40), channel_id=1, source_target_pairs={{0,14},{2,12},{4,10},{6,8},{8,6},{10,4},{12,2},{14,0},{16,30},{18,... | collective-permute-start | bytes 98312 | tf_op jit(solution)/shard_map/ppermute | solution.py:420
  24.4 4.9 %collective-permute-start.1 = (bf16[128,128]{1,0:T(8,128)(2,1)S(1)}, bf16[128,128]{1,0:T(8,128)(2,1)S(1)}, u32[]{:S(2)}, u32[]{:S(2)}) collective-permute-start(bf16[128,128]{1,0:T(8,128)(2,1)S(1)} %get-tuple-element.33.picks_ref), channel_id=1, source_target_pairs={{0,16},{2,18},{4,20},{6,22},{8,24},{10,26},{12,28},{14,30},{16,0},... | collective-permute-start | bytes 98312 | tf_op jit(solution)/shard_map/ppermute | solution.py:429
  31.1 10.9 %collective-permute-start.9 = (f32[128,128]{1,0:T(8,128)S(1)}, f32[128,128]{1,0:T(8,128)S(1)}, u32[]{:S(2)}, u32[]{:S(2)}) collective-permute-start(f32[128,128]{1,0:T(8,128)S(1)} %get-tuple-element.46), channel_id=1, source_target_pairs={{0,16},{2,18},{4,20},{6,22},{8,24},{10,26},{12,28},{14,30},{16,0},... | collective-permute-start | bytes 196616 | tf_op jit(solution)/shard_map/ppermute | solution.py:429
  50.7 4.3 %collective-permute-start.10 = (bf16[384,128]{1,0:T(8,128)(2,1)S(1)}, bf16[384,128]{1,0:T(8,128)(2,1)S(1)}, u32[]{:S(2)}, u32[]{:S(2)}) collective-permute-start(bf16[384,128]{1,0:T(8,128)(2,1)S(1)} %get-tuple-element.48), channel_id=1, source_target_pairs={{0,2},{2,0},{4,6},{6,4},{8,10},{10,8},{12,14},{14,12},{16,18},{18,... | collective-permute-start | bytes 294920 | tf_op jit(solution)/shard_map/ppermute | solution.py:420
  50.8 5.6 %collective-permute-start.11 = (bf16[384,128]{1,0:T(8,128)(2,1)S(1)}, bf16[384,128]{1,0:T(8,128)(2,1)S(1)}, u32[]{:S(2)}, u32[]{:S(2)}) collective-permute-start(bf16[384,128]{1,0:T(8,128)(2,1)S(1)} %get-tuple-element.49), channel_id=1, source_target_pairs={{0,4},{2,6},{4,0},{6,2},{8,12},{10,14},{12,8},{14,10},{16,20},{18,... | collective-permute-start | bytes 294920 | tf_op jit(solution)/shard_map/ppermute | solution.py:420
  52.3 5.4 %collective-permute-start.12 = (bf16[384,128]{1,0:T(8,128)(2,1)S(1)}, bf16[384,128]{1,0:T(8,128)(2,1)S(1)}, u32[]{:S(2)}, u32[]{:S(2)}) collective-permute-start(bf16[384,128]{1,0:T(8,128)(2,1)S(1)} %get-tuple-element.50), channel_id=1, source_target_pairs={{0,6},{2,4},{4,2},{6,0},{8,14},{10,12},{12,10},{14,8},{16,22},{18,... | collective-permute-start | bytes 294920 | tf_op jit(solution)/shard_map/ppermute | solution.py:420
  52.7 5.8 %collective-permute-start.13 = (bf16[384,128]{1,0:T(8,128)(2,1)S(1)}, bf16[384,128]{1,0:T(8,128)(2,1)S(1)}, u32[]{:S(2)}, u32[]{:S(2)}) collective-permute-start(bf16[384,128]{1,0:T(8,128)(2,1)S(1)} %get-tuple-element.51), channel_id=1, source_target_pairs={{0,8},{2,10},{4,12},{6,14},{8,0},{10,2},{12,4},{14,6},{16,24},{18,... | collective-permute-start | bytes 294920 | tf_op jit(solution)/shard_map/ppermute | solution.py:420
  55.0 5.2 %collective-permute-start.14 = (bf16[384,128]{1,0:T(8,128)(2,1)S(1)}, bf16[384,128]{1,0:T(8,128)(2,1)S(1)}, u32[]{:S(2)}, u32[]{:S(2)}) collective-permute-start(bf16[384,128]{1,0:T(8,128)(2,1)S(1)} %get-tuple-element.52), channel_id=1, source_target_pairs={{0,10},{2,8},{4,14},{6,12},{8,2},{10,0},{12,6},{14,4},{16,26},{18,... | collective-permute-start | bytes 294920 | tf_op jit(solution)/shard_map/ppermute | solution.py:420
  55.0 8.4 %collective-permute-start.15 = (bf16[384,128]{1,0:T(8,128)(2,1)S(1)}, bf16[384,128]{1,0:T(8,128)(2,1)S(1)}, u32[]{:S(2)}, u32[]{:S(2)}) collective-permute-start(bf16[384,128]{1,0:T(8,128)(2,1)S(1)} %get-tuple-element.53), channel_id=1, source_target_pairs={{0,12},{2,14},{4,8},{6,10},{8,4},{10,6},{12,0},{14,2},{16,28},{18,... | collective-permute-start | bytes 294920 | tf_op jit(solution)/shard_map/ppermute | solution.py:420
  56.5 7.9 %collective-permute-start.16 = (bf16[384,128]{1,0:T(8,128)(2,1)S(1)}, bf16[384,128]{1,0:T(8,128)(2,1)S(1)}, u32[]{:S(2)}, u32[]{:S(2)}) collective-permute-start(bf16[384,128]{1,0:T(8,128)(2,1)S(1)} %get-tuple-element.54), channel_id=1, source_target_pairs={{0,14},{2,12},{4,10},{6,8},{8,6},{10,4},{12,2},{14,0},{16,30},{18,... | collective-permute-start | bytes 294920 | tf_op jit(solution)/shard_map/ppermute | solution.py:420

commit v13 on v7

--- a/solution.py
+++ b/solution.py
@@ -215,10 +215,10 @@
 
 def near_blocks(
     places, offset, keys_ref, key_t_ref, queries_ref, grads_ref, extra_ref,
-    prob_ref, dprob_ref, work_ref, top_ref, acc_ref, emit,
+    work_ref, acc_ref, emit,
 ):
     near = keys_ref.shape[0]
-    rows = prob_ref.shape[2]
+    rows = work_ref.shape[2] // 2
     half = rows // 2
     count = extra_ref.shape[1]
     row_lane = lax.broadcasted_iota(jnp.int32, (1, rows), 1)
@@ -232,12 +232,10 @@
 
     def first_pass(index, weights, start, state):
         top, total, delta = state
-        slot = index % 2
         query, grad = weights
         keys = keys_ref[start : start + PIECE, :]
         scores, dprobs = dot_nt(keys, query), dot_nt(keys, grad)
         for inner in range(0, PIECE, STRIP):
-            strip = slice(start + inner, start + inner + STRIP)
             score, dprob = scores[inner : inner + STRIP], dprobs[inner : inner + STRIP]
             part = fold(score, jnp.maximum) * SCORE_FACTOR
             raised = part if top is None else jnp.maximum(top, part)
@@ -250,21 +248,20 @@
                 shrink = jnp.exp2(top - raised)
                 total, delta = total * shrink + part_total, delta * shrink + part_delta
             top = raised
-            prob_ref[slot, strip, :] = prob.reshape(STRIP, rows)
-            dprob_ref[slot, strip, :] = dprob
-            top_ref[slot, strip.start // STRIP] = raised
         return top, total, delta
 
-    def last_pass(index, lse, delta, both, start, query_grad):
+    def last_pass(index, lse, delta, weights, both, start, query_grad):
         slot = index % 2
         piece = slice(start, start + PIECE)
+        query, grad = weights
+        keys = keys_ref[piece, :]
+        scores, dprobs = dot_nt(keys, query), dot_nt(keys, grad)
         for inner in range(0, PIECE, STRIP):
             strip = slice(start + inner, start + inner + STRIP)
-            factor = jnp.exp2(top_ref[slot, strip.start // STRIP] - lse)
-            prob = by_eight(prob_ref[slot, strip, :]) * factor[None]
-            dscore = prob * (by_eight(dprob_ref[slot, strip, :]) - delta)
-            work_ref[slot, strip, :rows] = dscore.reshape(STRIP, rows).astype(jnp.bfloat16)
-            work_ref[slot, strip, rows:] = prob.reshape(STRIP, rows).astype(jnp.bfloat16)
+            prob = jnp.exp2(scores[inner : inner + STRIP] * SCORE_FACTOR - lse)
+            dscore = prob * (dprobs[inner : inner + STRIP] - delta)
+            work_ref[slot, strip, :rows] = dscore.astype(jnp.bfloat16)
+            work_ref[slot, strip, rows:] = prob.astype(jnp.bfloat16)
         acc_ref[piece, :] += dot_nn(work_ref[slot, piece, :], both)
         return query_grad + dot_nn(key_t_ref[:, piece], work_ref[slot, piece, :rows])
 
@@ -287,12 +284,13 @@
         delta = jnp.where(picked, stats[3] + stats[4] + stats[5], delta)
         both = jnp.concatenate(weights, 0)
         query_grad = extra[:HEAD_SIZE] + extra[HEAD_SIZE:PAIR]
+        now = weights
         weights = None if last else weights_of(index + 1)
         state = (None, None, None)
         for start in starts:
             if not last:
                 state = first_pass(index + 1, weights, start, state)
-            query_grad = last_pass(index, lse, delta, both, start, query_grad)
+            query_grad = last_pass(index, lse, delta, now, both, start, query_grad)
         query_grad = (query_grad * SCALE).T.astype(jnp.bfloat16)
         emit(place, jnp.concatenate([query_grad[:half], query_grad[half:]], 1))
 
@@ -455,10 +453,7 @@
         for shift in range(1, others + 1)
     ]
     steps = group // 2
-    scratch = [
-        ((2, near, rows), f32), ((2, near, rows), f32), ((2, near, 2 * rows), bf16),
-        ((2, near // STRIP, 8, rows), f32),
-    ]
+    scratch = [((2, near, 2 * rows), bf16)]
     half_flops = 10 * near * near // 2 * PAIR
     acc, query_half = call(
         functools.partial(first_kernel, head_count, steps), "first_rows",

time: 65.2 us -> 72.8 us (1.12)
  Pallas kernels: 24 us -> 31.6 us
    pallas_call x7, Pallas kernels: 24 us -> 31.6 us  [call(): pl.pallas_call(kernel, out_shape=tuple((jax.ShapeDtypeStruct(*shape) for...]
  transfers between devices with their start and end apart: 18 -> 18, of which waited for: 11 -> 11; matrix products, arithmetic and copies ran while one was open for 0% -> 0% of each run, Pallas kernels for 19% -> 22%
where the time goes in v13:
time: 72.8 us; the launch traced here: 72.6 us
  Pallas kernels  31.6 us (43%)
  starting transfers between devices  24.2 us (33%)
  waiting for transfers between devices  16 us (22%)
  between operations  0.73 us (1%)
    pallas_call x7, Pallas kernels, call(): pl.pallas_call(kernel, out_shape=tuple((jax.ShapeDtypeStruct(*shape) for...  31.6 us
    ppermute x14, starting transfers between devices, swap(): lax.ppermute(values[bits], 'context', pairs[bits])  11.9 us
    ppermute x14, waiting for transfers between devices, swap(): lax.ppermute(values[bits], 'context', pairs[bits])  8.74 us
    all_to_all x1, waiting for transfers between devices, exchange(): return lax.all_to_all(value, 'context', 0, 0, axis_index_groups=groups)  6.43 us
    ppermute x2, starting transfers between devices, segment_shift(): return lax.ppermute(value, 'context', pairs)  5.35 us
    all_to_all x1, starting transfers between devices, exchange(): return lax.all_to_all(value, 'context', 0, 0, axis_index_groups=groups)  3.95 us
    ppermute x1, starting transfers between devices, body(): upstreams.append(lax.ppermute(upstream, 'heads', pairs))  3 us
  transfers between devices with their start and end apart: 18, of which 11 were waited for; matrix products, arithmetic and copies ran while one was open for 0% of the time, Pallas kernels for 22%

profile of v13, /device:TPU:0, one launch (start us, length us, event | category | flops | bytes accessed | tf_op | source)
XLA Modules:
  0.0 72.6 jit_solution(1390886369778761757)
XLA Ops:
  0.6 3.0 %collective-permute-start = (bf16[128,1024]{1,0:T(8,128)(2,1)}, bf16[128,1024]{1,0:T(8,128)(2,1)S(1)}, u32[]{:S(2)}, u32[]{:S(2)}) collective-permute-start(bf16[128,1024]{1,0:T(8,128)(2,1)} %refs_0_.1), channel_id=1, source_target_pairs={{0,1},{1,0},{2,3},{3,2},{4,5},{5,4},{6,7},{7,6},{8,9},{9,8},{10,11... | collective-permute-start | bytes 786440 | tf_op jit(solution)/shard_map/ppermute | solution.py:413
  3.6 2.3 %pack_rows.1 = bf16[8,384,128]{2,1,0:T(8,128)(2,1)} custom-call(bf16[256,512]{1,0:T(8,128)(2,1)} %query_hbm.1, bf16[256,512]{1,0:T(8,128)(2,1)} %key_hbm.1, bf16[256,512]{1,0:T(8,128)(2,1)} %value_hbm.1), custom_call_target="tpu_custom_call" | custom-call | flops 2147483648 | bytes 2097152 | tf_op jit(solution)/shard_map/pack_rows/pallas_call | solution.py:366
  5.9 0.0 copy-start.1
  5.9 0.0 copy-start.2
  6.0 4.0 %all-to-all-start = ((bf16[8,384,128]{2,1,0:T(8,128)(2,1)}), bf16[8,384,128]{2,1,0:T(8,128)(2,1)S(1)}, u32[]{:S(2)}, u32[]{:S(2)}) async-start(bf16[8,384,128]{2,1,0:T(8,128)(2,1)} %pack_rows.1), calls=%async_computation | async-start | bytes 1572864 | tf_op jit(solution)/shard_map/all_to_all | solution.py:404
  9.9 0.1 pad_add_fusion.place_ref
  10.0 0.2 collective-permute-done.refs_1_
  10.2 0.0 copy-done.1
  10.2 0.0 copy-done.2
  10.2 1.5 %project_pack.1 = (bf16[128,128]{1,0:T(8,128)(2,1)S(1)}, bf16[128,128]{1,0:T(8,128)(2,1)S(1)}, bf16[128,128]{1,0:T(8,128)(2,1)S(1)}, bf16[128,128]{1,0:T(8,128)(...) custom-call(s32[2]{0:T(128)S(1)} %pad_add_fusion.place_ref, ...), custom_call_target="tpu_custom_call" | custom-call | flops 34359738368 | bytes 2097152 | tf_op jit(solution)/shard_map/project_pack/pallas_call | solution.py:366
  11.7 0.4 collective-permute-start.2
  12.1 1.7 %collective-permute-start.3 = (bf16[128,128]{1,0:T(8,128)(2,1)S(1)}, bf16[128,128]{1,0:T(8,128)(2,1)S(1)}, u32[]{:S(2)}, u32[]{:S(2)}) collective-permute-start(bf16[128,128]{1,0:T(8,128)(2,1)S(1)} %get-tuple-element.35), channel_id=1, source_target_pairs={{0,4},{2,6},{4,0},{6,2},{8,12},{10,14},{12,8},{14,10},{16,20},{18,... | collective-permute-start | bytes 98312 | tf_op jit(solution)/shard_map/ppermute | solution.py:399
  13.8 0.0 collective-permute-start.4
  13.8 1.7 %collective-permute-start.5 = (bf16[128,128]{1,0:T(8,128)(2,1)S(1)}, bf16[128,128]{1,0:T(8,128)(2,1)S(1)}, u32[]{:S(2)}, u32[]{:S(2)}) collective-permute-start(bf16[128,128]{1,0:T(8,128)(2,1)S(1)} %get-tuple-element.37), channel_id=1, source_target_pairs={{0,8},{2,10},{4,12},{6,14},{8,0},{10,2},{12,4},{14,6},{16,24},{18,... | collective-permute-start | bytes 98312 | tf_op jit(solution)/shard_map/ppermute | solution.py:399
  15.5 0.0 copy-start
  15.5 0.1 collective-permute-start.6
  15.6 6.4 %all-to-all-done.sent_ref = bf16[8,384,128]{2,1,0:T(8,128)(2,1)S(1)} async-done(((bf16[8,384,128]{2,1,0:T(8,128)(2,1)}), bf16[8,384,128]{2,1,0:T(8,128)(2,1)S(1)}, u32[]{:S(2)}, u32[]{:S(2)}) %all-to-all-start) | async-done | bytes 786464 | tf_op jit(solution)/shard_map/all_to_all | solution.py:404
  22.0 0.0 copy-done
  22.0 0.8 %gather_keys.1 = (bf16[2048,128]{1,0:T(8,128)(2,1)S(1)}, bf16[64,2048]{1,0:T(8,128)(2,1)S(1)}, bf16[8,128,128]{2,1,0:T(8,128)(2,1)S(1)}, bf16[128,128]{1,0:T(8,128)(2,1)S(1)}) custom-call(s32[2]{0:T(128)S(1)} %pad_add_fusion.place_ref, s32[16]{0:T(128)S(1)} %copy-done, bf16[8,384,128]{2,1,0:T(8,128)(2,1)S(1)} %all-to-all-done.sent_ref, ...), custom_call_target="tpu_custom_call" | custom-call | bytes 2097152 | tf_op jit(solution)/shard_map/gather_keys/pallas_call | solution.py:366
  22.8 0.0 collective-permute-done.2.refs_2_
  22.8 1.5 %collective-permute-start.7 = (bf16[128,128]{1,0:T(8,128)(2,1)S(1)}, bf16[128,128]{1,0:T(8,128)(2,1)S(1)}, u32[]{:S(2)}, u32[]{:S(2)}) collective-permute-start(bf16[128,128]{1,0:T(8,128)(2,1)S(1)} %get-tuple-element.39), channel_id=1, source_target_pairs={{0,12},{2,14},{4,8},{6,10},{8,4},{10,6},{12,0},{14,2},{16,28},{18,... | collective-permute-start | bytes 98312 | tf_op jit(solution)/shard_map/ppermute | solution.py:399
  24.4 0.0 collective-permute-done.3.refs_3_
  24.4 0.0 collective-permute-start.8
  24.4 0.0 collective-permute-done.4.refs_4_
  24.4 2.7 %collective-permute-start.1 = (bf16[128,128]{1,0:T(8,128)(2,1)S(1)}, bf16[128,128]{1,0:T(8,128)(2,1)S(1)}, u32[]{:S(2)}, u32[]{:S(2)}) collective-permute-start(bf16[128,128]{1,0:T(8,128)(2,1)S(1)} %get-tuple-element.33.picks_ref), channel_id=1, source_target_pairs={{0,16},{2,18},{4,20},{6,22},{8,24},{10,26},{12,28},{14,30},{16,0},... | collective-permute-start | bytes 98312 | tf_op jit(solution)/shard_map/ppermute | solution.py:408
  27.0 0.0 collective-permute-done.5.refs_5_
  27.0 0.0 collective-permute-done.6.refs_6_
  27.0 0.7 collective-permute-done.7.refs_7_
  27.7 0.9 %collective-permute-done.8.refs_8_ = bf16[128,128]{1,0:T(8,128)(2,1)S(1)} collective-permute-done((bf16[128,128]{1,0:T(8,128)(2,1)S(1)}, bf16[128,128]{1,0:T(8,128)(2,1)S(1)}, u32[]{:S(2)}, u32[]{:S(2)}) %collective-permute-start.8) | collective-permute-done | bytes 32800 | tf_op jit(solution)/shard_map/ppermute | solution.py:399
  28.6 0.6 collective-permute-done.1.refs_0_
  29.3 1.9 %picked_rows.1 = (bf16[144,128]{1,0:T(8,128)(2,1)S(1)}, f32[128,128]{1,0:T(8,128)S(1)}, f32[128,128]{1,0:T(8,128)S(1)}, bf16[8,128,128]{2,1,0:T(8,128)(2,1)S(1)}) custom-call(s32[2]{0:T(128)S(1)} %pad_add_fusion.place_ref, s32[16]{0:T(128)S(1)} %copy-done, bf16[2048,128]{1,0:T(8,128)(2,1)S(1)} %get-tuple-element.30.near_ref.keys_ref, ...), custom_call_target="tpu_custom_call" | custom-call | flops 268435456 | bytes 2097152 | tf_op jit(solution)/shard_map/picked_rows/pallas_call | solution.py:366
  31.1 2.7 %collective-permute-start.9 = (f32[128,128]{1,0:T(8,128)S(1)}, f32[128,128]{1,0:T(8,128)S(1)}, u32[]{:S(2)}, u32[]{:S(2)}) collective-permute-start(f32[128,128]{1,0:T(8,128)S(1)} %get-tuple-element.46), channel_id=1, source_target_pairs={{0,16},{2,18},{4,20},{6,22},{8,24},{10,26},{12,28},{14,30},{16,0},... | collective-permute-start | bytes 196616 | tf_op jit(solution)/shard_map/ppermute | solution.py:408
  33.8 11.6 %first_rows.1 = (f32[2048,128]{1,0:T(8,128)S(1)}, bf16[4,128,128]{2,1,0:T(8,128)(2,1)S(1)}) custom-call(s32[2]{0:T(128)S(1)} %pad_add_fusion.place_ref, s32[16]{0:T(128)S(1)} %copy-done, bf16[2048,128]{1,0:T(8,128)(2,1)S(1)} %get-tuple-element.30.near_ref.keys_ref, bf16[64,2048]{1,0:T(8,128)(2,1)S(1)} %get-tuple-element.31.key_t_ref, ...), custom_call_target="tpu_custom_call" | custom-call | flops 2684354560 | bytes 2097152 | tf_op jit(solution)/shard_map/first_rows/pallas_call | solution.py:366
  45.5 0.0 collective-permute-done.9.refs_0_
  45.5 11.6 %second_rows.1 = (bf16[384,128]{1,0:T(8,128)(2,1)S(1)}, bf16[384,128]{1,0:T(8,128)(2,1)S(1)}, bf16[384,128]{1,0:T(8,128)(2,1)S(1)}, bf16[384,128]{1,0:T(8,128)(2...) custom-call(s32[2]{0:T(128)S(1)} %pad_add_fusion.place_ref, ...), custom_call_target="tpu_custom_call" | custom-call | flops 2684354560 | bytes 2097152 | tf_op jit(solution)/shard_map/second_rows/pallas_call | solution.py:366
  57.1 0.1 collective-permute-start.10
  57.2 1.5 %collective-permute-start.11 = (bf16[384,128]{1,0:T(8,128)(2,1)S(1)}, bf16[384,128]{1,0:T(8,128)(2,1)S(1)}, u32[]{:S(2)}, u32[]{:S(2)}) collective-permute-start(bf16[384,128]{1,0:T(8,128)(2,1)S(1)} %get-tuple-element.49), channel_id=1, source_target_pairs={{0,4},{2,6},{4,0},{6,2},{8,12},{10,14},{12,8},{14,10},{16,20},{18,... | collective-permute-start | bytes 294920 | tf_op jit(solution)/shard_map/ppermute | solution.py:399
  58.7 0.3 collective-permute-start.12
  59.0 2.3 %collective-permute-start.13 = (bf16[384,128]{1,0:T(8,128)(2,1)S(1)}, bf16[384,128]{1,0:T(8,128)(2,1)S(1)}, u32[]{:S(2)}, u32[]{:S(2)}) collective-permute-start(bf16[384,128]{1,0:T(8,128)(2,1)S(1)} %get-tuple-element.51), channel_id=1, source_target_pairs={{0,8},{2,10},{4,12},{6,14},{8,0},{10,2},{12,4},{14,6},{16,24},{18,... | collective-permute-start | bytes 294920 | tf_op jit(solution)/shard_map/ppermute | solution.py:399
  61.3 0.0 collective-permute-start.14
  61.3 0.0 collective-permute-done.10.refs_1_
  61.3 1.2 %collective-permute-start.15 = (bf16[384,128]{1,0:T(8,128)(2,1)S(1)}, bf16[384,128]{1,0:T(8,128)(2,1)S(1)}, u32[]{:S(2)}, u32[]{:S(2)}) collective-permute-start(bf16[384,128]{1,0:T(8,128)(2,1)S(1)} %get-tuple-element.53), channel_id=1, source_target_pairs={{0,12},{2,14},{4,8},{6,10},{8,4},{10,6},{12,0},{14,2},{16,28},{18,... | collective-permute-start | bytes 294920 | tf_op jit(solution)/shard_map/ppermute | solution.py:399
  62.5 0.3 collective-permute-done.11.refs_2_
  62.8 1.0 %collective-permute-start.16 = (bf16[384,128]{1,0:T(8,128)(2,1)S(1)}, bf16[384,128]{1,0:T(8,128)(2,1)S(1)}, u32[]{:S(2)}, u32[]{:S(2)}) collective-permute-start(bf16[384,128]{1,0:T(8,128)(2,1)S(1)} %get-tuple-element.54), channel_id=1, source_target_pairs={{0,14},{2,12},{4,10},{6,8},{8,6},{10,4},{12,2},{14,0},{16,30},{18,... | collective-permute-start | bytes 294920 | tf_op jit(solution)/shard_map/ppermute | solution.py:399
  63.8 0.2 collective-permute-done.12.refs_3_
  64.0 0.8 %collective-permute-done.13.refs_4_ = bf16[384,128]{1,0:T(8,128)(2,1)S(1)} collective-permute-done((bf16[384,128]{1,0:T(8,128)(2,1)S(1)}, bf16[384,128]{1,0:T(8,128)(2,1)S(1)}, u32[]{:S(2)}, u32[]{:S(2)}) %collective-permute-start.13) | collective-permute-done | bytes 98336 | tf_op jit(solution)/shard_map/ppermute | solution.py:399
  64.9 1.7 %collective-permute-done.14.refs_5_ = bf16[384,128]{1,0:T(8,128)(2,1)S(1)} collective-permute-done((bf16[384,128]{1,0:T(8,128)(2,1)S(1)}, bf16[384,128]{1,0:T(8,128)(2,1)S(1)}, u32[]{:S(2)}, u32[]{:S(2)}) %collective-permute-start.14) | collective-permute-done | bytes 98336 | tf_op jit(solution)/shard_map/ppermute | solution.py:399
  66.6 3.2 %collective-permute-done.15.refs_6_ = bf16[384,128]{1,0:T(8,128)(2,1)S(1)} collective-permute-done((bf16[384,128]{1,0:T(8,128)(2,1)S(1)}, bf16[384,128]{1,0:T(8,128)(2,1)S(1)}, u32[]{:S(2)}, u32[]{:S(2)}) %collective-permute-start.15) | collective-permute-done | bytes 98336 | tf_op jit(solution)/shard_map/ppermute | solution.py:399
  69.7 1.0 %collective-permute-done.16.refs_7_ = bf16[384,128]{1,0:T(8,128)(2,1)S(1)} collective-permute-done((bf16[384,128]{1,0:T(8,128)(2,1)S(1)}, bf16[384,128]{1,0:T(8,128)(2,1)S(1)}, u32[]{:S(2)}, u32[]{:S(2)}) %collective-permute-start.16) | collective-permute-done | bytes 98336 | tf_op jit(solution)/shard_map/ppermute | solution.py:399
  70.7 1.9 %unpack.1 = (bf16[256,512]{1,0:T(8,128)(2,1)}, bf16[256,512]{1,0:T(8,128)(2,1)}, bf16[256,512]{1,0:T(8,128)(2,1)}) custom-call(s32[2]{0:T(128)S(1)} %pad_add_fusion.place_ref, bf16[384,128]{1,0:T(8,128)(2,1)S(1)} %get-tuple-element.47.refs_0_, bf16[384,128]{1,0:T(8,128)(2,1)S(1)} %collective-permute-done.10.refs_1_, ...), custom_call_target="tpu_custom_call" | custom-call | bytes 2097152 | tf_op jit(solution)/shard_map/unpack/pallas_call | solution.py:366
Async XLA Ops:
  0.6 9.5 %collective-permute-start = (bf16[128,1024]{1,0:T(8,128)(2,1)}, bf16[128,1024]{1,0:T(8,128)(2,1)S(1)}, u32[]{:S(2)}, u32[]{:S(2)}) collective-permute-start(bf16[128,1024]{1,0:T(8,128)(2,1)} %refs_0_.1), channel_id=1, source_target_pairs={{0,1},{1,0},{2,3},{3,2},{4,5},{5,4},{6,7},{7,6},{8,9},{9,8},{10,11... | collective-permute-start | bytes 786440 | tf_op jit(solution)/shard_map/ppermute | solution.py:413
  5.9 4.2 %copy-start.1 = (bf16[512,1024]{1,0:T(8,128)(2,1)S(1)}, bf16[512,1024]{1,0:T(8,128)(2,1)}, u32[]{:S(2)}) copy-start(bf16[512,1024]{1,0:T(8,128)(2,1)} %weight_ref.1) | copy-start | bytes 3145732
  5.9 4.2 %copy-start.2 = (bf16[128,1024]{1,0:T(8,128)(2,1)S(1)}, bf16[128,1024]{1,0:T(8,128)(2,1)}, u32[]{:S(2)}) copy-start(bf16[128,1024]{1,0:T(8,128)(2,1)} %refs_0_.1) | copy-start | bytes 786436
  6.0 16.1 %all-to-all-start = ((bf16[8,384,128]{2,1,0:T(8,128)(2,1)}), bf16[8,384,128]{2,1,0:T(8,128)(2,1)S(1)}, u32[]{:S(2)}, u32[]{:S(2)}) async-start(bf16[8,384,128]{2,1,0:T(8,128)(2,1)} %pack_rows.1), calls=%async_computation | async-start | bytes 1572864 | tf_op jit(solution)/shard_map/all_to_all | solution.py:404
  11.7 11.1 %collective-permute-start.2 = (bf16[128,128]{1,0:T(8,128)(2,1)S(1)}, bf16[128,128]{1,0:T(8,128)(2,1)S(1)}, u32[]{:S(2)}, u32[]{:S(2)}) collective-permute-start(bf16[128,128]{1,0:T(8,128)(2,1)S(1)} %get-tuple-element.34), channel_id=1, source_target_pairs={{0,2},{2,0},{4,6},{6,4},{8,10},{10,8},{12,14},{14,12},{16,18},{18,... | collective-permute-start | bytes 98312 | tf_op jit(solution)/shard_map/ppermute | solution.py:399
  12.1 12.3 %collective-permute-start.3 = (bf16[128,128]{1,0:T(8,128)(2,1)S(1)}, bf16[128,128]{1,0:T(8,128)(2,1)S(1)}, u32[]{:S(2)}, u32[]{:S(2)}) collective-permute-start(bf16[128,128]{1,0:T(8,128)(2,1)S(1)} %get-tuple-element.35), channel_id=1, source_target_pairs={{0,4},{2,6},{4,0},{6,2},{8,12},{10,14},{12,8},{14,10},{16,20},{18,... | collective-permute-start | bytes 98312 | tf_op jit(solution)/shard_map/ppermute | solution.py:399
  13.8 10.6 %collective-permute-start.4 = (bf16[128,128]{1,0:T(8,128)(2,1)S(1)}, bf16[128,128]{1,0:T(8,128)(2,1)S(1)}, u32[]{:S(2)}, u32[]{:S(2)}) collective-permute-start(bf16[128,128]{1,0:T(8,128)(2,1)S(1)} %get-tuple-element.36), channel_id=1, source_target_pairs={{0,6},{2,4},{4,2},{6,0},{8,14},{10,12},{12,10},{14,8},{16,22},{18,... | collective-permute-start | bytes 98312 | tf_op jit(solution)/shard_map/ppermute | solution.py:399
  13.8 13.2 %collective-permute-start.5 = (bf16[128,128]{1,0:T(8,128)(2,1)S(1)}, bf16[128,128]{1,0:T(8,128)(2,1)S(1)}, u32[]{:S(2)}, u32[]{:S(2)}) collective-permute-start(bf16[128,128]{1,0:T(8,128)(2,1)S(1)} %get-tuple-element.37), channel_id=1, source_target_pairs={{0,8},{2,10},{4,12},{6,14},{8,0},{10,2},{12,4},{14,6},{16,24},{18,... | collective-permute-start | bytes 98312 | tf_op jit(solution)/shard_map/ppermute | solution.py:399
  15.5 6.6 %copy-start = (s32[16]{0:T(128)S(1)}, s32[16]{0:T(128)}, u32[]{:S(2)}) copy-start(s32[16]{0:T(128)} %offset_ref.7) | copy-start | bytes 196
  15.5 11.6 %collective-permute-start.6 = (bf16[128,128]{1,0:T(8,128)(2,1)S(1)}, bf16[128,128]{1,0:T(8,128)(2,1)S(1)}, u32[]{:S(2)}, u32[]{:S(2)}) collective-permute-start(bf16[128,128]{1,0:T(8,128)(2,1)S(1)} %get-tuple-element.38), channel_id=1, source_target_pairs={{0,10},{2,8},{4,14},{6,12},{8,2},{10,0},{12,6},{14,4},{16,26},{18,... | collective-permute-start | bytes 98312 | tf_op jit(solution)/shard_map/ppermute | solution.py:399
  22.8 4.9 %collective-permute-start.7 = (bf16[128,128]{1,0:T(8,128)(2,1)S(1)}, bf16[128,128]{1,0:T(8,128)(2,1)S(1)}, u32[]{:S(2)}, u32[]{:S(2)}) collective-permute-start(bf16[128,128]{1,0:T(8,128)(2,1)S(1)} %get-tuple-element.39), channel_id=1, source_target_pairs={{0,12},{2,14},{4,8},{6,10},{8,4},{10,6},{12,0},{14,2},{16,28},{18,... | collective-permute-start | bytes 98312 | tf_op jit(solution)/shard_map/ppermute | solution.py:399
  24.4 4.2 %collective-permute-start.8 = (bf16[128,128]{1,0:T(8,128)(2,1)S(1)}, bf16[128,128]{1,0:T(8,128)(2,1)S(1)}, u32[]{:S(2)}, u32[]{:S(2)}) collective-permute-start(bf16[128,128]{1,0:T(8,128)(2,1)S(1)} %get-tuple-element.40), channel_id=1, source_target_pairs={{0,14},{2,12},{4,10},{6,8},{8,6},{10,4},{12,2},{14,0},{16,30},{18,... | collective-permute-start | bytes 98312 | tf_op jit(solution)/shard_map/ppermute | solution.py:399
  24.4 4.9 %collective-permute-start.1 = (bf16[128,128]{1,0:T(8,128)(2,1)S(1)}, bf16[128,128]{1,0:T(8,128)(2,1)S(1)}, u32[]{:S(2)}, u32[]{:S(2)}) collective-permute-start(bf16[128,128]{1,0:T(8,128)(2,1)S(1)} %get-tuple-element.33.picks_ref), channel_id=1, source_target_pairs={{0,16},{2,18},{4,20},{6,22},{8,24},{10,26},{12,28},{14,30},{16,0},... | collective-permute-start | bytes 98312 | tf_op jit(solution)/shard_map/ppermute | solution.py:408
  31.1 14.3 %collective-permute-start.9 = (f32[128,128]{1,0:T(8,128)S(1)}, f32[128,128]{1,0:T(8,128)S(1)}, u32[]{:S(2)}, u32[]{:S(2)}) collective-permute-start(f32[128,128]{1,0:T(8,128)S(1)} %get-tuple-element.46), channel_id=1, source_target_pairs={{0,16},{2,18},{4,20},{6,22},{8,24},{10,26},{12,28},{14,30},{16,0},... | collective-permute-start | bytes 196616 | tf_op jit(solution)/shard_map/ppermute | solution.py:408
  57.1 4.3 %collective-permute-start.10 = (bf16[384,128]{1,0:T(8,128)(2,1)S(1)}, bf16[384,128]{1,0:T(8,128)(2,1)S(1)}, u32[]{:S(2)}, u32[]{:S(2)}) collective-permute-start(bf16[384,128]{1,0:T(8,128)(2,1)S(1)} %get-tuple-element.48), channel_id=1, source_target_pairs={{0,2},{2,0},{4,6},{6,4},{8,10},{10,8},{12,14},{14,12},{16,18},{18,... | collective-permute-start | bytes 294920 | tf_op jit(solution)/shard_map/ppermute | solution.py:399
  57.2 5.6 %collective-permute-start.11 = (bf16[384,128]{1,0:T(8,128)(2,1)S(1)}, bf16[384,128]{1,0:T(8,128)(2,1)S(1)}, u32[]{:S(2)}, u32[]{:S(2)}) collective-permute-start(bf16[384,128]{1,0:T(8,128)(2,1)S(1)} %get-tuple-element.49), channel_id=1, source_target_pairs={{0,4},{2,6},{4,0},{6,2},{8,12},{10,14},{12,8},{14,10},{16,20},{18,... | collective-permute-start | bytes 294920 | tf_op jit(solution)/shard_map/ppermute | solution.py:399
  58.7 5.3 %collective-permute-start.12 = (bf16[384,128]{1,0:T(8,128)(2,1)S(1)}, bf16[384,128]{1,0:T(8,128)(2,1)S(1)}, u32[]{:S(2)}, u32[]{:S(2)}) collective-permute-start(bf16[384,128]{1,0:T(8,128)(2,1)S(1)} %get-tuple-element.50), channel_id=1, source_target_pairs={{0,6},{2,4},{4,2},{6,0},{8,14},{10,12},{12,10},{14,8},{16,22},{18,... | collective-permute-start | bytes 294920 | tf_op jit(solution)/shard_map/ppermute | solution.py:399
  59.0 5.8 %collective-permute-start.13 = (bf16[384,128]{1,0:T(8,128)(2,1)S(1)}, bf16[384,128]{1,0:T(8,128)(2,1)S(1)}, u32[]{:S(2)}, u32[]{:S(2)}) collective-permute-start(bf16[384,128]{1,0:T(8,128)(2,1)S(1)} %get-tuple-element.51), channel_id=1, source_target_pairs={{0,8},{2,10},{4,12},{6,14},{8,0},{10,2},{12,4},{14,6},{16,24},{18,... | collective-permute-start | bytes 294920 | tf_op jit(solution)/shard_map/ppermute | solution.py:399
  61.3 5.2 %collective-permute-start.14 = (bf16[384,128]{1,0:T(8,128)(2,1)S(1)}, bf16[384,128]{1,0:T(8,128)(2,1)S(1)}, u32[]{:S(2)}, u32[]{:S(2)}) collective-permute-start(bf16[384,128]{1,0:T(8,128)(2,1)S(1)} %get-tuple-element.52), channel_id=1, source_target_pairs={{0,10},{2,8},{4,14},{6,12},{8,2},{10,0},{12,6},{14,4},{16,26},{18,... | collective-permute-start | bytes 294920 | tf_op jit(solution)/shard_map/ppermute | solution.py:399
  61.3 8.4 %collective-permute-start.15 = (bf16[384,128]{1,0:T(8,128)(2,1)S(1)}, bf16[384,128]{1,0:T(8,128)(2,1)S(1)}, u32[]{:S(2)}, u32[]{:S(2)}) collective-permute-start(bf16[384,128]{1,0:T(8,128)(2,1)S(1)} %get-tuple-element.53), channel_id=1, source_target_pairs={{0,12},{2,14},{4,8},{6,10},{8,4},{10,6},{12,0},{14,2},{16,28},{18,... | collective-permute-start | bytes 294920 | tf_op jit(solution)/shard_map/ppermute | solution.py:399
  62.8 7.9 %collective-permute-start.16 = (bf16[384,128]{1,0:T(8,128)(2,1)S(1)}, bf16[384,128]{1,0:T(8,128)(2,1)S(1)}, u32[]{:S(2)}, u32[]{:S(2)}) collective-permute-start(bf16[384,128]{1,0:T(8,128)(2,1)S(1)} %get-tuple-element.54), channel_id=1, source_target_pairs={{0,14},{2,12},{4,10},{6,8},{8,6},{10,4},{12,2},{14,0},{16,30},{18,... | collective-permute-start | bytes 294920 | tf_op jit(solution)/shard_map/ppermute | solution.py:399

commit v14 on v10

--- a/solution.py
+++ b/solution.py
@@ -16,7 +16,7 @@
 LOG2E = math.log2(math.e)
 SCORE_FACTOR = SCALE * LOG2E
 STRIP = 64
-PIECE = 128
+PIECE = 256
 BUSY = 2**35
 STAT_ROWS = 16
 
@@ -238,14 +238,15 @@
         zero = jnp.zeros((HEAD_SIZE, rows), jnp.bfloat16)
         query = columns_of(queries_ref.at[places[index]])
         grad = columns_of(grads_ref.at[places[index]])
-        return jnp.concatenate([query, zero], 0), jnp.concatenate([zero, grad], 0)
+        return jnp.concatenate(
+            [jnp.concatenate([query, zero], 0), jnp.concatenate([zero, grad], 0)], 1
+        )
 
     def first_pass(index, weights, start, state):
         top, total, delta = state
         slot = index % 2
-        query, grad = weights
-        keys = keys_ref[start : start + PIECE, :]
-        scores, dprobs = dot_nn(keys, query), dot_nn(keys, grad)
+        products = dot_nn(keys_ref[start : start + PIECE, :], weights)
+        scores, dprobs = products[:, :rows], products[:, rows:]
         for inner in range(0, PIECE, STRIP):
             strip = slice(start + inner, start + inner + STRIP)
             score, dprob = scores[inner : inner + STRIP], dprobs[inner : inner + STRIP]

time: 65.7 us -> 65 us (0.989)
  Pallas kernels: 24.5 us -> 23.8 us
    pallas_call x7, Pallas kernels: 24.5 us -> 23.8 us  [call(): pl.pallas_call(kernel, out_shape=tuple((jax.ShapeDtypeStruct(*shape) for...]
where the time goes in v14:
time: 65 us; the launch traced here: 64.8 us
  starting transfers between devices  24.2 us (37%)
  Pallas kernels  23.8 us (37%)
  waiting for transfers between devices  16 us (25%)
  between operations  0.73 us (1%)
    pallas_call x7, Pallas kernels, call(): pl.pallas_call(kernel, out_shape=tuple((jax.ShapeDtypeStruct(*shape) for...  23.8 us
    ppermute x14, starting transfers between devices, swap(): lax.ppermute(values[bits], 'context', pairs[bits])  11.9 us
    ppermute x14, waiting for transfers between devices, swap(): lax.ppermute(values[bits], 'context', pairs[bits])  8.73 us
    all_to_all x1, waiting for transfers between devices, exchange(): return lax.all_to_all(value, 'context', 0, 0, axis_index_groups=groups)  6.43 us
    ppermute x2, starting transfers between devices, segment_shift(): return lax.ppermute(value, 'context', pairs)  5.35 us
    all_to_all x1, starting transfers between devices, exchange(): return lax.all_to_all(value, 'context', 0, 0, axis_index_groups=groups)  3.95 us
    ppermute x1, starting transfers between devices, body(): upstreams.append(lax.ppermute(upstream, 'heads', pairs))  3 us
  transfers between devices with their start and end apart: 18, of which 11 were waited for; matrix products, arithmetic and copies ran while one was open for 0% of the time, Pallas kernels for 19%

profile of v14, /device:TPU:0, one launch (start us, length us, event | category | flops | bytes accessed | tf_op | source)
XLA Modules:
  0.0 64.8 jit_solution(515975707822175038)
XLA Ops:
  0.6 3.0 %collective-permute-start = (bf16[128,1024]{1,0:T(8,128)(2,1)}, bf16[128,1024]{1,0:T(8,128)(2,1)S(1)}, u32[]{:S(2)}, u32[]{:S(2)}) collective-permute-start(bf16[128,1024]{1,0:T(8,128)(2,1)} %refs_0_.1), channel_id=1, source_target_pairs={{0,1},{1,0},{2,3},{3,2},{4,5},{5,4},{6,7},{7,6},{8,9},{9,8},{10,11... | collective-permute-start | bytes 786440 | tf_op jit(solution)/shard_map/ppermute | solution.py:426
  3.6 2.3 %pack_rows.1 = bf16[8,384,128]{2,1,0:T(8,128)(2,1)} custom-call(bf16[256,512]{1,0:T(8,128)(2,1)} %query_hbm.1, bf16[256,512]{1,0:T(8,128)(2,1)} %key_hbm.1, bf16[256,512]{1,0:T(8,128)(2,1)} %value_hbm.1), custom_call_target="tpu_custom_call" | custom-call | flops 2147483648 | bytes 2097152 | tf_op jit(solution)/shard_map/pack_rows/pallas_call | solution.py:379
  5.9 0.0 copy-start.1
  5.9 0.0 copy-start.2
  6.0 4.0 %all-to-all-start = ((bf16[8,384,128]{2,1,0:T(8,128)(2,1)}), bf16[8,384,128]{2,1,0:T(8,128)(2,1)S(1)}, u32[]{:S(2)}, u32[]{:S(2)}) async-start(bf16[8,384,128]{2,1,0:T(8,128)(2,1)} %pack_rows.1), calls=%async_computation | async-start | bytes 1572864 | tf_op jit(solution)/shard_map/all_to_all | solution.py:417
  9.9 0.1 pad_add_fusion.place_ref
  10.0 0.2 collective-permute-done.refs_1_
  10.2 0.0 copy-done.1
  10.2 0.0 copy-done.2
  10.2 1.5 %project_pack.1 = (bf16[128,128]{1,0:T(8,128)(2,1)S(1)}, bf16[128,128]{1,0:T(8,128)(2,1)S(1)}, bf16[128,128]{1,0:T(8,128)(2,1)S(1)}, bf16[128,128]{1,0:T(8,128)(...) custom-call(s32[2]{0:T(128)S(1)} %pad_add_fusion.place_ref, ...), custom_call_target="tpu_custom_call" | custom-call | flops 34359738368 | bytes 2097152 | tf_op jit(solution)/shard_map/project_pack/pallas_call | solution.py:379
  11.7 0.4 collective-permute-start.2
  12.1 1.7 %collective-permute-start.3 = (bf16[128,128]{1,0:T(8,128)(2,1)S(1)}, bf16[128,128]{1,0:T(8,128)(2,1)S(1)}, u32[]{:S(2)}, u32[]{:S(2)}) collective-permute-start(bf16[128,128]{1,0:T(8,128)(2,1)S(1)} %get-tuple-element.35), channel_id=1, source_target_pairs={{0,4},{2,6},{4,0},{6,2},{8,12},{10,14},{12,8},{14,10},{16,20},{18,... | collective-permute-start | bytes 98312 | tf_op jit(solution)/shard_map/ppermute | solution.py:412
  13.8 0.0 collective-permute-start.4
  13.8 1.7 %collective-permute-start.5 = (bf16[128,128]{1,0:T(8,128)(2,1)S(1)}, bf16[128,128]{1,0:T(8,128)(2,1)S(1)}, u32[]{:S(2)}, u32[]{:S(2)}) collective-permute-start(bf16[128,128]{1,0:T(8,128)(2,1)S(1)} %get-tuple-element.37), channel_id=1, source_target_pairs={{0,8},{2,10},{4,12},{6,14},{8,0},{10,2},{12,4},{14,6},{16,24},{18,... | collective-permute-start | bytes 98312 | tf_op jit(solution)/shard_map/ppermute | solution.py:412
  15.5 0.0 copy-start
  15.5 0.1 collective-permute-start.6
  15.6 6.4 %all-to-all-done.sent_ref = bf16[8,384,128]{2,1,0:T(8,128)(2,1)S(1)} async-done(((bf16[8,384,128]{2,1,0:T(8,128)(2,1)}), bf16[8,384,128]{2,1,0:T(8,128)(2,1)S(1)}, u32[]{:S(2)}, u32[]{:S(2)}) %all-to-all-start) | async-done | bytes 786464 | tf_op jit(solution)/shard_map/all_to_all | solution.py:417
  22.0 0.0 copy-done
  22.0 0.8 %gather_keys.1 = (bf16[2048,128]{1,0:T(8,128)(2,1)S(1)}, bf16[64,2048]{1,0:T(8,128)(2,1)S(1)}, bf16[8,128,128]{2,1,0:T(8,128)(2,1)S(1)}, bf16[128,128]{1,0:T(8,128)(2,1)S(1)}) custom-call(s32[2]{0:T(128)S(1)} %pad_add_fusion.place_ref, s32[16]{0:T(128)S(1)} %copy-done, bf16[8,384,128]{2,1,0:T(8,128)(2,1)S(1)} %all-to-all-done.sent_ref, ...), custom_call_target="tpu_custom_call" | custom-call | bytes 2097152 | tf_op jit(solution)/shard_map/gather_keys/pallas_call | solution.py:379
  22.8 0.0 collective-permute-done.2.refs_2_
  22.8 1.5 %collective-permute-start.7 = (bf16[128,128]{1,0:T(8,128)(2,1)S(1)}, bf16[128,128]{1,0:T(8,128)(2,1)S(1)}, u32[]{:S(2)}, u32[]{:S(2)}) collective-permute-start(bf16[128,128]{1,0:T(8,128)(2,1)S(1)} %get-tuple-element.39), channel_id=1, source_target_pairs={{0,12},{2,14},{4,8},{6,10},{8,4},{10,6},{12,0},{14,2},{16,28},{18,... | collective-permute-start | bytes 98312 | tf_op jit(solution)/shard_map/ppermute | solution.py:412
  24.4 0.0 collective-permute-done.3.refs_3_
  24.4 0.0 collective-permute-start.8
  24.4 0.0 collective-permute-done.4.refs_4_
  24.4 2.7 %collective-permute-start.1 = (bf16[128,128]{1,0:T(8,128)(2,1)S(1)}, bf16[128,128]{1,0:T(8,128)(2,1)S(1)}, u32[]{:S(2)}, u32[]{:S(2)}) collective-permute-start(bf16[128,128]{1,0:T(8,128)(2,1)S(1)} %get-tuple-element.33.picks_ref), channel_id=1, source_target_pairs={{0,16},{2,18},{4,20},{6,22},{8,24},{10,26},{12,28},{14,30},{16,0},... | collective-permute-start | bytes 98312 | tf_op jit(solution)/shard_map/ppermute | solution.py:421
  27.0 0.0 collective-permute-done.5.refs_5_
  27.0 0.0 collective-permute-done.6.refs_6_
  27.0 0.7 %collective-permute-done.7.refs_7_ = bf16[128,128]{1,0:T(8,128)(2,1)S(1)} collective-permute-done((bf16[128,128]{1,0:T(8,128)(2,1)S(1)}, bf16[128,128]{1,0:T(8,128)(2,1)S(1)}, u32[]{:S(2)}, u32[]{:S(2)}) %collective-permute-start.7) | collective-permute-done | bytes 32800 | tf_op jit(solution)/shard_map/ppermute | solution.py:412
  27.7 0.9 %collective-permute-done.8.refs_8_ = bf16[128,128]{1,0:T(8,128)(2,1)S(1)} collective-permute-done((bf16[128,128]{1,0:T(8,128)(2,1)S(1)}, bf16[128,128]{1,0:T(8,128)(2,1)S(1)}, u32[]{:S(2)}, u32[]{:S(2)}) %collective-permute-start.8) | collective-permute-done | bytes 32800 | tf_op jit(solution)/shard_map/ppermute | solution.py:412
  28.6 0.6 %collective-permute-done.1.refs_0_ = bf16[128,128]{1,0:T(8,128)(2,1)S(1)} collective-permute-done((bf16[128,128]{1,0:T(8,128)(2,1)S(1)}, bf16[128,128]{1,0:T(8,128)(2,1)S(1)}, u32[]{:S(2)}, u32[]{:S(2)}) %collective-permute-start.1) | collective-permute-done | bytes 32800 | tf_op jit(solution)/shard_map/ppermute | solution.py:421
  29.3 1.9 %picked_rows.1 = (bf16[144,128]{1,0:T(8,128)(2,1)S(1)}, f32[128,128]{1,0:T(8,128)S(1)}, f32[128,128]{1,0:T(8,128)S(1)}, bf16[8,128,128]{2,1,0:T(8,128)(2,1)S(1)}) custom-call(s32[2]{0:T(128)S(1)} %pad_add_fusion.place_ref, s32[16]{0:T(128)S(1)} %copy-done, bf16[2048,128]{1,0:T(8,128)(2,1)S(1)} %get-tuple-element.30.near_ref.keys_ref, ...), custom_call_target="tpu_custom_call" | custom-call | flops 268435456 | bytes 2097152 | tf_op jit(solution)/shard_map/picked_rows/pallas_call | solution.py:379
  31.1 2.7 %collective-permute-start.9 = (f32[128,128]{1,0:T(8,128)S(1)}, f32[128,128]{1,0:T(8,128)S(1)}, u32[]{:S(2)}, u32[]{:S(2)}) collective-permute-start(f32[128,128]{1,0:T(8,128)S(1)} %get-tuple-element.46), channel_id=1, source_target_pairs={{0,16},{2,18},{4,20},{6,22},{8,24},{10,26},{12,28},{14,30},{16,0},... | collective-permute-start | bytes 196616 | tf_op jit(solution)/shard_map/ppermute | solution.py:421
  33.8 7.5 %first_rows.1 = (f32[2048,128]{1,0:T(8,128)S(1)}, bf16[4,128,128]{2,1,0:T(8,128)(2,1)S(1)}) custom-call(s32[2]{0:T(128)S(1)} %pad_add_fusion.place_ref, s32[16]{0:T(128)S(1)} %copy-done, bf16[2048,128]{1,0:T(8,128)(2,1)S(1)} %get-tuple-element.30.near_ref.keys_ref, bf16[64,2048]{1,0:T(8,128)(2,1)S(1)} %get-tuple-element.31.key_t_ref, ...), custom_call_target="tpu_custom_call" | custom-call | flops 2684354560 | bytes 2097152 | tf_op jit(solution)/shard_map/first_rows/pallas_call | solution.py:379
  41.4 0.0 collective-permute-done.9.refs_0_
  41.4 7.9 %second_rows.1 = (bf16[384,128]{1,0:T(8,128)(2,1)S(1)}, bf16[384,128]{1,0:T(8,128)(2,1)S(1)}, bf16[384,128]{1,0:T(8,128)(2,1)S(1)}, bf16[384,128]{1,0:T(8,128)(2...) custom-call(s32[2]{0:T(128)S(1)} %pad_add_fusion.place_ref, ...), custom_call_target="tpu_custom_call" | custom-call | flops 2684354560 | bytes 2097152 | tf_op jit(solution)/shard_map/second_rows/pallas_call | solution.py:379
  49.2 0.1 collective-permute-start.10
  49.3 1.5 %collective-permute-start.11 = (bf16[384,128]{1,0:T(8,128)(2,1)S(1)}, bf16[384,128]{1,0:T(8,128)(2,1)S(1)}, u32[]{:S(2)}, u32[]{:S(2)}) collective-permute-start(bf16[384,128]{1,0:T(8,128)(2,1)S(1)} %get-tuple-element.49), channel_id=1, source_target_pairs={{0,4},{2,6},{4,0},{6,2},{8,12},{10,14},{12,8},{14,10},{16,20},{18,... | collective-permute-start | bytes 294920 | tf_op jit(solution)/shard_map/ppermute | solution.py:412
  50.8 0.4 collective-permute-start.12
  51.2 2.3 %collective-permute-start.13 = (bf16[384,128]{1,0:T(8,128)(2,1)S(1)}, bf16[384,128]{1,0:T(8,128)(2,1)S(1)}, u32[]{:S(2)}, u32[]{:S(2)}) collective-permute-start(bf16[384,128]{1,0:T(8,128)(2,1)S(1)} %get-tuple-element.51), channel_id=1, source_target_pairs={{0,8},{2,10},{4,12},{6,14},{8,0},{10,2},{12,4},{14,6},{16,24},{18,... | collective-permute-start | bytes 294920 | tf_op jit(solution)/shard_map/ppermute | solution.py:412
  53.5 0.0 collective-permute-start.14
  53.5 0.0 collective-permute-done.10.refs_1_
  53.5 1.2 %collective-permute-start.15 = (bf16[384,128]{1,0:T(8,128)(2,1)S(1)}, bf16[384,128]{1,0:T(8,128)(2,1)S(1)}, u32[]{:S(2)}, u32[]{:S(2)}) collective-permute-start(bf16[384,128]{1,0:T(8,128)(2,1)S(1)} %get-tuple-element.53), channel_id=1, source_target_pairs={{0,12},{2,14},{4,8},{6,10},{8,4},{10,6},{12,0},{14,2},{16,28},{18,... | collective-permute-start | bytes 294920 | tf_op jit(solution)/shard_map/ppermute | solution.py:412
  54.7 0.3 collective-permute-done.11.refs_2_
  55.0 1.0 %collective-permute-start.16 = (bf16[384,128]{1,0:T(8,128)(2,1)S(1)}, bf16[384,128]{1,0:T(8,128)(2,1)S(1)}, u32[]{:S(2)}, u32[]{:S(2)}) collective-permute-start(bf16[384,128]{1,0:T(8,128)(2,1)S(1)} %get-tuple-element.54), channel_id=1, source_target_pairs={{0,14},{2,12},{4,10},{6,8},{8,6},{10,4},{12,2},{14,0},{16,30},{18,... | collective-permute-start | bytes 294920 | tf_op jit(solution)/shard_map/ppermute | solution.py:412
  56.0 0.2 collective-permute-done.12.refs_3_
  56.2 0.8 %collective-permute-done.13.refs_4_ = bf16[384,128]{1,0:T(8,128)(2,1)S(1)} collective-permute-done((bf16[384,128]{1,0:T(8,128)(2,1)S(1)}, bf16[384,128]{1,0:T(8,128)(2,1)S(1)}, u32[]{:S(2)}, u32[]{:S(2)}) %collective-permute-start.13) | collective-permute-done | bytes 98336 | tf_op jit(solution)/shard_map/ppermute | solution.py:412
  57.0 1.7 %collective-permute-done.14.refs_5_ = bf16[384,128]{1,0:T(8,128)(2,1)S(1)} collective-permute-done((bf16[384,128]{1,0:T(8,128)(2,1)S(1)}, bf16[384,128]{1,0:T(8,128)(2,1)S(1)}, u32[]{:S(2)}, u32[]{:S(2)}) %collective-permute-start.14) | collective-permute-done | bytes 98336 | tf_op jit(solution)/shard_map/ppermute | solution.py:412
  58.7 3.2 %collective-permute-done.15.refs_6_ = bf16[384,128]{1,0:T(8,128)(2,1)S(1)} collective-permute-done((bf16[384,128]{1,0:T(8,128)(2,1)S(1)}, bf16[384,128]{1,0:T(8,128)(2,1)S(1)}, u32[]{:S(2)}, u32[]{:S(2)}) %collective-permute-start.15) | collective-permute-done | bytes 98336 | tf_op jit(solution)/shard_map/ppermute | solution.py:412
  61.9 1.0 %collective-permute-done.16.refs_7_ = bf16[384,128]{1,0:T(8,128)(2,1)S(1)} collective-permute-done((bf16[384,128]{1,0:T(8,128)(2,1)S(1)}, bf16[384,128]{1,0:T(8,128)(2,1)S(1)}, u32[]{:S(2)}, u32[]{:S(2)}) %collective-permute-start.16) | collective-permute-done | bytes 98336 | tf_op jit(solution)/shard_map/ppermute | solution.py:412
  62.8 1.9 %unpack.1 = (bf16[256,512]{1,0:T(8,128)(2,1)}, bf16[256,512]{1,0:T(8,128)(2,1)}, bf16[256,512]{1,0:T(8,128)(2,1)}) custom-call(s32[2]{0:T(128)S(1)} %pad_add_fusion.place_ref, bf16[384,128]{1,0:T(8,128)(2,1)S(1)} %get-tuple-element.47.refs_0_, bf16[384,128]{1,0:T(8,128)(2,1)S(1)} %collective-permute-done.10.refs_1_, ...), custom_call_target="tpu_custom_call" | custom-call | bytes 2097152 | tf_op jit(solution)/shard_map/unpack/pallas_call | solution.py:379
Async XLA Ops:
  0.6 9.5 %collective-permute-start = (bf16[128,1024]{1,0:T(8,128)(2,1)}, bf16[128,1024]{1,0:T(8,128)(2,1)S(1)}, u32[]{:S(2)}, u32[]{:S(2)}) collective-permute-start(bf16[128,1024]{1,0:T(8,128)(2,1)} %refs_0_.1), channel_id=1, source_target_pairs={{0,1},{1,0},{2,3},{3,2},{4,5},{5,4},{6,7},{7,6},{8,9},{9,8},{10,11... | collective-permute-start | bytes 786440 | tf_op jit(solution)/shard_map/ppermute | solution.py:426
  5.9 4.2 %copy-start.1 = (bf16[512,1024]{1,0:T(8,128)(2,1)S(1)}, bf16[512,1024]{1,0:T(8,128)(2,1)}, u32[]{:S(2)}) copy-start(bf16[512,1024]{1,0:T(8,128)(2,1)} %weight_ref.1) | copy-start | bytes 3145732
  5.9 4.2 %copy-start.2 = (bf16[128,1024]{1,0:T(8,128)(2,1)S(1)}, bf16[128,1024]{1,0:T(8,128)(2,1)}, u32[]{:S(2)}) copy-start(bf16[128,1024]{1,0:T(8,128)(2,1)} %refs_0_.1) | copy-start | bytes 786436
  6.0 16.1 %all-to-all-start = ((bf16[8,384,128]{2,1,0:T(8,128)(2,1)}), bf16[8,384,128]{2,1,0:T(8,128)(2,1)S(1)}, u32[]{:S(2)}, u32[]{:S(2)}) async-start(bf16[8,384,128]{2,1,0:T(8,128)(2,1)} %pack_rows.1), calls=%async_computation | async-start | bytes 1572864 | tf_op jit(solution)/shard_map/all_to_all | solution.py:417
  11.7 11.1 %collective-permute-start.2 = (bf16[128,128]{1,0:T(8,128)(2,1)S(1)}, bf16[128,128]{1,0:T(8,128)(2,1)S(1)}, u32[]{:S(2)}, u32[]{:S(2)}) collective-permute-start(bf16[128,128]{1,0:T(8,128)(2,1)S(1)} %get-tuple-element.34), channel_id=1, source_target_pairs={{0,2},{2,0},{4,6},{6,4},{8,10},{10,8},{12,14},{14,12},{16,18},{18,... | collective-permute-start | bytes 98312 | tf_op jit(solution)/shard_map/ppermute | solution.py:412
  12.1 12.3 %collective-permute-start.3 = (bf16[128,128]{1,0:T(8,128)(2,1)S(1)}, bf16[128,128]{1,0:T(8,128)(2,1)S(1)}, u32[]{:S(2)}, u32[]{:S(2)}) collective-permute-start(bf16[128,128]{1,0:T(8,128)(2,1)S(1)} %get-tuple-element.35), channel_id=1, source_target_pairs={{0,4},{2,6},{4,0},{6,2},{8,12},{10,14},{12,8},{14,10},{16,20},{18,... | collective-permute-start | bytes 98312 | tf_op jit(solution)/shard_map/ppermute | solution.py:412
  13.8 10.6 %collective-permute-start.4 = (bf16[128,128]{1,0:T(8,128)(2,1)S(1)}, bf16[128,128]{1,0:T(8,128)(2,1)S(1)}, u32[]{:S(2)}, u32[]{:S(2)}) collective-permute-start(bf16[128,128]{1,0:T(8,128)(2,1)S(1)} %get-tuple-element.36), channel_id=1, source_target_pairs={{0,6},{2,4},{4,2},{6,0},{8,14},{10,12},{12,10},{14,8},{16,22},{18,... | collective-permute-start | bytes 98312 | tf_op jit(solution)/shard_map/ppermute | solution.py:412
  13.8 13.2 %collective-permute-start.5 = (bf16[128,128]{1,0:T(8,128)(2,1)S(1)}, bf16[128,128]{1,0:T(8,128)(2,1)S(1)}, u32[]{:S(2)}, u32[]{:S(2)}) collective-permute-start(bf16[128,128]{1,0:T(8,128)(2,1)S(1)} %get-tuple-element.37), channel_id=1, source_target_pairs={{0,8},{2,10},{4,12},{6,14},{8,0},{10,2},{12,4},{14,6},{16,24},{18,... | collective-permute-start | bytes 98312 | tf_op jit(solution)/shard_map/ppermute | solution.py:412
  15.5 6.6 %copy-start = (s32[16]{0:T(128)S(1)}, s32[16]{0:T(128)}, u32[]{:S(2)}) copy-start(s32[16]{0:T(128)} %offset_ref.7) | copy-start | bytes 196
  15.5 11.6 %collective-permute-start.6 = (bf16[128,128]{1,0:T(8,128)(2,1)S(1)}, bf16[128,128]{1,0:T(8,128)(2,1)S(1)}, u32[]{:S(2)}, u32[]{:S(2)}) collective-permute-start(bf16[128,128]{1,0:T(8,128)(2,1)S(1)} %get-tuple-element.38), channel_id=1, source_target_pairs={{0,10},{2,8},{4,14},{6,12},{8,2},{10,0},{12,6},{14,4},{16,26},{18,... | collective-permute-start | bytes 98312 | tf_op jit(solution)/shard_map/ppermute | solution.py:412
  22.8 4.9 %collective-permute-start.7 = (bf16[128,128]{1,0:T(8,128)(2,1)S(1)}, bf16[128,128]{1,0:T(8,128)(2,1)S(1)}, u32[]{:S(2)}, u32[]{:S(2)}) collective-permute-start(bf16[128,128]{1,0:T(8,128)(2,1)S(1)} %get-tuple-element.39), channel_id=1, source_target_pairs={{0,12},{2,14},{4,8},{6,10},{8,4},{10,6},{12,0},{14,2},{16,28},{18,... | collective-permute-start | bytes 98312 | tf_op jit(solution)/shard_map/ppermute | solution.py:412
  24.4 4.2 %collective-permute-start.8 = (bf16[128,128]{1,0:T(8,128)(2,1)S(1)}, bf16[128,128]{1,0:T(8,128)(2,1)S(1)}, u32[]{:S(2)}, u32[]{:S(2)}) collective-permute-start(bf16[128,128]{1,0:T(8,128)(2,1)S(1)} %get-tuple-element.40), channel_id=1, source_target_pairs={{0,14},{2,12},{4,10},{6,8},{8,6},{10,4},{12,2},{14,0},{16,30},{18,... | collective-permute-start | bytes 98312 | tf_op jit(solution)/shard_map/ppermute | solution.py:412
  24.4 4.9 %collective-permute-start.1 = (bf16[128,128]{1,0:T(8,128)(2,1)S(1)}, bf16[128,128]{1,0:T(8,128)(2,1)S(1)}, u32[]{:S(2)}, u32[]{:S(2)}) collective-permute-start(bf16[128,128]{1,0:T(8,128)(2,1)S(1)} %get-tuple-element.33.picks_ref), channel_id=1, source_target_pairs={{0,16},{2,18},{4,20},{6,22},{8,24},{10,26},{12,28},{14,30},{16,0},... | collective-permute-start | bytes 98312 | tf_op jit(solution)/shard_map/ppermute | solution.py:421
  31.1 10.2 %collective-permute-start.9 = (f32[128,128]{1,0:T(8,128)S(1)}, f32[128,128]{1,0:T(8,128)S(1)}, u32[]{:S(2)}, u32[]{:S(2)}) collective-permute-start(f32[128,128]{1,0:T(8,128)S(1)} %get-tuple-element.46), channel_id=1, source_target_pairs={{0,16},{2,18},{4,20},{6,22},{8,24},{10,26},{12,28},{14,30},{16,0},... | collective-permute-start | bytes 196616 | tf_op jit(solution)/shard_map/ppermute | solution.py:421
  49.2 4.3 %collective-permute-start.10 = (bf16[384,128]{1,0:T(8,128)(2,1)S(1)}, bf16[384,128]{1,0:T(8,128)(2,1)S(1)}, u32[]{:S(2)}, u32[]{:S(2)}) collective-permute-start(bf16[384,128]{1,0:T(8,128)(2,1)S(1)} %get-tuple-element.48), channel_id=1, source_target_pairs={{0,2},{2,0},{4,6},{6,4},{8,10},{10,8},{12,14},{14,12},{16,18},{18,... | collective-permute-start | bytes 294920 | tf_op jit(solution)/shard_map/ppermute | solution.py:412
  49.3 5.6 %collective-permute-start.11 = (bf16[384,128]{1,0:T(8,128)(2,1)S(1)}, bf16[384,128]{1,0:T(8,128)(2,1)S(1)}, u32[]{:S(2)}, u32[]{:S(2)}) collective-permute-start(bf16[384,128]{1,0:T(8,128)(2,1)S(1)} %get-tuple-element.49), channel_id=1, source_target_pairs={{0,4},{2,6},{4,0},{6,2},{8,12},{10,14},{12,8},{14,10},{16,20},{18,... | collective-permute-start | bytes 294920 | tf_op jit(solution)/shard_map/ppermute | solution.py:412
  50.8 5.4 %collective-permute-start.12 = (bf16[384,128]{1,0:T(8,128)(2,1)S(1)}, bf16[384,128]{1,0:T(8,128)(2,1)S(1)}, u32[]{:S(2)}, u32[]{:S(2)}) collective-permute-start(bf16[384,128]{1,0:T(8,128)(2,1)S(1)} %get-tuple-element.50), channel_id=1, source_target_pairs={{0,6},{2,4},{4,2},{6,0},{8,14},{10,12},{12,10},{14,8},{16,22},{18,... | collective-permute-start | bytes 294920 | tf_op jit(solution)/shard_map/ppermute | solution.py:412
  51.2 5.8 %collective-permute-start.13 = (bf16[384,128]{1,0:T(8,128)(2,1)S(1)}, bf16[384,128]{1,0:T(8,128)(2,1)S(1)}, u32[]{:S(2)}, u32[]{:S(2)}) collective-permute-start(bf16[384,128]{1,0:T(8,128)(2,1)S(1)} %get-tuple-element.51), channel_id=1, source_target_pairs={{0,8},{2,10},{4,12},{6,14},{8,0},{10,2},{12,4},{14,6},{16,24},{18,... | collective-permute-start | bytes 294920 | tf_op jit(solution)/shard_map/ppermute | solution.py:412
  53.5 5.2 %collective-permute-start.14 = (bf16[384,128]{1,0:T(8,128)(2,1)S(1)}, bf16[384,128]{1,0:T(8,128)(2,1)S(1)}, u32[]{:S(2)}, u32[]{:S(2)}) collective-permute-start(bf16[384,128]{1,0:T(8,128)(2,1)S(1)} %get-tuple-element.52), channel_id=1, source_target_pairs={{0,10},{2,8},{4,14},{6,12},{8,2},{10,0},{12,6},{14,4},{16,26},{18,... | collective-permute-start | bytes 294920 | tf_op jit(solution)/shard_map/ppermute | solution.py:412
  53.5 8.4 %collective-permute-start.15 = (bf16[384,128]{1,0:T(8,128)(2,1)S(1)}, bf16[384,128]{1,0:T(8,128)(2,1)S(1)}, u32[]{:S(2)}, u32[]{:S(2)}) collective-permute-start(bf16[384,128]{1,0:T(8,128)(2,1)S(1)} %get-tuple-element.53), channel_id=1, source_target_pairs={{0,12},{2,14},{4,8},{6,10},{8,4},{10,6},{12,0},{14,2},{16,28},{18,... | collective-permute-start | bytes 294920 | tf_op jit(solution)/shard_map/ppermute | solution.py:412
  55.0 7.9 %collective-permute-start.16 = (bf16[384,128]{1,0:T(8,128)(2,1)S(1)}, bf16[384,128]{1,0:T(8,128)(2,1)S(1)}, u32[]{:S(2)}, u32[]{:S(2)}) collective-permute-start(bf16[384,128]{1,0:T(8,128)(2,1)S(1)} %get-tuple-element.54), channel_id=1, source_target_pairs={{0,14},{2,12},{4,10},{6,8},{8,6},{10,4},{12,2},{14,0},{16,30},{18,... | collective-permute-start | bytes 294920 | tf_op jit(solution)/shard_map/ppermute | solution.py:412

commit v15 on v14

v15 whole, which is shorter than its diff:
```python
import functools
import math

import jax
import jax.numpy as jnp
from jax import lax
from jax.experimental import pallas as pl
from jax.experimental.pallas import tpu as pltpu
from jax.sharding import PartitionSpec as P

HEAD_SIZE = 64
PAIR = 2 * HEAD_SIZE
DILATION_RATE = 16
FIRST_SEGMENT = 2048
SCALE = 1.0 / math.sqrt(HEAD_SIZE)
LOG2E = math.log2(math.e)
SCORE_FACTOR = SCALE * LOG2E
STRIP = 64
PIECE = 256
BUSY = 2**35
NEVER = -1e30

SMEM = pl.BlockSpec(memory_space=pltpu.SMEM)
VMEM = pl.BlockSpec(memory_space=pltpu.VMEM)
ANY = pl.BlockSpec(memory_space=pl.ANY)


def dot_nt(left, right):
    return lax.dot_general(
        left, right, (((1,), (1,)), ((), ())), preferred_element_type=jnp.float32
    )


def dot_nn(left, right):
    return jnp.dot(left, right, preferred_element_type=jnp.float32)


def head_columns(ref, head):
    return ref[:, head * HEAD_SIZE : (head + 1) * HEAD_SIZE]


def pick_matrix(offset, picked, rows):
    source = lax.broadcasted_iota(jnp.int32, (picked, rows), 1)
    index = lax.broadcasted_iota(jnp.int32, (picked, rows), 0)
    return (source == index * DILATION_RATE + offset).astype(jnp.bfloat16)


def spread_matrix(offset, first, picked, rows, axis):
    shape = (picked, rows) if axis == 0 else (rows, picked)
    index = lax.broadcasted_iota(jnp.int32, shape, axis)
    source = lax.broadcasted_iota(jnp.int32, shape, 1 - axis)
    return (source == (index - first) * DILATION_RATE + offset).astype(jnp.bfloat16)


def split_two(value):
    high = value.astype(jnp.bfloat16)
    low = (value - high.astype(jnp.float32)).astype(jnp.bfloat16)
    return high, low


def fold(value, combine):
    parts = [value[start : start + 8] for start in range(0, value.shape[0], 8)]
    while len(parts) > 1:
        merged = [combine(parts[i], parts[i + 1]) for i in range(0, len(parts) - 1, 2)]
        parts = merged + parts[len(merged) * 2 :]
    return parts[0]


def left_half(shape):
    return lax.broadcasted_iota(jnp.int32, shape, 1) < HEAD_SIZE


def side_by_side(block):
    half = block.shape[0] // 2
    return jnp.concatenate([block[:half], block[half:]], 1)


def send_out(place, stage_ref, out_refs):
    for bits, out_ref in enumerate(out_refs):
        out_ref[...] = stage_ref[lax.bitwise_xor(place, bits)]


def pack_kernel(head_count, key_hbm, value_hbm, out_ref, key_ref, value_ref, sems):
    copies = [
        pltpu.make_async_copy(source, target, sems.at[index])
        for index, (source, target) in enumerate([(key_hbm, key_ref), (value_hbm, value_ref)])
    ]
    for copy in copies:
        copy.start()
    for copy in copies:
        copy.wait()
    for head in range(head_count):
        pair = jnp.concatenate([head_columns(key_ref, head), head_columns(value_ref, head)], 1)
        for place in range(head, out_ref.shape[0], head_count):
            out_ref[place] = pair


def project_kernel(head_count, group, shards, place_ref, weight_ref, query_ref, *refs):
    upstream_refs, refs = refs[:shards], refs[shards:]
    out_refs, (grad_ref, stage_ref) = refs[:group], refs[group:]
    shard_rows = upstream_refs[0].shape[0]
    for step, upstream_ref in enumerate(upstream_refs):
        owner = lax.rem(place_ref[1] + (shards - step), shards)
        start = pl.multiple_of(owner * shard_rows, shard_rows)
        grad_ref[pl.ds(start, shard_rows), :] = dot_nt(
            upstream_ref[...], weight_ref[...]
        ).astype(jnp.bfloat16)
    for head in range(head_count):
        pair = jnp.concatenate([head_columns(query_ref, head), head_columns(grad_ref, head)], 1)
        for place in range(head, group, head_count):
            stage_ref[place] = pair
    send_out(place_ref[0], stage_ref, out_refs)


def own_offset(head_count, place_ref, offset_ref):
    return offset_ref[place_ref[1] * head_count + lax.rem(place_ref[0], head_count)]


def gather_kernel(
    head_count, group, place_ref, offset_ref, keys_ref, after_ref, key_t_out, picks_out
):
    rows = keys_ref.shape[0] // group
    picked = rows // DILATION_RATE
    pick = pick_matrix(own_offset(head_count, place_ref, offset_ref), picked, rows)
    for place in range(group):
        picks_out[place * picked : (place + 1) * picked, :] = dot_nn(
            pick, keys_ref[place * rows : (place + 1) * rows, :]
        ).astype(jnp.bfloat16)
    key_t_out[...] = keys_ref[...].astype(jnp.float32).T[:HEAD_SIZE].astype(jnp.bfloat16)


def halves(both):
    left = left_half(both.shape)
    zero = jnp.zeros((), both.dtype)
    return jnp.where(left, both, zero), jnp.where(left, zero, both)


def far_kernel(
    head_count, group, others, place_ref, offset_ref, near_ref, start_ref, picks_ref, *refs
):
    other_refs, refs = refs[:others], refs[others:]
    block_refs, refs = refs[:group], refs[group:]
    acc_out, query_out, own_out, other_out, keys_ref, rows_ref = refs
    near = near_ref.shape[0]
    rows = near // group
    picked = rows // DILATION_RATE
    count = group * picked
    far = count * (1 + others)
    pick = pick_matrix(own_offset(head_count, place_ref, offset_ref), picked, rows)
    keys_ref[:near, :] = near_ref[...]
    for index, ref in enumerate([picks_ref, *other_refs]):
        keys_ref[near + index * count : near + (index + 1) * count, :] = ref[...]
    for bits, ref in enumerate(block_refs):
        rows_ref[bits * picked : (bits + 1) * picked, :] = dot_nn(pick, ref[...]).astype(
            jnp.bfloat16
        )
    key_t = keys_ref[...].astype(jnp.float32).T[:HEAD_SIZE].astype(jnp.bfloat16)
    query, grad = halves(rows_ref[...])
    score = dot_nt(keys_ref[...], query)
    dprob = dot_nt(keys_ref[...], grad)
    top = jnp.max(score, 0, keepdims=True)
    prob = jnp.exp2((score - top) * SCORE_FACTOR)
    inverse = 1.0 / jnp.sum(prob, 0, keepdims=True)
    delta = jnp.sum(prob * dprob, 0, keepdims=True) * inverse
    prob = prob * inverse
    dscore = (prob * (dprob - delta)).astype(jnp.bfloat16)
    terms = dot_nn(
        jnp.concatenate([dscore, prob.astype(jnp.bfloat16)], 1), jnp.concatenate([query, grad], 0)
    )
    acc_out[...] = start_ref[...] + terms[:near]
    terms = terms[near:] * jnp.where(left_half((far, PAIR)), SCALE, 1.0)
    own_out[...] = terms[:count]
    other_out[...] = terms[count:]
    query_grad = (dot_nn(key_t, dscore) * SCALE).T.astype(jnp.bfloat16)
    zero = jnp.zeros_like(query_grad)
    query_out[:count, :] = jnp.concatenate([query_grad, zero], 1)
    query_out[count:, :] = jnp.concatenate([zero, query_grad], 1)


def near_blocks(
    offset, keys_ref, key_t_ref, block_refs, prob_ref, dprob_ref, work_ref, top_ref, acc_ref, emit
):
    near = keys_ref.shape[0]
    rows = prob_ref.shape[2]
    half = rows // 2
    row_lane = lax.broadcasted_iota(jnp.int32, (1, rows), 1)
    picked = lax.rem(row_lane, DILATION_RATE) == offset

    def by_eight(value):
        return value.reshape(value.shape[0] // 8, 8, rows)

    def transposed_of(index):
        both = block_refs[index][...].astype(jnp.float32).T.astype(jnp.bfloat16)
        zero = jnp.zeros((HEAD_SIZE, rows), jnp.bfloat16)
        query, grad = both[:HEAD_SIZE], both[HEAD_SIZE:]
        return jnp.concatenate(
            [jnp.concatenate([query, zero], 0), jnp.concatenate([zero, grad], 0)], 1
        )

    def first_pass(index, weights, start, state):
        top, total, delta = state
        slot = index % 2
        products = dot_nn(keys_ref[start : start + PIECE, :], weights)
        scores, dprobs = products[:, :rows], products[:, rows:]
        for inner in range(0, PIECE, STRIP):
            strip = slice(start + inner, start + inner + STRIP)
            score, dprob = scores[inner : inner + STRIP], dprobs[inner : inner + STRIP]
            part = fold(score, jnp.maximum) * SCORE_FACTOR
            raised = part if top is None else jnp.maximum(top, part)
            prob = jnp.exp2(by_eight(score) * SCORE_FACTOR - raised[None])
            part_total = jnp.sum(prob, 0)
            part_delta = jnp.sum(prob * by_eight(dprob), 0)
            if top is None:
                total, delta = part_total, part_delta
            else:
                shrink = jnp.exp2(top - raised)
                total, delta = total * shrink + part_total, delta * shrink + part_delta
            top = raised
            prob_ref[slot, strip, :] = prob.reshape(STRIP, rows)
            dprob_ref[slot, strip, :] = dprob
            top_ref[slot, strip.start // STRIP] = raised
        return top, total, delta

    def last_pass(index, lse, delta, both, start, query_grad):
        slot = index % 2
        piece = slice(start, start + PIECE)
        for inner in range(0, PIECE, STRIP):
            strip = slice(start + inner, start + inner + STRIP)
            factor = jnp.exp2(top_ref[slot, strip.start // STRIP] - lse)
            prob = by_eight(prob_ref[slot, strip, :]) * factor[None]
            dscore = prob * (by_eight(dprob_ref[slot, strip, :]) - delta)
            work_ref[slot, strip, :rows] = dscore.reshape(STRIP, rows).astype(jnp.bfloat16)
            work_ref[slot, strip, rows:] = prob.reshape(STRIP, rows).astype(jnp.bfloat16)
        acc_ref[piece, :] += dot_nn(work_ref[slot, piece, :], both)
        return query_grad + dot_nn(key_t_ref[:, piece], work_ref[slot, piece, :rows])

    starts = range(0, near, PIECE)
    weights = transposed_of(0)
    state = (None, None, None)
    for start in starts:
        state = first_pass(0, weights, start, state)
    for index, block_ref in enumerate(block_refs):
        last = index + 1 == len(block_refs)
        top, total, delta = state
        highest = jnp.max(top, 0, keepdims=True)
        shrink = jnp.exp2(top - highest)
        total = jnp.sum(total * shrink, 0, keepdims=True)
        delta = jnp.sum(delta * shrink, 0, keepdims=True) / total
        lse = jnp.where(picked, -NEVER, highest + jnp.log2(total))
        both = jnp.concatenate(halves(block_ref[...]), 0)
        query_grad = jnp.zeros((HEAD_SIZE, rows), jnp.float32)
        weights = None if last else transposed_of(index + 1)
        state = (None, None, None)
        for start in starts:
            if not last:
                state = first_pass(index + 1, weights, start, state)
            query_grad = last_pass(index, lse, delta, both, start, query_grad)
        query_grad = (query_grad * SCALE).T.astype(jnp.bfloat16)
        emit(index, jnp.concatenate([query_grad[:half], query_grad[half:]], 1))


def some_kernel(head_count, steps, begin, place_ref, offset_ref, keys_ref, key_t_ref, *refs):
    if not begin:
        start_ref, refs = refs[0], refs[1:]
    block_refs, (acc_ref, query_out, *scratch) = refs[:steps], refs[steps:]
    acc_ref[...] = jnp.zeros_like(acc_ref) if begin else start_ref[...]

    def emit(index, query_grad):
        query_out[index] = query_grad

    near_blocks(
        own_offset(head_count, place_ref, offset_ref), keys_ref, key_t_ref, block_refs,
        *scratch, acc_ref, emit,
    )


def end_kernel(
    head_count, steps, others, place_ref, offset_ref, keys_ref, key_t_ref, start_ref, query_ref,
    later_query_ref, picked_query_ref, own_ref, *refs,
):
    back_refs, refs = refs[:others], refs[others:]
    block_refs, refs = refs[:steps], refs[steps:]
    half = query_ref.shape[1]
    rows = 2 * half
    group = keys_ref.shape[0] // rows
    out_refs, refs = refs[:group], refs[group:]
    acc_ref, *scratch = refs
    count = own_ref.shape[0]
    picked = count // group
    offset = own_offset(head_count, place_ref, offset_ref)
    acc_ref[...] = start_ref[...]

    def finish(bits, query_grad):
        spread = spread_matrix(offset, bits * picked, count, rows, 1)
        spread = jnp.concatenate([spread[:half], spread[half:]], 1)
        placed = dot_nn(spread, picked_query_ref[...])
        out_refs[bits][rows:, :] = (query_grad.astype(jnp.float32) + placed).astype(jnp.bfloat16)

    def emit(index, query_grad):
        finish(group - steps + index, query_grad)

    near_blocks(offset, keys_ref, key_t_ref, block_refs, *scratch, acc_ref, emit)
    terms = own_ref[...]
    for back_ref in back_refs:
        terms = terms + back_ref[...]
    terms = jnp.concatenate(split_two(terms), 0)
    factor = jnp.where(left_half((rows, PAIR)), SCALE, 1.0)
    for bits in range(group):
        place = lax.bitwise_xor(place_ref[0], bits)
        spread = spread_matrix(offset, place * picked, count, rows, 1)
        placed = dot_nn(jnp.concatenate([spread, spread], 1), terms)
        acc = acc_ref[pl.ds(pl.multiple_of(place * rows, rows), rows), :]
        out_refs[bits][:rows, :] = (acc * factor + placed).astype(jnp.bfloat16)
        done = query_ref.shape[0]
        if bits < done:
            finish(bits, query_ref[bits])
        elif bits < group - steps:
            finish(bits, later_query_ref[bits - done])


def unpack_kernel(head_count, group, place_ref, *refs):
    near_refs, refs = refs[:group], refs[group:]
    query_out, key_out, value_out, stage_ref = refs
    rows = query_out.shape[0]
    half = rows // 2
    for bits, near_ref in enumerate(near_refs):
        stage_ref[lax.bitwise_xor(place_ref[0], bits)] = near_ref[...]
    for head in range(head_count):
        columns = slice(head * HEAD_SIZE, (head + 1) * HEAD_SIZE)
        key_out[:, columns] = stage_ref[head, :rows, :HEAD_SIZE]
        value_out[:, columns] = stage_ref[head, :rows, HEAD_SIZE:]
        query_out[:half, columns] = stage_ref[head, rows:, :HEAD_SIZE]
        query_out[half:, columns] = stage_ref[head, rows:, HEAD_SIZE:]


def call(kernel, name, out_shape, scalars, operands, scratch=(), flops=0, space=VMEM, limit=40):
    return pl.pallas_call(
        kernel,
        out_shape=tuple(jax.ShapeDtypeStruct(*shape) for shape in out_shape),
        in_specs=[SMEM] * len(scalars) + [space] * len(operands),
        out_specs=tuple(VMEM for _ in out_shape),
        scratch_shapes=[
            pltpu.VMEM(*shape) if isinstance(shape, tuple) else shape for shape in scratch
        ],
        compiler_params=pltpu.CompilerParams(vmem_limit_bytes=limit * 1024 * 1024),
        cost_estimate=pl.CostEstimate(flops=flops, bytes_accessed=2**21, transcendentals=0),
        name=name,
    )(*scalars, *operands)


def body(upstream, out_weight, query_rows, key_rows, value_rows, head_offsets):
    rows, width = query_rows.shape
    head_count = width // HEAD_SIZE
    devices = lax.axis_size("context")
    shards = lax.axis_size("heads")
    group = FIRST_SEGMENT // rows
    others = devices // group - 1
    half = rows // 2
    picked = rows // DILATION_RATE
    count = group * picked
    near = group * rows
    place = jnp.stack(
        [lax.rem(lax.axis_index("context"), group), lax.axis_index("heads")]
    ).astype(jnp.int32)
    scalars = [place, head_offsets]

    def swap(values):
        pairs = [[(source, source ^ bits) for source in range(devices)] for bits in range(group)]
        return [values[0]] + [
            lax.ppermute(values[bits], "context", pairs[bits]) for bits in range(1, group)
        ]

    def exchange(value):
        groups = [list(range(first, first + group)) for first in range(0, devices, group)]
        return lax.all_to_all(value, "context", 0, 0, axis_index_groups=groups)

    def segment_shift(value, shift):
        pairs = [(source, (source + shift * group) % devices) for source in range(devices)]
        return lax.ppermute(value, "context", pairs)

    upstreams = [upstream]
    for step in range(1, shards):
        pairs = [(source, (source + step) % shards) for source in range(shards)]
        upstreams.append(lax.ppermute(upstream, "heads", pairs))

    bf16, f32 = jnp.bfloat16, jnp.float32
    (sent,) = call(
        functools.partial(pack_kernel, head_count), "pack_rows",
        [((group, rows, PAIR), bf16)],
        [], [key_rows, value_rows],
        [((rows, width), bf16)] * 2 + [pltpu.SemaphoreType.DMA((2,))],
        flops=2**31, space=ANY, limit=60,
    )
    groups = [list(range(first, first + group)) for first in range(0, devices, group)]
    sent = lax.all_to_all(sent, "context", 0, 0, axis_index_groups=groups)
    blocks_send = call(
        functools.partial(project_kernel, head_count, group, shards), "project_pack",
        [((rows, PAIR), bf16)] * group,
        [place], [out_weight, query_rows, *upstreams],
        [((rows, width), bf16), ((group, rows, PAIR), bf16)],
        flops=BUSY,
    )
    blocks = swap(blocks_send)
    keys = sent.reshape(near, PAIR)
    key_t, picks = call(
        functools.partial(gather_kernel, head_count, group), "gather_keys",
        [((HEAD_SIZE, near), bf16), ((count, PAIR), bf16)],
        scalars, [keys, blocks_send[0]],
    )
    other_picks = [segment_shift(picks, shift) for shift in range(1, others + 1)]
    steps = group // 2
    scratch = [
        ((2, near, rows), f32), ((2, near, rows), f32), ((2, near, 2 * rows), bf16),
        ((2, near // STRIP, 8, rows), f32),
    ]
    half_flops = 30 * near * near // 2 * PAIR
    early, late = blocks[:steps], blocks[steps:-1]
    acc, query_early = call(
        functools.partial(some_kernel, head_count, len(early), True), "first_rows",
        [((near, PAIR), f32), ((len(early), half, PAIR), bf16)],
        scalars, [keys, key_t, *early], scratch, half_flops,
    )
    acc, picked_query, own_terms, other_terms = call(
        functools.partial(far_kernel, head_count, group, others), "picked_rows",
        [
            ((near, PAIR), f32), ((2 * count, PAIR), bf16), ((count, PAIR), f32),
            ((others * count, PAIR), f32),
        ],
        scalars, [keys, acc, picks, *other_picks, *blocks],
        [((near + count * (1 + others), PAIR), bf16), ((count, PAIR), bf16)],
        flops=20 * near * count * PAIR,
    )
    back = [
        segment_shift(other_terms[(shift - 1) * count : shift * count], -shift)
        for shift in range(1, others + 1)
    ]
    acc, query_late = call(
        functools.partial(some_kernel, head_count, len(late), False), "second_rows",
        [((near, PAIR), f32), ((len(late), half, PAIR), bf16)],
        scalars, [keys, key_t, acc, *late], scratch, half_flops,
    )
    near_send = call(
        functools.partial(end_kernel, head_count, 1, others), "last_rows",
        [((rows + half, PAIR), bf16)] * group,
        scalars,
        [
            keys, key_t, acc, query_early, query_late, picked_query, own_terms, *back, blocks[-1],
        ],
        [((near, PAIR), f32)] + scratch, half_flops // steps,
    )
    return tuple(
        call(
            functools.partial(unpack_kernel, head_count, group), "unpack",
            [((rows, width), bf16)] * 3,
            [place], swap(near_send),
            [((group, rows + half, PAIR), bf16)],
        )
    )


def solution(mesh):
    return jax.shard_map(
        body,
        mesh=mesh,
        in_specs=(
            P(("context", "heads"), None),
            P("heads", None),
            P("context", "heads"),
            P("context", "heads"),
            P("context", "heads"),
            P(),
        ),
        out_specs=(P("context", "heads"), P("context", "heads"), P("context", "heads")),
        check_vma=False,
    )
```

time: 65 us -> 61 us (0.938)
  waiting for transfers between devices: 16 us -> 12.4 us
  starting transfers between devices: 24.2 us -> 21.5 us
  Pallas kernels: 23.8 us -> 25.4 us
  local copies, waits for them, and re-layouts: 0.02 us -> 0.67 us
    all_to_all x1, waiting for transfers between devices: 6.43 us -> 3.55 us  [body(): sent = lax.all_to_all(sent, 'context', 0, 0, axis_index_groups=groups)]
    ppermute x2, starting transfers between devices: 5.35 us -> 3.06 us  [segment_shift(): return lax.ppermute(value, 'context', pairs)]
    pallas_call x7 -> x8, Pallas kernels: 23.8 us -> 25.4 us  [call(): pl.pallas_call(kernel, out_shape=tuple((jax.ShapeDtypeStruct(*shape) for...]
    ppermute x14, waiting for transfers between devices: 8.73 us -> 7.94 us  [swap(): lax.ppermute(values[bits], 'context', pairs[bits])]
    unnamed x6 -> x8, local copies, waits for them, and re-layouts: 0.02 us -> 0.67 us
  transfers between devices with their start and end apart: 18 -> 18, of which waited for: 11 -> 9; matrix products, arithmetic and copies ran while one was open for 0% -> 0% of each run, Pallas kernels for 19% -> 30%
where the time goes in v15:
time: 61 us; the launch traced here: 60.8 us
  Pallas kernels  25.4 us (42%)
  starting transfers between devices  21.5 us (35%)
  waiting for transfers between devices  12.4 us (20%)
  between operations  0.75 us (1%)
  local copies, waits for them, and re-layouts  0.67 us (1%)
    pallas_call x8, Pallas kernels, call(): pl.pallas_call(kernel, out_shape=tuple((jax.ShapeDtypeStruct(*shape) for...  25.4 us
    ppermute x14, starting transfers between devices, swap(): lax.ppermute(values[bits], 'context', pairs[bits])  11.5 us
    ppermute x14, waiting for transfers between devices, swap(): lax.ppermute(values[bits], 'context', pairs[bits])  7.94 us
    all_to_all x1, starting transfers between devices, body(): sent = lax.all_to_all(sent, 'context', 0, 0, axis_index_groups=groups)  3.95 us
    all_to_all x1, waiting for transfers between devices, body(): sent = lax.all_to_all(sent, 'context', 0, 0, axis_index_groups=groups)  3.55 us
    ppermute x2, starting transfers between devices, segment_shift(): return lax.ppermute(value, 'context', pairs)  3.06 us
    ppermute x1, starting transfers between devices, body(): upstreams.append(lax.ppermute(upstream, 'heads', pairs))  3 us
  transfers between devices with their start and end apart: 18, of which 9 were waited for; matrix products, arithmetic and copies ran while one was open for 0% of the time, Pallas kernels for 30%

profile of v15, /device:TPU:0, one launch (start us, length us, event | category | flops | bytes accessed | tf_op | source)
XLA Modules:
  0.0 60.8 jit_solution(18381301064030397480)
XLA Ops:
  0.6 3.0 %collective-permute-start = (bf16[128,1024]{1,0:T(8,128)(2,1)}, bf16[128,1024]{1,0:T(8,128)(2,1)S(1)}, u32[]{:S(2)}, u32[]{:S(2)}) collective-permute-start(bf16[128,1024]{1,0:T(8,128)(2,1)} %refs_0_.1), channel_id=1, source_target_pairs={{0,1},{1,0},{2,3},{3,2},{4,5},{5,4},{6,7},{7,6},{8,9},{9,8},{10,11... | collective-permute-start | bytes 786440 | tf_op jit(solution)/shard_map/ppermute | solution.py:384
  3.6 0.0 copy-start.2
  3.6 0.0 copy-start.3
  3.6 2.1 %pack_rows.1 = bf16[8,256,128]{2,1,0:T(8,128)(2,1)} custom-call(bf16[256,512]{1,0:T(8,128)(2,1)} %key_hbm.1, bf16[256,512]{1,0:T(8,128)(2,1)} %value_hbm.1), custom_call_target="tpu_custom_call" | custom-call | flops 2147483648 | bytes 2097152 | tf_op jit(solution)/shard_map/pack_rows/pallas_call | solution.py:337
  5.8 0.0 copy-start.1
  5.8 4.0 %all-to-all-start = ((bf16[8,256,128]{2,1,0:T(8,128)(2,1)}), bf16[8,256,128]{2,1,0:T(8,128)(2,1)S(1)}, u32[]{:S(2)}, u32[]{:S(2)}) async-start(bf16[8,256,128]{2,1,0:T(8,128)(2,1)} %pack_rows.1), calls=%async_computation | async-start | bytes 1048576 | tf_op jit(solution)/shard_map/all_to_all | solution.py:395
  9.7 0.1 pad_add_fusion.place_ref
  9.8 0.3 collective-permute-done.refs_1_
  10.2 0.0 copy-done.2
  10.2 0.0 copy-done.3
  10.2 0.0 copy-done.1
  10.2 1.5 %project_pack.1 = (bf16[256,128]{1,0:T(8,128)(2,1)S(1)}, bf16[256,128]{1,0:T(8,128)(2,1)S(1)}, bf16[256,128]{1,0:T(8,128)(2,1)S(1)}, bf16[256,128]{1,0:T(8,128)(...) custom-call(s32[2]{0:T(128)S(1)} %pad_add_fusion.place_ref, ...), custom_call_target="tpu_custom_call" | custom-call | flops 34359738368 | bytes 2097152 | tf_op jit(solution)/shard_map/project_pack/pallas_call | solution.py:337
  11.7 0.2 collective-permute-start.1
  11.9 1.7 %collective-permute-start.2 = (bf16[256,128]{1,0:T(8,128)(2,1)S(1)}, bf16[256,128]{1,0:T(8,128)(2,1)S(1)}, u32[]{:S(2)}, u32[]{:S(2)}) collective-permute-start(bf16[256,128]{1,0:T(8,128)(2,1)S(1)} %get-tuple-element.32), channel_id=1, source_target_pairs={{0,4},{2,6},{4,0},{6,2},{8,12},{10,14},{12,8},{14,10},{16,20},{18,... | collective-permute-start | bytes 196616 | tf_op jit(solution)/shard_map/ppermute | solution.py:370
  13.6 0.1 collective-permute-start.3
  13.7 1.8 %collective-permute-start.5 = (bf16[256,128]{1,0:T(8,128)(2,1)S(1)}, bf16[256,128]{1,0:T(8,128)(2,1)S(1)}, u32[]{:S(2)}, u32[]{:S(2)}) collective-permute-start(bf16[256,128]{1,0:T(8,128)(2,1)S(1)} %get-tuple-element.36), channel_id=1, source_target_pairs={{0,8},{2,10},{4,12},{6,14},{8,0},{10,2},{12,4},{14,6},{16,24},{18,... | collective-permute-start | bytes 196616 | tf_op jit(solution)/shard_map/ppermute | solution.py:370
  15.5 0.0 collective-permute-start.6
  15.5 3.6 %all-to-all-done = bf16[8,256,128]{2,1,0:T(8,128)(2,1)S(1)} async-done(((bf16[8,256,128]{2,1,0:T(8,128)(2,1)}), bf16[8,256,128]{2,1,0:T(8,128)(2,1)S(1)}, u32[]{:S(2)}, u32[]{:S(2)}) %all-to-all-start) | async-done | bytes 524320 | tf_op jit(solution)/shard_map/all_to_all | solution.py:395
  19.0 0.0 copy-start
  19.0 0.7 %copy-done = s32[16]{0:T(128)S(1)} copy-done((s32[16]{0:T(128)S(1)}, s32[16]{0:T(128)}, u32[]{:S(2)}) %copy-start) | copy-done | bytes 88
  19.7 0.7 %gather_keys.1 = (bf16[64,2048]{1,0:T(8,128)(2,1)S(1)}, bf16[128,128]{1,0:T(8,128)(2,1)S(1)}) custom-call(s32[2]{0:T(128)S(1)} %pad_add_fusion.place_ref, s32[16]{0:T(128)S(1)} %copy-done, bf16[2048,128]{1,0:T(8,128)(2,1)S(1)} %bitcast.3, bf16[256,128]{1,0:T(8,128)(2,1)S(1)} %get-tuple-element.29.after_ref.refs_0_.refs_1_), custom_call_target="tpu_custom_call" | custom-call | bytes 2097152 | tf_op jit(solution)/shard_map/gather_keys/pallas_call | solution.py:337
  20.4 0.0 collective-permute-done.1.refs_1_.refs_2_
  20.4 1.5 %collective-permute-start.7 = (bf16[256,128]{1,0:T(8,128)(2,1)S(1)}, bf16[256,128]{1,0:T(8,128)(2,1)S(1)}, u32[]{:S(2)}, u32[]{:S(2)}) collective-permute-start(bf16[256,128]{1,0:T(8,128)(2,1)S(1)} %get-tuple-element.38), channel_id=1, source_target_pairs={{0,12},{2,14},{4,8},{6,10},{8,4},{10,6},{12,0},{14,2},{16,28},{18,... | collective-permute-start | bytes 196616 | tf_op jit(solution)/shard_map/ppermute | solution.py:370
  22.0 0.0 collective-permute-done.2.refs_2_.refs_3_
  22.0 0.0 collective-permute-start.8
  22.0 0.0 collective-permute-done.3.refs_3_.refs_4_
  22.0 2.7 %collective-permute-start.4 = (bf16[128,128]{1,0:T(8,128)(2,1)S(1)}, bf16[128,128]{1,0:T(8,128)(2,1)S(1)}, u32[]{:S(2)}, u32[]{:S(2)}) collective-permute-start(bf16[128,128]{1,0:T(8,128)(2,1)S(1)} %get-tuple-element.35.picks_ref), channel_id=1, source_target_pairs={{0,16},{2,18},{4,20},{6,22},{8,24},{10,26},{12,28},{14,30},{16,0},... | collective-permute-start | bytes 98312 | tf_op jit(solution)/shard_map/ppermute | solution.py:379
  24.6 7.6 %first_rows.1 = (f32[2048,128]{1,0:T(8,128)S(1)}, bf16[4,128,128]{2,1,0:T(8,128)(2,1)S(1)}) custom-call(s32[2]{0:T(128)S(1)} %pad_add_fusion.place_ref, s32[16]{0:T(128)S(1)} %copy-done, bf16[2048,128]{1,0:T(8,128)(2,1)S(1)} %bitcast.4, bf16[64,2048]{1,0:T(8,128)(2,1)S(1)} %get-tuple-element.30.key_t_ref, ...), custom_call_target="tpu_custom_call" | custom-call | flops 8053063680 | bytes 2097152 | tf_op jit(solution)/shard_map/first_rows/pallas_call | solution.py:337
  32.2 0.0 collective-permute-done.5.refs_5_.refs_1_
  32.2 0.0 collective-permute-done.6.refs_6_.refs_2_
  32.2 0.0 collective-permute-done.7.refs_7_.refs_3_
  32.2 0.0 collective-permute-done.8.refs_8_.refs_1_
  32.3 0.0 collective-permute-done.4.refs_0_
  32.3 2.5 %picked_rows.1 = (f32[2048,128]{1,0:T(8,128)S(1)}, bf16[256,128]{1,0:T(8,128)(2,1)S(1)}, f32[128,128]{1,0:T(8,128)S(1)}, f32[128,128]{1,0:T(8,128)S(1)}) custom-call(s32[2]{0:T(128)S(1)} %pad_add_fusion.place_ref, s32[16]{0:T(128)S(1)} %copy-done, bf16[2048,128]{1,0:T(8,128)(2,1)S(1)} %bitcast.5, f32[2048,128]{1,0:T(8,128)S(1)} %get-tuple-element.34.start_ref, ...), custom_call_target="tpu_custom_call" | custom-call | flops 671088640 | bytes 2097152 | tf_op jit(solution)/shard_map/picked_rows/pallas_call | solution.py:337
  34.7 0.4 collective-permute-start.9
  35.1 6.1 %second_rows.1 = (f32[2048,128]{1,0:T(8,128)S(1)}, bf16[3,128,128]{2,1,0:T(8,128)(2,1)S(1)}) custom-call(s32[2]{0:T(128)S(1)} %pad_add_fusion.place_ref, s32[16]{0:T(128)S(1)} %copy-done, bf16[2048,128]{1,0:T(8,128)(2,1)S(1)} %bitcast.6, bf16[64,2048]{1,0:T(8,128)(2,1)S(1)} %get-tuple-element.30.key_t_ref, f32[2048,128]{1,0:T(8,128)S(1)} %get-tuple-element.40.refs_0_, ...), custom_call_target="tpu_custom_call" | custom-call | flops 8053063680 | bytes 2097152 | tf_op jit(solution)/shard_map/second_rows/pallas_call | solution.py:337
  41.3 0.6 collective-permute-done.9.refs_0_
  41.8 2.9 %last_rows.1 = (bf16[384,128]{1,0:T(8,128)(2,1)S(1)}, bf16[384,128]{1,0:T(8,128)(2,1)S(1)}, bf16[384,128]{1,0:T(8,128)(2,1)S(1)}, bf16[384,128]{1,0:T(8,128)(2,1...) custom-call(s32[2]{0:T(128)S(1)} %pad_add_fusion.place_ref, ...), custom_call_target="tpu_custom_call" | custom-call | flops 2013265920 | bytes 2097152 | tf_op jit(solution)/shard_map/last_rows/pallas_call | solution.py:337
  44.7 0.5 collective-permute-start.10
  45.2 1.5 %collective-permute-start.11 = (bf16[384,128]{1,0:T(8,128)(2,1)S(1)}, bf16[384,128]{1,0:T(8,128)(2,1)S(1)}, u32[]{:S(2)}, u32[]{:S(2)}) collective-permute-start(bf16[384,128]{1,0:T(8,128)(2,1)S(1)} %get-tuple-element.49), channel_id=1, source_target_pairs={{0,4},{2,6},{4,0},{6,2},{8,12},{10,14},{12,8},{14,10},{16,20},{18,... | collective-permute-start | bytes 294920 | tf_op jit(solution)/shard_map/ppermute | solution.py:370
  46.7 0.0 collective-permute-start.12
  46.7 1.4 %collective-permute-start.13 = (bf16[384,128]{1,0:T(8,128)(2,1)S(1)}, bf16[384,128]{1,0:T(8,128)(2,1)S(1)}, u32[]{:S(2)}, u32[]{:S(2)}) collective-permute-start(bf16[384,128]{1,0:T(8,128)(2,1)S(1)} %get-tuple-element.51), channel_id=1, source_target_pairs={{0,8},{2,10},{4,12},{6,14},{8,0},{10,2},{12,4},{14,6},{16,24},{18,... | collective-permute-start | bytes 294920 | tf_op jit(solution)/shard_map/ppermute | solution.py:370
  48.1 0.6 collective-permute-start.14
  48.7 0.0 collective-permute-done.10.refs_1_
  48.7 1.5 %collective-permute-start.15 = (bf16[384,128]{1,0:T(8,128)(2,1)S(1)}, bf16[384,128]{1,0:T(8,128)(2,1)S(1)}, u32[]{:S(2)}, u32[]{:S(2)}) collective-permute-start(bf16[384,128]{1,0:T(8,128)(2,1)S(1)} %get-tuple-element.53), channel_id=1, source_target_pairs={{0,12},{2,14},{4,8},{6,10},{8,4},{10,6},{12,0},{14,2},{16,28},{18,... | collective-permute-start | bytes 294920 | tf_op jit(solution)/shard_map/ppermute | solution.py:370
  50.2 0.2 collective-permute-done.11.refs_2_
  50.3 0.8 %collective-permute-start.16 = (bf16[384,128]{1,0:T(8,128)(2,1)S(1)}, bf16[384,128]{1,0:T(8,128)(2,1)S(1)}, u32[]{:S(2)}, u32[]{:S(2)}) collective-permute-start(bf16[384,128]{1,0:T(8,128)(2,1)S(1)} %get-tuple-element.54), channel_id=1, source_target_pairs={{0,14},{2,12},{4,10},{6,8},{8,6},{10,4},{12,2},{14,0},{16,30},{18,... | collective-permute-start | bytes 294920 | tf_op jit(solution)/shard_map/ppermute | solution.py:370
  51.1 0.7 %collective-permute-done.12.refs_3_ = bf16[384,128]{1,0:T(8,128)(2,1)S(1)} collective-permute-done((bf16[384,128]{1,0:T(8,128)(2,1)S(1)}, bf16[384,128]{1,0:T(8,128)(2,1)S(1)}, u32[]{:S(2)}, u32[]{:S(2)}) %collective-permute-start.12) | collective-permute-done | bytes 98336 | tf_op jit(solution)/shard_map/ppermute | solution.py:370
  51.8 0.6 collective-permute-done.13.refs_4_
  52.4 1.5 %collective-permute-done.14.refs_5_ = bf16[384,128]{1,0:T(8,128)(2,1)S(1)} collective-permute-done((bf16[384,128]{1,0:T(8,128)(2,1)S(1)}, bf16[384,128]{1,0:T(8,128)(2,1)S(1)}, u32[]{:S(2)}, u32[]{:S(2)}) %collective-permute-start.14) | collective-permute-done | bytes 98336 | tf_op jit(solution)/shard_map/ppermute | solution.py:370
  53.9 3.7 %collective-permute-done.15.refs_6_ = bf16[384,128]{1,0:T(8,128)(2,1)S(1)} collective-permute-done((bf16[384,128]{1,0:T(8,128)(2,1)S(1)}, bf16[384,128]{1,0:T(8,128)(2,1)S(1)}, u32[]{:S(2)}, u32[]{:S(2)}) %collective-permute-start.15) | collective-permute-done | bytes 98336 | tf_op jit(solution)/shard_map/ppermute | solution.py:370
  57.6 1.3 %collective-permute-done.16.refs_7_ = bf16[384,128]{1,0:T(8,128)(2,1)S(1)} collective-permute-done((bf16[384,128]{1,0:T(8,128)(2,1)S(1)}, bf16[384,128]{1,0:T(8,128)(2,1)S(1)}, u32[]{:S(2)}, u32[]{:S(2)}) %collective-permute-start.16) | collective-permute-done | bytes 98336 | tf_op jit(solution)/shard_map/ppermute | solution.py:370
  58.9 1.9 %unpack.1 = (bf16[256,512]{1,0:T(8,128)(2,1)}, bf16[256,512]{1,0:T(8,128)(2,1)}, bf16[256,512]{1,0:T(8,128)(2,1)}) custom-call(s32[2]{0:T(128)S(1)} %pad_add_fusion.place_ref, bf16[384,128]{1,0:T(8,128)(2,1)S(1)} %get-tuple-element.47.refs_0_, bf16[384,128]{1,0:T(8,128)(2,1)S(1)} %collective-permute-done.10.refs_1_, ...), custom_call_target="tpu_custom_call" | custom-call | bytes 2097152 | tf_op jit(solution)/shard_map/unpack/pallas_call | solution.py:337
Async XLA Ops:
  0.6 9.5 %collective-permute-start = (bf16[128,1024]{1,0:T(8,128)(2,1)}, bf16[128,1024]{1,0:T(8,128)(2,1)S(1)}, u32[]{:S(2)}, u32[]{:S(2)}) collective-permute-start(bf16[128,1024]{1,0:T(8,128)(2,1)} %refs_0_.1), channel_id=1, source_target_pairs={{0,1},{1,0},{2,3},{3,2},{4,5},{5,4},{6,7},{7,6},{8,9},{9,8},{10,11... | collective-permute-start | bytes 786440 | tf_op jit(solution)/shard_map/ppermute | solution.py:384
  3.6 6.5 %copy-start.2 = (bf16[256,512]{1,0:T(8,128)(2,1)S(1)}, bf16[256,512]{1,0:T(8,128)(2,1)}, u32[]{:S(2)}) copy-start(bf16[256,512]{1,0:T(8,128)(2,1)} %query_ref.1) | copy-start | bytes 786436
  3.6 6.5 %copy-start.3 = (bf16[128,1024]{1,0:T(8,128)(2,1)S(1)}, bf16[128,1024]{1,0:T(8,128)(2,1)}, u32[]{:S(2)}) copy-start(bf16[128,1024]{1,0:T(8,128)(2,1)} %refs_0_.1) | copy-start | bytes 786436
  5.8 4.4 %copy-start.1 = (bf16[512,1024]{1,0:T(8,128)(2,1)S(1)}, bf16[512,1024]{1,0:T(8,128)(2,1)}, u32[]{:S(2)}) copy-start(bf16[512,1024]{1,0:T(8,128)(2,1)} %weight_ref.1) | copy-start | bytes 3145732
  5.8 13.3 %all-to-all-start = ((bf16[8,256,128]{2,1,0:T(8,128)(2,1)}), bf16[8,256,128]{2,1,0:T(8,128)(2,1)S(1)}, u32[]{:S(2)}, u32[]{:S(2)}) async-start(bf16[8,256,128]{2,1,0:T(8,128)(2,1)} %pack_rows.1), calls=%async_computation | async-start | bytes 1048576 | tf_op jit(solution)/shard_map/all_to_all | solution.py:395
  11.7 8.7 %collective-permute-start.1 = (bf16[256,128]{1,0:T(8,128)(2,1)S(1)}, bf16[256,128]{1,0:T(8,128)(2,1)S(1)}, u32[]{:S(2)}, u32[]{:S(2)}) collective-permute-start(bf16[256,128]{1,0:T(8,128)(2,1)S(1)} %get-tuple-element.31), channel_id=1, source_target_pairs={{0,2},{2,0},{4,6},{6,4},{8,10},{10,8},{12,14},{14,12},{16,18},{18,... | collective-permute-start | bytes 196616 | tf_op jit(solution)/shard_map/ppermute | solution.py:370
  11.9 10.0 %collective-permute-start.2 = (bf16[256,128]{1,0:T(8,128)(2,1)S(1)}, bf16[256,128]{1,0:T(8,128)(2,1)S(1)}, u32[]{:S(2)}, u32[]{:S(2)}) collective-permute-start(bf16[256,128]{1,0:T(8,128)(2,1)S(1)} %get-tuple-element.32), channel_id=1, source_target_pairs={{0,4},{2,6},{4,0},{6,2},{8,12},{10,14},{12,8},{14,10},{16,20},{18,... | collective-permute-start | bytes 196616 | tf_op jit(solution)/shard_map/ppermute | solution.py:370
  13.6 8.4 %collective-permute-start.3 = (bf16[256,128]{1,0:T(8,128)(2,1)S(1)}, bf16[256,128]{1,0:T(8,128)(2,1)S(1)}, u32[]{:S(2)}, u32[]{:S(2)}) collective-permute-start(bf16[256,128]{1,0:T(8,128)(2,1)S(1)} %get-tuple-element.33), channel_id=1, source_target_pairs={{0,6},{2,4},{4,2},{6,0},{8,14},{10,12},{12,10},{14,8},{16,22},{18,... | collective-permute-start | bytes 196616 | tf_op jit(solution)/shard_map/ppermute | solution.py:370
  13.7 18.5 %collective-permute-start.5 = (bf16[256,128]{1,0:T(8,128)(2,1)S(1)}, bf16[256,128]{1,0:T(8,128)(2,1)S(1)}, u32[]{:S(2)}, u32[]{:S(2)}) collective-permute-start(bf16[256,128]{1,0:T(8,128)(2,1)S(1)} %get-tuple-element.36), channel_id=1, source_target_pairs={{0,8},{2,10},{4,12},{6,14},{8,0},{10,2},{12,4},{14,6},{16,24},{18,... | collective-permute-start | bytes 196616 | tf_op jit(solution)/shard_map/ppermute | solution.py:370
  15.5 16.7 %collective-permute-start.6 = (bf16[256,128]{1,0:T(8,128)(2,1)S(1)}, bf16[256,128]{1,0:T(8,128)(2,1)S(1)}, u32[]{:S(2)}, u32[]{:S(2)}) collective-permute-start(bf16[256,128]{1,0:T(8,128)(2,1)S(1)} %get-tuple-element.37), channel_id=1, source_target_pairs={{0,10},{2,8},{4,14},{6,12},{8,2},{10,0},{12,6},{14,4},{16,26},{18,... | collective-permute-start | bytes 196616 | tf_op jit(solution)/shard_map/ppermute | solution.py:370
  19.0 0.7 %copy-start = (s32[16]{0:T(128)S(1)}, s32[16]{0:T(128)}, u32[]{:S(2)}) copy-start(s32[16]{0:T(128)} %offset_ref.9) | copy-start | bytes 196
  20.4 11.8 %collective-permute-start.7 = (bf16[256,128]{1,0:T(8,128)(2,1)S(1)}, bf16[256,128]{1,0:T(8,128)(2,1)S(1)}, u32[]{:S(2)}, u32[]{:S(2)}) collective-permute-start(bf16[256,128]{1,0:T(8,128)(2,1)S(1)} %get-tuple-element.38), channel_id=1, source_target_pairs={{0,12},{2,14},{4,8},{6,10},{8,4},{10,6},{12,0},{14,2},{16,28},{18,... | collective-permute-start | bytes 196616 | tf_op jit(solution)/shard_map/ppermute | solution.py:370
  22.0 10.3 %collective-permute-start.8 = (bf16[256,128]{1,0:T(8,128)(2,1)S(1)}, bf16[256,128]{1,0:T(8,128)(2,1)S(1)}, u32[]{:S(2)}, u32[]{:S(2)}) collective-permute-start(bf16[256,128]{1,0:T(8,128)(2,1)S(1)} %get-tuple-element.39), channel_id=1, source_target_pairs={{0,14},{2,12},{4,10},{6,8},{8,6},{10,4},{12,2},{14,0},{16,30},{18,... | collective-permute-start | bytes 196616 | tf_op jit(solution)/shard_map/ppermute | solution.py:370
  22.0 10.3 %collective-permute-start.4 = (bf16[128,128]{1,0:T(8,128)(2,1)S(1)}, bf16[128,128]{1,0:T(8,128)(2,1)S(1)}, u32[]{:S(2)}, u32[]{:S(2)}) collective-permute-start(bf16[128,128]{1,0:T(8,128)(2,1)S(1)} %get-tuple-element.35.picks_ref), channel_id=1, source_target_pairs={{0,16},{2,18},{4,20},{6,22},{8,24},{10,26},{12,28},{14,30},{16,0},... | collective-permute-start | bytes 98312 | tf_op jit(solution)/shard_map/ppermute | solution.py:379
  34.7 7.1 %collective-permute-start.9 = (f32[128,128]{1,0:T(8,128)S(1)}, f32[128,128]{1,0:T(8,128)S(1)}, u32[]{:S(2)}, u32[]{:S(2)}) collective-permute-start(f32[128,128]{1,0:T(8,128)S(1)} %get-tuple-element.46), channel_id=1, source_target_pairs={{0,16},{2,18},{4,20},{6,22},{8,24},{10,26},{12,28},{14,30},{16,0},... | collective-permute-start | bytes 196616 | tf_op jit(solution)/shard_map/ppermute | solution.py:379
  44.7 4.0 %collective-permute-start.10 = (bf16[384,128]{1,0:T(8,128)(2,1)S(1)}, bf16[384,128]{1,0:T(8,128)(2,1)S(1)}, u32[]{:S(2)}, u32[]{:S(2)}) collective-permute-start(bf16[384,128]{1,0:T(8,128)(2,1)S(1)} %get-tuple-element.48), channel_id=1, source_target_pairs={{0,2},{2,0},{4,6},{6,4},{8,10},{10,8},{12,14},{14,12},{16,18},{18,... | collective-permute-start | bytes 294920 | tf_op jit(solution)/shard_map/ppermute | solution.py:370
  45.2 5.1 %collective-permute-start.11 = (bf16[384,128]{1,0:T(8,128)(2,1)S(1)}, bf16[384,128]{1,0:T(8,128)(2,1)S(1)}, u32[]{:S(2)}, u32[]{:S(2)}) collective-permute-start(bf16[384,128]{1,0:T(8,128)(2,1)S(1)} %get-tuple-element.49), channel_id=1, source_target_pairs={{0,4},{2,6},{4,0},{6,2},{8,12},{10,14},{12,8},{14,10},{16,20},{18,... | collective-permute-start | bytes 294920 | tf_op jit(solution)/shard_map/ppermute | solution.py:370
  46.7 5.1 %collective-permute-start.12 = (bf16[384,128]{1,0:T(8,128)(2,1)S(1)}, bf16[384,128]{1,0:T(8,128)(2,1)S(1)}, u32[]{:S(2)}, u32[]{:S(2)}) collective-permute-start(bf16[384,128]{1,0:T(8,128)(2,1)S(1)} %get-tuple-element.50), channel_id=1, source_target_pairs={{0,6},{2,4},{4,2},{6,0},{8,14},{10,12},{12,10},{14,8},{16,22},{18,... | collective-permute-start | bytes 294920 | tf_op jit(solution)/shard_map/ppermute | solution.py:370
  46.7 5.7 %collective-permute-start.13 = (bf16[384,128]{1,0:T(8,128)(2,1)S(1)}, bf16[384,128]{1,0:T(8,128)(2,1)S(1)}, u32[]{:S(2)}, u32[]{:S(2)}) collective-permute-start(bf16[384,128]{1,0:T(8,128)(2,1)S(1)} %get-tuple-element.51), channel_id=1, source_target_pairs={{0,8},{2,10},{4,12},{6,14},{8,0},{10,2},{12,4},{14,6},{16,24},{18,... | collective-permute-start | bytes 294920 | tf_op jit(solution)/shard_map/ppermute | solution.py:370
  48.1 5.7 %collective-permute-start.14 = (bf16[384,128]{1,0:T(8,128)(2,1)S(1)}, bf16[384,128]{1,0:T(8,128)(2,1)S(1)}, u32[]{:S(2)}, u32[]{:S(2)}) collective-permute-start(bf16[384,128]{1,0:T(8,128)(2,1)S(1)} %get-tuple-element.52), channel_id=1, source_target_pairs={{0,10},{2,8},{4,14},{6,12},{8,2},{10,0},{12,6},{14,4},{16,26},{18,... | collective-permute-start | bytes 294920 | tf_op jit(solution)/shard_map/ppermute | solution.py:370
  48.7 8.9 %collective-permute-start.15 = (bf16[384,128]{1,0:T(8,128)(2,1)S(1)}, bf16[384,128]{1,0:T(8,128)(2,1)S(1)}, u32[]{:S(2)}, u32[]{:S(2)}) collective-permute-start(bf16[384,128]{1,0:T(8,128)(2,1)S(1)} %get-tuple-element.53), channel_id=1, source_target_pairs={{0,12},{2,14},{4,8},{6,10},{8,4},{10,6},{12,0},{14,2},{16,28},{18,... | collective-permute-start | bytes 294920 | tf_op jit(solution)/shard_map/ppermute | solution.py:370
  50.3 8.5 %collective-permute-start.16 = (bf16[384,128]{1,0:T(8,128)(2,1)S(1)}, bf16[384,128]{1,0:T(8,128)(2,1)S(1)}, u32[]{:S(2)}, u32[]{:S(2)}) collective-permute-start(bf16[384,128]{1,0:T(8,128)(2,1)S(1)} %get-tuple-element.54), channel_id=1, source_target_pairs={{0,14},{2,12},{4,10},{6,8},{8,6},{10,4},{12,2},{14,0},{16,30},{18,... | collective-permute-start | bytes 294920 | tf_op jit(solution)/shard_map/ppermute | solution.py:370

commit v16 on v15

--- a/solution.py
+++ b/solution.py
@@ -75,9 +75,26 @@
     return jnp.concatenate([block[:half], block[half:]], 1)
 
 
-def send_out(place, stage_ref, out_refs):
-    for bits, out_ref in enumerate(out_refs):
-        out_ref[...] = stage_ref[lax.bitwise_xor(place, bits)]
+def swap_steps(group):
+    if group == 8:
+        return [(2, 4), (4, 2), (7, 1), (1, 7), (3, 5), (5, 3), (6, 6)]
+    return [(bits, bits) for bits in range(1, group)]
+
+
+def mirrored(step):
+    return (step[1], step[0]) if step[0] % 2 else step
+
+
+def target_of(place, step):
+    return lax.bitwise_xor(place, jnp.where(lax.rem(place, 2) == 1, step[1], step[0]))
+
+
+def targets(place, group):
+    return [place] + [target_of(place, step) for step in swap_steps(group)]
+
+
+def sources(place, group):
+    return [place] + [target_of(place, mirrored(step)) for step in swap_steps(group)]
 
 
 def pack_kernel(head_count, key_hbm, value_hbm, out_ref, key_ref, value_ref, sems):
@@ -109,7 +126,8 @@
         pair = jnp.concatenate([head_columns(query_ref, head), head_columns(grad_ref, head)], 1)
         for place in range(head, group, head_count):
             stage_ref[place] = pair
-    send_out(place_ref[0], stage_ref, out_refs)
+    for place, out_ref in zip(targets(place_ref[0], group), out_refs):
+        out_ref[...] = stage_ref[place]
 
 
 def own_offset(head_count, place_ref, offset_ref):
@@ -305,8 +323,7 @@
         terms = terms + back_ref[...]
     terms = jnp.concatenate(split_two(terms), 0)
     factor = jnp.where(left_half((rows, PAIR)), SCALE, 1.0)
-    for bits in range(group):
-        place = lax.bitwise_xor(place_ref[0], bits)
+    for bits, place in enumerate(sources(place_ref[0], group)):
         spread = spread_matrix(offset, place * picked, count, rows, 1)
         placed = dot_nn(jnp.concatenate([spread, spread], 1), terms)
         acc = acc_ref[pl.ds(pl.multiple_of(place * rows, rows), rows), :]
@@ -323,8 +340,8 @@
     query_out, key_out, value_out, stage_ref = refs
     rows = query_out.shape[0]
     half = rows // 2
-    for bits, near_ref in enumerate(near_refs):
-        stage_ref[lax.bitwise_xor(place_ref[0], bits)] = near_ref[...]
+    for place, near_ref in zip(targets(place_ref[0], group), near_refs):
+        stage_ref[place] = near_ref[...]
     for head in range(head_count):
         columns = slice(head * HEAD_SIZE, (head + 1) * HEAD_SIZE)
         key_out[:, columns] = stage_ref[head, :rows, :HEAD_SIZE]
@@ -364,15 +381,15 @@
     ).astype(jnp.int32)
     scalars = [place, head_offsets]
 
-    def swap(values):
-        pairs = [[(source, source ^ bits) for source in range(devices)] for bits in range(group)]
-        return [values[0]] + [
-            lax.ppermute(values[bits], "context", pairs[bits]) for bits in range(1, group)
-        ]
-
-    def exchange(value):
-        groups = [list(range(first, first + group)) for first in range(0, devices, group)]
-        return lax.all_to_all(value, "context", 0, 0, axis_index_groups=groups)
+    def swap(values, steps):
+        result = [values[0]]
+        for step, value in zip(steps, values[1:]):
+            pairs = [(source, source ^ step[source % 2]) for source in range(devices)]
+            result.append(lax.ppermute(value, "context", pairs))
+        return result
+
+    out_steps = swap_steps(group)
+    back_steps = [mirrored(step) for step in out_steps]
 
     def segment_shift(value, shift):
         pairs = [(source, (source + shift * group) % devices) for source in range(devices)]
@@ -400,7 +417,7 @@
         [((rows, width), bf16), ((group, rows, PAIR), bf16)],
         flops=BUSY,
     )
-    blocks = swap(blocks_send)
+    blocks = swap(blocks_send, out_steps)
     keys = sent.reshape(near, PAIR)
     key_t, picks = call(
         functools.partial(gather_kernel, head_count, group), "gather_keys",
@@ -452,7 +469,7 @@
         call(
             functools.partial(unpack_kernel, head_count, group), "unpack",
             [((rows, width), bf16)] * 3,
-            [place], swap(near_send),
+            [place], swap(near_send, back_steps),
             [((group, rows + half, PAIR), bf16)],
         )
     )

time: 61 us -> 60.2 us (0.987)
  waiting for transfers between devices: 12.4 us -> 9.15 us
  starting transfers between devices: 21.5 us -> 23.9 us
    ppermute x14, starting transfers between devices: 11.5 us -> 14 us  [swap(): result.append(lax.ppermute(value, 'context', pairs))]
    all_to_all x1, waiting for transfers between devices: 3.55 us -> 1.72 us  [body(): sent = lax.all_to_all(sent, 'context', 0, 0, axis_index_groups=groups)]
    ppermute x14, waiting for transfers between devices: 7.94 us -> 7.01 us  [swap(): result.append(lax.ppermute(value, 'context', pairs))]
  transfers between devices with their start and end apart: 18 -> 18, of which waited for: 9 -> 8; matrix products, arithmetic and copies ran while one was open for 0% -> 0% of each run, Pallas kernels for 30% -> 30%
where the time goes in v16:
time: 60.2 us; the launch traced here: 59.9 us
  Pallas kernels  25.4 us (42%)
  starting transfers between devices  23.9 us (40%)
  waiting for transfers between devices  9.15 us (15%)
  between operations  0.76 us (1%)
  local copies, waits for them, and re-layouts  0.67 us (1%)
    pallas_call x8, Pallas kernels, call(): pl.pallas_call(kernel, out_shape=tuple((jax.ShapeDtypeStruct(*shape) for...  25.4 us
    ppermute x14, starting transfers between devices, swap(): result.append(lax.ppermute(value, 'context', pairs))  14 us
    ppermute x14, waiting for transfers between devices, swap(): result.append(lax.ppermute(value, 'context', pairs))  7.01 us
    all_to_all x1, starting transfers between devices, body(): sent = lax.all_to_all(sent, 'context', 0, 0, axis_index_groups=groups)  3.95 us
    ppermute x1, starting transfers between devices, body(): upstreams.append(lax.ppermute(upstream, 'heads', pairs))  3 us
    ppermute x2, starting transfers between devices, segment_shift(): return lax.ppermute(value, 'context', pairs)  3 us
    all_to_all x1, waiting for transfers between devices, body(): sent = lax.all_to_all(sent, 'context', 0, 0, axis_index_groups=groups)  1.72 us
  transfers between devices with their start and end apart: 18, of which 8 were waited for; matrix products, arithmetic and copies ran while one was open for 0% of the time, Pallas kernels for 30%

profile of v16, /device:TPU:0, one launch (start us, length us, event | category | flops | bytes accessed | tf_op | source)
XLA Modules:
  0.0 59.9 jit_solution(4623317938929436066)
XLA Ops:
  0.6 3.0 %collective-permute-start = (bf16[128,1024]{1,0:T(8,128)(2,1)}, bf16[128,1024]{1,0:T(8,128)(2,1)S(1)}, u32[]{:S(2)}, u32[]{:S(2)}) collective-permute-start(bf16[128,1024]{1,0:T(8,128)(2,1)} %refs_0_.1), channel_id=1, source_target_pairs={{0,1},{1,0},{2,3},{3,2},{4,5},{5,4},{6,7},{7,6},{8,9},{9,8},{10,11... | collective-permute-start | bytes 786440 | tf_op jit(solution)/shard_map/ppermute | solution.py:401
  3.6 0.0 copy-start.2
  3.6 0.0 copy-start.3
  3.6 2.1 %pack_rows.1 = bf16[8,256,128]{2,1,0:T(8,128)(2,1)} custom-call(bf16[256,512]{1,0:T(8,128)(2,1)} %key_hbm.1, bf16[256,512]{1,0:T(8,128)(2,1)} %value_hbm.1), custom_call_target="tpu_custom_call" | custom-call | flops 2147483648 | bytes 2097152 | tf_op jit(solution)/shard_map/pack_rows/pallas_call | solution.py:354
  5.8 0.0 copy-start.1
  5.8 4.0 %all-to-all-start = ((bf16[8,256,128]{2,1,0:T(8,128)(2,1)}), bf16[8,256,128]{2,1,0:T(8,128)(2,1)S(1)}, u32[]{:S(2)}, u32[]{:S(2)}) async-start(bf16[8,256,128]{2,1,0:T(8,128)(2,1)} %pack_rows.1), calls=%async_computation | async-start | bytes 1048576 | tf_op jit(solution)/shard_map/all_to_all | solution.py:412
  9.7 0.1 pad_add_fusion.place_ref
  9.8 0.3 collective-permute-done.refs_1_
  10.2 0.0 copy-done.2
  10.2 0.0 copy-done.3
  10.2 0.0 copy-done.1
  10.2 1.5 %project_pack.1 = (bf16[256,128]{1,0:T(8,128)(2,1)S(1)}, bf16[256,128]{1,0:T(8,128)(2,1)S(1)}, bf16[256,128]{1,0:T(8,128)(2,1)S(1)}, bf16[256,128]{1,0:T(8,128)(...) custom-call(s32[2]{0:T(128)S(1)} %pad_add_fusion.place_ref, ...), custom_call_target="tpu_custom_call" | custom-call | flops 34359738368 | bytes 2097152 | tf_op jit(solution)/shard_map/project_pack/pallas_call | solution.py:354
  11.7 1.8 %collective-permute-start.1 = (bf16[256,128]{1,0:T(8,128)(2,1)S(1)}, bf16[256,128]{1,0:T(8,128)(2,1)S(1)}, u32[]{:S(2)}, u32[]{:S(2)}) collective-permute-start(bf16[256,128]{1,0:T(8,128)(2,1)S(1)} %get-tuple-element.31), channel_id=1, source_target_pairs={{0,4},{2,10},{4,0},{6,14},{8,12},{10,2},{12,8},{14,6},{16,20},{18,... | collective-permute-start | bytes 196616 | tf_op jit(solution)/shard_map/ppermute | solution.py:388
  13.5 1.6 %collective-permute-start.2 = (bf16[256,128]{1,0:T(8,128)(2,1)S(1)}, bf16[256,128]{1,0:T(8,128)(2,1)S(1)}, u32[]{:S(2)}, u32[]{:S(2)}) collective-permute-start(bf16[256,128]{1,0:T(8,128)(2,1)S(1)} %get-tuple-element.32), channel_id=1, source_target_pairs={{0,8},{2,6},{4,12},{6,2},{8,0},{10,14},{12,4},{14,10},{16,24},{18,... | collective-permute-start | bytes 196616 | tf_op jit(solution)/shard_map/ppermute | solution.py:388
  15.1 0.0 collective-permute-start.3
  15.1 0.5 collective-permute-start.5
  15.6 1.7 %collective-permute-start.6 = (bf16[256,128]{1,0:T(8,128)(2,1)S(1)}, bf16[256,128]{1,0:T(8,128)(2,1)S(1)}, u32[]{:S(2)}, u32[]{:S(2)}) collective-permute-start(bf16[256,128]{1,0:T(8,128)(2,1)S(1)} %get-tuple-element.37), channel_id=1, source_target_pairs={{0,6},{2,8},{4,2},{6,12},{8,14},{10,0},{12,10},{14,4},{16,22},{18,... | collective-permute-start | bytes 196616 | tf_op jit(solution)/shard_map/ppermute | solution.py:388
  17.3 1.7 %all-to-all-done = bf16[8,256,128]{2,1,0:T(8,128)(2,1)S(1)} async-done(((bf16[8,256,128]{2,1,0:T(8,128)(2,1)}), bf16[8,256,128]{2,1,0:T(8,128)(2,1)S(1)}, u32[]{:S(2)}, u32[]{:S(2)}) %all-to-all-start) | async-done | bytes 524320 | tf_op jit(solution)/shard_map/all_to_all | solution.py:412
  19.0 0.0 copy-start
  19.0 0.7 %copy-done = s32[16]{0:T(128)S(1)} copy-done((s32[16]{0:T(128)S(1)}, s32[16]{0:T(128)}, u32[]{:S(2)}) %copy-start) | copy-done | bytes 88
  19.7 0.7 %gather_keys.1 = (bf16[64,2048]{1,0:T(8,128)(2,1)S(1)}, bf16[128,128]{1,0:T(8,128)(2,1)S(1)}) custom-call(s32[2]{0:T(128)S(1)} %pad_add_fusion.place_ref, s32[16]{0:T(128)S(1)} %copy-done, bf16[2048,128]{1,0:T(8,128)(2,1)S(1)} %bitcast.3, bf16[256,128]{1,0:T(8,128)(2,1)S(1)} %get-tuple-element.29.after_ref.refs_0_.refs_1_), custom_call_target="tpu_custom_call" | custom-call | bytes 2097152 | tf_op jit(solution)/shard_map/gather_keys/pallas_call | solution.py:354
  20.4 0.0 collective-permute-done.1.refs_1_.refs_2_
  20.4 0.1 collective-permute-start.7
  20.5 0.0 collective-permute-done.2.refs_2_.refs_3_
  20.5 2.2 %collective-permute-start.8 = (bf16[256,128]{1,0:T(8,128)(2,1)S(1)}, bf16[256,128]{1,0:T(8,128)(2,1)S(1)}, u32[]{:S(2)}, u32[]{:S(2)}) collective-permute-start(bf16[256,128]{1,0:T(8,128)(2,1)S(1)} %get-tuple-element.39), channel_id=1, source_target_pairs={{0,12},{2,14},{4,8},{6,10},{8,4},{10,6},{12,0},{14,2},{16,28},{18,... | collective-permute-start | bytes 196616 | tf_op jit(solution)/shard_map/ppermute | solution.py:388
  22.8 0.0 collective-permute-done.3.refs_3_.refs_4_
  22.8 2.6 %collective-permute-start.4 = (bf16[128,128]{1,0:T(8,128)(2,1)S(1)}, bf16[128,128]{1,0:T(8,128)(2,1)S(1)}, u32[]{:S(2)}, u32[]{:S(2)}) collective-permute-start(bf16[128,128]{1,0:T(8,128)(2,1)S(1)} %get-tuple-element.35.picks_ref), channel_id=1, source_target_pairs={{0,16},{2,18},{4,20},{6,22},{8,24},{10,26},{12,28},{14,30},{16,0},... | collective-permute-start | bytes 98312 | tf_op jit(solution)/shard_map/ppermute | solution.py:396
  25.4 7.6 %first_rows.1 = (f32[2048,128]{1,0:T(8,128)S(1)}, bf16[4,128,128]{2,1,0:T(8,128)(2,1)S(1)}) custom-call(s32[2]{0:T(128)S(1)} %pad_add_fusion.place_ref, s32[16]{0:T(128)S(1)} %copy-done, bf16[2048,128]{1,0:T(8,128)(2,1)S(1)} %bitcast.4, bf16[64,2048]{1,0:T(8,128)(2,1)S(1)} %get-tuple-element.30.key_t_ref, ...), custom_call_target="tpu_custom_call" | custom-call | flops 8053063680 | bytes 2097152 | tf_op jit(solution)/shard_map/first_rows/pallas_call | solution.py:354
  32.9 0.0 collective-permute-done.5.refs_5_.refs_1_
  32.9 0.0 collective-permute-done.6.refs_6_.refs_2_
  32.9 0.0 collective-permute-done.7.refs_7_.refs_3_
  32.9 0.0 collective-permute-done.8.refs_8_.refs_1_
  33.0 0.0 collective-permute-done.4.refs_0_
  33.0 2.5 %picked_rows.1 = (f32[2048,128]{1,0:T(8,128)S(1)}, bf16[256,128]{1,0:T(8,128)(2,1)S(1)}, f32[128,128]{1,0:T(8,128)S(1)}, f32[128,128]{1,0:T(8,128)S(1)}) custom-call(s32[2]{0:T(128)S(1)} %pad_add_fusion.place_ref, s32[16]{0:T(128)S(1)} %copy-done, bf16[2048,128]{1,0:T(8,128)(2,1)S(1)} %bitcast.5, f32[2048,128]{1,0:T(8,128)S(1)} %get-tuple-element.34.start_ref, ...), custom_call_target="tpu_custom_call" | custom-call | flops 671088640 | bytes 2097152 | tf_op jit(solution)/shard_map/picked_rows/pallas_call | solution.py:354
  35.4 0.4 collective-permute-start.9
  35.8 6.1 %second_rows.1 = (f32[2048,128]{1,0:T(8,128)S(1)}, bf16[3,128,128]{2,1,0:T(8,128)(2,1)S(1)}) custom-call(s32[2]{0:T(128)S(1)} %pad_add_fusion.place_ref, s32[16]{0:T(128)S(1)} %copy-done, bf16[2048,128]{1,0:T(8,128)(2,1)S(1)} %bitcast.6, bf16[64,2048]{1,0:T(8,128)(2,1)S(1)} %get-tuple-element.30.key_t_ref, f32[2048,128]{1,0:T(8,128)S(1)} %get-tuple-element.40.refs_0_, ...), custom_call_target="tpu_custom_call" | custom-call | flops 8053063680 | bytes 2097152 | tf_op jit(solution)/shard_map/second_rows/pallas_call | solution.py:354
  42.0 0.1 collective-permute-done.9.refs_0_
  42.0 2.9 %last_rows.1 = (bf16[384,128]{1,0:T(8,128)(2,1)S(1)}, bf16[384,128]{1,0:T(8,128)(2,1)S(1)}, bf16[384,128]{1,0:T(8,128)(2,1)S(1)}, bf16[384,128]{1,0:T(8,128)(2,1...) custom-call(s32[2]{0:T(128)S(1)} %pad_add_fusion.place_ref, ...), custom_call_target="tpu_custom_call" | custom-call | flops 2013265920 | bytes 2097152 | tf_op jit(solution)/shard_map/last_rows/pallas_call | solution.py:354
  44.9 1.4 %collective-permute-start.10 = (bf16[384,128]{1,0:T(8,128)(2,1)S(1)}, bf16[384,128]{1,0:T(8,128)(2,1)S(1)}, u32[]{:S(2)}, u32[]{:S(2)}) collective-permute-start(bf16[384,128]{1,0:T(8,128)(2,1)S(1)} %get-tuple-element.48), channel_id=1, source_target_pairs={{0,4},{2,10},{4,0},{6,14},{8,12},{10,2},{12,8},{14,6},{16,20},{18,... | collective-permute-start | bytes 294920 | tf_op jit(solution)/shard_map/ppermute | solution.py:388
  46.4 0.0 collective-permute-start.11
  46.4 0.0 collective-permute-start.12
  46.4 2.6 %collective-permute-start.13 = (bf16[384,128]{1,0:T(8,128)(2,1)S(1)}, bf16[384,128]{1,0:T(8,128)(2,1)S(1)}, u32[]{:S(2)}, u32[]{:S(2)}) collective-permute-start(bf16[384,128]{1,0:T(8,128)(2,1)S(1)} %get-tuple-element.51), channel_id=1, source_target_pairs={{0,14},{2,0},{4,10},{6,4},{8,6},{10,8},{12,2},{14,12},{16,30},{18,... | collective-permute-start | bytes 294920 | tf_op jit(solution)/shard_map/ppermute | solution.py:388
  49.0 0.0 collective-permute-start.14
  49.0 0.9 %collective-permute-done.10.refs_1_ = bf16[384,128]{1,0:T(8,128)(2,1)S(1)} collective-permute-done((bf16[384,128]{1,0:T(8,128)(2,1)S(1)}, bf16[384,128]{1,0:T(8,128)(2,1)S(1)}, u32[]{:S(2)}, u32[]{:S(2)}) %collective-permute-start.10) | collective-permute-done | bytes 98336 | tf_op jit(solution)/shard_map/ppermute | solution.py:388
  49.9 0.9 %collective-permute-start.15 = (bf16[384,128]{1,0:T(8,128)(2,1)S(1)}, bf16[384,128]{1,0:T(8,128)(2,1)S(1)}, u32[]{:S(2)}, u32[]{:S(2)}) collective-permute-start(bf16[384,128]{1,0:T(8,128)(2,1)S(1)} %get-tuple-element.53), channel_id=1, source_target_pairs={{0,6},{2,8},{4,2},{6,12},{8,14},{10,0},{12,10},{14,4},{16,22},{18,... | collective-permute-start | bytes 294920 | tf_op jit(solution)/shard_map/ppermute | solution.py:388
  50.8 1.0 %collective-permute-done.11.refs_2_ = bf16[384,128]{1,0:T(8,128)(2,1)S(1)} collective-permute-done((bf16[384,128]{1,0:T(8,128)(2,1)S(1)}, bf16[384,128]{1,0:T(8,128)(2,1)S(1)}, u32[]{:S(2)}, u32[]{:S(2)}) %collective-permute-start.11) | collective-permute-done | bytes 98336 | tf_op jit(solution)/shard_map/ppermute | solution.py:388
  51.8 1.1 %collective-permute-start.16 = (bf16[384,128]{1,0:T(8,128)(2,1)S(1)}, bf16[384,128]{1,0:T(8,128)(2,1)S(1)}, u32[]{:S(2)}, u32[]{:S(2)}) collective-permute-start(bf16[384,128]{1,0:T(8,128)(2,1)S(1)} %get-tuple-element.54), channel_id=1, source_target_pairs={{0,12},{2,14},{4,8},{6,10},{8,4},{10,6},{12,0},{14,2},{16,28},{18,... | collective-permute-start | bytes 294920 | tf_op jit(solution)/shard_map/ppermute | solution.py:388
  52.9 0.0 collective-permute-done.12.refs_3_
  52.9 0.0 collective-permute-done.13.refs_4_
  52.9 1.7 %collective-permute-done.14.refs_5_ = bf16[384,128]{1,0:T(8,128)(2,1)S(1)} collective-permute-done((bf16[384,128]{1,0:T(8,128)(2,1)S(1)}, bf16[384,128]{1,0:T(8,128)(2,1)S(1)}, u32[]{:S(2)}, u32[]{:S(2)}) %collective-permute-start.14) | collective-permute-done | bytes 98336 | tf_op jit(solution)/shard_map/ppermute | solution.py:388
  54.6 0.4 collective-permute-done.15.refs_6_
  55.0 3.0 %collective-permute-done.16.refs_7_ = bf16[384,128]{1,0:T(8,128)(2,1)S(1)} collective-permute-done((bf16[384,128]{1,0:T(8,128)(2,1)S(1)}, bf16[384,128]{1,0:T(8,128)(2,1)S(1)}, u32[]{:S(2)}, u32[]{:S(2)}) %collective-permute-start.16) | collective-permute-done | bytes 98336 | tf_op jit(solution)/shard_map/ppermute | solution.py:388
  58.0 1.9 %unpack.1 = (bf16[256,512]{1,0:T(8,128)(2,1)}, bf16[256,512]{1,0:T(8,128)(2,1)}, bf16[256,512]{1,0:T(8,128)(2,1)}) custom-call(s32[2]{0:T(128)S(1)} %pad_add_fusion.place_ref, bf16[384,128]{1,0:T(8,128)(2,1)S(1)} %get-tuple-element.47.refs_0_, bf16[384,128]{1,0:T(8,128)(2,1)S(1)} %collective-permute-done.10.refs_1_, ...), custom_call_target="tpu_custom_call" | custom-call | bytes 2097152 | tf_op jit(solution)/shard_map/unpack/pallas_call | solution.py:354
Async XLA Ops:
  0.6 9.5 %collective-permute-start = (bf16[128,1024]{1,0:T(8,128)(2,1)}, bf16[128,1024]{1,0:T(8,128)(2,1)S(1)}, u32[]{:S(2)}, u32[]{:S(2)}) collective-permute-start(bf16[128,1024]{1,0:T(8,128)(2,1)} %refs_0_.1), channel_id=1, source_target_pairs={{0,1},{1,0},{2,3},{3,2},{4,5},{5,4},{6,7},{7,6},{8,9},{9,8},{10,11... | collective-permute-start | bytes 786440 | tf_op jit(solution)/shard_map/ppermute | solution.py:401
  3.6 6.5 %copy-start.2 = (bf16[256,512]{1,0:T(8,128)(2,1)S(1)}, bf16[256,512]{1,0:T(8,128)(2,1)}, u32[]{:S(2)}) copy-start(bf16[256,512]{1,0:T(8,128)(2,1)} %query_ref.1) | copy-start | bytes 786436
  3.6 6.5 %copy-start.3 = (bf16[128,1024]{1,0:T(8,128)(2,1)S(1)}, bf16[128,1024]{1,0:T(8,128)(2,1)}, u32[]{:S(2)}) copy-start(bf16[128,1024]{1,0:T(8,128)(2,1)} %refs_0_.1) | copy-start | bytes 786436
  5.8 4.4 %copy-start.1 = (bf16[512,1024]{1,0:T(8,128)(2,1)S(1)}, bf16[512,1024]{1,0:T(8,128)(2,1)}, u32[]{:S(2)}) copy-start(bf16[512,1024]{1,0:T(8,128)(2,1)} %weight_ref.1) | copy-start | bytes 3145732
  5.8 13.3 %all-to-all-start = ((bf16[8,256,128]{2,1,0:T(8,128)(2,1)}), bf16[8,256,128]{2,1,0:T(8,128)(2,1)S(1)}, u32[]{:S(2)}, u32[]{:S(2)}) async-start(bf16[8,256,128]{2,1,0:T(8,128)(2,1)} %pack_rows.1), calls=%async_computation | async-start | bytes 1048576 | tf_op jit(solution)/shard_map/all_to_all | solution.py:412
  11.7 8.7 %collective-permute-start.1 = (bf16[256,128]{1,0:T(8,128)(2,1)S(1)}, bf16[256,128]{1,0:T(8,128)(2,1)S(1)}, u32[]{:S(2)}, u32[]{:S(2)}) collective-permute-start(bf16[256,128]{1,0:T(8,128)(2,1)S(1)} %get-tuple-element.31), channel_id=1, source_target_pairs={{0,4},{2,10},{4,0},{6,14},{8,12},{10,2},{12,8},{14,6},{16,20},{18,... | collective-permute-start | bytes 196616 | tf_op jit(solution)/shard_map/ppermute | solution.py:388
  13.5 7.0 %collective-permute-start.2 = (bf16[256,128]{1,0:T(8,128)(2,1)S(1)}, bf16[256,128]{1,0:T(8,128)(2,1)S(1)}, u32[]{:S(2)}, u32[]{:S(2)}) collective-permute-start(bf16[256,128]{1,0:T(8,128)(2,1)S(1)} %get-tuple-element.32), channel_id=1, source_target_pairs={{0,8},{2,6},{4,12},{6,2},{8,0},{10,14},{12,4},{14,10},{16,24},{18,... | collective-permute-start | bytes 196616 | tf_op jit(solution)/shard_map/ppermute | solution.py:388
  15.1 7.6 %collective-permute-start.3 = (bf16[256,128]{1,0:T(8,128)(2,1)S(1)}, bf16[256,128]{1,0:T(8,128)(2,1)S(1)}, u32[]{:S(2)}, u32[]{:S(2)}) collective-permute-start(bf16[256,128]{1,0:T(8,128)(2,1)S(1)} %get-tuple-element.33), channel_id=1, source_target_pairs={{0,14},{2,0},{4,10},{6,4},{8,6},{10,8},{12,2},{14,12},{16,30},{18,... | collective-permute-start | bytes 196616 | tf_op jit(solution)/shard_map/ppermute | solution.py:388
  15.1 17.8 %collective-permute-start.5 = (bf16[256,128]{1,0:T(8,128)(2,1)S(1)}, bf16[256,128]{1,0:T(8,128)(2,1)S(1)}, u32[]{:S(2)}, u32[]{:S(2)}) collective-permute-start(bf16[256,128]{1,0:T(8,128)(2,1)S(1)} %get-tuple-element.36), channel_id=1, source_target_pairs={{0,2},{2,12},{4,6},{6,8},{8,10},{10,4},{12,14},{14,0},{16,18},{18,... | collective-permute-start | bytes 196616 | tf_op jit(solution)/shard_map/ppermute | solution.py:388
  15.6 17.3 %collective-permute-start.6 = (bf16[256,128]{1,0:T(8,128)(2,1)S(1)}, bf16[256,128]{1,0:T(8,128)(2,1)S(1)}, u32[]{:S(2)}, u32[]{:S(2)}) collective-permute-start(bf16[256,128]{1,0:T(8,128)(2,1)S(1)} %get-tuple-element.37), channel_id=1, source_target_pairs={{0,6},{2,8},{4,2},{6,12},{8,14},{10,0},{12,10},{14,4},{16,22},{18,... | collective-permute-start | bytes 196616 | tf_op jit(solution)/shard_map/ppermute | solution.py:388
  19.0 0.7 %copy-start = (s32[16]{0:T(128)S(1)}, s32[16]{0:T(128)}, u32[]{:S(2)}) copy-start(s32[16]{0:T(128)} %offset_ref.9) | copy-start | bytes 196
  20.4 12.5 %collective-permute-start.7 = (bf16[256,128]{1,0:T(8,128)(2,1)S(1)}, bf16[256,128]{1,0:T(8,128)(2,1)S(1)}, u32[]{:S(2)}, u32[]{:S(2)}) collective-permute-start(bf16[256,128]{1,0:T(8,128)(2,1)S(1)} %get-tuple-element.38), channel_id=1, source_target_pairs={{0,10},{2,4},{4,14},{6,0},{8,2},{10,12},{12,6},{14,8},{16,26},{18,... | collective-permute-start | bytes 196616 | tf_op jit(solution)/shard_map/ppermute | solution.py:388
  20.5 12.4 %collective-permute-start.8 = (bf16[256,128]{1,0:T(8,128)(2,1)S(1)}, bf16[256,128]{1,0:T(8,128)(2,1)S(1)}, u32[]{:S(2)}, u32[]{:S(2)}) collective-permute-start(bf16[256,128]{1,0:T(8,128)(2,1)S(1)} %get-tuple-element.39), channel_id=1, source_target_pairs={{0,12},{2,14},{4,8},{6,10},{8,4},{10,6},{12,0},{14,2},{16,28},{18,... | collective-permute-start | bytes 196616 | tf_op jit(solution)/shard_map/ppermute | solution.py:388
  22.8 10.2 %collective-permute-start.4 = (bf16[128,128]{1,0:T(8,128)(2,1)S(1)}, bf16[128,128]{1,0:T(8,128)(2,1)S(1)}, u32[]{:S(2)}, u32[]{:S(2)}) collective-permute-start(bf16[128,128]{1,0:T(8,128)(2,1)S(1)} %get-tuple-element.35.picks_ref), channel_id=1, source_target_pairs={{0,16},{2,18},{4,20},{6,22},{8,24},{10,26},{12,28},{14,30},{16,0},... | collective-permute-start | bytes 98312 | tf_op jit(solution)/shard_map/ppermute | solution.py:396
  35.4 6.6 %collective-permute-start.9 = (f32[128,128]{1,0:T(8,128)S(1)}, f32[128,128]{1,0:T(8,128)S(1)}, u32[]{:S(2)}, u32[]{:S(2)}) collective-permute-start(f32[128,128]{1,0:T(8,128)S(1)} %get-tuple-element.46), channel_id=1, source_target_pairs={{0,16},{2,18},{4,20},{6,22},{8,24},{10,26},{12,28},{14,30},{16,0},... | collective-permute-start | bytes 196616 | tf_op jit(solution)/shard_map/ppermute | solution.py:396
  44.9 4.9 %collective-permute-start.10 = (bf16[384,128]{1,0:T(8,128)(2,1)S(1)}, bf16[384,128]{1,0:T(8,128)(2,1)S(1)}, u32[]{:S(2)}, u32[]{:S(2)}) collective-permute-start(bf16[384,128]{1,0:T(8,128)(2,1)S(1)} %get-tuple-element.48), channel_id=1, source_target_pairs={{0,4},{2,10},{4,0},{6,14},{8,12},{10,2},{12,8},{14,6},{16,20},{18,... | collective-permute-start | bytes 294920 | tf_op jit(solution)/shard_map/ppermute | solution.py:388
  46.4 5.4 %collective-permute-start.11 = (bf16[384,128]{1,0:T(8,128)(2,1)S(1)}, bf16[384,128]{1,0:T(8,128)(2,1)S(1)}, u32[]{:S(2)}, u32[]{:S(2)}) collective-permute-start(bf16[384,128]{1,0:T(8,128)(2,1)S(1)} %get-tuple-element.49), channel_id=1, source_target_pairs={{0,8},{2,6},{4,12},{6,2},{8,0},{10,14},{12,4},{14,10},{16,24},{18,... | collective-permute-start | bytes 294920 | tf_op jit(solution)/shard_map/ppermute | solution.py:388
  46.4 6.5 %collective-permute-start.12 = (bf16[384,128]{1,0:T(8,128)(2,1)S(1)}, bf16[384,128]{1,0:T(8,128)(2,1)S(1)}, u32[]{:S(2)}, u32[]{:S(2)}) collective-permute-start(bf16[384,128]{1,0:T(8,128)(2,1)S(1)} %get-tuple-element.50), channel_id=1, source_target_pairs={{0,2},{2,12},{4,6},{6,8},{8,10},{10,4},{12,14},{14,0},{16,18},{18,... | collective-permute-start | bytes 294920 | tf_op jit(solution)/shard_map/ppermute | solution.py:388
  46.4 6.5 %collective-permute-start.13 = (bf16[384,128]{1,0:T(8,128)(2,1)S(1)}, bf16[384,128]{1,0:T(8,128)(2,1)S(1)}, u32[]{:S(2)}, u32[]{:S(2)}) collective-permute-start(bf16[384,128]{1,0:T(8,128)(2,1)S(1)} %get-tuple-element.51), channel_id=1, source_target_pairs={{0,14},{2,0},{4,10},{6,4},{8,6},{10,8},{12,2},{14,12},{16,30},{18,... | collective-permute-start | bytes 294920 | tf_op jit(solution)/shard_map/ppermute | solution.py:388
  49.0 5.6 %collective-permute-start.14 = (bf16[384,128]{1,0:T(8,128)(2,1)S(1)}, bf16[384,128]{1,0:T(8,128)(2,1)S(1)}, u32[]{:S(2)}, u32[]{:S(2)}) collective-permute-start(bf16[384,128]{1,0:T(8,128)(2,1)S(1)} %get-tuple-element.52), channel_id=1, source_target_pairs={{0,10},{2,4},{4,14},{6,0},{8,2},{10,12},{12,6},{14,8},{16,26},{18,... | collective-permute-start | bytes 294920 | tf_op jit(solution)/shard_map/ppermute | solution.py:388
  49.9 5.1 %collective-permute-start.15 = (bf16[384,128]{1,0:T(8,128)(2,1)S(1)}, bf16[384,128]{1,0:T(8,128)(2,1)S(1)}, u32[]{:S(2)}, u32[]{:S(2)}) collective-permute-start(bf16[384,128]{1,0:T(8,128)(2,1)S(1)} %get-tuple-element.53), channel_id=1, source_target_pairs={{0,6},{2,8},{4,2},{6,12},{8,14},{10,0},{12,10},{14,4},{16,22},{18,... | collective-permute-start | bytes 294920 | tf_op jit(solution)/shard_map/ppermute | solution.py:388
  51.8 6.2 %collective-permute-start.16 = (bf16[384,128]{1,0:T(8,128)(2,1)S(1)}, bf16[384,128]{1,0:T(8,128)(2,1)S(1)}, u32[]{:S(2)}, u32[]{:S(2)}) collective-permute-start(bf16[384,128]{1,0:T(8,128)(2,1)S(1)} %get-tuple-element.54), channel_id=1, source_target_pairs={{0,12},{2,14},{4,8},{6,10},{8,4},{10,6},{12,0},{14,2},{16,28},{18,... | collective-permute-start | bytes 294920 | tf_op jit(solution)/shard_map/ppermute | solution.py:388

commit v17 on v16

--- a/solution.py
+++ b/solution.py
@@ -97,19 +97,26 @@
     return [place] + [target_of(place, mirrored(step)) for step in swap_steps(group)]
 
 
-def pack_kernel(head_count, key_hbm, value_hbm, out_ref, key_ref, value_ref, sems):
+def pack_kernel(head_count, group, place_ref, key_hbm, value_hbm, offset_hbm, *refs):
+    out_refs, refs = refs[:group], refs[group:]
+    own_out, key_ref, value_ref, stage_ref, offset_ref, sems = refs
+    loads = [(key_hbm, key_ref), (value_hbm, value_ref), (offset_hbm, offset_ref)]
     copies = [
         pltpu.make_async_copy(source, target, sems.at[index])
-        for index, (source, target) in enumerate([(key_hbm, key_ref), (value_hbm, value_ref)])
+        for index, (source, target) in enumerate(loads)
     ]
     for copy in copies:
         copy.start()
     for copy in copies:
         copy.wait()
+    own_out[0] = place_ref[0]
+    own_out[1] = offset_ref[place_ref[1] * head_count + lax.rem(place_ref[0], head_count)]
     for head in range(head_count):
         pair = jnp.concatenate([head_columns(key_ref, head), head_columns(value_ref, head)], 1)
-        for place in range(head, out_ref.shape[0], head_count):
-            out_ref[place] = pair
+        for place in range(head, group, head_count):
+            stage_ref[place] = pair
+    for place, out_ref in zip(targets(place_ref[0], group), out_refs):
+        out_ref[...] = stage_ref[place]
 
 
 def project_kernel(head_count, group, shards, place_ref, weight_ref, query_ref, *refs):
@@ -130,21 +137,18 @@
         out_ref[...] = stage_ref[place]
 
 
-def own_offset(head_count, place_ref, offset_ref):
-    return offset_ref[place_ref[1] * head_count + lax.rem(place_ref[0], head_count)]
-
-
-def gather_kernel(
-    head_count, group, place_ref, offset_ref, keys_ref, after_ref, key_t_out, picks_out
-):
-    rows = keys_ref.shape[0] // group
+def gather_kernel(group, place_ref, *refs):
+    chunk_refs, (keys_out, key_t_out, picks_out) = refs[:group], refs[group + 1 :]
+    rows = keys_out.shape[0] // group
     picked = rows // DILATION_RATE
-    pick = pick_matrix(own_offset(head_count, place_ref, offset_ref), picked, rows)
+    for place, ref in zip(sources(place_ref[0], group), chunk_refs):
+        keys_out[pl.ds(pl.multiple_of(place * rows, rows), rows), :] = ref[...]
+    key_t_out[...] = keys_out[...].astype(jnp.float32).T[:HEAD_SIZE].astype(jnp.bfloat16)
+    pick = pick_matrix(place_ref[1], picked, rows)
     for place in range(group):
         picks_out[place * picked : (place + 1) * picked, :] = dot_nn(
-            pick, keys_ref[place * rows : (place + 1) * rows, :]
+            pick, keys_out[place * rows : (place + 1) * rows, :]
         ).astype(jnp.bfloat16)
-    key_t_out[...] = keys_ref[...].astype(jnp.float32).T[:HEAD_SIZE].astype(jnp.bfloat16)
 
 
 def halves(both):
@@ -154,7 +158,7 @@
 
 
 def far_kernel(
-    head_count, group, others, place_ref, offset_ref, near_ref, start_ref, picks_ref, *refs
+    group, others, place_ref, near_ref, start_ref, picks_ref, *refs
 ):
     other_refs, refs = refs[:others], refs[others:]
     block_refs, refs = refs[:group], refs[group:]
@@ -164,7 +168,7 @@
     picked = rows // DILATION_RATE
     count = group * picked
     far = count * (1 + others)
-    pick = pick_matrix(own_offset(head_count, place_ref, offset_ref), picked, rows)
+    pick = pick_matrix(place_ref[1], picked, rows)
     keys_ref[:near, :] = near_ref[...]
     for index, ref in enumerate([picks_ref, *other_refs]):
         keys_ref[near + index * count : near + (index + 1) * count, :] = ref[...]
@@ -277,7 +281,7 @@
         emit(index, jnp.concatenate([query_grad[:half], query_grad[half:]], 1))
 
 
-def some_kernel(head_count, steps, begin, place_ref, offset_ref, keys_ref, key_t_ref, *refs):
+def some_kernel(steps, begin, place_ref, keys_ref, key_t_ref, *refs):
     if not begin:
         start_ref, refs = refs[0], refs[1:]
     block_refs, (acc_ref, query_out, *scratch) = refs[:steps], refs[steps:]
@@ -287,13 +291,13 @@
         query_out[index] = query_grad
 
     near_blocks(
-        own_offset(head_count, place_ref, offset_ref), keys_ref, key_t_ref, block_refs,
+        place_ref[1], keys_ref, key_t_ref, block_refs,
         *scratch, acc_ref, emit,
     )
 
 
 def end_kernel(
-    head_count, steps, others, place_ref, offset_ref, keys_ref, key_t_ref, start_ref, query_ref,
+    steps, others, place_ref, keys_ref, key_t_ref, start_ref, query_ref,
     later_query_ref, picked_query_ref, own_ref, *refs,
 ):
     back_refs, refs = refs[:others], refs[others:]
@@ -305,7 +309,7 @@
     acc_ref, *scratch = refs
     count = own_ref.shape[0]
     picked = count // group
-    offset = own_offset(head_count, place_ref, offset_ref)
+    offset = place_ref[1]
     acc_ref[...] = start_ref[...]
 
     def finish(bits, query_grad):
@@ -342,27 +346,32 @@
     half = rows // 2
     for place, near_ref in zip(targets(place_ref[0], group), near_refs):
         stage_ref[place] = near_ref[...]
-    for head in range(head_count):
-        columns = slice(head * HEAD_SIZE, (head + 1) * HEAD_SIZE)
-        key_out[:, columns] = stage_ref[head, :rows, :HEAD_SIZE]
-        value_out[:, columns] = stage_ref[head, :rows, HEAD_SIZE:]
-        query_out[:half, columns] = stage_ref[head, rows:, :HEAD_SIZE]
-        query_out[half:, columns] = stage_ref[head, rows:, HEAD_SIZE:]
-
-
-def call(kernel, name, out_shape, scalars, operands, scratch=(), flops=0, space=VMEM, limit=40):
+    for head in range(0, head_count, 2):
+        columns = slice(head * HEAD_SIZE, (head + 2) * HEAD_SIZE)
+        pairs = [stage_ref[head, :rows, :], stage_ref[head + 1, :rows, :]]
+        packed = [stage_ref[head, rows:, :], stage_ref[head + 1, rows:, :]]
+        key_out[:, columns] = jnp.concatenate([pair[:, :HEAD_SIZE] for pair in pairs], 1)
+        value_out[:, columns] = jnp.concatenate([pair[:, HEAD_SIZE:] for pair in pairs], 1)
+        query_out[:half, columns] = jnp.concatenate([pair[:, :HEAD_SIZE] for pair in packed], 1)
+        query_out[half:, columns] = jnp.concatenate([pair[:, HEAD_SIZE:] for pair in packed], 1)
+
+
+def call(
+    kernel, name, out_shape, scalars, operands, scratch=(), flops=0, hbm=(), limit=40, scalars_out=0
+):
+    last = len(out_shape) - scalars_out
     return pl.pallas_call(
         kernel,
         out_shape=tuple(jax.ShapeDtypeStruct(*shape) for shape in out_shape),
-        in_specs=[SMEM] * len(scalars) + [space] * len(operands),
-        out_specs=tuple(VMEM for _ in out_shape),
+        in_specs=[SMEM] * len(scalars) + [VMEM] * len(operands) + [ANY] * len(hbm),
+        out_specs=tuple(VMEM if index < last else SMEM for index in range(len(out_shape))),
         scratch_shapes=[
             pltpu.VMEM(*shape) if isinstance(shape, tuple) else shape for shape in scratch
         ],
         compiler_params=pltpu.CompilerParams(vmem_limit_bytes=limit * 1024 * 1024),
         cost_estimate=pl.CostEstimate(flops=flops, bytes_accessed=2**21, transcendentals=0),
         name=name,
-    )(*scalars, *operands)
+    )(*scalars, *operands, *hbm)
 
 
 def body(upstream, out_weight, query_rows, key_rows, value_rows, head_offsets):
@@ -379,7 +388,6 @@
     place = jnp.stack(
         [lax.rem(lax.axis_index("context"), group), lax.axis_index("heads")]
     ).astype(jnp.int32)
-    scalars = [place, head_offsets]
 
     def swap(values, steps):
         result = [values[0]]
@@ -401,15 +409,18 @@
         upstreams.append(lax.ppermute(upstream, "heads", pairs))
 
     bf16, f32 = jnp.bfloat16, jnp.float32
-    (sent,) = call(
-        functools.partial(pack_kernel, head_count), "pack_rows",
-        [((group, rows, PAIR), bf16)],
-        [], [key_rows, value_rows],
-        [((rows, width), bf16)] * 2 + [pltpu.SemaphoreType.DMA((2,))],
-        flops=2**31, space=ANY, limit=60,
-    )
-    groups = [list(range(first, first + group)) for first in range(0, devices, group)]
-    sent = lax.all_to_all(sent, "context", 0, 0, axis_index_groups=groups)
+    *sent, own = call(
+        functools.partial(pack_kernel, head_count, group), "pack_rows",
+        [((rows, PAIR), bf16)] * group + [((2,), jnp.int32)],
+        [place], [],
+        [((rows, width), bf16)] * 2
+        + [
+            ((group, rows, PAIR), bf16), pltpu.SMEM(head_offsets.shape, jnp.int32),
+            pltpu.SemaphoreType.DMA((3,)),
+        ],
+        flops=2**31, hbm=[key_rows, value_rows, head_offsets], limit=60, scalars_out=1,
+    )
+    sent = swap(sent, out_steps)
     blocks_send = call(
         functools.partial(project_kernel, head_count, group, shards), "project_pack",
         [((rows, PAIR), bf16)] * group,
@@ -418,11 +429,10 @@
         flops=BUSY,
     )
     blocks = swap(blocks_send, out_steps)
-    keys = sent.reshape(near, PAIR)
-    key_t, picks = call(
-        functools.partial(gather_kernel, head_count, group), "gather_keys",
-        [((HEAD_SIZE, near), bf16), ((count, PAIR), bf16)],
-        scalars, [keys, blocks_send[0]],
+    keys, key_t, picks = call(
+        functools.partial(gather_kernel, group), "gather_keys",
+        [((near, PAIR), bf16), ((HEAD_SIZE, near), bf16), ((count, PAIR), bf16)],
+        [own], [*sent, blocks_send[0]],
     )
     other_picks = [segment_shift(picks, shift) for shift in range(1, others + 1)]
     steps = group // 2
@@ -433,17 +443,17 @@
     half_flops = 30 * near * near // 2 * PAIR
     early, late = blocks[:steps], blocks[steps:-1]
     acc, query_early = call(
-        functools.partial(some_kernel, head_count, len(early), True), "first_rows",
+        functools.partial(some_kernel, len(early), True), "first_rows",
         [((near, PAIR), f32), ((len(early), half, PAIR), bf16)],
-        scalars, [keys, key_t, *early], scratch, half_flops,
+        [own], [keys, key_t, *early], scratch, half_flops,
     )
     acc, picked_query, own_terms, other_terms = call(
-        functools.partial(far_kernel, head_count, group, others), "picked_rows",
+        functools.partial(far_kernel, group, others), "picked_rows",
         [
             ((near, PAIR), f32), ((2 * count, PAIR), bf16), ((count, PAIR), f32),
             ((others * count, PAIR), f32),
         ],
-        scalars, [keys, acc, picks, *other_picks, *blocks],
+        [own], [keys, acc, picks, *other_picks, *blocks],
         [((near + count * (1 + others), PAIR), bf16), ((count, PAIR), bf16)],
         flops=20 * near * count * PAIR,
     )
@@ -452,14 +462,14 @@
         for shift in range(1, others + 1)
     ]
     acc, query_late = call(
-        functools.partial(some_kernel, head_count, len(late), False), "second_rows",
+        functools.partial(some_kernel, len(late), False), "second_rows",
         [((near, PAIR), f32), ((len(late), half, PAIR), bf16)],
-        scalars, [keys, key_t, acc, *late], scratch, half_flops,
+        [own], [keys, key_t, acc, *late], scratch, half_flops,
     )
     near_send = call(
-        functools.partial(end_kernel, head_count, 1, others), "last_rows",
+        functools.partial(end_kernel, 1, others), "last_rows",
         [((rows + half, PAIR), bf16)] * group,
-        scalars,
+        [own],
         [
             keys, key_t, acc, query_early, query_late, picked_query, own_terms, *back, blocks[-1],
         ],

time: 60.2 us -> 62.9 us (1.045)
  starting transfers between devices: 23.9 us -> 25.7 us
    ppermute x14 -> x21, starting transfers between devices: 14 us -> 19.7 us  [swap(): result.append(lax.ppermute(value, 'context', pairs))]
    all_to_all x1 -> x0, starting transfers between devices: 3.95 us -> none  [body(): sent = lax.all_to_all(sent, 'context', 0, 0, axis_index_groups=groups)]
    all_to_all x1 -> x0, waiting for transfers between devices: 1.72 us -> none  [body(): sent = lax.all_to_all(sent, 'context', 0, 0, axis_index_groups=groups)]
    ppermute x14 -> x21, waiting for transfers between devices: 7.01 us -> 8.35 us  [swap(): result.append(lax.ppermute(value, 'context', pairs))]
    ppermute x2, waiting for transfers between devices: 0.07 us -> 0.72 us  [segment_shift(): return lax.ppermute(value, 'context', pairs)]
  transfers between devices with their start and end apart: 18 -> 24, of which waited for: 8 -> 7; matrix products, arithmetic and copies ran while one was open for 0% -> 1% of each run, Pallas kernels for 30% -> 30%
where the time goes in v17:
time: 62.9 us; the launch traced here: 62.7 us
  Pallas kernels  25.9 us (41%)
  starting transfers between devices  25.7 us (41%)
  waiting for transfers between devices  9.07 us (14%)
  between operations  0.75 us (1%)
  local copies, waits for them, and re-layouts  0.68 us (1%)
  other arithmetic  0.65 us (1%)
    pallas_call x8, Pallas kernels, call(): pl.pallas_call(kernel, out_shape=tuple((jax.ShapeDtypeStruct(*shape) for...  25.9 us
    ppermute x21, starting transfers between devices, swap(): result.append(lax.ppermute(value, 'context', pairs))  19.7 us
    ppermute x21, waiting for transfers between devices, swap(): result.append(lax.ppermute(value, 'context', pairs))  8.35 us
    ppermute x1, starting transfers between devices, body(): upstreams.append(lax.ppermute(upstream, 'heads', pairs))  3 us
    ppermute x2, starting transfers between devices, segment_shift(): return lax.ppermute(value, 'context', pairs)  2.99 us
  transfers between devices with their start and end apart: 24, of which 7 were waited for; matrix products, arithmetic and copies ran while one was open for 1% of the time, Pallas kernels for 30%

profile of v17, /device:TPU:0, one launch (start us, length us, event | category | flops | bytes accessed | tf_op | source)
XLA Modules:
  0.0 62.7 jit_solution(2947890979612803173)
XLA Ops:
  0.6 3.0 %collective-permute-start.7 = (bf16[128,1024]{1,0:T(8,128)(2,1)}, bf16[128,1024]{1,0:T(8,128)(2,1)S(1)}, u32[]{:S(2)}, u32[]{:S(2)}) collective-permute-start(bf16[128,1024]{1,0:T(8,128)(2,1)} %refs_0_.1), channel_id=1, source_target_pairs={{0,1},{1,0},{2,3},{3,2},{4,5},{5,4},{6,7},{7,6},{8,9},{9,8},{10,11... | collective-permute-start | bytes 786440 | tf_op jit(solution)/shard_map/ppermute | solution.py:409
  3.6 0.6 %pad_add_fusion.place_ref = s32[2]{0:T(128)} fusion(s32[1]{0:T(128)} %bitcast.1, s32[1]{0:T(128)} %bitcast), kind=kLoop, calls=%fused_computation | loop fusion | flops 2 | bytes 16 | tf_op jit(solution)/shard_map/stack | solution.py:388
  4.3 0.0 copy-start.3
  4.3 2.9 %pack_rows.1 = (bf16[256,128]{1,0:T(8,128)(2,1)}, bf16[256,128]{1,0:T(8,128)(2,1)}, bf16[256,128]{1,0:T(8,128)(2,1)}, bf16[256,128]{1,0:T(8,128)(2,1)}, bf16[256...) custom-call(s32[2]{0:T(128)} %pad_add_fusion.place_ref, ...), custom_call_target="tpu_custom_call" | custom-call | flops 2147483648 | bytes 2097152 | tf_op jit(solution)/shard_map/pack_rows/pallas_call | solution.py:363
  7.1 1.6 %collective-permute-start = (bf16[256,128]{1,0:T(8,128)(2,1)}, bf16[256,128]{1,0:T(8,128)(2,1)S(1)}, u32[]{:S(2)}, u32[]{:S(2)}) collective-permute-start(bf16[256,128]{1,0:T(8,128)(2,1)} %get-tuple-element.41), channel_id=1, source_target_pairs={{0,4},{2,10},{4,0},{6,14},{8,12},{10,2},{12,8},{14,6},{16,20},{18,... | collective-permute-start | bytes 196616 | tf_op jit(solution)/shard_map/ppermute | solution.py:396
  8.7 1.6 %collective-permute-start.1 = (bf16[256,128]{1,0:T(8,128)(2,1)}, bf16[256,128]{1,0:T(8,128)(2,1)S(1)}, u32[]{:S(2)}, u32[]{:S(2)}) collective-permute-start(bf16[256,128]{1,0:T(8,128)(2,1)} %get-tuple-element.42), channel_id=1, source_target_pairs={{0,8},{2,6},{4,12},{6,2},{8,0},{10,14},{12,4},{14,10},{16,24},{18,... | collective-permute-start | bytes 196616 | tf_op jit(solution)/shard_map/ppermute | solution.py:396
  10.3 0.0 collective-permute-start.2
  10.3 0.5 collective-permute-start.3
  10.8 1.5 %collective-permute-done.refs_1_ = bf16[256,128]{1,0:T(8,128)(2,1)S(1)} collective-permute-done((bf16[256,128]{1,0:T(8,128)(2,1)}, bf16[256,128]{1,0:T(8,128)(2,1)S(1)}, u32[]{:S(2)}, u32[]{:S(2)}) %collective-permute-start) | collective-permute-done | bytes 65568 | tf_op jit(solution)/shard_map/ppermute | solution.py:396
  12.3 0.0 collective-permute-start.4
  12.3 0.9 %collective-permute-done.1.refs_2_ = bf16[256,128]{1,0:T(8,128)(2,1)S(1)} collective-permute-done((bf16[256,128]{1,0:T(8,128)(2,1)}, bf16[256,128]{1,0:T(8,128)(2,1)S(1)}, u32[]{:S(2)}, u32[]{:S(2)}) %collective-permute-start.1) | collective-permute-done | bytes 65568 | tf_op jit(solution)/shard_map/ppermute | solution.py:396
  13.2 0.8 %collective-permute-start.5 = (bf16[256,128]{1,0:T(8,128)(2,1)}, bf16[256,128]{1,0:T(8,128)(2,1)S(1)}, u32[]{:S(2)}, u32[]{:S(2)}) collective-permute-start(bf16[256,128]{1,0:T(8,128)(2,1)} %get-tuple-element.46), channel_id=1, source_target_pairs={{0,10},{2,4},{4,14},{6,0},{8,2},{10,12},{12,6},{14,8},{16,26},{18,... | collective-permute-start | bytes 196616 | tf_op jit(solution)/shard_map/ppermute | solution.py:396
  14.0 0.0 collective-permute-done.7.refs_1_
  14.0 2.0 %collective-permute-start.6 = (bf16[256,128]{1,0:T(8,128)(2,1)}, bf16[256,128]{1,0:T(8,128)(2,1)S(1)}, u32[]{:S(2)}, u32[]{:S(2)}) collective-permute-start(bf16[256,128]{1,0:T(8,128)(2,1)} %get-tuple-element.47), channel_id=1, source_target_pairs={{0,12},{2,14},{4,8},{6,10},{8,4},{10,6},{12,0},{14,2},{16,28},{18,... | collective-permute-start | bytes 196616 | tf_op jit(solution)/shard_map/ppermute | solution.py:396
  16.0 0.0 copy-done.3
  16.0 0.0 copy-done.4
  16.0 0.0 copy-done.5
  16.0 0.0 copy-done.1
  16.0 1.5 %project_pack.1 = (bf16[256,128]{1,0:T(8,128)(2,1)S(1)}, bf16[256,128]{1,0:T(8,128)(2,1)S(1)}, bf16[256,128]{1,0:T(8,128)(2,1)S(1)}, bf16[256,128]{1,0:T(8,128)(...) custom-call(s32[2]{0:T(128)S(1)} %copy-done.1, ...), custom_call_target="tpu_custom_call" | custom-call | flops 34359738368 | bytes 2097152 | tf_op jit(solution)/shard_map/project_pack/pallas_call | solution.py:363
  17.6 0.0 collective-permute-done.2.refs_3_
  17.6 0.6 collective-permute-start.8
  18.1 0.0 collective-permute-done.3.refs_4_
  18.2 1.0 %collective-permute-start.9 = (bf16[256,128]{1,0:T(8,128)(2,1)S(1)}, bf16[256,128]{1,0:T(8,128)(2,1)S(1)}, u32[]{:S(2)}, u32[]{:S(2)}) collective-permute-start(bf16[256,128]{1,0:T(8,128)(2,1)S(1)} %get-tuple-element.52), channel_id=1, source_target_pairs={{0,8},{2,6},{4,12},{6,2},{8,0},{10,14},{12,4},{14,10},{16,24},{18,... | collective-permute-start | bytes 196616 | tf_op jit(solution)/shard_map/ppermute | solution.py:396
  19.2 0.0 collective-permute-done.4.refs_5_
  19.2 1.1 %collective-permute-start.10 = (bf16[256,128]{1,0:T(8,128)(2,1)S(1)}, bf16[256,128]{1,0:T(8,128)(2,1)S(1)}, u32[]{:S(2)}, u32[]{:S(2)}) collective-permute-start(bf16[256,128]{1,0:T(8,128)(2,1)S(1)} %get-tuple-element.53), channel_id=1, source_target_pairs={{0,14},{2,0},{4,10},{6,4},{8,6},{10,8},{12,2},{14,12},{16,30},{18,... | collective-permute-start | bytes 196616 | tf_op jit(solution)/shard_map/ppermute | solution.py:396
  20.3 0.0 collective-permute-done.5.refs_6_
  20.3 0.0 collective-permute-start.12
  20.3 0.0 collective-permute-done.6.refs_7_
  20.3 1.6 %collective-permute-start.13 = (bf16[256,128]{1,0:T(8,128)(2,1)S(1)}, bf16[256,128]{1,0:T(8,128)(2,1)S(1)}, u32[]{:S(2)}, u32[]{:S(2)}) collective-permute-start(bf16[256,128]{1,0:T(8,128)(2,1)S(1)} %get-tuple-element.57), channel_id=1, source_target_pairs={{0,6},{2,8},{4,2},{6,12},{8,14},{10,0},{12,10},{14,4},{16,22},{18,... | collective-permute-start | bytes 196616 | tf_op jit(solution)/shard_map/ppermute | solution.py:396
  21.9 0.0 copy-done
  21.9 0.7 %copy-done.2 = s32[2]{0:T(128)S(1)} copy-done((s32[2]{0:T(128)S(1)}, s32[2]{0:T(128)}, u32[]{:S(2)}) %copy-start.2) | copy-done | bytes 32
  22.6 0.8 %gather_keys.1 = (bf16[2048,128]{1,0:T(8,128)(2,1)S(1)}, bf16[64,2048]{1,0:T(8,128)(2,1)S(1)}, bf16[128,128]{1,0:T(8,128)(2,1)S(1)}) custom-call(s32[2]{0:T(128)S(1)} %copy-done.2, bf16[256,128]{1,0:T(8,128)(2,1)S(1)} %copy-done, bf16[256,128]{1,0:T(8,128)(2,1)S(1)} %collective-permute-done.refs_1_, bf16[256,128]{1,0:T(8,128)(2,1)S(1)} %collective-permute-done.1.refs_2_, ...), custom_call_target="tpu_custom_call" | custom-call | bytes 2097152 | tf_op jit(solution)/shard_map/gather_keys/pallas_call | solution.py:363
  23.4 0.0 collective-permute-done.8.refs_1_.refs_2_
  23.4 0.4 collective-permute-start.14
  23.8 0.0 collective-permute-done.9.refs_2_.refs_3_
  23.8 1.4 %collective-permute-start.15 = (bf16[256,128]{1,0:T(8,128)(2,1)S(1)}, bf16[256,128]{1,0:T(8,128)(2,1)S(1)}, u32[]{:S(2)}, u32[]{:S(2)}) collective-permute-start(bf16[256,128]{1,0:T(8,128)(2,1)S(1)} %get-tuple-element.59), channel_id=1, source_target_pairs={{0,12},{2,14},{4,8},{6,10},{8,4},{10,6},{12,0},{14,2},{16,28},{18,... | collective-permute-start | bytes 196616 | tf_op jit(solution)/shard_map/ppermute | solution.py:396
  25.2 0.0 collective-permute-done.10.refs_3_.refs_4_
  25.2 2.6 %collective-permute-start.11 = (bf16[128,128]{1,0:T(8,128)(2,1)S(1)}, bf16[128,128]{1,0:T(8,128)(2,1)S(1)}, u32[]{:S(2)}, u32[]{:S(2)}) collective-permute-start(bf16[128,128]{1,0:T(8,128)(2,1)S(1)} %get-tuple-element.55.picks_ref), channel_id=1, source_target_pairs={{0,16},{2,18},{4,20},{6,22},{8,24},{10,26},{12,28},{14,30},{16,0},... | collective-permute-start | bytes 98312 | tf_op jit(solution)/shard_map/ppermute | solution.py:404
  27.8 7.5 %first_rows.1 = (f32[2048,128]{1,0:T(8,128)S(1)}, bf16[4,128,128]{2,1,0:T(8,128)(2,1)S(1)}) custom-call(s32[2]{0:T(128)S(1)} %copy-done.2, bf16[2048,128]{1,0:T(8,128)(2,1)S(1)} %get-tuple-element.49.keys_ref.near_ref, bf16[64,2048]{1,0:T(8,128)(2,1)S(1)} %get-tuple-element.50.key_t_ref, bf16[256,128]{1,0:T(8,128)(2,1)S(1)} %get-tuple-element.48.refs_8_.refs_0_.refs_1_, ...), custom_call_target="tpu_custom_call" | custom-call | flops 8053063680 | bytes 2097152 | tf_op jit(solution)/shard_map/first_rows/pallas_call | solution.py:363
  35.3 0.0 collective-permute-done.11.refs_0_
  35.3 0.0 collective-permute-done.12.refs_5_.refs_1_
  35.4 0.0 collective-permute-done.13.refs_6_.refs_2_
  35.4 0.0 collective-permute-done.14.refs_7_.refs_3_
  35.4 0.0 collective-permute-done.15.refs_8_.refs_1_
  35.4 2.5 %picked_rows.1 = (f32[2048,128]{1,0:T(8,128)S(1)}, bf16[256,128]{1,0:T(8,128)(2,1)S(1)}, f32[128,128]{1,0:T(8,128)S(1)}, f32[128,128]{1,0:T(8,128)S(1)}) custom-call(s32[2]{0:T(128)S(1)} %copy-done.2, bf16[2048,128]{1,0:T(8,128)(2,1)S(1)} %get-tuple-element.49.keys_ref.near_ref, f32[2048,128]{1,0:T(8,128)S(1)} %get-tuple-element.54.start_ref, ...), custom_call_target="tpu_custom_call" | custom-call | flops 671088640 | bytes 2097152 | tf_op jit(solution)/shard_map/picked_rows/pallas_call | solution.py:363
  37.9 0.4 collective-permute-start.16
  38.3 6.1 %second_rows.1 = (f32[2048,128]{1,0:T(8,128)S(1)}, bf16[3,128,128]{2,1,0:T(8,128)(2,1)S(1)}) custom-call(s32[2]{0:T(128)S(1)} %copy-done.2, bf16[2048,128]{1,0:T(8,128)(2,1)S(1)} %get-tuple-element.49.keys_ref.near_ref, bf16[64,2048]{1,0:T(8,128)(2,1)S(1)} %get-tuple-element.50.key_t_ref, f32[2048,128]{1,0:T(8,128)S(1)} %get-tuple-element.60.refs_0_, ...), custom_call_target="tpu_custom_call" | custom-call | flops 8053063680 | bytes 2097152 | tf_op jit(solution)/shard_map/second_rows/pallas_call | solution.py:363
  44.4 0.7 %collective-permute-done.16.refs_0_ = f32[128,128]{1,0:T(8,128)S(1)} collective-permute-done((f32[128,128]{1,0:T(8,128)S(1)}, f32[128,128]{1,0:T(8,128)S(1)}, u32[]{:S(2)}, u32[]{:S(2)}) %collective-permute-start.16) | collective-permute-done | bytes 65568 | tf_op jit(solution)/shard_map/ppermute | solution.py:404
  45.1 2.9 %last_rows.1 = (bf16[384,128]{1,0:T(8,128)(2,1)S(1)}, bf16[384,128]{1,0:T(8,128)(2,1)S(1)}, bf16[384,128]{1,0:T(8,128)(2,1)S(1)}, bf16[384,128]{1,0:T(8,128)(2,1...) custom-call(s32[2]{0:T(128)S(1)} %copy-done.2, ...), custom_call_target="tpu_custom_call" | custom-call | flops 2013265920 | bytes 2097152 | tf_op jit(solution)/shard_map/last_rows/pallas_call | solution.py:363
  48.0 0.9 %collective-permute-start.17 = (bf16[384,128]{1,0:T(8,128)(2,1)S(1)}, bf16[384,128]{1,0:T(8,128)(2,1)S(1)}, u32[]{:S(2)}, u32[]{:S(2)}) collective-permute-start(bf16[384,128]{1,0:T(8,128)(2,1)S(1)} %get-tuple-element.68), channel_id=1, source_target_pairs={{0,4},{2,10},{4,0},{6,14},{8,12},{10,2},{12,8},{14,6},{16,20},{18,... | collective-permute-start | bytes 294920 | tf_op jit(solution)/shard_map/ppermute | solution.py:396
  48.9 0.5 collective-permute-start.18
  49.4 0.0 collective-permute-start.19
  49.4 2.6 %collective-permute-start.20 = (bf16[384,128]{1,0:T(8,128)(2,1)S(1)}, bf16[384,128]{1,0:T(8,128)(2,1)S(1)}, u32[]{:S(2)}, u32[]{:S(2)}) collective-permute-start(bf16[384,128]{1,0:T(8,128)(2,1)S(1)} %get-tuple-element.71), channel_id=1, source_target_pairs={{0,14},{2,0},{4,10},{6,4},{8,6},{10,8},{12,2},{14,12},{16,30},{18,... | collective-permute-start | bytes 294920 | tf_op jit(solution)/shard_map/ppermute | solution.py:396
  52.1 0.0 collective-permute-start.21
  52.1 0.9 %collective-permute-done.17.refs_1_ = bf16[384,128]{1,0:T(8,128)(2,1)S(1)} collective-permute-done((bf16[384,128]{1,0:T(8,128)(2,1)S(1)}, bf16[384,128]{1,0:T(8,128)(2,1)S(1)}, u32[]{:S(2)}, u32[]{:S(2)}) %collective-permute-start.17) | collective-permute-done | bytes 98336 | tf_op jit(solution)/shard_map/ppermute | solution.py:396
  52.9 0.9 %collective-permute-start.22 = (bf16[384,128]{1,0:T(8,128)(2,1)S(1)}, bf16[384,128]{1,0:T(8,128)(2,1)S(1)}, u32[]{:S(2)}, u32[]{:S(2)}) collective-permute-start(bf16[384,128]{1,0:T(8,128)(2,1)S(1)} %get-tuple-element.73), channel_id=1, source_target_pairs={{0,6},{2,8},{4,2},{6,12},{8,14},{10,0},{12,10},{14,4},{16,22},{18,... | collective-permute-start | bytes 294920 | tf_op jit(solution)/shard_map/ppermute | solution.py:396
  53.8 0.0 collective-permute-done.18.refs_2_
  53.8 2.1 %collective-permute-start.23 = (bf16[384,128]{1,0:T(8,128)(2,1)S(1)}, bf16[384,128]{1,0:T(8,128)(2,1)S(1)}, u32[]{:S(2)}, u32[]{:S(2)}) collective-permute-start(bf16[384,128]{1,0:T(8,128)(2,1)S(1)} %get-tuple-element.74), channel_id=1, source_target_pairs={{0,12},{2,14},{4,8},{6,10},{8,4},{10,6},{12,0},{14,2},{16,28},{18,... | collective-permute-start | bytes 294920 | tf_op jit(solution)/shard_map/ppermute | solution.py:396
  55.9 0.0 collective-permute-done.19.refs_3_
  55.9 0.0 collective-permute-done.20.refs_4_
  55.9 1.6 %collective-permute-done.21.refs_5_ = bf16[384,128]{1,0:T(8,128)(2,1)S(1)} collective-permute-done((bf16[384,128]{1,0:T(8,128)(2,1)S(1)}, bf16[384,128]{1,0:T(8,128)(2,1)S(1)}, u32[]{:S(2)}, u32[]{:S(2)}) %collective-permute-start.21) | collective-permute-done | bytes 98336 | tf_op jit(solution)/shard_map/ppermute | solution.py:396
  57.5 0.5 collective-permute-done.22.refs_6_
  58.0 3.0 %collective-permute-done.23.refs_7_ = bf16[384,128]{1,0:T(8,128)(2,1)S(1)} collective-permute-done((bf16[384,128]{1,0:T(8,128)(2,1)S(1)}, bf16[384,128]{1,0:T(8,128)(2,1)S(1)}, u32[]{:S(2)}, u32[]{:S(2)}) %collective-permute-start.23) | collective-permute-done | bytes 98336 | tf_op jit(solution)/shard_map/ppermute | solution.py:396
  61.0 1.7 %unpack.1 = (bf16[256,512]{1,0:T(8,128)(2,1)}, bf16[256,512]{1,0:T(8,128)(2,1)}, bf16[256,512]{1,0:T(8,128)(2,1)}) custom-call(s32[2]{0:T(128)S(1)} %copy-done.1, bf16[384,128]{1,0:T(8,128)(2,1)S(1)} %get-tuple-element.67.refs_0_, bf16[384,128]{1,0:T(8,128)(2,1)S(1)} %collective-permute-done.17.refs_1_, ...), custom_call_target="tpu_custom_call" | custom-call | bytes 2097152 | tf_op jit(solution)/shard_map/unpack/pallas_call | solution.py:363
  (5 shorter events, 0.0 us)
Async XLA Ops:
  0.6 13.4 %collective-permute-start.7 = (bf16[128,1024]{1,0:T(8,128)(2,1)}, bf16[128,1024]{1,0:T(8,128)(2,1)S(1)}, u32[]{:S(2)}, u32[]{:S(2)}) collective-permute-start(bf16[128,1024]{1,0:T(8,128)(2,1)} %refs_0_.1), channel_id=1, source_target_pairs={{0,1},{1,0},{2,3},{3,2},{4,5},{5,4},{6,7},{7,6},{8,9},{9,8},{10,11... | collective-permute-start | bytes 786440 | tf_op jit(solution)/shard_map/ppermute | solution.py:409
  4.3 11.7 %copy-start.3 = (bf16[512,1024]{1,0:T(8,128)(2,1)S(1)}, bf16[512,1024]{1,0:T(8,128)(2,1)}, u32[]{:S(2)}) copy-start(bf16[512,1024]{1,0:T(8,128)(2,1)} %weight_ref.1) | copy-start | bytes 3145732
  4.3 11.7 %copy-start.4 = (bf16[256,512]{1,0:T(8,128)(2,1)S(1)}, bf16[256,512]{1,0:T(8,128)(2,1)}, u32[]{:S(2)}) copy-start(bf16[256,512]{1,0:T(8,128)(2,1)} %query_ref.1) | copy-start | bytes 786436
  4.3 11.7 %copy-start.5 = (bf16[128,1024]{1,0:T(8,128)(2,1)S(1)}, bf16[128,1024]{1,0:T(8,128)(2,1)}, u32[]{:S(2)}) copy-start(bf16[128,1024]{1,0:T(8,128)(2,1)} %refs_0_.1) | copy-start | bytes 786436
  7.1 5.1 %collective-permute-start = (bf16[256,128]{1,0:T(8,128)(2,1)}, bf16[256,128]{1,0:T(8,128)(2,1)S(1)}, u32[]{:S(2)}, u32[]{:S(2)}) collective-permute-start(bf16[256,128]{1,0:T(8,128)(2,1)} %get-tuple-element.41), channel_id=1, source_target_pairs={{0,4},{2,10},{4,0},{6,14},{8,12},{10,2},{12,8},{14,6},{16,20},{18,... | collective-permute-start | bytes 196616 | tf_op jit(solution)/shard_map/ppermute | solution.py:396
  8.7 4.5 %collective-permute-start.1 = (bf16[256,128]{1,0:T(8,128)(2,1)}, bf16[256,128]{1,0:T(8,128)(2,1)S(1)}, u32[]{:S(2)}, u32[]{:S(2)}) collective-permute-start(bf16[256,128]{1,0:T(8,128)(2,1)} %get-tuple-element.42), channel_id=1, source_target_pairs={{0,8},{2,6},{4,12},{6,2},{8,0},{10,14},{12,4},{14,10},{16,24},{18,... | collective-permute-start | bytes 196616 | tf_op jit(solution)/shard_map/ppermute | solution.py:396
  10.3 7.3 %collective-permute-start.2 = (bf16[256,128]{1,0:T(8,128)(2,1)}, bf16[256,128]{1,0:T(8,128)(2,1)S(1)}, u32[]{:S(2)}, u32[]{:S(2)}) collective-permute-start(bf16[256,128]{1,0:T(8,128)(2,1)} %get-tuple-element.43), channel_id=1, source_target_pairs={{0,14},{2,0},{4,10},{6,4},{8,6},{10,8},{12,2},{14,12},{16,30},{18,... | collective-permute-start | bytes 196616 | tf_op jit(solution)/shard_map/ppermute | solution.py:396
  10.3 7.8 %collective-permute-start.3 = (bf16[256,128]{1,0:T(8,128)(2,1)}, bf16[256,128]{1,0:T(8,128)(2,1)S(1)}, u32[]{:S(2)}, u32[]{:S(2)}) collective-permute-start(bf16[256,128]{1,0:T(8,128)(2,1)} %get-tuple-element.44), channel_id=1, source_target_pairs={{0,2},{2,12},{4,6},{6,8},{8,10},{10,4},{12,14},{14,0},{16,18},{18,... | collective-permute-start | bytes 196616 | tf_op jit(solution)/shard_map/ppermute | solution.py:396
  12.3 6.9 %collective-permute-start.4 = (bf16[256,128]{1,0:T(8,128)(2,1)}, bf16[256,128]{1,0:T(8,128)(2,1)S(1)}, u32[]{:S(2)}, u32[]{:S(2)}) collective-permute-start(bf16[256,128]{1,0:T(8,128)(2,1)} %get-tuple-element.45), channel_id=1, source_target_pairs={{0,6},{2,8},{4,2},{6,12},{8,14},{10,0},{12,10},{14,4},{16,22},{18,... | collective-permute-start | bytes 196616 | tf_op jit(solution)/shard_map/ppermute | solution.py:396
  13.2 2.8 %copy-start.1 = (s32[2]{0:T(128)S(1)}, s32[2]{0:T(128)}, u32[]{:S(2)}) copy-start(s32[2]{0:T(128)} %pad_add_fusion.place_ref) | copy-start | bytes 28
  13.2 7.1 %collective-permute-start.5 = (bf16[256,128]{1,0:T(8,128)(2,1)}, bf16[256,128]{1,0:T(8,128)(2,1)S(1)}, u32[]{:S(2)}, u32[]{:S(2)}) collective-permute-start(bf16[256,128]{1,0:T(8,128)(2,1)} %get-tuple-element.46), channel_id=1, source_target_pairs={{0,10},{2,4},{4,14},{6,0},{8,2},{10,12},{12,6},{14,8},{16,26},{18,... | collective-permute-start | bytes 196616 | tf_op jit(solution)/shard_map/ppermute | solution.py:396
  14.0 7.9 %copy-start = (bf16[256,128]{1,0:T(8,128)(2,1)S(1)}, bf16[256,128]{1,0:T(8,128)(2,1)}, u32[]{:S(2)}) copy-start(bf16[256,128]{1,0:T(8,128)(2,1)} %get-tuple-element.40.refs_0_) | copy-start | bytes 196612
  14.0 6.2 %collective-permute-start.6 = (bf16[256,128]{1,0:T(8,128)(2,1)}, bf16[256,128]{1,0:T(8,128)(2,1)S(1)}, u32[]{:S(2)}, u32[]{:S(2)}) collective-permute-start(bf16[256,128]{1,0:T(8,128)(2,1)} %get-tuple-element.47), channel_id=1, source_target_pairs={{0,12},{2,14},{4,8},{6,10},{8,4},{10,6},{12,0},{14,2},{16,28},{18,... | collective-permute-start | bytes 196616 | tf_op jit(solution)/shard_map/ppermute | solution.py:396
  17.6 5.8 %collective-permute-start.8 = (bf16[256,128]{1,0:T(8,128)(2,1)S(1)}, bf16[256,128]{1,0:T(8,128)(2,1)S(1)}, u32[]{:S(2)}, u32[]{:S(2)}) collective-permute-start(bf16[256,128]{1,0:T(8,128)(2,1)S(1)} %get-tuple-element.51), channel_id=1, source_target_pairs={{0,4},{2,10},{4,0},{6,14},{8,12},{10,2},{12,8},{14,6},{16,20},{18,... | collective-permute-start | bytes 196616 | tf_op jit(solution)/shard_map/ppermute | solution.py:396
  18.2 5.6 %collective-permute-start.9 = (bf16[256,128]{1,0:T(8,128)(2,1)S(1)}, bf16[256,128]{1,0:T(8,128)(2,1)S(1)}, u32[]{:S(2)}, u32[]{:S(2)}) collective-permute-start(bf16[256,128]{1,0:T(8,128)(2,1)S(1)} %get-tuple-element.52), channel_id=1, source_target_pairs={{0,8},{2,6},{4,12},{6,2},{8,0},{10,14},{12,4},{14,10},{16,24},{18,... | collective-permute-start | bytes 196616 | tf_op jit(solution)/shard_map/ppermute | solution.py:396
  19.2 6.0 %collective-permute-start.10 = (bf16[256,128]{1,0:T(8,128)(2,1)S(1)}, bf16[256,128]{1,0:T(8,128)(2,1)S(1)}, u32[]{:S(2)}, u32[]{:S(2)}) collective-permute-start(bf16[256,128]{1,0:T(8,128)(2,1)S(1)} %get-tuple-element.53), channel_id=1, source_target_pairs={{0,14},{2,0},{4,10},{6,4},{8,6},{10,8},{12,2},{14,12},{16,30},{18,... | collective-permute-start | bytes 196616 | tf_op jit(solution)/shard_map/ppermute | solution.py:396
  20.3 15.1 %collective-permute-start.12 = (bf16[256,128]{1,0:T(8,128)(2,1)S(1)}, bf16[256,128]{1,0:T(8,128)(2,1)S(1)}, u32[]{:S(2)}, u32[]{:S(2)}) collective-permute-start(bf16[256,128]{1,0:T(8,128)(2,1)S(1)} %get-tuple-element.56), channel_id=1, source_target_pairs={{0,2},{2,12},{4,6},{6,8},{8,10},{10,4},{12,14},{14,0},{16,18},{18,... | collective-permute-start | bytes 196616 | tf_op jit(solution)/shard_map/ppermute | solution.py:396
  20.3 15.1 %collective-permute-start.13 = (bf16[256,128]{1,0:T(8,128)(2,1)S(1)}, bf16[256,128]{1,0:T(8,128)(2,1)S(1)}, u32[]{:S(2)}, u32[]{:S(2)}) collective-permute-start(bf16[256,128]{1,0:T(8,128)(2,1)S(1)} %get-tuple-element.57), channel_id=1, source_target_pairs={{0,6},{2,8},{4,2},{6,12},{8,14},{10,0},{12,10},{14,4},{16,22},{18,... | collective-permute-start | bytes 196616 | tf_op jit(solution)/shard_map/ppermute | solution.py:396
  21.9 0.7 %copy-start.2 = (s32[2]{0:T(128)S(1)}, s32[2]{0:T(128)}, u32[]{:S(2)}) copy-start(s32[2]{0:T(128)} %get-tuple-element.39.place_ref) | copy-start | bytes 28
  23.4 12.0 %collective-permute-start.14 = (bf16[256,128]{1,0:T(8,128)(2,1)S(1)}, bf16[256,128]{1,0:T(8,128)(2,1)S(1)}, u32[]{:S(2)}, u32[]{:S(2)}) collective-permute-start(bf16[256,128]{1,0:T(8,128)(2,1)S(1)} %get-tuple-element.58), channel_id=1, source_target_pairs={{0,10},{2,4},{4,14},{6,0},{8,2},{10,12},{12,6},{14,8},{16,26},{18,... | collective-permute-start | bytes 196616 | tf_op jit(solution)/shard_map/ppermute | solution.py:396
  23.8 11.6 %collective-permute-start.15 = (bf16[256,128]{1,0:T(8,128)(2,1)S(1)}, bf16[256,128]{1,0:T(8,128)(2,1)S(1)}, u32[]{:S(2)}, u32[]{:S(2)}) collective-permute-start(bf16[256,128]{1,0:T(8,128)(2,1)S(1)} %get-tuple-element.59), channel_id=1, source_target_pairs={{0,12},{2,14},{4,8},{6,10},{8,4},{10,6},{12,0},{14,2},{16,28},{18,... | collective-permute-start | bytes 196616 | tf_op jit(solution)/shard_map/ppermute | solution.py:396
  25.2 10.1 %collective-permute-start.11 = (bf16[128,128]{1,0:T(8,128)(2,1)S(1)}, bf16[128,128]{1,0:T(8,128)(2,1)S(1)}, u32[]{:S(2)}, u32[]{:S(2)}) collective-permute-start(bf16[128,128]{1,0:T(8,128)(2,1)S(1)} %get-tuple-element.55.picks_ref), channel_id=1, source_target_pairs={{0,16},{2,18},{4,20},{6,22},{8,24},{10,26},{12,28},{14,30},{16,0},... | collective-permute-start | bytes 98312 | tf_op jit(solution)/shard_map/ppermute | solution.py:404
  37.9 7.2 %collective-permute-start.16 = (f32[128,128]{1,0:T(8,128)S(1)}, f32[128,128]{1,0:T(8,128)S(1)}, u32[]{:S(2)}, u32[]{:S(2)}) collective-permute-start(f32[128,128]{1,0:T(8,128)S(1)} %get-tuple-element.66), channel_id=1, source_target_pairs={{0,16},{2,18},{4,20},{6,22},{8,24},{10,26},{12,28},{14,30},{16,0},... | collective-permute-start | bytes 196616 | tf_op jit(solution)/shard_map/ppermute | solution.py:404
  48.0 5.0 %collective-permute-start.17 = (bf16[384,128]{1,0:T(8,128)(2,1)S(1)}, bf16[384,128]{1,0:T(8,128)(2,1)S(1)}, u32[]{:S(2)}, u32[]{:S(2)}) collective-permute-start(bf16[384,128]{1,0:T(8,128)(2,1)S(1)} %get-tuple-element.68), channel_id=1, source_target_pairs={{0,4},{2,10},{4,0},{6,14},{8,12},{10,2},{12,8},{14,6},{16,20},{18,... | collective-permute-start | bytes 294920 | tf_op jit(solution)/shard_map/ppermute | solution.py:396
  48.9 4.9 %collective-permute-start.18 = (bf16[384,128]{1,0:T(8,128)(2,1)S(1)}, bf16[384,128]{1,0:T(8,128)(2,1)S(1)}, u32[]{:S(2)}, u32[]{:S(2)}) collective-permute-start(bf16[384,128]{1,0:T(8,128)(2,1)S(1)} %get-tuple-element.69), channel_id=1, source_target_pairs={{0,8},{2,6},{4,12},{6,2},{8,0},{10,14},{12,4},{14,10},{16,24},{18,... | collective-permute-start | bytes 294920 | tf_op jit(solution)/shard_map/ppermute | solution.py:396
  49.4 6.5 %collective-permute-start.19 = (bf16[384,128]{1,0:T(8,128)(2,1)S(1)}, bf16[384,128]{1,0:T(8,128)(2,1)S(1)}, u32[]{:S(2)}, u32[]{:S(2)}) collective-permute-start(bf16[384,128]{1,0:T(8,128)(2,1)S(1)} %get-tuple-element.70), channel_id=1, source_target_pairs={{0,2},{2,12},{4,6},{6,8},{8,10},{10,4},{12,14},{14,0},{16,18},{18,... | collective-permute-start | bytes 294920 | tf_op jit(solution)/shard_map/ppermute | solution.py:396
  49.4 6.5 %collective-permute-start.20 = (bf16[384,128]{1,0:T(8,128)(2,1)S(1)}, bf16[384,128]{1,0:T(8,128)(2,1)S(1)}, u32[]{:S(2)}, u32[]{:S(2)}) collective-permute-start(bf16[384,128]{1,0:T(8,128)(2,1)S(1)} %get-tuple-element.71), channel_id=1, source_target_pairs={{0,14},{2,0},{4,10},{6,4},{8,6},{10,8},{12,2},{14,12},{16,30},{18,... | collective-permute-start | bytes 294920 | tf_op jit(solution)/shard_map/ppermute | solution.py:396
  52.1 5.5 %collective-permute-start.21 = (bf16[384,128]{1,0:T(8,128)(2,1)S(1)}, bf16[384,128]{1,0:T(8,128)(2,1)S(1)}, u32[]{:S(2)}, u32[]{:S(2)}) collective-permute-start(bf16[384,128]{1,0:T(8,128)(2,1)S(1)} %get-tuple-element.72), channel_id=1, source_target_pairs={{0,10},{2,4},{4,14},{6,0},{8,2},{10,12},{12,6},{14,8},{16,26},{18,... | collective-permute-start | bytes 294920 | tf_op jit(solution)/shard_map/ppermute | solution.py:396
  52.9 5.1 %collective-permute-start.22 = (bf16[384,128]{1,0:T(8,128)(2,1)S(1)}, bf16[384,128]{1,0:T(8,128)(2,1)S(1)}, u32[]{:S(2)}, u32[]{:S(2)}) collective-permute-start(bf16[384,128]{1,0:T(8,128)(2,1)S(1)} %get-tuple-element.73), channel_id=1, source_target_pairs={{0,6},{2,8},{4,2},{6,12},{8,14},{10,0},{12,10},{14,4},{16,22},{18,... | collective-permute-start | bytes 294920 | tf_op jit(solution)/shard_map/ppermute | solution.py:396
  53.8 7.2 %collective-permute-start.23 = (bf16[384,128]{1,0:T(8,128)(2,1)S(1)}, bf16[384,128]{1,0:T(8,128)(2,1)S(1)}, u32[]{:S(2)}, u32[]{:S(2)}) collective-permute-start(bf16[384,128]{1,0:T(8,128)(2,1)S(1)} %get-tuple-element.74), channel_id=1, source_target_pairs={{0,12},{2,14},{4,8},{6,10},{8,4},{10,6},{12,0},{14,2},{16,28},{18,... | collective-permute-start | bytes 294920 | tf_op jit(solution)/shard_map/ppermute | solution.py:396

commit v18 on v16

--- a/solution.py
+++ b/solution.py
@@ -77,7 +77,7 @@
 
 def swap_steps(group):
     if group == 8:
-        return [(2, 4), (4, 2), (7, 1), (1, 7), (3, 5), (5, 3), (6, 6)]
+        return [(2, 4), (4, 2), (6, 6), (3, 5), (5, 3), (7, 1), (1, 7)]
     return [(bits, bits) for bits in range(1, group)]
 
 
@@ -130,16 +130,16 @@
         out_ref[...] = stage_ref[place]
 
 
-def own_offset(head_count, place_ref, offset_ref):
-    return offset_ref[place_ref[1] * head_count + lax.rem(place_ref[0], head_count)]
+def own_offset(head_count, place_ref):
+    return place_ref[2 + place_ref[1] * head_count + lax.rem(place_ref[0], head_count)]
 
 
 def gather_kernel(
-    head_count, group, place_ref, offset_ref, keys_ref, after_ref, key_t_out, picks_out
+    head_count, group, place_ref, keys_ref, after_ref, key_t_out, picks_out
 ):
     rows = keys_ref.shape[0] // group
     picked = rows // DILATION_RATE
-    pick = pick_matrix(own_offset(head_count, place_ref, offset_ref), picked, rows)
+    pick = pick_matrix(own_offset(head_count, place_ref), picked, rows)
     for place in range(group):
         picks_out[place * picked : (place + 1) * picked, :] = dot_nn(
             pick, keys_ref[place * rows : (place + 1) * rows, :]
@@ -154,7 +154,7 @@
 
 
 def far_kernel(
-    head_count, group, others, place_ref, offset_ref, near_ref, start_ref, picks_ref, *refs
+    head_count, group, others, place_ref, near_ref, start_ref, picks_ref, *refs
 ):
     other_refs, refs = refs[:others], refs[others:]
     block_refs, refs = refs[:group], refs[group:]
@@ -164,7 +164,7 @@
     picked = rows // DILATION_RATE
     count = group * picked
     far = count * (1 + others)
-    pick = pick_matrix(own_offset(head_count, place_ref, offset_ref), picked, rows)
+    pick = pick_matrix(own_offset(head_count, place_ref), picked, rows)
     keys_ref[:near, :] = near_ref[...]
     for index, ref in enumerate([picks_ref, *other_refs]):
         keys_ref[near + index * count : near + (index + 1) * count, :] = ref[...]
@@ -277,7 +277,7 @@
         emit(index, jnp.concatenate([query_grad[:half], query_grad[half:]], 1))
 
 
-def some_kernel(head_count, steps, begin, place_ref, offset_ref, keys_ref, key_t_ref, *refs):
+def some_kernel(head_count, steps, begin, place_ref, keys_ref, key_t_ref, *refs):
     if not begin:
         start_ref, refs = refs[0], refs[1:]
     block_refs, (acc_ref, query_out, *scratch) = refs[:steps], refs[steps:]
@@ -287,13 +287,13 @@
         query_out[index] = query_grad
 
     near_blocks(
-        own_offset(head_count, place_ref, offset_ref), keys_ref, key_t_ref, block_refs,
+        own_offset(head_count, place_ref), keys_ref, key_t_ref, block_refs,
         *scratch, acc_ref, emit,
     )
 
 
 def end_kernel(
-    head_count, steps, others, place_ref, offset_ref, keys_ref, key_t_ref, start_ref, query_ref,
+    head_count, steps, others, place_ref, keys_ref, key_t_ref, start_ref, query_ref,
     later_query_ref, picked_query_ref, own_ref, *refs,
 ):
     back_refs, refs = refs[:others], refs[others:]
@@ -305,7 +305,7 @@
     acc_ref, *scratch = refs
     count = own_ref.shape[0]
     picked = count // group
-    offset = own_offset(head_count, place_ref, offset_ref)
+    offset = own_offset(head_count, place_ref)
     acc_ref[...] = start_ref[...]
 
     def finish(bits, query_grad):
@@ -342,12 +342,14 @@
     half = rows // 2
     for place, near_ref in zip(targets(place_ref[0], group), near_refs):
         stage_ref[place] = near_ref[...]
-    for head in range(head_count):
-        columns = slice(head * HEAD_SIZE, (head + 1) * HEAD_SIZE)
-        key_out[:, columns] = stage_ref[head, :rows, :HEAD_SIZE]
-        value_out[:, columns] = stage_ref[head, :rows, HEAD_SIZE:]
-        query_out[:half, columns] = stage_ref[head, rows:, :HEAD_SIZE]
-        query_out[half:, columns] = stage_ref[head, rows:, HEAD_SIZE:]
+    for head in range(0, head_count, 2):
+        columns = slice(head * HEAD_SIZE, (head + 2) * HEAD_SIZE)
+        pairs = [stage_ref[head, :rows, :], stage_ref[head + 1, :rows, :]]
+        packed = [stage_ref[head, rows:, :], stage_ref[head + 1, rows:, :]]
+        key_out[:, columns] = jnp.concatenate([pair[:, :HEAD_SIZE] for pair in pairs], 1)
+        value_out[:, columns] = jnp.concatenate([pair[:, HEAD_SIZE:] for pair in pairs], 1)
+        query_out[:half, columns] = jnp.concatenate([pair[:, :HEAD_SIZE] for pair in packed], 1)
+        query_out[half:, columns] = jnp.concatenate([pair[:, HEAD_SIZE:] for pair in packed], 1)
 
 
 def call(kernel, name, out_shape, scalars, operands, scratch=(), flops=0, space=VMEM, limit=40):
@@ -379,7 +381,8 @@
     place = jnp.stack(
         [lax.rem(lax.axis_index("context"), group), lax.axis_index("heads")]
     ).astype(jnp.int32)
-    scalars = [place, head_offsets]
+    place = jnp.concatenate([place, head_offsets])
+    scalars = [place]
 
     def swap(values, steps):
         result = [values[0]]

time: 60.2 us -> 58.4 us (0.970)
  waiting for transfers between devices: 9.15 us -> 8.15 us
  starting transfers between devices: 23.9 us -> 23.2 us
    ppermute x14, starting transfers between devices: 14 us -> 13.3 us  [swap(): result.append(lax.ppermute(value, 'context', pairs))]
  transfers between devices with their start and end apart: 18 -> 18, of which waited for: 8 -> 7; matrix products, arithmetic and copies ran while one was open for 0% -> 0% of each run, Pallas kernels for 30% -> 31%
where the time goes in v18:
time: 58.4 us; the launch traced here: 58 us
  Pallas kernels  25.1 us (43%)
  starting transfers between devices  23.2 us (40%)
  waiting for transfers between devices  8.15 us (14%)
  between operations  0.76 us (1%)
  local copies, waits for them, and re-layouts  0.67 us (1%)
    pallas_call x8, Pallas kernels, call(): pl.pallas_call(kernel, out_shape=tuple((jax.ShapeDtypeStruct(*shape) for...  25.1 us
    ppermute x14, starting transfers between devices, swap(): result.append(lax.ppermute(value, 'context', pairs))  13.3 us
    ppermute x14, waiting for transfers between devices, swap(): result.append(lax.ppermute(value, 'context', pairs))  6.5 us
    all_to_all x1, starting transfers between devices, body(): sent = lax.all_to_all(sent, 'context', 0, 0, axis_index_groups=groups)  3.95 us
    ppermute x1, starting transfers between devices, body(): upstreams.append(lax.ppermute(upstream, 'heads', pairs))  3 us
    ppermute x2, starting transfers between devices, segment_shift(): return lax.ppermute(value, 'context', pairs)  2.99 us
    all_to_all x1, waiting for transfers between devices, body(): sent = lax.all_to_all(sent, 'context', 0, 0, axis_index_groups=groups)  1.64 us
  transfers between devices with their start and end apart: 18, of which 7 were waited for; matrix products, arithmetic and copies ran while one was open for 0% of the time, Pallas kernels for 31%

profile of v18, /device:TPU:0, one launch (start us, length us, event | category | flops | bytes accessed | tf_op | source)
XLA Modules:
  0.0 58.0 jit_solution(17226040530738621795)
XLA Ops:
  0.6 3.0 %collective-permute-start = (bf16[128,1024]{1,0:T(8,128)(2,1)}, bf16[128,1024]{1,0:T(8,128)(2,1)S(1)}, u32[]{:S(2)}, u32[]{:S(2)}) collective-permute-start(bf16[128,1024]{1,0:T(8,128)(2,1)} %refs_0_.1), channel_id=1, source_target_pairs={{0,1},{1,0},{2,3},{3,2},{4,5},{5,4},{6,7},{7,6},{8,9},{9,8},{10,11... | collective-permute-start | bytes 786440 | tf_op jit(solution)/shard_map/ppermute | solution.py:404
  3.6 0.0 copy-start.1
  3.6 0.0 copy-start.2
  3.6 2.1 %pack_rows.1 = bf16[8,256,128]{2,1,0:T(8,128)(2,1)} custom-call(bf16[256,512]{1,0:T(8,128)(2,1)} %key_hbm.1, bf16[256,512]{1,0:T(8,128)(2,1)} %value_hbm.1), custom_call_target="tpu_custom_call" | custom-call | flops 2147483648 | bytes 2097152 | tf_op jit(solution)/shard_map/pack_rows/pallas_call | solution.py:356
  5.8 0.0 copy-start
  5.8 4.0 %all-to-all-start = ((bf16[8,256,128]{2,1,0:T(8,128)(2,1)}), bf16[8,256,128]{2,1,0:T(8,128)(2,1)S(1)}, u32[]{:S(2)}, u32[]{:S(2)}) async-start(bf16[8,256,128]{2,1,0:T(8,128)(2,1)} %pack_rows.1), calls=%async_computation | async-start | bytes 1048576 | tf_op jit(solution)/shard_map/all_to_all | solution.py:415
  9.7 0.0 copy-start.3
  9.7 0.7 %copy-done.3 = s32[16]{0:T(128)S(1)} copy-done((s32[16]{0:T(128)S(1)}, s32[16]{0:T(128)}, u32[]{:S(2)}) %copy-start.3) | copy-done | bytes 88
  10.4 0.1 pad_add_fusion.place_ref
  10.5 0.0 collective-permute-done.refs_1_
  10.5 0.0 copy-done.1
  10.5 0.0 copy-done.2
  10.5 0.0 copy-done
  10.5 1.5 %project_pack.1 = (bf16[256,128]{1,0:T(8,128)(2,1)S(1)}, bf16[256,128]{1,0:T(8,128)(2,1)S(1)}, bf16[256,128]{1,0:T(8,128)(2,1)S(1)}, bf16[256,128]{1,0:T(8,128)(...) custom-call(s32[18]{0:T(128)S(1)} %pad_add_fusion.place_ref, ...), custom_call_target="tpu_custom_call" | custom-call | flops 34359738368 | bytes 2097152 | tf_op jit(solution)/shard_map/project_pack/pallas_call | solution.py:356
  12.0 2.1 %collective-permute-start.1 = (bf16[256,128]{1,0:T(8,128)(2,1)S(1)}, bf16[256,128]{1,0:T(8,128)(2,1)S(1)}, u32[]{:S(2)}, u32[]{:S(2)}) collective-permute-start(bf16[256,128]{1,0:T(8,128)(2,1)S(1)} %get-tuple-element.31), channel_id=1, source_target_pairs={{0,4},{2,10},{4,0},{6,14},{8,12},{10,2},{12,8},{14,6},{16,20},{18,... | collective-permute-start | bytes 196616 | tf_op jit(solution)/shard_map/ppermute | solution.py:391
  14.1 1.5 %collective-permute-start.2 = (bf16[256,128]{1,0:T(8,128)(2,1)S(1)}, bf16[256,128]{1,0:T(8,128)(2,1)S(1)}, u32[]{:S(2)}, u32[]{:S(2)}) collective-permute-start(bf16[256,128]{1,0:T(8,128)(2,1)S(1)} %get-tuple-element.32), channel_id=1, source_target_pairs={{0,8},{2,6},{4,12},{6,2},{8,0},{10,14},{12,4},{14,10},{16,24},{18,... | collective-permute-start | bytes 196616 | tf_op jit(solution)/shard_map/ppermute | solution.py:391
  15.6 0.1 collective-permute-start.3
  15.7 0.9 %collective-permute-start.5 = (bf16[256,128]{1,0:T(8,128)(2,1)S(1)}, bf16[256,128]{1,0:T(8,128)(2,1)S(1)}, u32[]{:S(2)}, u32[]{:S(2)}) collective-permute-start(bf16[256,128]{1,0:T(8,128)(2,1)S(1)} %get-tuple-element.36), channel_id=1, source_target_pairs={{0,6},{2,8},{4,2},{6,12},{8,14},{10,0},{12,10},{14,4},{16,22},{18,... | collective-permute-start | bytes 196616 | tf_op jit(solution)/shard_map/ppermute | solution.py:391
  16.5 0.9 %collective-permute-start.6 = (bf16[256,128]{1,0:T(8,128)(2,1)S(1)}, bf16[256,128]{1,0:T(8,128)(2,1)S(1)}, u32[]{:S(2)}, u32[]{:S(2)}) collective-permute-start(bf16[256,128]{1,0:T(8,128)(2,1)S(1)} %get-tuple-element.37), channel_id=1, source_target_pairs={{0,10},{2,4},{4,14},{6,0},{8,2},{10,12},{12,6},{14,8},{16,26},{18,... | collective-permute-start | bytes 196616 | tf_op jit(solution)/shard_map/ppermute | solution.py:391
  17.4 1.6 %all-to-all-done = bf16[8,256,128]{2,1,0:T(8,128)(2,1)S(1)} async-done(((bf16[8,256,128]{2,1,0:T(8,128)(2,1)}), bf16[8,256,128]{2,1,0:T(8,128)(2,1)S(1)}, u32[]{:S(2)}, u32[]{:S(2)}) %all-to-all-start) | async-done | bytes 524320 | tf_op jit(solution)/shard_map/all_to_all | solution.py:415
  19.0 0.7 %gather_keys.1 = (bf16[64,2048]{1,0:T(8,128)(2,1)S(1)}, bf16[128,128]{1,0:T(8,128)(2,1)S(1)}) custom-call(s32[18]{0:T(128)S(1)} %pad_add_fusion.place_ref, bf16[2048,128]{1,0:T(8,128)(2,1)S(1)} %bitcast.3, bf16[256,128]{1,0:T(8,128)(2,1)S(1)} %get-tuple-element.29.after_ref.refs_0_.refs_1_), custom_call_target="tpu_custom_call" | custom-call | bytes 2097152 | tf_op jit(solution)/shard_map/gather_keys/pallas_call | solution.py:356
  19.8 0.2 collective-permute-done.1.refs_1_.refs_2_
  20.0 0.7 %collective-permute-start.7 = (bf16[256,128]{1,0:T(8,128)(2,1)S(1)}, bf16[256,128]{1,0:T(8,128)(2,1)S(1)}, u32[]{:S(2)}, u32[]{:S(2)}) collective-permute-start(bf16[256,128]{1,0:T(8,128)(2,1)S(1)} %get-tuple-element.38), channel_id=1, source_target_pairs={{0,14},{2,0},{4,10},{6,4},{8,6},{10,8},{12,2},{14,12},{16,30},{18,... | collective-permute-start | bytes 196616 | tf_op jit(solution)/shard_map/ppermute | solution.py:391
  20.7 0.0 collective-permute-done.2.refs_2_.refs_3_
  20.7 0.0 collective-permute-start.8
  20.7 2.1 %collective-permute-done.3.refs_3_.refs_4_ = bf16[256,128]{1,0:T(8,128)(2,1)S(1)} collective-permute-done((bf16[256,128]{1,0:T(8,128)(2,1)S(1)}, bf16[256,128]{1,0:T(8,128)(2,1)S(1)}, u32[]{:S(2)}, u32[]{:S(2)}) %collective-permute-start.3) | collective-permute-done | bytes 65568 | tf_op jit(solution)/shard_map/ppermute | solution.py:391
  22.8 2.6 %collective-permute-start.4 = (bf16[128,128]{1,0:T(8,128)(2,1)S(1)}, bf16[128,128]{1,0:T(8,128)(2,1)S(1)}, u32[]{:S(2)}, u32[]{:S(2)}) collective-permute-start(bf16[128,128]{1,0:T(8,128)(2,1)S(1)} %get-tuple-element.35.picks_ref), channel_id=1, source_target_pairs={{0,16},{2,18},{4,20},{6,22},{8,24},{10,26},{12,28},{14,30},{16,0},... | collective-permute-start | bytes 98312 | tf_op jit(solution)/shard_map/ppermute | solution.py:399
  25.3 7.6 %first_rows.1 = (f32[2048,128]{1,0:T(8,128)S(1)}, bf16[4,128,128]{2,1,0:T(8,128)(2,1)S(1)}) custom-call(s32[18]{0:T(128)S(1)} %pad_add_fusion.place_ref, bf16[2048,128]{1,0:T(8,128)(2,1)S(1)} %bitcast.4, bf16[64,2048]{1,0:T(8,128)(2,1)S(1)} %get-tuple-element.30.key_t_ref, bf16[256,128]{1,0:T(8,128)(2,1)S(1)} %get-tuple-element.29.after_ref.refs_0_.refs_1_, ...), custom_call_target="tpu_custom_call" | custom-call | flops 8053063680 | bytes 2097152 | tf_op jit(solution)/shard_map/first_rows/pallas_call | solution.py:356
  32.9 0.0 collective-permute-done.5.refs_5_.refs_1_
  32.9 0.0 collective-permute-done.6.refs_6_.refs_2_
  32.9 0.0 collective-permute-done.7.refs_7_.refs_3_
  32.9 0.0 collective-permute-done.8.refs_8_.refs_1_
  33.0 0.0 collective-permute-done.4.refs_0_
  33.0 2.5 %picked_rows.1 = (f32[2048,128]{1,0:T(8,128)S(1)}, bf16[256,128]{1,0:T(8,128)(2,1)S(1)}, f32[128,128]{1,0:T(8,128)S(1)}, f32[128,128]{1,0:T(8,128)S(1)}) custom-call(s32[18]{0:T(128)S(1)} %pad_add_fusion.place_ref, bf16[2048,128]{1,0:T(8,128)(2,1)S(1)} %bitcast.5, f32[2048,128]{1,0:T(8,128)S(1)} %get-tuple-element.34.start_ref, ...), custom_call_target="tpu_custom_call" | custom-call | flops 671088640 | bytes 2097152 | tf_op jit(solution)/shard_map/picked_rows/pallas_call | solution.py:356
  35.4 0.4 collective-permute-start.9
  35.8 6.1 %second_rows.1 = (f32[2048,128]{1,0:T(8,128)S(1)}, bf16[3,128,128]{2,1,0:T(8,128)(2,1)S(1)}) custom-call(s32[18]{0:T(128)S(1)} %pad_add_fusion.place_ref, bf16[2048,128]{1,0:T(8,128)(2,1)S(1)} %bitcast.6, bf16[64,2048]{1,0:T(8,128)(2,1)S(1)} %get-tuple-element.30.key_t_ref, f32[2048,128]{1,0:T(8,128)S(1)} %get-tuple-element.40.refs_0_, ...), custom_call_target="tpu_custom_call" | custom-call | flops 8053063680 | bytes 2097152 | tf_op jit(solution)/shard_map/second_rows/pallas_call | solution.py:356
  41.9 0.0 collective-permute-done.9.refs_0_
  42.0 2.9 %last_rows.1 = (bf16[384,128]{1,0:T(8,128)(2,1)S(1)}, bf16[384,128]{1,0:T(8,128)(2,1)S(1)}, bf16[384,128]{1,0:T(8,128)(2,1)S(1)}, bf16[384,128]{1,0:T(8,128)(2,1...) custom-call(s32[18]{0:T(128)S(1)} %pad_add_fusion.place_ref, ...), custom_call_target="tpu_custom_call" | custom-call | flops 2013265920 | bytes 2097152 | tf_op jit(solution)/shard_map/last_rows/pallas_call | solution.py:356
  44.9 0.6 %collective-permute-start.10 = (bf16[384,128]{1,0:T(8,128)(2,1)S(1)}, bf16[384,128]{1,0:T(8,128)(2,1)S(1)}, u32[]{:S(2)}, u32[]{:S(2)}) collective-permute-start(bf16[384,128]{1,0:T(8,128)(2,1)S(1)} %get-tuple-element.48), channel_id=1, source_target_pairs={{0,4},{2,10},{4,0},{6,14},{8,12},{10,2},{12,8},{14,6},{16,20},{18,... | collective-permute-start | bytes 294920 | tf_op jit(solution)/shard_map/ppermute | solution.py:391
  45.5 0.6 %collective-permute-start.11 = (bf16[384,128]{1,0:T(8,128)(2,1)S(1)}, bf16[384,128]{1,0:T(8,128)(2,1)S(1)}, u32[]{:S(2)}, u32[]{:S(2)}) collective-permute-start(bf16[384,128]{1,0:T(8,128)(2,1)S(1)} %get-tuple-element.49), channel_id=1, source_target_pairs={{0,8},{2,6},{4,12},{6,2},{8,0},{10,14},{12,4},{14,10},{16,24},{18,... | collective-permute-start | bytes 294920 | tf_op jit(solution)/shard_map/ppermute | solution.py:391
  46.1 2.3 %collective-permute-start.12 = (bf16[384,128]{1,0:T(8,128)(2,1)S(1)}, bf16[384,128]{1,0:T(8,128)(2,1)S(1)}, u32[]{:S(2)}, u32[]{:S(2)}) collective-permute-start(bf16[384,128]{1,0:T(8,128)(2,1)S(1)} %get-tuple-element.50), channel_id=1, source_target_pairs={{0,12},{2,14},{4,8},{6,10},{8,4},{10,6},{12,0},{14,2},{16,28},{18,... | collective-permute-start | bytes 294920 | tf_op jit(solution)/shard_map/ppermute | solution.py:391
  48.4 0.0 collective-permute-start.13
  48.4 1.7 %collective-permute-start.14 = (bf16[384,128]{1,0:T(8,128)(2,1)S(1)}, bf16[384,128]{1,0:T(8,128)(2,1)S(1)}, u32[]{:S(2)}, u32[]{:S(2)}) collective-permute-start(bf16[384,128]{1,0:T(8,128)(2,1)S(1)} %get-tuple-element.52), channel_id=1, source_target_pairs={{0,6},{2,8},{4,2},{6,12},{8,14},{10,0},{12,10},{14,4},{16,22},{18,... | collective-permute-start | bytes 294920 | tf_op jit(solution)/shard_map/ppermute | solution.py:391
  50.2 0.0 collective-permute-done.10.refs_1_
  50.2 0.0 collective-permute-start.15
  50.2 0.8 %collective-permute-done.11.refs_2_ = bf16[384,128]{1,0:T(8,128)(2,1)S(1)} collective-permute-done((bf16[384,128]{1,0:T(8,128)(2,1)S(1)}, bf16[384,128]{1,0:T(8,128)(2,1)S(1)}, u32[]{:S(2)}, u32[]{:S(2)}) %collective-permute-start.11) | collective-permute-done | bytes 98336 | tf_op jit(solution)/shard_map/ppermute | solution.py:391
  51.0 1.9 %collective-permute-start.16 = (bf16[384,128]{1,0:T(8,128)(2,1)S(1)}, bf16[384,128]{1,0:T(8,128)(2,1)S(1)}, u32[]{:S(2)}, u32[]{:S(2)}) collective-permute-start(bf16[384,128]{1,0:T(8,128)(2,1)S(1)} %get-tuple-element.54), channel_id=1, source_target_pairs={{0,14},{2,0},{4,10},{6,4},{8,6},{10,8},{12,2},{14,12},{16,30},{18,... | collective-permute-start | bytes 294920 | tf_op jit(solution)/shard_map/ppermute | solution.py:391
  52.9 0.9 %collective-permute-done.12.refs_3_ = bf16[384,128]{1,0:T(8,128)(2,1)S(1)} collective-permute-done((bf16[384,128]{1,0:T(8,128)(2,1)S(1)}, bf16[384,128]{1,0:T(8,128)(2,1)S(1)}, u32[]{:S(2)}, u32[]{:S(2)}) %collective-permute-start.12) | collective-permute-done | bytes 98336 | tf_op jit(solution)/shard_map/ppermute | solution.py:391
  53.8 0.3 collective-permute-done.13.refs_4_
  54.1 0.0 collective-permute-done.14.refs_5_
  54.1 2.2 %collective-permute-done.15.refs_6_ = bf16[384,128]{1,0:T(8,128)(2,1)S(1)} collective-permute-done((bf16[384,128]{1,0:T(8,128)(2,1)S(1)}, bf16[384,128]{1,0:T(8,128)(2,1)S(1)}, u32[]{:S(2)}, u32[]{:S(2)}) %collective-permute-start.15) | collective-permute-done | bytes 98336 | tf_op jit(solution)/shard_map/ppermute | solution.py:391
  56.3 0.0 collective-permute-done.16.refs_7_
  56.3 1.7 %unpack.1 = (bf16[256,512]{1,0:T(8,128)(2,1)}, bf16[256,512]{1,0:T(8,128)(2,1)}, bf16[256,512]{1,0:T(8,128)(2,1)}) custom-call(s32[18]{0:T(128)S(1)} %pad_add_fusion.place_ref, bf16[384,128]{1,0:T(8,128)(2,1)S(1)} %get-tuple-element.47.refs_0_, bf16[384,128]{1,0:T(8,128)(2,1)S(1)} %collective-permute-done.10.refs_1_, ...), custom_call_target="tpu_custom_call" | custom-call | bytes 2097152 | tf_op jit(solution)/shard_map/unpack/pallas_call | solution.py:356
Async XLA Ops:
  0.6 9.8 %collective-permute-start = (bf16[128,1024]{1,0:T(8,128)(2,1)}, bf16[128,1024]{1,0:T(8,128)(2,1)S(1)}, u32[]{:S(2)}, u32[]{:S(2)}) collective-permute-start(bf16[128,1024]{1,0:T(8,128)(2,1)} %refs_0_.1), channel_id=1, source_target_pairs={{0,1},{1,0},{2,3},{3,2},{4,5},{5,4},{6,7},{7,6},{8,9},{9,8},{10,11... | collective-permute-start | bytes 786440 | tf_op jit(solution)/shard_map/ppermute | solution.py:404
  3.6 6.8 %copy-start.1 = (bf16[256,512]{1,0:T(8,128)(2,1)S(1)}, bf16[256,512]{1,0:T(8,128)(2,1)}, u32[]{:S(2)}) copy-start(bf16[256,512]{1,0:T(8,128)(2,1)} %query_ref.1) | copy-start | bytes 786436
  3.6 6.8 %copy-start.2 = (bf16[128,1024]{1,0:T(8,128)(2,1)S(1)}, bf16[128,1024]{1,0:T(8,128)(2,1)}, u32[]{:S(2)}) copy-start(bf16[128,1024]{1,0:T(8,128)(2,1)} %refs_0_.1) | copy-start | bytes 786436
  5.8 4.7 %copy-start = (bf16[512,1024]{1,0:T(8,128)(2,1)S(1)}, bf16[512,1024]{1,0:T(8,128)(2,1)}, u32[]{:S(2)}) copy-start(bf16[512,1024]{1,0:T(8,128)(2,1)} %weight_ref.1) | copy-start | bytes 3145732
  5.8 13.3 %all-to-all-start = ((bf16[8,256,128]{2,1,0:T(8,128)(2,1)}), bf16[8,256,128]{2,1,0:T(8,128)(2,1)S(1)}, u32[]{:S(2)}, u32[]{:S(2)}) async-start(bf16[8,256,128]{2,1,0:T(8,128)(2,1)} %pack_rows.1), calls=%async_computation | async-start | bytes 1048576 | tf_op jit(solution)/shard_map/all_to_all | solution.py:415
  9.7 0.7 %copy-start.3 = (s32[16]{0:T(128)S(1)}, s32[16]{0:T(128)}, u32[]{:S(2)}) copy-start(s32[16]{0:T(128)} %param.11) | copy-start | bytes 196
  12.0 8.0 %collective-permute-start.1 = (bf16[256,128]{1,0:T(8,128)(2,1)S(1)}, bf16[256,128]{1,0:T(8,128)(2,1)S(1)}, u32[]{:S(2)}, u32[]{:S(2)}) collective-permute-start(bf16[256,128]{1,0:T(8,128)(2,1)S(1)} %get-tuple-element.31), channel_id=1, source_target_pairs={{0,4},{2,10},{4,0},{6,14},{8,12},{10,2},{12,8},{14,6},{16,20},{18,... | collective-permute-start | bytes 196616 | tf_op jit(solution)/shard_map/ppermute | solution.py:391
  14.1 6.6 %collective-permute-start.2 = (bf16[256,128]{1,0:T(8,128)(2,1)S(1)}, bf16[256,128]{1,0:T(8,128)(2,1)S(1)}, u32[]{:S(2)}, u32[]{:S(2)}) collective-permute-start(bf16[256,128]{1,0:T(8,128)(2,1)S(1)} %get-tuple-element.32), channel_id=1, source_target_pairs={{0,8},{2,6},{4,12},{6,2},{8,0},{10,14},{12,4},{14,10},{16,24},{18,... | collective-permute-start | bytes 196616 | tf_op jit(solution)/shard_map/ppermute | solution.py:391
  15.6 7.2 %collective-permute-start.3 = (bf16[256,128]{1,0:T(8,128)(2,1)S(1)}, bf16[256,128]{1,0:T(8,128)(2,1)S(1)}, u32[]{:S(2)}, u32[]{:S(2)}) collective-permute-start(bf16[256,128]{1,0:T(8,128)(2,1)S(1)} %get-tuple-element.33), channel_id=1, source_target_pairs={{0,12},{2,14},{4,8},{6,10},{8,4},{10,6},{12,0},{14,2},{16,28},{18,... | collective-permute-start | bytes 196616 | tf_op jit(solution)/shard_map/ppermute | solution.py:391
  15.7 17.3 %collective-permute-start.5 = (bf16[256,128]{1,0:T(8,128)(2,1)S(1)}, bf16[256,128]{1,0:T(8,128)(2,1)S(1)}, u32[]{:S(2)}, u32[]{:S(2)}) collective-permute-start(bf16[256,128]{1,0:T(8,128)(2,1)S(1)} %get-tuple-element.36), channel_id=1, source_target_pairs={{0,6},{2,8},{4,2},{6,12},{8,14},{10,0},{12,10},{14,4},{16,22},{18,... | collective-permute-start | bytes 196616 | tf_op jit(solution)/shard_map/ppermute | solution.py:391
  16.5 16.4 %collective-permute-start.6 = (bf16[256,128]{1,0:T(8,128)(2,1)S(1)}, bf16[256,128]{1,0:T(8,128)(2,1)S(1)}, u32[]{:S(2)}, u32[]{:S(2)}) collective-permute-start(bf16[256,128]{1,0:T(8,128)(2,1)S(1)} %get-tuple-element.37), channel_id=1, source_target_pairs={{0,10},{2,4},{4,14},{6,0},{8,2},{10,12},{12,6},{14,8},{16,26},{18,... | collective-permute-start | bytes 196616 | tf_op jit(solution)/shard_map/ppermute | solution.py:391
  20.0 13.0 %collective-permute-start.7 = (bf16[256,128]{1,0:T(8,128)(2,1)S(1)}, bf16[256,128]{1,0:T(8,128)(2,1)S(1)}, u32[]{:S(2)}, u32[]{:S(2)}) collective-permute-start(bf16[256,128]{1,0:T(8,128)(2,1)S(1)} %get-tuple-element.38), channel_id=1, source_target_pairs={{0,14},{2,0},{4,10},{6,4},{8,6},{10,8},{12,2},{14,12},{16,30},{18,... | collective-permute-start | bytes 196616 | tf_op jit(solution)/shard_map/ppermute | solution.py:391
  20.7 12.3 %collective-permute-start.8 = (bf16[256,128]{1,0:T(8,128)(2,1)S(1)}, bf16[256,128]{1,0:T(8,128)(2,1)S(1)}, u32[]{:S(2)}, u32[]{:S(2)}) collective-permute-start(bf16[256,128]{1,0:T(8,128)(2,1)S(1)} %get-tuple-element.39), channel_id=1, source_target_pairs={{0,2},{2,12},{4,6},{6,8},{8,10},{10,4},{12,14},{14,0},{16,18},{18,... | collective-permute-start | bytes 196616 | tf_op jit(solution)/shard_map/ppermute | solution.py:391
  22.8 10.2 %collective-permute-start.4 = (bf16[128,128]{1,0:T(8,128)(2,1)S(1)}, bf16[128,128]{1,0:T(8,128)(2,1)S(1)}, u32[]{:S(2)}, u32[]{:S(2)}) collective-permute-start(bf16[128,128]{1,0:T(8,128)(2,1)S(1)} %get-tuple-element.35.picks_ref), channel_id=1, source_target_pairs={{0,16},{2,18},{4,20},{6,22},{8,24},{10,26},{12,28},{14,30},{16,0},... | collective-permute-start | bytes 98312 | tf_op jit(solution)/shard_map/ppermute | solution.py:399
  35.4 6.5 %collective-permute-start.9 = (f32[128,128]{1,0:T(8,128)S(1)}, f32[128,128]{1,0:T(8,128)S(1)}, u32[]{:S(2)}, u32[]{:S(2)}) collective-permute-start(f32[128,128]{1,0:T(8,128)S(1)} %get-tuple-element.46), channel_id=1, source_target_pairs={{0,16},{2,18},{4,20},{6,22},{8,24},{10,26},{12,28},{14,30},{16,0},... | collective-permute-start | bytes 196616 | tf_op jit(solution)/shard_map/ppermute | solution.py:399
  44.9 5.3 %collective-permute-start.10 = (bf16[384,128]{1,0:T(8,128)(2,1)S(1)}, bf16[384,128]{1,0:T(8,128)(2,1)S(1)}, u32[]{:S(2)}, u32[]{:S(2)}) collective-permute-start(bf16[384,128]{1,0:T(8,128)(2,1)S(1)} %get-tuple-element.48), channel_id=1, source_target_pairs={{0,4},{2,10},{4,0},{6,14},{8,12},{10,2},{12,8},{14,6},{16,20},{18,... | collective-permute-start | bytes 294920 | tf_op jit(solution)/shard_map/ppermute | solution.py:391
  45.5 5.5 %collective-permute-start.11 = (bf16[384,128]{1,0:T(8,128)(2,1)S(1)}, bf16[384,128]{1,0:T(8,128)(2,1)S(1)}, u32[]{:S(2)}, u32[]{:S(2)}) collective-permute-start(bf16[384,128]{1,0:T(8,128)(2,1)S(1)} %get-tuple-element.49), channel_id=1, source_target_pairs={{0,8},{2,6},{4,12},{6,2},{8,0},{10,14},{12,4},{14,10},{16,24},{18,... | collective-permute-start | bytes 294920 | tf_op jit(solution)/shard_map/ppermute | solution.py:391
  46.1 7.7 %collective-permute-start.12 = (bf16[384,128]{1,0:T(8,128)(2,1)S(1)}, bf16[384,128]{1,0:T(8,128)(2,1)S(1)}, u32[]{:S(2)}, u32[]{:S(2)}) collective-permute-start(bf16[384,128]{1,0:T(8,128)(2,1)S(1)} %get-tuple-element.50), channel_id=1, source_target_pairs={{0,12},{2,14},{4,8},{6,10},{8,4},{10,6},{12,0},{14,2},{16,28},{18,... | collective-permute-start | bytes 294920 | tf_op jit(solution)/shard_map/ppermute | solution.py:391
  48.4 5.7 %collective-permute-start.13 = (bf16[384,128]{1,0:T(8,128)(2,1)S(1)}, bf16[384,128]{1,0:T(8,128)(2,1)S(1)}, u32[]{:S(2)}, u32[]{:S(2)}) collective-permute-start(bf16[384,128]{1,0:T(8,128)(2,1)S(1)} %get-tuple-element.51), channel_id=1, source_target_pairs={{0,10},{2,4},{4,14},{6,0},{8,2},{10,12},{12,6},{14,8},{16,26},{18,... | collective-permute-start | bytes 294920 | tf_op jit(solution)/shard_map/ppermute | solution.py:391
  48.4 5.7 %collective-permute-start.14 = (bf16[384,128]{1,0:T(8,128)(2,1)S(1)}, bf16[384,128]{1,0:T(8,128)(2,1)S(1)}, u32[]{:S(2)}, u32[]{:S(2)}) collective-permute-start(bf16[384,128]{1,0:T(8,128)(2,1)S(1)} %get-tuple-element.52), channel_id=1, source_target_pairs={{0,6},{2,8},{4,2},{6,12},{8,14},{10,0},{12,10},{14,4},{16,22},{18,... | collective-permute-start | bytes 294920 | tf_op jit(solution)/shard_map/ppermute | solution.py:391
  50.2 6.1 %collective-permute-start.15 = (bf16[384,128]{1,0:T(8,128)(2,1)S(1)}, bf16[384,128]{1,0:T(8,128)(2,1)S(1)}, u32[]{:S(2)}, u32[]{:S(2)}) collective-permute-start(bf16[384,128]{1,0:T(8,128)(2,1)S(1)} %get-tuple-element.53), channel_id=1, source_target_pairs={{0,2},{2,12},{4,6},{6,8},{8,10},{10,4},{12,14},{14,0},{16,18},{18,... | collective-permute-start | bytes 294920 | tf_op jit(solution)/shard_map/ppermute | solution.py:391
  51.0 5.3 %collective-permute-start.16 = (bf16[384,128]{1,0:T(8,128)(2,1)S(1)}, bf16[384,128]{1,0:T(8,128)(2,1)S(1)}, u32[]{:S(2)}, u32[]{:S(2)}) collective-permute-start(bf16[384,128]{1,0:T(8,128)(2,1)S(1)} %get-tuple-element.54), channel_id=1, source_target_pairs={{0,14},{2,0},{4,10},{6,4},{8,6},{10,8},{12,2},{14,12},{16,30},{18,... | collective-permute-start | bytes 294920 | tf_op jit(solution)/shard_map/ppermute | solution.py:391

commit v19 on v18

--- a/solution.py
+++ b/solution.py
@@ -77,7 +77,7 @@
 
 def swap_steps(group):
     if group == 8:
-        return [(2, 4), (4, 2), (6, 6), (3, 5), (5, 3), (7, 1), (1, 7)]
+        return [(2, 4), (4, 2), (7, 1), (1, 7), (3, 5), (5, 3), (6, 6)]
     return [(bits, bits) for bits in range(1, group)]
 
 
@@ -384,15 +384,17 @@
     place = jnp.concatenate([place, head_offsets])
     scalars = [place]
 
-    def swap(values, steps):
-        result = [values[0]]
-        for step, value in zip(steps, values[1:]):
+    def swap(values, steps, order=None):
+        result = list(values)
+        for index in order or range(1, group):
+            step = steps[index - 1]
             pairs = [(source, source ^ step[source % 2]) for source in range(devices)]
-            result.append(lax.ppermute(value, "context", pairs))
+            result[index] = lax.ppermute(values[index], "context", pairs)
         return result
 
     out_steps = swap_steps(group)
     back_steps = [mirrored(step) for step in out_steps]
+    back_order = [1, 2, 7, 5, 6, 3, 4] if group == 8 else None
 
     def segment_shift(value, shift):
         pairs = [(source, (source + shift * group) % devices) for source in range(devices)]
@@ -428,7 +430,7 @@
         scalars, [keys, blocks_send[0]],
     )
     other_picks = [segment_shift(picks, shift) for shift in range(1, others + 1)]
-    steps = group // 2
+    steps = group // 2 - 1
     scratch = [
         ((2, near, rows), f32), ((2, near, rows), f32), ((2, near, 2 * rows), bf16),
         ((2, near // STRIP, 8, rows), f32),
@@ -466,13 +468,13 @@
         [
             keys, key_t, acc, query_early, query_late, picked_query, own_terms, *back, blocks[-1],
         ],
-        [((near, PAIR), f32)] + scratch, half_flops // steps,
+        [((near, PAIR), f32)] + scratch, half_flops // 4,
     )
     return tuple(
         call(
             functools.partial(unpack_kernel, head_count, group), "unpack",
             [((rows, width), bf16)] * 3,
-            [place], swap(near_send, back_steps),
+            [place], swap(near_send, back_steps, back_order),
             [((group, rows + half, PAIR), bf16)],
         )
     )

time: 58.4 us -> 59.9 us (1.026)
  starting transfers between devices: 23.2 us -> 25.4 us
    ppermute x14, starting transfers between devices: 13.3 us -> 15.4 us  [swap(): result[index] = lax.ppermute(values[index], 'context', pairs)]
  transfers between devices with their start and end apart: 18 -> 18, of which waited for: 7 -> 7; matrix products, arithmetic and copies ran while one was open for 0% -> 0% of each run, Pallas kernels for 31% -> 30%
where the time goes in v19:
time: 59.9 us; the launch traced here: 59.7 us
  starting transfers between devices  25.4 us (42%)
  Pallas kernels  25.1 us (42%)
  waiting for transfers between devices  7.68 us (13%)
  between operations  0.76 us (1%)
  local copies, waits for them, and re-layouts  0.67 us (1%)
    pallas_call x8, Pallas kernels, call(): pl.pallas_call(kernel, out_shape=tuple((jax.ShapeDtypeStruct(*shape) for...  25.1 us
    ppermute x14, starting transfers between devices, swap(): result[index] = lax.ppermute(values[index], 'context', pairs)  15.4 us
    ppermute x14, waiting for transfers between devices, swap(): result[index] = lax.ppermute(values[index], 'context', pairs)  6.6 us
    all_to_all x1, starting transfers between devices, body(): sent = lax.all_to_all(sent, 'context', 0, 0, axis_index_groups=groups)  3.95 us
    ppermute x1, starting transfers between devices, body(): upstreams.append(lax.ppermute(upstream, 'heads', pairs))  3 us
    ppermute x2, starting transfers between devices, segment_shift(): return lax.ppermute(value, 'context', pairs)  3 us
  transfers between devices with their start and end apart: 18, of which 7 were waited for; matrix products, arithmetic and copies ran while one was open for 0% of the time, Pallas kernels for 30%

profile of v19, /device:TPU:0, one launch (start us, length us, event | category | flops | bytes accessed | tf_op | source)
XLA Modules:
  0.0 59.7 jit_solution(4316430438209902998)
XLA Ops:
  0.6 3.0 %collective-permute-start = (bf16[128,1024]{1,0:T(8,128)(2,1)}, bf16[128,1024]{1,0:T(8,128)(2,1)S(1)}, u32[]{:S(2)}, u32[]{:S(2)}) collective-permute-start(bf16[128,1024]{1,0:T(8,128)(2,1)} %refs_0_.1), channel_id=1, source_target_pairs={{0,1},{1,0},{2,3},{3,2},{4,5},{5,4},{6,7},{7,6},{8,9},{9,8},{10,11... | collective-permute-start | bytes 786440 | tf_op jit(solution)/shard_map/ppermute | solution.py:406
  3.6 0.0 copy-start.1
  3.6 0.0 copy-start.2
  3.6 2.1 %pack_rows.1 = bf16[8,256,128]{2,1,0:T(8,128)(2,1)} custom-call(bf16[256,512]{1,0:T(8,128)(2,1)} %key_hbm.1, bf16[256,512]{1,0:T(8,128)(2,1)} %value_hbm.1), custom_call_target="tpu_custom_call" | custom-call | flops 2147483648 | bytes 2097152 | tf_op jit(solution)/shard_map/pack_rows/pallas_call | solution.py:356
  5.8 0.0 copy-start
  5.8 4.0 %all-to-all-start = ((bf16[8,256,128]{2,1,0:T(8,128)(2,1)}), bf16[8,256,128]{2,1,0:T(8,128)(2,1)S(1)}, u32[]{:S(2)}, u32[]{:S(2)}) async-start(bf16[8,256,128]{2,1,0:T(8,128)(2,1)} %pack_rows.1), calls=%async_computation | async-start | bytes 1048576 | tf_op jit(solution)/shard_map/all_to_all | solution.py:417
  9.7 0.0 copy-start.3
  9.7 0.7 %copy-done.3 = s32[16]{0:T(128)S(1)} copy-done((s32[16]{0:T(128)S(1)}, s32[16]{0:T(128)}, u32[]{:S(2)}) %copy-start.3) | copy-done | bytes 88
  10.4 0.1 pad_add_fusion.place_ref
  10.5 0.0 collective-permute-done.refs_1_
  10.5 0.0 copy-done.1
  10.5 0.0 copy-done.2
  10.5 0.0 copy-done
  10.5 1.5 %project_pack.1 = (bf16[256,128]{1,0:T(8,128)(2,1)S(1)}, bf16[256,128]{1,0:T(8,128)(2,1)S(1)}, bf16[256,128]{1,0:T(8,128)(2,1)S(1)}, bf16[256,128]{1,0:T(8,128)(...) custom-call(s32[18]{0:T(128)S(1)} %pad_add_fusion.place_ref, ...), custom_call_target="tpu_custom_call" | custom-call | flops 34359738368 | bytes 2097152 | tf_op jit(solution)/shard_map/project_pack/pallas_call | solution.py:356
  12.0 2.1 %collective-permute-start.1 = (bf16[256,128]{1,0:T(8,128)(2,1)S(1)}, bf16[256,128]{1,0:T(8,128)(2,1)S(1)}, u32[]{:S(2)}, u32[]{:S(2)}) collective-permute-start(bf16[256,128]{1,0:T(8,128)(2,1)S(1)} %get-tuple-element.31), channel_id=1, source_target_pairs={{0,4},{2,10},{4,0},{6,14},{8,12},{10,2},{12,8},{14,6},{16,20},{18,... | collective-permute-start | bytes 196616 | tf_op jit(solution)/shard_map/ppermute | solution.py:392
  14.1 1.5 %collective-permute-start.2 = (bf16[256,128]{1,0:T(8,128)(2,1)S(1)}, bf16[256,128]{1,0:T(8,128)(2,1)S(1)}, u32[]{:S(2)}, u32[]{:S(2)}) collective-permute-start(bf16[256,128]{1,0:T(8,128)(2,1)S(1)} %get-tuple-element.32), channel_id=1, source_target_pairs={{0,8},{2,6},{4,12},{6,2},{8,0},{10,14},{12,4},{14,10},{16,24},{18,... | collective-permute-start | bytes 196616 | tf_op jit(solution)/shard_map/ppermute | solution.py:392
  15.6 0.0 collective-permute-start.4
  15.6 0.5 collective-permute-start.5
  16.1 1.9 %collective-permute-start.6 = (bf16[256,128]{1,0:T(8,128)(2,1)S(1)}, bf16[256,128]{1,0:T(8,128)(2,1)S(1)}, u32[]{:S(2)}, u32[]{:S(2)}) collective-permute-start(bf16[256,128]{1,0:T(8,128)(2,1)S(1)} %get-tuple-element.37), channel_id=1, source_target_pairs={{0,6},{2,8},{4,2},{6,12},{8,14},{10,0},{12,10},{14,4},{16,22},{18,... | collective-permute-start | bytes 196616 | tf_op jit(solution)/shard_map/ppermute | solution.py:392
  18.0 1.1 %all-to-all-done = bf16[8,256,128]{2,1,0:T(8,128)(2,1)S(1)} async-done(((bf16[8,256,128]{2,1,0:T(8,128)(2,1)}), bf16[8,256,128]{2,1,0:T(8,128)(2,1)S(1)}, u32[]{:S(2)}, u32[]{:S(2)}) %all-to-all-start) | async-done | bytes 524320 | tf_op jit(solution)/shard_map/all_to_all | solution.py:417
  19.0 0.7 %gather_keys.1 = (bf16[64,2048]{1,0:T(8,128)(2,1)S(1)}, bf16[128,128]{1,0:T(8,128)(2,1)S(1)}) custom-call(s32[18]{0:T(128)S(1)} %pad_add_fusion.place_ref, bf16[2048,128]{1,0:T(8,128)(2,1)S(1)} %bitcast.3, bf16[256,128]{1,0:T(8,128)(2,1)S(1)} %get-tuple-element.29.after_ref.refs_0_.refs_1_), custom_call_target="tpu_custom_call" | custom-call | bytes 2097152 | tf_op jit(solution)/shard_map/gather_keys/pallas_call | solution.py:356
  19.8 0.2 collective-permute-done.1.refs_1_.refs_2_
  20.0 0.0 collective-permute-start.7
  20.0 0.5 collective-permute-done.2.refs_2_.refs_3_
  20.4 2.4 %collective-permute-start.8 = (bf16[256,128]{1,0:T(8,128)(2,1)S(1)}, bf16[256,128]{1,0:T(8,128)(2,1)S(1)}, u32[]{:S(2)}, u32[]{:S(2)}) collective-permute-start(bf16[256,128]{1,0:T(8,128)(2,1)S(1)} %get-tuple-element.39), channel_id=1, source_target_pairs={{0,12},{2,14},{4,8},{6,10},{8,4},{10,6},{12,0},{14,2},{16,28},{18,... | collective-permute-start | bytes 196616 | tf_op jit(solution)/shard_map/ppermute | solution.py:392
  22.8 0.0 collective-permute-done.4.refs_4_.refs_1_
  22.8 2.6 %collective-permute-start.3 = (bf16[128,128]{1,0:T(8,128)(2,1)S(1)}, bf16[128,128]{1,0:T(8,128)(2,1)S(1)}, u32[]{:S(2)}, u32[]{:S(2)}) collective-permute-start(bf16[128,128]{1,0:T(8,128)(2,1)S(1)} %get-tuple-element.34.picks_ref), channel_id=1, source_target_pairs={{0,16},{2,18},{4,20},{6,22},{8,24},{10,26},{12,28},{14,30},{16,0},... | collective-permute-start | bytes 98312 | tf_op jit(solution)/shard_map/ppermute | solution.py:401
  25.4 5.9 %first_rows.1 = (f32[2048,128]{1,0:T(8,128)S(1)}, bf16[3,128,128]{2,1,0:T(8,128)(2,1)S(1)}) custom-call(s32[18]{0:T(128)S(1)} %pad_add_fusion.place_ref, bf16[2048,128]{1,0:T(8,128)(2,1)S(1)} %bitcast.4, bf16[64,2048]{1,0:T(8,128)(2,1)S(1)} %get-tuple-element.30.key_t_ref, bf16[256,128]{1,0:T(8,128)(2,1)S(1)} %get-tuple-element.29.after_ref.refs_0_.refs_1_, ...), custom_call_target="tpu_custom_call" | custom-call | flops 8053063680 | bytes 2097152 | tf_op jit(solution)/shard_map/first_rows/pallas_call | solution.py:356
  31.3 0.0 collective-permute-done.5.refs_5_.refs_2_
  31.3 0.0 collective-permute-done.6.refs_6_.refs_3_
  31.4 0.0 collective-permute-done.7.refs_7_.refs_4_
  31.4 0.0 collective-permute-done.8.refs_8_.refs_1_
  31.4 0.0 collective-permute-done.3.refs_0_
  31.4 2.5 %picked_rows.1 = (f32[2048,128]{1,0:T(8,128)S(1)}, bf16[256,128]{1,0:T(8,128)(2,1)S(1)}, f32[128,128]{1,0:T(8,128)S(1)}, f32[128,128]{1,0:T(8,128)S(1)}) custom-call(s32[18]{0:T(128)S(1)} %pad_add_fusion.place_ref, bf16[2048,128]{1,0:T(8,128)(2,1)S(1)} %bitcast.5, f32[2048,128]{1,0:T(8,128)S(1)} %get-tuple-element.33.start_ref, ...), custom_call_target="tpu_custom_call" | custom-call | flops 671088640 | bytes 2097152 | tf_op jit(solution)/shard_map/picked_rows/pallas_call | solution.py:356
  33.8 0.4 collective-permute-start.9
  34.2 7.8 %second_rows.1 = (f32[2048,128]{1,0:T(8,128)S(1)}, bf16[4,128,128]{2,1,0:T(8,128)(2,1)S(1)}) custom-call(s32[18]{0:T(128)S(1)} %pad_add_fusion.place_ref, bf16[2048,128]{1,0:T(8,128)(2,1)S(1)} %bitcast.6, bf16[64,2048]{1,0:T(8,128)(2,1)S(1)} %get-tuple-element.30.key_t_ref, f32[2048,128]{1,0:T(8,128)S(1)} %get-tuple-element.40.refs_0_, ...), custom_call_target="tpu_custom_call" | custom-call | flops 8053063680 | bytes 2097152 | tf_op jit(solution)/shard_map/second_rows/pallas_call | solution.py:356
  42.0 0.0 collective-permute-done.9.refs_0_
  42.1 2.9 %last_rows.1 = (bf16[384,128]{1,0:T(8,128)(2,1)S(1)}, bf16[384,128]{1,0:T(8,128)(2,1)S(1)}, bf16[384,128]{1,0:T(8,128)(2,1)S(1)}, bf16[384,128]{1,0:T(8,128)(2,1...) custom-call(s32[18]{0:T(128)S(1)} %pad_add_fusion.place_ref, ...), custom_call_target="tpu_custom_call" | custom-call | flops 2013265920 | bytes 2097152 | tf_op jit(solution)/shard_map/last_rows/pallas_call | solution.py:356
  45.0 0.6 %collective-permute-start.10 = (bf16[384,128]{1,0:T(8,128)(2,1)S(1)}, bf16[384,128]{1,0:T(8,128)(2,1)S(1)}, u32[]{:S(2)}, u32[]{:S(2)}) collective-permute-start(bf16[384,128]{1,0:T(8,128)(2,1)S(1)} %get-tuple-element.48), channel_id=1, source_target_pairs={{0,4},{2,10},{4,0},{6,14},{8,12},{10,2},{12,8},{14,6},{16,20},{18,... | collective-permute-start | bytes 294920 | tf_op jit(solution)/shard_map/ppermute | solution.py:392
  45.6 0.6 collective-permute-start.11
  46.1 0.0 collective-permute-start.12
  46.1 2.6 %collective-permute-start.13 = (bf16[384,128]{1,0:T(8,128)(2,1)S(1)}, bf16[384,128]{1,0:T(8,128)(2,1)S(1)}, u32[]{:S(2)}, u32[]{:S(2)}) collective-permute-start(bf16[384,128]{1,0:T(8,128)(2,1)S(1)} %get-tuple-element.51), channel_id=1, source_target_pairs={{0,14},{2,0},{4,10},{6,4},{8,6},{10,8},{12,2},{14,12},{16,30},{18,... | collective-permute-start | bytes 294920 | tf_op jit(solution)/shard_map/ppermute | solution.py:392
  48.8 0.0 collective-permute-start.14
  48.8 0.9 %collective-permute-done.10.refs_1_ = bf16[384,128]{1,0:T(8,128)(2,1)S(1)} collective-permute-done((bf16[384,128]{1,0:T(8,128)(2,1)S(1)}, bf16[384,128]{1,0:T(8,128)(2,1)S(1)}, u32[]{:S(2)}, u32[]{:S(2)}) %collective-permute-start.10) | collective-permute-done | bytes 98336 | tf_op jit(solution)/shard_map/ppermute | solution.py:392
  49.7 0.9 %collective-permute-start.15 = (bf16[384,128]{1,0:T(8,128)(2,1)S(1)}, bf16[384,128]{1,0:T(8,128)(2,1)S(1)}, u32[]{:S(2)}, u32[]{:S(2)}) collective-permute-start(bf16[384,128]{1,0:T(8,128)(2,1)S(1)} %get-tuple-element.53), channel_id=1, source_target_pairs={{0,6},{2,8},{4,2},{6,12},{8,14},{10,0},{12,10},{14,4},{16,22},{18,... | collective-permute-start | bytes 294920 | tf_op jit(solution)/shard_map/ppermute | solution.py:392
  50.5 0.0 collective-permute-done.11.refs_2_
  50.5 2.4 %collective-permute-start.16 = (bf16[384,128]{1,0:T(8,128)(2,1)S(1)}, bf16[384,128]{1,0:T(8,128)(2,1)S(1)}, u32[]{:S(2)}, u32[]{:S(2)}) collective-permute-start(bf16[384,128]{1,0:T(8,128)(2,1)S(1)} %get-tuple-element.54), channel_id=1, source_target_pairs={{0,12},{2,14},{4,8},{6,10},{8,4},{10,6},{12,0},{14,2},{16,28},{18,... | collective-permute-start | bytes 294920 | tf_op jit(solution)/shard_map/ppermute | solution.py:392
  52.9 0.0 collective-permute-done.12.refs_3_
  52.9 0.0 collective-permute-done.13.refs_4_
  52.9 1.2 %collective-permute-done.14.refs_5_ = bf16[384,128]{1,0:T(8,128)(2,1)S(1)} collective-permute-done((bf16[384,128]{1,0:T(8,128)(2,1)S(1)}, bf16[384,128]{1,0:T(8,128)(2,1)S(1)}, u32[]{:S(2)}, u32[]{:S(2)}) %collective-permute-start.14) | collective-permute-done | bytes 98336 | tf_op jit(solution)/shard_map/ppermute | solution.py:392
  54.1 0.7 %collective-permute-done.15.refs_6_ = bf16[384,128]{1,0:T(8,128)(2,1)S(1)} collective-permute-done((bf16[384,128]{1,0:T(8,128)(2,1)S(1)}, bf16[384,128]{1,0:T(8,128)(2,1)S(1)}, u32[]{:S(2)}, u32[]{:S(2)}) %collective-permute-start.15) | collective-permute-done | bytes 98336 | tf_op jit(solution)/shard_map/ppermute | solution.py:392
  54.8 3.2 %collective-permute-done.16.refs_7_ = bf16[384,128]{1,0:T(8,128)(2,1)S(1)} collective-permute-done((bf16[384,128]{1,0:T(8,128)(2,1)S(1)}, bf16[384,128]{1,0:T(8,128)(2,1)S(1)}, u32[]{:S(2)}, u32[]{:S(2)}) %collective-permute-start.16) | collective-permute-done | bytes 98336 | tf_op jit(solution)/shard_map/ppermute | solution.py:392
  58.0 1.7 %unpack.1 = (bf16[256,512]{1,0:T(8,128)(2,1)}, bf16[256,512]{1,0:T(8,128)(2,1)}, bf16[256,512]{1,0:T(8,128)(2,1)}) custom-call(s32[18]{0:T(128)S(1)} %pad_add_fusion.place_ref, bf16[384,128]{1,0:T(8,128)(2,1)S(1)} %get-tuple-element.47.refs_0_, bf16[384,128]{1,0:T(8,128)(2,1)S(1)} %collective-permute-done.10.refs_1_, ...), custom_call_target="tpu_custom_call" | custom-call | bytes 2097152 | tf_op jit(solution)/shard_map/unpack/pallas_call | solution.py:356
Async XLA Ops:
  0.6 9.8 %collective-permute-start = (bf16[128,1024]{1,0:T(8,128)(2,1)}, bf16[128,1024]{1,0:T(8,128)(2,1)S(1)}, u32[]{:S(2)}, u32[]{:S(2)}) collective-permute-start(bf16[128,1024]{1,0:T(8,128)(2,1)} %refs_0_.1), channel_id=1, source_target_pairs={{0,1},{1,0},{2,3},{3,2},{4,5},{5,4},{6,7},{7,6},{8,9},{9,8},{10,11... | collective-permute-start | bytes 786440 | tf_op jit(solution)/shard_map/ppermute | solution.py:406
  3.6 6.8 %copy-start.1 = (bf16[256,512]{1,0:T(8,128)(2,1)S(1)}, bf16[256,512]{1,0:T(8,128)(2,1)}, u32[]{:S(2)}) copy-start(bf16[256,512]{1,0:T(8,128)(2,1)} %query_ref.1) | copy-start | bytes 786436
  3.6 6.8 %copy-start.2 = (bf16[128,1024]{1,0:T(8,128)(2,1)S(1)}, bf16[128,1024]{1,0:T(8,128)(2,1)}, u32[]{:S(2)}) copy-start(bf16[128,1024]{1,0:T(8,128)(2,1)} %refs_0_.1) | copy-start | bytes 786436
  5.8 4.7 %copy-start = (bf16[512,1024]{1,0:T(8,128)(2,1)S(1)}, bf16[512,1024]{1,0:T(8,128)(2,1)}, u32[]{:S(2)}) copy-start(bf16[512,1024]{1,0:T(8,128)(2,1)} %weight_ref.1) | copy-start | bytes 3145732
  5.8 13.3 %all-to-all-start = ((bf16[8,256,128]{2,1,0:T(8,128)(2,1)}), bf16[8,256,128]{2,1,0:T(8,128)(2,1)S(1)}, u32[]{:S(2)}, u32[]{:S(2)}) async-start(bf16[8,256,128]{2,1,0:T(8,128)(2,1)} %pack_rows.1), calls=%async_computation | async-start | bytes 1048576 | tf_op jit(solution)/shard_map/all_to_all | solution.py:417
  9.7 0.7 %copy-start.3 = (s32[16]{0:T(128)S(1)}, s32[16]{0:T(128)}, u32[]{:S(2)}) copy-start(s32[16]{0:T(128)} %param.11) | copy-start | bytes 196
  12.0 8.0 %collective-permute-start.1 = (bf16[256,128]{1,0:T(8,128)(2,1)S(1)}, bf16[256,128]{1,0:T(8,128)(2,1)S(1)}, u32[]{:S(2)}, u32[]{:S(2)}) collective-permute-start(bf16[256,128]{1,0:T(8,128)(2,1)S(1)} %get-tuple-element.31), channel_id=1, source_target_pairs={{0,4},{2,10},{4,0},{6,14},{8,12},{10,2},{12,8},{14,6},{16,20},{18,... | collective-permute-start | bytes 196616 | tf_op jit(solution)/shard_map/ppermute | solution.py:392
  14.1 6.3 %collective-permute-start.2 = (bf16[256,128]{1,0:T(8,128)(2,1)S(1)}, bf16[256,128]{1,0:T(8,128)(2,1)S(1)}, u32[]{:S(2)}, u32[]{:S(2)}) collective-permute-start(bf16[256,128]{1,0:T(8,128)(2,1)S(1)} %get-tuple-element.32), channel_id=1, source_target_pairs={{0,8},{2,6},{4,12},{6,2},{8,0},{10,14},{12,4},{14,10},{16,24},{18,... | collective-permute-start | bytes 196616 | tf_op jit(solution)/shard_map/ppermute | solution.py:392
  15.6 7.3 %collective-permute-start.4 = (bf16[256,128]{1,0:T(8,128)(2,1)S(1)}, bf16[256,128]{1,0:T(8,128)(2,1)S(1)}, u32[]{:S(2)}, u32[]{:S(2)}) collective-permute-start(bf16[256,128]{1,0:T(8,128)(2,1)S(1)} %get-tuple-element.35), channel_id=1, source_target_pairs={{0,14},{2,0},{4,10},{6,4},{8,6},{10,8},{12,2},{14,12},{16,30},{18,... | collective-permute-start | bytes 196616 | tf_op jit(solution)/shard_map/ppermute | solution.py:392
  15.6 15.8 %collective-permute-start.5 = (bf16[256,128]{1,0:T(8,128)(2,1)S(1)}, bf16[256,128]{1,0:T(8,128)(2,1)S(1)}, u32[]{:S(2)}, u32[]{:S(2)}) collective-permute-start(bf16[256,128]{1,0:T(8,128)(2,1)S(1)} %get-tuple-element.36), channel_id=1, source_target_pairs={{0,2},{2,12},{4,6},{6,8},{8,10},{10,4},{12,14},{14,0},{16,18},{18,... | collective-permute-start | bytes 196616 | tf_op jit(solution)/shard_map/ppermute | solution.py:392
  16.1 15.3 %collective-permute-start.6 = (bf16[256,128]{1,0:T(8,128)(2,1)S(1)}, bf16[256,128]{1,0:T(8,128)(2,1)S(1)}, u32[]{:S(2)}, u32[]{:S(2)}) collective-permute-start(bf16[256,128]{1,0:T(8,128)(2,1)S(1)} %get-tuple-element.37), channel_id=1, source_target_pairs={{0,6},{2,8},{4,2},{6,12},{8,14},{10,0},{12,10},{14,4},{16,22},{18,... | collective-permute-start | bytes 196616 | tf_op jit(solution)/shard_map/ppermute | solution.py:392
  20.0 11.4 %collective-permute-start.7 = (bf16[256,128]{1,0:T(8,128)(2,1)S(1)}, bf16[256,128]{1,0:T(8,128)(2,1)S(1)}, u32[]{:S(2)}, u32[]{:S(2)}) collective-permute-start(bf16[256,128]{1,0:T(8,128)(2,1)S(1)} %get-tuple-element.38), channel_id=1, source_target_pairs={{0,10},{2,4},{4,14},{6,0},{8,2},{10,12},{12,6},{14,8},{16,26},{18,... | collective-permute-start | bytes 196616 | tf_op jit(solution)/shard_map/ppermute | solution.py:392
  20.4 10.9 %collective-permute-start.8 = (bf16[256,128]{1,0:T(8,128)(2,1)S(1)}, bf16[256,128]{1,0:T(8,128)(2,1)S(1)}, u32[]{:S(2)}, u32[]{:S(2)}) collective-permute-start(bf16[256,128]{1,0:T(8,128)(2,1)S(1)} %get-tuple-element.39), channel_id=1, source_target_pairs={{0,12},{2,14},{4,8},{6,10},{8,4},{10,6},{12,0},{14,2},{16,28},{18,... | collective-permute-start | bytes 196616 | tf_op jit(solution)/shard_map/ppermute | solution.py:392
  22.8 8.5 %collective-permute-start.3 = (bf16[128,128]{1,0:T(8,128)(2,1)S(1)}, bf16[128,128]{1,0:T(8,128)(2,1)S(1)}, u32[]{:S(2)}, u32[]{:S(2)}) collective-permute-start(bf16[128,128]{1,0:T(8,128)(2,1)S(1)} %get-tuple-element.34.picks_ref), channel_id=1, source_target_pairs={{0,16},{2,18},{4,20},{6,22},{8,24},{10,26},{12,28},{14,30},{16,0},... | collective-permute-start | bytes 98312 | tf_op jit(solution)/shard_map/ppermute | solution.py:401
  33.8 8.2 %collective-permute-start.9 = (f32[128,128]{1,0:T(8,128)S(1)}, f32[128,128]{1,0:T(8,128)S(1)}, u32[]{:S(2)}, u32[]{:S(2)}) collective-permute-start(f32[128,128]{1,0:T(8,128)S(1)} %get-tuple-element.46), channel_id=1, source_target_pairs={{0,16},{2,18},{4,20},{6,22},{8,24},{10,26},{12,28},{14,30},{16,0},... | collective-permute-start | bytes 196616 | tf_op jit(solution)/shard_map/ppermute | solution.py:401
  45.0 4.7 %collective-permute-start.10 = (bf16[384,128]{1,0:T(8,128)(2,1)S(1)}, bf16[384,128]{1,0:T(8,128)(2,1)S(1)}, u32[]{:S(2)}, u32[]{:S(2)}) collective-permute-start(bf16[384,128]{1,0:T(8,128)(2,1)S(1)} %get-tuple-element.48), channel_id=1, source_target_pairs={{0,4},{2,10},{4,0},{6,14},{8,12},{10,2},{12,8},{14,6},{16,20},{18,... | collective-permute-start | bytes 294920 | tf_op jit(solution)/shard_map/ppermute | solution.py:392
  45.6 5.0 %collective-permute-start.11 = (bf16[384,128]{1,0:T(8,128)(2,1)S(1)}, bf16[384,128]{1,0:T(8,128)(2,1)S(1)}, u32[]{:S(2)}, u32[]{:S(2)}) collective-permute-start(bf16[384,128]{1,0:T(8,128)(2,1)S(1)} %get-tuple-element.49), channel_id=1, source_target_pairs={{0,8},{2,6},{4,12},{6,2},{8,0},{10,14},{12,4},{14,10},{16,24},{18,... | collective-permute-start | bytes 294920 | tf_op jit(solution)/shard_map/ppermute | solution.py:392
  46.1 6.8 %collective-permute-start.12 = (bf16[384,128]{1,0:T(8,128)(2,1)S(1)}, bf16[384,128]{1,0:T(8,128)(2,1)S(1)}, u32[]{:S(2)}, u32[]{:S(2)}) collective-permute-start(bf16[384,128]{1,0:T(8,128)(2,1)S(1)} %get-tuple-element.50), channel_id=1, source_target_pairs={{0,2},{2,12},{4,6},{6,8},{8,10},{10,4},{12,14},{14,0},{16,18},{18,... | collective-permute-start | bytes 294920 | tf_op jit(solution)/shard_map/ppermute | solution.py:392
  46.1 6.8 %collective-permute-start.13 = (bf16[384,128]{1,0:T(8,128)(2,1)S(1)}, bf16[384,128]{1,0:T(8,128)(2,1)S(1)}, u32[]{:S(2)}, u32[]{:S(2)}) collective-permute-start(bf16[384,128]{1,0:T(8,128)(2,1)S(1)} %get-tuple-element.51), channel_id=1, source_target_pairs={{0,14},{2,0},{4,10},{6,4},{8,6},{10,8},{12,2},{14,12},{16,30},{18,... | collective-permute-start | bytes 294920 | tf_op jit(solution)/shard_map/ppermute | solution.py:392
  48.8 5.4 %collective-permute-start.14 = (bf16[384,128]{1,0:T(8,128)(2,1)S(1)}, bf16[384,128]{1,0:T(8,128)(2,1)S(1)}, u32[]{:S(2)}, u32[]{:S(2)}) collective-permute-start(bf16[384,128]{1,0:T(8,128)(2,1)S(1)} %get-tuple-element.52), channel_id=1, source_target_pairs={{0,10},{2,4},{4,14},{6,0},{8,2},{10,12},{12,6},{14,8},{16,26},{18,... | collective-permute-start | bytes 294920 | tf_op jit(solution)/shard_map/ppermute | solution.py:392
  49.7 5.1 %collective-permute-start.15 = (bf16[384,128]{1,0:T(8,128)(2,1)S(1)}, bf16[384,128]{1,0:T(8,128)(2,1)S(1)}, u32[]{:S(2)}, u32[]{:S(2)}) collective-permute-start(bf16[384,128]{1,0:T(8,128)(2,1)S(1)} %get-tuple-element.53), channel_id=1, source_target_pairs={{0,6},{2,8},{4,2},{6,12},{8,14},{10,0},{12,10},{14,4},{16,22},{18,... | collective-permute-start | bytes 294920 | tf_op jit(solution)/shard_map/ppermute | solution.py:392
  50.5 7.4 %collective-permute-start.16 = (bf16[384,128]{1,0:T(8,128)(2,1)S(1)}, bf16[384,128]{1,0:T(8,128)(2,1)S(1)}, u32[]{:S(2)}, u32[]{:S(2)}) collective-permute-start(bf16[384,128]{1,0:T(8,128)(2,1)S(1)} %get-tuple-element.54), channel_id=1, source_target_pairs={{0,12},{2,14},{4,8},{6,10},{8,4},{10,6},{12,0},{14,2},{16,28},{18,... | collective-permute-start | bytes 294920 | tf_op jit(solution)/shard_map/ppermute | solution.py:392

commit v20 on v18

--- a/solution.py
+++ b/solution.py
@@ -77,7 +77,7 @@
 
 def swap_steps(group):
     if group == 8:
-        return [(2, 4), (4, 2), (6, 6), (3, 5), (5, 3), (7, 1), (1, 7)]
+        return [(2, 4), (4, 2), (3, 5), (6, 6), (5, 3), (7, 1), (1, 7)]
     return [(bits, bits) for bits in range(1, group)]
 
 

time: 58.4 us -> 57.6 us (0.986)
  starting transfers between devices: 23.2 us -> 22.5 us
    ppermute x14, waiting for transfers between devices: 6.5 us -> 5.41 us  [swap(): result.append(lax.ppermute(value, 'context', pairs))]
    ppermute x2, waiting for transfers between devices: 0.01 us -> 0.71 us  [segment_shift(): return lax.ppermute(value, 'context', pairs)]
    ppermute x14, starting transfers between devices: 13.3 us -> 12.6 us  [swap(): result.append(lax.ppermute(value, 'context', pairs))]
  transfers between devices with their start and end apart: 18 -> 18, of which waited for: 7 -> 8; matrix products, arithmetic and copies ran while one was open for 0% -> 0% of each run, Pallas kernels for 31% -> 32%
where the time goes in v20:
time: 57.6 us; the launch traced here: 57 us
  Pallas kernels  25.1 us (44%)
  starting transfers between devices  22.5 us (39%)
  waiting for transfers between devices  7.84 us (14%)
  between operations  0.75 us (1%)
  local copies, waits for them, and re-layouts  0.67 us (1%)
    pallas_call x8, Pallas kernels, call(): pl.pallas_call(kernel, out_shape=tuple((jax.ShapeDtypeStruct(*shape) for...  25.1 us
    ppermute x14, starting transfers between devices, swap(): result.append(lax.ppermute(value, 'context', pairs))  12.6 us
    ppermute x14, waiting for transfers between devices, swap(): result.append(lax.ppermute(value, 'context', pairs))  5.41 us
    all_to_all x1, starting transfers between devices, body(): sent = lax.all_to_all(sent, 'context', 0, 0, axis_index_groups=groups)  3.95 us
    ppermute x1, starting transfers between devices, body(): upstreams.append(lax.ppermute(upstream, 'heads', pairs))  3 us
    ppermute x2, starting transfers between devices, segment_shift(): return lax.ppermute(value, 'context', pairs)  2.99 us
    all_to_all x1, waiting for transfers between devices, body(): sent = lax.all_to_all(sent, 'context', 0, 0, axis_index_groups=groups)  1.71 us
  transfers between devices with their start and end apart: 18, of which 8 were waited for; matrix products, arithmetic and copies ran while one was open for 0% of the time, Pallas kernels for 32%

profile of v20, /device:TPU:0, one launch (start us, length us, event | category | flops | bytes accessed | tf_op | source)
XLA Modules:
  0.0 57.0 jit_solution(7438163252995593983)
XLA Ops:
  0.6 3.0 %collective-permute-start = (bf16[128,1024]{1,0:T(8,128)(2,1)}, bf16[128,1024]{1,0:T(8,128)(2,1)S(1)}, u32[]{:S(2)}, u32[]{:S(2)}) collective-permute-start(bf16[128,1024]{1,0:T(8,128)(2,1)} %refs_0_.1), channel_id=1, source_target_pairs={{0,1},{1,0},{2,3},{3,2},{4,5},{5,4},{6,7},{7,6},{8,9},{9,8},{10,11... | collective-permute-start | bytes 786440 | tf_op jit(solution)/shard_map/ppermute | solution.py:404
  3.6 0.0 copy-start.1
  3.6 0.0 copy-start.2
  3.6 2.1 %pack_rows.1 = bf16[8,256,128]{2,1,0:T(8,128)(2,1)} custom-call(bf16[256,512]{1,0:T(8,128)(2,1)} %key_hbm.1, bf16[256,512]{1,0:T(8,128)(2,1)} %value_hbm.1), custom_call_target="tpu_custom_call" | custom-call | flops 2147483648 | bytes 2097152 | tf_op jit(solution)/shard_map/pack_rows/pallas_call | solution.py:356
  5.8 0.0 copy-start
  5.8 4.0 %all-to-all-start = ((bf16[8,256,128]{2,1,0:T(8,128)(2,1)}), bf16[8,256,128]{2,1,0:T(8,128)(2,1)S(1)}, u32[]{:S(2)}, u32[]{:S(2)}) async-start(bf16[8,256,128]{2,1,0:T(8,128)(2,1)} %pack_rows.1), calls=%async_computation | async-start | bytes 1048576 | tf_op jit(solution)/shard_map/all_to_all | solution.py:415
  9.7 0.0 copy-start.3
  9.7 0.7 %copy-done.3 = s32[16]{0:T(128)S(1)} copy-done((s32[16]{0:T(128)S(1)}, s32[16]{0:T(128)}, u32[]{:S(2)}) %copy-start.3) | copy-done | bytes 88
  10.4 0.1 pad_add_fusion.place_ref
  10.5 0.0 collective-permute-done.refs_1_
  10.5 0.0 copy-done.1
  10.5 0.0 copy-done.2
  10.5 0.0 copy-done
  10.5 1.5 %project_pack.1 = (bf16[256,128]{1,0:T(8,128)(2,1)S(1)}, bf16[256,128]{1,0:T(8,128)(2,1)S(1)}, bf16[256,128]{1,0:T(8,128)(2,1)S(1)}, bf16[256,128]{1,0:T(8,128)(...) custom-call(s32[18]{0:T(128)S(1)} %pad_add_fusion.place_ref, ...), custom_call_target="tpu_custom_call" | custom-call | flops 34359738368 | bytes 2097152 | tf_op jit(solution)/shard_map/project_pack/pallas_call | solution.py:356
  12.0 2.1 %collective-permute-start.1 = (bf16[256,128]{1,0:T(8,128)(2,1)S(1)}, bf16[256,128]{1,0:T(8,128)(2,1)S(1)}, u32[]{:S(2)}, u32[]{:S(2)}) collective-permute-start(bf16[256,128]{1,0:T(8,128)(2,1)S(1)} %get-tuple-element.31), channel_id=1, source_target_pairs={{0,4},{2,10},{4,0},{6,14},{8,12},{10,2},{12,8},{14,6},{16,20},{18,... | collective-permute-start | bytes 196616 | tf_op jit(solution)/shard_map/ppermute | solution.py:391
  14.1 1.5 %collective-permute-start.2 = (bf16[256,128]{1,0:T(8,128)(2,1)S(1)}, bf16[256,128]{1,0:T(8,128)(2,1)S(1)}, u32[]{:S(2)}, u32[]{:S(2)}) collective-permute-start(bf16[256,128]{1,0:T(8,128)(2,1)S(1)} %get-tuple-element.32), channel_id=1, source_target_pairs={{0,8},{2,6},{4,12},{6,2},{8,0},{10,14},{12,4},{14,10},{16,24},{18,... | collective-permute-start | bytes 196616 | tf_op jit(solution)/shard_map/ppermute | solution.py:391
  15.6 0.0 collective-permute-start.3
  15.6 1.2 %collective-permute-start.5 = (bf16[256,128]{1,0:T(8,128)(2,1)S(1)}, bf16[256,128]{1,0:T(8,128)(2,1)S(1)}, u32[]{:S(2)}, u32[]{:S(2)}) collective-permute-start(bf16[256,128]{1,0:T(8,128)(2,1)S(1)} %get-tuple-element.36), channel_id=1, source_target_pairs={{0,12},{2,14},{4,8},{6,10},{8,4},{10,6},{12,0},{14,2},{16,28},{18,... | collective-permute-start | bytes 196616 | tf_op jit(solution)/shard_map/ppermute | solution.py:391
  16.8 0.5 collective-permute-start.6
  17.3 1.7 %all-to-all-done = bf16[8,256,128]{2,1,0:T(8,128)(2,1)S(1)} async-done(((bf16[8,256,128]{2,1,0:T(8,128)(2,1)}), bf16[8,256,128]{2,1,0:T(8,128)(2,1)S(1)}, u32[]{:S(2)}, u32[]{:S(2)}) %all-to-all-start) | async-done | bytes 524320 | tf_op jit(solution)/shard_map/all_to_all | solution.py:415
  19.0 0.7 %gather_keys.1 = (bf16[64,2048]{1,0:T(8,128)(2,1)S(1)}, bf16[128,128]{1,0:T(8,128)(2,1)S(1)}) custom-call(s32[18]{0:T(128)S(1)} %pad_add_fusion.place_ref, bf16[2048,128]{1,0:T(8,128)(2,1)S(1)} %bitcast.3, bf16[256,128]{1,0:T(8,128)(2,1)S(1)} %get-tuple-element.29.after_ref.refs_0_.refs_1_), custom_call_target="tpu_custom_call" | custom-call | bytes 2097152 | tf_op jit(solution)/shard_map/gather_keys/pallas_call | solution.py:356
  19.8 0.3 collective-permute-done.1.refs_1_.refs_2_
  20.1 0.6 %collective-permute-start.7 = (bf16[256,128]{1,0:T(8,128)(2,1)S(1)}, bf16[256,128]{1,0:T(8,128)(2,1)S(1)}, u32[]{:S(2)}, u32[]{:S(2)}) collective-permute-start(bf16[256,128]{1,0:T(8,128)(2,1)S(1)} %get-tuple-element.38), channel_id=1, source_target_pairs={{0,14},{2,0},{4,10},{6,4},{8,6},{10,8},{12,2},{14,12},{16,30},{18,... | collective-permute-start | bytes 196616 | tf_op jit(solution)/shard_map/ppermute | solution.py:391
  20.7 0.0 collective-permute-done.2.refs_2_.refs_3_
  20.7 0.0 collective-permute-start.8
  20.7 0.2 collective-permute-done.3.refs_3_.refs_4_
  20.9 2.6 %collective-permute-start.4 = (bf16[128,128]{1,0:T(8,128)(2,1)S(1)}, bf16[128,128]{1,0:T(8,128)(2,1)S(1)}, u32[]{:S(2)}, u32[]{:S(2)}) collective-permute-start(bf16[128,128]{1,0:T(8,128)(2,1)S(1)} %get-tuple-element.35.picks_ref), channel_id=1, source_target_pairs={{0,16},{2,18},{4,20},{6,22},{8,24},{10,26},{12,28},{14,30},{16,0},... | collective-permute-start | bytes 98312 | tf_op jit(solution)/shard_map/ppermute | solution.py:399
  23.5 7.6 %first_rows.1 = (f32[2048,128]{1,0:T(8,128)S(1)}, bf16[4,128,128]{2,1,0:T(8,128)(2,1)S(1)}) custom-call(s32[18]{0:T(128)S(1)} %pad_add_fusion.place_ref, bf16[2048,128]{1,0:T(8,128)(2,1)S(1)} %bitcast.4, bf16[64,2048]{1,0:T(8,128)(2,1)S(1)} %get-tuple-element.30.key_t_ref, bf16[256,128]{1,0:T(8,128)(2,1)S(1)} %get-tuple-element.29.after_ref.refs_0_.refs_1_, ...), custom_call_target="tpu_custom_call" | custom-call | flops 8053063680 | bytes 2097152 | tf_op jit(solution)/shard_map/first_rows/pallas_call | solution.py:356
  31.1 0.0 collective-permute-done.5.refs_5_.refs_1_
  31.1 0.0 collective-permute-done.6.refs_6_.refs_2_
  31.1 0.0 collective-permute-done.7.refs_7_.refs_3_
  31.1 0.0 collective-permute-done.8.refs_8_.refs_1_
  31.1 0.0 collective-permute-done.4.refs_0_
  31.1 2.5 %picked_rows.1 = (f32[2048,128]{1,0:T(8,128)S(1)}, bf16[256,128]{1,0:T(8,128)(2,1)S(1)}, f32[128,128]{1,0:T(8,128)S(1)}, f32[128,128]{1,0:T(8,128)S(1)}) custom-call(s32[18]{0:T(128)S(1)} %pad_add_fusion.place_ref, bf16[2048,128]{1,0:T(8,128)(2,1)S(1)} %bitcast.5, f32[2048,128]{1,0:T(8,128)S(1)} %get-tuple-element.34.start_ref, ...), custom_call_target="tpu_custom_call" | custom-call | flops 671088640 | bytes 2097152 | tf_op jit(solution)/shard_map/picked_rows/pallas_call | solution.py:356
  33.6 0.4 collective-permute-start.9
  34.0 6.1 %second_rows.1 = (f32[2048,128]{1,0:T(8,128)S(1)}, bf16[3,128,128]{2,1,0:T(8,128)(2,1)S(1)}) custom-call(s32[18]{0:T(128)S(1)} %pad_add_fusion.place_ref, bf16[2048,128]{1,0:T(8,128)(2,1)S(1)} %bitcast.6, bf16[64,2048]{1,0:T(8,128)(2,1)S(1)} %get-tuple-element.30.key_t_ref, f32[2048,128]{1,0:T(8,128)S(1)} %get-tuple-element.40.refs_0_, ...), custom_call_target="tpu_custom_call" | custom-call | flops 8053063680 | bytes 2097152 | tf_op jit(solution)/shard_map/second_rows/pallas_call | solution.py:356
  40.1 0.7 %collective-permute-done.9.refs_0_ = f32[128,128]{1,0:T(8,128)S(1)} collective-permute-done((f32[128,128]{1,0:T(8,128)S(1)}, f32[128,128]{1,0:T(8,128)S(1)}, u32[]{:S(2)}, u32[]{:S(2)}) %collective-permute-start.9) | collective-permute-done | bytes 65568 | tf_op jit(solution)/shard_map/ppermute | solution.py:399
  40.8 2.9 %last_rows.1 = (bf16[384,128]{1,0:T(8,128)(2,1)S(1)}, bf16[384,128]{1,0:T(8,128)(2,1)S(1)}, bf16[384,128]{1,0:T(8,128)(2,1)S(1)}, bf16[384,128]{1,0:T(8,128)(2,1...) custom-call(s32[18]{0:T(128)S(1)} %pad_add_fusion.place_ref, ...), custom_call_target="tpu_custom_call" | custom-call | flops 2013265920 | bytes 2097152 | tf_op jit(solution)/shard_map/last_rows/pallas_call | solution.py:356
  43.7 1.5 %collective-permute-start.10 = (bf16[384,128]{1,0:T(8,128)(2,1)S(1)}, bf16[384,128]{1,0:T(8,128)(2,1)S(1)}, u32[]{:S(2)}, u32[]{:S(2)}) collective-permute-start(bf16[384,128]{1,0:T(8,128)(2,1)S(1)} %get-tuple-element.48), channel_id=1, source_target_pairs={{0,4},{2,10},{4,0},{6,14},{8,12},{10,2},{12,8},{14,6},{16,20},{18,... | collective-permute-start | bytes 294920 | tf_op jit(solution)/shard_map/ppermute | solution.py:391
  45.2 0.7 %collective-permute-start.11 = (bf16[384,128]{1,0:T(8,128)(2,1)S(1)}, bf16[384,128]{1,0:T(8,128)(2,1)S(1)}, u32[]{:S(2)}, u32[]{:S(2)}) collective-permute-start(bf16[384,128]{1,0:T(8,128)(2,1)S(1)} %get-tuple-element.49), channel_id=1, source_target_pairs={{0,8},{2,6},{4,12},{6,2},{8,0},{10,14},{12,4},{14,10},{16,24},{18,... | collective-permute-start | bytes 294920 | tf_op jit(solution)/shard_map/ppermute | solution.py:391
  45.9 0.5 collective-permute-start.12
  46.4 2.0 %collective-permute-start.13 = (bf16[384,128]{1,0:T(8,128)(2,1)S(1)}, bf16[384,128]{1,0:T(8,128)(2,1)S(1)}, u32[]{:S(2)}, u32[]{:S(2)}) collective-permute-start(bf16[384,128]{1,0:T(8,128)(2,1)S(1)} %get-tuple-element.51), channel_id=1, source_target_pairs={{0,12},{2,14},{4,8},{6,10},{8,4},{10,6},{12,0},{14,2},{16,28},{18,... | collective-permute-start | bytes 294920 | tf_op jit(solution)/shard_map/ppermute | solution.py:391
  48.4 0.3 collective-permute-start.14
  48.7 0.0 collective-permute-done.10.refs_1_
  48.7 0.1 collective-permute-start.15
  48.9 1.0 %collective-permute-done.11.refs_2_ = bf16[384,128]{1,0:T(8,128)(2,1)S(1)} collective-permute-done((bf16[384,128]{1,0:T(8,128)(2,1)S(1)}, bf16[384,128]{1,0:T(8,128)(2,1)S(1)}, u32[]{:S(2)}, u32[]{:S(2)}) %collective-permute-start.11) | collective-permute-done | bytes 98336 | tf_op jit(solution)/shard_map/ppermute | solution.py:391
  49.9 1.5 %collective-permute-start.16 = (bf16[384,128]{1,0:T(8,128)(2,1)S(1)}, bf16[384,128]{1,0:T(8,128)(2,1)S(1)}, u32[]{:S(2)}, u32[]{:S(2)}) collective-permute-start(bf16[384,128]{1,0:T(8,128)(2,1)S(1)} %get-tuple-element.54), channel_id=1, source_target_pairs={{0,14},{2,0},{4,10},{6,4},{8,6},{10,8},{12,2},{14,12},{16,30},{18,... | collective-permute-start | bytes 294920 | tf_op jit(solution)/shard_map/ppermute | solution.py:391
  51.4 0.0 collective-permute-done.12.refs_3_
  51.4 2.6 %collective-permute-done.13.refs_4_ = bf16[384,128]{1,0:T(8,128)(2,1)S(1)} collective-permute-done((bf16[384,128]{1,0:T(8,128)(2,1)S(1)}, bf16[384,128]{1,0:T(8,128)(2,1)S(1)}, u32[]{:S(2)}, u32[]{:S(2)}) %collective-permute-start.13) | collective-permute-done | bytes 98336 | tf_op jit(solution)/shard_map/ppermute | solution.py:391
  54.0 0.3 collective-permute-done.14.refs_5_
  54.3 0.9 %collective-permute-done.15.refs_6_ = bf16[384,128]{1,0:T(8,128)(2,1)S(1)} collective-permute-done((bf16[384,128]{1,0:T(8,128)(2,1)S(1)}, bf16[384,128]{1,0:T(8,128)(2,1)S(1)}, u32[]{:S(2)}, u32[]{:S(2)}) %collective-permute-start.15) | collective-permute-done | bytes 98336 | tf_op jit(solution)/shard_map/ppermute | solution.py:391
  55.2 0.0 collective-permute-done.16.refs_7_
  55.3 1.7 %unpack.1 = (bf16[256,512]{1,0:T(8,128)(2,1)}, bf16[256,512]{1,0:T(8,128)(2,1)}, bf16[256,512]{1,0:T(8,128)(2,1)}) custom-call(s32[18]{0:T(128)S(1)} %pad_add_fusion.place_ref, bf16[384,128]{1,0:T(8,128)(2,1)S(1)} %get-tuple-element.47.refs_0_, bf16[384,128]{1,0:T(8,128)(2,1)S(1)} %collective-permute-done.10.refs_1_, ...), custom_call_target="tpu_custom_call" | custom-call | bytes 2097152 | tf_op jit(solution)/shard_map/unpack/pallas_call | solution.py:356
Async XLA Ops:
  0.6 9.8 %collective-permute-start = (bf16[128,1024]{1,0:T(8,128)(2,1)}, bf16[128,1024]{1,0:T(8,128)(2,1)S(1)}, u32[]{:S(2)}, u32[]{:S(2)}) collective-permute-start(bf16[128,1024]{1,0:T(8,128)(2,1)} %refs_0_.1), channel_id=1, source_target_pairs={{0,1},{1,0},{2,3},{3,2},{4,5},{5,4},{6,7},{7,6},{8,9},{9,8},{10,11... | collective-permute-start | bytes 786440 | tf_op jit(solution)/shard_map/ppermute | solution.py:404
  3.6 6.8 %copy-start.1 = (bf16[256,512]{1,0:T(8,128)(2,1)S(1)}, bf16[256,512]{1,0:T(8,128)(2,1)}, u32[]{:S(2)}) copy-start(bf16[256,512]{1,0:T(8,128)(2,1)} %query_ref.1) | copy-start | bytes 786436
  3.6 6.8 %copy-start.2 = (bf16[128,1024]{1,0:T(8,128)(2,1)S(1)}, bf16[128,1024]{1,0:T(8,128)(2,1)}, u32[]{:S(2)}) copy-start(bf16[128,1024]{1,0:T(8,128)(2,1)} %refs_0_.1) | copy-start | bytes 786436
  5.8 4.7 %copy-start = (bf16[512,1024]{1,0:T(8,128)(2,1)S(1)}, bf16[512,1024]{1,0:T(8,128)(2,1)}, u32[]{:S(2)}) copy-start(bf16[512,1024]{1,0:T(8,128)(2,1)} %weight_ref.1) | copy-start | bytes 3145732
  5.8 13.3 %all-to-all-start = ((bf16[8,256,128]{2,1,0:T(8,128)(2,1)}), bf16[8,256,128]{2,1,0:T(8,128)(2,1)S(1)}, u32[]{:S(2)}, u32[]{:S(2)}) async-start(bf16[8,256,128]{2,1,0:T(8,128)(2,1)} %pack_rows.1), calls=%async_computation | async-start | bytes 1048576 | tf_op jit(solution)/shard_map/all_to_all | solution.py:415
  9.7 0.7 %copy-start.3 = (s32[16]{0:T(128)S(1)}, s32[16]{0:T(128)}, u32[]{:S(2)}) copy-start(s32[16]{0:T(128)} %param.11) | copy-start | bytes 196
  12.0 8.1 %collective-permute-start.1 = (bf16[256,128]{1,0:T(8,128)(2,1)S(1)}, bf16[256,128]{1,0:T(8,128)(2,1)S(1)}, u32[]{:S(2)}, u32[]{:S(2)}) collective-permute-start(bf16[256,128]{1,0:T(8,128)(2,1)S(1)} %get-tuple-element.31), channel_id=1, source_target_pairs={{0,4},{2,10},{4,0},{6,14},{8,12},{10,2},{12,8},{14,6},{16,20},{18,... | collective-permute-start | bytes 196616 | tf_op jit(solution)/shard_map/ppermute | solution.py:391
  14.1 6.6 %collective-permute-start.2 = (bf16[256,128]{1,0:T(8,128)(2,1)S(1)}, bf16[256,128]{1,0:T(8,128)(2,1)S(1)}, u32[]{:S(2)}, u32[]{:S(2)}) collective-permute-start(bf16[256,128]{1,0:T(8,128)(2,1)S(1)} %get-tuple-element.32), channel_id=1, source_target_pairs={{0,8},{2,6},{4,12},{6,2},{8,0},{10,14},{12,4},{14,10},{16,24},{18,... | collective-permute-start | bytes 196616 | tf_op jit(solution)/shard_map/ppermute | solution.py:391
  15.6 5.3 %collective-permute-start.3 = (bf16[256,128]{1,0:T(8,128)(2,1)S(1)}, bf16[256,128]{1,0:T(8,128)(2,1)S(1)}, u32[]{:S(2)}, u32[]{:S(2)}) collective-permute-start(bf16[256,128]{1,0:T(8,128)(2,1)S(1)} %get-tuple-element.33), channel_id=1, source_target_pairs={{0,6},{2,8},{4,2},{6,12},{8,14},{10,0},{12,10},{14,4},{16,22},{18,... | collective-permute-start | bytes 196616 | tf_op jit(solution)/shard_map/ppermute | solution.py:391
  15.6 15.5 %collective-permute-start.5 = (bf16[256,128]{1,0:T(8,128)(2,1)S(1)}, bf16[256,128]{1,0:T(8,128)(2,1)S(1)}, u32[]{:S(2)}, u32[]{:S(2)}) collective-permute-start(bf16[256,128]{1,0:T(8,128)(2,1)S(1)} %get-tuple-element.36), channel_id=1, source_target_pairs={{0,12},{2,14},{4,8},{6,10},{8,4},{10,6},{12,0},{14,2},{16,28},{18,... | collective-permute-start | bytes 196616 | tf_op jit(solution)/shard_map/ppermute | solution.py:391
  16.8 14.3 %collective-permute-start.6 = (bf16[256,128]{1,0:T(8,128)(2,1)S(1)}, bf16[256,128]{1,0:T(8,128)(2,1)S(1)}, u32[]{:S(2)}, u32[]{:S(2)}) collective-permute-start(bf16[256,128]{1,0:T(8,128)(2,1)S(1)} %get-tuple-element.37), channel_id=1, source_target_pairs={{0,10},{2,4},{4,14},{6,0},{8,2},{10,12},{12,6},{14,8},{16,26},{18,... | collective-permute-start | bytes 196616 | tf_op jit(solution)/shard_map/ppermute | solution.py:391
  20.1 11.0 %collective-permute-start.7 = (bf16[256,128]{1,0:T(8,128)(2,1)S(1)}, bf16[256,128]{1,0:T(8,128)(2,1)S(1)}, u32[]{:S(2)}, u32[]{:S(2)}) collective-permute-start(bf16[256,128]{1,0:T(8,128)(2,1)S(1)} %get-tuple-element.38), channel_id=1, source_target_pairs={{0,14},{2,0},{4,10},{6,4},{8,6},{10,8},{12,2},{14,12},{16,30},{18,... | collective-permute-start | bytes 196616 | tf_op jit(solution)/shard_map/ppermute | solution.py:391
  20.7 10.4 %collective-permute-start.8 = (bf16[256,128]{1,0:T(8,128)(2,1)S(1)}, bf16[256,128]{1,0:T(8,128)(2,1)S(1)}, u32[]{:S(2)}, u32[]{:S(2)}) collective-permute-start(bf16[256,128]{1,0:T(8,128)(2,1)S(1)} %get-tuple-element.39), channel_id=1, source_target_pairs={{0,2},{2,12},{4,6},{6,8},{8,10},{10,4},{12,14},{14,0},{16,18},{18,... | collective-permute-start | bytes 196616 | tf_op jit(solution)/shard_map/ppermute | solution.py:391
  20.9 10.2 %collective-permute-start.4 = (bf16[128,128]{1,0:T(8,128)(2,1)S(1)}, bf16[128,128]{1,0:T(8,128)(2,1)S(1)}, u32[]{:S(2)}, u32[]{:S(2)}) collective-permute-start(bf16[128,128]{1,0:T(8,128)(2,1)S(1)} %get-tuple-element.35.picks_ref), channel_id=1, source_target_pairs={{0,16},{2,18},{4,20},{6,22},{8,24},{10,26},{12,28},{14,30},{16,0},... | collective-permute-start | bytes 98312 | tf_op jit(solution)/shard_map/ppermute | solution.py:399
  33.6 7.2 %collective-permute-start.9 = (f32[128,128]{1,0:T(8,128)S(1)}, f32[128,128]{1,0:T(8,128)S(1)}, u32[]{:S(2)}, u32[]{:S(2)}) collective-permute-start(f32[128,128]{1,0:T(8,128)S(1)} %get-tuple-element.46), channel_id=1, source_target_pairs={{0,16},{2,18},{4,20},{6,22},{8,24},{10,26},{12,28},{14,30},{16,0},... | collective-permute-start | bytes 196616 | tf_op jit(solution)/shard_map/ppermute | solution.py:399
  43.7 5.0 %collective-permute-start.10 = (bf16[384,128]{1,0:T(8,128)(2,1)S(1)}, bf16[384,128]{1,0:T(8,128)(2,1)S(1)}, u32[]{:S(2)}, u32[]{:S(2)}) collective-permute-start(bf16[384,128]{1,0:T(8,128)(2,1)S(1)} %get-tuple-element.48), channel_id=1, source_target_pairs={{0,4},{2,10},{4,0},{6,14},{8,12},{10,2},{12,8},{14,6},{16,20},{18,... | collective-permute-start | bytes 294920 | tf_op jit(solution)/shard_map/ppermute | solution.py:391
  45.2 4.6 %collective-permute-start.11 = (bf16[384,128]{1,0:T(8,128)(2,1)S(1)}, bf16[384,128]{1,0:T(8,128)(2,1)S(1)}, u32[]{:S(2)}, u32[]{:S(2)}) collective-permute-start(bf16[384,128]{1,0:T(8,128)(2,1)S(1)} %get-tuple-element.49), channel_id=1, source_target_pairs={{0,8},{2,6},{4,12},{6,2},{8,0},{10,14},{12,4},{14,10},{16,24},{18,... | collective-permute-start | bytes 294920 | tf_op jit(solution)/shard_map/ppermute | solution.py:391
  45.9 5.4 %collective-permute-start.12 = (bf16[384,128]{1,0:T(8,128)(2,1)S(1)}, bf16[384,128]{1,0:T(8,128)(2,1)S(1)}, u32[]{:S(2)}, u32[]{:S(2)}) collective-permute-start(bf16[384,128]{1,0:T(8,128)(2,1)S(1)} %get-tuple-element.50), channel_id=1, source_target_pairs={{0,10},{2,4},{4,14},{6,0},{8,2},{10,12},{12,6},{14,8},{16,26},{18,... | collective-permute-start | bytes 294920 | tf_op jit(solution)/shard_map/ppermute | solution.py:391
  46.4 7.6 %collective-permute-start.13 = (bf16[384,128]{1,0:T(8,128)(2,1)S(1)}, bf16[384,128]{1,0:T(8,128)(2,1)S(1)}, u32[]{:S(2)}, u32[]{:S(2)}) collective-permute-start(bf16[384,128]{1,0:T(8,128)(2,1)S(1)} %get-tuple-element.51), channel_id=1, source_target_pairs={{0,12},{2,14},{4,8},{6,10},{8,4},{10,6},{12,0},{14,2},{16,28},{18,... | collective-permute-start | bytes 294920 | tf_op jit(solution)/shard_map/ppermute | solution.py:391
  48.4 5.9 %collective-permute-start.14 = (bf16[384,128]{1,0:T(8,128)(2,1)S(1)}, bf16[384,128]{1,0:T(8,128)(2,1)S(1)}, u32[]{:S(2)}, u32[]{:S(2)}) collective-permute-start(bf16[384,128]{1,0:T(8,128)(2,1)S(1)} %get-tuple-element.52), channel_id=1, source_target_pairs={{0,6},{2,8},{4,2},{6,12},{8,14},{10,0},{12,10},{14,4},{16,22},{18,... | collective-permute-start | bytes 294920 | tf_op jit(solution)/shard_map/ppermute | solution.py:391
  48.7 6.5 %collective-permute-start.15 = (bf16[384,128]{1,0:T(8,128)(2,1)S(1)}, bf16[384,128]{1,0:T(8,128)(2,1)S(1)}, u32[]{:S(2)}, u32[]{:S(2)}) collective-permute-start(bf16[384,128]{1,0:T(8,128)(2,1)S(1)} %get-tuple-element.53), channel_id=1, source_target_pairs={{0,2},{2,12},{4,6},{6,8},{8,10},{10,4},{12,14},{14,0},{16,18},{18,... | collective-permute-start | bytes 294920 | tf_op jit(solution)/shard_map/ppermute | solution.py:391
  49.9 5.4 %collective-permute-start.16 = (bf16[384,128]{1,0:T(8,128)(2,1)S(1)}, bf16[384,128]{1,0:T(8,128)(2,1)S(1)}, u32[]{:S(2)}, u32[]{:S(2)}) collective-permute-start(bf16[384,128]{1,0:T(8,128)(2,1)S(1)} %get-tuple-element.54), channel_id=1, source_target_pairs={{0,14},{2,0},{4,10},{6,4},{8,6},{10,8},{12,2},{14,12},{16,30},{18,... | collective-permute-start | bytes 294920 | tf_op jit(solution)/shard_map/ppermute | solution.py:391
